TPU v7x, 32 devices: a whole 2x2x4 slice. The times are simulated.
32 devices in a mesh: dp: 8 (over z, x), tensor: 4 (over y, core).
Axes of the slice: x: 2, y: 2, z: 4, core: 2. Of those that a mesh axis runs over, the one named last changes fastest.
Arguments:
- x_first: bfloat16 [64, 8192], P('dp', 'tensor'), may hold values from -64 to 64
- x_second: bfloat16 [64, 8192], P('dp', 'tensor'), may hold values from -64 to 64
- cache_keys: bfloat16 [64, 32, 1024], P('dp', 'tensor'), may hold values from -512 to 512
- cache_values: bfloat16 [64, 32, 1024], P('dp', 'tensor'), may hold values from -6 to 6
- ancestors: int32 [64], replicated, may hold values from 0 to 63, as said below
- attn_gain: float32 [8192], P('tensor'), may hold values from 0.1 to 1.9
- ffn_gain: float32 [8192], P('tensor'), may hold values from 0.1 to 1.9
- w_query: bfloat16 [8192, 8192], P('tensor', 'dp'), may hold values from -0.0625 to 0.0625
- w_keyval: bfloat16 [8192, 2048], P('tensor', 'dp'), may hold values from -0.0625 to 0.0625
- w_out: bfloat16 [8192, 8192], P('dp', 'tensor'), may hold values from -0.5 to 0.5
- w_gate: bfloat16 [8192, 14336], P('tensor', 'dp'), may hold values from -0.0625 to 0.0625
- w_up: bfloat16 [8192, 14336], P('tensor', 'dp'), may hold values from -0.0625 to 0.0625
- w_down: bfloat16 [14336, 8192], P('dp', 'tensor'), may hold values from -0.046875 to 0.046875
Outputs:
- attn_update: bfloat16 [2, 64, 8192], P(None, 'dp', 'tensor')
- ffn_update: bfloat16 [2, 64, 8192], P(None, 'dp', 'tensor')
Inputs may be any that keep to these rules, and one draw needn't show every extreme that they name: Particle p continues the cache of particle ancestors[p]. Among the 8 particles of one index of dp, at most 2 have ancestors in any one aligned block of 8 particles, and for every index of dp some block is named exactly 2 times.
All inputs are finite; a program needn't handle non-finite values.
Results may differ from a plain program's by a relative error of at most 0.04.
Values may be sent and summed in bfloat16 or wider, within the bound.
No kernel may reach another device: no remote copies, remote signals or barrier semaphores. Data moves between devices by JAX's collectives and lax.ppermute only.
A program may use at most 64 MiB of HBM per device.

v0:
```python
import math

import jax
import jax.numpy as jnp
from jax import lax
from jax.sharding import PartitionSpec as P

KVH = 8
HD = 128
GROUP = 8


EPS = 1e-05
ROPE_BASE = 500000.0


def combined_all(x, axis, combine):
    everything = jax.tree.map(lambda part: lax.all_gather(part, axis), x)
    leading = jax.tree.map(lambda part: part[0], everything)

    def turn(k, so_far):
        return combine(so_far, jax.tree.map(lambda part: part[k], everything))

    return lax.fori_loop(1, lax.axis_size(axis), turn, leading)


def normalize(residual_in, gain):
    wide = residual_in.astype(jnp.float32)
    squares = lax.psum(jnp.sum(wide * wide, axis=1), "tensor")
    model_width = residual_in.shape[1] * lax.axis_size("tensor")
    return (wide * lax.rsqrt(squares[:, None] / model_width + EPS) * gain[None, :]).astype(
        jnp.bfloat16
    )


def project_rows(normed, weights):
    piece = lax.all_gather(normed, "dp", axis=0, tiled=True)
    return jnp.concatenate(
        [jnp.dot(piece, weight, preferred_element_type=jnp.float32) for weight in weights], axis=1
    )


def reduce_rows(left, weight):
    return lax.psum_scatter(
        jnp.dot(left, weight, preferred_element_type=jnp.float32).astype(jnp.bfloat16),
        "dp",
        scatter_dimension=0,
        tiled=True,
    ).astype(jnp.float32)


def rotate(tensor, position):
    half_width = tensor.shape[-1] // 2
    freq = jnp.power(
        jnp.float32(ROPE_BASE), -2.0 * jnp.arange(half_width, dtype=jnp.float32) / tensor.shape[-1]
    )
    angle = jnp.float32(position) * freq
    cosine = jnp.cos(angle)
    sine = jnp.sin(angle)
    first_half = tensor[..., :half_width]
    second_half = tensor[..., half_width:]
    return jnp.concatenate(
        [first_half * cosine - second_half * sine, second_half * cosine + first_half * sine],
        axis=-1,
    )


def project_step(residual_in, gain, w_query, w_keyval, position):
    normed = normalize(residual_in, gain)
    partial_value = project_rows(normed, (w_query, w_keyval))
    summed = lax.psum(partial_value, "tensor").astype(jnp.bfloat16)
    query_cols = w_query.shape[1]
    queries, keyvals = (
        lax.all_to_all(summed[:, :query_cols], "dp", split_axis=0, concat_axis=1, tiled=True),
        lax.all_to_all(summed[:, query_cols:], "dp", split_axis=0, concat_axis=1, tiled=True),
    )
    count = residual_in.shape[0]
    queries = rotate(queries.astype(jnp.float32).reshape(count, KVH, GROUP, HD), position).astype(
        jnp.bfloat16
    )
    keyvals = keyvals.reshape(count, 2, KVH, HD)
    new_keys = rotate(keyvals[:, 0].astype(jnp.float32), position).astype(jnp.bfloat16)
    return (queries, new_keys, keyvals[:, 1])


def partial_attention(queries, keys, values):
    scores = jnp.einsum("rkgd,rlkd->rkgl", queries, keys, preferred_element_type=jnp.float32) * (
        1.0 / math.sqrt(HD)
    )
    highest = jnp.max(scores, axis=-1)
    weights = jnp.exp(scores - highest[..., None])
    totals = jnp.sum(weights, axis=-1)
    mixed = jnp.einsum(
        "rkgl,rlkd->rkgd", weights, values.astype(jnp.float32), precision=lax.Precision.HIGHEST
    )
    return (highest, totals, mixed)


def combine(first, second):
    highest = jnp.maximum(first[0], second[0])
    first_scale = jnp.exp(first[0] - highest)
    second_scale = jnp.exp(second[0] - highest)
    totals = first[1] * first_scale + second[1] * second_scale
    mixed = first[2] * first_scale[..., None] + second[2] * second_scale[..., None]
    return (highest, totals, mixed)


def merge_positions(attn_state):
    return combined_all(attn_state, "tensor", combine)


def add_key(attn_state, queries, key_one, value_one):
    score = jnp.einsum("rkgd,rkd->rkg", queries, key_one, preferred_element_type=jnp.float32) * (
        1.0 / math.sqrt(HD)
    )
    spread = jnp.broadcast_to(value_one.astype(jnp.float32)[:, :, None, :], attn_state[2].shape)
    return combine(attn_state, (score, jnp.ones_like(score), spread))


def finish(attn_state):
    count = attn_state[2].shape[0]
    return (attn_state[2] / attn_state[1][..., None]).reshape(count, -1).astype(jnp.bfloat16)


def updates(residual_in, mixed, ffn_gain, w_out, w_gate, w_up, w_down):
    spread = lax.all_to_all(mixed, "dp", split_axis=1, concat_axis=0, tiled=True)
    attn_part = reduce_rows(spread, w_out).astype(jnp.bfloat16)
    hidden_in = (residual_in.astype(jnp.float32) + attn_part.astype(jnp.float32)).astype(
        jnp.bfloat16
    )
    normed = normalize(hidden_in, ffn_gain)
    partial_value = project_rows(normed, (w_gate, w_up))
    hidden_cols = w_gate.shape[1]
    summed = lax.psum(partial_value.astype(jnp.bfloat16), "tensor").astype(jnp.float32)
    hidden = (jax.nn.silu(summed[:, :hidden_cols]) * summed[:, hidden_cols:]).astype(jnp.bfloat16)
    ffn_part = reduce_rows(hidden, w_down).astype(jnp.bfloat16)
    return (attn_part, ffn_part)


def route_tables(ancestors, part_dev, groups):
    source_dev = (ancestors // part_dev).reshape(groups, part_dev)
    local_index = (ancestors % part_dev).reshape(groups, part_dev)
    same_source = source_dev[:, :, None] == source_dev[:, None, :]
    members = jnp.arange(part_dev, dtype=jnp.int32)
    earlier = members[None, :] < members[:, None]
    order_rank = jnp.sum((same_source & earlier[None, :, :]).astype(jnp.int32), axis=2)
    return (source_dev, local_index, order_rank)


def local(
    x_first,
    x_second,
    cache_keys,
    cache_values,
    ancestors,
    attn_gain,
    ffn_gain,
    w_query,
    w_keyval,
    w_out,
    w_gate,
    w_up,
    w_down,
):
    groups = lax.axis_size("dp")
    part_dev = x_first.shape[0]
    cache_span = cache_keys.shape[1]
    context = cache_span * lax.axis_size("tensor")
    capacity = max(2, -(-part_dev // groups))
    keys_here = cache_keys.reshape(part_dev, cache_span, KVH, HD)
    values_here = cache_values.reshape(part_dev, cache_span, KVH, HD)
    queries_one, keys_one, values_one = project_step(x_first, attn_gain, w_query, w_keyval, context)
    attn_state = merge_positions(partial_attention(queries_one, keys_here, values_here))
    mixed_one = finish(add_key(attn_state, queries_one, keys_one, values_one))
    attn_one, ffn_one = updates(x_first, mixed_one, ffn_gain, w_out, w_gate, w_up, w_down)
    queries_two, keys_two, values_two = project_step(
        x_second, attn_gain, w_query, w_keyval, context + 1
    )
    token_pairs = jnp.concatenate(
        [keys_one.reshape(part_dev, -1), values_one.reshape(part_dev, -1)], axis=1
    )
    source_dev, local_index, order_rank = route_tables(ancestors, part_dev, groups)
    device_index = lax.axis_index("dp")
    home_source = lax.dynamic_index_in_dim(source_dev, device_index, 0, keepdims=False)
    home_rank = lax.dynamic_index_in_dim(order_rank, device_index, 0, keepdims=False)
    pick_index = home_source * capacity + home_rank
    slot_ids = jnp.arange(capacity, dtype=jnp.int32)
    wanted_here = (source_dev[:, None, :] == device_index) & (
        order_rank[:, None, :] == slot_ids[None, :, None]
    )
    chosen = jnp.sum(jnp.where(wanted_here, local_index[:, None, :], 0), axis=2).reshape(-1)
    arrived = (
        lax.all_to_all(
            jnp.take(cache_keys, chosen, axis=0).reshape(groups, capacity, cache_span, -1),
            "dp",
            split_axis=0,
            concat_axis=0,
            tiled=True,
        ),
        lax.all_to_all(
            jnp.take(cache_values, chosen, axis=0).reshape(groups, capacity, cache_span, -1),
            "dp",
            split_axis=0,
            concat_axis=0,
            tiled=True,
        ),
        lax.all_to_all(
            jnp.take(token_pairs, chosen, axis=0).reshape(groups, capacity, -1),
            "dp",
            split_axis=0,
            concat_axis=0,
            tiled=True,
        ),
    )
    moved_keys = jnp.take(
        arrived[0].reshape(groups * capacity, cache_span, KVH, HD), pick_index, axis=0
    )
    moved_values = jnp.take(
        arrived[1].reshape(groups * capacity, cache_span, KVH, HD), pick_index, axis=0
    )
    moved_token = jnp.take(arrived[2].reshape(groups * capacity, -1), pick_index, axis=0)
    attn_state = partial_attention(queries_two, moved_keys, moved_values)
    attn_state = merge_positions(attn_state)
    key_width = KVH * HD
    attn_state = add_key(
        attn_state,
        queries_two,
        moved_token[:, :key_width].reshape(part_dev, KVH, HD),
        moved_token[:, key_width:].reshape(part_dev, KVH, HD),
    )
    attn_state = add_key(attn_state, queries_two, keys_two, values_two)
    mixed_two = finish(attn_state)
    attn_two, ffn_two = updates(x_second, mixed_two, ffn_gain, w_out, w_gate, w_up, w_down)
    return (jnp.stack([attn_one, attn_two]), jnp.stack([ffn_one, ffn_two]))


def solution(mesh):
    return jax.shard_map(
        local,
        mesh=mesh,
        in_specs=(
            P("dp", "tensor"),
            P("dp", "tensor"),
            P("dp", "tensor", None),
            P("dp", "tensor", None),
            P(),
            P("tensor"),
            P("tensor"),
            P("tensor", "dp"),
            P("tensor", "dp"),
            P("dp", "tensor"),
            P("tensor", "dp"),
            P("tensor", "dp"),
            P("dp", "tensor"),
        ),
        out_specs=(P(None, "dp", "tensor"), P(None, "dp", "tensor")),
        check_vma=False,
    )
```

profile of v0, /device:TPU:0, one launch (start us, length us, event | category | flops | bytes accessed | tf_op | source)
XLA Modules:
  0.0 616.3 jit_solution(8599089540115529691)
XLA Ops:
  7.2 1.0 fusion.32
  8.2 0.9 fusion.36
  9.0 8.4 %all-reduce.2 = (f32[8]{0:T(128)S(1)}, f32[8]{0:T(128)S(1)}) all-reduce(f32[8]{0:T(128)S(1)} %fusion.36, f32[8]{0:T(128)S(1)} %fusion.32), channel_id=1, replica_groups=mesh['dp'=8,'tensor'=4] {'tensor'}, use_global_device_ids=true, to_apply=%region_9.0 | all-reduce | flops 16 | bytes 128 | tf_op jit(solution)/shard_map/psum | solution.py:29
  17.4 1.0 fusion.34
  18.4 31.3 %all_gather.48 = bf16[64,2048]{1,0:T(8,128)(2,1)S(1)} all-gather(bf16[8,2048]{1,0:T(8,128)(2,1)S(1)} %get-tuple-element.441), channel_id=1, replica_groups=mesh['dp'=8,'tensor'=4] {'dp'}, dimensions={0}, use_global_device_ids=true | all-gather | bytes 294912 | tf_op jit(solution)/shard_map/all_gather | solution.py:37
  50.1 3.1 fusion.83
  53.2 30.9 %all_gather.55 = bf16[64,2048]{1,0:T(8,128)(2,1)S(1)} all-gather(bf16[8,2048]{1,0:T(8,128)(2,1)S(1)} %get-tuple-element.442), channel_id=1, replica_groups=mesh['dp'=8,'tensor'=4] {'dp'}, dimensions={0}, use_global_device_ids=true | all-gather | bytes 294912 | tf_op jit(solution)/shard_map/all_gather | solution.py:37
  84.4 0.8 fusion.85
  85.3 17.0 %all-reduce.8 = (bf16[64,1280]{1,0:T(8,128)(2,1)S(1)}, bf16[64,1280]{1,0:T(8,128)(2,1)S(1)}) all-reduce(f32[64,1280]{1,0:T(8,128)S(1)} %pad_maximum_fusion.3, f32[64,1280]{1,0:T(8,128)S(1)} %pad_maximum_fusion.2), channel_id=1, replica_groups=mesh['dp'=8,'tensor'=4] {'tensor'}, use_global_device_ids=true, to_apply=%region_10.0 | all-reduce | flops 163840 | bytes 983040 | tf_op jit(solution)/shard_map/psum | solution.py:71
  102.9 5.1 all-to-all-start.7
  112.3 0.9 broadcast_select_fusion
  113.2 1.5 all-to-all-done.7
  114.7 4.6 all-to-all-start.1
  119.3 6.6 %all-to-all-done.1 = bf16[8,8,256]{2,1,0:T(8,128)(2,1)S(1)} async-done(((bf16[8,8,256]{2,1,0:T(8,128)(2,1)}), bf16[8,8,256]{2,1,0:T(8,128)(2,1)S(1)}, u32[]{:S(2)}, u32[]{:S(2)}) %all-to-all-start.1) | async-done | bytes 32800 | tf_op jit(solution)/shard_map/all_to_all | solution.py:75
  127.5 3.4 all-to-all-start.6
  131.2 6.6 %all-to-all-done.6 = bf16[8,2,2048]{2,1,0:T(2,128)(2,1)S(1)} async-done(((bf16[8,2,2048]{2,1,0:T(2,128)(2,1)}), bf16[8,2,2048]{2,1,0:T(2,128)(2,1)S(1)}, u32[]{:S(2)}, u32[]{:S(2)}) %all-to-all-start.6) | async-done | bytes 65568 | tf_op jit(solution)/shard_map/all_to_all | solution.py:207
  137.7 3.4 all-to-all-start
  141.8 6.6 %all-to-all-done = bf16[8,8,1024]{2,1,0:T(8,128)(2,1)S(1)} async-done(((bf16[8,8,1024]{2,1,0:T(8,128)(2,1)}), bf16[8,8,1024]{2,1,0:T(8,128)(2,1)S(1)}, u32[]{:S(2)}, u32[]{:S(2)}) %all-to-all-start) | async-done | bytes 131104 | tf_op jit(solution)/shard_map/all_to_all | solution.py:74
  148.4 3.4 all-to-all-start.3
  151.9 7.2 %all-to-all-done.3 = bf16[8,8,1024]{2,1,0:T(8,128)(2,1)S(1)} async-done(((bf16[8,8,1024]{2,1,0:T(8,128)(2,1)}), bf16[8,8,1024]{2,1,0:T(8,128)(2,1)S(1)}, u32[]{:S(2)}, u32[]{:S(2)}) %all-to-all-start.3) | async-done | bytes 131104 | tf_op jit(solution)/shard_map/all_to_all | solution.py:74
  159.1 3.4 all-to-all-start.4
  163.3 1.2 fusion.8
  164.8 5.9 all-to-all-done.4
  170.7 3.4 all-to-all-start.5
  174.3 6.1 all-gather
  180.4 5.4 all-gather.1
  187.9 5.4 all-gather.3
  193.4 5.4 all-gather.4
  198.9 1.2 fusion.10
  200.1 1.0 slice.135
  201.1 3.8 while.38
  201.1 1.2 fusion.112
  202.4 1.2 fusion.112
  203.7 1.2 fusion.112
  206.0 5.9 all-to-all-start.2
  211.8 6.0 all-gather.11.cloned.1.call-done
  217.8 1.0 slice.146
  218.8 3.8 while.39
  218.9 1.2 fusion.114
  220.2 1.2 fusion.114
  221.4 1.2 fusion.114
  223.9 5.5 all-to-all-start.8
  229.4 3.7 convolution_convert_fusion.7
  233.4 3.4 all-to-all-done.8
  236.8 3.7 convolution_convert_fusion.6
  240.6 54.7 %reduce-scatter.5.cloned.1.call-done = bf16[8,2048]{1,0:T(8,128)(2,1)} async-done(((bf16[64,2048]{1,0:T(8,128)(2,1)}), bf16[8,2048]{1,0:T(8,128)(2,1)}) %reduce-scatter.5.cloned.1.call-update) | async-done | bytes 32784 | tf_op jit(solution)/shard_map/reduce_scatter | solution.py:44
  295.2 0.9 fusion.26
  296.1 62.6 %reduce-scatter.7.cloned.1.call-done = bf16[8,2048]{1,0:T(8,128)(2,1)} async-done(((bf16[64,2048]{1,0:T(8,128)(2,1)}), bf16[8,2048]{1,0:T(8,128)(2,1)}) %reduce-scatter.7.cloned.1.call-update) | async-done | bytes 32784 | tf_op jit(solution)/shard_map/reduce_scatter | solution.py:44
  358.7 0.9 fusion.29
  359.6 5.7 all-reduce
  365.3 0.9 fusion.28
  366.2 30.8 %all_gather.62 = bf16[64,2048]{1,0:T(8,128)(2,1)S(1)} all-gather(bf16[8,2048]{1,0:T(8,128)(2,1)S(1)} %get-tuple-element.439), channel_id=1, replica_groups=mesh['dp'=8,'tensor'=4] {'dp'}, dimensions={0}, use_global_device_ids=true | all-gather | bytes 294912 | tf_op jit(solution)/shard_map/all_gather | solution.py:37
  397.0 4.6 convolution_convert_fusion.4
  401.6 4.6 convolution_convert_fusion.5
  406.2 30.8 %all_gather.63 = bf16[64,2048]{1,0:T(8,128)(2,1)S(1)} all-gather(bf16[8,2048]{1,0:T(8,128)(2,1)S(1)} %get-tuple-element.440), channel_id=1, replica_groups=mesh['dp'=8,'tensor'=4] {'dp'}, dimensions={0}, use_global_device_ids=true | all-gather | bytes 294912 | tf_op jit(solution)/shard_map/all_gather | solution.py:37
  437.1 1.4 convolution_convert_fusion.1
  438.4 1.4 convolution_convert_fusion.2
  441.5 34.9 %all-reduce.7.cloned.1.call-done = (bf16[64,3584]{1,0:T(8,128)(2,1)}, bf16[64,3584]{1,0:T(8,128)(2,1)}) async-done(((bf16[64,3584]{1,0:T(8,128)(2,1)}, bf16[64,3584]{1,0:T(8,128)(2,1)}), (bf16[64,3584]{1,0:T(8,128)(2,1)}, bf16[64,3584]{1,0:T(8,128)(2,1)})) %all-reduce.7.cloned.1.call-update) | async-done | bytes 917520 | tf_op jit(solution)/shard_map/psum | solution.py:134
  476.4 1.1 convert_element_type.211
  477.5 5.3 convolution_convert_fusion
  482.9 5.2 convolution_convert_fusion.3
  488.8 55.6 %reduce-scatter.11.cloned.1.call-done = bf16[8,2048]{1,0:T(8,128)(2,1)} async-done(((bf16[64,2048]{1,0:T(8,128)(2,1)}), bf16[8,2048]{1,0:T(8,128)(2,1)}) %reduce-scatter.11.cloned.1.call-update) | async-done | bytes 32784 | tf_op jit(solution)/shard_map/reduce_scatter | solution.py:44
  544.4 63.7 %reduce-scatter.9.cloned.1.call-done = bf16[8,2048]{1,0:T(8,128)(2,1)} async-done(((bf16[64,2048]{1,0:T(8,128)(2,1)}), bf16[8,2048]{1,0:T(8,128)(2,1)}) %reduce-scatter.9.cloned.1.call-update) | async-done | bytes 32784 | tf_op jit(solution)/shard_map/reduce_scatter | solution.py:44
  608.1 1.4 pad_maximum_fusion.7
  (142 shorter events, 16.8 us)
Async XLA Ops:
  7.2 42.6 %copy-start = (bf16[2048,256]{1,0:T(8,128)(2,1)S(1)}, bf16[2048,256]{1,0:T(8,128)(2,1)}, u32[]{:S(2)}) copy-start(bf16[2048,256]{1,0:T(8,128)(2,1)} %param.29) | copy-start | bytes 3145732
  17.4 67.0 %copy-start.1 = (bf16[2048,1024]{1,0:T(8,128)(2,1)S(1)}, bf16[2048,1024]{1,0:T(8,128)(2,1)}, u32[]{:S(2)}) copy-start(bf16[2048,1024]{1,0:T(8,128)(2,1)} %param.28) | copy-start | bytes 12582916
  49.8 58.3 %copy-start.10 = (s32[64]{0:T(128)S(1)}, s32[64]{0:T(128)}, u32[]{:S(2)}) copy-start(s32[64]{0:T(128)} %param.25) | copy-start | bytes 772
  49.8 61.3 %copy-start.3 = (bf16[8,8,1024]{2,1,0:T(8,128)(2,1)S(1)}, bf16[8,8,1024]{2,1,0:T(8,128)(2,1)}, u32[]{:S(2)}) copy-start(bf16[8,8,1024]{2,1,0:T(8,128)(2,1)} %param.24) | copy-start | bytes 393220
  50.1 61.6 %copy-start.2 = (bf16[8,8,1024]{2,1,0:T(8,128)(2,1)S(1)}, bf16[8,8,1024]{2,1,0:T(8,128)(2,1)}, u32[]{:S(2)}) copy-start(bf16[8,8,1024]{2,1,0:T(8,128)(2,1)} %param.23) | copy-start | bytes 393220
  102.9 11.8 %all-to-all-start.7 = ((bf16[8,8,256]{2,1,0:T(8,128)(2,1)}), bf16[8,8,256]{2,1,0:T(8,128)(2,1)S(1)}, u32[]{:S(2)}, u32[]{:S(2)}) async-start(bf16[8,8,256]{2,1,0:T(8,128)(2,1)} %slice_bitcast_fusion.2), calls=%async_computation.8 | async-start | bytes 65536 | tf_op jit(solution)/shard_map/all_to_all | solution.py:75
  114.7 11.3 %all-to-all-start.1 = ((bf16[8,8,256]{2,1,0:T(8,128)(2,1)}), bf16[8,8,256]{2,1,0:T(8,128)(2,1)S(1)}, u32[]{:S(2)}, u32[]{:S(2)}) async-start(bf16[8,8,256]{2,1,0:T(8,128)(2,1)} %slice_bitcast_fusion.3), calls=%async_computation.1 | async-start | bytes 65536 | tf_op jit(solution)/shard_map/all_to_all | solution.py:75
  127.5 10.2 %all-to-all-start.6 = ((bf16[8,2,2048]{2,1,0:T(2,128)(2,1)}), bf16[8,2,2048]{2,1,0:T(2,128)(2,1)S(1)}, u32[]{:S(2)}, u32[]{:S(2)}) async-start(bf16[8,2,2048]{2,1,0:T(2,128)(2,1)} %broadcast_select_fusion.2), calls=%async_computation.7 | async-start | bytes 131072 | tf_op jit(solution)/shard_map/all_to_all | solution.py:207
  137.7 10.7 %all-to-all-start = ((bf16[8,8,1024]{2,1,0:T(8,128)(2,1)}), bf16[8,8,1024]{2,1,0:T(8,128)(2,1)S(1)}, u32[]{:S(2)}, u32[]{:S(2)}) async-start(bf16[8,8,1024]{2,1,0:T(8,128)(2,1)} %slice_bitcast_fusion.1), calls=%async_computation | async-start | bytes 262144 | tf_op jit(solution)/shard_map/all_to_all | solution.py:74
  148.4 10.7 %all-to-all-start.3 = ((bf16[8,8,1024]{2,1,0:T(8,128)(2,1)}), bf16[8,8,1024]{2,1,0:T(8,128)(2,1)S(1)}, u32[]{:S(2)}, u32[]{:S(2)}) async-start(bf16[8,8,1024]{2,1,0:T(8,128)(2,1)} %slice_bitcast_fusion), calls=%async_computation.4 | async-start | bytes 262144 | tf_op jit(solution)/shard_map/all_to_all | solution.py:74
  159.1 11.7 %all-to-all-start.4 = ((bf16[8,2,8,1024]{3,2,1,0:T(8,128)(2,1)}), bf16[8,2,8,1024]{3,2,1,0:T(8,128)(2,1)S(1)}, u32[]{:S(2)}, u32[]{:S(2)}) async-start(bf16[8,2,8,1024]{3,2,1,0:T(8,128)(2,1)} %bitcast.30), calls=%async_computation.5 | async-start | bytes 524288 | tf_op jit(solution)/shard_map/all_to_all | solution.py:193
  162.5 37.6 %all-gather.9.cloned.1.call-start = ((), (), s32[]{:S(2)}) async-start(), calls=%async_computation.17 | async-start | bytes 1310720 | tf_op jit(solution)/shard_map/all_gather | solution.py:18
  170.7 16.2 %all-to-all-start.5 = ((bf16[8,2,8,1024]{3,2,1,0:T(8,128)(2,1)}), bf16[8,2,8,1024]{3,2,1,0:T(8,128)(2,1)S(1)}, u32[]{:S(2)}, u32[]{:S(2)}) async-start(bf16[8,2,8,1024]{3,2,1,0:T(8,128)(2,1)} %bitcast.32), calls=%async_computation.6 | async-start | bytes 524288 | tf_op jit(solution)/shard_map/all_to_all | solution.py:200
  174.2 43.7 %all-gather.11.cloned.1.call-start = ((), (), s32[]{:S(2)}) async-start(), calls=%async_computation.18 | async-start | bytes 1310720 | tf_op jit(solution)/shard_map/all_gather | solution.py:18
  206.0 17.9 %all-to-all-start.2 = ((bf16[8,8,1024]{2,0,1:T(8,128)(2,1)}), bf16[8,8,1024]{2,0,1:T(8,128)(2,1)S(1)}, u32[]{:S(2)}, u32[]{:S(2)}) async-start(bf16[8,8,1024]{2,0,1:T(8,128)(2,1)} %bitcast.170), calls=%async_computation.2 | async-start | bytes 262144 | tf_op jit(solution)/shard_map/all_to_all | solution.py:126
  218.8 76.4 %copy-start.4 = (bf16[8,2048]{1,0:T(8,128)(2,1)S(1)}, bf16[8,2048]{1,0:T(8,128)(2,1)}, u32[]{:S(2)}) copy-start(bf16[8,2048]{1,0:T(8,128)(2,1)} %param.21) | copy-start | bytes 98308
  218.8 139.9 %copy-start.5 = (bf16[8,2048]{1,0:T(8,128)(2,1)S(1)}, bf16[8,2048]{1,0:T(8,128)(2,1)}, u32[]{:S(2)}) copy-start(bf16[8,2048]{1,0:T(8,128)(2,1)} %param.22) | copy-start | bytes 98308
  218.8 146.5 %copy-start.9 = (f32[2048]{0:T(1024)S(1)}, f32[2048]{0:T(1024)}, u32[]{:S(2)}) copy-start(f32[2048]{0:T(1024)} %param.27) | copy-start | bytes 24580
  223.9 12.9 %all-to-all-start.8 = ((bf16[8,8,1024]{2,0,1:T(8,128)(2,1)}), bf16[8,8,1024]{2,0,1:T(8,128)(2,1)S(1)}, u32[]{:S(2)}, u32[]{:S(2)}) async-start(bf16[8,8,1024]{2,0,1:T(8,128)(2,1)} %bitcast.169), calls=%async_computation.9 | async-start | bytes 262144 | tf_op jit(solution)/shard_map/all_to_all | solution.py:126
  229.4 65.9 %reduce-scatter.5.cloned.1.call-start = ((), (), s32[]{:S(2)}) async-start(), calls=%async_computation.13 | async-start | bytes 294912 | tf_op jit(solution)/shard_map/reduce_scatter | solution.py:44
  233.2 125.5 %reduce-scatter.7.cloned.1.call-start = ((), (), s32[]{:S(2)}) async-start(), calls=%async_computation.14 | async-start | bytes 294912 | tf_op jit(solution)/shard_map/reduce_scatter | solution.py:44
  240.5 235.9 %all-reduce.7.cloned.1.call-start = ((), (), s32[]{:S(2)}) async-start(), calls=%async_computation.19 | async-start | bytes 1835008 | tf_op jit(solution)/shard_map/psum | solution.py:134
  397.0 40.0 %slice-start = ((s8[7340032]{0:T(1024)(128)(4,1)}), s8[4194304]{0:T(1024)(128)(4,1)S(1)}, s32[]{:S(2)}) async-start(s8[7340032]{0:T(1024)(128)(4,1)} %bitcast.179), calls=%async_computation.20 | async-start | bytes 8388608
  397.0 41.4 %slice-start.2 = ((s8[7340032]{0:T(1024)(128)(4,1)}), s8[4194304]{0:T(1024)(128)(4,1)S(1)}, s32[]{:S(2)}) async-start(s8[7340032]{0:T(1024)(128)(4,1)} %bitcast.181), calls=%async_computation.22 | async-start | bytes 8388608
  401.6 35.4 %slice-start.1 = ((s8[7340032]{0:T(1024)(128)(4,1)}), s8[3145728]{0:T(1024)(128)(4,1)S(1)}, s32[]{:S(2)}) async-start(s8[7340032]{0:T(1024)(128)(4,1)} %bitcast.179), calls=%async_computation.21 | async-start | bytes 6291456
  401.6 36.8 %slice-start.3 = ((s8[7340032]{0:T(1024)(128)(4,1)}), s8[3145728]{0:T(1024)(128)(4,1)S(1)}, s32[]{:S(2)}) async-start(s8[7340032]{0:T(1024)(128)(4,1)} %bitcast.181), calls=%async_computation.23 | async-start | bytes 6291456
  441.5 103.0 %reduce-scatter.11.cloned.1.call-start = ((), (), s32[]{:S(2)}) async-start(), calls=%async_computation.16 | async-start | bytes 294912 | tf_op jit(solution)/shard_map/reduce_scatter | solution.py:44
  477.5 5.4 copy-start.6
  482.8 125.3 %reduce-scatter.9.cloned.1.call-start = ((), (), s32[]{:S(2)}) async-start(), calls=%async_computation.15 | async-start | bytes 294912 | tf_op jit(solution)/shard_map/reduce_scatter | solution.py:44
  482.9 5.2 copy-start.7
  482.9 5.2 copy-start.8
Sparse Core Ops, SparseCore 0:
  164.9 18.4 all-gather.8
  200.2 17.5 all-gather.10
  233.5 61.6 reduce-scatter.4
  298.4 60.2 reduce-scatter.6
  441.6 34.7 all-reduce.6
  482.9 61.4 reduce-scatter.10
  547.8 60.2 reduce-scatter.8
where the time goes:
time: 618 us; the launch traced here: 616 us
  waiting for transfers between devices  315 us (51%)
  blocking collectives  177 us (29%)
  starting transfers between devices  38.4 us (6%)
  matrix products  38.1 us (6%)
  other arithmetic  21.8 us (4%)
  between operations  14.7 us (2%)
  local copies, waits for them, and re-layouts  10.5 us (2%)
    reduce_scatter x4, waiting for transfers between devices, reduce_rows(): lax.psum_scatter(jnp.dot(left, weight, preferred_element_type=jnp.float32...  237 us
    all_gather x4, blocking collectives, project_rows(): piece = lax.all_gather(normed, 'dp', axis=0, tiled=True)  124 us
    psum x1, waiting for transfers between devices, updates(): lax.psum(partial_value.astype(jnp.bfloat16), 'tensor').astype(jnp.float32)  34.9 us
    all_gather x4, blocking collectives, combined_all(): everything = jax.tree.map(lambda part: lax.all_gather(part, axis), x)  22.4 us
    dot_general x4, matrix products, reduce_rows(): jnp.dot(left, weight, preferred_element_type=jnp.float32)  17.9 us
    psum x1, blocking collectives, project_step(): summed = lax.psum(partial_value, 'tensor').astype(jnp.bfloat16)  17 us
    dot_general x8, matrix products, project_rows(): jnp.dot(piece, weight, preferred_element_type=jnp.float32)  16.4 us
    psum x2, blocking collectives, normalize(): squares = lax.psum(jnp.sum(wide * wide, axis=1), 'tensor')  14 us
  transfers between devices with their start and end apart: 16, of which 13 were waited for; matrix products, arithmetic and copies ran while one was open for 6% of the time, Pallas kernels for 0%

commit v1 on v0

v1 whole, which is shorter than its diff:
```python
import functools
import math

import jax
import jax.numpy as jnp
import numpy as np
from jax import lax
from jax.experimental import pallas as pl
from jax.experimental.pallas import tpu as pltpu
from jax.sharding import PartitionSpec as P

KVH = 8
HD = 128
EPS = 1e-05
ROPE_BASE = 500000.0
MASKED = -1e30
BF16 = jnp.bfloat16
F32 = jnp.float32


def swap(x, axis, bits):
    size = lax.axis_size(axis)
    return lax.ppermute(x, axis, [(i, i ^ bits) for i in range(size)])


def rope_tables(position):
    half = HD // 2
    freq = np.power(np.float32(ROPE_BASE), -2.0 * np.arange(half, dtype=np.float32) / HD)
    angle = (np.float32(position) * freq.astype(np.float32)).astype(np.float32)
    cosine, sine = np.cos(angle), np.sin(angle)
    return (
        np.concatenate([cosine, cosine]).astype(np.float32),
        np.concatenate([-sine, sine]).astype(np.float32),
    )


def gather_rows(rows):
    groups = lax.axis_size("dp")
    return jnp.stack([rows] + [swap(rows, "dp", k) for k in range(1, groups)])


def split_ss(x):
    high = x.astype(BF16)
    low = (x - high.astype(F32)).astype(BF16)
    return jnp.pad(jnp.stack([high, low], axis=-1), ((0, 0), (0, 126)))


def scale_of(summed, width):
    return lax.rsqrt((summed[..., 0] + summed[..., 1]) / width + EPS)[..., None]


def attention_kernel(
    sizes, own_ref, anc_ref, q_ref, scale_ref, kv_ref, nk_ref, nv_ref, target_ref, rope_ref, out_ref, keys_ref, values_ref
):
    parts, part_dev, heads, tensor, span = sizes
    ctx = tensor * span
    scale = 1.0 / math.sqrt(HD)
    queries = q_ref[...] * scale_ref[...]
    blocks = parts // part_dev
    rows = heads * parts
    pieces = []
    cos_key = jnp.concatenate([jnp.broadcast_to(rope_ref[2 * s : 2 * s + 1, :], (part_dev, HD)) for s in range(2)])
    sin_key = jnp.concatenate([jnp.broadcast_to(rope_ref[2 * s + 1 : 2 * s + 2, :], (part_dev, HD)) for s in range(2)])
    groups = nk_ref.shape[0] // (2 * part_dev)
    new_keys = nk_ref[...].astype(F32).reshape(groups, 2 * part_dev, HD)
    turned = pltpu.roll(nk_ref[...].astype(F32), HD // 2, 1).reshape(groups, 2 * part_dev, HD)
    new_keys = (new_keys * cos_key[None] + turned * sin_key[None]).reshape(-1, HD).astype(BF16)
    new_values = nv_ref[...]
    for step in range(2):
        source = own_ref if step == 0 else anc_ref

        def bring(i, _, source=source):
            particle = source[i]
            for t in range(tensor):
                both = kv_ref[t, particle].astype(F32)
                start = pl.multiple_of(i * ctx + t * span, 8)
                keys_ref[pl.ds(start, span), :] = both[:span]
                values_ref[pl.ds(start, span), :] = both[span:]
            return 0

        lax.fori_loop(0, parts, bring, 0)
        keys = keys_ref[...].astype(BF16)
        values = values_ref[...].astype(BF16)
        cosine = rope_ref[2 * step : 2 * step + 1, :]
        sine = rope_ref[2 * step + 1 : 2 * step + 2, :]
        per_head = []
        for h in range(heads):
            for b in range(blocks):
                first = b * 2 * part_dev + step * part_dev
                per_head.append(queries[first : first + part_dev, h * HD : (h + 1) * HD])
        query = jnp.concatenate(per_head, axis=0)
        query = query.astype(BF16).astype(F32)
        query = (query * cosine + pltpu.roll(query, HD // 2, 1) * sine).astype(BF16)
        contract = (((1,), (1,)), ((), ()))
        cached = lax.dot_general(query, keys, contract, preferred_element_type=F32) * scale
        fresh = lax.dot_general(query, new_keys, contract, preferred_element_type=F32) * scale
        row_part = lax.rem(lax.broadcasted_iota(jnp.int32, (rows, 1), 0), parts)
        col_part = lax.div(lax.broadcasted_iota(jnp.int32, (1, parts * ctx), 1), ctx)
        cached = jnp.where(row_part == col_part, cached, MASKED)
        col = lax.broadcasted_iota(jnp.int32, (1, new_keys.shape[0]), 1)
        wanted = col == target_ref[:, step : step + 1]
        if step == 1:
            wanted = wanted | (col == target_ref[:, 2:3])
        fresh = jnp.where(wanted, fresh, MASKED)
        highest = jnp.maximum(jnp.max(cached, axis=1, keepdims=True), jnp.max(fresh, axis=1, keepdims=True))
        cached = jnp.exp(cached - highest)
        fresh = jnp.exp(fresh - highest)
        total = jnp.sum(cached, axis=1, keepdims=True) + jnp.sum(fresh, axis=1, keepdims=True)
        mixed = jnp.dot(cached.astype(BF16), values, preferred_element_type=F32)
        mixed += jnp.dot(fresh.astype(BF16), new_values, preferred_element_type=F32)
        pieces.append(mixed / total)
    for h in range(heads):
        for b in range(blocks):
            first = h * parts + b * part_dev
            both = jnp.concatenate([piece[first : first + part_dev] for piece in pieces], axis=0)
            out_ref[b * 2 * part_dev : (b + 1) * 2 * part_dev, h * HD : (h + 1) * HD] = both.astype(BF16)


def attention(own, anc, q, scale, kv, nk, nv, targets, rope, part_dev):
    parts = own.shape[0]
    heads = q.shape[1] // HD
    tensor, _, span2, _ = kv.shape
    span = span2 // 2
    ctx = tensor * span
    smem = pl.BlockSpec(memory_space=pltpu.SMEM)
    vmem = pl.BlockSpec(memory_space=pltpu.VMEM)
    return pl.pallas_call(
        functools.partial(attention_kernel, (parts, part_dev, heads, tensor, span)),
        out_shape=jax.ShapeDtypeStruct((q.shape[0], q.shape[1]), BF16),
        in_specs=[smem, smem] + [vmem] * 7,
        out_specs=vmem,
        scratch_shapes=[pltpu.VMEM((parts * ctx, HD), F32), pltpu.VMEM((parts * ctx, HD), F32)],
        compiler_params=pltpu.CompilerParams(vmem_limit_bytes=40 << 20),
        cost_estimate=pl.CostEstimate(flops=100 << 20, bytes_accessed=2 << 20, transcendentals=1 << 18),
    )(own, anc, q, scale, kv, nk, nv, targets, rope)


def local(
    x_first,
    x_second,
    cache_keys,
    cache_values,
    ancestors,
    attn_gain,
    ffn_gain,
    w_query,
    w_keyval,
    w_out,
    w_gate,
    w_up,
    w_down,
):
    groups = lax.axis_size("dp")
    tensor = lax.axis_size("tensor")
    part_dev, features = x_first.shape
    span = cache_keys.shape[1]
    width = features * tensor
    context = span * tensor
    d = lax.axis_index("dp")
    t = lax.axis_index("tensor")
    pair = 2 * part_dev
    near = groups // tensor

    heads_of = np.arange(groups) * KVH // groups
    both = jnp.concatenate(
        [
            cache_keys.reshape(part_dev, span, KVH, HD),
            cache_values.reshape(part_dev, span, KVH, HD),
        ],
        axis=1,
    )
    sent = jnp.stack([both[:, :, h] for h in heads_of])
    cache = lax.all_to_all(sent, "dp", split_axis=0, concat_axis=0, tiled=True)
    cache = lax.all_gather(cache.reshape(groups * part_dev, 2 * span, HD), "tensor", axis=0)

    x = jnp.concatenate([x_first, x_second], axis=0)
    rows = gather_rows(x).reshape(groups * pair, features)
    wide = rows.astype(F32)
    squares = split_ss(jnp.sum(wide * wide, axis=1))
    lifted = (wide * attn_gain[None, :]).astype(BF16)
    kv_part = jnp.dot(lifted, w_keyval, preferred_element_type=F32).astype(BF16)
    kv_part = jnp.concatenate([kv_part, squares], axis=1)
    q_part = jnp.dot(lifted, w_query, preferred_element_type=F32).astype(BF16)
    q_part = q_part.reshape(tensor, near * pair, -1)
    kv_sum = kv_part.astype(F32)
    for k in range(1, tensor):
        kv_sum = kv_sum + swap(kv_part, "tensor", k).astype(F32)
    kv_cols = w_keyval.shape[1]
    scale = scale_of(kv_sum[:, kv_cols:], width)
    keyvals = (kv_sum[:, :kv_cols] * scale).astype(BF16).reshape(groups, pair, kv_cols)
    keyvals = jnp.take(keyvals, jnp.arange(groups) ^ d, axis=0).reshape(groups * pair, kv_cols)
    if groups == KVH:
        halves = (keyvals[:, :HD], keyvals[:, HD:])
        half = groups // 2
        lower = d < half
        one = lax.ppermute(
            jnp.where(lower, halves[0], halves[1]),
            "dp",
            [(i, 2 * i) for i in range(half)] + [(half + i, 2 * i + 1) for i in range(half)],
        )
        two = lax.ppermute(
            jnp.where(lower, halves[1], halves[0]),
            "dp",
            [(i, 2 * i + 1) for i in range(half)] + [(half + i, 2 * i) for i in range(half)],
        )
        even = d % 2 == 0
        new_keys = jnp.where(even, one, two)
        new_values = jnp.where(even, two, one)
    else:
        every = lax.all_gather(keyvals, "dp", axis=1, tiled=True)
        start = (d * KVH // groups) * HD
        new_keys = lax.dynamic_slice_in_dim(every, start, HD, axis=1)
        new_values = lax.dynamic_slice_in_dim(every, KVH * HD + start, HD, axis=1)

    queries = lax.dynamic_index_in_dim(q_part, t, 0, keepdims=False).astype(F32)
    for k in range(1, tensor):
        piece = lax.dynamic_index_in_dim(q_part, t ^ k, 0, keepdims=False)
        queries = queries + swap(piece, "tensor", k).astype(F32)
    own_scale = lax.dynamic_slice_in_dim(scale, t * near * pair, near * pair, axis=0)

    own_blocks = (t * near + jnp.arange(near)) ^ d
    own = (own_blocks[:, None] * part_dev + jnp.arange(part_dev)[None, :]).reshape(-1).astype(jnp.int32)
    anc = jnp.take(ancestors, own, axis=0)
    heads = w_query.shape[1] // HD

    def row_of(particle, step):
        return (particle // part_dev) * pair + step * part_dev + particle % part_dev

    targets = jnp.stack([row_of(own, 0), row_of(anc, 0), row_of(own, 1)], axis=1)
    targets = jnp.tile(targets, (heads, 1)).astype(jnp.int32)
    rope = jnp.asarray(np.stack(rope_tables(context) + rope_tables(context + 1)))
    mixed = attention(own, anc, queries, own_scale, cache, new_keys, new_values, targets, rope, part_dev)

    def gather_near(block, order):
        blocks = jnp.stack([block] + [swap(block, "tensor", k) for k in range(1, tensor)])
        return jnp.take(blocks.reshape(groups, pair, -1), order, axis=0).reshape(groups * pair, -1)

    def stacked(k):
        return ((k // near) ^ t) * near + k % near

    relative = jnp.arange(groups)
    spread = gather_near(mixed, stacked(relative ^ d))
    out_part = jnp.dot(spread, w_out, preferred_element_type=F32).astype(BF16)
    arrived = lax.all_to_all(out_part.reshape(groups, pair, -1), "dp", split_axis=0, concat_axis=0, tiled=True)
    attn_part = jnp.sum(arrived.astype(F32), axis=0).astype(BF16)
    residual = (x.astype(F32) + attn_part.astype(F32)).astype(BF16)

    rows = gather_rows(residual).reshape(groups * pair, features)
    wide = rows.astype(F32)
    squares = split_ss(jnp.sum(wide * wide, axis=1))
    lifted = (wide * ffn_gain[None, :]).astype(BF16)
    gate = jnp.dot(lifted, w_gate, preferred_element_type=F32).astype(BF16)
    up = jnp.dot(lifted, w_up, preferred_element_type=F32).astype(BF16)
    hidden_cols = w_gate.shape[1]
    part = jnp.concatenate([gate, up, squares], axis=1).reshape(tensor, near * pair, -1)
    summed = lax.dynamic_index_in_dim(part, t, 0, keepdims=False).astype(F32)
    for k in range(1, tensor):
        piece = lax.dynamic_index_in_dim(part, t ^ k, 0, keepdims=False)
        summed = summed + swap(piece, "tensor", k).astype(F32)
    scale = scale_of(summed[:, 2 * hidden_cols :], width)
    hidden = jax.nn.silu(summed[:, :hidden_cols] * scale) * (summed[:, hidden_cols : 2 * hidden_cols] * scale)
    spread = gather_near(hidden.astype(BF16), stacked(relative))
    down = jnp.dot(spread, w_down, preferred_element_type=F32).astype(BF16).reshape(groups, pair, -1)
    total = down[0].astype(F32)
    for k in range(1, groups):
        total = total + swap(down[k], "dp", k).astype(F32)
    ffn_part = total.astype(BF16)
    return (attn_part.reshape(2, part_dev, features), ffn_part.reshape(2, part_dev, features))


def solution(mesh):
    return jax.shard_map(
        local,
        mesh=mesh,
        in_specs=(
            P("dp", "tensor"),
            P("dp", "tensor"),
            P("dp", "tensor", None),
            P("dp", "tensor", None),
            P(),
            P("tensor"),
            P("tensor"),
            P("tensor", "dp"),
            P("tensor", "dp"),
            P("dp", "tensor"),
            P("tensor", "dp"),
            P("tensor", "dp"),
            P("dp", "tensor"),
        ),
        out_specs=(P(None, "dp", "tensor"), P(None, "dp", "tensor")),
        check_vma=False,
    )
```

time: 618 us -> 176 us (0.28)
  waiting for transfers between devices: 315 us -> 43.2 us
  blocking collectives: 177 us -> 20.1 us
  matrix products: 38.1 us -> 16.1 us
  starting transfers between devices: 38.4 us -> 56.4 us
  other arithmetic: 21.8 us -> 13.9 us
    reduce_scatter x4 -> x0, waiting for transfers between devices: 237 us -> none  [reduce_rows(): lax.psum_scatter(jnp.dot(left, weight, preferred_element_type=jnp.float32...]
    all_gather x8 -> x0, blocking collectives: 146 us -> none  [the longest x4 124 us: project_rows(): piece = lax.all_gather(normed, 'dp', axis=0, tiled=True)]
    ppermute x0 -> x38, starting transfers between devices: none -> 51.5 us  [the longest x36 46.6 us: swap(): return lax.ppermute(x, axis, [(i, i ^ bits) for i in range(size)])]
    ppermute x0 -> x38, waiting for transfers between devices: none -> 43.1 us  [the longest x36 40.2 us: swap(): return lax.ppermute(x, axis, [(i, i ^ bits) for i in range(size)])]
    all_to_all x9 -> x1, waiting for transfers between devices: 37.7 us -> 0.01 us  [local(): cache = lax.all_to_all(sent, 'dp', split_axis=0, concat_axis=0, tiled=True)]
    psum x1 -> x0, waiting for transfers between devices: 34.9 us -> none  [updates(): lax.psum(partial_value.astype(jnp.bfloat16), 'tensor').astype(jnp.float32)]
    all_to_all x9 -> x1, starting transfers between devices: 37.9 us -> 4.88 us  [local(): cache = lax.all_to_all(sent, 'dp', split_axis=0, concat_axis=0, tiled=True)]
    psum x3 -> x0, blocking collectives: 31 us -> none  [the longest x1 17 us: project_step(): summed = lax.psum(partial_value, 'tensor').astype(jnp.bfloat16)]
  transfers between devices with their start and end apart: 16 -> 40, of which waited for: 13 -> 17; matrix products, arithmetic and copies ran while one was open for 6% -> 10% of each run, Pallas kernels for 0% -> 0%
where the time goes in v1:
time: 176 us; the launch traced here: 175 us
  starting transfers between devices  56.4 us (32%)
  waiting for transfers between devices  43.2 us (25%)
  blocking collectives  20.1 us (11%)
  matrix products  16.1 us (9%)
  between operations  14.7 us (8%)
  other arithmetic  13.9 us (8%)
  local copies, waits for them, and re-layouts  8.77 us (5%)
  Pallas kernels  1.9 us (1%)
    ppermute x36, starting transfers between devices, swap(): return lax.ppermute(x, axis, [(i, i ^ bits) for i in range(size)])  46.6 us
    ppermute x36, waiting for transfers between devices, swap(): return lax.ppermute(x, axis, [(i, i ^ bits) for i in range(size)])  40.2 us
    all_to_all x1, blocking collectives, local(): lax.all_to_all(out_part.reshape(groups, pair, -1), 'dp', split_axis=0, co...  20.1 us
    unnamed x9, other arithmetic  9.48 us
    all_to_all x1, starting transfers between devices, local(): cache = lax.all_to_all(sent, 'dp', split_axis=0, concat_axis=0, tiled=True)  4.88 us
    dot_general x1, matrix products, local(): up = jnp.dot(lifted, w_up, preferred_element_type=F32).astype(BF16)  4.38 us
    dot_general x1, matrix products, local(): jnp.dot(spread, w_down, preferred_element_type=F32).astype(BF16)  4.31 us
    ppermute x1, starting transfers between devices, local(): lax.ppermute(jnp.where(lower, halves[1], halves[0]), 'dp', [(i, 2 * i + 1...  4.3 us
  transfers between devices with their start and end apart: 40, of which 17 were waited for; matrix products, arithmetic and copies ran while one was open for 10% of the time, Pallas kernels for 0%

profile of v1, /device:TPU:0, one launch (start us, length us, event | category | flops | bytes accessed | tf_op | source)
XLA Modules:
  0.0 175.0 jit_solution(11410072829744422622)
XLA Ops:
  7.2 0.9 constant_dynamic-update-slice_fusion.1
  8.0 0.8 constant_dynamic-update-slice_fusion
  8.8 2.9 %collective-permute-start = (bf16[16,2048]{1,0:T(8,128)(2,1)S(1)}, bf16[16,2048]{1,0:T(8,128)(2,1)S(1)}, u32[]{:S(2)}, u32[]{:S(2)}) collective-permute-start(bf16[16,2048]{1,0:T(8,128)(2,1)S(1)} %constant_dynamic-update-slice_fusion), channel_id=1, source_target_pairs={{0,4},{4,0},{8,12},{12,8},{16,20},{20,16},{24,28},{28,24},{1,5},{5... | collective-permute-start | bytes 196616 | tf_op jit(solution)/shard_map/ppermute | solution.py:23
  11.7 1.6 collective-permute-start.1
  13.3 3.0 %collective-permute-start.3 = (bf16[16,2048]{1,0:T(8,128)(2,1)S(1)}, bf16[16,2048]{1,0:T(8,128)(2,1)S(1)}, u32[]{:S(2)}, u32[]{:S(2)}) collective-permute-start(bf16[16,2048]{1,0:T(8,128)(2,1)S(1)} %constant_dynamic-update-slice_fusion), channel_id=1, source_target_pairs={{0,16},{4,20},{8,24},{12,28},{16,0},{20,4},{24,8},{28,12},{1,17},{... | collective-permute-start | bytes 196616 | tf_op jit(solution)/shard_map/ppermute | solution.py:23
  16.3 1.3 collective-permute-start.4
  17.6 1.4 constant_dynamic-update-slice_fusion.9
  18.9 1.4 constant_dynamic-update-slice_fusion.8
  20.3 1.4 constant_dynamic-update-slice_fusion.7
  21.7 1.3 constant_dynamic-update-slice_fusion.6
  23.0 1.4 constant_dynamic-update-slice_fusion.5
  24.4 1.3 constant_dynamic-update-slice_fusion.4
  25.7 1.4 constant_dynamic-update-slice_fusion.3
  27.1 1.4 constant_dynamic-update-slice_fusion.2
  28.4 4.9 %all-to-all-start = ((bf16[8,8,16,128]{3,2,1,0:T(8,128)(2,1)}), bf16[8,8,16,128]{3,2,1,0:T(8,128)(2,1)S(1)}, u32[]{:S(2)}, u32[]{:S(2)}) async-start(bf16[8,8,16,128]{3,2,1,0:T(8,128)(2,1)} %constant_dynamic-update-slice_fusion.2), calls=%async_computation | async-start | bytes 524288 | tf_op jit(solution)/shard_map/all_to_all | solution.py:173
  33.9 1.3 gather_fusion
  35.5 3.8 %collective-permute-start.5 = (bf16[16,2048]{1,0:T(8,128)(2,1)S(1)}, bf16[16,2048]{1,0:T(8,128)(2,1)S(1)}, u32[]{:S(2)}, u32[]{:S(2)}) collective-permute-start(bf16[16,2048]{1,0:T(8,128)(2,1)S(1)} %constant_dynamic-update-slice_fusion), channel_id=1, source_target_pairs={{0,24},{4,28},{8,16},{12,20},{16,8},{20,12},{24,0},{28,4},{1,25},{... | collective-permute-start | bytes 196616 | tf_op jit(solution)/shard_map/ppermute | solution.py:23
  39.4 1.5 collective-permute-start.6
  41.0 0.7 collective-permute-done.5
  41.7 4.8 %collective-permute-done.6 = bf16[16,2048]{1,0:T(8,128)(2,1)S(1)} collective-permute-done((bf16[16,2048]{1,0:T(8,128)(2,1)S(1)}, bf16[16,2048]{1,0:T(8,128)(2,1)S(1)}, u32[]{:S(2)}, u32[]{:S(2)}) %collective-permute-start.6) | collective-permute-done | bytes 65568 | tf_op jit(solution)/shard_map/ppermute | solution.py:23
  47.1 3.0 %convolution_convert_fusion.4 = bf16[128,1024]{1,0:T(8,128)(2,1)S(1)} fusion(bf16[128,2048]{1,0:T(8,128)(2,1)S(1)} %fusion.2, bf16[2048,1024]{1,0:T(8,128)(2,1)} %param.21), kind=kOutput, calls=%fused_computation.10 | convolution fusion | flops 537001984 | bytes 4980736 | tf_op jit(solution)/shard_map/dot_general | solution.py:183
  50.1 1.6 collective-permute-start.8
  52.8 1.5 collective-permute-start.11
  54.3 0.7 copy-done.3
  55.8 2.5 %collective-permute-done.11 = bf16[128,384]{1,0:T(8,128)(2,1)S(1)} collective-permute-done((bf16[128,384]{1,0:T(8,128)(2,1)S(1)}, bf16[128,384]{1,0:T(8,128)(2,1)S(1)}, u32[]{:S(2)}, u32[]{:S(2)}) %collective-permute-start.11) | collective-permute-done | bytes 98336 | tf_op jit(solution)/shard_map/ppermute | solution.py:23
  58.3 1.9 %collective-permute-done.12 = bf16[128,384]{1,0:T(8,128)(2,1)S(1)} collective-permute-done((bf16[128,384]{1,0:T(8,128)(2,1)S(1)}, bf16[128,384]{1,0:T(8,128)(2,1)S(1)}, u32[]{:S(2)}, u32[]{:S(2)}) %collective-permute-start.12) | collective-permute-done | bytes 98336 | tf_op jit(solution)/shard_map/ppermute | solution.py:23
  61.9 4.3 %collective-permute-start.14 = (bf16[128,128]{1,0:T(8,128)(2,1)S(1)}, bf16[128,128]{1,0:T(8,128)(2,1)S(1)}, u32[]{:S(2)}, u32[]{:S(2)}) collective-permute-start(bf16[128,128]{1,0:T(8,128)(2,1)S(1)} %get-tuple-element.22), channel_id=1, source_target_pairs={{0,4},{4,12},{8,20},{12,28},{16,0},{20,8},{24,16},{28,24},{1,5},{5... | collective-permute-start | bytes 98312 | tf_op jit(solution)/shard_map/ppermute | solution.py:201
  66.2 3.0 %collective-permute-done.14 = bf16[128,128]{1,0:T(8,128)(2,1)S(1)} collective-permute-done((bf16[128,128]{1,0:T(8,128)(2,1)S(1)}, bf16[128,128]{1,0:T(8,128)(2,1)S(1)}, u32[]{:S(2)}, u32[]{:S(2)}) %collective-permute-start.14) | collective-permute-done | bytes 32800 | tf_op jit(solution)/shard_map/ppermute | solution.py:201
  69.3 1.2 copy-done.1
  70.5 1.9 %shard_map.149 = bf16[32,1024]{1,0:T(8,128)(2,1)S(1)} custom-call(s32[16]{0:T(128)S(1)} %add.410.own_ref, s32[16]{0:T(128)S(1)} %and_select_fusion.11.anc_ref, f32[32,1024]{1,0:T(8,128)S(1)} %fusion.14.q_ref, f32[32,1]{1,0:T(8,128)S(1)} %constant_dynamic-slice_fusion.scale_ref, bf16[4,64,16,128]{3,2,1,0:T(8,128)(2,1)S(1)} %copy-done.1, ...), custom_call_target="tpu_custom_call" | custom-call | flops 104857600 | bytes 2097152 | tf_op jit(solution)/shard_map/pallas_call | solution.py:127
  72.6 1.0 collective-permute-start.16
  74.3 3.1 %collective-permute-done.16 = bf16[32,1024]{1,0:T(8,128)(2,1)S(1)} collective-permute-done((bf16[32,1024]{1,0:T(8,128)(2,1)S(1)}, bf16[32,1024]{1,0:T(8,128)(2,1)S(1)}, u32[]{:S(2)}, u32[]{:S(2)}) %collective-permute-start.16) | collective-permute-done | bytes 65568 | tf_op jit(solution)/shard_map/ppermute | solution.py:23
  78.7 2.9 %convolution_convert_fusion.3 = bf16[128,2048]{1,0:T(8,128)(2,1)S(1)} fusion(bf16[128,1024]{1,0:T(8,128)(2,1)S(1)} %bitcast_select_fusion.1, bf16[1024,2048]{1,0:T(8,128)(2,1)} %param.23), kind=kOutput, calls=%fused_computation.7 | convolution fusion | flops 537133056 | bytes 4980736 | tf_op jit(solution)/shard_map/dot_general | solution.py:243
  81.6 20.1 %all_to_all.10 = bf16[8,16,2048]{2,1,0:T(8,128)(2,1)S(1)} all-to-all(bf16[8,16,2048]{2,1,0:T(8,128)(2,1)S(1)} %bitcast.174), channel_id=1, replica_groups=mesh['dp'=8,'tensor'=4] {'dp'}, dimensions={0} | all-to-all | bytes 1048576 | tf_op jit(solution)/shard_map/all_to_all | solution.py:244
  101.9 1.5 collective-permute-start.18
  103.4 2.0 %collective-permute-start.20 = (bf16[16,2048]{1,0:T(8,128)(2,1)S(1)}, bf16[16,2048]{1,0:T(8,128)(2,1)S(1)}, u32[]{:S(2)}, u32[]{:S(2)}) collective-permute-start(bf16[16,2048]{1,0:T(8,128)(2,1)S(1)} %fusion.11), channel_id=1, source_target_pairs={{0,12},{4,8},{8,4},{12,0},{16,28},{20,24},{24,20},{28,16},{1,13},{... | collective-permute-start | bytes 196616 | tf_op jit(solution)/shard_map/ppermute | solution.py:23
  105.4 0.8 collective-permute-start.21
  106.3 3.0 %collective-permute-start.22 = (bf16[16,2048]{1,0:T(8,128)(2,1)S(1)}, bf16[16,2048]{1,0:T(8,128)(2,1)S(1)}, u32[]{:S(2)}, u32[]{:S(2)}) collective-permute-start(bf16[16,2048]{1,0:T(8,128)(2,1)S(1)} %fusion.11), channel_id=1, source_target_pairs={{0,20},{4,16},{8,28},{12,24},{16,4},{20,0},{24,12},{28,8},{1,21},{... | collective-permute-start | bytes 196616 | tf_op jit(solution)/shard_map/ppermute | solution.py:23
  109.3 1.5 collective-permute-start.23
  110.8 2.4 %collective-permute-start.24 = (bf16[16,2048]{1,0:T(8,128)(2,1)S(1)}, bf16[16,2048]{1,0:T(8,128)(2,1)S(1)}, u32[]{:S(2)}, u32[]{:S(2)}) collective-permute-start(bf16[16,2048]{1,0:T(8,128)(2,1)S(1)} %fusion.11), channel_id=1, source_target_pairs={{0,28},{4,24},{8,20},{12,16},{16,12},{20,8},{24,4},{28,0},{1,29},{... | collective-permute-start | bytes 196616 | tf_op jit(solution)/shard_map/ppermute | solution.py:23
  113.3 1.5 collective-permute-done.21
  114.8 2.4 %collective-permute-done.22 = bf16[16,2048]{1,0:T(8,128)(2,1)S(1)} collective-permute-done((bf16[16,2048]{1,0:T(8,128)(2,1)S(1)}, bf16[16,2048]{1,0:T(8,128)(2,1)S(1)}, u32[]{:S(2)}, u32[]{:S(2)}) %collective-permute-start.22) | collective-permute-done | bytes 65568 | tf_op jit(solution)/shard_map/ppermute | solution.py:23
  117.2 0.7 collective-permute-done.24
  118.3 4.4 %convolution_convert_fusion.1 = bf16[128,1792]{1,0:T(8,128)(2,1)S(1)} fusion(bf16[128,2048]{1,0:T(8,128)(2,1)S(1)} %fusion.1, bf16[2048,1792]{1,0:T(8,128)(2,1)} %param.25), kind=kOutput, calls=%fused_computation.5 | convolution fusion | flops 939753472 | bytes 8323072 | tf_op jit(solution)/shard_map/dot_general | solution.py:253
  122.7 0.8 slice-done.1
  123.4 1.2 convolution_convert_fusion.2
  125.1 0.9 collective-permute-start.26
  126.0 0.9 collective-permute-start.27
  127.2 6.6 %collective-permute-done.26 = bf16[32,3712]{1,0:T(8,128)(2,1)S(1)} collective-permute-done((bf16[32,3712]{1,0:T(8,128)(2,1)S(1)}, bf16[32,3712]{1,0:T(8,128)(2,1)S(1)}, u32[]{:S(2)}, u32[]{:S(2)}) %collective-permute-start.26) | collective-permute-done | bytes 237600 | tf_op jit(solution)/shard_map/ppermute | solution.py:23
  133.7 4.2 %collective-permute-done.27 = bf16[32,3712]{1,0:T(8,128)(2,1)S(1)} collective-permute-done((bf16[32,3712]{1,0:T(8,128)(2,1)S(1)}, bf16[32,3712]{1,0:T(8,128)(2,1)S(1)}, u32[]{:S(2)}, u32[]{:S(2)}) %collective-permute-start.27) | collective-permute-done | bytes 237600 | tf_op jit(solution)/shard_map/ppermute | solution.py:23
  138.7 0.9 collective-permute-start.29
  139.6 0.7 collective-permute-start.30
  140.5 4.2 %collective-permute-done.29 = bf16[32,1792]{1,0:T(8,128)(2,1)S(1)} collective-permute-done((bf16[32,1792]{1,0:T(8,128)(2,1)S(1)}, bf16[32,1792]{1,0:T(8,128)(2,1)S(1)}, u32[]{:S(2)}, u32[]{:S(2)}) %collective-permute-start.29) | collective-permute-done | bytes 114720 | tf_op jit(solution)/shard_map/ppermute | solution.py:23
  144.7 1.1 collective-permute-done.30
  146.6 4.3 %convolution_convert_fusion = bf16[128,2048]{1,0:T(8,128)(2,1)S(1)} fusion(bf16[128,1792]{1,0:T(8,128)(2,1)S(1)} %bitcast_select_fusion, bf16[1792,2048]{1,0:T(8,128)(2,1)} %param.26), kind=kOutput, calls=%fused_computation.4 | convolution fusion | flops 939786240 | bytes 8323072 | tf_op jit(solution)/shard_map/dot_general | solution.py:263
  150.9 1.1 collective-permute-start.31
  152.0 1.9 %collective-permute-start.32 = (bf16[16,2048]{1,0:T(8,128)(2,1)S(1)}, bf16[16,2048]{1,0:T(8,128)(2,1)S(1)}, u32[]{:S(2)}, u32[]{:S(2)}) collective-permute-start(bf16[16,2048]{1,0:T(8,128)(2,1)S(1)} %get-tuple-element.16), channel_id=1, source_target_pairs={{0,8},{4,12},{8,0},{12,4},{16,24},{20,28},{24,16},{28,20},{1,9},{5... | collective-permute-start | bytes 196616 | tf_op jit(solution)/shard_map/ppermute | solution.py:23
  153.9 0.7 collective-permute-start.33
  154.6 2.7 %collective-permute-start.34 = (bf16[16,2048]{1,0:T(8,128)(2,1)S(1)}, bf16[16,2048]{1,0:T(8,128)(2,1)S(1)}, u32[]{:S(2)}, u32[]{:S(2)}) collective-permute-start(bf16[16,2048]{1,0:T(8,128)(2,1)S(1)} %get-tuple-element.14), channel_id=1, source_target_pairs={{0,16},{4,20},{8,24},{12,28},{16,0},{20,4},{24,8},{28,12},{1,17},{... | collective-permute-start | bytes 196616 | tf_op jit(solution)/shard_map/ppermute | solution.py:23
  157.8 1.9 %collective-permute-start.36 = (bf16[16,2048]{1,0:T(8,128)(2,1)S(1)}, bf16[16,2048]{1,0:T(8,128)(2,1)S(1)}, u32[]{:S(2)}, u32[]{:S(2)}) collective-permute-start(bf16[16,2048]{1,0:T(8,128)(2,1)S(1)} %get-tuple-element.12), channel_id=1, source_target_pairs={{0,24},{4,28},{8,16},{12,20},{16,8},{20,12},{24,0},{28,4},{1,25},{... | collective-permute-start | bytes 196616 | tf_op jit(solution)/shard_map/ppermute | solution.py:23
  159.8 2.5 %collective-permute-start.37 = (bf16[16,2048]{1,0:T(8,128)(2,1)S(1)}, bf16[16,2048]{1,0:T(8,128)(2,1)S(1)}, u32[]{:S(2)}, u32[]{:S(2)}) collective-permute-start(bf16[16,2048]{1,0:T(8,128)(2,1)S(1)} %get-tuple-element.11), channel_id=1, source_target_pairs={{0,28},{4,24},{8,20},{12,16},{16,12},{20,8},{24,4},{28,0},{1,29},{... | collective-permute-start | bytes 196616 | tf_op jit(solution)/shard_map/ppermute | solution.py:23
  162.3 2.9 %collective-permute-done.34 = bf16[16,2048]{1,0:T(8,128)(2,1)S(1)} collective-permute-done((bf16[16,2048]{1,0:T(8,128)(2,1)S(1)}, bf16[16,2048]{1,0:T(8,128)(2,1)S(1)}, u32[]{:S(2)}, u32[]{:S(2)}) %collective-permute-start.34) | collective-permute-done | bytes 65568 | tf_op jit(solution)/shard_map/ppermute | solution.py:23
  165.2 2.3 %collective-permute-done.35 = bf16[16,2048]{1,0:T(8,128)(2,1)S(1)} collective-permute-done((bf16[16,2048]{1,0:T(8,128)(2,1)S(1)}, bf16[16,2048]{1,0:T(8,128)(2,1)S(1)}, u32[]{:S(2)}, u32[]{:S(2)}) %collective-permute-start.35) | collective-permute-done | bytes 65568 | tf_op jit(solution)/shard_map/ppermute | solution.py:23
  167.5 0.7 fusion.16
  (139 shorter events, 10.5 us)
Async XLA Ops:
  7.2 44.8 %copy-start = (bf16[2048,256]{1,0:T(8,128)(2,1)S(1)}, bf16[2048,256]{1,0:T(8,128)(2,1)}, u32[]{:S(2)}) copy-start(bf16[2048,256]{1,0:T(8,128)(2,1)} %param.22) | copy-start | bytes 3145732
  7.2 39.8 %copy-start.7 = (f32[2048]{0:T(1024)S(1)}, f32[2048]{0:T(1024)}, u32[]{:S(2)}) copy-start(f32[2048]{0:T(1024)} %param.19) | copy-start | bytes 24580
  8.8 26.7 %collective-permute-start = (bf16[16,2048]{1,0:T(8,128)(2,1)S(1)}, bf16[16,2048]{1,0:T(8,128)(2,1)S(1)}, u32[]{:S(2)}, u32[]{:S(2)}) collective-permute-start(bf16[16,2048]{1,0:T(8,128)(2,1)S(1)} %constant_dynamic-update-slice_fusion), channel_id=1, source_target_pairs={{0,4},{4,0},{8,12},{12,8},{16,20},{20,16},{24,28},{28,24},{1,5},{5... | collective-permute-start | bytes 196616 | tf_op jit(solution)/shard_map/ppermute | solution.py:23
  11.7 27.6 %collective-permute-start.1 = (bf16[16,2048]{1,0:T(8,128)(2,1)S(1)}, bf16[16,2048]{1,0:T(8,128)(2,1)S(1)}, u32[]{:S(2)}, u32[]{:S(2)}) collective-permute-start(bf16[16,2048]{1,0:T(8,128)(2,1)S(1)} %constant_dynamic-update-slice_fusion), channel_id=1, source_target_pairs={{0,8},{4,12},{8,0},{12,4},{16,24},{20,28},{24,16},{28,20},{1,9},{5... | collective-permute-start | bytes 196616 | tf_op jit(solution)/shard_map/ppermute | solution.py:23
  13.3 27.6 %collective-permute-start.2 = (bf16[16,2048]{1,0:T(8,128)(2,1)S(1)}, bf16[16,2048]{1,0:T(8,128)(2,1)S(1)}, u32[]{:S(2)}, u32[]{:S(2)}) collective-permute-start(bf16[16,2048]{1,0:T(8,128)(2,1)S(1)} %constant_dynamic-update-slice_fusion), channel_id=1, source_target_pairs={{0,12},{4,8},{8,4},{12,0},{16,28},{20,24},{24,20},{28,16},{1,13},{... | collective-permute-start | bytes 196616 | tf_op jit(solution)/shard_map/ppermute | solution.py:23
  13.3 27.6 %collective-permute-start.3 = (bf16[16,2048]{1,0:T(8,128)(2,1)S(1)}, bf16[16,2048]{1,0:T(8,128)(2,1)S(1)}, u32[]{:S(2)}, u32[]{:S(2)}) collective-permute-start(bf16[16,2048]{1,0:T(8,128)(2,1)S(1)} %constant_dynamic-update-slice_fusion), channel_id=1, source_target_pairs={{0,16},{4,20},{8,24},{12,28},{16,0},{20,4},{24,8},{28,12},{1,17},{... | collective-permute-start | bytes 196616 | tf_op jit(solution)/shard_map/ppermute | solution.py:23
  16.3 24.6 %collective-permute-start.4 = (bf16[16,2048]{1,0:T(8,128)(2,1)S(1)}, bf16[16,2048]{1,0:T(8,128)(2,1)S(1)}, u32[]{:S(2)}, u32[]{:S(2)}) collective-permute-start(bf16[16,2048]{1,0:T(8,128)(2,1)S(1)} %constant_dynamic-update-slice_fusion), channel_id=1, source_target_pairs={{0,20},{4,16},{8,28},{12,24},{16,4},{20,0},{24,12},{28,8},{1,21},{... | collective-permute-start | bytes 196616 | tf_op jit(solution)/shard_map/ppermute | solution.py:23
  28.4 25.9 %all-to-all-start = ((bf16[8,8,16,128]{3,2,1,0:T(8,128)(2,1)}), bf16[8,8,16,128]{3,2,1,0:T(8,128)(2,1)S(1)}, u32[]{:S(2)}, u32[]{:S(2)}) async-start(bf16[8,8,16,128]{3,2,1,0:T(8,128)(2,1)} %constant_dynamic-update-slice_fusion.2), calls=%async_computation | async-start | bytes 524288 | tf_op jit(solution)/shard_map/all_to_all | solution.py:173
  33.3 36.0 %all-gather.2.cloned.1.call-start = ((), (), s32[]{:S(2)}) async-start(), calls=%async_computation.2 | async-start | bytes 1310720 | tf_op jit(solution)/shard_map/all_gather | solution.py:174
  35.5 6.2 %collective-permute-start.5 = (bf16[16,2048]{1,0:T(8,128)(2,1)S(1)}, bf16[16,2048]{1,0:T(8,128)(2,1)S(1)}, u32[]{:S(2)}, u32[]{:S(2)}) collective-permute-start(bf16[16,2048]{1,0:T(8,128)(2,1)S(1)} %constant_dynamic-update-slice_fusion), channel_id=1, source_target_pairs={{0,24},{4,28},{8,16},{12,20},{16,8},{20,12},{24,0},{28,4},{1,25},{... | collective-permute-start | bytes 196616 | tf_op jit(solution)/shard_map/ppermute | solution.py:23
  39.4 7.1 %collective-permute-start.6 = (bf16[16,2048]{1,0:T(8,128)(2,1)S(1)}, bf16[16,2048]{1,0:T(8,128)(2,1)S(1)}, u32[]{:S(2)}, u32[]{:S(2)}) collective-permute-start(bf16[16,2048]{1,0:T(8,128)(2,1)S(1)} %constant_dynamic-update-slice_fusion), channel_id=1, source_target_pairs={{0,28},{4,24},{8,20},{12,16},{16,12},{20,8},{24,4},{28,0},{1,29},{... | collective-permute-start | bytes 196616 | tf_op jit(solution)/shard_map/ppermute | solution.py:23
  47.1 22.2 %copy-start.2 = (f32[4,128]{1,0:T(4,128)S(1)}, f32[4,128]{1,0:T(4,128)}, u32[]{:S(2)}) copy-start(f32[4,128]{1,0:T(4,128)} %constant.211.clone.rope_ref) | copy-start | bytes 6148
  50.1 4.9 %collective-permute-start.7 = (bf16[32,1024]{1,0:T(8,128)(2,1)S(1)}, bf16[32,1024]{1,0:T(8,128)(2,1)S(1)}, u32[]{:S(2)}, u32[]{:S(2)}) collective-permute-start(bf16[32,1024]{1,0:T(8,128)(2,1)S(1)} %get-tuple-element.17), channel_id=1, source_target_pairs={{0,1},{1,0},{2,3},{3,2},{4,5},{5,4},{6,7},{7,6},{8,9},{9,8},{10,11... | collective-permute-start | bytes 196616 | tf_op jit(solution)/shard_map/ppermute | solution.py:23
  50.1 5.0 %collective-permute-start.8 = (bf16[32,1024]{1,0:T(8,128)(2,1)S(1)}, bf16[32,1024]{1,0:T(8,128)(2,1)S(1)}, u32[]{:S(2)}, u32[]{:S(2)}) collective-permute-start(bf16[32,1024]{1,0:T(8,128)(2,1)S(1)} %get-tuple-element.19), channel_id=1, source_target_pairs={{0,2},{1,3},{2,0},{3,1},{4,6},{5,7},{6,4},{7,5},{8,10},{9,11},{10,... | collective-permute-start | bytes 196616 | tf_op jit(solution)/shard_map/ppermute | solution.py:23
  51.7 4.0 %collective-permute-start.9 = (bf16[32,1024]{1,0:T(8,128)(2,1)S(1)}, bf16[32,1024]{1,0:T(8,128)(2,1)S(1)}, u32[]{:S(2)}, u32[]{:S(2)}) collective-permute-start(bf16[32,1024]{1,0:T(8,128)(2,1)S(1)} %get-tuple-element.18), channel_id=1, source_target_pairs={{0,3},{1,2},{2,1},{3,0},{4,7},{5,6},{6,5},{7,4},{8,11},{9,10},{10,... | collective-permute-start | bytes 196616 | tf_op jit(solution)/shard_map/ppermute | solution.py:23
  52.3 3.5 %collective-permute-start.10 = (bf16[128,384]{1,0:T(8,128)(2,1)S(1)}, bf16[128,384]{1,0:T(8,128)(2,1)S(1)}, u32[]{:S(2)}, u32[]{:S(2)}) collective-permute-start(bf16[128,384]{1,0:T(8,128)(2,1)S(1)} %fusion.15), channel_id=1, source_target_pairs={{0,1},{1,0},{2,3},{3,2},{4,5},{5,4},{6,7},{7,6},{8,9},{9,8},{10,11... | collective-permute-start | bytes 294920 | tf_op jit(solution)/shard_map/ppermute | solution.py:23
  52.8 5.5 %collective-permute-start.11 = (bf16[128,384]{1,0:T(8,128)(2,1)S(1)}, bf16[128,384]{1,0:T(8,128)(2,1)S(1)}, u32[]{:S(2)}, u32[]{:S(2)}) collective-permute-start(bf16[128,384]{1,0:T(8,128)(2,1)S(1)} %fusion.15), channel_id=1, source_target_pairs={{0,2},{1,3},{2,0},{3,1},{4,6},{5,7},{6,4},{7,5},{8,10},{9,11},{10,... | collective-permute-start | bytes 294920 | tf_op jit(solution)/shard_map/ppermute | solution.py:23
  54.3 0.7 copy-start.3
  55.0 5.2 %collective-permute-start.12 = (bf16[128,384]{1,0:T(8,128)(2,1)S(1)}, bf16[128,384]{1,0:T(8,128)(2,1)S(1)}, u32[]{:S(2)}, u32[]{:S(2)}) collective-permute-start(bf16[128,384]{1,0:T(8,128)(2,1)S(1)} %fusion.15), channel_id=1, source_target_pairs={{0,3},{1,2},{2,1},{3,0},{4,7},{5,6},{6,5},{7,4},{8,11},{9,10},{10,... | collective-permute-start | bytes 294920 | tf_op jit(solution)/shard_map/ppermute | solution.py:23
  61.3 5.0 %collective-permute-start.13 = (bf16[128,128]{1,0:T(8,128)(2,1)S(1)}, bf16[128,128]{1,0:T(8,128)(2,1)S(1)}, u32[]{:S(2)}, u32[]{:S(2)}) collective-permute-start(bf16[128,128]{1,0:T(8,128)(2,1)S(1)} %get-tuple-element.23), channel_id=1, source_target_pairs={{0,0},{4,8},{8,16},{12,24},{16,4},{20,12},{24,20},{28,28},{1,1},{5... | collective-permute-start | bytes 98312 | tf_op jit(solution)/shard_map/ppermute | solution.py:196
  61.9 7.3 %collective-permute-start.14 = (bf16[128,128]{1,0:T(8,128)(2,1)S(1)}, bf16[128,128]{1,0:T(8,128)(2,1)S(1)}, u32[]{:S(2)}, u32[]{:S(2)}) collective-permute-start(bf16[128,128]{1,0:T(8,128)(2,1)S(1)} %get-tuple-element.22), channel_id=1, source_target_pairs={{0,4},{4,12},{8,20},{12,28},{16,0},{20,8},{24,16},{28,24},{1,5},{5... | collective-permute-start | bytes 98312 | tf_op jit(solution)/shard_map/ppermute | solution.py:201
  69.3 1.2 copy-start.1
  72.4 1.9 %collective-permute-start.15 = (bf16[32,1024]{1,0:T(8,128)(2,1)S(1)}, bf16[32,1024]{1,0:T(8,128)(2,1)S(1)}, u32[]{:S(2)}, u32[]{:S(2)}) collective-permute-start(bf16[32,1024]{1,0:T(8,128)(2,1)S(1)} %shard_map.149), channel_id=1, source_target_pairs={{0,1},{1,0},{2,3},{3,2},{4,5},{5,4},{6,7},{7,6},{8,9},{9,8},{10,11... | collective-permute-start | bytes 196616 | tf_op jit(solution)/shard_map/ppermute | solution.py:23
  72.6 4.8 %collective-permute-start.16 = (bf16[32,1024]{1,0:T(8,128)(2,1)S(1)}, bf16[32,1024]{1,0:T(8,128)(2,1)S(1)}, u32[]{:S(2)}, u32[]{:S(2)}) collective-permute-start(bf16[32,1024]{1,0:T(8,128)(2,1)S(1)} %shard_map.149), channel_id=1, source_target_pairs={{0,2},{1,3},{2,0},{3,1},{4,6},{5,7},{6,4},{7,5},{8,10},{9,11},{10,... | collective-permute-start | bytes 196616 | tf_op jit(solution)/shard_map/ppermute | solution.py:23
  73.7 4.3 %collective-permute-start.17 = (bf16[32,1024]{1,0:T(8,128)(2,1)S(1)}, bf16[32,1024]{1,0:T(8,128)(2,1)S(1)}, u32[]{:S(2)}, u32[]{:S(2)}) collective-permute-start(bf16[32,1024]{1,0:T(8,128)(2,1)S(1)} %shard_map.149), channel_id=1, source_target_pairs={{0,3},{1,2},{2,1},{3,0},{4,7},{5,6},{6,5},{7,4},{8,11},{9,10},{10,... | collective-permute-start | bytes 196616 | tf_op jit(solution)/shard_map/ppermute | solution.py:23
  78.0 31.3 %copy-start.5 = (bf16[8,2048]{1,0:T(8,128)(2,1)S(1)}, bf16[8,2048]{1,0:T(8,128)(2,1)}, u32[]{:S(2)}) copy-start(bf16[8,2048]{1,0:T(8,128)(2,1)} %param.14) | copy-start | bytes 98308
  78.0 31.3 %copy-start.6 = (bf16[8,2048]{1,0:T(8,128)(2,1)S(1)}, bf16[8,2048]{1,0:T(8,128)(2,1)}, u32[]{:S(2)}) copy-start(bf16[8,2048]{1,0:T(8,128)(2,1)} %param.15) | copy-start | bytes 98308
  78.7 39.5 %copy-start.8 = (f32[2048]{0:T(1024)S(1)}, f32[2048]{0:T(1024)}, u32[]{:S(2)}) copy-start(f32[2048]{0:T(1024)} %param.20) | copy-start | bytes 24580
  101.8 20.8 %copy-start.4 = (bf16[16,2048]{1,0:T(8,128)(2,1)}, bf16[16,2048]{1,0:T(8,128)(2,1)S(1)}, u32[]{:S(2)}) copy-start(bf16[16,2048]{1,0:T(8,128)(2,1)S(1)} %reduce_sum.36) | copy-start | bytes 196612
  101.9 7.4 %collective-permute-start.18 = (bf16[16,2048]{1,0:T(8,128)(2,1)S(1)}, bf16[16,2048]{1,0:T(8,128)(2,1)S(1)}, u32[]{:S(2)}, u32[]{:S(2)}) collective-permute-start(bf16[16,2048]{1,0:T(8,128)(2,1)S(1)} %fusion.11), channel_id=1, source_target_pairs={{0,4},{4,0},{8,12},{12,8},{16,20},{20,16},{24,28},{28,24},{1,5},{5... | collective-permute-start | bytes 196616 | tf_op jit(solution)/shard_map/ppermute | solution.py:23
  103.4 7.4 %collective-permute-start.19 = (bf16[16,2048]{1,0:T(8,128)(2,1)S(1)}, bf16[16,2048]{1,0:T(8,128)(2,1)S(1)}, u32[]{:S(2)}, u32[]{:S(2)}) collective-permute-start(bf16[16,2048]{1,0:T(8,128)(2,1)S(1)} %fusion.11), channel_id=1, source_target_pairs={{0,8},{4,12},{8,0},{12,4},{16,24},{20,28},{24,16},{28,20},{1,9},{5... | collective-permute-start | bytes 196616 | tf_op jit(solution)/shard_map/ppermute | solution.py:23
  103.4 9.9 %collective-permute-start.20 = (bf16[16,2048]{1,0:T(8,128)(2,1)S(1)}, bf16[16,2048]{1,0:T(8,128)(2,1)S(1)}, u32[]{:S(2)}, u32[]{:S(2)}) collective-permute-start(bf16[16,2048]{1,0:T(8,128)(2,1)S(1)} %fusion.11), channel_id=1, source_target_pairs={{0,12},{4,8},{8,4},{12,0},{16,28},{20,24},{24,20},{28,16},{1,13},{... | collective-permute-start | bytes 196616 | tf_op jit(solution)/shard_map/ppermute | solution.py:23
  105.4 9.4 %collective-permute-start.21 = (bf16[16,2048]{1,0:T(8,128)(2,1)S(1)}, bf16[16,2048]{1,0:T(8,128)(2,1)S(1)}, u32[]{:S(2)}, u32[]{:S(2)}) collective-permute-start(bf16[16,2048]{1,0:T(8,128)(2,1)S(1)} %fusion.11), channel_id=1, source_target_pairs={{0,16},{4,20},{8,24},{12,28},{16,0},{20,4},{24,8},{28,12},{1,17},{... | collective-permute-start | bytes 196616 | tf_op jit(solution)/shard_map/ppermute | solution.py:23
  106.3 10.9 %collective-permute-start.22 = (bf16[16,2048]{1,0:T(8,128)(2,1)S(1)}, bf16[16,2048]{1,0:T(8,128)(2,1)S(1)}, u32[]{:S(2)}, u32[]{:S(2)}) collective-permute-start(bf16[16,2048]{1,0:T(8,128)(2,1)S(1)} %fusion.11), channel_id=1, source_target_pairs={{0,20},{4,16},{8,28},{12,24},{16,4},{20,0},{24,12},{28,8},{1,21},{... | collective-permute-start | bytes 196616 | tf_op jit(solution)/shard_map/ppermute | solution.py:23
  109.3 7.9 %collective-permute-start.23 = (bf16[16,2048]{1,0:T(8,128)(2,1)S(1)}, bf16[16,2048]{1,0:T(8,128)(2,1)S(1)}, u32[]{:S(2)}, u32[]{:S(2)}) collective-permute-start(bf16[16,2048]{1,0:T(8,128)(2,1)S(1)} %fusion.11), channel_id=1, source_target_pairs={{0,24},{4,28},{8,16},{12,20},{16,8},{20,12},{24,0},{28,4},{1,25},{... | collective-permute-start | bytes 196616 | tf_op jit(solution)/shard_map/ppermute | solution.py:23
  110.8 7.1 %collective-permute-start.24 = (bf16[16,2048]{1,0:T(8,128)(2,1)S(1)}, bf16[16,2048]{1,0:T(8,128)(2,1)S(1)}, u32[]{:S(2)}, u32[]{:S(2)}) collective-permute-start(bf16[16,2048]{1,0:T(8,128)(2,1)S(1)} %fusion.11), channel_id=1, source_target_pairs={{0,28},{4,24},{8,20},{12,16},{16,12},{20,8},{24,4},{28,0},{1,29},{... | collective-permute-start | bytes 196616 | tf_op jit(solution)/shard_map/ppermute | solution.py:23
  118.1 4.5 %slice-start = ((s8[7340032]{0:T(1024)(128)(4,1)}), s8[4194304]{0:T(1024)(128)(4,1)S(1)}, s32[]{:S(2)}) async-start(s8[7340032]{0:T(1024)(128)(4,1)} %bitcast.154), calls=%async_computation.3 | async-start | bytes 8388608
  118.3 5.2 %slice-start.1 = ((s8[7340032]{0:T(1024)(128)(4,1)}), s8[3145728]{0:T(1024)(128)(4,1)S(1)}, s32[]{:S(2)}) async-start(s8[7340032]{0:T(1024)(128)(4,1)} %bitcast.154), calls=%async_computation.4 | async-start | bytes 6291456
  125.0 2.2 %collective-permute-start.25 = (bf16[32,3712]{1,0:T(8,128)(2,1)S(1)}, bf16[32,3712]{1,0:T(8,128)(2,1)S(1)}, u32[]{:S(2)}, u32[]{:S(2)}) collective-permute-start(bf16[32,3712]{1,0:T(8,128)(2,1)S(1)} %get-tuple-element.7), channel_id=1, source_target_pairs={{0,1},{1,0},{2,3},{3,2},{4,5},{5,4},{6,7},{7,6},{8,9},{9,8},{10,11... | collective-permute-start | bytes 712712 | tf_op jit(solution)/shard_map/ppermute | solution.py:23
  125.1 8.6 %collective-permute-start.26 = (bf16[32,3712]{1,0:T(8,128)(2,1)S(1)}, bf16[32,3712]{1,0:T(8,128)(2,1)S(1)}, u32[]{:S(2)}, u32[]{:S(2)}) collective-permute-start(bf16[32,3712]{1,0:T(8,128)(2,1)S(1)} %get-tuple-element.9), channel_id=1, source_target_pairs={{0,2},{1,3},{2,0},{3,1},{4,6},{5,7},{6,4},{7,5},{8,10},{9,11},{10,... | collective-permute-start | bytes 712712 | tf_op jit(solution)/shard_map/ppermute | solution.py:23
  126.0 11.9 %collective-permute-start.27 = (bf16[32,3712]{1,0:T(8,128)(2,1)S(1)}, bf16[32,3712]{1,0:T(8,128)(2,1)S(1)}, u32[]{:S(2)}, u32[]{:S(2)}) collective-permute-start(bf16[32,3712]{1,0:T(8,128)(2,1)S(1)} %get-tuple-element.8), channel_id=1, source_target_pairs={{0,3},{1,2},{2,1},{3,0},{4,7},{5,6},{6,5},{7,4},{8,11},{9,10},{10,... | collective-permute-start | bytes 712712 | tf_op jit(solution)/shard_map/ppermute | solution.py:23
  138.4 2.1 %collective-permute-start.28 = (bf16[32,1792]{1,0:T(8,128)(2,1)S(1)}, bf16[32,1792]{1,0:T(8,128)(2,1)S(1)}, u32[]{:S(2)}, u32[]{:S(2)}) collective-permute-start(bf16[32,1792]{1,0:T(8,128)(2,1)S(1)} %fusion.7), channel_id=1, source_target_pairs={{0,1},{1,0},{2,3},{3,2},{4,5},{5,4},{6,7},{7,6},{8,9},{9,8},{10,11... | collective-permute-start | bytes 344072 | tf_op jit(solution)/shard_map/ppermute | solution.py:23
  138.7 6.0 %collective-permute-start.29 = (bf16[32,1792]{1,0:T(8,128)(2,1)S(1)}, bf16[32,1792]{1,0:T(8,128)(2,1)S(1)}, u32[]{:S(2)}, u32[]{:S(2)}) collective-permute-start(bf16[32,1792]{1,0:T(8,128)(2,1)S(1)} %fusion.7), channel_id=1, source_target_pairs={{0,2},{1,3},{2,0},{3,1},{4,6},{5,7},{6,4},{7,5},{8,10},{9,11},{10,... | collective-permute-start | bytes 344072 | tf_op jit(solution)/shard_map/ppermute | solution.py:23
  139.6 6.2 %collective-permute-start.30 = (bf16[32,1792]{1,0:T(8,128)(2,1)S(1)}, bf16[32,1792]{1,0:T(8,128)(2,1)S(1)}, u32[]{:S(2)}, u32[]{:S(2)}) collective-permute-start(bf16[32,1792]{1,0:T(8,128)(2,1)S(1)} %fusion.7), channel_id=1, source_target_pairs={{0,3},{1,2},{2,1},{3,0},{4,7},{5,6},{6,5},{7,4},{8,11},{9,10},{10,... | collective-permute-start | bytes 344072 | tf_op jit(solution)/shard_map/ppermute | solution.py:23
  150.9 6.9 %collective-permute-start.31 = (bf16[16,2048]{1,0:T(8,128)(2,1)S(1)}, bf16[16,2048]{1,0:T(8,128)(2,1)S(1)}, u32[]{:S(2)}, u32[]{:S(2)}) collective-permute-start(bf16[16,2048]{1,0:T(8,128)(2,1)S(1)} %get-tuple-element.10), channel_id=1, source_target_pairs={{0,4},{4,0},{8,12},{12,8},{16,20},{20,16},{24,28},{28,24},{1,5},{5... | collective-permute-start | bytes 196616 | tf_op jit(solution)/shard_map/ppermute | solution.py:23
  152.0 7.8 %collective-permute-start.32 = (bf16[16,2048]{1,0:T(8,128)(2,1)S(1)}, bf16[16,2048]{1,0:T(8,128)(2,1)S(1)}, u32[]{:S(2)}, u32[]{:S(2)}) collective-permute-start(bf16[16,2048]{1,0:T(8,128)(2,1)S(1)} %get-tuple-element.16), channel_id=1, source_target_pairs={{0,8},{4,12},{8,0},{12,4},{16,24},{20,28},{24,16},{28,20},{1,9},{5... | collective-permute-start | bytes 196616 | tf_op jit(solution)/shard_map/ppermute | solution.py:23
  153.9 8.4 %collective-permute-start.33 = (bf16[16,2048]{1,0:T(8,128)(2,1)S(1)}, bf16[16,2048]{1,0:T(8,128)(2,1)S(1)}, u32[]{:S(2)}, u32[]{:S(2)}) collective-permute-start(bf16[16,2048]{1,0:T(8,128)(2,1)S(1)} %get-tuple-element.15), channel_id=1, source_target_pairs={{0,12},{4,8},{8,4},{12,0},{16,28},{20,24},{24,20},{28,16},{1,13},{... | collective-permute-start | bytes 196616 | tf_op jit(solution)/shard_map/ppermute | solution.py:23
  154.6 10.5 %collective-permute-start.34 = (bf16[16,2048]{1,0:T(8,128)(2,1)S(1)}, bf16[16,2048]{1,0:T(8,128)(2,1)S(1)}, u32[]{:S(2)}, u32[]{:S(2)}) collective-permute-start(bf16[16,2048]{1,0:T(8,128)(2,1)S(1)} %get-tuple-element.14), channel_id=1, source_target_pairs={{0,16},{4,20},{8,24},{12,28},{16,0},{20,4},{24,8},{28,12},{1,17},{... | collective-permute-start | bytes 196616 | tf_op jit(solution)/shard_map/ppermute | solution.py:23
  157.3 10.2 %collective-permute-start.35 = (bf16[16,2048]{1,0:T(8,128)(2,1)S(1)}, bf16[16,2048]{1,0:T(8,128)(2,1)S(1)}, u32[]{:S(2)}, u32[]{:S(2)}) collective-permute-start(bf16[16,2048]{1,0:T(8,128)(2,1)S(1)} %get-tuple-element.13), channel_id=1, source_target_pairs={{0,20},{4,16},{8,28},{12,24},{16,4},{20,0},{24,12},{28,8},{1,21},{... | collective-permute-start | bytes 196616 | tf_op jit(solution)/shard_map/ppermute | solution.py:23
  157.8 9.6 %collective-permute-start.36 = (bf16[16,2048]{1,0:T(8,128)(2,1)S(1)}, bf16[16,2048]{1,0:T(8,128)(2,1)S(1)}, u32[]{:S(2)}, u32[]{:S(2)}) collective-permute-start(bf16[16,2048]{1,0:T(8,128)(2,1)S(1)} %get-tuple-element.12), channel_id=1, source_target_pairs={{0,24},{4,28},{8,16},{12,20},{16,8},{20,12},{24,0},{28,4},{1,25},{... | collective-permute-start | bytes 196616 | tf_op jit(solution)/shard_map/ppermute | solution.py:23
  159.8 7.7 %collective-permute-start.37 = (bf16[16,2048]{1,0:T(8,128)(2,1)S(1)}, bf16[16,2048]{1,0:T(8,128)(2,1)S(1)}, u32[]{:S(2)}, u32[]{:S(2)}) collective-permute-start(bf16[16,2048]{1,0:T(8,128)(2,1)S(1)} %get-tuple-element.11), channel_id=1, source_target_pairs={{0,28},{4,24},{8,20},{12,16},{16,12},{20,8},{24,4},{28,0},{1,29},{... | collective-permute-start | bytes 196616 | tf_op jit(solution)/shard_map/ppermute | solution.py:23
Sparse Core Ops, SparseCore 0:
  55.1 14.0 all-gather.1

commit v2 on v1

--- a/solution.py
+++ b/solution.py
@@ -36,7 +36,50 @@
 
 def gather_rows(rows):
     groups = lax.axis_size("dp")
-    return jnp.stack([rows] + [swap(rows, "dp", k) for k in range(1, groups)])
+    blocks = {0: rows}
+    for k in range(groups - 2, 0, -2):
+        blocks[k] = swap(rows, "dp", k)
+    blocks[1] = swap(rows, "dp", 1)
+    for k in range(groups - 2, 0, -2):
+        blocks[k + 1] = swap(blocks[k], "dp", 1)
+    return jnp.stack([blocks[k] for k in range(groups)])
+
+
+def sum_rows(parts):
+    groups = lax.axis_size("dp")
+    paired = {}
+    for k in list(range(groups - 2, 0, -2)) + [0]:
+        paired[k] = parts[k].astype(F32) + swap(parts[k + 1], "dp", 1).astype(F32)
+    total = paired[0]
+    for k in range(groups - 2, 0, -2):
+        total = total + swap(paired[k].astype(BF16), "dp", k).astype(F32)
+    return total
+
+
+def sum_blocks(blocks):
+    tensor = lax.axis_size("tensor")
+    t = lax.axis_index("tensor")
+
+    def take(bits):
+        return jnp.concatenate([lax.dynamic_index_in_dim(blocks, t ^ k, 0, keepdims=True) for k in bits])
+
+    even = range(0, tensor, 2)
+    paired = take(even).astype(F32) + swap(take([k + 1 for k in even]), "tensor", 1).astype(F32)
+    total = paired[0]
+    for i in range(1, tensor // 2):
+        total = total + swap(paired[i].astype(BF16), "tensor", 2 * i).astype(F32)
+    return total
+
+
+def gather_blocks(block):
+    tensor = lax.axis_size("tensor")
+    blocks = {0: block}
+    for k in range(2, tensor, 2):
+        blocks[k] = swap(block, "tensor", k)
+    blocks[1] = swap(block, "tensor", 1)
+    for k in range(2, tensor, 2):
+        blocks[k + 1] = swap(blocks[k], "tensor", 1)
+    return jnp.stack([blocks[k] for k in range(tensor)])
 
 
 def split_ss(x):
@@ -47,6 +90,24 @@
 
 def scale_of(summed, width):
     return lax.rsqrt((summed[..., 0] + summed[..., 1]) / width + EPS)[..., None]
+
+
+def pack_kernel(heads_of, keys_ref, values_ref, out_ref):
+    for g, h in enumerate(heads_of):
+        out_ref[g, 0] = keys_ref[:, :, h * HD : (h + 1) * HD]
+        out_ref[g, 1] = values_ref[:, :, h * HD : (h + 1) * HD]
+
+
+def pack(cache_keys, cache_values, heads_of):
+    part_dev, span, _ = cache_keys.shape
+    vmem = pl.BlockSpec(memory_space=pltpu.VMEM)
+    return pl.pallas_call(
+        functools.partial(pack_kernel, heads_of),
+        out_shape=jax.ShapeDtypeStruct((len(heads_of), 2, part_dev, span, HD), BF16),
+        in_specs=[vmem] * 2,
+        out_specs=vmem,
+        compiler_params=pltpu.CompilerParams(vmem_limit_bytes=8 << 20),
+    )(cache_keys, cache_values)
 
 
 def attention_kernel(
@@ -71,11 +132,11 @@
 
         def bring(i, _, source=source):
             particle = source[i]
+            place = (particle // part_dev) * 2 * part_dev + particle % part_dev
             for t in range(tensor):
-                both = kv_ref[t, particle].astype(F32)
                 start = pl.multiple_of(i * ctx + t * span, 8)
-                keys_ref[pl.ds(start, span), :] = both[:span]
-                values_ref[pl.ds(start, span), :] = both[span:]
+                keys_ref[pl.ds(start, span), :] = kv_ref[t, place].astype(F32)
+                values_ref[pl.ds(start, span), :] = kv_ref[t, place + part_dev].astype(F32)
             return 0
 
         lax.fori_loop(0, parts, bring, 0)
@@ -119,18 +180,18 @@
 def attention(own, anc, q, scale, kv, nk, nv, targets, rope, part_dev):
     parts = own.shape[0]
     heads = q.shape[1] // HD
-    tensor, _, span2, _ = kv.shape
-    span = span2 // 2
+    tensor, _, span, _ = kv.shape
     ctx = tensor * span
     smem = pl.BlockSpec(memory_space=pltpu.SMEM)
     vmem = pl.BlockSpec(memory_space=pltpu.VMEM)
+    limit = (8 << 20) + 2 * kv.size * 2 + 4 * (2 * heads * parts * parts * ctx)
     return pl.pallas_call(
         functools.partial(attention_kernel, (parts, part_dev, heads, tensor, span)),
         out_shape=jax.ShapeDtypeStruct((q.shape[0], q.shape[1]), BF16),
         in_specs=[smem, smem] + [vmem] * 7,
         out_specs=vmem,
         scratch_shapes=[pltpu.VMEM((parts * ctx, HD), F32), pltpu.VMEM((parts * ctx, HD), F32)],
-        compiler_params=pltpu.CompilerParams(vmem_limit_bytes=40 << 20),
+        compiler_params=pltpu.CompilerParams(vmem_limit_bytes=limit),
         cost_estimate=pl.CostEstimate(flops=100 << 20, bytes_accessed=2 << 20, transcendentals=1 << 18),
     )(own, anc, q, scale, kv, nk, nv, targets, rope)
 
@@ -161,34 +222,22 @@
     pair = 2 * part_dev
     near = groups // tensor
 
-    heads_of = np.arange(groups) * KVH // groups
-    both = jnp.concatenate(
-        [
-            cache_keys.reshape(part_dev, span, KVH, HD),
-            cache_values.reshape(part_dev, span, KVH, HD),
-        ],
-        axis=1,
-    )
-    sent = jnp.stack([both[:, :, h] for h in heads_of])
+    sent = pack(cache_keys, cache_values, [g * KVH // groups for g in range(groups)])
     cache = lax.all_to_all(sent, "dp", split_axis=0, concat_axis=0, tiled=True)
-    cache = lax.all_gather(cache.reshape(groups * part_dev, 2 * span, HD), "tensor", axis=0)
+    cache = lax.all_gather(cache.reshape(groups * pair, span, HD), "tensor", axis=0)
 
     x = jnp.concatenate([x_first, x_second], axis=0)
     rows = gather_rows(x).reshape(groups * pair, features)
     wide = rows.astype(F32)
-    squares = split_ss(jnp.sum(wide * wide, axis=1))
     lifted = (wide * attn_gain[None, :]).astype(BF16)
     kv_part = jnp.dot(lifted, w_keyval, preferred_element_type=F32).astype(BF16)
-    kv_part = jnp.concatenate([kv_part, squares], axis=1)
     q_part = jnp.dot(lifted, w_query, preferred_element_type=F32).astype(BF16)
     q_part = q_part.reshape(tensor, near * pair, -1)
-    kv_sum = kv_part.astype(F32)
-    for k in range(1, tensor):
-        kv_sum = kv_sum + swap(kv_part, "tensor", k).astype(F32)
+    squares = jnp.sum(wide * wide, axis=1)
+    relative = jnp.arange(groups)
+    squares = jnp.take(squares.reshape(groups, pair), relative ^ d, axis=0).reshape(-1)
     kv_cols = w_keyval.shape[1]
-    scale = scale_of(kv_sum[:, kv_cols:], width)
-    keyvals = (kv_sum[:, :kv_cols] * scale).astype(BF16).reshape(groups, pair, kv_cols)
-    keyvals = jnp.take(keyvals, jnp.arange(groups) ^ d, axis=0).reshape(groups * pair, kv_cols)
+    keyvals = jnp.take(kv_part.reshape(groups, pair, kv_cols), relative ^ d, axis=0).reshape(groups * pair, kv_cols)
     if groups == KVH:
         halves = (keyvals[:, :HD], keyvals[:, HD:])
         half = groups // 2
@@ -204,18 +253,26 @@
             [(i, 2 * i + 1) for i in range(half)] + [(half + i, 2 * i) for i in range(half)],
         )
         even = d % 2 == 0
-        new_keys = jnp.where(even, one, two)
-        new_values = jnp.where(even, two, one)
+        new_kv = jnp.concatenate([jnp.where(even, one, two), jnp.where(even, two, one)], axis=1)
     else:
         every = lax.all_gather(keyvals, "dp", axis=1, tiled=True)
         start = (d * KVH // groups) * HD
-        new_keys = lax.dynamic_slice_in_dim(every, start, HD, axis=1)
-        new_values = lax.dynamic_slice_in_dim(every, KVH * HD + start, HD, axis=1)
-
-    queries = lax.dynamic_index_in_dim(q_part, t, 0, keepdims=False).astype(F32)
-    for k in range(1, tensor):
-        piece = lax.dynamic_index_in_dim(q_part, t ^ k, 0, keepdims=False)
-        queries = queries + swap(piece, "tensor", k).astype(F32)
+        new_kv = jnp.concatenate(
+            [lax.dynamic_slice_in_dim(every, first + start, HD, axis=1) for first in (0, KVH * HD)], axis=1
+        )
+    new_kv = new_kv.astype(F32)
+    bits = 1
+    while bits < tensor:
+        message = jnp.concatenate([new_kv.astype(BF16), split_ss(squares)], axis=1)
+        arrived = swap(message, "tensor", bits).astype(F32)
+        new_kv = new_kv + arrived[:, : 2 * HD]
+        squares = squares + (arrived[:, 2 * HD] + arrived[:, 2 * HD + 1])
+        bits *= 2
+    scale = lax.rsqrt(squares / width + EPS)[:, None]
+    new_kv = (new_kv * scale).astype(BF16)
+    new_keys, new_values = new_kv[:, :HD], new_kv[:, HD:]
+    queries = sum_blocks(q_part)
+    scale = jnp.take(scale.reshape(groups, pair), relative ^ d, axis=0).reshape(groups * pair, 1)
     own_scale = lax.dynamic_slice_in_dim(scale, t * near * pair, near * pair, axis=0)
 
     own_blocks = (t * near + jnp.arange(near)) ^ d
@@ -231,40 +288,29 @@
     rope = jnp.asarray(np.stack(rope_tables(context) + rope_tables(context + 1)))
     mixed = attention(own, anc, queries, own_scale, cache, new_keys, new_values, targets, rope, part_dev)
 
-    def gather_near(block, order):
-        blocks = jnp.stack([block] + [swap(block, "tensor", k) for k in range(1, tensor)])
-        return jnp.take(blocks.reshape(groups, pair, -1), order, axis=0).reshape(groups * pair, -1)
-
-    def stacked(k):
-        return ((k // near) ^ t) * near + k % near
-
-    relative = jnp.arange(groups)
-    spread = gather_near(mixed, stacked(relative ^ d))
-    out_part = jnp.dot(spread, w_out, preferred_element_type=F32).astype(BF16)
-    arrived = lax.all_to_all(out_part.reshape(groups, pair, -1), "dp", split_axis=0, concat_axis=0, tiled=True)
-    attn_part = jnp.sum(arrived.astype(F32), axis=0).astype(BF16)
+    stacked = ((relative // near) ^ t) * near + relative % near
+
+    def spread(block):
+        blocks = gather_blocks(block).reshape(groups, pair, -1)
+        return jnp.take(blocks, stacked, axis=0).reshape(groups * pair, -1)
+
+    out_part = jnp.dot(spread(mixed), w_out, preferred_element_type=F32).astype(BF16)
+    attn_part = sum_rows(out_part.reshape(groups, pair, -1)).astype(BF16)
     residual = (x.astype(F32) + attn_part.astype(F32)).astype(BF16)
 
     rows = gather_rows(residual).reshape(groups * pair, features)
     wide = rows.astype(F32)
     squares = split_ss(jnp.sum(wide * wide, axis=1))
     lifted = (wide * ffn_gain[None, :]).astype(BF16)
+    hidden_cols = w_gate.shape[1]
     gate = jnp.dot(lifted, w_gate, preferred_element_type=F32).astype(BF16)
+    gate = sum_blocks(jnp.concatenate([gate, squares], axis=1).reshape(tensor, near * pair, -1))
     up = jnp.dot(lifted, w_up, preferred_element_type=F32).astype(BF16)
-    hidden_cols = w_gate.shape[1]
-    part = jnp.concatenate([gate, up, squares], axis=1).reshape(tensor, near * pair, -1)
-    summed = lax.dynamic_index_in_dim(part, t, 0, keepdims=False).astype(F32)
-    for k in range(1, tensor):
-        piece = lax.dynamic_index_in_dim(part, t ^ k, 0, keepdims=False)
-        summed = summed + swap(piece, "tensor", k).astype(F32)
-    scale = scale_of(summed[:, 2 * hidden_cols :], width)
-    hidden = jax.nn.silu(summed[:, :hidden_cols] * scale) * (summed[:, hidden_cols : 2 * hidden_cols] * scale)
-    spread = gather_near(hidden.astype(BF16), stacked(relative))
-    down = jnp.dot(spread, w_down, preferred_element_type=F32).astype(BF16).reshape(groups, pair, -1)
-    total = down[0].astype(F32)
-    for k in range(1, groups):
-        total = total + swap(down[k], "dp", k).astype(F32)
-    ffn_part = total.astype(BF16)
+    up = sum_blocks(up.reshape(tensor, near * pair, -1))
+    scale = scale_of(gate[:, hidden_cols:], width)
+    hidden = jax.nn.silu(gate[:, :hidden_cols] * scale) * (up * scale)
+    down = jnp.dot(spread(hidden.astype(BF16)), w_down, preferred_element_type=F32).astype(BF16)
+    ffn_part = sum_rows(down.reshape(groups, pair, -1)).astype(BF16)
     return (attn_part.reshape(2, part_dev, features), ffn_part.reshape(2, part_dev, features))
 
 

time: 176 us -> 160 us (0.909)
  blocking collectives: 20.1 us -> 0 us
  waiting for transfers between devices: 43.2 us -> 59.1 us
  other arithmetic: 13.9 us -> 4.78 us
  starting transfers between devices: 56.4 us -> 49.6 us
  local copies, waits for them, and re-layouts: 8.77 us -> 11.9 us
    all_to_all x1 -> x0, blocking collectives: 20.1 us -> none  [local(): lax.all_to_all(out_part.reshape(groups, pair, -1), 'dp', split_axis=0, co...]
    all_gather x1, waiting for transfers between devices: 0.02 us -> 12.6 us  [local(): lax.all_gather(cache.reshape(groups * pair, span, HD), 'tensor', axis=0)]
    unnamed x9 -> x2, other arithmetic: 9.48 us -> 0.69 us
    ppermute x36 -> x42, waiting for transfers between devices: 40.2 us -> 46.5 us  [swap(): return lax.ppermute(x, axis, [(i, i ^ bits) for i in range(size)])]
    ppermute x36 -> x42, starting transfers between devices: 46.6 us -> 43.1 us  [swap(): return lax.ppermute(x, axis, [(i, i ^ bits) for i in range(size)])]
    ppermute x1, starting transfers between devices: 4.3 us -> 0.96 us  [local(): lax.ppermute(jnp.where(lower, halves[1], halves[0]), 'dp', [(i, 2 * i + 1...]
    dot_general x1, matrix products: 1.16 us -> 4.38 us  [local(): gate = jnp.dot(lifted, w_gate, preferred_element_type=F32).astype(BF16)]
    dot_general x1, matrix products: 4.38 us -> 1.16 us  [local(): up = jnp.dot(lifted, w_up, preferred_element_type=F32).astype(BF16)]
  transfers between devices with their start and end apart: 40 -> 46, of which waited for: 17 -> 29; matrix products, arithmetic and copies ran while one was open for 10% -> 6% of each run, Pallas kernels for 0% -> 0%
where the time goes in v2:
time: 160 us; the launch traced here: 159 us
  waiting for transfers between devices  59.1 us (37%)
  starting transfers between devices  49.6 us (31%)
  matrix products  16.1 us (10%)
  between operations  14.7 us (9%)
  local copies, waits for them, and re-layouts  11.9 us (7%)
  other arithmetic  4.78 us (3%)
  Pallas kernels  2.95 us (2%)
    ppermute x42, waiting for transfers between devices, swap(): return lax.ppermute(x, axis, [(i, i ^ bits) for i in range(size)])  46.5 us
    ppermute x42, starting transfers between devices, swap(): return lax.ppermute(x, axis, [(i, i ^ bits) for i in range(size)])  43.1 us
    all_gather x1, waiting for transfers between devices, local(): lax.all_gather(cache.reshape(groups * pair, span, HD), 'tensor', axis=0)  12.6 us
    unnamed x32, local copies, waits for them, and re-layouts  5.37 us
    all_to_all x1, starting transfers between devices, local(): cache = lax.all_to_all(sent, 'dp', split_axis=0, concat_axis=0, tiled=True)  4.88 us
    dot_general x1, matrix products, local(): gate = jnp.dot(lifted, w_gate, preferred_element_type=F32).astype(BF16)  4.38 us
    dot_general x1, matrix products, local(): jnp.dot(spread(hidden.astype(BF16)), w_down, preferred_element_type=F32)  4.31 us
  transfers between devices with their start and end apart: 46, of which 29 were waited for; matrix products, arithmetic and copies ran while one was open for 6% of the time, Pallas kernels for 0%

profile of v2, /device:TPU:0, one launch (start us, length us, event | category | flops | bytes accessed | tf_op | source)
XLA Modules:
  0.0 159.1 jit_solution(17759168712750426209)
XLA Ops:
  7.2 0.8 constant_dynamic-update-slice_fusion.1
  8.0 0.8 constant_dynamic-update-slice_fusion
  8.8 2.9 %collective-permute-start = (bf16[16,2048]{1,0:T(8,128)(2,1)S(1)}, bf16[16,2048]{1,0:T(8,128)(2,1)S(1)}, u32[]{:S(2)}, u32[]{:S(2)}) collective-permute-start(bf16[16,2048]{1,0:T(8,128)(2,1)S(1)} %constant_dynamic-update-slice_fusion), channel_id=1, source_target_pairs={{0,4},{4,0},{8,12},{12,8},{16,20},{20,16},{24,28},{28,24},{1,5},{5... | collective-permute-start | bytes 196616 | tf_op jit(solution)/shard_map/ppermute | solution.py:23
  11.7 1.6 collective-permute-start.1
  13.3 2.6 %collective-permute-start.3 = (bf16[16,2048]{1,0:T(8,128)(2,1)S(1)}, bf16[16,2048]{1,0:T(8,128)(2,1)S(1)}, u32[]{:S(2)}, u32[]{:S(2)}) collective-permute-start(bf16[16,2048]{1,0:T(8,128)(2,1)S(1)} %constant_dynamic-update-slice_fusion), channel_id=1, source_target_pairs={{0,16},{4,20},{8,24},{12,28},{16,0},{20,4},{24,8},{28,12},{1,17},{... | collective-permute-start | bytes 196616 | tf_op jit(solution)/shard_map/ppermute | solution.py:23
  16.1 0.9 copy-done.2
  17.0 0.9 copy-done.3
  17.9 0.8 shard_map.149
  18.7 4.9 %all-to-all-start = ((bf16[8,2,8,8,128]{4,3,2,1,0:T(8,128)(2,1)}), bf16[8,2,8,8,128]{4,3,2,1,0:T(8,128)(2,1)S(1)}, u32[]{:S(2)}, u32[]{:S(2)}) async-start(bf16[8,2,8,8,128]{4,3,2,1,0:T(8,128)(2,1)} %shard_map.149), calls=%async_computation | async-start | bytes 524288 | tf_op jit(solution)/shard_map/all_to_all | solution.py:226
  24.1 1.3 gather_fusion
  25.7 2.0 %collective-permute-start.2 = (bf16[16,2048]{1,0:T(8,128)(2,1)S(1)}, bf16[16,2048]{1,0:T(8,128)(2,1)S(1)}, u32[]{:S(2)}, u32[]{:S(2)}) collective-permute-start(bf16[16,2048]{1,0:T(8,128)(2,1)S(1)} %collective-permute-done.1), channel_id=1, source_target_pairs={{0,4},{4,0},{8,12},{12,8},{16,20},{20,16},{24,28},{28,24},{1,5},{5... | collective-permute-start | bytes 196616 | tf_op jit(solution)/shard_map/ppermute | solution.py:23
  27.9 2.0 %collective-permute-start.6 = (bf16[16,2048]{1,0:T(8,128)(2,1)S(1)}, bf16[16,2048]{1,0:T(8,128)(2,1)S(1)}, u32[]{:S(2)}, u32[]{:S(2)}) collective-permute-start(bf16[16,2048]{1,0:T(8,128)(2,1)S(1)} %collective-permute-done.5), channel_id=1, source_target_pairs={{0,4},{4,0},{8,12},{12,8},{16,20},{20,16},{24,28},{28,24},{1,5},{5... | collective-permute-start | bytes 196616 | tf_op jit(solution)/shard_map/ppermute | solution.py:23
  29.8 1.6 %collective-permute-done.2 = bf16[16,2048]{1,0:T(8,128)(2,1)S(1)} collective-permute-done((bf16[16,2048]{1,0:T(8,128)(2,1)S(1)}, bf16[16,2048]{1,0:T(8,128)(2,1)S(1)}, u32[]{:S(2)}, u32[]{:S(2)}) %collective-permute-start.2) | collective-permute-done | bytes 65568 | tf_op jit(solution)/shard_map/ppermute | solution.py:23
  31.4 1.0 collective-permute-done.4
  33.3 0.8 fusion.1
  35.2 1.0 collective-permute-start.10
  37.5 3.0 %convolution_convert_fusion.4 = bf16[128,1024]{1,0:T(8,128)(2,1)S(1)} fusion(bf16[128,2048]{1,0:T(8,128)(2,1)S(1)} %fusion.1, bf16[2048,1024]{1,0:T(8,128)(2,1)} %param.23), kind=kOutput, calls=%fused_computation.10 | convolution fusion | flops 537001984 | bytes 4980736 | tf_op jit(solution)/shard_map/dot_general | solution.py:234
  41.5 0.7 collective-permute-done.7
  42.3 1.6 collective-permute-start.8
  44.1 0.7 copy-done.5
  45.6 1.0 collective-permute-done.8
  46.6 3.0 %collective-permute-done.12 = bf16[128,384]{1,0:T(8,128)(2,1)S(1)} collective-permute-done((bf16[128,384]{1,0:T(8,128)(2,1)S(1)}, bf16[128,384]{1,0:T(8,128)(2,1)S(1)}, u32[]{:S(2)}, u32[]{:S(2)}) %collective-permute-start.12) | collective-permute-done | bytes 98336 | tf_op jit(solution)/shard_map/ppermute | solution.py:23
  50.9 12.6 %all-gather.2.cloned.1.call-done.kv_ref = bf16[4,128,8,128]{3,2,1,0:T(8,128)(2,1)} async-done(((bf16[1,128,8,128]{3,2,1,0:T(8,128)(2,1)}), bf16[4,128,8,128]{3,2,1,0:T(8,128)(2,1)}) %all-gather.2.cloned.1.call-update) | async-done | bytes 1048592 | tf_op jit(solution)/shard_map/all_gather | solution.py:227
  63.5 1.2 copy-done.1
  64.7 2.2 %shard_map.150 = bf16[32,1024]{1,0:T(8,128)(2,1)S(1)} custom-call(s32[16]{0:T(128)S(1)} %add.410.own_ref, s32[16]{0:T(128)S(1)} %and_select_fusion.7.anc_ref, f32[32,1024]{1,0:T(8,128)S(1)} %fusion.12.q_ref, f32[32,1]{1,0:T(8,128)S(1)} %constant_dynamic-slice_fusion.8.scale_ref, bf16[4,128,8,128]{3,2,1,0:T(8,128)(2,1)S(1)} %copy-done.1, ...), custom_call_target="tpu_custom_call" | custom-call | flops 104857600 | bytes 2097152 | tf_op jit(solution)/shard_map/pallas_call | solution.py:188
  67.3 3.9 %collective-permute-done.14 = bf16[32,1024]{1,0:T(8,128)(2,1)S(1)} collective-permute-done((bf16[32,1024]{1,0:T(8,128)(2,1)S(1)}, bf16[32,1024]{1,0:T(8,128)(2,1)S(1)}, u32[]{:S(2)}, u32[]{:S(2)}) %collective-permute-start.14) | collective-permute-done | bytes 65568 | tf_op jit(solution)/shard_map/ppermute | solution.py:23
  71.4 1.1 collective-permute-done.15
  73.2 2.9 %convolution_convert_fusion.3 = bf16[128,2048]{1,0:T(8,128)(2,1)S(1)} fusion(bf16[128,1024]{1,0:T(8,128)(2,1)S(1)} %bitcast_select_fusion.1, bf16[1024,2048]{1,0:T(8,128)(2,1)} %param.25), kind=kOutput, calls=%fused_computation.9 | convolution fusion | flops 537133056 | bytes 4980736 | tf_op jit(solution)/shard_map/dot_general | solution.py:297
  76.1 1.5 collective-permute-start.17
  78.2 1.5 collective-permute-start.21
  80.9 1.8 %collective-permute-done.19 = bf16[16,2048]{1,0:T(8,128)(2,1)S(1)} collective-permute-done((bf16[16,2048]{1,0:T(8,128)(2,1)S(1)}, bf16[16,2048]{1,0:T(8,128)(2,1)S(1)}, u32[]{:S(2)}, u32[]{:S(2)}) %collective-permute-start.19) | collective-permute-done | bytes 65568 | tf_op jit(solution)/shard_map/ppermute | solution.py:23
  82.7 1.3 collective-permute-done.21
  84.0 3.4 %collective-permute-start.18 = (bf16[16,2048]{1,0:T(8,128)(2,1)S(1)}, bf16[16,2048]{1,0:T(8,128)(2,1)S(1)}, u32[]{:S(2)}, u32[]{:S(2)}) collective-permute-start(bf16[16,2048]{1,0:T(8,128)(2,1)S(1)} %get-tuple-element.25), channel_id=1, source_target_pairs={{0,24},{4,28},{8,16},{12,20},{16,8},{20,12},{24,0},{28,4},{1,25},{... | collective-permute-start | bytes 196616 | tf_op jit(solution)/shard_map/ppermute | solution.py:23
  87.4 1.1 collective-permute-start.22
  88.5 1.7 %collective-permute-done.18 = bf16[16,2048]{1,0:T(8,128)(2,1)S(1)} collective-permute-done((bf16[16,2048]{1,0:T(8,128)(2,1)S(1)}, bf16[16,2048]{1,0:T(8,128)(2,1)S(1)}, u32[]{:S(2)}, u32[]{:S(2)}) %collective-permute-start.18) | collective-permute-done | bytes 65568 | tf_op jit(solution)/shard_map/ppermute | solution.py:23
  90.2 2.4 %collective-permute-done.20 = bf16[16,2048]{1,0:T(8,128)(2,1)S(1)} collective-permute-done((bf16[16,2048]{1,0:T(8,128)(2,1)S(1)}, bf16[16,2048]{1,0:T(8,128)(2,1)S(1)}, u32[]{:S(2)}, u32[]{:S(2)}) %collective-permute-start.20) | collective-permute-done | bytes 65568 | tf_op jit(solution)/shard_map/ppermute | solution.py:23
  93.8 1.4 collective-permute-start.23
  95.2 2.1 %collective-permute-start.26 = (bf16[16,2048]{1,0:T(8,128)(2,1)S(1)}, bf16[16,2048]{1,0:T(8,128)(2,1)S(1)}, u32[]{:S(2)}, u32[]{:S(2)}) collective-permute-start(bf16[16,2048]{1,0:T(8,128)(2,1)S(1)} %get-tuple-element.6), channel_id=1, source_target_pairs={{0,16},{4,20},{8,24},{12,28},{16,0},{20,4},{24,8},{28,12},{1,17},{... | collective-permute-start | bytes 196616 | tf_op jit(solution)/shard_map/ppermute | solution.py:23
  97.3 1.7 %collective-permute-start.28 = (bf16[16,2048]{1,0:T(8,128)(2,1)S(1)}, bf16[16,2048]{1,0:T(8,128)(2,1)S(1)}, u32[]{:S(2)}, u32[]{:S(2)}) collective-permute-start(bf16[16,2048]{1,0:T(8,128)(2,1)S(1)} %get-tuple-element.6), channel_id=1, source_target_pairs={{0,24},{4,28},{8,16},{12,20},{16,8},{20,12},{24,0},{28,4},{1,25},{... | collective-permute-start | bytes 196616 | tf_op jit(solution)/shard_map/ppermute | solution.py:23
  99.7 0.7 collective-permute-done.26
  100.5 0.8 collective-permute-start.27
  101.3 2.1 %collective-permute-done.28 = bf16[16,2048]{1,0:T(8,128)(2,1)S(1)} collective-permute-done((bf16[16,2048]{1,0:T(8,128)(2,1)S(1)}, bf16[16,2048]{1,0:T(8,128)(2,1)S(1)}, u32[]{:S(2)}, u32[]{:S(2)}) %collective-permute-start.28) | collective-permute-done | bytes 65568 | tf_op jit(solution)/shard_map/ppermute | solution.py:23
  104.8 2.9 %collective-permute-done.29 = bf16[16,2048]{1,0:T(8,128)(2,1)S(1)} collective-permute-done((bf16[16,2048]{1,0:T(8,128)(2,1)S(1)}, bf16[16,2048]{1,0:T(8,128)(2,1)S(1)}, u32[]{:S(2)}, u32[]{:S(2)}) %collective-permute-start.29) | collective-permute-done | bytes 65568 | tf_op jit(solution)/shard_map/ppermute | solution.py:23
  108.2 4.4 %convolution_convert_fusion.2 = bf16[128,1792]{1,0:T(8,128)(2,1)S(1)} fusion(bf16[128,2048]{1,0:T(8,128)(2,1)S(1)} %fusion, bf16[2048,1792]{1,0:T(8,128)(2,1)} %param.26), kind=kOutput, calls=%fused_computation.8 | convolution fusion | flops 939753472 | bytes 8323072 | tf_op jit(solution)/shard_map/dot_general | solution.py:306
  113.4 1.2 convolution_convert_fusion.1
  115.3 0.9 collective-permute-done.32
  116.6 0.7 collective-permute-start.31
  117.3 1.5 collective-permute-start.33
  118.8 4.0 %collective-permute-done.31 = bf16[32,1920]{1,0:T(8,128)(2,1)S(1)} collective-permute-done((bf16[32,1920]{1,0:T(8,128)(2,1)S(1)}, bf16[32,1920]{1,0:T(8,128)(2,1)S(1)}, u32[]{:S(2)}, u32[]{:S(2)}) %collective-permute-start.31) | collective-permute-done | bytes 122912 | tf_op jit(solution)/shard_map/ppermute | solution.py:23
  123.0 1.6 %collective-permute-done.33 = bf16[32,1792]{1,0:T(8,128)(2,1)S(1)} collective-permute-done((bf16[32,1792]{1,0:T(8,128)(2,1)S(1)}, bf16[32,1792]{1,0:T(8,128)(2,1)S(1)}, u32[]{:S(2)}, u32[]{:S(2)}) %collective-permute-start.33) | collective-permute-done | bytes 114720 | tf_op jit(solution)/shard_map/ppermute | solution.py:23
  124.8 0.7 collective-permute-start.35
  125.5 4.2 %collective-permute-done.35 = bf16[32,1792]{1,0:T(8,128)(2,1)S(1)} collective-permute-done((bf16[32,1792]{1,0:T(8,128)(2,1)S(1)}, bf16[32,1792]{1,0:T(8,128)(2,1)S(1)}, u32[]{:S(2)}, u32[]{:S(2)}) %collective-permute-start.35) | collective-permute-done | bytes 114720 | tf_op jit(solution)/shard_map/ppermute | solution.py:23
  129.7 1.3 collective-permute-done.36
  131.7 4.3 %convolution_convert_fusion = bf16[128,2048]{1,0:T(8,128)(2,1)S(1)} fusion(bf16[128,1792]{1,0:T(8,128)(2,1)S(1)} %bitcast_select_fusion, bf16[1792,2048]{1,0:T(8,128)(2,1)} %param.28), kind=kOutput, calls=%fused_computation.6 | convolution fusion | flops 939786240 | bytes 8323072 | tf_op jit(solution)/shard_map/dot_general | solution.py:312
  136.1 0.7 collective-permute-start.38
  136.8 1.4 collective-permute-start.40
  138.8 1.4 collective-permute-start.37
  140.2 0.9 collective-permute-done.38
  141.1 1.4 collective-permute-done.40
  142.5 1.3 collective-permute-done.42
  143.9 1.9 %collective-permute-start.39 = (bf16[16,2048]{1,0:T(8,128)(2,1)S(1)}, bf16[16,2048]{1,0:T(8,128)(2,1)S(1)}, u32[]{:S(2)}, u32[]{:S(2)}) collective-permute-start(bf16[16,2048]{1,0:T(8,128)(2,1)S(1)} %get-tuple-element.18), channel_id=1, source_target_pairs={{0,24},{4,28},{8,16},{12,20},{16,8},{20,12},{24,0},{28,4},{1,25},{... | collective-permute-start | bytes 196616 | tf_op jit(solution)/shard_map/ppermute | solution.py:23
  145.8 2.5 %collective-permute-start.43 = (bf16[16,2048]{1,0:T(8,128)(2,1)S(1)}, bf16[16,2048]{1,0:T(8,128)(2,1)S(1)}, u32[]{:S(2)}, u32[]{:S(2)}) collective-permute-start(bf16[16,2048]{1,0:T(8,128)(2,1)S(1)} %get-tuple-element.19), channel_id=1, source_target_pairs={{0,8},{4,12},{8,0},{12,4},{16,24},{20,28},{24,16},{28,20},{1,9},{5... | collective-permute-start | bytes 196616 | tf_op jit(solution)/shard_map/ppermute | solution.py:23
  148.3 1.9 %collective-permute-done.39 = bf16[16,2048]{1,0:T(8,128)(2,1)S(1)} collective-permute-done((bf16[16,2048]{1,0:T(8,128)(2,1)S(1)}, bf16[16,2048]{1,0:T(8,128)(2,1)S(1)}, u32[]{:S(2)}, u32[]{:S(2)}) %collective-permute-start.39) | collective-permute-done | bytes 65568 | tf_op jit(solution)/shard_map/ppermute | solution.py:23
  150.2 1.4 collective-permute-done.41
  (161 shorter events, 18.7 us)
Async XLA Ops:
  7.2 27.0 %copy-start = (bf16[2048,256]{1,0:T(8,128)(2,1)S(1)}, bf16[2048,256]{1,0:T(8,128)(2,1)}, u32[]{:S(2)}) copy-start(bf16[2048,256]{1,0:T(8,128)(2,1)} %param.24) | copy-start | bytes 3145732
  8.8 18.9 %collective-permute-start = (bf16[16,2048]{1,0:T(8,128)(2,1)S(1)}, bf16[16,2048]{1,0:T(8,128)(2,1)S(1)}, u32[]{:S(2)}, u32[]{:S(2)}) collective-permute-start(bf16[16,2048]{1,0:T(8,128)(2,1)S(1)} %constant_dynamic-update-slice_fusion), channel_id=1, source_target_pairs={{0,4},{4,0},{8,12},{12,8},{16,20},{20,16},{24,28},{28,24},{1,5},{5... | collective-permute-start | bytes 196616 | tf_op jit(solution)/shard_map/ppermute | solution.py:23
  11.7 13.9 %collective-permute-start.1 = (bf16[16,2048]{1,0:T(8,128)(2,1)S(1)}, bf16[16,2048]{1,0:T(8,128)(2,1)S(1)}, u32[]{:S(2)}, u32[]{:S(2)}) collective-permute-start(bf16[16,2048]{1,0:T(8,128)(2,1)S(1)} %constant_dynamic-update-slice_fusion), channel_id=1, source_target_pairs={{0,8},{4,12},{8,0},{12,4},{16,24},{20,28},{24,16},{28,20},{1,9},{5... | collective-permute-start | bytes 196616 | tf_op jit(solution)/shard_map/ppermute | solution.py:23
  13.3 14.4 %collective-permute-start.3 = (bf16[16,2048]{1,0:T(8,128)(2,1)S(1)}, bf16[16,2048]{1,0:T(8,128)(2,1)S(1)}, u32[]{:S(2)}, u32[]{:S(2)}) collective-permute-start(bf16[16,2048]{1,0:T(8,128)(2,1)S(1)} %constant_dynamic-update-slice_fusion), channel_id=1, source_target_pairs={{0,16},{4,20},{8,24},{12,28},{16,0},{20,4},{24,8},{28,12},{1,17},{... | collective-permute-start | bytes 196616 | tf_op jit(solution)/shard_map/ppermute | solution.py:23
  15.9 12.0 %collective-permute-start.5 = (bf16[16,2048]{1,0:T(8,128)(2,1)S(1)}, bf16[16,2048]{1,0:T(8,128)(2,1)S(1)}, u32[]{:S(2)}, u32[]{:S(2)}) collective-permute-start(bf16[16,2048]{1,0:T(8,128)(2,1)S(1)} %constant_dynamic-update-slice_fusion), channel_id=1, source_target_pairs={{0,24},{4,28},{8,16},{12,20},{16,8},{20,12},{24,0},{28,4},{1,25},{... | collective-permute-start | bytes 196616 | tf_op jit(solution)/shard_map/ppermute | solution.py:23
  16.1 0.9 copy-start.2
  17.0 0.9 copy-start.3
  18.7 25.4 %all-to-all-start = ((bf16[8,2,8,8,128]{4,3,2,1,0:T(8,128)(2,1)}), bf16[8,2,8,8,128]{4,3,2,1,0:T(8,128)(2,1)S(1)}, u32[]{:S(2)}, u32[]{:S(2)}) async-start(bf16[8,2,8,8,128]{4,3,2,1,0:T(8,128)(2,1)} %shard_map.149), calls=%async_computation | async-start | bytes 524288 | tf_op jit(solution)/shard_map/all_to_all | solution.py:226
  23.6 39.9 %all-gather.2.cloned.1.call-start = ((), (), s32[]{:S(2)}) async-start(), calls=%async_computation.1 | async-start | bytes 1310720 | tf_op jit(solution)/shard_map/all_gather | solution.py:227
  25.5 38.0 %copy-start.4 = (f32[4,128]{1,0:T(4,128)S(1)}, f32[4,128]{1,0:T(4,128)}, u32[]{:S(2)}) copy-start(f32[4,128]{1,0:T(4,128)} %constant.215.clone.rope_ref) | copy-start | bytes 6148
  25.7 5.8 %collective-permute-start.2 = (bf16[16,2048]{1,0:T(8,128)(2,1)S(1)}, bf16[16,2048]{1,0:T(8,128)(2,1)S(1)}, u32[]{:S(2)}, u32[]{:S(2)}) collective-permute-start(bf16[16,2048]{1,0:T(8,128)(2,1)S(1)} %collective-permute-done.1), channel_id=1, source_target_pairs={{0,4},{4,0},{8,12},{12,8},{16,20},{20,16},{24,28},{28,24},{1,5},{5... | collective-permute-start | bytes 196616 | tf_op jit(solution)/shard_map/ppermute | solution.py:23
  27.7 4.7 %collective-permute-start.4 = (bf16[16,2048]{1,0:T(8,128)(2,1)S(1)}, bf16[16,2048]{1,0:T(8,128)(2,1)S(1)}, u32[]{:S(2)}, u32[]{:S(2)}) collective-permute-start(bf16[16,2048]{1,0:T(8,128)(2,1)S(1)} %collective-permute-done.3), channel_id=1, source_target_pairs={{0,4},{4,0},{8,12},{12,8},{16,20},{20,16},{24,28},{28,24},{1,5},{5... | collective-permute-start | bytes 196616 | tf_op jit(solution)/shard_map/ppermute | solution.py:23
  27.9 5.3 %collective-permute-start.6 = (bf16[16,2048]{1,0:T(8,128)(2,1)S(1)}, bf16[16,2048]{1,0:T(8,128)(2,1)S(1)}, u32[]{:S(2)}, u32[]{:S(2)}) collective-permute-start(bf16[16,2048]{1,0:T(8,128)(2,1)S(1)} %collective-permute-done.5), channel_id=1, source_target_pairs={{0,4},{4,0},{8,12},{12,8},{16,20},{20,16},{24,28},{28,24},{1,5},{5... | collective-permute-start | bytes 196616 | tf_op jit(solution)/shard_map/ppermute | solution.py:23
  35.2 5.7 %collective-permute-start.10 = (bf16[128,128]{1,0:T(8,128)(2,1)S(1)}, bf16[128,128]{1,0:T(8,128)(2,1)S(1)}, u32[]{:S(2)}, u32[]{:S(2)}) collective-permute-start(bf16[128,128]{1,0:T(8,128)(2,1)S(1)} %get-tuple-element.46), channel_id=1, source_target_pairs={{0,4},{4,12},{8,20},{12,28},{16,0},{20,8},{24,16},{28,24},{1,5},{5... | collective-permute-start | bytes 98312 | tf_op jit(solution)/shard_map/ppermute | solution.py:250
  36.1 4.7 %collective-permute-start.9 = (bf16[128,128]{1,0:T(8,128)(2,1)S(1)}, bf16[128,128]{1,0:T(8,128)(2,1)S(1)}, u32[]{:S(2)}, u32[]{:S(2)}) collective-permute-start(bf16[128,128]{1,0:T(8,128)(2,1)S(1)} %get-tuple-element.45), channel_id=1, source_target_pairs={{0,0},{4,8},{8,16},{12,24},{16,4},{20,12},{24,20},{28,28},{1,1},{5... | collective-permute-start | bytes 98312 | tf_op jit(solution)/shard_map/ppermute | solution.py:245
  40.8 1.4 collective-permute-start.7
  40.9 2.9 %collective-permute-start.11 = (bf16[128,384]{1,0:T(8,128)(2,1)S(1)}, bf16[128,384]{1,0:T(8,128)(2,1)S(1)}, u32[]{:S(2)}, u32[]{:S(2)}) collective-permute-start(bf16[128,384]{1,0:T(8,128)(2,1)S(1)} %fusion.15), channel_id=1, source_target_pairs={{0,1},{1,0},{2,3},{3,2},{4,5},{5,4},{6,7},{7,6},{8,9},{9,8},{10,11... | collective-permute-start | bytes 294920 | tf_op jit(solution)/shard_map/ppermute | solution.py:23
  42.2 65.9 %copy-start.6 = (f32[2048]{0:T(1024)S(1)}, f32[2048]{0:T(1024)}, u32[]{:S(2)}) copy-start(f32[2048]{0:T(1024)} %param.22) | copy-start | bytes 24580
  42.3 4.3 %collective-permute-start.8 = (bf16[32,1024]{1,0:T(8,128)(2,1)S(1)}, bf16[32,1024]{1,0:T(8,128)(2,1)S(1)}, u32[]{:S(2)}, u32[]{:S(2)}) collective-permute-start(bf16[32,1024]{1,0:T(8,128)(2,1)S(1)} %fusion.18), channel_id=1, source_target_pairs={{0,2},{1,3},{2,0},{3,1},{4,6},{5,7},{6,4},{7,5},{8,10},{9,11},{10,... | collective-permute-start | bytes 196616 | tf_op jit(solution)/shard_map/ppermute | solution.py:23
  44.1 0.7 copy-start.5
  45.0 4.7 %collective-permute-start.12 = (bf16[128,384]{1,0:T(8,128)(2,1)S(1)}, bf16[128,384]{1,0:T(8,128)(2,1)S(1)}, u32[]{:S(2)}, u32[]{:S(2)}) collective-permute-start(bf16[128,384]{1,0:T(8,128)(2,1)S(1)} %pad_maximum_fusion.5), channel_id=1, source_target_pairs={{0,2},{1,3},{2,0},{3,1},{4,6},{5,7},{6,4},{7,5},{8,10},{9,11},{10,... | collective-permute-start | bytes 294920 | tf_op jit(solution)/shard_map/ppermute | solution.py:23
  63.5 1.2 copy-start.1
  66.9 4.3 %collective-permute-start.14 = (bf16[32,1024]{1,0:T(8,128)(2,1)S(1)}, bf16[32,1024]{1,0:T(8,128)(2,1)S(1)}, u32[]{:S(2)}, u32[]{:S(2)}) collective-permute-start(bf16[32,1024]{1,0:T(8,128)(2,1)S(1)} %shard_map.150), channel_id=1, source_target_pairs={{0,2},{1,3},{2,0},{3,1},{4,6},{5,7},{6,4},{7,5},{8,10},{9,11},{10,... | collective-permute-start | bytes 196616 | tf_op jit(solution)/shard_map/ppermute | solution.py:23
  67.3 4.1 %collective-permute-start.13 = (bf16[32,1024]{1,0:T(8,128)(2,1)S(1)}, bf16[32,1024]{1,0:T(8,128)(2,1)S(1)}, u32[]{:S(2)}, u32[]{:S(2)}) collective-permute-start(bf16[32,1024]{1,0:T(8,128)(2,1)S(1)} %shard_map.150), channel_id=1, source_target_pairs={{0,1},{1,0},{2,3},{3,2},{4,5},{5,4},{6,7},{7,6},{8,9},{9,8},{10,11... | collective-permute-start | bytes 196616 | tf_op jit(solution)/shard_map/ppermute | solution.py:23
  71.2 1.3 collective-permute-start.15
  76.1 4.7 %collective-permute-start.17 = (bf16[16,2048]{1,0:T(8,128)(2,1)S(1)}, bf16[16,2048]{1,0:T(8,128)(2,1)S(1)}, u32[]{:S(2)}, u32[]{:S(2)}) collective-permute-start(bf16[16,2048]{1,0:T(8,128)(2,1)S(1)} %get-tuple-element.24), channel_id=1, source_target_pairs={{0,4},{4,0},{8,12},{12,8},{16,20},{20,16},{24,28},{28,24},{1,5},{5... | collective-permute-start | bytes 196616 | tf_op jit(solution)/shard_map/ppermute | solution.py:23
  77.7 5.0 %collective-permute-start.19 = (bf16[16,2048]{1,0:T(8,128)(2,1)S(1)}, bf16[16,2048]{1,0:T(8,128)(2,1)S(1)}, u32[]{:S(2)}, u32[]{:S(2)}) collective-permute-start(bf16[16,2048]{1,0:T(8,128)(2,1)S(1)} %get-tuple-element.23), channel_id=1, source_target_pairs={{0,4},{4,0},{8,12},{12,8},{16,20},{20,16},{24,28},{28,24},{1,5},{5... | collective-permute-start | bytes 196616 | tf_op jit(solution)/shard_map/ppermute | solution.py:23
  78.2 5.8 %collective-permute-start.21 = (bf16[16,2048]{1,0:T(8,128)(2,1)S(1)}, bf16[16,2048]{1,0:T(8,128)(2,1)S(1)}, u32[]{:S(2)}, u32[]{:S(2)}) collective-permute-start(bf16[16,2048]{1,0:T(8,128)(2,1)S(1)} %get-tuple-element.22), channel_id=1, source_target_pairs={{0,4},{4,0},{8,12},{12,8},{16,20},{20,16},{24,28},{28,24},{1,5},{5... | collective-permute-start | bytes 196616 | tf_op jit(solution)/shard_map/ppermute | solution.py:23
  79.7 8.8 %collective-permute-start.16 = (bf16[16,2048]{1,0:T(8,128)(2,1)S(1)}, bf16[16,2048]{1,0:T(8,128)(2,1)S(1)}, u32[]{:S(2)}, u32[]{:S(2)}) collective-permute-start(bf16[16,2048]{1,0:T(8,128)(2,1)S(1)} %get-tuple-element.21), channel_id=1, source_target_pairs={{0,4},{4,0},{8,12},{12,8},{16,20},{20,16},{24,28},{28,24},{1,5},{5... | collective-permute-start | bytes 196616 | tf_op jit(solution)/shard_map/ppermute | solution.py:23
  84.0 6.1 %collective-permute-start.18 = (bf16[16,2048]{1,0:T(8,128)(2,1)S(1)}, bf16[16,2048]{1,0:T(8,128)(2,1)S(1)}, u32[]{:S(2)}, u32[]{:S(2)}) collective-permute-start(bf16[16,2048]{1,0:T(8,128)(2,1)S(1)} %get-tuple-element.25), channel_id=1, source_target_pairs={{0,24},{4,28},{8,16},{12,20},{16,8},{20,12},{24,0},{28,4},{1,25},{... | collective-permute-start | bytes 196616 | tf_op jit(solution)/shard_map/ppermute | solution.py:23
  87.4 5.2 %collective-permute-start.20 = (bf16[16,2048]{1,0:T(8,128)(2,1)S(1)}, bf16[16,2048]{1,0:T(8,128)(2,1)S(1)}, u32[]{:S(2)}, u32[]{:S(2)}) collective-permute-start(bf16[16,2048]{1,0:T(8,128)(2,1)S(1)} %get-tuple-element.27), channel_id=1, source_target_pairs={{0,16},{4,20},{8,24},{12,28},{16,0},{20,4},{24,8},{28,12},{1,17},{... | collective-permute-start | bytes 196616 | tf_op jit(solution)/shard_map/ppermute | solution.py:23
  87.4 5.2 %collective-permute-start.22 = (bf16[16,2048]{1,0:T(8,128)(2,1)S(1)}, bf16[16,2048]{1,0:T(8,128)(2,1)S(1)}, u32[]{:S(2)}, u32[]{:S(2)}) collective-permute-start(bf16[16,2048]{1,0:T(8,128)(2,1)S(1)} %get-tuple-element.26), channel_id=1, source_target_pairs={{0,8},{4,12},{8,0},{12,4},{16,24},{20,28},{24,16},{28,20},{1,9},{5... | collective-permute-start | bytes 196616 | tf_op jit(solution)/shard_map/ppermute | solution.py:23
  93.3 5.8 %collective-permute-start.24 = (bf16[16,2048]{1,0:T(8,128)(2,1)S(1)}, bf16[16,2048]{1,0:T(8,128)(2,1)S(1)}, u32[]{:S(2)}, u32[]{:S(2)}) collective-permute-start(bf16[16,2048]{1,0:T(8,128)(2,1)S(1)} %get-tuple-element.6), channel_id=1, source_target_pairs={{0,8},{4,12},{8,0},{12,4},{16,24},{20,28},{24,16},{28,20},{1,9},{5... | collective-permute-start | bytes 196616 | tf_op jit(solution)/shard_map/ppermute | solution.py:23
  93.8 5.9 %collective-permute-start.23 = (bf16[16,2048]{1,0:T(8,128)(2,1)S(1)}, bf16[16,2048]{1,0:T(8,128)(2,1)S(1)}, u32[]{:S(2)}, u32[]{:S(2)}) collective-permute-start(bf16[16,2048]{1,0:T(8,128)(2,1)S(1)} %get-tuple-element.6), channel_id=1, source_target_pairs={{0,4},{4,0},{8,12},{12,8},{16,20},{20,16},{24,28},{28,24},{1,5},{5... | collective-permute-start | bytes 196616 | tf_op jit(solution)/shard_map/ppermute | solution.py:23
  95.2 5.3 %collective-permute-start.26 = (bf16[16,2048]{1,0:T(8,128)(2,1)S(1)}, bf16[16,2048]{1,0:T(8,128)(2,1)S(1)}, u32[]{:S(2)}, u32[]{:S(2)}) collective-permute-start(bf16[16,2048]{1,0:T(8,128)(2,1)S(1)} %get-tuple-element.6), channel_id=1, source_target_pairs={{0,16},{4,20},{8,24},{12,28},{16,0},{20,4},{24,8},{28,12},{1,17},{... | collective-permute-start | bytes 196616 | tf_op jit(solution)/shard_map/ppermute | solution.py:23
  97.3 6.1 %collective-permute-start.28 = (bf16[16,2048]{1,0:T(8,128)(2,1)S(1)}, bf16[16,2048]{1,0:T(8,128)(2,1)S(1)}, u32[]{:S(2)}, u32[]{:S(2)}) collective-permute-start(bf16[16,2048]{1,0:T(8,128)(2,1)S(1)} %get-tuple-element.6), channel_id=1, source_target_pairs={{0,24},{4,28},{8,16},{12,20},{16,8},{20,12},{24,0},{28,4},{1,25},{... | collective-permute-start | bytes 196616 | tf_op jit(solution)/shard_map/ppermute | solution.py:23
  99.0 5.0 %collective-permute-start.25 = (bf16[16,2048]{1,0:T(8,128)(2,1)S(1)}, bf16[16,2048]{1,0:T(8,128)(2,1)S(1)}, u32[]{:S(2)}, u32[]{:S(2)}) collective-permute-start(bf16[16,2048]{1,0:T(8,128)(2,1)S(1)} %collective-permute-done.24), channel_id=1, source_target_pairs={{0,4},{4,0},{8,12},{12,8},{16,20},{20,16},{24,28},{28,24},{1,5},{5... | collective-permute-start | bytes 196616 | tf_op jit(solution)/shard_map/ppermute | solution.py:23
  100.5 4.3 %collective-permute-start.27 = (bf16[16,2048]{1,0:T(8,128)(2,1)S(1)}, bf16[16,2048]{1,0:T(8,128)(2,1)S(1)}, u32[]{:S(2)}, u32[]{:S(2)}) collective-permute-start(bf16[16,2048]{1,0:T(8,128)(2,1)S(1)} %collective-permute-done.26), channel_id=1, source_target_pairs={{0,4},{4,0},{8,12},{12,8},{16,20},{20,16},{24,28},{28,24},{1,5},{5... | collective-permute-start | bytes 196616 | tf_op jit(solution)/shard_map/ppermute | solution.py:23
  103.4 4.3 %collective-permute-start.29 = (bf16[16,2048]{1,0:T(8,128)(2,1)S(1)}, bf16[16,2048]{1,0:T(8,128)(2,1)S(1)}, u32[]{:S(2)}, u32[]{:S(2)}) collective-permute-start(bf16[16,2048]{1,0:T(8,128)(2,1)S(1)} %collective-permute-done.28), channel_id=1, source_target_pairs={{0,4},{4,0},{8,12},{12,8},{16,20},{20,16},{24,28},{28,24},{1,5},{5... | collective-permute-start | bytes 196616 | tf_op jit(solution)/shard_map/ppermute | solution.py:23
  108.1 4.6 %slice-start = ((s8[7340032]{0:T(1024)(128)(4,1)}), s8[4194304]{0:T(1024)(128)(4,1)S(1)}, s32[]{:S(2)}) async-start(s8[7340032]{0:T(1024)(128)(4,1)} %bitcast.113), calls=%async_computation.2 | async-start | bytes 8388608
  108.2 5.2 %slice-start.1 = ((s8[7340032]{0:T(1024)(128)(4,1)}), s8[3145728]{0:T(1024)(128)(4,1)S(1)}, s32[]{:S(2)}) async-start(s8[7340032]{0:T(1024)(128)(4,1)} %bitcast.113), calls=%async_computation.3 | async-start | bytes 6291456
  114.6 1.6 collective-permute-start.32
  114.7 1.8 %collective-permute-start.30 = (bf16[2,32,1920]{2,1,0:T(8,128)(2,1)S(1)}, bf16[2,32,1920]{2,1,0:T(8,128)(2,1)S(1)}, u32[]{:S(2)}, u32[]{:S(2)}) collective-permute-start(bf16[2,32,1920]{2,1,0:T(8,128)(2,1)S(1)} %pad_maximum_fusion.2), channel_id=1, source_target_pairs={{0,1},{1,0},{2,3},{3,2},{4,5},{5,4},{6,7},{7,6},{8,9},{9,8},{10,11... | collective-permute-start | bytes 737288 | tf_op jit(solution)/shard_map/ppermute | solution.py:23
  116.6 6.2 %collective-permute-start.31 = (bf16[32,1920]{1,0:T(8,128)(2,1)S(1)}, bf16[32,1920]{1,0:T(8,128)(2,1)S(1)}, u32[]{:S(2)}, u32[]{:S(2)}) collective-permute-start(bf16[32,1920]{1,0:T(8,128)(2,1)S(1)} %fusion.13), channel_id=1, source_target_pairs={{0,2},{1,3},{2,0},{3,1},{4,6},{5,7},{6,4},{7,5},{8,10},{9,11},{10,... | collective-permute-start | bytes 368648 | tf_op jit(solution)/shard_map/ppermute | solution.py:23
  117.3 7.3 %collective-permute-start.33 = (bf16[32,1792]{1,0:T(8,128)(2,1)S(1)}, bf16[32,1792]{1,0:T(8,128)(2,1)S(1)}, u32[]{:S(2)}, u32[]{:S(2)}) collective-permute-start(bf16[32,1792]{1,0:T(8,128)(2,1)S(1)} %fusion.14), channel_id=1, source_target_pairs={{0,2},{1,3},{2,0},{3,1},{4,6},{5,7},{6,4},{7,5},{8,10},{9,11},{10,... | collective-permute-start | bytes 344072 | tf_op jit(solution)/shard_map/ppermute | solution.py:23
  124.8 4.9 %collective-permute-start.35 = (bf16[32,1792]{1,0:T(8,128)(2,1)S(1)}, bf16[32,1792]{1,0:T(8,128)(2,1)S(1)}, u32[]{:S(2)}, u32[]{:S(2)}) collective-permute-start(bf16[32,1792]{1,0:T(8,128)(2,1)S(1)} %fusion.8), channel_id=1, source_target_pairs={{0,2},{1,3},{2,0},{3,1},{4,6},{5,7},{6,4},{7,5},{8,10},{9,11},{10,... | collective-permute-start | bytes 344072 | tf_op jit(solution)/shard_map/ppermute | solution.py:23
  125.5 4.2 %collective-permute-start.34 = (bf16[32,1792]{1,0:T(8,128)(2,1)S(1)}, bf16[32,1792]{1,0:T(8,128)(2,1)S(1)}, u32[]{:S(2)}, u32[]{:S(2)}) collective-permute-start(bf16[32,1792]{1,0:T(8,128)(2,1)S(1)} %fusion.8), channel_id=1, source_target_pairs={{0,1},{1,0},{2,3},{3,2},{4,5},{5,4},{6,7},{7,6},{8,9},{9,8},{10,11... | collective-permute-start | bytes 344072 | tf_op jit(solution)/shard_map/ppermute | solution.py:23
  129.6 1.3 collective-permute-start.36
  136.1 5.0 %collective-permute-start.38 = (bf16[16,2048]{1,0:T(8,128)(2,1)S(1)}, bf16[16,2048]{1,0:T(8,128)(2,1)S(1)}, u32[]{:S(2)}, u32[]{:S(2)}) collective-permute-start(bf16[16,2048]{1,0:T(8,128)(2,1)S(1)} %get-tuple-element.17), channel_id=1, source_target_pairs={{0,4},{4,0},{8,12},{12,8},{16,20},{20,16},{24,28},{28,24},{1,5},{5... | collective-permute-start | bytes 196616 | tf_op jit(solution)/shard_map/ppermute | solution.py:23
  136.8 5.7 %collective-permute-start.40 = (bf16[16,2048]{1,0:T(8,128)(2,1)S(1)}, bf16[16,2048]{1,0:T(8,128)(2,1)S(1)}, u32[]{:S(2)}, u32[]{:S(2)}) collective-permute-start(bf16[16,2048]{1,0:T(8,128)(2,1)S(1)} %get-tuple-element.16), channel_id=1, source_target_pairs={{0,4},{4,0},{8,12},{12,8},{16,20},{20,16},{24,28},{28,24},{1,5},{5... | collective-permute-start | bytes 196616 | tf_op jit(solution)/shard_map/ppermute | solution.py:23
  138.2 5.6 %collective-permute-start.42 = (bf16[16,2048]{1,0:T(8,128)(2,1)S(1)}, bf16[16,2048]{1,0:T(8,128)(2,1)S(1)}, u32[]{:S(2)}, u32[]{:S(2)}) collective-permute-start(bf16[16,2048]{1,0:T(8,128)(2,1)S(1)} %get-tuple-element.15), channel_id=1, source_target_pairs={{0,4},{4,0},{8,12},{12,8},{16,20},{20,16},{24,28},{28,24},{1,5},{5... | collective-permute-start | bytes 196616 | tf_op jit(solution)/shard_map/ppermute | solution.py:23
  138.8 9.5 %collective-permute-start.37 = (bf16[16,2048]{1,0:T(8,128)(2,1)S(1)}, bf16[16,2048]{1,0:T(8,128)(2,1)S(1)}, u32[]{:S(2)}, u32[]{:S(2)}) collective-permute-start(bf16[16,2048]{1,0:T(8,128)(2,1)S(1)} %get-tuple-element.14), channel_id=1, source_target_pairs={{0,4},{4,0},{8,12},{12,8},{16,20},{20,16},{24,28},{28,24},{1,5},{5... | collective-permute-start | bytes 196616 | tf_op jit(solution)/shard_map/ppermute | solution.py:23
  143.9 6.4 %collective-permute-start.39 = (bf16[16,2048]{1,0:T(8,128)(2,1)S(1)}, bf16[16,2048]{1,0:T(8,128)(2,1)S(1)}, u32[]{:S(2)}, u32[]{:S(2)}) collective-permute-start(bf16[16,2048]{1,0:T(8,128)(2,1)S(1)} %get-tuple-element.18), channel_id=1, source_target_pairs={{0,24},{4,28},{8,16},{12,20},{16,8},{20,12},{24,0},{28,4},{1,25},{... | collective-permute-start | bytes 196616 | tf_op jit(solution)/shard_map/ppermute | solution.py:23
  145.8 5.8 %collective-permute-start.41 = (bf16[16,2048]{1,0:T(8,128)(2,1)S(1)}, bf16[16,2048]{1,0:T(8,128)(2,1)S(1)}, u32[]{:S(2)}, u32[]{:S(2)}) collective-permute-start(bf16[16,2048]{1,0:T(8,128)(2,1)S(1)} %get-tuple-element.20), channel_id=1, source_target_pairs={{0,16},{4,20},{8,24},{12,28},{16,0},{20,4},{24,8},{28,12},{1,17},{... | collective-permute-start | bytes 196616 | tf_op jit(solution)/shard_map/ppermute | solution.py:23
  145.8 5.8 %collective-permute-start.43 = (bf16[16,2048]{1,0:T(8,128)(2,1)S(1)}, bf16[16,2048]{1,0:T(8,128)(2,1)S(1)}, u32[]{:S(2)}, u32[]{:S(2)}) collective-permute-start(bf16[16,2048]{1,0:T(8,128)(2,1)S(1)} %get-tuple-element.19), channel_id=1, source_target_pairs={{0,8},{4,12},{8,0},{12,4},{16,24},{20,28},{24,16},{28,20},{1,9},{5... | collective-permute-start | bytes 196616 | tf_op jit(solution)/shard_map/ppermute | solution.py:23
Sparse Core Ops, SparseCore 0:
  45.0 18.4 all-gather.1

commit v3 on v2

v3 whole, which is shorter than its diff:
```python
import functools
import math

import jax
import jax.numpy as jnp
import numpy as np
from jax import lax
from jax.experimental import pallas as pl
from jax.experimental.pallas import tpu as pltpu
from jax.sharding import PartitionSpec as P

KVH = 8
HD = 128
EPS = 1e-05
ROPE_BASE = 500000.0
MASKED = -1e30
BF16 = jnp.bfloat16
F32 = jnp.float32


def swap(x, axis, bits):
    size = lax.axis_size(axis)
    return lax.ppermute(x, axis, [(i, i ^ bits) for i in range(size)])


def rope_tables(position):
    half = HD // 2
    freq = np.power(np.float32(ROPE_BASE), -2.0 * np.arange(half, dtype=np.float32) / HD)
    angle = (np.float32(position) * freq.astype(np.float32)).astype(np.float32)
    cosine, sine = np.cos(angle), np.sin(angle)
    return (
        np.concatenate([cosine, cosine]).astype(np.float32),
        np.concatenate([-sine, sine]).astype(np.float32),
    )


SMEM = pl.BlockSpec(memory_space=pltpu.SMEM)
VMEM = pl.BlockSpec(memory_space=pltpu.VMEM)
ANY = pl.BlockSpec(memory_space=pl.ANY)


def call(body, outs, ins, specs, scratch=(), limit=16 << 20, flops=0, moved=0):
    return pl.pallas_call(
        body,
        out_shape=outs,
        in_specs=specs,
        out_specs=jax.tree.map(lambda _: VMEM, outs),
        scratch_shapes=scratch,
        compiler_params=pltpu.CompilerParams(vmem_limit_bytes=limit),
        cost_estimate=pl.CostEstimate(flops=flops, bytes_accessed=moved, transcendentals=0),
    )(*ins)


def shaped(shape, dtype=BF16):
    return jax.ShapeDtypeStruct(shape, dtype)


def gather_rows(rows):
    groups = lax.axis_size("dp")
    blocks = {0: rows}
    for k in range(groups - 2, 0, -2):
        blocks[k] = swap(rows, "dp", k)
    blocks[1] = swap(rows, "dp", 1)
    for k in range(groups - 2, 0, -2):
        blocks[k + 1] = swap(blocks[k], "dp", 1)
    return [blocks[k] for k in range(groups)]


def gather_blocks(block):
    tensor = lax.axis_size("tensor")
    blocks = {0: block}
    for k in range(2, tensor, 2):
        blocks[k] = swap(block, "tensor", k)
    blocks[1] = swap(block, "tensor", 1)
    for k in range(2, tensor, 2):
        blocks[k + 1] = swap(blocks[k], "tensor", 1)
    return [blocks[k] for k in range(tensor)]


def sum_blocks(keep, send):
    tensor = lax.axis_size("tensor")
    rows = keep.shape[0] // (tensor // 2)
    paired = (keep + swap(send, "tensor", 1).astype(F32)).reshape(tensor // 2, rows, -1)
    return paired[0], [swap(paired[i].astype(BF16), "tensor", 2 * i) for i in range(1, tensor // 2)]


def slot(relative, size):
    return lax.shift_right_logical(relative, 1) + (relative & 1) * (size // 2)


def tiles(columns):
    for tile in (256, 384, 128):
        if columns % tile == 0:
            return tile
    return columns


def multiply(left_ref, w_ref, write):
    columns = w_ref.shape[1]
    tile = tiles(columns)
    left = left_ref[...]

    def turn(i, _):
        first = pl.multiple_of(i * tile, tile)
        write(first, tile, jnp.dot(left, w_ref[:, pl.ds(first, tile)], preferred_element_type=F32))
        return 0

    if tile == columns:
        write(0, tile, jnp.dot(left, w_ref[...], preferred_element_type=F32))
    else:
        lax.fori_loop(0, columns // tile, turn, 0)


def hold(w, after):
    pieces = 4 if w.shape[0] % 64 == 0 else 1
    rows = w.shape[0] // pieces

    def body(w_ref, after_ref, out_ref, sems):
        copies = [
            pltpu.make_async_copy(w_ref.at[pl.ds(i * rows, rows)], out_ref.at[pl.ds(i * rows, rows)], sems.at[i])
            for i in range(pieces)
        ]
        for copy in copies:
            copy.start()
        for copy in copies:
            copy.wait()

    return call(
        body, shaped(w.shape), (w, after), [ANY, ANY], [pltpu.SemaphoreType.DMA((pieces,))], moved=2 * w.size
    )


def stack_tokens(x_first, x_second):
    part_dev, features = x_first.shape

    def body(first_ref, second_ref, out_ref, one, two, sems):
        copies = [pltpu.make_async_copy(first_ref, one, sems.at[0]), pltpu.make_async_copy(second_ref, two, sems.at[1])]
        for copy in copies:
            copy.start()
        for copy in copies:
            copy.wait()
        out_ref[...] = jnp.concatenate([one[...].astype(F32), two[...].astype(F32)], axis=0).astype(BF16)

    return call(
        body,
        shaped((2 * part_dev, features)),
        (x_first, x_second),
        [ANY, ANY],
        [pltpu.VMEM(x_first.shape, BF16), pltpu.VMEM(x_first.shape, BF16), pltpu.SemaphoreType.DMA((2,))],
        moved=4 * x_first.size * 2,
    )


def pack(cache_keys, cache_values, where, after):
    groups = lax.axis_size("dp")
    part_dev, span, _ = cache_keys.shape
    shape = (groups // 2, 2, part_dev, span, HD)

    def body(where_ref, keys_hbm, values_hbm, after_ref, keep_ref, send_ref, keys_ref, values_ref, sems):
        copies = [
            pltpu.make_async_copy(keys_hbm, keys_ref, sems.at[0]),
            pltpu.make_async_copy(values_hbm, values_ref, sems.at[1]),
        ]
        for copy in copies:
            copy.start()
        for copy in copies:
            copy.wait()
        for k in range(groups):
            head = lax.div((where_ref[0] ^ k) * KVH, groups)
            lanes = pl.ds(pl.multiple_of(head * HD, HD), HD)
            out_ref = send_ref if k % 2 else keep_ref
            out_ref[k // 2, 0] = keys_ref[:, :, lanes]
            out_ref[k // 2, 1] = values_ref[:, :, lanes]

    return call(
        body,
        (shaped(shape), shaped(shape)),
        (where, cache_keys, cache_values, after),
        [SMEM, ANY, ANY, ANY],
        [pltpu.VMEM(cache_keys.shape, BF16), pltpu.VMEM(cache_keys.shape, BF16), pltpu.SemaphoreType.DMA((2,))],
        moved=8 * cache_keys.size,
    )


def move_cache(keep, send):
    groups = lax.axis_size("dp")
    tensor = lax.axis_size("tensor")
    both = jnp.stack([keep, swap(send, "dp", 1)], axis=1)
    both = jnp.concatenate([both[:1]] + [swap(both[i : i + 1], "dp", 2 * i) for i in range(1, groups // 2)])
    both = both.reshape(groups * both.shape[2] * both.shape[3], *both.shape[4:])
    return gather_blocks(both)


def lift(where_ref, gain_ref, block_refs, h_ref, ss_ref, absolute):
    groups = len(block_refs)
    tensor = lax.axis_size("tensor")
    pair = block_refs[0].shape[0]
    near = groups // tensor
    d, t = where_ref[0], where_ref[1]
    gain = gain_ref[...]
    places = []
    for k in range(groups):
        g = d ^ k
        place = slot(lax.div(g, near) ^ t, tensor) * near + lax.rem(g, near)
        place = pl.multiple_of(place * pair, pair)
        wide = block_refs[k][...].astype(F32)
        squares = jnp.broadcast_to(jnp.sum(wide * wide, axis=1, keepdims=True), (pair, 128))
        ss_ref[pl.ds(pl.multiple_of(g * pair, pair) if absolute else place, pair), :] = squares
        h_ref[pl.ds(place, pair), :] = (wide * gain).astype(BF16)
        places.append((pl.multiple_of(g * pair, pair), place))
    return places


def project_keyval(where, blocks, gain, w):
    pair, features = blocks[0].shape
    rows = len(blocks) * pair
    columns = w.shape[1]

    def body(where_ref, gain_ref, *refs):
        block_refs, (w_ref, h_ref, ss_ref, kv_ref, product) = refs[: len(blocks)], refs[len(blocks) :]
        places = lift(where_ref, gain_ref, block_refs, h_ref, ss_ref, True)
        product[...] = jnp.dot(h_ref[...], w_ref[...], preferred_element_type=F32)
        for to, place in places:
            kv_ref[pl.ds(to, pair), :] = product[pl.ds(place, pair), :].astype(BF16)

    return call(
        body,
        (shaped((rows, features)), shaped((rows, 128), F32), shaped((rows, columns))),
        (where, gain[None], *blocks, w),
        [SMEM] + [VMEM] * (2 + len(blocks)),
        [pltpu.VMEM((rows, columns), F32)],
        flops=2 * rows * w.size,
        moved=4 * rows * features + 2 * w.size,
    )


def project(h, w):
    half = h.shape[0] // 2

    def body(h_ref, w_ref, keep_ref, send_ref):
        def write(first, tile, product):
            keep_ref[:, pl.ds(first, tile)] = product[:half]
            send_ref[:, pl.ds(first, tile)] = product[half:].astype(BF16)

        multiply(h_ref, w_ref, write)

    columns = w.shape[1]
    return call(
        body,
        (shaped((half, columns), F32), shaped((half, columns))),
        (h, w),
        [VMEM] * 2,
        flops=4 * half * w.size,
        moved=2 * w.size,
    )


def project_gate(where, blocks, gain, w):
    pair, features = blocks[0].shape
    rows = len(blocks) * pair
    half = rows // 2
    columns = w.shape[1]

    def body(where_ref, gain_ref, *refs):
        block_refs, (w_ref, h_ref, keep_ref, send_ref, ss_ref) = refs[: len(blocks)], refs[len(blocks) :]
        lift(where_ref, gain_ref, block_refs, h_ref, ss_ref, False)

        def write(first, tile, product):
            keep_ref[:, pl.ds(first, tile)] = product[:half]
            send_ref[:, pl.ds(first, tile)] = product[half:].astype(BF16)

        multiply(h_ref, w_ref, write)
        squares = ss_ref[...]
        high = squares.astype(BF16).astype(F32)
        lane = lax.broadcasted_iota(jnp.int32, squares.shape, 1)
        ends = jnp.where(lane == 0, high, jnp.where(lane == 1, squares - high, 0.0))
        keep_ref[:, columns:] = ends[:half]
        send_ref[:, columns:] = ends[half:].astype(BF16)

    return call(
        body,
        (shaped((rows, features)), shaped((half, columns + 128), F32), shaped((half, columns + 128))),
        (where, gain[None], *blocks, w),
        [SMEM] + [VMEM] * (2 + len(blocks)),
        [pltpu.VMEM((rows, 128), F32)],
        flops=2 * rows * w.size,
        moved=4 * rows * features + 2 * w.size,
    )


def project_back(where, blocks, w):
    groups = lax.axis_size("dp")
    rows, depth = blocks[0].shape
    near = groups // len(blocks)
    pair = rows // near
    total = len(blocks) * rows
    half = total // 2
    columns = w.shape[1]

    def body(where_ref, *refs):
        block_refs, (w_ref, keep_ref, far_ref, close_ref, left) = refs[: len(blocks)], refs[len(blocks) :]
        d, t = where_ref[0], where_ref[1]
        for k, block_ref in enumerate(block_refs):
            for i in range(near):
                place = slot(((t ^ k) * near + i) ^ d, groups)
                left[pl.ds(pl.multiple_of(place * pair, pair), pair), :] = block_ref[i * pair : (i + 1) * pair, :]

        def write(first, tile, product):
            keep_ref[:, pl.ds(first, tile)] = product[:half]
            middle = half + half // 2
            close_ref[:, pl.ds(first, tile)] = product[half:middle].astype(BF16)
            far_ref[:, pl.ds(first, tile)] = product[middle:].astype(BF16)

        multiply(left, w_ref, write)

    return call(
        body,
        (shaped((half, columns), F32), shaped((half // 2, columns)), shaped((half // 2, columns))),
        (where, *blocks, w),
        [SMEM] + [VMEM] * (1 + len(blocks)),
        [pltpu.VMEM((total, depth), BF16)],
        flops=2 * total * w.size,
        moved=2 * w.size,
    )


def add_pairs(keep, arrived, first, pair, own):
    count = arrived.shape[0] // pair
    columns = keep.shape[1]

    def body(keep_ref, arrived_ref, *out_refs):
        for i, out_ref in enumerate(out_refs):
            start = (first + i) * pair
            summed = keep_ref[start : start + pair, :] + arrived_ref[i * pair : (i + 1) * pair, :].astype(F32)
            out_ref[...] = summed.astype(out_ref.dtype)

    outs = tuple(shaped((pair, columns), F32 if own and i == 0 else BF16) for i in range(count))
    return call(body, outs, (keep, arrived), [VMEM] * 2, moved=8 * arrived.size)


def sum_rows(keep, far, close, pair):
    groups = lax.axis_size("dp")
    far = swap(far, "dp", 1)
    close = swap(close, "dp", 1)
    quarter = groups // 4
    sums = add_pairs(keep, far, quarter, pair, False)
    arrived = [swap(sums[i], "dp", 2 * (quarter + i)) for i in range(quarter)]
    own = add_pairs(keep, close, 0, pair, True)
    arrived += [swap(own[i], "dp", 2 * i) for i in range(1, quarter)]
    return own[0], arrived


def finish(own, arrived, x=None):
    rows, columns = own.shape

    def body(own_ref, *refs):
        total = own_ref[...]
        for ref in refs[: len(arrived)]:
            total = total + ref[...].astype(F32)
        rounded = total.astype(BF16)
        if x is None:
            refs[-1][...] = rounded
        else:
            refs[-2][...] = rounded
            refs[-1][...] = (refs[len(arrived)][...].astype(F32) + rounded.astype(F32)).astype(BF16)

    outs = (shaped(own.shape),) * (1 if x is None else 2)
    ins = (own, *arrived) + (() if x is None else (x,))
    return call(body, outs, ins, [VMEM] * len(ins), moved=8 * own.size)


def attention_kernel(sizes, where_ref, anc_ref, rope_ref, target_ref, *refs):
    tensor, groups, part_dev, span, n_q, n_kv = sizes
    q_refs, kv_refs = refs[:n_q], refs[n_q : n_q + n_kv]
    cache_refs, (out_ref, keys_ref, values_ref, scale_ref) = refs[n_q + n_kv : n_q + n_kv + tensor], refs[n_q + n_kv + tensor :]
    d, t = where_ref[0], where_ref[1]
    near = groups // tensor
    parts = near * part_dev
    pair = 2 * part_dev
    ctx = tensor * span
    scale = 1.0 / math.sqrt(HD)
    summed = kv_refs[0][...].astype(F32)
    squares = summed[:, 2 * HD : 2 * HD + 1] + summed[:, 2 * HD + 1 : 2 * HD + 2]
    new_kv = summed[:, : 2 * HD]
    for ref in kv_refs[1:]:
        more = ref[...].astype(F32)
        squares = squares + (more[:, 2 * HD : 2 * HD + 1] + more[:, 2 * HD + 1 : 2 * HD + 2])
        new_kv = new_kv + more[:, : 2 * HD]
    width = rope_ref[4:5, 0:1]
    norm = lax.rsqrt(squares / width + EPS)
    scale_ref[...] = jnp.broadcast_to(norm, (groups * pair, 128))
    new_kv = (new_kv * norm).astype(BF16)
    new_values = new_kv[:, HD:]
    plain = new_kv[:, :HD].astype(F32)
    cos_key = jnp.concatenate([jnp.broadcast_to(rope_ref[2 * s : 2 * s + 1, :], (part_dev, HD)) for s in range(2)])
    sin_key = jnp.concatenate([jnp.broadcast_to(rope_ref[2 * s + 1 : 2 * s + 2, :], (part_dev, HD)) for s in range(2)])
    turned = pltpu.roll(plain, HD // 2, 1).reshape(groups, pair, HD)
    new_keys = plain.reshape(groups, pair, HD) * cos_key[None] + turned * sin_key[None]
    new_keys = new_keys.reshape(groups * pair, HD).astype(BF16)
    queries = q_refs[0][...]
    for ref in q_refs[1:]:
        queries = queries + ref[...].astype(F32)
    heads = queries.shape[1] // HD
    rows = heads * parts
    queries = queries * scale_ref[pl.ds(pl.multiple_of(t * near * pair, pair), near * pair), 0:1]
    pieces = []
    for step in range(2):

        def bring(i, _, step=step):
            if step == 0:
                block, member = (t * near + lax.div(i, part_dev)) ^ d, lax.rem(i, part_dev)
            else:
                block, member = lax.div(anc_ref[i], part_dev) ^ d, lax.rem(anc_ref[i], part_dev)
            place = block * pair + member
            for k in range(tensor):
                start = pl.multiple_of(i * ctx + k * span, 8)
                keys_ref[pl.ds(start, span), :] = cache_refs[k][place].astype(F32)
                values_ref[pl.ds(start, span), :] = cache_refs[k][place + part_dev].astype(F32)
            return 0

        lax.fori_loop(0, parts, bring, 0)
        keys = keys_ref[...].astype(BF16)
        values = values_ref[...].astype(BF16)
        cosine = rope_ref[2 * step : 2 * step + 1, :]
        sine = rope_ref[2 * step + 1 : 2 * step + 2, :]
        per_head = []
        for h in range(heads):
            for b in range(near):
                first = b * pair + step * part_dev
                per_head.append(queries[first : first + part_dev, h * HD : (h + 1) * HD])
        query = jnp.concatenate(per_head, axis=0)
        query = query.astype(BF16).astype(F32)
        query = (query * cosine + pltpu.roll(query, HD // 2, 1) * sine).astype(BF16)
        contract = (((1,), (1,)), ((), ()))
        cached = lax.dot_general(query, keys, contract, preferred_element_type=F32) * scale
        fresh = lax.dot_general(query, new_keys, contract, preferred_element_type=F32) * scale
        row_part = lax.rem(lax.broadcasted_iota(jnp.int32, (rows, 1), 0), parts)
        col_part = lax.div(lax.broadcasted_iota(jnp.int32, (1, parts * ctx), 1), ctx)
        cached = jnp.where(row_part == col_part, cached, MASKED)
        col = lax.broadcasted_iota(jnp.int32, (1, groups * pair), 1)
        wanted = col == target_ref[:, step : step + 1]
        if step == 1:
            wanted = wanted | (col == target_ref[:, 2:3])
        fresh = jnp.where(wanted, fresh, MASKED)
        highest = jnp.maximum(jnp.max(cached, axis=1, keepdims=True), jnp.max(fresh, axis=1, keepdims=True))
        cached = jnp.exp(cached - highest)
        fresh = jnp.exp(fresh - highest)
        total = jnp.sum(cached, axis=1, keepdims=True) + jnp.sum(fresh, axis=1, keepdims=True)
        mixed = jnp.dot(cached.astype(BF16), values, preferred_element_type=F32)
        mixed += jnp.dot(fresh.astype(BF16), new_values, preferred_element_type=F32)
        pieces.append(mixed / total)
    for h in range(heads):
        for b in range(near):
            first = h * parts + b * part_dev
            both = jnp.concatenate([piece[first : first + part_dev] for piece in pieces], axis=0)
            out_ref[b * pair : (b + 1) * pair, h * HD : (h + 1) * HD] = both.astype(BF16)


def attention(where, anc, rope, targets, queries, new_kv, cache, part_dev):
    tensor = lax.axis_size("tensor")
    groups = lax.axis_size("dp")
    span = cache[0].shape[1]
    rows, columns = queries[0].shape
    parts = rows // 2
    heads = columns // HD
    limit = (16 << 20) + 4 * (3 * heads * parts * parts * tensor * span)
    ins = (where, anc, rope, targets, *queries, *new_kv, *cache)
    return call(
        functools.partial(attention_kernel, (tensor, groups, part_dev, span, len(queries), len(new_kv))),
        shaped((rows, columns)),
        ins,
        [SMEM] * 2 + [VMEM] * (len(ins) - 2),
        [
            pltpu.VMEM((parts * tensor * span, HD), F32),
            pltpu.VMEM((parts * tensor * span, HD), F32),
            pltpu.VMEM((groups * 2 * part_dev, 128), F32),
        ],
        limit=limit,
        flops=1 << 30,
        moved=4 << 20,
    )


def split_ss(x):
    high = x.astype(BF16)
    low = (x - high.astype(F32)).astype(BF16)
    return jnp.pad(jnp.stack([high, low], axis=-1), ((0, 0), (0, 126)))


def move_keyvals(kv):
    groups = lax.axis_size("dp")
    d = lax.axis_index("dp")
    if groups == KVH:
        halves = (kv[:, :HD], kv[:, HD:])
        half = groups // 2
        lower = d < half
        one = lax.ppermute(
            jnp.where(lower, halves[0], halves[1]),
            "dp",
            [(i, 2 * i) for i in range(half)] + [(half + i, 2 * i + 1) for i in range(half)],
        )
        two = lax.ppermute(
            jnp.where(lower, halves[1], halves[0]),
            "dp",
            [(i, 2 * i + 1) for i in range(half)] + [(half + i, 2 * i) for i in range(half)],
        )
        even = d % 2 == 0
        return jnp.concatenate([jnp.where(even, one, two), jnp.where(even, two, one)], axis=1)
    every = lax.all_gather(kv, "dp", axis=1, tiled=True)
    start = (d * KVH // groups) * HD
    return jnp.concatenate(
        [lax.dynamic_slice_in_dim(every, first + start, HD, axis=1) for first in (0, KVH * HD)], axis=1
    )


def local(
    x_first,
    x_second,
    cache_keys,
    cache_values,
    ancestors,
    attn_gain,
    ffn_gain,
    w_query,
    w_keyval,
    w_out,
    w_gate,
    w_up,
    w_down,
):
    groups = lax.axis_size("dp")
    tensor = lax.axis_size("tensor")
    part_dev, features = x_first.shape
    span = cache_keys.shape[1]
    width = features * tensor
    context = span * tensor
    d = lax.axis_index("dp")
    t = lax.axis_index("tensor")
    pair = 2 * part_dev
    near = groups // tensor
    parts = near * part_dev
    where = jnp.stack([d, t]).astype(jnp.int32)

    x = stack_tokens(x_first, x_second)
    blocks = gather_rows(x)
    held_keyval = hold(w_keyval, x)
    held_query = hold(w_query, x)
    cache = move_cache(*pack(cache_keys, cache_values, where, x))

    h, squares, keyvals = project_keyval(where, blocks, attn_gain, held_keyval)
    new_kv = move_keyvals(keyvals)
    queries, queries_arrived = sum_blocks(*project(h, held_query))
    held_out = hold(w_out, h)
    message = jnp.concatenate([new_kv, split_ss(squares[:, 0])], axis=1)
    bits = 1
    while bits < tensor:
        arrived = swap(message, "tensor", bits)
        bits *= 2
        if bits == tensor:
            break
        summed = message.astype(F32) + arrived.astype(F32)
        squares = summed[:, 2 * HD] + summed[:, 2 * HD + 1]
        message = jnp.concatenate([summed[:, : 2 * HD].astype(BF16), split_ss(squares)], axis=1)

    own = t * parts + jnp.arange(parts, dtype=jnp.int32)
    anc = lax.dynamic_slice_in_dim(ancestors, t * parts, parts).astype(jnp.int32)
    heads = w_query.shape[1] // HD

    def row_of(particle, step):
        return (particle // part_dev) * pair + step * part_dev + particle % part_dev

    targets = jnp.stack([row_of(own, 0), row_of(anc, 0), row_of(own, 1)], axis=1)
    targets = jnp.tile(targets, (heads, 1)).astype(jnp.int32)
    rope = rope_tables(context) + rope_tables(context + 1)
    rope = jnp.asarray(np.stack(rope + (np.full(HD, width, np.float32),) * 4))
    mixed = attention(where, anc, rope, targets, [queries] + queries_arrived, [message, arrived], cache, part_dev)

    keep, far, close = project_back(where, gather_blocks(mixed), held_out)
    held_gate = hold(w_gate, far)
    held_up = hold(w_up, far)
    attn_part, residual = finish(*sum_rows(keep, far, close, pair), x)

    hidden_cols = w_gate.shape[1]
    h, keep, send = project_gate(where, gather_rows(residual), ffn_gain, held_gate)
    gate, gate_arrived = sum_blocks(keep, send)
    up, up_arrived = sum_blocks(*project(h, held_up))
    held_down = hold(w_down, h)
    for piece in gate_arrived:
        gate = gate + piece.astype(F32)
    for piece in up_arrived:
        up = up + piece.astype(F32)
    scale = lax.rsqrt((gate[:, hidden_cols] + gate[:, hidden_cols + 1]) / width + EPS)[:, None]
    hidden = jax.nn.silu(gate[:, :hidden_cols] * scale) * (up * scale)
    keep, far, close = project_back(where, gather_blocks(hidden.astype(BF16)), held_down)
    (ffn_part,) = finish(*sum_rows(keep, far, close, pair))
    return (attn_part.reshape(2, part_dev, features), ffn_part.reshape(2, part_dev, features))


def solution(mesh):
    return jax.shard_map(
        local,
        mesh=mesh,
        in_specs=(
            P("dp", "tensor"),
            P("dp", "tensor"),
            P("dp", "tensor", None),
            P("dp", "tensor", None),
            P(),
            P("tensor"),
            P("tensor"),
            P("tensor", "dp"),
            P("tensor", "dp"),
            P("dp", "tensor"),
            P("tensor", "dp"),
            P("tensor", "dp"),
            P("dp", "tensor"),
        ),
        out_specs=(P(None, "dp", "tensor"), P(None, "dp", "tensor")),
        check_vma=False,
    )
```

time: 160 us -> 139 us (0.87)
  Pallas kernels: 2.95 us -> 20.4 us
  matrix products: 16.1 us -> 0 us
  between operations: 14.7 us -> 1.15 us
  waiting for transfers between devices: 59.1 us -> 48.2 us
  starting transfers between devices: 49.6 us -> 53.8 us
  other arithmetic: 4.78 us -> 0.95 us
  local copies, waits for them, and re-layouts: 11.9 us -> 13.7 us
    pallas_call x2 -> x21, Pallas kernels: 2.95 us -> 20.4 us  [call(): pl.pallas_call(body, out_shape=outs, in_specs=specs, out_specs=jax.tree.m...]
    dot_general x6 -> x0, matrix products: 16.1 us -> none  [the longest x1 4.38 us: local(): gate = jnp.dot(lifted, w_gate, preferred_element_type=F32).astype(BF16)]
    all_gather x1 -> x0, waiting for transfers between devices: 12.6 us -> none  [local(): lax.all_gather(cache.reshape(groups * pair, span, HD), 'tensor', axis=0)]
    ppermute x42 -> x45, starting transfers between devices: 43.1 us -> 51.8 us  [swap(): return lax.ppermute(x, axis, [(i, i ^ bits) for i in range(size)])]
    unnamed x32 -> x38, local copies, waits for them, and re-layouts: 5.37 us -> 13.2 us
    all_to_all x1 -> x0, starting transfers between devices: 4.88 us -> none  [local(): cache = lax.all_to_all(sent, 'dp', split_axis=0, concat_axis=0, tiled=True)]
    gather x6 -> x0, local copies, waits for them, and re-layouts: 4.13 us -> none  [the longest x1 1.32 us: local(): anc = jnp.take(ancestors, own, axis=0)]
    ppermute x42 -> x45, waiting for transfers between devices: 46.5 us -> 48.2 us  [swap(): return lax.ppermute(x, axis, [(i, i ^ bits) for i in range(size)])]
  transfers between devices with their start and end apart: 46 -> 47, of which waited for: 29 -> 23; matrix products, arithmetic and copies ran while one was open for 6% -> 1% of each run, Pallas kernels for 0% -> 6%
where the time goes in v3:
time: 139 us; the launch traced here: 138 us
  starting transfers between devices  53.8 us (39%)
  waiting for transfers between devices  48.2 us (35%)
  Pallas kernels  20.4 us (15%)
  local copies, waits for them, and re-layouts  13.7 us (10%)
    ppermute x45, starting transfers between devices, swap(): return lax.ppermute(x, axis, [(i, i ^ bits) for i in range(size)])  51.8 us
    ppermute x45, waiting for transfers between devices, swap(): return lax.ppermute(x, axis, [(i, i ^ bits) for i in range(size)])  48.2 us
    pallas_call x21, Pallas kernels, call(): pl.pallas_call(body, out_shape=outs, in_specs=specs, out_specs=jax.tree.m...  20.4 us
    unnamed x38, local copies, waits for them, and re-layouts  13.2 us
  transfers between devices with their start and end apart: 47, of which 23 were waited for; matrix products, arithmetic and copies ran while one was open for 1% of the time, Pallas kernels for 6%

profile of v3, /device:TPU:0, one launch (start us, length us, event | category | flops | bytes accessed | tf_op | source)
XLA Modules:
  0.0 138.3 jit_solution(9258620770996089434)
XLA Ops:
  0.6 0.7 copy-done.7
  1.4 0.8 copy-done.8
  2.3 3.1 %collective-permute-start.1 = (bf16[16,2048]{1,0:T(8,128)(2,1)S(1)}, bf16[16,2048]{1,0:T(8,128)(2,1)S(1)}, u32[]{:S(2)}, u32[]{:S(2)}) collective-permute-start(bf16[16,2048]{1,0:T(8,128)(2,1)S(1)} %shard_map.149.after_ref.refs_0_.refs_3_), channel_id=1, source_target_pairs={{0,8},{4,12},{8,0},{12,4},{16,24},{20,28},{24,16},{28,20},{1,9},{5... | collective-permute-start | bytes 196616 | tf_op jit(solution)/shard_map/ppermute | solution.py:23
  5.3 2.6 %collective-permute-start.3 = (bf16[16,2048]{1,0:T(8,128)(2,1)S(1)}, bf16[16,2048]{1,0:T(8,128)(2,1)S(1)}, u32[]{:S(2)}, u32[]{:S(2)}) collective-permute-start(bf16[16,2048]{1,0:T(8,128)(2,1)S(1)} %shard_map.149.after_ref.refs_0_.refs_3_), channel_id=1, source_target_pairs={{0,16},{4,20},{8,24},{12,28},{16,0},{20,4},{24,8},{28,12},{1,17},{... | collective-permute-start | bytes 196616 | tf_op jit(solution)/shard_map/ppermute | solution.py:23
  7.9 1.7 %collective-permute-start = (bf16[16,2048]{1,0:T(8,128)(2,1)S(1)}, bf16[16,2048]{1,0:T(8,128)(2,1)S(1)}, u32[]{:S(2)}, u32[]{:S(2)}) collective-permute-start(bf16[16,2048]{1,0:T(8,128)(2,1)S(1)} %shard_map.149.after_ref.refs_0_.refs_3_), channel_id=1, source_target_pairs={{0,4},{4,0},{8,12},{12,8},{16,20},{20,16},{24,28},{28,24},{1,5},{5... | collective-permute-start | bytes 196616 | tf_op jit(solution)/shard_map/ppermute | solution.py:23
  9.7 0.9 copy-done.5
  10.6 0.9 copy-done.6
  11.5 1.0 shard_map.154
  12.9 1.2 copy-done.4
  14.3 2.2 %copy-done.2 = bf16[2048,1024]{1,0:T(8,128)(2,1)S(1)} copy-done((bf16[2048,1024]{1,0:T(8,128)(2,1)S(1)}, bf16[2048,1024]{1,0:T(8,128)(2,1)}, u32[]{:S(2)}) %copy-start.2) | copy-done | bytes 4194328
  16.8 2.0 %copy-done = bf16[2048,1024]{1,0:T(8,128)(2,1)} copy-done((bf16[2048,1024]{1,0:T(8,128)(2,1)}, bf16[2048,1024]{1,0:T(8,128)(2,1)S(1)}, u32[]{:S(2)}) %copy-start) | copy-done | bytes 4194328
  18.8 1.8 %collective-permute-start.2 = (bf16[16,2048]{1,0:T(8,128)(2,1)S(1)}, bf16[16,2048]{1,0:T(8,128)(2,1)S(1)}, u32[]{:S(2)}, u32[]{:S(2)}) collective-permute-start(bf16[16,2048]{1,0:T(8,128)(2,1)S(1)} %collective-permute-done.1.refs_2_), channel_id=1, source_target_pairs={{0,4},{4,0},{8,12},{12,8},{16,20},{20,16},{24,28},{28,24},{1,5},{5... | collective-permute-start | bytes 196616 | tf_op jit(solution)/shard_map/ppermute | solution.py:23
  20.9 1.7 %collective-permute-start.6 = (bf16[16,2048]{1,0:T(8,128)(2,1)S(1)}, bf16[16,2048]{1,0:T(8,128)(2,1)S(1)}, u32[]{:S(2)}, u32[]{:S(2)}) collective-permute-start(bf16[16,2048]{1,0:T(8,128)(2,1)S(1)} %collective-permute-done.5.refs_6_), channel_id=1, source_target_pairs={{0,4},{4,0},{8,12},{12,8},{16,20},{20,16},{24,28},{28,24},{1,5},{5... | collective-permute-start | bytes 196616 | tf_op jit(solution)/shard_map/ppermute | solution.py:23
  22.7 0.8 collective-permute-done.2.refs_3_
  23.5 1.3 collective-permute-done.4.refs_5_
  24.9 0.7 collective-permute-done.6.refs_7_
  25.6 1.0 shard_map.151
  26.6 1.4 collective-permute-start.10
  28.8 2.2 %copy-done.1 = bf16[2048,1024]{1,0:T(8,128)(2,1)S(1)} copy-done((bf16[2048,1024]{1,0:T(8,128)(2,1)S(1)}, bf16[2048,1024]{1,0:T(8,128)(2,1)}, u32[]{:S(2)}) %copy-start.1) | copy-done | bytes 4194328
  31.0 1.3 shard_map.153
  32.5 3.5 %collective-permute-start.14 = (bf16[1,2,2,8,8,128]{5,4,3,2,0,1:T(8,128)(2,1)S(1)}, bf16[1,2,2,8,8,128]{5,4,3,2,0,1:T(8,128)(2,1)S(1)}, u32[]{:S(2)}, u32[]{:S(2)}) collective-permute-start(bf16[1,2,2,8,8,128]{5,4,3,2,0,1:T(8,128)(2,1)S(1)} %get-tuple-element.61), channel_id=1, source_target_pairs={{0,8},{4,12},{8,0},{12,4},{16,24},{20,28},{24,16},{28,20},{1,9},{5... | collective-permute-start | bytes 196616 | tf_op jit(solution)/shard_map/ppermute | solution.py:23
  36.0 1.6 %collective-permute-start.15 = (bf16[1,2,2,8,8,128]{5,4,3,2,0,1:T(8,128)(2,1)S(1)}, bf16[1,2,2,8,8,128]{5,4,3,2,0,1:T(8,128)(2,1)S(1)}, u32[]{:S(2)}, u32[]{:S(2)}) collective-permute-start(bf16[1,2,2,8,8,128]{5,4,3,2,0,1:T(8,128)(2,1)S(1)} %get-tuple-element.63), channel_id=1, source_target_pairs={{0,16},{4,20},{8,24},{12,28},{16,0},{20,4},{24,8},{28,12},{1,17},{... | collective-permute-start | bytes 196616 | tf_op jit(solution)/shard_map/ppermute | solution.py:23
  37.6 0.9 collective-permute-start.16
  38.7 5.7 %collective-permute-done.15 = bf16[1,2,2,8,8,128]{5,4,3,2,0,1:T(8,128)(2,1)S(1)} collective-permute-done((bf16[1,2,2,8,8,128]{5,4,3,2,0,1:T(8,128)(2,1)S(1)}, bf16[1,2,2,8,8,128]{5,4,3,2,0,1:T(8,128)(2,1)S(1)}, u32[]{:S(2)}, u32[]{:S(2)}) %collective-permute-start.15) | collective-permute-done | bytes 65568 | tf_op jit(solution)/shard_map/ppermute | solution.py:23
  44.5 1.6 %collective-permute-start.18 = (bf16[128,8,128]{2,1,0:T(8,128)(2,1)S(1)}, bf16[128,8,128]{2,1,0:T(8,128)(2,1)S(1)}, u32[]{:S(2)}, u32[]{:S(2)}) collective-permute-start(bf16[128,8,128]{2,1,0:T(8,128)(2,1)S(1)} %bitcast.19), channel_id=1, source_target_pairs={{0,2},{1,3},{2,0},{3,1},{4,6},{5,7},{6,4},{7,5},{8,10},{9,11},{10,... | collective-permute-start | bytes 786440 | tf_op jit(solution)/shard_map/ppermute | solution.py:23
  47.1 5.1 %collective-permute-done.18.refs_6_ = bf16[128,8,128]{2,1,0:T(8,128)(2,1)S(1)} collective-permute-done((bf16[128,8,128]{2,1,0:T(8,128)(2,1)S(1)}, bf16[128,8,128]{2,1,0:T(8,128)(2,1)S(1)}, u32[]{:S(2)}, u32[]{:S(2)}) %collective-permute-start.18) | collective-permute-done | bytes 262176 | tf_op jit(solution)/shard_map/ppermute | solution.py:23
  52.3 1.6 %collective-permute-start.8 = (bf16[32,1024]{1,0:T(8,128)(2,1)S(1)}, bf16[32,1024]{1,0:T(8,128)(2,1)S(1)}, u32[]{:S(2)}, u32[]{:S(2)}) collective-permute-start(bf16[32,1024]{1,0:T(8,128)(2,1)S(1)} %slice.156), channel_id=1, source_target_pairs={{0,2},{1,3},{2,0},{3,1},{4,6},{5,7},{6,4},{7,5},{8,10},{9,11},{10,... | collective-permute-start | bytes 196616 | tf_op jit(solution)/shard_map/ppermute | solution.py:23
  54.0 2.9 %collective-permute-done.8.refs_1_ = bf16[32,1024]{1,0:T(8,128)(2,1)S(1)} collective-permute-done((bf16[32,1024]{1,0:T(8,128)(2,1)S(1)}, bf16[32,1024]{1,0:T(8,128)(2,1)S(1)}, u32[]{:S(2)}, u32[]{:S(2)}) %collective-permute-start.8) | collective-permute-done | bytes 65568 | tf_op jit(solution)/shard_map/ppermute | solution.py:23
  56.9 2.2 %shard_map.155.refs_0_ = bf16[32,1024]{1,0:T(8,128)(2,1)S(1)} custom-call(s32[2]{0:T(128)S(1)} %pad_add_fusion.1.where_ref, s32[16]{0:T(128)S(1)} %get-tuple-element.59.anc_ref, f32[8,128]{1,0:T(8,128)S(1)} %copy-done.11, s32[128,3]{1,0:T(8,128)S(1)} %bitcast.23, f32[32,1024]{1,0:T(8,128)S(1)} %slice.86.refs_0_, ...), custom_call_target="tpu_custom_call" | custom-call | flops 1073741824 | bytes 4194304 | tf_op jit(solution)/shard_map/pallas_call | solution.py:43
  59.1 1.6 %collective-permute-start.21 = (bf16[32,1024]{1,0:T(8,128)(2,1)S(1)}, bf16[32,1024]{1,0:T(8,128)(2,1)S(1)}, u32[]{:S(2)}, u32[]{:S(2)}) collective-permute-start(bf16[32,1024]{1,0:T(8,128)(2,1)S(1)} %shard_map.155.refs_0_), channel_id=1, source_target_pairs={{0,2},{1,3},{2,0},{3,1},{4,6},{5,7},{6,4},{7,5},{8,10},{9,11},{10,... | collective-permute-start | bytes 196616 | tf_op jit(solution)/shard_map/ppermute | solution.py:23
  60.7 2.7 %collective-permute-done.21.refs_2_ = bf16[32,1024]{1,0:T(8,128)(2,1)S(1)} collective-permute-done((bf16[32,1024]{1,0:T(8,128)(2,1)S(1)}, bf16[32,1024]{1,0:T(8,128)(2,1)S(1)}, u32[]{:S(2)}, u32[]{:S(2)}) %collective-permute-start.21) | collective-permute-done | bytes 65568 | tf_op jit(solution)/shard_map/ppermute | solution.py:23
  63.4 2.2 %copy-done.3 = bf16[1024,2048]{1,0:T(8,128)(2,1)S(1)} copy-done((bf16[1024,2048]{1,0:T(8,128)(2,1)S(1)}, bf16[1024,2048]{1,0:T(8,128)(2,1)}, u32[]{:S(2)}) %copy-start.3) | copy-done | bytes 4194328
  66.0 2.5 %shard_map.157 = (f32[64,2048]{1,0:T(8,128)S(1)}, bf16[32,2048]{1,0:T(8,128)(2,1)S(1)}, bf16[32,2048]{1,0:T(8,128)(2,1)S(1)}) custom-call(s32[2]{0:T(128)S(1)} %pad_add_fusion.1.where_ref, bf16[32,1024]{1,0:T(8,128)(2,1)S(1)} %shard_map.155.refs_0_, bf16[32,1024]{1,0:T(8,128)(2,1)S(1)} %collective-permute-done.20.refs_1_, ...), custom_call_target="tpu_custom_call" | custom-call | flops 536870912 | bytes 4194304 | tf_op jit(solution)/shard_map/pallas_call | solution.py:43
  68.5 3.2 %collective-permute-start.24 = (bf16[32,2048]{1,0:T(8,128)(2,1)S(1)}, bf16[32,2048]{1,0:T(8,128)(2,1)S(1)}, u32[]{:S(2)}, u32[]{:S(2)}) collective-permute-start(bf16[32,2048]{1,0:T(8,128)(2,1)S(1)} %get-tuple-element.40.after_ref), channel_id=1, source_target_pairs={{0,4},{4,0},{8,12},{12,8},{16,20},{20,16},{24,28},{28,24},{1,5},{5... | collective-permute-start | bytes 393224 | tf_op jit(solution)/shard_map/ppermute | solution.py:23
  71.8 4.3 %collective-permute-done.24.arrived_ref = bf16[32,2048]{1,0:T(8,128)(2,1)S(1)} collective-permute-done((bf16[32,2048]{1,0:T(8,128)(2,1)S(1)}, bf16[32,2048]{1,0:T(8,128)(2,1)S(1)}, u32[]{:S(2)}, u32[]{:S(2)}) %collective-permute-start.24) | collective-permute-done | bytes 131104 | tf_op jit(solution)/shard_map/ppermute | solution.py:23
  76.1 3.2 %collective-permute-start.25 = (bf16[16,2048]{1,0:T(8,128)(2,1)S(1)}, bf16[16,2048]{1,0:T(8,128)(2,1)S(1)}, u32[]{:S(2)}, u32[]{:S(2)}) collective-permute-start(bf16[16,2048]{1,0:T(8,128)(2,1)S(1)} %get-tuple-element.41), channel_id=1, source_target_pairs={{0,16},{4,20},{8,24},{12,28},{16,0},{20,4},{24,8},{28,12},{1,17},{... | collective-permute-start | bytes 196616 | tf_op jit(solution)/shard_map/ppermute | solution.py:23
  79.3 1.3 collective-permute-start.26
  80.9 3.4 %collective-permute-done.25.refs_0_ = bf16[16,2048]{1,0:T(8,128)(2,1)S(1)} collective-permute-done((bf16[16,2048]{1,0:T(8,128)(2,1)S(1)}, bf16[16,2048]{1,0:T(8,128)(2,1)S(1)}, u32[]{:S(2)}, u32[]{:S(2)}) %collective-permute-start.25) | collective-permute-done | bytes 65568 | tf_op jit(solution)/shard_map/ppermute | solution.py:23
  84.3 1.3 collective-permute-done.26.refs_1_
  85.7 0.7 shard_map.160
  87.0 2.1 %collective-permute-start.31 = (bf16[16,2048]{1,0:T(8,128)(2,1)S(1)}, bf16[16,2048]{1,0:T(8,128)(2,1)S(1)}, u32[]{:S(2)}, u32[]{:S(2)}) collective-permute-start(bf16[16,2048]{1,0:T(8,128)(2,1)S(1)} %get-tuple-element.45.refs_0_), channel_id=1, source_target_pairs={{0,16},{4,20},{8,24},{12,28},{16,0},{20,4},{24,8},{28,12},{1,17},{... | collective-permute-start | bytes 196616 | tf_op jit(solution)/shard_map/ppermute | solution.py:23
  89.1 1.6 %collective-permute-start.33 = (bf16[16,2048]{1,0:T(8,128)(2,1)S(1)}, bf16[16,2048]{1,0:T(8,128)(2,1)S(1)}, u32[]{:S(2)}, u32[]{:S(2)}) collective-permute-start(bf16[16,2048]{1,0:T(8,128)(2,1)S(1)} %get-tuple-element.45.refs_0_), channel_id=1, source_target_pairs={{0,24},{4,28},{8,16},{12,20},{16,8},{20,12},{24,0},{28,4},{1,25},{... | collective-permute-start | bytes 196616 | tf_op jit(solution)/shard_map/ppermute | solution.py:23
  90.8 1.9 %collective-permute-start.28 = (bf16[16,2048]{1,0:T(8,128)(2,1)S(1)}, bf16[16,2048]{1,0:T(8,128)(2,1)S(1)}, u32[]{:S(2)}, u32[]{:S(2)}) collective-permute-start(bf16[16,2048]{1,0:T(8,128)(2,1)S(1)} %get-tuple-element.45.refs_0_), channel_id=1, source_target_pairs={{0,4},{4,0},{8,12},{12,8},{16,20},{20,16},{24,28},{28,24},{1,5},{5... | collective-permute-start | bytes 196616 | tf_op jit(solution)/shard_map/ppermute | solution.py:23
  92.8 2.2 %collective-permute-start.32 = (bf16[16,2048]{1,0:T(8,128)(2,1)S(1)}, bf16[16,2048]{1,0:T(8,128)(2,1)S(1)}, u32[]{:S(2)}, u32[]{:S(2)}) collective-permute-start(bf16[16,2048]{1,0:T(8,128)(2,1)S(1)} %collective-permute-done.31.refs_4_), channel_id=1, source_target_pairs={{0,4},{4,0},{8,12},{12,8},{16,20},{20,16},{24,28},{28,24},{1,5},{5... | collective-permute-start | bytes 196616 | tf_op jit(solution)/shard_map/ppermute | solution.py:23
  95.2 1.7 %collective-permute-start.34 = (bf16[16,2048]{1,0:T(8,128)(2,1)S(1)}, bf16[16,2048]{1,0:T(8,128)(2,1)S(1)}, u32[]{:S(2)}, u32[]{:S(2)}) collective-permute-start(bf16[16,2048]{1,0:T(8,128)(2,1)S(1)} %collective-permute-done.33.refs_6_), channel_id=1, source_target_pairs={{0,4},{4,0},{8,12},{12,8},{16,20},{20,16},{24,28},{28,24},{1,5},{5... | collective-permute-start | bytes 196616 | tf_op jit(solution)/shard_map/ppermute | solution.py:23
  97.9 1.5 %collective-permute-done.34.refs_7_ = bf16[16,2048]{1,0:T(8,128)(2,1)S(1)} collective-permute-done((bf16[16,2048]{1,0:T(8,128)(2,1)S(1)}, bf16[16,2048]{1,0:T(8,128)(2,1)S(1)}, u32[]{:S(2)}, u32[]{:S(2)}) %collective-permute-start.34) | collective-permute-done | bytes 65568 | tf_op jit(solution)/shard_map/ppermute | solution.py:23
  99.5 3.1 %shard_map.162 = (bf16[128,2048]{1,0:T(8,128)(2,1)S(1)}, f32[64,1920]{1,0:T(8,128)S(1)}, bf16[64,1920]{1,0:T(8,128)(2,1)S(1)}) custom-call(s32[2]{0:T(128)S(1)} %pad_add_fusion.1.where_ref, f32[1,2048]{1,0:T(1,128)S(1)} %bitcast.26, bf16[16,2048]{1,0:T(8,128)(2,1)S(1)} %get-tuple-element.45.refs_0_, bf16[16,2048]{1,0:T(8,128)(2,1)S(1)} %collective-permute-done.28.refs_1_, ...), custom_call_target="tpu_custom_call" | custom-call | flops 939524096 | bytes 8388608 | tf_op jit(solution)/shard_map/pallas_call | solution.py:43
  103.2 2.3 %shard_map.164 = (f32[64,1792]{1,0:T(8,128)S(1)}, bf16[64,1792]{1,0:T(8,128)(2,1)S(1)}) custom-call(bf16[128,2048]{1,0:T(8,128)(2,1)S(1)} %get-tuple-element.48.h_ref.after_ref, bf16[2048,1792]{1,0:T(8,128)(2,1)S(1)} %shard_map.163.w_ref), custom_call_target="tpu_custom_call" | custom-call | flops 939524096 | bytes 7340032 | tf_op jit(solution)/shard_map/pallas_call | solution.py:43
  106.2 1.6 %collective-permute-start.36 = (bf16[32,1920]{1,0:T(8,128)(2,1)S(1)}, bf16[32,1920]{1,0:T(8,128)(2,1)S(1)}, u32[]{:S(2)}, u32[]{:S(2)}) collective-permute-start(bf16[32,1920]{1,0:T(8,128)(2,1)S(1)} %slice.153), channel_id=1, source_target_pairs={{0,2},{1,3},{2,0},{3,1},{4,6},{5,7},{6,4},{7,5},{8,10},{9,11},{10,... | collective-permute-start | bytes 368648 | tf_op jit(solution)/shard_map/ppermute | solution.py:23
  107.8 1.0 collective-permute-start.38
  108.8 3.6 %collective-permute-done.36 = bf16[32,1920]{1,0:T(8,128)(2,1)S(1)} collective-permute-done((bf16[32,1920]{1,0:T(8,128)(2,1)S(1)}, bf16[32,1920]{1,0:T(8,128)(2,1)S(1)}, u32[]{:S(2)}, u32[]{:S(2)}) %collective-permute-start.36) | collective-permute-done | bytes 122912 | tf_op jit(solution)/shard_map/ppermute | solution.py:23
  112.6 1.3 collective-permute-done.38
  114.1 1.6 %collective-permute-start.40 = (bf16[32,1792]{1,0:T(8,128)(2,1)S(1)}, bf16[32,1792]{1,0:T(8,128)(2,1)S(1)}, u32[]{:S(2)}, u32[]{:S(2)}) collective-permute-start(bf16[32,1792]{1,0:T(8,128)(2,1)S(1)} %fusion.2.refs_0_), channel_id=1, source_target_pairs={{0,2},{1,3},{2,0},{3,1},{4,6},{5,7},{6,4},{7,5},{8,10},{9,11},{10,... | collective-permute-start | bytes 344072 | tf_op jit(solution)/shard_map/ppermute | solution.py:23
  115.7 3.3 %collective-permute-done.40.refs_2_ = bf16[32,1792]{1,0:T(8,128)(2,1)S(1)} collective-permute-done((bf16[32,1792]{1,0:T(8,128)(2,1)S(1)}, bf16[32,1792]{1,0:T(8,128)(2,1)S(1)}, u32[]{:S(2)}, u32[]{:S(2)}) %collective-permute-start.40) | collective-permute-done | bytes 114720 | tf_op jit(solution)/shard_map/ppermute | solution.py:23
  119.5 0.8 collective-permute-done.41.refs_3_
  120.3 3.1 %shard_map.166 = (f32[64,2048]{1,0:T(8,128)S(1)}, bf16[32,2048]{1,0:T(8,128)(2,1)S(1)}, bf16[32,2048]{1,0:T(8,128)(2,1)S(1)}) custom-call(s32[2]{0:T(128)S(1)} %pad_add_fusion.1.where_ref, bf16[32,1792]{1,0:T(8,128)(2,1)S(1)} %fusion.2.refs_0_, bf16[32,1792]{1,0:T(8,128)(2,1)S(1)} %collective-permute-done.39.refs_1_, ...), custom_call_target="tpu_custom_call" | custom-call | flops 939524096 | bytes 7340032 | tf_op jit(solution)/shard_map/pallas_call | solution.py:43
  123.4 1.7 %collective-permute-start.43 = (bf16[32,2048]{1,0:T(8,128)(2,1)S(1)}, bf16[32,2048]{1,0:T(8,128)(2,1)S(1)}, u32[]{:S(2)}, u32[]{:S(2)}) collective-permute-start(bf16[32,2048]{1,0:T(8,128)(2,1)S(1)} %get-tuple-element.54), channel_id=1, source_target_pairs={{0,4},{4,0},{8,12},{12,8},{16,20},{20,16},{24,28},{28,24},{1,5},{5... | collective-permute-start | bytes 393224 | tf_op jit(solution)/shard_map/ppermute | solution.py:23
  125.4 4.3 %collective-permute-done.43.arrived_ref = bf16[32,2048]{1,0:T(8,128)(2,1)S(1)} collective-permute-done((bf16[32,2048]{1,0:T(8,128)(2,1)S(1)}, bf16[32,2048]{1,0:T(8,128)(2,1)S(1)}, u32[]{:S(2)}, u32[]{:S(2)}) %collective-permute-start.43) | collective-permute-done | bytes 131104 | tf_op jit(solution)/shard_map/ppermute | solution.py:23
  129.8 1.1 collective-permute-start.44
  130.9 1.6 %collective-permute-start.45 = (bf16[16,2048]{1,0:T(8,128)(2,1)S(1)}, bf16[16,2048]{1,0:T(8,128)(2,1)S(1)}, u32[]{:S(2)}, u32[]{:S(2)}) collective-permute-start(bf16[16,2048]{1,0:T(8,128)(2,1)S(1)} %get-tuple-element.56), channel_id=1, source_target_pairs={{0,24},{4,28},{8,16},{12,20},{16,8},{20,12},{24,0},{28,4},{1,25},{... | collective-permute-start | bytes 196616 | tf_op jit(solution)/shard_map/ppermute | solution.py:23
  132.6 0.9 collective-permute-start.46
  133.5 2.4 %collective-permute-done.44.refs_0_ = bf16[16,2048]{1,0:T(8,128)(2,1)S(1)} collective-permute-done((bf16[16,2048]{1,0:T(8,128)(2,1)S(1)}, bf16[16,2048]{1,0:T(8,128)(2,1)S(1)}, u32[]{:S(2)}, u32[]{:S(2)}) %collective-permute-start.44) | collective-permute-done | bytes 65568 | tf_op jit(solution)/shard_map/ppermute | solution.py:23
  135.8 1.3 collective-permute-done.45.refs_1_
  137.6 0.7 shard_map.169
  (126 shorter events, 9.8 us)
Async XLA Ops:
  2.1 20.5 %copy-start.12 = (s32[64]{0:T(128)S(1)}, s32[64]{0:T(128)}, u32[]{:S(2)}) copy-start(s32[64]{0:T(128)} %param.18) | copy-start | bytes 772
  2.1 23.4 %copy-start.9 = (f32[2048]{0:T(1024)S(1)}, f32[2048]{0:T(1024)}, u32[]{:S(2)}) copy-start(f32[2048]{0:T(1024)} %param.19) | copy-start | bytes 24580
  2.3 16.6 %collective-permute-start.1 = (bf16[16,2048]{1,0:T(8,128)(2,1)S(1)}, bf16[16,2048]{1,0:T(8,128)(2,1)S(1)}, u32[]{:S(2)}, u32[]{:S(2)}) collective-permute-start(bf16[16,2048]{1,0:T(8,128)(2,1)S(1)} %shard_map.149.after_ref.refs_0_.refs_3_), channel_id=1, source_target_pairs={{0,8},{4,12},{8,0},{12,4},{16,24},{20,28},{24,16},{28,20},{1,9},{5... | collective-permute-start | bytes 196616 | tf_op jit(solution)/shard_map/ppermute | solution.py:23
  5.3 15.3 %collective-permute-start.3 = (bf16[16,2048]{1,0:T(8,128)(2,1)S(1)}, bf16[16,2048]{1,0:T(8,128)(2,1)S(1)}, u32[]{:S(2)}, u32[]{:S(2)}) collective-permute-start(bf16[16,2048]{1,0:T(8,128)(2,1)S(1)} %shard_map.149.after_ref.refs_0_.refs_3_), channel_id=1, source_target_pairs={{0,16},{4,20},{8,24},{12,28},{16,0},{20,4},{24,8},{28,12},{1,17},{... | collective-permute-start | bytes 196616 | tf_op jit(solution)/shard_map/ppermute | solution.py:23
  7.9 13.0 %collective-permute-start.5 = (bf16[16,2048]{1,0:T(8,128)(2,1)S(1)}, bf16[16,2048]{1,0:T(8,128)(2,1)S(1)}, u32[]{:S(2)}, u32[]{:S(2)}) collective-permute-start(bf16[16,2048]{1,0:T(8,128)(2,1)S(1)} %shard_map.149.after_ref.refs_0_.refs_3_), channel_id=1, source_target_pairs={{0,24},{4,28},{8,16},{12,20},{16,8},{20,12},{24,0},{28,4},{1,25},{... | collective-permute-start | bytes 196616 | tf_op jit(solution)/shard_map/ppermute | solution.py:23
  7.9 14.8 %collective-permute-start = (bf16[16,2048]{1,0:T(8,128)(2,1)S(1)}, bf16[16,2048]{1,0:T(8,128)(2,1)S(1)}, u32[]{:S(2)}, u32[]{:S(2)}) collective-permute-start(bf16[16,2048]{1,0:T(8,128)(2,1)S(1)} %shard_map.149.after_ref.refs_0_.refs_3_), channel_id=1, source_target_pairs={{0,4},{4,0},{8,12},{12,8},{16,20},{20,16},{24,28},{28,24},{1,5},{5... | collective-permute-start | bytes 196616 | tf_op jit(solution)/shard_map/ppermute | solution.py:23
  9.7 0.9 copy-start.5
  10.6 0.9 copy-start.6
  12.5 20.0 %collective-permute-start.13 = (bf16[4,2,8,8,128]{4,3,2,1,0:T(8,128)(2,1)S(1)}, bf16[4,2,8,8,128]{4,3,2,1,0:T(8,128)(2,1)S(1)}, u32[]{:S(2)}, u32[]{:S(2)}) collective-permute-start(bf16[4,2,8,8,128]{4,3,2,1,0:T(8,128)(2,1)S(1)} %get-tuple-element.36), channel_id=1, source_target_pairs={{0,4},{4,0},{8,12},{12,8},{16,20},{20,16},{24,28},{28,24},{1,5},{5... | collective-permute-start | bytes 393224 | tf_op jit(solution)/shard_map/ppermute | solution.py:23
  12.9 1.2 copy-start.4
  14.2 2.2 %copy-start.2 = (bf16[2048,1024]{1,0:T(8,128)(2,1)S(1)}, bf16[2048,1024]{1,0:T(8,128)(2,1)}, u32[]{:S(2)}) copy-start(bf16[2048,1024]{1,0:T(8,128)(2,1)} %w_ref.7) | copy-start | bytes 12582916
  16.8 2.0 %copy-start = (bf16[2048,1024]{1,0:T(8,128)(2,1)}, bf16[2048,1024]{1,0:T(8,128)(2,1)S(1)}, u32[]{:S(2)}) copy-start(bf16[2048,1024]{1,0:T(8,128)(2,1)S(1)} %shard_map.152.w_ref) | copy-start | bytes 12582916
  18.8 38.0 %copy-start.11 = (f32[8,128]{1,0:T(8,128)S(1)}, f32[8,128]{1,0:T(8,128)}, u32[]{:S(2)}) copy-start(f32[8,128]{1,0:T(8,128)} %constant.86.clone.rope_ref) | copy-start | bytes 12292
  18.8 4.7 %collective-permute-start.2 = (bf16[16,2048]{1,0:T(8,128)(2,1)S(1)}, bf16[16,2048]{1,0:T(8,128)(2,1)S(1)}, u32[]{:S(2)}, u32[]{:S(2)}) collective-permute-start(bf16[16,2048]{1,0:T(8,128)(2,1)S(1)} %collective-permute-done.1.refs_2_), channel_id=1, source_target_pairs={{0,4},{4,0},{8,12},{12,8},{16,20},{20,16},{24,28},{28,24},{1,5},{5... | collective-permute-start | bytes 196616 | tf_op jit(solution)/shard_map/ppermute | solution.py:23
  20.6 4.3 %collective-permute-start.4 = (bf16[16,2048]{1,0:T(8,128)(2,1)S(1)}, bf16[16,2048]{1,0:T(8,128)(2,1)S(1)}, u32[]{:S(2)}, u32[]{:S(2)}) collective-permute-start(bf16[16,2048]{1,0:T(8,128)(2,1)S(1)} %collective-permute-done.3.refs_4_), channel_id=1, source_target_pairs={{0,4},{4,0},{8,12},{12,8},{16,20},{20,16},{24,28},{28,24},{1,5},{5... | collective-permute-start | bytes 196616 | tf_op jit(solution)/shard_map/ppermute | solution.py:23
  20.9 4.6 %collective-permute-start.6 = (bf16[16,2048]{1,0:T(8,128)(2,1)S(1)}, bf16[16,2048]{1,0:T(8,128)(2,1)S(1)}, u32[]{:S(2)}, u32[]{:S(2)}) collective-permute-start(bf16[16,2048]{1,0:T(8,128)(2,1)S(1)} %collective-permute-done.5.refs_6_), channel_id=1, source_target_pairs={{0,4},{4,0},{8,12},{12,8},{16,20},{20,16},{24,28},{28,24},{1,5},{5... | collective-permute-start | bytes 196616 | tf_op jit(solution)/shard_map/ppermute | solution.py:23
  26.6 11.0 %collective-permute-start.10 = (bf16[128,128]{1,0:T(8,128)(2,1)S(1)}, bf16[128,128]{1,0:T(8,128)(2,1)S(1)}, u32[]{:S(2)}, u32[]{:S(2)}) collective-permute-start(bf16[128,128]{1,0:T(8,128)(2,1)S(1)} %get-tuple-element.67), channel_id=1, source_target_pairs={{0,4},{4,12},{8,20},{12,28},{16,0},{20,8},{24,16},{28,24},{1,5},{5... | collective-permute-start | bytes 98312 | tf_op jit(solution)/shard_map/ppermute | solution.py:502
  27.9 10.5 %collective-permute-start.9 = (bf16[128,128]{1,0:T(8,128)(2,1)S(1)}, bf16[128,128]{1,0:T(8,128)(2,1)S(1)}, u32[]{:S(2)}, u32[]{:S(2)}) collective-permute-start(bf16[128,128]{1,0:T(8,128)(2,1)S(1)} %get-tuple-element.66), channel_id=1, source_target_pairs={{0,0},{4,8},{8,16},{12,24},{16,4},{20,12},{24,20},{28,28},{1,1},{5... | collective-permute-start | bytes 98312 | tf_op jit(solution)/shard_map/ppermute | solution.py:497
  28.8 2.2 %copy-start.1 = (bf16[2048,1024]{1,0:T(8,128)(2,1)S(1)}, bf16[2048,1024]{1,0:T(8,128)(2,1)}, u32[]{:S(2)}) copy-start(bf16[2048,1024]{1,0:T(8,128)(2,1)} %copy-done) | copy-start | bytes 12582916
  32.4 19.8 %collective-permute-start.7 = (bf16[64,1024]{1,0:T(8,128)(2,1)S(1)}, bf16[64,1024]{1,0:T(8,128)(2,1)S(1)}, u32[]{:S(2)}, u32[]{:S(2)}) collective-permute-start(bf16[64,1024]{1,0:T(8,128)(2,1)S(1)} %get-tuple-element.32), channel_id=1, source_target_pairs={{0,1},{1,0},{2,3},{3,2},{4,5},{5,4},{6,7},{7,6},{8,9},{9,8},{10,11... | collective-permute-start | bytes 393224 | tf_op jit(solution)/shard_map/ppermute | solution.py:23
  32.5 6.2 %collective-permute-start.14 = (bf16[1,2,2,8,8,128]{5,4,3,2,0,1:T(8,128)(2,1)S(1)}, bf16[1,2,2,8,8,128]{5,4,3,2,0,1:T(8,128)(2,1)S(1)}, u32[]{:S(2)}, u32[]{:S(2)}) collective-permute-start(bf16[1,2,2,8,8,128]{5,4,3,2,0,1:T(8,128)(2,1)S(1)} %get-tuple-element.61), channel_id=1, source_target_pairs={{0,8},{4,12},{8,0},{12,4},{16,24},{20,28},{24,16},{28,20},{1,9},{5... | collective-permute-start | bytes 196616 | tf_op jit(solution)/shard_map/ppermute | solution.py:23
  36.0 8.4 %collective-permute-start.15 = (bf16[1,2,2,8,8,128]{5,4,3,2,0,1:T(8,128)(2,1)S(1)}, bf16[1,2,2,8,8,128]{5,4,3,2,0,1:T(8,128)(2,1)S(1)}, u32[]{:S(2)}, u32[]{:S(2)}) collective-permute-start(bf16[1,2,2,8,8,128]{5,4,3,2,0,1:T(8,128)(2,1)S(1)} %get-tuple-element.63), channel_id=1, source_target_pairs={{0,16},{4,20},{8,24},{12,28},{16,0},{20,4},{24,8},{28,12},{1,17},{... | collective-permute-start | bytes 196616 | tf_op jit(solution)/shard_map/ppermute | solution.py:23
  37.6 6.9 %collective-permute-start.16 = (bf16[1,2,2,8,8,128]{5,4,3,2,0,1:T(8,128)(2,1)S(1)}, bf16[1,2,2,8,8,128]{5,4,3,2,0,1:T(8,128)(2,1)S(1)}, u32[]{:S(2)}, u32[]{:S(2)}) collective-permute-start(bf16[1,2,2,8,8,128]{5,4,3,2,0,1:T(8,128)(2,1)S(1)} %get-tuple-element.62), channel_id=1, source_target_pairs={{0,24},{4,28},{8,16},{12,20},{16,8},{20,12},{24,0},{28,4},{1,25},{... | collective-permute-start | bytes 196616 | tf_op jit(solution)/shard_map/ppermute | solution.py:23
  38.5 7.6 %collective-permute-start.11 = (bf16[128,384]{1,0:T(8,128)(2,1)S(1)}, bf16[128,384]{1,0:T(8,128)(2,1)S(1)}, u32[]{:S(2)}, u32[]{:S(2)}) collective-permute-start(bf16[128,384]{1,0:T(8,128)(2,1)S(1)} %fusion.5), channel_id=1, source_target_pairs={{0,1},{1,0},{2,3},{3,2},{4,5},{5,4},{6,7},{7,6},{8,9},{9,8},{10,11... | collective-permute-start | bytes 294920 | tf_op jit(solution)/shard_map/ppermute | solution.py:23
  44.5 7.7 %collective-permute-start.18 = (bf16[128,8,128]{2,1,0:T(8,128)(2,1)S(1)}, bf16[128,8,128]{2,1,0:T(8,128)(2,1)S(1)}, u32[]{:S(2)}, u32[]{:S(2)}) collective-permute-start(bf16[128,8,128]{2,1,0:T(8,128)(2,1)S(1)} %bitcast.19), channel_id=1, source_target_pairs={{0,2},{1,3},{2,0},{3,1},{4,6},{5,7},{6,4},{7,5},{8,10},{9,11},{10,... | collective-permute-start | bytes 786440 | tf_op jit(solution)/shard_map/ppermute | solution.py:23
  46.1 10.8 %collective-permute-start.17 = (bf16[128,8,128]{2,1,0:T(8,128)(2,1)S(1)}, bf16[128,8,128]{2,1,0:T(8,128)(2,1)S(1)}, u32[]{:S(2)}, u32[]{:S(2)}) collective-permute-start(bf16[128,8,128]{2,1,0:T(8,128)(2,1)S(1)} %bitcast.20), channel_id=1, source_target_pairs={{0,1},{1,0},{2,3},{3,2},{4,5},{5,4},{6,7},{7,6},{8,9},{9,8},{10,11... | collective-permute-start | bytes 786440 | tf_op jit(solution)/shard_map/ppermute | solution.py:23
  46.5 10.4 %collective-permute-start.12 = (bf16[128,384]{1,0:T(8,128)(2,1)S(1)}, bf16[128,384]{1,0:T(8,128)(2,1)S(1)}, u32[]{:S(2)}, u32[]{:S(2)}) collective-permute-start(bf16[128,384]{1,0:T(8,128)(2,1)S(1)} %fusion.6.refs_2_), channel_id=1, source_target_pairs={{0,2},{1,3},{2,0},{3,1},{4,6},{5,7},{6,4},{7,5},{8,10},{9,11},{10,... | collective-permute-start | bytes 294920 | tf_op jit(solution)/shard_map/ppermute | solution.py:23
  52.2 4.6 %collective-permute-start.19 = (bf16[128,8,128]{2,1,0:T(8,128)(2,1)S(1)}, bf16[128,8,128]{2,1,0:T(8,128)(2,1)S(1)}, u32[]{:S(2)}, u32[]{:S(2)}) collective-permute-start(bf16[128,8,128]{2,1,0:T(8,128)(2,1)S(1)} %collective-permute-done.18.refs_6_), channel_id=1, source_target_pairs={{0,1},{1,0},{2,3},{3,2},{4,5},{5,4},{6,7},{7,6},{8,9},{9,8},{10,11... | collective-permute-start | bytes 786440 | tf_op jit(solution)/shard_map/ppermute | solution.py:23
  52.3 4.6 %collective-permute-start.8 = (bf16[32,1024]{1,0:T(8,128)(2,1)S(1)}, bf16[32,1024]{1,0:T(8,128)(2,1)S(1)}, u32[]{:S(2)}, u32[]{:S(2)}) collective-permute-start(bf16[32,1024]{1,0:T(8,128)(2,1)S(1)} %slice.156), channel_id=1, source_target_pairs={{0,2},{1,3},{2,0},{3,1},{4,6},{5,7},{6,4},{7,5},{8,10},{9,11},{10,... | collective-permute-start | bytes 196616 | tf_op jit(solution)/shard_map/ppermute | solution.py:23
  56.9 40.0 %slice-start = ((s8[7340032]{0:T(1024)(128)(4,1)}), s8[4194304]{0:T(1024)(128)(4,1)S(1)}, s32[]{:S(2)}) async-start(s8[7340032]{0:T(1024)(128)(4,1)} %bitcast.13), calls=%async_computation | async-start | bytes 8388608
  59.1 37.8 %slice-start.1 = ((s8[7340032]{0:T(1024)(128)(4,1)}), s8[3145728]{0:T(1024)(128)(4,1)S(1)}, s32[]{:S(2)}) async-start(s8[7340032]{0:T(1024)(128)(4,1)} %bitcast.13), calls=%async_computation.1 | async-start | bytes 6291456
  59.1 4.3 %collective-permute-start.21 = (bf16[32,1024]{1,0:T(8,128)(2,1)S(1)}, bf16[32,1024]{1,0:T(8,128)(2,1)S(1)}, u32[]{:S(2)}, u32[]{:S(2)}) collective-permute-start(bf16[32,1024]{1,0:T(8,128)(2,1)S(1)} %shard_map.155.refs_0_), channel_id=1, source_target_pairs={{0,2},{1,3},{2,0},{3,1},{4,6},{5,7},{6,4},{7,5},{8,10},{9,11},{10,... | collective-permute-start | bytes 196616 | tf_op jit(solution)/shard_map/ppermute | solution.py:23
  60.7 5.3 %collective-permute-start.20 = (bf16[32,1024]{1,0:T(8,128)(2,1)S(1)}, bf16[32,1024]{1,0:T(8,128)(2,1)S(1)}, u32[]{:S(2)}, u32[]{:S(2)}) collective-permute-start(bf16[32,1024]{1,0:T(8,128)(2,1)S(1)} %shard_map.155.refs_0_), channel_id=1, source_target_pairs={{0,1},{1,0},{2,3},{3,2},{4,5},{5,4},{6,7},{7,6},{8,9},{9,8},{10,11... | collective-permute-start | bytes 196616 | tf_op jit(solution)/shard_map/ppermute | solution.py:23
  63.4 2.5 %collective-permute-start.22 = (bf16[32,1024]{1,0:T(8,128)(2,1)S(1)}, bf16[32,1024]{1,0:T(8,128)(2,1)S(1)}, u32[]{:S(2)}, u32[]{:S(2)}) collective-permute-start(bf16[32,1024]{1,0:T(8,128)(2,1)S(1)} %collective-permute-done.21.refs_2_), channel_id=1, source_target_pairs={{0,1},{1,0},{2,3},{3,2},{4,5},{5,4},{6,7},{7,6},{8,9},{9,8},{10,11... | collective-permute-start | bytes 196616 | tf_op jit(solution)/shard_map/ppermute | solution.py:23
  63.4 2.2 %copy-start.3 = (bf16[1024,2048]{1,0:T(8,128)(2,1)S(1)}, bf16[1024,2048]{1,0:T(8,128)(2,1)}, u32[]{:S(2)}) copy-start(bf16[1024,2048]{1,0:T(8,128)(2,1)} %w_ref.8) | copy-start | bytes 12582916
  68.5 7.5 %collective-permute-start.24 = (bf16[32,2048]{1,0:T(8,128)(2,1)S(1)}, bf16[32,2048]{1,0:T(8,128)(2,1)S(1)}, u32[]{:S(2)}, u32[]{:S(2)}) collective-permute-start(bf16[32,2048]{1,0:T(8,128)(2,1)S(1)} %get-tuple-element.40.after_ref), channel_id=1, source_target_pairs={{0,4},{4,0},{8,12},{12,8},{16,20},{20,16},{24,28},{28,24},{1,5},{5... | collective-permute-start | bytes 393224 | tf_op jit(solution)/shard_map/ppermute | solution.py:23
  71.7 8.9 %collective-permute-start.23 = (bf16[32,2048]{1,0:T(8,128)(2,1)S(1)}, bf16[32,2048]{1,0:T(8,128)(2,1)S(1)}, u32[]{:S(2)}, u32[]{:S(2)}) collective-permute-start(bf16[32,2048]{1,0:T(8,128)(2,1)S(1)} %get-tuple-element.38), channel_id=1, source_target_pairs={{0,4},{4,0},{8,12},{12,8},{16,20},{20,16},{24,28},{28,24},{1,5},{5... | collective-permute-start | bytes 393224 | tf_op jit(solution)/shard_map/ppermute | solution.py:23
  76.1 8.2 %collective-permute-start.25 = (bf16[16,2048]{1,0:T(8,128)(2,1)S(1)}, bf16[16,2048]{1,0:T(8,128)(2,1)S(1)}, u32[]{:S(2)}, u32[]{:S(2)}) collective-permute-start(bf16[16,2048]{1,0:T(8,128)(2,1)S(1)} %get-tuple-element.41), channel_id=1, source_target_pairs={{0,16},{4,20},{8,24},{12,28},{16,0},{20,4},{24,8},{28,12},{1,17},{... | collective-permute-start | bytes 196616 | tf_op jit(solution)/shard_map/ppermute | solution.py:23
  79.3 6.2 %collective-permute-start.26 = (bf16[16,2048]{1,0:T(8,128)(2,1)S(1)}, bf16[16,2048]{1,0:T(8,128)(2,1)S(1)}, u32[]{:S(2)}, u32[]{:S(2)}) collective-permute-start(bf16[16,2048]{1,0:T(8,128)(2,1)S(1)} %get-tuple-element.42), channel_id=1, source_target_pairs={{0,24},{4,28},{8,16},{12,20},{16,8},{20,12},{24,0},{28,4},{1,25},{... | collective-permute-start | bytes 196616 | tf_op jit(solution)/shard_map/ppermute | solution.py:23
  80.6 22.0 %slice-start.2 = ((s8[7340032]{0:T(1024)(128)(4,1)}), s8[4194304]{0:T(1024)(128)(4,1)S(1)}, s32[]{:S(2)}) async-start(s8[7340032]{0:T(1024)(128)(4,1)} %bitcast.15), calls=%async_computation.2 | async-start | bytes 8388608
  80.7 5.0 %collective-permute-start.27 = (bf16[16,2048]{1,0:T(8,128)(2,1)S(1)}, bf16[16,2048]{1,0:T(8,128)(2,1)S(1)}, u32[]{:S(2)}, u32[]{:S(2)}) collective-permute-start(bf16[16,2048]{1,0:T(8,128)(2,1)S(1)} %get-tuple-element.43), channel_id=1, source_target_pairs={{0,8},{4,12},{8,0},{12,4},{16,24},{20,28},{24,16},{28,20},{1,9},{5... | collective-permute-start | bytes 196616 | tf_op jit(solution)/shard_map/ppermute | solution.py:23
  86.4 13.1 %copy-start.10 = (f32[2048]{0:T(1024)S(1)}, f32[2048]{0:T(1024)}, u32[]{:S(2)}) copy-start(f32[2048]{0:T(1024)} %param.20) | copy-start | bytes 24580
  86.4 16.3 %slice-start.3 = ((s8[7340032]{0:T(1024)(128)(4,1)}), s8[3145728]{0:T(1024)(128)(4,1)S(1)}, s32[]{:S(2)}) async-start(s8[7340032]{0:T(1024)(128)(4,1)} %bitcast.15), calls=%async_computation.3 | async-start | bytes 6291456
  86.4 6.3 %collective-permute-start.29 = (bf16[16,2048]{1,0:T(8,128)(2,1)S(1)}, bf16[16,2048]{1,0:T(8,128)(2,1)S(1)}, u32[]{:S(2)}, u32[]{:S(2)}) collective-permute-start(bf16[16,2048]{1,0:T(8,128)(2,1)S(1)} %get-tuple-element.45.refs_0_), channel_id=1, source_target_pairs={{0,8},{4,12},{8,0},{12,4},{16,24},{20,28},{24,16},{28,20},{1,9},{5... | collective-permute-start | bytes 196616 | tf_op jit(solution)/shard_map/ppermute | solution.py:23
  87.0 5.8 %collective-permute-start.31 = (bf16[16,2048]{1,0:T(8,128)(2,1)S(1)}, bf16[16,2048]{1,0:T(8,128)(2,1)S(1)}, u32[]{:S(2)}, u32[]{:S(2)}) collective-permute-start(bf16[16,2048]{1,0:T(8,128)(2,1)S(1)} %get-tuple-element.45.refs_0_), channel_id=1, source_target_pairs={{0,16},{4,20},{8,24},{12,28},{16,0},{20,4},{24,8},{28,12},{1,17},{... | collective-permute-start | bytes 196616 | tf_op jit(solution)/shard_map/ppermute | solution.py:23
  89.1 6.1 %collective-permute-start.33 = (bf16[16,2048]{1,0:T(8,128)(2,1)S(1)}, bf16[16,2048]{1,0:T(8,128)(2,1)S(1)}, u32[]{:S(2)}, u32[]{:S(2)}) collective-permute-start(bf16[16,2048]{1,0:T(8,128)(2,1)S(1)} %get-tuple-element.45.refs_0_), channel_id=1, source_target_pairs={{0,24},{4,28},{8,16},{12,20},{16,8},{20,12},{24,0},{28,4},{1,25},{... | collective-permute-start | bytes 196616 | tf_op jit(solution)/shard_map/ppermute | solution.py:23
  90.8 6.7 %collective-permute-start.28 = (bf16[16,2048]{1,0:T(8,128)(2,1)S(1)}, bf16[16,2048]{1,0:T(8,128)(2,1)S(1)}, u32[]{:S(2)}, u32[]{:S(2)}) collective-permute-start(bf16[16,2048]{1,0:T(8,128)(2,1)S(1)} %get-tuple-element.45.refs_0_), channel_id=1, source_target_pairs={{0,4},{4,0},{8,12},{12,8},{16,20},{20,16},{24,28},{28,24},{1,5},{5... | collective-permute-start | bytes 196616 | tf_op jit(solution)/shard_map/ppermute | solution.py:23
  92.7 4.8 %collective-permute-start.30 = (bf16[16,2048]{1,0:T(8,128)(2,1)S(1)}, bf16[16,2048]{1,0:T(8,128)(2,1)S(1)}, u32[]{:S(2)}, u32[]{:S(2)}) collective-permute-start(bf16[16,2048]{1,0:T(8,128)(2,1)S(1)} %collective-permute-done.29.refs_2_), channel_id=1, source_target_pairs={{0,4},{4,0},{8,12},{12,8},{16,20},{20,16},{24,28},{28,24},{1,5},{5... | collective-permute-start | bytes 196616 | tf_op jit(solution)/shard_map/ppermute | solution.py:23
  92.8 5.2 %collective-permute-start.32 = (bf16[16,2048]{1,0:T(8,128)(2,1)S(1)}, bf16[16,2048]{1,0:T(8,128)(2,1)S(1)}, u32[]{:S(2)}, u32[]{:S(2)}) collective-permute-start(bf16[16,2048]{1,0:T(8,128)(2,1)S(1)} %collective-permute-done.31.refs_4_), channel_id=1, source_target_pairs={{0,4},{4,0},{8,12},{12,8},{16,20},{20,16},{24,28},{28,24},{1,5},{5... | collective-permute-start | bytes 196616 | tf_op jit(solution)/shard_map/ppermute | solution.py:23
  95.2 4.3 %collective-permute-start.34 = (bf16[16,2048]{1,0:T(8,128)(2,1)S(1)}, bf16[16,2048]{1,0:T(8,128)(2,1)S(1)}, u32[]{:S(2)}, u32[]{:S(2)}) collective-permute-start(bf16[16,2048]{1,0:T(8,128)(2,1)S(1)} %collective-permute-done.33.refs_6_), channel_id=1, source_target_pairs={{0,4},{4,0},{8,12},{12,8},{16,20},{20,16},{24,28},{28,24},{1,5},{5... | collective-permute-start | bytes 196616 | tf_op jit(solution)/shard_map/ppermute | solution.py:23
  102.6 16.4 %slice-start.4 = ((s8[7340032]{0:T(1024)(128)(4,1)}), s8[4194304]{0:T(1024)(128)(4,1)S(1)}, s32[]{:S(2)}) async-start(s8[7340032]{0:T(1024)(128)(4,1)} %bitcast.17), calls=%async_computation.4 | async-start | bytes 8388608
  102.6 16.4 %slice-start.5 = ((s8[7340032]{0:T(1024)(128)(4,1)}), s8[3145728]{0:T(1024)(128)(4,1)S(1)}, s32[]{:S(2)}) async-start(s8[7340032]{0:T(1024)(128)(4,1)} %bitcast.17), calls=%async_computation.5 | async-start | bytes 6291456
  102.6 3.5 %collective-permute-start.35 = (bf16[64,1920]{1,0:T(8,128)(2,1)S(1)}, bf16[64,1920]{1,0:T(8,128)(2,1)S(1)}, u32[]{:S(2)}, u32[]{:S(2)}) collective-permute-start(bf16[64,1920]{1,0:T(8,128)(2,1)S(1)} %get-tuple-element.47), channel_id=1, source_target_pairs={{0,1},{1,0},{2,3},{3,2},{4,5},{5,4},{6,7},{7,6},{8,9},{9,8},{10,11... | collective-permute-start | bytes 737288 | tf_op jit(solution)/shard_map/ppermute | solution.py:23
  105.5 2.2 %collective-permute-start.37 = (bf16[64,1792]{1,0:T(8,128)(2,1)S(1)}, bf16[64,1792]{1,0:T(8,128)(2,1)S(1)}, u32[]{:S(2)}, u32[]{:S(2)}) collective-permute-start(bf16[64,1792]{1,0:T(8,128)(2,1)S(1)} %get-tuple-element.50), channel_id=1, source_target_pairs={{0,1},{1,0},{2,3},{3,2},{4,5},{5,4},{6,7},{7,6},{8,9},{9,8},{10,11... | collective-permute-start | bytes 688136 | tf_op jit(solution)/shard_map/ppermute | solution.py:23
  106.2 6.2 %collective-permute-start.36 = (bf16[32,1920]{1,0:T(8,128)(2,1)S(1)}, bf16[32,1920]{1,0:T(8,128)(2,1)S(1)}, u32[]{:S(2)}, u32[]{:S(2)}) collective-permute-start(bf16[32,1920]{1,0:T(8,128)(2,1)S(1)} %slice.153), channel_id=1, source_target_pairs={{0,2},{1,3},{2,0},{3,1},{4,6},{5,7},{6,4},{7,5},{8,10},{9,11},{10,... | collective-permute-start | bytes 368648 | tf_op jit(solution)/shard_map/ppermute | solution.py:23
  107.8 6.2 %collective-permute-start.38 = (bf16[32,1792]{1,0:T(8,128)(2,1)S(1)}, bf16[32,1792]{1,0:T(8,128)(2,1)S(1)}, u32[]{:S(2)}, u32[]{:S(2)}) collective-permute-start(bf16[32,1792]{1,0:T(8,128)(2,1)S(1)} %slice.154), channel_id=1, source_target_pairs={{0,2},{1,3},{2,0},{3,1},{4,6},{5,7},{6,4},{7,5},{8,10},{9,11},{10,... | collective-permute-start | bytes 344072 | tf_op jit(solution)/shard_map/ppermute | solution.py:23
  114.1 4.9 %collective-permute-start.40 = (bf16[32,1792]{1,0:T(8,128)(2,1)S(1)}, bf16[32,1792]{1,0:T(8,128)(2,1)S(1)}, u32[]{:S(2)}, u32[]{:S(2)}) collective-permute-start(bf16[32,1792]{1,0:T(8,128)(2,1)S(1)} %fusion.2.refs_0_), channel_id=1, source_target_pairs={{0,2},{1,3},{2,0},{3,1},{4,6},{5,7},{6,4},{7,5},{8,10},{9,11},{10,... | collective-permute-start | bytes 344072 | tf_op jit(solution)/shard_map/ppermute | solution.py:23
  115.7 3.9 %collective-permute-start.39 = (bf16[32,1792]{1,0:T(8,128)(2,1)S(1)}, bf16[32,1792]{1,0:T(8,128)(2,1)S(1)}, u32[]{:S(2)}, u32[]{:S(2)}) collective-permute-start(bf16[32,1792]{1,0:T(8,128)(2,1)S(1)} %fusion.2.refs_0_), channel_id=1, source_target_pairs={{0,1},{1,0},{2,3},{3,2},{4,5},{5,4},{6,7},{7,6},{8,9},{9,8},{10,11... | collective-permute-start | bytes 344072 | tf_op jit(solution)/shard_map/ppermute | solution.py:23
  119.0 1.3 collective-permute-start.41
  123.4 6.4 %collective-permute-start.43 = (bf16[32,2048]{1,0:T(8,128)(2,1)S(1)}, bf16[32,2048]{1,0:T(8,128)(2,1)S(1)}, u32[]{:S(2)}, u32[]{:S(2)}) collective-permute-start(bf16[32,2048]{1,0:T(8,128)(2,1)S(1)} %get-tuple-element.54), channel_id=1, source_target_pairs={{0,4},{4,0},{8,12},{12,8},{16,20},{20,16},{24,28},{28,24},{1,5},{5... | collective-permute-start | bytes 393224 | tf_op jit(solution)/shard_map/ppermute | solution.py:23
  125.1 7.4 %collective-permute-start.42 = (bf16[32,2048]{1,0:T(8,128)(2,1)S(1)}, bf16[32,2048]{1,0:T(8,128)(2,1)S(1)}, u32[]{:S(2)}, u32[]{:S(2)}) collective-permute-start(bf16[32,2048]{1,0:T(8,128)(2,1)S(1)} %get-tuple-element.52), channel_id=1, source_target_pairs={{0,4},{4,0},{8,12},{12,8},{16,20},{20,16},{24,28},{28,24},{1,5},{5... | collective-permute-start | bytes 393224 | tf_op jit(solution)/shard_map/ppermute | solution.py:23
  129.8 6.0 %collective-permute-start.44 = (bf16[16,2048]{1,0:T(8,128)(2,1)S(1)}, bf16[16,2048]{1,0:T(8,128)(2,1)S(1)}, u32[]{:S(2)}, u32[]{:S(2)}) collective-permute-start(bf16[16,2048]{1,0:T(8,128)(2,1)S(1)} %get-tuple-element.55), channel_id=1, source_target_pairs={{0,16},{4,20},{8,24},{12,28},{16,0},{20,4},{24,8},{28,12},{1,17},{... | collective-permute-start | bytes 196616 | tf_op jit(solution)/shard_map/ppermute | solution.py:23
  130.9 6.2 %collective-permute-start.45 = (bf16[16,2048]{1,0:T(8,128)(2,1)S(1)}, bf16[16,2048]{1,0:T(8,128)(2,1)S(1)}, u32[]{:S(2)}, u32[]{:S(2)}) collective-permute-start(bf16[16,2048]{1,0:T(8,128)(2,1)S(1)} %get-tuple-element.56), channel_id=1, source_target_pairs={{0,24},{4,28},{8,16},{12,20},{16,8},{20,12},{24,0},{28,4},{1,25},{... | collective-permute-start | bytes 196616 | tf_op jit(solution)/shard_map/ppermute | solution.py:23
  132.6 5.0 %collective-permute-start.46 = (bf16[16,2048]{1,0:T(8,128)(2,1)S(1)}, bf16[16,2048]{1,0:T(8,128)(2,1)S(1)}, u32[]{:S(2)}, u32[]{:S(2)}) collective-permute-start(bf16[16,2048]{1,0:T(8,128)(2,1)S(1)} %get-tuple-element.57), channel_id=1, source_target_pairs={{0,8},{4,12},{8,0},{12,4},{16,24},{20,28},{24,16},{28,20},{1,9},{5... | collective-permute-start | bytes 196616 | tf_op jit(solution)/shard_map/ppermute | solution.py:23
  (2 other events, 1.5 us)

commit v4 on v3

--- a/solution.py
+++ b/solution.py
@@ -37,6 +37,7 @@
 SMEM = pl.BlockSpec(memory_space=pltpu.SMEM)
 VMEM = pl.BlockSpec(memory_space=pltpu.VMEM)
 ANY = pl.BlockSpec(memory_space=pl.ANY)
+HBM = pl.BlockSpec(memory_space=pltpu.HBM)
 
 
 def call(body, outs, ins, specs, scratch=(), limit=16 << 20, flops=0, moved=0):
@@ -95,39 +96,33 @@
     return columns
 
 
-def multiply(left_ref, w_ref, write):
+def multiply(left, w_ref, write):
     columns = w_ref.shape[1]
     tile = tiles(columns)
-    left = left_ref[...]
-
-    def turn(i, _):
-        first = pl.multiple_of(i * tile, tile)
-        write(first, tile, jnp.dot(left, w_ref[:, pl.ds(first, tile)], preferred_element_type=F32))
-        return 0
-
-    if tile == columns:
-        write(0, tile, jnp.dot(left, w_ref[...], preferred_element_type=F32))
-    else:
-        lax.fori_loop(0, columns // tile, turn, 0)
-
-
-def hold(w, after):
-    pieces = 4 if w.shape[0] % 64 == 0 else 1
-    rows = w.shape[0] // pieces
-
-    def body(w_ref, after_ref, out_ref, sems):
-        copies = [
-            pltpu.make_async_copy(w_ref.at[pl.ds(i * rows, rows)], out_ref.at[pl.ds(i * rows, rows)], sems.at[i])
-            for i in range(pieces)
-        ]
-        for copy in copies:
-            copy.start()
-        for copy in copies:
-            copy.wait()
-
-    return call(
-        body, shaped(w.shape), (w, after), [ANY, ANY], [pltpu.SemaphoreType.DMA((pieces,))], moved=2 * w.size
-    )
+    for first in range(0, columns, tile):
+        write(first, tile, jnp.dot(left, w_ref[:, first : first + tile], preferred_element_type=F32))
+
+
+def streamed(w_hbm, w_ref, sems):
+    columns = w_ref.shape[1]
+    tile = tiles(columns)
+    copies = [
+        pltpu.make_async_copy(w_hbm.at[:, pl.ds(first, tile)], w_ref.at[:, pl.ds(first, tile)], sems.at[i])
+        for i, first in enumerate(range(0, columns, tile))
+    ]
+    for copy in copies:
+        copy.start()
+
+    def run(left, write):
+        for i, first in enumerate(range(0, columns, tile)):
+            copies[i].wait()
+            write(first, tile, jnp.dot(left, w_ref[:, first : first + tile], preferred_element_type=F32))
+
+    return run
+
+
+def stream_scratch(w):
+    return [pltpu.VMEM(w.shape, BF16), pltpu.SemaphoreType.DMA((w.shape[1] // tiles(w.shape[1]),))]
 
 
 def stack_tokens(x_first, x_second):
@@ -145,18 +140,17 @@
         body,
         shaped((2 * part_dev, features)),
         (x_first, x_second),
-        [ANY, ANY],
+        [HBM, HBM],
         [pltpu.VMEM(x_first.shape, BF16), pltpu.VMEM(x_first.shape, BF16), pltpu.SemaphoreType.DMA((2,))],
         moved=4 * x_first.size * 2,
     )
 
 
-def pack(cache_keys, cache_values, where, after):
+def pack(cache_keys, cache_values, after):
     groups = lax.axis_size("dp")
     part_dev, span, _ = cache_keys.shape
-    shape = (groups // 2, 2, part_dev, span, HD)
-
-    def body(where_ref, keys_hbm, values_hbm, after_ref, keep_ref, send_ref, keys_ref, values_ref, sems):
+
+    def body(keys_hbm, values_hbm, after_ref, out_ref, keys_ref, values_ref, sems):
         copies = [
             pltpu.make_async_copy(keys_hbm, keys_ref, sems.at[0]),
             pltpu.make_async_copy(values_hbm, values_ref, sems.at[1]),
@@ -165,30 +159,19 @@
             copy.start()
         for copy in copies:
             copy.wait()
-        for k in range(groups):
-            head = lax.div((where_ref[0] ^ k) * KVH, groups)
-            lanes = pl.ds(pl.multiple_of(head * HD, HD), HD)
-            out_ref = send_ref if k % 2 else keep_ref
-            out_ref[k // 2, 0] = keys_ref[:, :, lanes]
-            out_ref[k // 2, 1] = values_ref[:, :, lanes]
+        for g in range(groups):
+            first = g * KVH // groups * HD
+            out_ref[g, 0] = keys_ref[:, :, first : first + HD]
+            out_ref[g, 1] = values_ref[:, :, first : first + HD]
 
     return call(
         body,
-        (shaped(shape), shaped(shape)),
-        (where, cache_keys, cache_values, after),
-        [SMEM, ANY, ANY, ANY],
+        shaped((groups, 2, part_dev, span, HD)),
+        (cache_keys, cache_values, after),
+        [HBM, HBM, ANY],
         [pltpu.VMEM(cache_keys.shape, BF16), pltpu.VMEM(cache_keys.shape, BF16), pltpu.SemaphoreType.DMA((2,))],
         moved=8 * cache_keys.size,
     )
-
-
-def move_cache(keep, send):
-    groups = lax.axis_size("dp")
-    tensor = lax.axis_size("tensor")
-    both = jnp.stack([keep, swap(send, "dp", 1)], axis=1)
-    both = jnp.concatenate([both[:1]] + [swap(both[i : i + 1], "dp", 2 * i) for i in range(1, groups // 2)])
-    both = both.reshape(groups * both.shape[2] * both.shape[3], *both.shape[4:])
-    return gather_blocks(both)
 
 
 def lift(where_ref, gain_ref, block_refs, h_ref, ss_ref, absolute):
@@ -234,22 +217,30 @@
     )
 
 
-def project(h, w):
+def project(h, w, after=None):
     half = h.shape[0] // 2
 
-    def body(h_ref, w_ref, keep_ref, send_ref):
+    def body(h_ref, w_ref, *refs):
+        run = None if after is None else streamed(w_ref, refs[-2], refs[-1])
+        keep_ref, send_ref = refs[:2] if after is None else refs[1:3]
+        left = h_ref[...]
+
         def write(first, tile, product):
-            keep_ref[:, pl.ds(first, tile)] = product[:half]
-            send_ref[:, pl.ds(first, tile)] = product[half:].astype(BF16)
-
-        multiply(h_ref, w_ref, write)
+            keep_ref[:, first : first + tile] = product[:half]
+            send_ref[:, first : first + tile] = product[half:].astype(BF16)
+
+        if run is None:
+            multiply(left, w_ref, write)
+        else:
+            run(left, write)
 
     columns = w.shape[1]
     return call(
         body,
         (shaped((half, columns), F32), shaped((half, columns))),
-        (h, w),
-        [VMEM] * 2,
+        (h, w) if after is None else (h, w, after),
+        [VMEM] * 2 if after is None else [VMEM, HBM, ANY],
+        () if after is None else stream_scratch(w),
         flops=4 * half * w.size,
         moved=2 * w.size,
     )
@@ -266,10 +257,10 @@
         lift(where_ref, gain_ref, block_refs, h_ref, ss_ref, False)
 
         def write(first, tile, product):
-            keep_ref[:, pl.ds(first, tile)] = product[:half]
-            send_ref[:, pl.ds(first, tile)] = product[half:].astype(BF16)
-
-        multiply(h_ref, w_ref, write)
+            keep_ref[:, first : first + tile] = product[:half]
+            send_ref[:, first : first + tile] = product[half:].astype(BF16)
+
+        multiply(h_ref[...], w_ref, write)
         squares = ss_ref[...]
         high = squares.astype(BF16).astype(F32)
         lane = lax.broadcasted_iota(jnp.int32, squares.shape, 1)
@@ -288,7 +279,7 @@
     )
 
 
-def project_back(where, blocks, w):
+def project_back(where, blocks, w, stream):
     groups = lax.axis_size("dp")
     rows, depth = blocks[0].shape
     near = groups // len(blocks)
@@ -298,7 +289,8 @@
     columns = w.shape[1]
 
     def body(where_ref, *refs):
-        block_refs, (w_ref, keep_ref, far_ref, close_ref, left) = refs[: len(blocks)], refs[len(blocks) :]
+        block_refs, (w_ref, keep_ref, far_ref, close_ref, left) = refs[: len(blocks)], refs[len(blocks) :][:5]
+        run = streamed(w_ref, refs[-2], refs[-1]) if stream else None
         d, t = where_ref[0], where_ref[1]
         for k, block_ref in enumerate(block_refs):
             for i in range(near):
@@ -306,19 +298,22 @@
                 left[pl.ds(pl.multiple_of(place * pair, pair), pair), :] = block_ref[i * pair : (i + 1) * pair, :]
 
         def write(first, tile, product):
-            keep_ref[:, pl.ds(first, tile)] = product[:half]
+            keep_ref[:, first : first + tile] = product[:half]
             middle = half + half // 2
-            close_ref[:, pl.ds(first, tile)] = product[half:middle].astype(BF16)
-            far_ref[:, pl.ds(first, tile)] = product[middle:].astype(BF16)
-
-        multiply(left, w_ref, write)
+            close_ref[:, first : first + tile] = product[half:middle].astype(BF16)
+            far_ref[:, first : first + tile] = product[middle:].astype(BF16)
+
+        if stream:
+            run(left[...], write)
+        else:
+            multiply(left[...], w_ref, write)
 
     return call(
         body,
         (shaped((half, columns), F32), shaped((half // 2, columns)), shaped((half // 2, columns))),
         (where, *blocks, w),
-        [SMEM] + [VMEM] * (1 + len(blocks)),
-        [pltpu.VMEM((total, depth), BF16)],
+        [SMEM] + [VMEM] * len(blocks) + [HBM if stream else VMEM],
+        [pltpu.VMEM((total, depth), BF16)] + (stream_scratch(w) if stream else []),
         flops=2 * total * w.size,
         moved=2 * w.size,
     )
@@ -373,7 +368,7 @@
     tensor, groups, part_dev, span, n_q, n_kv = sizes
     q_refs, kv_refs = refs[:n_q], refs[n_q : n_q + n_kv]
     cache_refs, (out_ref, keys_ref, values_ref, scale_ref) = refs[n_q + n_kv : n_q + n_kv + tensor], refs[n_q + n_kv + tensor :]
-    d, t = where_ref[0], where_ref[1]
+    t = where_ref[1]
     near = groups // tensor
     parts = near * part_dev
     pair = 2 * part_dev
@@ -408,9 +403,9 @@
 
         def bring(i, _, step=step):
             if step == 0:
-                block, member = (t * near + lax.div(i, part_dev)) ^ d, lax.rem(i, part_dev)
+                block, member = t * near + lax.div(i, part_dev), lax.rem(i, part_dev)
             else:
-                block, member = lax.div(anc_ref[i], part_dev) ^ d, lax.rem(anc_ref[i], part_dev)
+                block, member = lax.div(anc_ref[i], part_dev), lax.rem(anc_ref[i], part_dev)
             place = block * pair + member
             for k in range(tensor):
                 start = pl.multiple_of(i * ctx + k * span, 8)
@@ -543,14 +538,13 @@
 
     x = stack_tokens(x_first, x_second)
     blocks = gather_rows(x)
-    held_keyval = hold(w_keyval, x)
-    held_query = hold(w_query, x)
-    cache = move_cache(*pack(cache_keys, cache_values, where, x))
-
-    h, squares, keyvals = project_keyval(where, blocks, attn_gain, held_keyval)
+    cache = lax.all_to_all(pack(cache_keys, cache_values, x), "dp", split_axis=0, concat_axis=0, tiled=True)
+    cache = cache.reshape(groups * pair, span, HD)
+    caches = gather_blocks(cache)
+
+    h, squares, keyvals = project_keyval(where, blocks, attn_gain, w_keyval)
     new_kv = move_keyvals(keyvals)
-    queries, queries_arrived = sum_blocks(*project(h, held_query))
-    held_out = hold(w_out, h)
+    queries, queries_arrived = sum_blocks(*project(h, w_query, cache))
     message = jnp.concatenate([new_kv, split_ss(squares[:, 0])], axis=1)
     bits = 1
     while bits < tensor:
@@ -573,25 +567,22 @@
     targets = jnp.tile(targets, (heads, 1)).astype(jnp.int32)
     rope = rope_tables(context) + rope_tables(context + 1)
     rope = jnp.asarray(np.stack(rope + (np.full(HD, width, np.float32),) * 4))
-    mixed = attention(where, anc, rope, targets, [queries] + queries_arrived, [message, arrived], cache, part_dev)
-
-    keep, far, close = project_back(where, gather_blocks(mixed), held_out)
-    held_gate = hold(w_gate, far)
-    held_up = hold(w_up, far)
+    mixed = attention(where, anc, rope, targets, [queries] + queries_arrived, [message, arrived], caches, part_dev)
+
+    keep, far, close = project_back(where, gather_blocks(mixed), w_out, True)
     attn_part, residual = finish(*sum_rows(keep, far, close, pair), x)
 
     hidden_cols = w_gate.shape[1]
-    h, keep, send = project_gate(where, gather_rows(residual), ffn_gain, held_gate)
+    h, keep, send = project_gate(where, gather_rows(residual), ffn_gain, w_gate)
     gate, gate_arrived = sum_blocks(keep, send)
-    up, up_arrived = sum_blocks(*project(h, held_up))
-    held_down = hold(w_down, h)
+    up, up_arrived = sum_blocks(*project(h, w_up))
     for piece in gate_arrived:
         gate = gate + piece.astype(F32)
     for piece in up_arrived:
         up = up + piece.astype(F32)
     scale = lax.rsqrt((gate[:, hidden_cols] + gate[:, hidden_cols + 1]) / width + EPS)[:, None]
     hidden = jax.nn.silu(gate[:, :hidden_cols] * scale) * (up * scale)
-    keep, far, close = project_back(where, gather_blocks(hidden.astype(BF16)), held_down)
+    keep, far, close = project_back(where, gather_blocks(hidden.astype(BF16)), w_down, False)
     (ffn_part,) = finish(*sum_rows(keep, far, close, pair))
     return (attn_part.reshape(2, part_dev, features), ffn_part.reshape(2, part_dev, features))
 

time: 139 us -> 146 us (1.050)
  other arithmetic: 0.95 us -> 9.09 us
  local copies, waits for them, and re-layouts: 13.7 us -> 20 us
  waiting for transfers between devices: 48.2 us -> 45.3 us
  Pallas kernels: 20.4 us -> 17.6 us
    ppermute x45 -> x41, starting transfers between devices: 51.8 us -> 42.7 us  [swap(): return lax.ppermute(x, axis, [(i, i ^ bits) for i in range(size)])]
    ppermute x45 -> x41, waiting for transfers between devices: 48.2 us -> 42.7 us  [swap(): return lax.ppermute(x, axis, [(i, i ^ bits) for i in range(size)])]
    all_to_all x0 -> x1, starting transfers between devices: none -> 4.89 us  [local(): lax.all_to_all(pack(cache_keys, cache_values, x), 'dp', split_axis=0, con...]
    ppermute x1, starting transfers between devices: 1.37 us -> 4.17 us  [move_keyvals(): lax.ppermute(jnp.where(lower, halves[1], halves[0]), 'dp', [(i, 2 * i + 1...]
    pallas_call x21 -> x15, Pallas kernels: 20.4 us -> 17.6 us  [call(): pl.pallas_call(body, out_shape=outs, in_specs=specs, out_specs=jax.tree.m...]
    ppermute x1, waiting for transfers between devices: 0.01 us -> 2.53 us  [move_keyvals(): lax.ppermute(jnp.where(lower, halves[1], halves[0]), 'dp', [(i, 2 * i + 1...]
    another operation x2, other arithmetic: 0.09 us -> 2.52 us  [local(): jnp.stack([row_of(own, 0), row_of(anc, 0), row_of(own, 1)], axis=1)]
    add x3, other arithmetic: 0.13 us -> 1.8 us  [sum_blocks(): keep + swap(send, 'tensor', 1).astype(F32)]
  transfers between devices with their start and end apart: 47 -> 44, of which waited for: 23 -> 21; matrix products, arithmetic and copies ran while one was open for 1% -> 11% of each run, Pallas kernels for 6% -> 4%
where the time goes in v4:
time: 146 us; the launch traced here: 145 us
  starting transfers between devices  52.4 us (36%)
  waiting for transfers between devices  45.3 us (31%)
  local copies, waits for them, and re-layouts  20 us (14%)
  Pallas kernels  17.6 us (12%)
  other arithmetic  9.09 us (6%)
    ppermute x41, waiting for transfers between devices, swap(): return lax.ppermute(x, axis, [(i, i ^ bits) for i in range(size)])  42.7 us
    ppermute x41, starting transfers between devices, swap(): return lax.ppermute(x, axis, [(i, i ^ bits) for i in range(size)])  42.7 us
    pallas_call x15, Pallas kernels, call(): pl.pallas_call(body, out_shape=outs, in_specs=specs, out_specs=jax.tree.m...  17.6 us
    unnamed x38, local copies, waits for them, and re-layouts  12.9 us
    all_to_all x1, starting transfers between devices, local(): lax.all_to_all(pack(cache_keys, cache_values, x), 'dp', split_axis=0, con...  4.89 us
    ppermute x1, starting transfers between devices, move_keyvals(): lax.ppermute(jnp.where(lower, halves[1], halves[0]), 'dp', [(i, 2 * i + 1...  4.17 us
  transfers between devices with their start and end apart: 44, of which 21 were waited for; matrix products, arithmetic and copies ran while one was open for 11% of the time, Pallas kernels for 4%

profile of v4, /device:TPU:0, one launch (start us, length us, event | category | flops | bytes accessed | tf_op | source)
XLA Modules:
  0.0 145.4 jit_solution(18010898417382625015)
XLA Ops:
  2.2 5.1 %collective-permute-start.5 = (bf16[16,2048]{1,0:T(8,128)(2,1)S(1)}, bf16[16,2048]{1,0:T(8,128)(2,1)S(1)}, u32[]{:S(2)}, u32[]{:S(2)}) collective-permute-start(bf16[16,2048]{1,0:T(8,128)(2,1)S(1)} %shard_map.149.refs_0_.after_ref.refs_3_), channel_id=1, source_target_pairs={{0,24},{4,28},{8,16},{12,20},{16,8},{20,12},{24,0},{28,4},{1,25},{... | collective-permute-start | bytes 196616 | tf_op jit(solution)/shard_map/ppermute | solution.py:23
  8.0 1.6 %collective-permute-start = (bf16[16,2048]{1,0:T(8,128)(2,1)S(1)}, bf16[16,2048]{1,0:T(8,128)(2,1)S(1)}, u32[]{:S(2)}, u32[]{:S(2)}) collective-permute-start(bf16[16,2048]{1,0:T(8,128)(2,1)S(1)} %shard_map.149.refs_0_.after_ref.refs_3_), channel_id=1, source_target_pairs={{0,4},{4,0},{8,12},{12,8},{16,20},{20,16},{24,28},{28,24},{1,5},{5... | collective-permute-start | bytes 196616 | tf_op jit(solution)/shard_map/ppermute | solution.py:23
  9.6 0.9 copy-done.6
  11.4 1.1 shard_map.151
  12.5 4.9 %all-to-all-start = ((bf16[8,2,8,8,128]{4,3,2,1,0:T(8,128)(2,1)}), bf16[8,2,8,8,128]{4,3,2,1,0:T(8,128)(2,1)S(1)}, u32[]{:S(2)}, u32[]{:S(2)}) async-start(bf16[8,2,8,8,128]{4,3,2,1,0:T(8,128)(2,1)} %shard_map.151), calls=%async_computation | async-start | bytes 524288 | tf_op jit(solution)/shard_map/all_to_all | solution.py:541
  18.0 2.0 %collective-permute-start.6 = (bf16[16,2048]{1,0:T(8,128)(2,1)S(1)}, bf16[16,2048]{1,0:T(8,128)(2,1)S(1)}, u32[]{:S(2)}, u32[]{:S(2)}) collective-permute-start(bf16[16,2048]{1,0:T(8,128)(2,1)S(1)} %collective-permute-done.5.refs_6_), channel_id=1, source_target_pairs={{0,4},{4,0},{8,12},{12,8},{16,20},{20,16},{24,28},{28,24},{1,5},{5... | collective-permute-start | bytes 196616 | tf_op jit(solution)/shard_map/ppermute | solution.py:23
  20.1 2.0 %collective-permute-start.2 = (bf16[16,2048]{1,0:T(8,128)(2,1)S(1)}, bf16[16,2048]{1,0:T(8,128)(2,1)S(1)}, u32[]{:S(2)}, u32[]{:S(2)}) collective-permute-start(bf16[16,2048]{1,0:T(8,128)(2,1)S(1)} %collective-permute-done.1.refs_2_), channel_id=1, source_target_pairs={{0,4},{4,0},{8,12},{12,8},{16,20},{20,16},{24,28},{28,24},{1,5},{5... | collective-permute-start | bytes 196616 | tf_op jit(solution)/shard_map/ppermute | solution.py:23
  22.1 2.1 %collective-permute-done.6.refs_7_ = bf16[16,2048]{1,0:T(8,128)(2,1)S(1)} collective-permute-done((bf16[16,2048]{1,0:T(8,128)(2,1)S(1)}, bf16[16,2048]{1,0:T(8,128)(2,1)S(1)}, u32[]{:S(2)}, u32[]{:S(2)}) %collective-permute-start.6) | collective-permute-done | bytes 65568 | tf_op jit(solution)/shard_map/ppermute | solution.py:23
  25.0 1.1 collective-permute-done.2.refs_3_
  26.1 1.2 copy-done.2
  28.0 1.0 shard_map.150
  30.5 4.2 %collective-permute-start.10 = (bf16[128,128]{1,0:T(8,128)(2,1)S(1)}, bf16[128,128]{1,0:T(8,128)(2,1)S(1)}, u32[]{:S(2)}, u32[]{:S(2)}) collective-permute-start(bf16[128,128]{1,0:T(8,128)(2,1)S(1)} %get-tuple-element.59), channel_id=1, source_target_pairs={{0,4},{4,12},{8,20},{12,28},{16,0},{20,8},{24,16},{28,24},{1,5},{5... | collective-permute-start | bytes 98312 | tf_op jit(solution)/shard_map/ppermute | solution.py:497
  34.9 2.5 %collective-permute-done.10 = bf16[128,128]{1,0:T(8,128)(2,1)S(1)} collective-permute-done((bf16[128,128]{1,0:T(8,128)(2,1)S(1)}, bf16[128,128]{1,0:T(8,128)(2,1)S(1)}, u32[]{:S(2)}, u32[]{:S(2)}) %collective-permute-start.10) | collective-permute-done | bytes 32800 | tf_op jit(solution)/shard_map/ppermute | solution.py:497
  37.5 1.3 fusion.12
  39.5 1.0 slice_add_fusion.2
  40.6 1.6 %collective-permute-start.14 = (bf16[128,8,128]{2,1,0:T(8,128)(2,1)S(1)}, bf16[128,8,128]{2,1,0:T(8,128)(2,1)}, u32[]{:S(2)}, u32[]{:S(2)}) collective-permute-start(bf16[128,8,128]{2,1,0:T(8,128)(2,1)S(1)} %bitcast.17), channel_id=1, source_target_pairs={{0,2},{1,3},{2,0},{3,1},{4,6},{5,7},{6,4},{7,5},{8,10},{9,11},{10,... | collective-permute-start | bytes 786440 | tf_op jit(solution)/shard_map/ppermute | solution.py:23
  42.2 2.2 %copy-done = bf16[2048,1024]{1,0:T(8,128)(2,1)S(1)} copy-done((bf16[2048,1024]{1,0:T(8,128)(2,1)S(1)}, bf16[2048,1024]{1,0:T(8,128)(2,1)}, u32[]{:S(2)}) %copy-start) | copy-done | bytes 4194328
  44.4 1.0 copy-done.4
  45.4 3.0 %shard_map.152 = (f32[64,1024]{1,0:T(8,128)S(1)}, bf16[64,1024]{1,0:T(8,128)(2,1)}) custom-call(bf16[128,2048]{1,0:T(8,128)(2,1)S(1)} %copy-done.4, bf16[2048,1024]{1,0:T(8,128)(2,1)S(1)} %copy-done, bf16[128,8,128]{2,1,0:T(8,128)(2,1)S(1)} %bitcast.18), custom_call_target="tpu_custom_call" | custom-call | flops 536870912 | bytes 4194304 | tf_op jit(solution)/shard_map/pallas_call | solution.py:44
  49.8 0.9 slice.115
  50.7 1.4 copy.31
  52.1 1.4 fusion.6.refs_2_
  54.5 1.7 %convert_add_fusion.2 = f32[64,1024]{1,0:T(8,128)} fusion(f32[64,1024]{1,0:T(8,128)} %copy-done.5, bf16[64,1024]{1,0:T(8,128)(2,1)} %collective-permute-done.7), kind=kLoop, calls=%fused_computation.2 | loop fusion | flops 131072 | bytes 655360 | tf_op jit(solution)/shard_map/add | solution.py:84
  56.3 1.5 %slice.116 = bf16[32,1024]{1,0:T(8,128)(2,1)} slice(f32[64,1024]{1,0:T(8,128)} %convert_add_fusion.2), slice={[32:64], [0:1024]} | slice | bytes 131072 | tf_op jit(solution)/shard_map/slice | solution.py:85
  57.8 1.5 %collective-permute-start.8 = (bf16[32,1024]{1,0:T(8,128)(2,1)}, bf16[32,1024]{1,0:T(8,128)(2,1)S(1)}, u32[]{:S(2)}, u32[]{:S(2)}) collective-permute-start(bf16[32,1024]{1,0:T(8,128)(2,1)} %slice.116), channel_id=1, source_target_pairs={{0,2},{1,3},{2,0},{3,1},{4,6},{5,7},{6,4},{7,5},{8,10},{9,11},{10,... | collective-permute-start | bytes 196616 | tf_op jit(solution)/shard_map/ppermute | solution.py:23
  59.3 1.3 pad_add_fusion
  60.6 1.3 copy.25
  61.9 0.9 slice.70.refs_0_
  64.3 3.0 %shard_map.153.refs_0_ = bf16[32,1024]{1,0:T(8,128)(2,1)S(1)} custom-call(s32[2]{0:T(128)S(1)} %pad_add_fusion.1.where_ref, s32[16]{0:T(128)S(1)} %get-tuple-element.55.anc_ref, f32[8,128]{1,0:T(8,128)S(1)} %copy-done.12, s32[128,3]{1,0:T(8,128)S(1)} %bitcast.21, f32[32,1024]{1,0:T(8,128)S(1)} %slice.70.refs_0_, ...), custom_call_target="tpu_custom_call" | custom-call | flops 1073741824 | bytes 4194304 | tf_op jit(solution)/shard_map/pallas_call | solution.py:44
  67.3 1.0 collective-permute-start.17
  68.3 3.3 %collective-permute-done.17.refs_2_ = bf16[32,1024]{1,0:T(8,128)(2,1)S(1)} collective-permute-done((bf16[32,1024]{1,0:T(8,128)(2,1)S(1)}, bf16[32,1024]{1,0:T(8,128)(2,1)S(1)}, u32[]{:S(2)}, u32[]{:S(2)}) %collective-permute-start.17) | collective-permute-done | bytes 65568 | tf_op jit(solution)/shard_map/ppermute | solution.py:23
  71.7 1.2 collective-permute-done.18.refs_3_
  72.9 2.2 %copy-done.1 = bf16[1024,2048]{1,0:T(8,128)(2,1)S(1)} copy-done((bf16[1024,2048]{1,0:T(8,128)(2,1)S(1)}, bf16[1024,2048]{1,0:T(8,128)(2,1)}, u32[]{:S(2)}) %copy-start.1) | copy-done | bytes 4194328
  75.1 3.5 %shard_map.154 = (f32[64,2048]{1,0:T(8,128)S(1)}, bf16[32,2048]{1,0:T(8,128)(2,1)S(1)}, bf16[32,2048]{1,0:T(8,128)(2,1)S(1)}) custom-call(s32[2]{0:T(128)S(1)} %pad_add_fusion.1.where_ref, bf16[32,1024]{1,0:T(8,128)(2,1)S(1)} %shard_map.153.refs_0_, bf16[32,1024]{1,0:T(8,128)(2,1)S(1)} %collective-permute-done.16.refs_1_, ...), custom_call_target="tpu_custom_call" | custom-call | flops 536870912 | bytes 4194304 | tf_op jit(solution)/shard_map/pallas_call | solution.py:44
  78.6 1.5 %collective-permute-start.19 = (bf16[32,2048]{1,0:T(8,128)(2,1)S(1)}, bf16[32,2048]{1,0:T(8,128)(2,1)S(1)}, u32[]{:S(2)}, u32[]{:S(2)}) collective-permute-start(bf16[32,2048]{1,0:T(8,128)(2,1)S(1)} %get-tuple-element.34), channel_id=1, source_target_pairs={{0,4},{4,0},{8,12},{12,8},{16,20},{20,16},{24,28},{28,24},{1,5},{5... | collective-permute-start | bytes 393224 | tf_op jit(solution)/shard_map/ppermute | solution.py:23
  80.7 4.3 %collective-permute-done.19.arrived_ref = bf16[32,2048]{1,0:T(8,128)(2,1)S(1)} collective-permute-done((bf16[32,2048]{1,0:T(8,128)(2,1)S(1)}, bf16[32,2048]{1,0:T(8,128)(2,1)S(1)}, u32[]{:S(2)}, u32[]{:S(2)}) %collective-permute-start.19) | collective-permute-done | bytes 131104 | tf_op jit(solution)/shard_map/ppermute | solution.py:23
  85.1 2.3 %collective-permute-start.23 = (bf16[16,2048]{1,0:T(8,128)(2,1)S(1)}, bf16[16,2048]{1,0:T(8,128)(2,1)S(1)}, u32[]{:S(2)}, u32[]{:S(2)}) collective-permute-start(bf16[16,2048]{1,0:T(8,128)(2,1)S(1)} %get-tuple-element.39), channel_id=1, source_target_pairs={{0,8},{4,12},{8,0},{12,4},{16,24},{20,28},{24,16},{28,20},{1,9},{5... | collective-permute-start | bytes 196616 | tf_op jit(solution)/shard_map/ppermute | solution.py:23
  87.4 1.5 %collective-permute-start.21 = (bf16[16,2048]{1,0:T(8,128)(2,1)S(1)}, bf16[16,2048]{1,0:T(8,128)(2,1)S(1)}, u32[]{:S(2)}, u32[]{:S(2)}) collective-permute-start(bf16[16,2048]{1,0:T(8,128)(2,1)S(1)} %get-tuple-element.37), channel_id=1, source_target_pairs={{0,16},{4,20},{8,24},{12,28},{16,0},{20,4},{24,8},{28,12},{1,17},{... | collective-permute-start | bytes 196616 | tf_op jit(solution)/shard_map/ppermute | solution.py:23
  88.9 2.8 %collective-permute-start.22 = (bf16[16,2048]{1,0:T(8,128)(2,1)S(1)}, bf16[16,2048]{1,0:T(8,128)(2,1)S(1)}, u32[]{:S(2)}, u32[]{:S(2)}) collective-permute-start(bf16[16,2048]{1,0:T(8,128)(2,1)S(1)} %get-tuple-element.38), channel_id=1, source_target_pairs={{0,24},{4,28},{8,16},{12,20},{16,8},{20,12},{24,0},{28,4},{1,25},{... | collective-permute-start | bytes 196616 | tf_op jit(solution)/shard_map/ppermute | solution.py:23
  91.8 4.1 %collective-permute-done.21.refs_0_ = bf16[16,2048]{1,0:T(8,128)(2,1)S(1)} collective-permute-done((bf16[16,2048]{1,0:T(8,128)(2,1)S(1)}, bf16[16,2048]{1,0:T(8,128)(2,1)S(1)}, u32[]{:S(2)}, u32[]{:S(2)}) %collective-permute-start.21) | collective-permute-done | bytes 65568 | tf_op jit(solution)/shard_map/ppermute | solution.py:23
  96.5 2.1 %collective-permute-start.29 = (bf16[16,2048]{1,0:T(8,128)(2,1)S(1)}, bf16[16,2048]{1,0:T(8,128)(2,1)S(1)}, u32[]{:S(2)}, u32[]{:S(2)}) collective-permute-start(bf16[16,2048]{1,0:T(8,128)(2,1)S(1)} %get-tuple-element.41.refs_0_), channel_id=1, source_target_pairs={{0,24},{4,28},{8,16},{12,20},{16,8},{20,12},{24,0},{28,4},{1,25},{... | collective-permute-start | bytes 196616 | tf_op jit(solution)/shard_map/ppermute | solution.py:23
  99.3 1.7 %collective-permute-start.25 = (bf16[16,2048]{1,0:T(8,128)(2,1)S(1)}, bf16[16,2048]{1,0:T(8,128)(2,1)S(1)}, u32[]{:S(2)}, u32[]{:S(2)}) collective-permute-start(bf16[16,2048]{1,0:T(8,128)(2,1)S(1)} %get-tuple-element.41.refs_0_), channel_id=1, source_target_pairs={{0,8},{4,12},{8,0},{12,4},{16,24},{20,28},{24,16},{28,20},{1,9},{5... | collective-permute-start | bytes 196616 | tf_op jit(solution)/shard_map/ppermute | solution.py:23
  100.9 1.2 collective-permute-start.24
  102.6 1.2 collective-permute-start.30
  104.2 1.1 collective-permute-start.28
  105.3 0.9 collective-permute-start.26
  106.9 1.6 %collective-permute-done.28.refs_5_ = bf16[16,2048]{1,0:T(8,128)(2,1)S(1)} collective-permute-done((bf16[16,2048]{1,0:T(8,128)(2,1)S(1)}, bf16[16,2048]{1,0:T(8,128)(2,1)S(1)}, u32[]{:S(2)}, u32[]{:S(2)}) %collective-permute-start.28) | collective-permute-done | bytes 65568 | tf_op jit(solution)/shard_map/ppermute | solution.py:23
  108.4 1.1 collective-permute-done.26.refs_3_
  109.6 1.8 %shard_map.158 = (bf16[128,2048]{1,0:T(8,128)(2,1)S(1)}, f32[64,1920]{1,0:T(8,128)S(1)}, bf16[64,1920]{1,0:T(8,128)(2,1)S(1)}) custom-call(s32[2]{0:T(128)S(1)} %pad_add_fusion.1.where_ref, f32[1,2048]{1,0:T(1,128)S(1)} %bitcast.24, bf16[16,2048]{1,0:T(8,128)(2,1)S(1)} %get-tuple-element.41.refs_0_, bf16[16,2048]{1,0:T(8,128)(2,1)S(1)} %collective-permute-done.24.refs_1_, ...), custom_call_target="tpu_custom_call" | custom-call | flops 939524096 | bytes 8388608 | tf_op jit(solution)/shard_map/pallas_call | solution.py:44
  111.5 1.1 shard_map.159
  113.2 1.0 collective-permute-start.32
  114.3 1.1 collective-permute-start.34
  115.5 4.0 %collective-permute-done.32 = bf16[32,1920]{1,0:T(8,128)(2,1)S(1)} collective-permute-done((bf16[32,1920]{1,0:T(8,128)(2,1)S(1)}, bf16[32,1920]{1,0:T(8,128)(2,1)S(1)}, u32[]{:S(2)}, u32[]{:S(2)}) %collective-permute-start.32) | collective-permute-done | bytes 122912 | tf_op jit(solution)/shard_map/ppermute | solution.py:23
  119.7 1.3 collective-permute-done.34
  121.2 1.0 collective-permute-start.36
  122.2 3.9 %collective-permute-done.36.refs_2_ = bf16[32,1792]{1,0:T(8,128)(2,1)S(1)} collective-permute-done((bf16[32,1792]{1,0:T(8,128)(2,1)S(1)}, bf16[32,1792]{1,0:T(8,128)(2,1)S(1)}, u32[]{:S(2)}, u32[]{:S(2)}) %collective-permute-start.36) | collective-permute-done | bytes 114720 | tf_op jit(solution)/shard_map/ppermute | solution.py:23
  126.0 1.3 collective-permute-done.37.refs_3_
  127.4 1.7 %shard_map.160 = (f32[64,2048]{1,0:T(8,128)S(1)}, bf16[32,2048]{1,0:T(8,128)(2,1)S(1)}, bf16[32,2048]{1,0:T(8,128)(2,1)S(1)}) custom-call(s32[2]{0:T(128)S(1)} %pad_add_fusion.1.where_ref, bf16[32,1792]{1,0:T(8,128)(2,1)S(1)} %fusion.2.refs_0_, bf16[32,1792]{1,0:T(8,128)(2,1)S(1)} %collective-permute-done.35.refs_1_, ...), custom_call_target="tpu_custom_call" | custom-call | flops 939524096 | bytes 7340032 | tf_op jit(solution)/shard_map/pallas_call | solution.py:44
  129.1 1.0 collective-permute-start.38
  130.1 1.1 collective-permute-start.39
  131.2 4.3 %collective-permute-done.38.arrived_ref = bf16[32,2048]{1,0:T(8,128)(2,1)S(1)} collective-permute-done((bf16[32,2048]{1,0:T(8,128)(2,1)S(1)}, bf16[32,2048]{1,0:T(8,128)(2,1)S(1)}, u32[]{:S(2)}, u32[]{:S(2)}) %collective-permute-start.38) | collective-permute-done | bytes 131104 | tf_op jit(solution)/shard_map/ppermute | solution.py:23
  135.6 1.9 %collective-permute-done.39.arrived_ref = bf16[32,2048]{1,0:T(8,128)(2,1)S(1)} collective-permute-done((bf16[32,2048]{1,0:T(8,128)(2,1)S(1)}, bf16[32,2048]{1,0:T(8,128)(2,1)S(1)}, u32[]{:S(2)}, u32[]{:S(2)}) %collective-permute-start.39) | collective-permute-done | bytes 131104 | tf_op jit(solution)/shard_map/ppermute | solution.py:23
  138.2 1.9 %collective-permute-start.41 = (bf16[16,2048]{1,0:T(8,128)(2,1)S(1)}, bf16[16,2048]{1,0:T(8,128)(2,1)S(1)}, u32[]{:S(2)}, u32[]{:S(2)}) collective-permute-start(bf16[16,2048]{1,0:T(8,128)(2,1)S(1)} %get-tuple-element.52), channel_id=1, source_target_pairs={{0,24},{4,28},{8,16},{12,20},{16,8},{20,12},{24,0},{28,4},{1,25},{... | collective-permute-start | bytes 196616 | tf_op jit(solution)/shard_map/ppermute | solution.py:23
  140.1 4.6 %collective-permute-done.40.refs_0_ = bf16[16,2048]{1,0:T(8,128)(2,1)S(1)} collective-permute-done((bf16[16,2048]{1,0:T(8,128)(2,1)S(1)}, bf16[16,2048]{1,0:T(8,128)(2,1)S(1)}, u32[]{:S(2)}, u32[]{:S(2)}) %collective-permute-start.40) | collective-permute-done | bytes 65568 | tf_op jit(solution)/shard_map/ppermute | solution.py:23
  (111 shorter events, 18.0 us)
Async XLA Ops:
  0.6 0.8 copy-start.8
  1.4 0.8 copy-start.9
  2.2 15.8 %collective-permute-start.5 = (bf16[16,2048]{1,0:T(8,128)(2,1)S(1)}, bf16[16,2048]{1,0:T(8,128)(2,1)S(1)}, u32[]{:S(2)}, u32[]{:S(2)}) collective-permute-start(bf16[16,2048]{1,0:T(8,128)(2,1)S(1)} %shard_map.149.refs_0_.after_ref.refs_3_), channel_id=1, source_target_pairs={{0,24},{4,28},{8,16},{12,20},{16,8},{20,12},{24,0},{28,4},{1,25},{... | collective-permute-start | bytes 196616 | tf_op jit(solution)/shard_map/ppermute | solution.py:23
  7.3 12.7 %collective-permute-start.3 = (bf16[16,2048]{1,0:T(8,128)(2,1)S(1)}, bf16[16,2048]{1,0:T(8,128)(2,1)S(1)}, u32[]{:S(2)}, u32[]{:S(2)}) collective-permute-start(bf16[16,2048]{1,0:T(8,128)(2,1)S(1)} %shard_map.149.refs_0_.after_ref.refs_3_), channel_id=1, source_target_pairs={{0,16},{4,20},{8,24},{12,28},{16,0},{20,4},{24,8},{28,12},{1,17},{... | collective-permute-start | bytes 196616 | tf_op jit(solution)/shard_map/ppermute | solution.py:23
  7.3 12.8 %collective-permute-start.1 = (bf16[16,2048]{1,0:T(8,128)(2,1)S(1)}, bf16[16,2048]{1,0:T(8,128)(2,1)S(1)}, u32[]{:S(2)}, u32[]{:S(2)}) collective-permute-start(bf16[16,2048]{1,0:T(8,128)(2,1)S(1)} %shard_map.149.refs_0_.after_ref.refs_3_), channel_id=1, source_target_pairs={{0,8},{4,12},{8,0},{12,4},{16,24},{20,28},{24,16},{28,20},{1,9},{5... | collective-permute-start | bytes 196616 | tf_op jit(solution)/shard_map/ppermute | solution.py:23
  8.0 14.1 %collective-permute-start = (bf16[16,2048]{1,0:T(8,128)(2,1)S(1)}, bf16[16,2048]{1,0:T(8,128)(2,1)S(1)}, u32[]{:S(2)}, u32[]{:S(2)}) collective-permute-start(bf16[16,2048]{1,0:T(8,128)(2,1)S(1)} %shard_map.149.refs_0_.after_ref.refs_3_), channel_id=1, source_target_pairs={{0,4},{4,0},{8,12},{12,8},{16,20},{20,16},{24,28},{28,24},{1,5},{5... | collective-permute-start | bytes 196616 | tf_op jit(solution)/shard_map/ppermute | solution.py:23
  9.6 0.9 copy-start.6
  10.5 0.9 copy-start.7
  12.5 28.1 %all-to-all-start = ((bf16[8,2,8,8,128]{4,3,2,1,0:T(8,128)(2,1)}), bf16[8,2,8,8,128]{4,3,2,1,0:T(8,128)(2,1)S(1)}, u32[]{:S(2)}, u32[]{:S(2)}) async-start(bf16[8,2,8,8,128]{4,3,2,1,0:T(8,128)(2,1)} %shard_map.151), calls=%async_computation | async-start | bytes 524288 | tf_op jit(solution)/shard_map/all_to_all | solution.py:541
  18.0 6.3 %collective-permute-start.6 = (bf16[16,2048]{1,0:T(8,128)(2,1)S(1)}, bf16[16,2048]{1,0:T(8,128)(2,1)S(1)}, u32[]{:S(2)}, u32[]{:S(2)}) collective-permute-start(bf16[16,2048]{1,0:T(8,128)(2,1)S(1)} %collective-permute-done.5.refs_6_), channel_id=1, source_target_pairs={{0,4},{4,0},{8,12},{12,8},{16,20},{20,16},{24,28},{28,24},{1,5},{5... | collective-permute-start | bytes 196616 | tf_op jit(solution)/shard_map/ppermute | solution.py:23
  20.0 5.0 %collective-permute-start.4 = (bf16[16,2048]{1,0:T(8,128)(2,1)S(1)}, bf16[16,2048]{1,0:T(8,128)(2,1)S(1)}, u32[]{:S(2)}, u32[]{:S(2)}) collective-permute-start(bf16[16,2048]{1,0:T(8,128)(2,1)S(1)} %collective-permute-done.3.refs_4_), channel_id=1, source_target_pairs={{0,4},{4,0},{8,12},{12,8},{16,20},{20,16},{24,28},{28,24},{1,5},{5... | collective-permute-start | bytes 196616 | tf_op jit(solution)/shard_map/ppermute | solution.py:23
  20.1 5.9 %collective-permute-start.2 = (bf16[16,2048]{1,0:T(8,128)(2,1)S(1)}, bf16[16,2048]{1,0:T(8,128)(2,1)S(1)}, u32[]{:S(2)}, u32[]{:S(2)}) collective-permute-start(bf16[16,2048]{1,0:T(8,128)(2,1)S(1)} %collective-permute-done.1.refs_2_), channel_id=1, source_target_pairs={{0,4},{4,0},{8,12},{12,8},{16,20},{20,16},{24,28},{28,24},{1,5},{5... | collective-permute-start | bytes 196616 | tf_op jit(solution)/shard_map/ppermute | solution.py:23
  26.0 1.2 copy-start.2
  27.3 0.7 copy-start.10
  29.0 0.8 copy-start.3
  29.9 5.0 %collective-permute-start.9 = (bf16[128,128]{1,0:T(8,128)(2,1)S(1)}, bf16[128,128]{1,0:T(8,128)(2,1)S(1)}, u32[]{:S(2)}, u32[]{:S(2)}) collective-permute-start(bf16[128,128]{1,0:T(8,128)(2,1)S(1)} %get-tuple-element.58), channel_id=1, source_target_pairs={{0,0},{4,8},{8,16},{12,24},{16,4},{20,12},{24,20},{28,28},{1,1},{5... | collective-permute-start | bytes 98312 | tf_op jit(solution)/shard_map/ppermute | solution.py:492
  30.5 6.9 %collective-permute-start.10 = (bf16[128,128]{1,0:T(8,128)(2,1)S(1)}, bf16[128,128]{1,0:T(8,128)(2,1)S(1)}, u32[]{:S(2)}, u32[]{:S(2)}) collective-permute-start(bf16[128,128]{1,0:T(8,128)(2,1)S(1)} %get-tuple-element.59), channel_id=1, source_target_pairs={{0,4},{4,12},{8,20},{12,28},{16,0},{20,8},{24,16},{28,24},{1,5},{5... | collective-permute-start | bytes 98312 | tf_op jit(solution)/shard_map/ppermute | solution.py:497
  37.4 1.4 collective-permute-start.11
  40.6 13.5 %collective-permute-start.14 = (bf16[128,8,128]{2,1,0:T(8,128)(2,1)S(1)}, bf16[128,8,128]{2,1,0:T(8,128)(2,1)}, u32[]{:S(2)}, u32[]{:S(2)}) collective-permute-start(bf16[128,8,128]{2,1,0:T(8,128)(2,1)S(1)} %bitcast.17), channel_id=1, source_target_pairs={{0,2},{1,3},{2,0},{3,1},{4,6},{5,7},{6,4},{7,5},{8,10},{9,11},{10,... | collective-permute-start | bytes 786440 | tf_op jit(solution)/shard_map/ppermute | solution.py:23
  42.2 2.2 %copy-start = (bf16[2048,1024]{1,0:T(8,128)(2,1)S(1)}, bf16[2048,1024]{1,0:T(8,128)(2,1)}, u32[]{:S(2)}) copy-start(bf16[2048,1024]{1,0:T(8,128)(2,1)} %w_ref.2) | copy-start | bytes 12582916
  44.4 1.0 copy-start.4
  45.4 64.1 %slice-start = ((s8[7340032]{0:T(1024)(128)(4,1)}), s8[3145728]{0:T(1024)(128)(4,1)S(1)}, s32[]{:S(2)}) async-start(s8[7340032]{0:T(1024)(128)(4,1)} %bitcast.11), calls=%async_computation.1 | async-start | bytes 6291456
  45.4 64.1 %copy-start.11 = (f32[2048]{0:T(1024)S(1)}, f32[2048]{0:T(1024)}, u32[]{:S(2)}) copy-start(f32[2048]{0:T(1024)} %param.20) | copy-start | bytes 24580
  48.4 0.7 copy-start.5
  49.1 5.5 %collective-permute-start.7 = (bf16[64,1024]{1,0:T(8,128)(2,1)}, bf16[64,1024]{1,0:T(8,128)(2,1)}, u32[]{:S(2)}, u32[]{:S(2)}) collective-permute-start(bf16[64,1024]{1,0:T(8,128)(2,1)} %get-tuple-element.30), channel_id=1, source_target_pairs={{0,1},{1,0},{2,3},{3,2},{4,5},{5,4},{6,7},{7,6},{8,9},{9,8},{10,11... | collective-permute-start | bytes 393224 | tf_op jit(solution)/shard_map/ppermute | solution.py:23
  53.5 9.3 %collective-permute-start.12 = (bf16[128,384]{1,0:T(8,128)(2,1)}, bf16[128,384]{1,0:T(8,128)(2,1)}, u32[]{:S(2)}, u32[]{:S(2)}) collective-permute-start(bf16[128,384]{1,0:T(8,128)(2,1)} %fusion.6.refs_2_), channel_id=1, source_target_pairs={{0,2},{1,3},{2,0},{3,1},{4,6},{5,7},{6,4},{7,5},{8,10},{9,11},{10,... | collective-permute-start | bytes 294920 | tf_op jit(solution)/shard_map/ppermute | solution.py:23
  54.0 8.8 %collective-permute-start.13 = (bf16[128,8,128]{2,1,0:T(8,128)(2,1)S(1)}, bf16[128,8,128]{2,1,0:T(8,128)(2,1)}, u32[]{:S(2)}, u32[]{:S(2)}) collective-permute-start(bf16[128,8,128]{2,1,0:T(8,128)(2,1)S(1)} %bitcast.19), channel_id=1, source_target_pairs={{0,1},{1,0},{2,3},{3,2},{4,5},{5,4},{6,7},{7,6},{8,9},{9,8},{10,11... | collective-permute-start | bytes 786440 | tf_op jit(solution)/shard_map/ppermute | solution.py:23
  54.1 8.8 %collective-permute-start.15 = (bf16[128,8,128]{2,1,0:T(8,128)(2,1)}, bf16[128,8,128]{2,1,0:T(8,128)(2,1)}, u32[]{:S(2)}, u32[]{:S(2)}) collective-permute-start(bf16[128,8,128]{2,1,0:T(8,128)(2,1)} %collective-permute-done.14.refs_6_), channel_id=1, source_target_pairs={{0,1},{1,0},{2,3},{3,2},{4,5},{5,4},{6,7},{7,6},{8,9},{9,8},{10,11... | collective-permute-start | bytes 786440 | tf_op jit(solution)/shard_map/ppermute | solution.py:23
  57.8 5.1 %collective-permute-start.8 = (bf16[32,1024]{1,0:T(8,128)(2,1)}, bf16[32,1024]{1,0:T(8,128)(2,1)S(1)}, u32[]{:S(2)}, u32[]{:S(2)}) collective-permute-start(bf16[32,1024]{1,0:T(8,128)(2,1)} %slice.116), channel_id=1, source_target_pairs={{0,2},{1,3},{2,0},{3,1},{4,6},{5,7},{6,4},{7,5},{8,10},{9,11},{10,... | collective-permute-start | bytes 196616 | tf_op jit(solution)/shard_map/ppermute | solution.py:23
  63.6 0.7 copy-start.12
  64.3 45.3 %slice-start.1 = ((s8[7340032]{0:T(1024)(128)(4,1)}), s8[4194304]{0:T(1024)(128)(4,1)S(1)}, s32[]{:S(2)}) async-start(s8[7340032]{0:T(1024)(128)(4,1)} %bitcast.11), calls=%async_computation.2 | async-start | bytes 8388608
  67.3 44.1 %slice-start.2 = ((s8[7340032]{0:T(1024)(128)(4,1)}), s8[4194304]{0:T(1024)(128)(4,1)S(1)}, s32[]{:S(2)}) async-start(s8[7340032]{0:T(1024)(128)(4,1)} %bitcast.13), calls=%async_computation.3 | async-start | bytes 8388608
  67.3 4.3 %collective-permute-start.17 = (bf16[32,1024]{1,0:T(8,128)(2,1)S(1)}, bf16[32,1024]{1,0:T(8,128)(2,1)S(1)}, u32[]{:S(2)}, u32[]{:S(2)}) collective-permute-start(bf16[32,1024]{1,0:T(8,128)(2,1)S(1)} %shard_map.153.refs_0_), channel_id=1, source_target_pairs={{0,2},{1,3},{2,0},{3,1},{4,6},{5,7},{6,4},{7,5},{8,10},{9,11},{10,... | collective-permute-start | bytes 196616 | tf_op jit(solution)/shard_map/ppermute | solution.py:23
  68.3 3.4 %collective-permute-start.16 = (bf16[32,1024]{1,0:T(8,128)(2,1)S(1)}, bf16[32,1024]{1,0:T(8,128)(2,1)S(1)}, u32[]{:S(2)}, u32[]{:S(2)}) collective-permute-start(bf16[32,1024]{1,0:T(8,128)(2,1)S(1)} %shard_map.153.refs_0_), channel_id=1, source_target_pairs={{0,1},{1,0},{2,3},{3,2},{4,5},{5,4},{6,7},{7,6},{8,9},{9,8},{10,11... | collective-permute-start | bytes 196616 | tf_op jit(solution)/shard_map/ppermute | solution.py:23
  71.7 1.3 collective-permute-start.18
  72.9 2.2 %copy-start.1 = (bf16[1024,2048]{1,0:T(8,128)(2,1)S(1)}, bf16[1024,2048]{1,0:T(8,128)(2,1)}, u32[]{:S(2)}) copy-start(bf16[1024,2048]{1,0:T(8,128)(2,1)} %refs_4_.2) | copy-start | bytes 12582916
  78.6 6.4 %collective-permute-start.19 = (bf16[32,2048]{1,0:T(8,128)(2,1)S(1)}, bf16[32,2048]{1,0:T(8,128)(2,1)S(1)}, u32[]{:S(2)}, u32[]{:S(2)}) collective-permute-start(bf16[32,2048]{1,0:T(8,128)(2,1)S(1)} %get-tuple-element.34), channel_id=1, source_target_pairs={{0,4},{4,0},{8,12},{12,8},{16,20},{20,16},{24,28},{28,24},{1,5},{5... | collective-permute-start | bytes 393224 | tf_op jit(solution)/shard_map/ppermute | solution.py:23
  80.1 7.2 %collective-permute-start.20 = (bf16[32,2048]{1,0:T(8,128)(2,1)S(1)}, bf16[32,2048]{1,0:T(8,128)(2,1)S(1)}, u32[]{:S(2)}, u32[]{:S(2)}) collective-permute-start(bf16[32,2048]{1,0:T(8,128)(2,1)S(1)} %get-tuple-element.36), channel_id=1, source_target_pairs={{0,4},{4,0},{8,12},{12,8},{16,20},{20,16},{24,28},{28,24},{1,5},{5... | collective-permute-start | bytes 393224 | tf_op jit(solution)/shard_map/ppermute | solution.py:23
  85.1 6.7 %collective-permute-start.23 = (bf16[16,2048]{1,0:T(8,128)(2,1)S(1)}, bf16[16,2048]{1,0:T(8,128)(2,1)S(1)}, u32[]{:S(2)}, u32[]{:S(2)}) collective-permute-start(bf16[16,2048]{1,0:T(8,128)(2,1)S(1)} %get-tuple-element.39), channel_id=1, source_target_pairs={{0,8},{4,12},{8,0},{12,4},{16,24},{20,28},{24,16},{28,20},{1,9},{5... | collective-permute-start | bytes 196616 | tf_op jit(solution)/shard_map/ppermute | solution.py:23
  87.4 8.4 %collective-permute-start.21 = (bf16[16,2048]{1,0:T(8,128)(2,1)S(1)}, bf16[16,2048]{1,0:T(8,128)(2,1)S(1)}, u32[]{:S(2)}, u32[]{:S(2)}) collective-permute-start(bf16[16,2048]{1,0:T(8,128)(2,1)S(1)} %get-tuple-element.37), channel_id=1, source_target_pairs={{0,16},{4,20},{8,24},{12,28},{16,0},{20,4},{24,8},{28,12},{1,17},{... | collective-permute-start | bytes 196616 | tf_op jit(solution)/shard_map/ppermute | solution.py:23
  88.9 6.9 %collective-permute-start.22 = (bf16[16,2048]{1,0:T(8,128)(2,1)S(1)}, bf16[16,2048]{1,0:T(8,128)(2,1)S(1)}, u32[]{:S(2)}, u32[]{:S(2)}) collective-permute-start(bf16[16,2048]{1,0:T(8,128)(2,1)S(1)} %get-tuple-element.38), channel_id=1, source_target_pairs={{0,24},{4,28},{8,16},{12,20},{16,8},{20,12},{24,0},{28,4},{1,25},{... | collective-permute-start | bytes 196616 | tf_op jit(solution)/shard_map/ppermute | solution.py:23
  96.5 6.1 %collective-permute-start.29 = (bf16[16,2048]{1,0:T(8,128)(2,1)S(1)}, bf16[16,2048]{1,0:T(8,128)(2,1)S(1)}, u32[]{:S(2)}, u32[]{:S(2)}) collective-permute-start(bf16[16,2048]{1,0:T(8,128)(2,1)S(1)} %get-tuple-element.41.refs_0_), channel_id=1, source_target_pairs={{0,24},{4,28},{8,16},{12,20},{16,8},{20,12},{24,0},{28,4},{1,25},{... | collective-permute-start | bytes 196616 | tf_op jit(solution)/shard_map/ppermute | solution.py:23
  98.6 5.6 %collective-permute-start.27 = (bf16[16,2048]{1,0:T(8,128)(2,1)S(1)}, bf16[16,2048]{1,0:T(8,128)(2,1)S(1)}, u32[]{:S(2)}, u32[]{:S(2)}) collective-permute-start(bf16[16,2048]{1,0:T(8,128)(2,1)S(1)} %get-tuple-element.41.refs_0_), channel_id=1, source_target_pairs={{0,16},{4,20},{8,24},{12,28},{16,0},{20,4},{24,8},{28,12},{1,17},{... | collective-permute-start | bytes 196616 | tf_op jit(solution)/shard_map/ppermute | solution.py:23
  99.3 6.0 %collective-permute-start.25 = (bf16[16,2048]{1,0:T(8,128)(2,1)S(1)}, bf16[16,2048]{1,0:T(8,128)(2,1)S(1)}, u32[]{:S(2)}, u32[]{:S(2)}) collective-permute-start(bf16[16,2048]{1,0:T(8,128)(2,1)S(1)} %get-tuple-element.41.refs_0_), channel_id=1, source_target_pairs={{0,8},{4,12},{8,0},{12,4},{16,24},{20,28},{24,16},{28,20},{1,9},{5... | collective-permute-start | bytes 196616 | tf_op jit(solution)/shard_map/ppermute | solution.py:23
  100.9 5.3 %collective-permute-start.24 = (bf16[16,2048]{1,0:T(8,128)(2,1)S(1)}, bf16[16,2048]{1,0:T(8,128)(2,1)S(1)}, u32[]{:S(2)}, u32[]{:S(2)}) collective-permute-start(bf16[16,2048]{1,0:T(8,128)(2,1)S(1)} %get-tuple-element.41.refs_0_), channel_id=1, source_target_pairs={{0,4},{4,0},{8,12},{12,8},{16,20},{20,16},{24,28},{28,24},{1,5},{5... | collective-permute-start | bytes 196616 | tf_op jit(solution)/shard_map/ppermute | solution.py:23
  102.6 4.3 %collective-permute-start.30 = (bf16[16,2048]{1,0:T(8,128)(2,1)S(1)}, bf16[16,2048]{1,0:T(8,128)(2,1)S(1)}, u32[]{:S(2)}, u32[]{:S(2)}) collective-permute-start(bf16[16,2048]{1,0:T(8,128)(2,1)S(1)} %collective-permute-done.29.refs_6_), channel_id=1, source_target_pairs={{0,4},{4,0},{8,12},{12,8},{16,20},{20,16},{24,28},{28,24},{1,5},{5... | collective-permute-start | bytes 196616 | tf_op jit(solution)/shard_map/ppermute | solution.py:23
  104.2 4.3 %collective-permute-start.28 = (bf16[16,2048]{1,0:T(8,128)(2,1)S(1)}, bf16[16,2048]{1,0:T(8,128)(2,1)S(1)}, u32[]{:S(2)}, u32[]{:S(2)}) collective-permute-start(bf16[16,2048]{1,0:T(8,128)(2,1)S(1)} %collective-permute-done.27.refs_4_), channel_id=1, source_target_pairs={{0,4},{4,0},{8,12},{12,8},{16,20},{20,16},{24,28},{28,24},{1,5},{5... | collective-permute-start | bytes 196616 | tf_op jit(solution)/shard_map/ppermute | solution.py:23
  105.3 4.3 %collective-permute-start.26 = (bf16[16,2048]{1,0:T(8,128)(2,1)S(1)}, bf16[16,2048]{1,0:T(8,128)(2,1)S(1)}, u32[]{:S(2)}, u32[]{:S(2)}) collective-permute-start(bf16[16,2048]{1,0:T(8,128)(2,1)S(1)} %collective-permute-done.25.refs_2_), channel_id=1, source_target_pairs={{0,4},{4,0},{8,12},{12,8},{16,20},{20,16},{24,28},{28,24},{1,5},{5... | collective-permute-start | bytes 196616 | tf_op jit(solution)/shard_map/ppermute | solution.py:23
  109.6 1.9 %slice-start.3 = ((s8[7340032]{0:T(1024)(128)(4,1)}), s8[3145728]{0:T(1024)(128)(4,1)S(1)}, s32[]{:S(2)}) async-start(s8[7340032]{0:T(1024)(128)(4,1)} %bitcast.13), calls=%async_computation.4 | async-start | bytes 6291456
  109.6 17.8 %slice-start.4 = ((s8[7340032]{0:T(1024)(128)(4,1)}), s8[4194304]{0:T(1024)(128)(4,1)S(1)}, s32[]{:S(2)}) async-start(s8[7340032]{0:T(1024)(128)(4,1)} %bitcast.15), calls=%async_computation.5 | async-start | bytes 8388608
  111.4 1.8 %collective-permute-start.31 = (bf16[64,1920]{1,0:T(8,128)(2,1)S(1)}, bf16[64,1920]{1,0:T(8,128)(2,1)S(1)}, u32[]{:S(2)}, u32[]{:S(2)}) collective-permute-start(bf16[64,1920]{1,0:T(8,128)(2,1)S(1)} %get-tuple-element.43), channel_id=1, source_target_pairs={{0,1},{1,0},{2,3},{3,2},{4,5},{5,4},{6,7},{7,6},{8,9},{9,8},{10,11... | collective-permute-start | bytes 737288 | tf_op jit(solution)/shard_map/ppermute | solution.py:23
  111.5 15.9 %slice-start.5 = ((s8[7340032]{0:T(1024)(128)(4,1)}), s8[3145728]{0:T(1024)(128)(4,1)S(1)}, s32[]{:S(2)}) async-start(s8[7340032]{0:T(1024)(128)(4,1)} %bitcast.15), calls=%async_computation.6 | async-start | bytes 6291456
  112.6 1.6 %collective-permute-start.33 = (bf16[64,1792]{1,0:T(8,128)(2,1)S(1)}, bf16[64,1792]{1,0:T(8,128)(2,1)S(1)}, u32[]{:S(2)}, u32[]{:S(2)}) collective-permute-start(bf16[64,1792]{1,0:T(8,128)(2,1)S(1)} %get-tuple-element.46), channel_id=1, source_target_pairs={{0,1},{1,0},{2,3},{3,2},{4,5},{5,4},{6,7},{7,6},{8,9},{9,8},{10,11... | collective-permute-start | bytes 688136 | tf_op jit(solution)/shard_map/ppermute | solution.py:23
  113.2 6.2 %collective-permute-start.32 = (bf16[32,1920]{1,0:T(8,128)(2,1)S(1)}, bf16[32,1920]{1,0:T(8,128)(2,1)S(1)}, u32[]{:S(2)}, u32[]{:S(2)}) collective-permute-start(bf16[32,1920]{1,0:T(8,128)(2,1)S(1)} %slice.113), channel_id=1, source_target_pairs={{0,2},{1,3},{2,0},{3,1},{4,6},{5,7},{6,4},{7,5},{8,10},{9,11},{10,... | collective-permute-start | bytes 368648 | tf_op jit(solution)/shard_map/ppermute | solution.py:23
  114.3 6.7 %collective-permute-start.34 = (bf16[32,1792]{1,0:T(8,128)(2,1)S(1)}, bf16[32,1792]{1,0:T(8,128)(2,1)S(1)}, u32[]{:S(2)}, u32[]{:S(2)}) collective-permute-start(bf16[32,1792]{1,0:T(8,128)(2,1)S(1)} %slice.114), channel_id=1, source_target_pairs={{0,2},{1,3},{2,0},{3,1},{4,6},{5,7},{6,4},{7,5},{8,10},{9,11},{10,... | collective-permute-start | bytes 344072 | tf_op jit(solution)/shard_map/ppermute | solution.py:23
  121.2 4.9 %collective-permute-start.36 = (bf16[32,1792]{1,0:T(8,128)(2,1)S(1)}, bf16[32,1792]{1,0:T(8,128)(2,1)S(1)}, u32[]{:S(2)}, u32[]{:S(2)}) collective-permute-start(bf16[32,1792]{1,0:T(8,128)(2,1)S(1)} %fusion.2.refs_0_), channel_id=1, source_target_pairs={{0,2},{1,3},{2,0},{3,1},{4,6},{5,7},{6,4},{7,5},{8,10},{9,11},{10,... | collective-permute-start | bytes 344072 | tf_op jit(solution)/shard_map/ppermute | solution.py:23
  122.2 3.9 %collective-permute-start.35 = (bf16[32,1792]{1,0:T(8,128)(2,1)S(1)}, bf16[32,1792]{1,0:T(8,128)(2,1)S(1)}, u32[]{:S(2)}, u32[]{:S(2)}) collective-permute-start(bf16[32,1792]{1,0:T(8,128)(2,1)S(1)} %fusion.2.refs_0_), channel_id=1, source_target_pairs={{0,1},{1,0},{2,3},{3,2},{4,5},{5,4},{6,7},{7,6},{8,9},{9,8},{10,11... | collective-permute-start | bytes 344072 | tf_op jit(solution)/shard_map/ppermute | solution.py:23
  126.0 1.3 collective-permute-start.37
  129.1 6.4 %collective-permute-start.38 = (bf16[32,2048]{1,0:T(8,128)(2,1)S(1)}, bf16[32,2048]{1,0:T(8,128)(2,1)S(1)}, u32[]{:S(2)}, u32[]{:S(2)}) collective-permute-start(bf16[32,2048]{1,0:T(8,128)(2,1)S(1)} %get-tuple-element.48), channel_id=1, source_target_pairs={{0,4},{4,0},{8,12},{12,8},{16,20},{20,16},{24,28},{28,24},{1,5},{5... | collective-permute-start | bytes 393224 | tf_op jit(solution)/shard_map/ppermute | solution.py:23
  130.1 7.5 %collective-permute-start.39 = (bf16[32,2048]{1,0:T(8,128)(2,1)S(1)}, bf16[32,2048]{1,0:T(8,128)(2,1)S(1)}, u32[]{:S(2)}, u32[]{:S(2)}) collective-permute-start(bf16[32,2048]{1,0:T(8,128)(2,1)S(1)} %get-tuple-element.50), channel_id=1, source_target_pairs={{0,4},{4,0},{8,12},{12,8},{16,20},{20,16},{24,28},{28,24},{1,5},{5... | collective-permute-start | bytes 393224 | tf_op jit(solution)/shard_map/ppermute | solution.py:23
  135.5 4.6 %collective-permute-start.42 = (bf16[16,2048]{1,0:T(8,128)(2,1)S(1)}, bf16[16,2048]{1,0:T(8,128)(2,1)S(1)}, u32[]{:S(2)}, u32[]{:S(2)}) collective-permute-start(bf16[16,2048]{1,0:T(8,128)(2,1)S(1)} %get-tuple-element.53), channel_id=1, source_target_pairs={{0,8},{4,12},{8,0},{12,4},{16,24},{20,28},{24,16},{28,20},{1,9},{5... | collective-permute-start | bytes 196616 | tf_op jit(solution)/shard_map/ppermute | solution.py:23
  137.5 7.2 %collective-permute-start.40 = (bf16[16,2048]{1,0:T(8,128)(2,1)S(1)}, bf16[16,2048]{1,0:T(8,128)(2,1)S(1)}, u32[]{:S(2)}, u32[]{:S(2)}) collective-permute-start(bf16[16,2048]{1,0:T(8,128)(2,1)S(1)} %get-tuple-element.51), channel_id=1, source_target_pairs={{0,16},{4,20},{8,24},{12,28},{16,0},{20,4},{24,8},{28,12},{1,17},{... | collective-permute-start | bytes 196616 | tf_op jit(solution)/shard_map/ppermute | solution.py:23
  138.2 6.5 %collective-permute-start.41 = (bf16[16,2048]{1,0:T(8,128)(2,1)S(1)}, bf16[16,2048]{1,0:T(8,128)(2,1)S(1)}, u32[]{:S(2)}, u32[]{:S(2)}) collective-permute-start(bf16[16,2048]{1,0:T(8,128)(2,1)S(1)} %get-tuple-element.52), channel_id=1, source_target_pairs={{0,24},{4,28},{8,16},{12,20},{16,8},{20,12},{24,0},{28,4},{1,25},{... | collective-permute-start | bytes 196616 | tf_op jit(solution)/shard_map/ppermute | solution.py:23

commit v5 on v4

--- a/solution.py
+++ b/solution.py
@@ -40,7 +40,7 @@
 HBM = pl.BlockSpec(memory_space=pltpu.HBM)
 
 
-def call(body, outs, ins, specs, scratch=(), limit=16 << 20, flops=0, moved=0):
+def call(body, outs, ins, specs, scratch=(), limit=8 << 20, flops=0, moved=0):
     return pl.pallas_call(
         body,
         out_shape=outs,
@@ -142,15 +142,17 @@
         (x_first, x_second),
         [HBM, HBM],
         [pltpu.VMEM(x_first.shape, BF16), pltpu.VMEM(x_first.shape, BF16), pltpu.SemaphoreType.DMA((2,))],
+        limit=None,
         moved=4 * x_first.size * 2,
     )
 
 
-def pack(cache_keys, cache_values, after):
+def pack(cache_keys, cache_values, afters):
     groups = lax.axis_size("dp")
     part_dev, span, _ = cache_keys.shape
 
-    def body(keys_hbm, values_hbm, after_ref, out_ref, keys_ref, values_ref, sems):
+    def body(keys_hbm, values_hbm, *refs):
+        out_ref, keys_ref, values_ref, sems = refs[len(afters) :]
         copies = [
             pltpu.make_async_copy(keys_hbm, keys_ref, sems.at[0]),
             pltpu.make_async_copy(values_hbm, values_ref, sems.at[1]),
@@ -167,9 +169,10 @@
     return call(
         body,
         shaped((groups, 2, part_dev, span, HD)),
-        (cache_keys, cache_values, after),
-        [HBM, HBM, ANY],
+        (cache_keys, cache_values, *afters),
+        [HBM, HBM] + [ANY] * len(afters),
         [pltpu.VMEM(cache_keys.shape, BF16), pltpu.VMEM(cache_keys.shape, BF16), pltpu.SemaphoreType.DMA((2,))],
+        limit=None,
         moved=8 * cache_keys.size,
     )
 
@@ -200,8 +203,11 @@
     columns = w.shape[1]
 
     def body(where_ref, gain_ref, *refs):
-        block_refs, (w_ref, h_ref, ss_ref, kv_ref, product) = refs[: len(blocks)], refs[len(blocks) :]
+        block_refs, (w_hbm, h_ref, ss_ref, kv_ref, product, w_ref, sem) = refs[: len(blocks)], refs[len(blocks) :]
+        copy = pltpu.make_async_copy(w_hbm, w_ref, sem)
+        copy.start()
         places = lift(where_ref, gain_ref, block_refs, h_ref, ss_ref, True)
+        copy.wait()
         product[...] = jnp.dot(h_ref[...], w_ref[...], preferred_element_type=F32)
         for to, place in places:
             kv_ref[pl.ds(to, pair), :] = product[pl.ds(place, pair), :].astype(BF16)
@@ -210,8 +216,9 @@
         body,
         (shaped((rows, features)), shaped((rows, 128), F32), shaped((rows, columns))),
         (where, gain[None], *blocks, w),
-        [SMEM] + [VMEM] * (2 + len(blocks)),
-        [pltpu.VMEM((rows, columns), F32)],
+        [SMEM] + [VMEM] * (1 + len(blocks)) + [HBM],
+        [pltpu.VMEM((rows, columns), F32), pltpu.VMEM(w.shape, BF16), pltpu.SemaphoreType.DMA],
+        limit=None,
         flops=2 * rows * w.size,
         moved=4 * rows * features + 2 * w.size,
     )
@@ -241,6 +248,7 @@
         (h, w) if after is None else (h, w, after),
         [VMEM] * 2 if after is None else [VMEM, HBM, ANY],
         () if after is None else stream_scratch(w),
+        limit=None if after is not None else 8 << 20,
         flops=4 * half * w.size,
         moved=2 * w.size,
     )
@@ -285,69 +293,68 @@
     near = groups // len(blocks)
     pair = rows // near
     total = len(blocks) * rows
-    half = total // 2
     columns = w.shape[1]
+    close = min(groups, 4)
+    far = (groups - close) // 2
 
     def body(where_ref, *refs):
-        block_refs, (w_ref, keep_ref, far_ref, close_ref, left) = refs[: len(blocks)], refs[len(blocks) :][:5]
+        block_refs, (w_ref, *out_refs) = refs[: len(blocks)], refs[len(blocks) :]
+        left = out_refs[close + 2]
         run = streamed(w_ref, refs[-2], refs[-1]) if stream else None
         d, t = where_ref[0], where_ref[1]
         for k, block_ref in enumerate(block_refs):
             for i in range(near):
-                place = slot(((t ^ k) * near + i) ^ d, groups)
+                relative = ((t ^ k) * near + i) ^ d
+                beyond = close + lax.shift_right_logical(relative - close, 1) + (relative & 1) * far
+                place = jnp.where(relative < close, relative, beyond)
                 left[pl.ds(pl.multiple_of(place * pair, pair), pair), :] = block_ref[i * pair : (i + 1) * pair, :]
 
         def write(first, tile, product):
-            keep_ref[:, first : first + tile] = product[:half]
-            middle = half + half // 2
-            close_ref[:, first : first + tile] = product[half:middle].astype(BF16)
-            far_ref[:, first : first + tile] = product[middle:].astype(BF16)
+            lanes = slice(first, first + tile)
+            for i in range(close):
+                out_refs[i][:, lanes] = product[i * pair : (i + 1) * pair].astype(out_refs[i].dtype)
+            middle = (close + far) * pair
+            out_refs[close][:, lanes] = product[close * pair : middle]
+            out_refs[close + 1][:, lanes] = product[middle:].astype(BF16)
 
         if stream:
             run(left[...], write)
         else:
             multiply(left[...], w_ref, write)
 
-    return call(
-        body,
-        (shaped((half, columns), F32), shaped((half // 2, columns)), shaped((half // 2, columns))),
+    outs = [shaped((pair, columns), F32)] + [shaped((pair, columns))] * (close - 1)
+    outs += [shaped((far * pair, columns), F32), shaped((far * pair, columns))]
+    return call(
+        body,
+        tuple(outs),
         (where, *blocks, w),
         [SMEM] + [VMEM] * len(blocks) + [HBM if stream else VMEM],
         [pltpu.VMEM((total, depth), BF16)] + (stream_scratch(w) if stream else []),
+        limit=None if stream else 8 << 20,
         flops=2 * total * w.size,
         moved=2 * w.size,
     )
 
 
-def add_pairs(keep, arrived, first, pair, own):
-    count = arrived.shape[0] // pair
-    columns = keep.shape[1]
-
+def add_pairs(keep, arrived, pair):
     def body(keep_ref, arrived_ref, *out_refs):
         for i, out_ref in enumerate(out_refs):
-            start = (first + i) * pair
-            summed = keep_ref[start : start + pair, :] + arrived_ref[i * pair : (i + 1) * pair, :].astype(F32)
-            out_ref[...] = summed.astype(out_ref.dtype)
-
-    outs = tuple(shaped((pair, columns), F32 if own and i == 0 else BF16) for i in range(count))
+            rows = slice(i * pair, (i + 1) * pair)
+            out_ref[...] = (keep_ref[rows, :] + arrived_ref[rows, :].astype(F32)).astype(BF16)
+
+    outs = (shaped((pair, keep.shape[1])),) * (keep.shape[0] // pair)
     return call(body, outs, (keep, arrived), [VMEM] * 2, moved=8 * arrived.size)
 
 
-def sum_rows(keep, far, close, pair):
-    groups = lax.axis_size("dp")
-    far = swap(far, "dp", 1)
-    close = swap(close, "dp", 1)
-    quarter = groups // 4
-    sums = add_pairs(keep, far, quarter, pair, False)
-    arrived = [swap(sums[i], "dp", 2 * (quarter + i)) for i in range(quarter)]
-    own = add_pairs(keep, close, 0, pair, True)
-    arrived += [swap(own[i], "dp", 2 * i) for i in range(1, quarter)]
-    return own[0], arrived
+def sum_rows(parts, pair):
+    own, *near, keep, send = parts
+    sums = add_pairs(keep, swap(send, "dp", 1), pair)
+    arrived = [swap(piece, "dp", len(near) + 1 + 2 * i) for i, piece in enumerate(sums)]
+    arrived += [swap(piece, "dp", k + 1) for k, piece in enumerate(near)]
+    return own, arrived
 
 
 def finish(own, arrived, x=None):
-    rows, columns = own.shape
-
     def body(own_ref, *refs):
         total = own_ref[...]
         for ref in refs[: len(arrived)]:
@@ -364,29 +371,26 @@
     return call(body, outs, ins, [VMEM] * len(ins), moved=8 * own.size)
 
 
-def attention_kernel(sizes, where_ref, anc_ref, rope_ref, target_ref, *refs):
+def attention_kernel(sizes, where_ref, anc_ref, rope_ref, target_ref, scale_ref, *refs):
     tensor, groups, part_dev, span, n_q, n_kv = sizes
-    q_refs, kv_refs = refs[:n_q], refs[n_q : n_q + n_kv]
-    cache_refs, (out_ref, keys_ref, values_ref, scale_ref) = refs[n_q + n_kv : n_q + n_kv + tensor], refs[n_q + n_kv + tensor :]
-    t = where_ref[1]
+    q_refs, kv_refs = refs[:n_q], refs[n_q : n_q + 2 * n_kv]
+    first_cache = n_q + 2 * n_kv
+    cache_refs, (out_ref, keys_ref, values_ref) = refs[first_cache : first_cache + tensor], refs[first_cache + tensor :]
+    d, t = where_ref[0], where_ref[1]
     near = groups // tensor
     parts = near * part_dev
     pair = 2 * part_dev
     ctx = tensor * span
     scale = 1.0 / math.sqrt(HD)
-    summed = kv_refs[0][...].astype(F32)
-    squares = summed[:, 2 * HD : 2 * HD + 1] + summed[:, 2 * HD + 1 : 2 * HD + 2]
-    new_kv = summed[:, : 2 * HD]
-    for ref in kv_refs[1:]:
-        more = ref[...].astype(F32)
-        squares = squares + (more[:, 2 * HD : 2 * HD + 1] + more[:, 2 * HD + 1 : 2 * HD + 2])
-        new_kv = new_kv + more[:, : 2 * HD]
-    width = rope_ref[4:5, 0:1]
-    norm = lax.rsqrt(squares / width + EPS)
-    scale_ref[...] = jnp.broadcast_to(norm, (groups * pair, 128))
-    new_kv = (new_kv * norm).astype(BF16)
-    new_values = new_kv[:, HD:]
-    plain = new_kv[:, :HD].astype(F32)
+    new = []
+    for which in range(2):
+        summed = kv_refs[which * n_kv][...].astype(F32)
+        for ref in kv_refs[which * n_kv + 1 : (which + 1) * n_kv]:
+            summed = summed + ref[...].astype(F32)
+        new.append(summed * scale_ref[...])
+    even = d % 2 == 0 if groups == KVH else True
+    plain = jnp.where(even, new[0], new[1]).astype(BF16).astype(F32)
+    new_values = jnp.where(even, new[1], new[0]).astype(BF16)
     cos_key = jnp.concatenate([jnp.broadcast_to(rope_ref[2 * s : 2 * s + 1, :], (part_dev, HD)) for s in range(2)])
     sin_key = jnp.concatenate([jnp.broadcast_to(rope_ref[2 * s + 1 : 2 * s + 2, :], (part_dev, HD)) for s in range(2)])
     turned = pltpu.roll(plain, HD // 2, 1).reshape(groups, pair, HD)
@@ -397,7 +401,7 @@
         queries = queries + ref[...].astype(F32)
     heads = queries.shape[1] // HD
     rows = heads * parts
-    queries = queries * scale_ref[pl.ds(pl.multiple_of(t * near * pair, pair), near * pair), 0:1]
+    queries = queries * scale_ref[pl.ds(pl.multiple_of(t * near * pair, pair), near * pair), :]
     pieces = []
     for step in range(2):
 
@@ -451,61 +455,48 @@
             out_ref[b * pair : (b + 1) * pair, h * HD : (h + 1) * HD] = both.astype(BF16)
 
 
-def attention(where, anc, rope, targets, queries, new_kv, cache, part_dev):
+def attention(where, anc, rope, targets, scale, queries, new_kv, cache, part_dev):
     tensor = lax.axis_size("tensor")
     groups = lax.axis_size("dp")
     span = cache[0].shape[1]
     rows, columns = queries[0].shape
     parts = rows // 2
     heads = columns // HD
-    limit = (16 << 20) + 4 * (3 * heads * parts * parts * tensor * span)
-    ins = (where, anc, rope, targets, *queries, *new_kv, *cache)
-    return call(
-        functools.partial(attention_kernel, (tensor, groups, part_dev, span, len(queries), len(new_kv))),
+    limit = (8 << 20) + 4 * (3 * heads * parts * parts * tensor * span)
+    ins = (where, anc, rope, targets, scale, *queries, *new_kv, *cache)
+    return call(
+        functools.partial(attention_kernel, (tensor, groups, part_dev, span, len(queries), len(new_kv) // 2)),
         shaped((rows, columns)),
         ins,
         [SMEM] * 2 + [VMEM] * (len(ins) - 2),
-        [
-            pltpu.VMEM((parts * tensor * span, HD), F32),
-            pltpu.VMEM((parts * tensor * span, HD), F32),
-            pltpu.VMEM((groups * 2 * part_dev, 128), F32),
-        ],
+        [pltpu.VMEM((parts * tensor * span, HD), F32), pltpu.VMEM((parts * tensor * span, HD), F32)],
         limit=limit,
         flops=1 << 30,
         moved=4 << 20,
     )
 
 
-def split_ss(x):
-    high = x.astype(BF16)
-    low = (x - high.astype(F32)).astype(BF16)
-    return jnp.pad(jnp.stack([high, low], axis=-1), ((0, 0), (0, 126)))
-
-
 def move_keyvals(kv):
     groups = lax.axis_size("dp")
+    tensor = lax.axis_size("tensor")
     d = lax.axis_index("dp")
+    kv = (kv.astype(F32) + swap(kv, "tensor", 1).astype(F32)).astype(BF16)
     if groups == KVH:
-        halves = (kv[:, :HD], kv[:, HD:])
         half = groups // 2
         lower = d < half
-        one = lax.ppermute(
-            jnp.where(lower, halves[0], halves[1]),
-            "dp",
-            [(i, 2 * i) for i in range(half)] + [(half + i, 2 * i + 1) for i in range(half)],
-        )
-        two = lax.ppermute(
-            jnp.where(lower, halves[1], halves[0]),
-            "dp",
-            [(i, 2 * i + 1) for i in range(half)] + [(half + i, 2 * i) for i in range(half)],
-        )
-        even = d % 2 == 0
-        return jnp.concatenate([jnp.where(even, one, two), jnp.where(even, two, one)], axis=1)
+        one = jnp.where(lower, kv[:, :HD], kv[:, HD:])
+        two = jnp.where(lower, kv[:, HD:], kv[:, :HD])
+
+        def move(x, flip, k):
+            to = [2 * i + flip for i in range(half)] + [2 * i + 1 - flip for i in range(half)]
+            pairs = [(i * tensor + t, to[i] * tensor + (t ^ k)) for i in range(groups) for t in range(tensor)]
+            return lax.ppermute(x, ("dp", "tensor"), pairs)
+
+        return [move(x, flip, k) for flip, x in enumerate((one, two)) for k in range(0, tensor, 2)]
     every = lax.all_gather(kv, "dp", axis=1, tiled=True)
     start = (d * KVH // groups) * HD
-    return jnp.concatenate(
-        [lax.dynamic_slice_in_dim(every, first + start, HD, axis=1) for first in (0, KVH * HD)], axis=1
-    )
+    mine = [lax.dynamic_slice_in_dim(every, first + start, HD, axis=1) for first in (0, KVH * HD)]
+    return [x if k == 0 else swap(x, "tensor", k) for x in mine for k in range(0, tensor, 2)]
 
 
 def local(
@@ -538,23 +529,18 @@
 
     x = stack_tokens(x_first, x_second)
     blocks = gather_rows(x)
-    cache = lax.all_to_all(pack(cache_keys, cache_values, x), "dp", split_axis=0, concat_axis=0, tiled=True)
+    cache = pack(cache_keys, cache_values, blocks[2::2])
+    cache = lax.all_to_all(cache, "dp", split_axis=0, concat_axis=0, tiled=True)
     cache = cache.reshape(groups * pair, span, HD)
     caches = gather_blocks(cache)
 
     h, squares, keyvals = project_keyval(where, blocks, attn_gain, w_keyval)
     new_kv = move_keyvals(keyvals)
     queries, queries_arrived = sum_blocks(*project(h, w_query, cache))
-    message = jnp.concatenate([new_kv, split_ss(squares[:, 0])], axis=1)
-    bits = 1
-    while bits < tensor:
-        arrived = swap(message, "tensor", bits)
-        bits *= 2
-        if bits == tensor:
-            break
-        summed = message.astype(F32) + arrived.astype(F32)
-        squares = summed[:, 2 * HD] + summed[:, 2 * HD + 1]
-        message = jnp.concatenate([summed[:, : 2 * HD].astype(BF16), split_ss(squares)], axis=1)
+    squares = squares[:, 0]
+    for bits in [1 << i for i in range(tensor.bit_length() - 1)]:
+        squares = squares + swap(squares, "tensor", bits)
+    scale = lax.rsqrt(squares / width + EPS)[:, None]
 
     own = t * parts + jnp.arange(parts, dtype=jnp.int32)
     anc = lax.dynamic_slice_in_dim(ancestors, t * parts, parts).astype(jnp.int32)
@@ -566,11 +552,11 @@
     targets = jnp.stack([row_of(own, 0), row_of(anc, 0), row_of(own, 1)], axis=1)
     targets = jnp.tile(targets, (heads, 1)).astype(jnp.int32)
     rope = rope_tables(context) + rope_tables(context + 1)
-    rope = jnp.asarray(np.stack(rope + (np.full(HD, width, np.float32),) * 4))
-    mixed = attention(where, anc, rope, targets, [queries] + queries_arrived, [message, arrived], caches, part_dev)
-
-    keep, far, close = project_back(where, gather_blocks(mixed), w_out, True)
-    attn_part, residual = finish(*sum_rows(keep, far, close, pair), x)
+    rope = jnp.asarray(np.stack(rope))
+    mixed = attention(where, anc, rope, targets, scale, [queries] + queries_arrived, new_kv, caches, part_dev)
+
+    parts = project_back(where, gather_blocks(mixed), w_out, True)
+    attn_part, residual = finish(*sum_rows(parts, pair), x)
 
     hidden_cols = w_gate.shape[1]
     h, keep, send = project_gate(where, gather_rows(residual), ffn_gain, w_gate)
@@ -582,8 +568,8 @@
         up = up + piece.astype(F32)
     scale = lax.rsqrt((gate[:, hidden_cols] + gate[:, hidden_cols + 1]) / width + EPS)[:, None]
     hidden = jax.nn.silu(gate[:, :hidden_cols] * scale) * (up * scale)
-    keep, far, close = project_back(where, gather_blocks(hidden.astype(BF16)), w_down, False)
-    (ffn_part,) = finish(*sum_rows(keep, far, close, pair))
+    parts = project_back(where, gather_blocks(hidden.astype(BF16)), w_down, False)
+    (ffn_part,) = finish(*sum_rows(parts, pair))
     return (attn_part.reshape(2, part_dev, features), ffn_part.reshape(2, part_dev, features))
 
 

time: 146 us -> 144 us (0.986)
  Pallas kernels: 17.6 us -> 24.6 us
  other arithmetic: 9.09 us -> 3.76 us
  local copies, waits for them, and re-layouts: 20 us -> 15.3 us
  starting transfers between devices: 52.4 us -> 54.4 us
    pallas_call x15 -> x13, Pallas kernels: 17.6 us -> 24.6 us  [call(): pl.pallas_call(body, out_shape=outs, in_specs=specs, out_specs=jax.tree.m...]
    ppermute x2 -> x4, starting transfers between devices: 4.84 us -> 9.72 us  [move(): return lax.ppermute(x, ('dp', 'tensor'), pairs)]
    ppermute x41 -> x44, starting transfers between devices: 42.7 us -> 40.1 us  [swap(): return lax.ppermute(x, axis, [(i, i ^ bits) for i in range(size)])]
    another operation x2, other arithmetic: 2.52 us -> 0.75 us  [local(): jnp.stack([row_of(own, 0), row_of(anc, 0), row_of(own, 1)], axis=1)]
    add x2 -> x1, other arithmetic: 1.7 us -> 0.01 us  [local(): squares = squares + swap(squares, 'tensor', bits)]
    slice x3, local copies, waits for them, and re-layouts: 1.57 us -> 0.04 us  [sum_blocks(): paired[i].astype(BF16)]
    another operation x2 -> x0, local copies, waits for them, and re-layouts: 1.52 us -> none  [split_ss(): return jnp.pad(jnp.stack([high, low], axis=-1), ((0, 0), (0, 126)))]
    unnamed x38 -> x64, local copies, waits for them, and re-layouts: 12.9 us -> 14.1 us
  transfers between devices with their start and end apart: 44 -> 49, of which waited for: 21 -> 24; matrix products, arithmetic and copies ran while one was open for 11% -> 3% of each run, Pallas kernels for 4% -> 8%
where the time goes in v5:
time: 144 us; the launch traced here: 143 us
  starting transfers between devices  54.4 us (38%)
  waiting for transfers between devices  44 us (31%)
  Pallas kernels  24.6 us (17%)
  local copies, waits for them, and re-layouts  15.3 us (11%)
  other arithmetic  3.76 us (3%)
    ppermute x44, waiting for transfers between devices, swap(): return lax.ppermute(x, axis, [(i, i ^ bits) for i in range(size)])  42.3 us
    ppermute x44, starting transfers between devices, swap(): return lax.ppermute(x, axis, [(i, i ^ bits) for i in range(size)])  40.1 us
    pallas_call x13, Pallas kernels, call(): pl.pallas_call(body, out_shape=outs, in_specs=specs, out_specs=jax.tree.m...  24.6 us
    unnamed x64, local copies, waits for them, and re-layouts  14.1 us
    ppermute x4, starting transfers between devices, move(): return lax.ppermute(x, ('dp', 'tensor'), pairs)  9.72 us
    all_to_all x1, starting transfers between devices, local(): cache = lax.all_to_all(cache, 'dp', split_axis=0, concat_axis=0, tiled=True)  4.51 us
  transfers between devices with their start and end apart: 49, of which 24 were waited for; matrix products, arithmetic and copies ran while one was open for 3% of the time, Pallas kernels for 8%

profile of v5, /device:TPU:0, one launch (start us, length us, event | category | flops | bytes accessed | tf_op | source)
XLA Modules:
  0.0 143.2 jit_solution(4885707710216684286)
XLA Ops:
  0.6 1.4 shard_map.149.refs_0_.refs_5_
  2.1 3.1 %collective-permute-start.1 = (bf16[16,2048]{1,0:T(8,128)(2,1)}, bf16[16,2048]{1,0:T(8,128)(2,1)S(1)}, u32[]{:S(2)}, u32[]{:S(2)}) collective-permute-start(bf16[16,2048]{1,0:T(8,128)(2,1)} %shard_map.149.refs_0_.refs_5_), channel_id=1, source_target_pairs={{0,8},{4,12},{8,0},{12,4},{16,24},{20,28},{24,16},{28,20},{1,9},{5... | collective-permute-start | bytes 196616 | tf_op jit(solution)/shard_map/ppermute | solution.py:23
  5.2 2.6 %collective-permute-start.3 = (bf16[16,2048]{1,0:T(8,128)(2,1)}, bf16[16,2048]{1,0:T(8,128)(2,1)S(1)}, u32[]{:S(2)}, u32[]{:S(2)}) collective-permute-start(bf16[16,2048]{1,0:T(8,128)(2,1)} %shard_map.149.refs_0_.refs_5_), channel_id=1, source_target_pairs={{0,16},{4,20},{8,24},{12,28},{16,0},{20,4},{24,8},{28,12},{1,17},{... | collective-permute-start | bytes 196616 | tf_op jit(solution)/shard_map/ppermute | solution.py:23
  7.8 1.7 %collective-permute-start = (bf16[16,2048]{1,0:T(8,128)(2,1)}, bf16[16,2048]{1,0:T(8,128)(2,1)S(1)}, u32[]{:S(2)}, u32[]{:S(2)}) collective-permute-start(bf16[16,2048]{1,0:T(8,128)(2,1)} %shard_map.149.refs_0_.refs_5_), channel_id=1, source_target_pairs={{0,4},{4,0},{8,12},{12,8},{16,20},{20,16},{24,28},{28,24},{1,5},{5... | collective-permute-start | bytes 196616 | tf_op jit(solution)/shard_map/ppermute | solution.py:23
  10.4 2.3 %collective-permute-done.3.refs_4_.refs_1_ = bf16[16,2048]{1,0:T(8,128)(2,1)S(1)} collective-permute-done((bf16[16,2048]{1,0:T(8,128)(2,1)}, bf16[16,2048]{1,0:T(8,128)(2,1)S(1)}, u32[]{:S(2)}, u32[]{:S(2)}) %collective-permute-start.3) | collective-permute-done | bytes 65568 | tf_op jit(solution)/shard_map/ppermute | solution.py:23
  12.7 1.5 %collective-permute-start.4 = (bf16[16,2048]{1,0:T(8,128)(2,1)S(1)}, bf16[16,2048]{1,0:T(8,128)(2,1)S(1)}, u32[]{:S(2)}, u32[]{:S(2)}) collective-permute-start(bf16[16,2048]{1,0:T(8,128)(2,1)S(1)} %collective-permute-done.3.refs_4_.refs_1_), channel_id=1, source_target_pairs={{0,4},{4,0},{8,12},{12,8},{16,20},{20,16},{24,28},{28,24},{1,5},{5... | collective-permute-start | bytes 196616 | tf_op jit(solution)/shard_map/ppermute | solution.py:23
  14.2 1.4 collective-permute-start.6
  15.6 0.7 fusion.8
  16.3 1.8 %shard_map.151 = bf16[8,2,8,8,128]{4,3,2,1,0:T(8,128)(2,1)} custom-call(bf16[8,8,1024]{2,1,0:T(8,128)(2,1)} %keys_hbm.1, bf16[8,8,1024]{2,1,0:T(8,128)(2,1)} %values_hbm.1, bf16[16,2048]{1,0:T(8,128)(2,1)} %copy-done.20, bf16[16,2048]{1,0:T(8,128)(2,1)} %copy-done.21, bf16[16,2048]{1,0:T(8,128)(2,1)} %copy-done.22), custom_call_target="tpu_custom_call" | custom-call | bytes 524288 | tf_op jit(solution)/shard_map/pallas_call | solution.py:44
  18.1 4.5 %all-to-all-start = ((bf16[8,2,8,8,128]{4,3,2,1,0:T(8,128)(2,1)}), bf16[8,2,8,8,128]{4,3,2,1,0:T(8,128)(2,1)S(1)}, u32[]{:S(2)}, u32[]{:S(2)}) async-start(bf16[8,2,8,8,128]{4,3,2,1,0:T(8,128)(2,1)} %shard_map.151), calls=%async_computation | async-start | bytes 524288 | tf_op jit(solution)/shard_map/all_to_all | solution.py:533
  23.3 3.4 %shard_map.150 = (bf16[128,2048]{1,0:T(8,128)(2,1)}, f32[128,128]{1,0:T(8,128)}, bf16[128,256]{1,0:T(8,128)(2,1)}) custom-call(s32[2]{0:T(128)} %pad_add_fusion.1.where_ref, f32[1,2048]{1,0:T(1,128)} %bitcast.21, bf16[16,2048]{1,0:T(8,128)(2,1)} %shard_map.149.refs_0_.refs_5_, bf16[16,2048]{1,0:T(8,128)(2,1)} %copy-done.26, bf16[16,2048]{1,0:T(8,128)(2,1)} %copy-done.20, ...), custom_call_target="tpu_custom_call" | custom-call | flops 134217728 | bytes 2097152 | tf_op jit(solution)/shard_map/pallas_call | solution.py:44
  26.7 0.9 slice_reduce_fusion
  28.8 1.5 %collective-permute-start.8 = (f32[128]{0:T(128)S(1)}, f32[128]{0:T(128)S(1)}, u32[]{:S(2)}, u32[]{:S(2)}) collective-permute-start(f32[128]{0:T(128)S(1)} %add.143), channel_id=1, source_target_pairs={{0,2},{1,3},{2,0},{3,1},{4,6},{5,7},{6,4},{7,5},{8,10},{9,11},{10,... | collective-permute-start | bytes 1544 | tf_op jit(solution)/shard_map/ppermute | solution.py:23
  30.3 0.9 add_convert_fusion
  31.2 1.1 collective-permute-start.17
  32.3 4.8 %shard_map.152 = (f32[64,1024]{1,0:T(8,128)}, bf16[64,1024]{1,0:T(8,128)(2,1)}) custom-call(bf16[128,2048]{1,0:T(8,128)(2,1)} %get-tuple-element.31.h_ref, bf16[2048,1024]{1,0:T(8,128)(2,1)} %w_ref.2, bf16[128,8,128]{2,1,0:T(8,128)(2,1)} %bitcast.15), custom_call_target="tpu_custom_call" | custom-call | flops 536870912 | bytes 4194304 | tf_op jit(solution)/shard_map/pallas_call | solution.py:44
  37.9 1.0 collective-permute-start.13
  39.4 1.1 convert_add_fusion.2
  40.5 5.6 %collective-permute-start.14 = (bf16[128,128]{1,0:T(8,128)(2,1)S(1)}, bf16[128,128]{1,0:T(8,128)(2,1)S(1)}, u32[]{:S(2)}, u32[]{:S(2)}) collective-permute-start(bf16[128,128]{1,0:T(8,128)(2,1)S(1)} %get-tuple-element.60), channel_id=1, source_target_pairs={{0,4},{1,5},{2,6},{3,7},{4,12},{5,13},{6,14},{7,15},{8,20},{9,21},... | collective-permute-start | bytes 98312 | tf_op jit(solution)/shard_map/ppermute | solution.py:493
  46.1 2.4 %collective-permute-start.15 = (bf16[128,128]{1,0:T(8,128)(2,1)S(1)}, bf16[128,128]{1,0:T(8,128)(2,1)S(1)}, u32[]{:S(2)}, u32[]{:S(2)}) collective-permute-start(bf16[128,128]{1,0:T(8,128)(2,1)S(1)} %get-tuple-element.60), channel_id=1, source_target_pairs={{0,6},{1,7},{2,4},{3,5},{4,14},{5,15},{6,12},{7,13},{8,22},{9,23},... | collective-permute-start | bytes 98312 | tf_op jit(solution)/shard_map/ppermute | solution.py:493
  48.6 1.4 collective-permute-start.10
  50.1 1.7 %collective-permute-done.15.refs_5_ = bf16[128,128]{1,0:T(8,128)(2,1)S(1)} collective-permute-done((bf16[128,128]{1,0:T(8,128)(2,1)S(1)}, bf16[128,128]{1,0:T(8,128)(2,1)S(1)}, u32[]{:S(2)}, u32[]{:S(2)}) %collective-permute-start.15) | collective-permute-done | bytes 32800 | tf_op jit(solution)/shard_map/ppermute | solution.py:493
  54.3 0.9 copy-done.3
  55.2 0.9 copy-done.12
  56.2 0.9 copy-done.14
  57.1 0.9 copy-done.16
  58.1 0.8 copy-done.18
  58.8 2.1 %shard_map.153.refs_0_ = bf16[32,1024]{1,0:T(8,128)(2,1)S(1)} custom-call(s32[2]{0:T(128)S(1)} %copy-done.9, s32[16]{0:T(128)S(1)} %get-tuple-element.59.anc_ref, f32[4,128]{1,0:T(4,128)S(1)} %copy-done.19, s32[128,3]{1,0:T(8,128)S(1)} %bitcast.18, f32[128,1]{1,0:T(8,128)S(1)} %copy.19.scale_ref, f32[32,1024]{1,0:T(8,128)S(1)} %slice.59.refs_0_, ...), custom_call_target="tpu_custom_call" | custom-call | flops 1073741824 | bytes 4194304 | tf_op jit(solution)/shard_map/pallas_call | solution.py:44
  61.0 1.4 %collective-permute-start.20 = (bf16[32,1024]{1,0:T(8,128)(2,1)S(1)}, bf16[32,1024]{1,0:T(8,128)(2,1)S(1)}, u32[]{:S(2)}, u32[]{:S(2)}) collective-permute-start(bf16[32,1024]{1,0:T(8,128)(2,1)S(1)} %shard_map.153.refs_0_), channel_id=1, source_target_pairs={{0,2},{1,3},{2,0},{3,1},{4,6},{5,7},{6,4},{7,5},{8,10},{9,11},{10,... | collective-permute-start | bytes 196616 | tf_op jit(solution)/shard_map/ppermute | solution.py:23
  62.4 2.9 %collective-permute-done.20.refs_2_ = bf16[32,1024]{1,0:T(8,128)(2,1)S(1)} collective-permute-done((bf16[32,1024]{1,0:T(8,128)(2,1)S(1)}, bf16[32,1024]{1,0:T(8,128)(2,1)S(1)}, u32[]{:S(2)}, u32[]{:S(2)}) %collective-permute-start.20) | collective-permute-done | bytes 65568 | tf_op jit(solution)/shard_map/ppermute | solution.py:23
  65.3 1.2 collective-permute-done.21.refs_3_
  67.2 5.2 %shard_map.154 = (f32[16,2048]{1,0:T(8,128)}, bf16[16,2048]{1,0:T(8,128)(2,1)}, bf16[16,2048]{1,0:T(8,128)(2,1)}, bf16[16,2048]{1,0:T(8,128)(2,1)}, f32[32,2048]{1,0:T(8,128)}, /*index=5*/bf16[32,2048]{1,0:T(8,128)(2,1)}) custom-call(s32[2]{0:T(128)} %pad_add_fusion.1.where_ref, bf16[32,1024]{1,0:T(8,128)(2,1)} %copy-done.7, bf16[32,1024]{1,0:T(8,128)(2,1)} %copy-done.24, ...), custom_call_target="tpu_custom_call" | custom-call | flops 536870912 | bytes 4194304 | tf_op jit(solution)/shard_map/pallas_call | solution.py:44
  72.5 1.3 collective-permute-start.22
  73.7 0.8 collective-permute-start.25
  74.5 2.0 %collective-permute-start.26 = (bf16[16,2048]{1,0:T(8,128)(2,1)}, bf16[16,2048]{1,0:T(8,128)(2,1)S(1)}, u32[]{:S(2)}, u32[]{:S(2)}) collective-permute-start(bf16[16,2048]{1,0:T(8,128)(2,1)} %get-tuple-element.41), channel_id=1, source_target_pairs={{0,8},{4,12},{8,0},{12,4},{16,24},{20,28},{24,16},{28,20},{1,9},{5... | collective-permute-start | bytes 196616 | tf_op jit(solution)/shard_map/ppermute | solution.py:23
  77.2 1.8 %collective-permute-done.22.arrived_ref = bf16[32,2048]{1,0:T(8,128)(2,1)S(1)} collective-permute-done((bf16[32,2048]{1,0:T(8,128)(2,1)}, bf16[32,2048]{1,0:T(8,128)(2,1)S(1)}, u32[]{:S(2)}, u32[]{:S(2)}) %collective-permute-start.22) | collective-permute-done | bytes 131104 | tf_op jit(solution)/shard_map/ppermute | solution.py:23
  79.0 0.9 copy-done.5
  80.0 1.5 %collective-permute-start.23 = (bf16[16,2048]{1,0:T(8,128)(2,1)S(1)}, bf16[16,2048]{1,0:T(8,128)(2,1)S(1)}, u32[]{:S(2)}, u32[]{:S(2)}) collective-permute-start(bf16[16,2048]{1,0:T(8,128)(2,1)S(1)} %get-tuple-element.38), channel_id=1, source_target_pairs={{0,16},{4,20},{8,24},{12,28},{16,0},{20,4},{24,8},{28,12},{1,17},{... | collective-permute-start | bytes 196616 | tf_op jit(solution)/shard_map/ppermute | solution.py:23
  81.5 4.3 %collective-permute-start.24 = (bf16[16,2048]{1,0:T(8,128)(2,1)S(1)}, bf16[16,2048]{1,0:T(8,128)(2,1)S(1)}, u32[]{:S(2)}, u32[]{:S(2)}) collective-permute-start(bf16[16,2048]{1,0:T(8,128)(2,1)S(1)} %get-tuple-element.39), channel_id=1, source_target_pairs={{0,24},{4,28},{8,16},{12,20},{16,8},{20,12},{24,0},{28,4},{1,25},{... | collective-permute-start | bytes 196616 | tf_op jit(solution)/shard_map/ppermute | solution.py:23
  85.9 3.0 %collective-permute-done.24.refs_1_ = bf16[16,2048]{1,0:T(8,128)(2,1)S(1)} collective-permute-done((bf16[16,2048]{1,0:T(8,128)(2,1)S(1)}, bf16[16,2048]{1,0:T(8,128)(2,1)S(1)}, u32[]{:S(2)}, u32[]{:S(2)}) %collective-permute-start.24) | collective-permute-done | bytes 65568 | tf_op jit(solution)/shard_map/ppermute | solution.py:23
  88.8 0.9 copy-done.6
  90.4 0.9 collective-permute-start.29
  91.4 3.0 %collective-permute-start.31 = (bf16[16,2048]{1,0:T(8,128)(2,1)S(1)}, bf16[16,2048]{1,0:T(8,128)(2,1)S(1)}, u32[]{:S(2)}, u32[]{:S(2)}) collective-permute-start(bf16[16,2048]{1,0:T(8,128)(2,1)S(1)} %get-tuple-element.44.refs_0_), channel_id=1, source_target_pairs={{0,16},{4,20},{8,24},{12,28},{16,0},{20,4},{24,8},{28,12},{1,17},{... | collective-permute-start | bytes 196616 | tf_op jit(solution)/shard_map/ppermute | solution.py:23
  94.8 1.6 %collective-permute-start.28 = (bf16[16,2048]{1,0:T(8,128)(2,1)S(1)}, bf16[16,2048]{1,0:T(8,128)(2,1)S(1)}, u32[]{:S(2)}, u32[]{:S(2)}) collective-permute-start(bf16[16,2048]{1,0:T(8,128)(2,1)S(1)} %get-tuple-element.44.refs_0_), channel_id=1, source_target_pairs={{0,4},{4,0},{8,12},{12,8},{16,20},{20,16},{24,28},{28,24},{1,5},{5... | collective-permute-start | bytes 196616 | tf_op jit(solution)/shard_map/ppermute | solution.py:23
  97.3 1.1 collective-permute-start.32
  98.4 2.0 %collective-permute-done.33.refs_6_ = bf16[16,2048]{1,0:T(8,128)(2,1)S(1)} collective-permute-done((bf16[16,2048]{1,0:T(8,128)(2,1)S(1)}, bf16[16,2048]{1,0:T(8,128)(2,1)S(1)}, u32[]{:S(2)}, u32[]{:S(2)}) %collective-permute-start.33) | collective-permute-done | bytes 65568 | tf_op jit(solution)/shard_map/ppermute | solution.py:23
  100.7 0.9 collective-permute-done.32.refs_5_
  101.6 3.1 %collective-permute-done.34.refs_7_ = bf16[16,2048]{1,0:T(8,128)(2,1)S(1)} collective-permute-done((bf16[16,2048]{1,0:T(8,128)(2,1)S(1)}, bf16[16,2048]{1,0:T(8,128)(2,1)S(1)}, u32[]{:S(2)}, u32[]{:S(2)}) %collective-permute-start.34) | collective-permute-done | bytes 65568 | tf_op jit(solution)/shard_map/ppermute | solution.py:23
  104.7 3.1 %copy-done = bf16[2048,1792]{1,0:T(8,128)(2,1)S(1)} copy-done((bf16[2048,1792]{1,0:T(8,128)(2,1)S(1)}, bf16[2048,1792]{1,0:T(8,128)(2,1)}, u32[]{:S(2)}) %copy-start) | copy-done | bytes 7340056
  107.8 1.8 %shard_map.157 = (bf16[128,2048]{1,0:T(8,128)(2,1)S(1)}, f32[64,1920]{1,0:T(8,128)S(1)}, bf16[64,1920]{1,0:T(8,128)(2,1)S(1)}) custom-call(s32[2]{0:T(128)S(1)} %copy-done.10, f32[1,2048]{1,0:T(1,128)S(1)} %bitcast.19, bf16[16,2048]{1,0:T(8,128)(2,1)S(1)} %get-tuple-element.44.refs_0_, bf16[16,2048]{1,0:T(8,128)(2,1)S(1)} %collective-permute-done.28.refs_1_, ...), custom_call_target="tpu_custom_call" | custom-call | flops 939524096 | bytes 8388608 | tf_op jit(solution)/shard_map/pallas_call | solution.py:44
  109.6 1.2 copy-done.1
  110.9 1.1 shard_map.158
  112.2 1.3 collective-permute-done.37
  113.6 0.8 collective-permute-start.38
  114.4 3.9 %collective-permute-done.36 = bf16[32,1920]{1,0:T(8,128)(2,1)S(1)} collective-permute-done((bf16[32,1920]{1,0:T(8,128)(2,1)S(1)}, bf16[32,1920]{1,0:T(8,128)(2,1)S(1)}, u32[]{:S(2)}, u32[]{:S(2)}) %collective-permute-start.36) | collective-permute-done | bytes 122912 | tf_op jit(solution)/shard_map/ppermute | solution.py:23
  118.5 1.8 %collective-permute-done.38 = bf16[32,1792]{1,0:T(8,128)(2,1)S(1)} collective-permute-done((bf16[32,1792]{1,0:T(8,128)(2,1)S(1)}, bf16[32,1792]{1,0:T(8,128)(2,1)S(1)}, u32[]{:S(2)}, u32[]{:S(2)}) %collective-permute-start.38) | collective-permute-done | bytes 114720 | tf_op jit(solution)/shard_map/ppermute | solution.py:23
  120.9 4.5 %collective-permute-done.40.refs_2_ = bf16[32,1792]{1,0:T(8,128)(2,1)S(1)} collective-permute-done((bf16[32,1792]{1,0:T(8,128)(2,1)S(1)}, bf16[32,1792]{1,0:T(8,128)(2,1)S(1)}, u32[]{:S(2)}, u32[]{:S(2)}) %collective-permute-start.40) | collective-permute-done | bytes 114720 | tf_op jit(solution)/shard_map/ppermute | solution.py:23
  125.4 1.3 collective-permute-done.41.refs_3_
  126.7 1.7 %shard_map.159 = (f32[16,2048]{1,0:T(8,128)S(1)}, bf16[16,2048]{1,0:T(8,128)(2,1)S(1)}, bf16[16,2048]{1,0:T(8,128)(2,1)S(1)}, bf16[16,2048]{1,0:T(8,128)(2,1)S(1...) custom-call(s32[2]{0:T(128)S(1)} %copy-done.10, bf16[32,1792]{1,0:T(8,128)(2,1)S(1)} %fusion.2.refs_0_, ...), custom_call_target="tpu_custom_call" | custom-call | flops 939524096 | bytes 7340032 | tf_op jit(solution)/shard_map/pallas_call | solution.py:44
  128.5 2.0 %collective-permute-start.45 = (bf16[16,2048]{1,0:T(8,128)(2,1)S(1)}, bf16[16,2048]{1,0:T(8,128)(2,1)S(1)}, u32[]{:S(2)}, u32[]{:S(2)}) collective-permute-start(bf16[16,2048]{1,0:T(8,128)(2,1)S(1)} %get-tuple-element.55), channel_id=1, source_target_pairs={{0,4},{4,0},{8,12},{12,8},{16,20},{20,16},{24,28},{28,24},{1,5},{5... | collective-permute-start | bytes 196616 | tf_op jit(solution)/shard_map/ppermute | solution.py:23
  130.5 1.5 %collective-permute-start.47 = (bf16[16,2048]{1,0:T(8,128)(2,1)S(1)}, bf16[16,2048]{1,0:T(8,128)(2,1)S(1)}, u32[]{:S(2)}, u32[]{:S(2)}) collective-permute-start(bf16[16,2048]{1,0:T(8,128)(2,1)S(1)} %get-tuple-element.57), channel_id=1, source_target_pairs={{0,12},{4,8},{8,4},{12,0},{16,28},{20,24},{24,20},{28,16},{1,13},{... | collective-permute-start | bytes 196616 | tf_op jit(solution)/shard_map/ppermute | solution.py:23
  132.0 4.1 %collective-permute-done.42.arrived_ref = bf16[32,2048]{1,0:T(8,128)(2,1)S(1)} collective-permute-done((bf16[32,2048]{1,0:T(8,128)(2,1)S(1)}, bf16[32,2048]{1,0:T(8,128)(2,1)S(1)}, u32[]{:S(2)}, u32[]{:S(2)}) %collective-permute-start.42) | collective-permute-done | bytes 131104 | tf_op jit(solution)/shard_map/ppermute | solution.py:23
  136.8 4.6 %collective-permute-done.43.refs_0_ = bf16[16,2048]{1,0:T(8,128)(2,1)S(1)} collective-permute-done((bf16[16,2048]{1,0:T(8,128)(2,1)S(1)}, bf16[16,2048]{1,0:T(8,128)(2,1)S(1)}, u32[]{:S(2)}, u32[]{:S(2)}) %collective-permute-start.43) | collective-permute-done | bytes 65568 | tf_op jit(solution)/shard_map/ppermute | solution.py:23
  141.4 1.1 collective-permute-done.44.refs_1_
  (134 shorter events, 12.9 us)
Async XLA Ops:
  0.6 53.6 %copy-start.19 = (f32[4,128]{1,0:T(4,128)S(1)}, f32[4,128]{1,0:T(4,128)}, u32[]{:S(2)}) copy-start(f32[4,128]{1,0:T(4,128)} %constant.76.clone.rope_ref) | copy-start | bytes 6148
  2.1 8.0 %collective-permute-start.1 = (bf16[16,2048]{1,0:T(8,128)(2,1)}, bf16[16,2048]{1,0:T(8,128)(2,1)S(1)}, u32[]{:S(2)}, u32[]{:S(2)}) collective-permute-start(bf16[16,2048]{1,0:T(8,128)(2,1)} %shard_map.149.refs_0_.refs_5_), channel_id=1, source_target_pairs={{0,8},{4,12},{8,0},{12,4},{16,24},{20,28},{24,16},{28,20},{1,9},{5... | collective-permute-start | bytes 196616 | tf_op jit(solution)/shard_map/ppermute | solution.py:23
  5.2 7.5 %collective-permute-start.3 = (bf16[16,2048]{1,0:T(8,128)(2,1)}, bf16[16,2048]{1,0:T(8,128)(2,1)S(1)}, u32[]{:S(2)}, u32[]{:S(2)}) collective-permute-start(bf16[16,2048]{1,0:T(8,128)(2,1)} %shard_map.149.refs_0_.refs_5_), channel_id=1, source_target_pairs={{0,16},{4,20},{8,24},{12,28},{16,0},{20,4},{24,8},{28,12},{1,17},{... | collective-permute-start | bytes 196616 | tf_op jit(solution)/shard_map/ppermute | solution.py:23
  7.8 6.4 %collective-permute-start.5 = (bf16[16,2048]{1,0:T(8,128)(2,1)}, bf16[16,2048]{1,0:T(8,128)(2,1)S(1)}, u32[]{:S(2)}, u32[]{:S(2)}) collective-permute-start(bf16[16,2048]{1,0:T(8,128)(2,1)} %shard_map.149.refs_0_.refs_5_), channel_id=1, source_target_pairs={{0,24},{4,28},{8,16},{12,20},{16,8},{20,12},{24,0},{28,4},{1,25},{... | collective-permute-start | bytes 196616 | tf_op jit(solution)/shard_map/ppermute | solution.py:23
  7.8 14.8 %collective-permute-start = (bf16[16,2048]{1,0:T(8,128)(2,1)}, bf16[16,2048]{1,0:T(8,128)(2,1)S(1)}, u32[]{:S(2)}, u32[]{:S(2)}) collective-permute-start(bf16[16,2048]{1,0:T(8,128)(2,1)} %shard_map.149.refs_0_.refs_5_), channel_id=1, source_target_pairs={{0,4},{4,0},{8,12},{12,8},{16,20},{20,16},{24,28},{28,24},{1,5},{5... | collective-permute-start | bytes 196616 | tf_op jit(solution)/shard_map/ppermute | solution.py:23
  10.1 44.2 %copy-start.9 = (s32[2]{0:T(128)S(1)}, s32[2]{0:T(128)}, u32[]{:S(2)}) copy-start(s32[2]{0:T(128)} %pad_add_fusion.1.where_ref) | copy-start | bytes 28
  10.1 6.2 %copy-start.20 = (bf16[16,2048]{1,0:T(8,128)(2,1)}, bf16[16,2048]{1,0:T(8,128)(2,1)S(1)}, u32[]{:S(2)}) copy-start(bf16[16,2048]{1,0:T(8,128)(2,1)S(1)} %collective-permute-done.1.refs_2_.refs_0_) | copy-start | bytes 196612
  10.1 12.5 %collective-permute-start.2 = (bf16[16,2048]{1,0:T(8,128)(2,1)S(1)}, bf16[16,2048]{1,0:T(8,128)(2,1)S(1)}, u32[]{:S(2)}, u32[]{:S(2)}) collective-permute-start(bf16[16,2048]{1,0:T(8,128)(2,1)S(1)} %collective-permute-done.1.refs_2_.refs_0_), channel_id=1, source_target_pairs={{0,4},{4,0},{8,12},{12,8},{16,20},{20,16},{24,28},{28,24},{1,5},{5... | collective-permute-start | bytes 196616 | tf_op jit(solution)/shard_map/ppermute | solution.py:23
  12.7 3.6 %copy-start.21 = (bf16[16,2048]{1,0:T(8,128)(2,1)}, bf16[16,2048]{1,0:T(8,128)(2,1)S(1)}, u32[]{:S(2)}) copy-start(bf16[16,2048]{1,0:T(8,128)(2,1)S(1)} %collective-permute-done.3.refs_4_.refs_1_) | copy-start | bytes 196612
  12.7 10.0 %collective-permute-start.4 = (bf16[16,2048]{1,0:T(8,128)(2,1)S(1)}, bf16[16,2048]{1,0:T(8,128)(2,1)S(1)}, u32[]{:S(2)}, u32[]{:S(2)}) collective-permute-start(bf16[16,2048]{1,0:T(8,128)(2,1)S(1)} %collective-permute-done.3.refs_4_.refs_1_), channel_id=1, source_target_pairs={{0,4},{4,0},{8,12},{12,8},{16,20},{20,16},{24,28},{28,24},{1,5},{5... | collective-permute-start | bytes 196616 | tf_op jit(solution)/shard_map/ppermute | solution.py:23
  14.2 2.2 %copy-start.22 = (bf16[16,2048]{1,0:T(8,128)(2,1)}, bf16[16,2048]{1,0:T(8,128)(2,1)S(1)}, u32[]{:S(2)}) copy-start(bf16[16,2048]{1,0:T(8,128)(2,1)S(1)} %collective-permute-done.5.refs_6_.refs_2_) | copy-start | bytes 196612
  14.2 8.5 %collective-permute-start.6 = (bf16[16,2048]{1,0:T(8,128)(2,1)S(1)}, bf16[16,2048]{1,0:T(8,128)(2,1)S(1)}, u32[]{:S(2)}, u32[]{:S(2)}) collective-permute-start(bf16[16,2048]{1,0:T(8,128)(2,1)S(1)} %collective-permute-done.5.refs_6_.refs_2_), channel_id=1, source_target_pairs={{0,4},{4,0},{8,12},{12,8},{16,20},{20,16},{24,28},{28,24},{1,5},{5... | collective-permute-start | bytes 196616 | tf_op jit(solution)/shard_map/ppermute | solution.py:23
  18.1 13.1 %all-to-all-start = ((bf16[8,2,8,8,128]{4,3,2,1,0:T(8,128)(2,1)}), bf16[8,2,8,8,128]{4,3,2,1,0:T(8,128)(2,1)S(1)}, u32[]{:S(2)}, u32[]{:S(2)}) async-start(bf16[8,2,8,8,128]{4,3,2,1,0:T(8,128)(2,1)} %shard_map.151), calls=%async_computation | async-start | bytes 524288 | tf_op jit(solution)/shard_map/all_to_all | solution.py:533
  27.6 1.2 collective-permute-start.7
  27.7 2.6 %collective-permute-start.11 = (bf16[128,256]{1,0:T(8,128)(2,1)}, bf16[128,256]{1,0:T(8,128)(2,1)S(1)}, u32[]{:S(2)}, u32[]{:S(2)}) collective-permute-start(bf16[128,256]{1,0:T(8,128)(2,1)} %get-tuple-element.34), channel_id=1, source_target_pairs={{0,1},{1,0},{2,3},{3,2},{4,5},{5,4},{6,7},{7,6},{8,9},{9,8},{10,11... | collective-permute-start | bytes 196616 | tf_op jit(solution)/shard_map/ppermute | solution.py:23
  28.8 11.7 %collective-permute-start.8 = (f32[128]{0:T(128)S(1)}, f32[128]{0:T(128)S(1)}, u32[]{:S(2)}, u32[]{:S(2)}) collective-permute-start(f32[128]{0:T(128)S(1)} %add.143), channel_id=1, source_target_pairs={{0,2},{1,3},{2,0},{3,1},{4,6},{5,7},{6,4},{7,5},{8,10},{9,11},{10,... | collective-permute-start | bytes 1544 | tf_op jit(solution)/shard_map/ppermute | solution.py:23
  31.2 8.2 %collective-permute-start.17 = (bf16[128,8,128]{2,1,0:T(8,128)(2,1)S(1)}, bf16[128,8,128]{2,1,0:T(8,128)(2,1)S(1)}, u32[]{:S(2)}, u32[]{:S(2)}) collective-permute-start(bf16[128,8,128]{2,1,0:T(8,128)(2,1)S(1)} %bitcast.14), channel_id=1, source_target_pairs={{0,2},{1,3},{2,0},{3,1},{4,6},{5,7},{6,4},{7,5},{8,10},{9,11},{10,... | collective-permute-start | bytes 786440 | tf_op jit(solution)/shard_map/ppermute | solution.py:23
  32.3 56.5 %copy-start.4 = (bf16[16,2048]{1,0:T(8,128)(2,1)S(1)}, bf16[16,2048]{1,0:T(8,128)(2,1)}, u32[]{:S(2)}) copy-start(bf16[16,2048]{1,0:T(8,128)(2,1)} %shard_map.149.refs_0_.refs_5_) | copy-start | bytes 196612
  32.3 72.3 %copy-start.8 = (f32[2048]{0:T(1024)S(1)}, f32[2048]{0:T(1024)}, u32[]{:S(2)}) copy-start(f32[2048]{0:T(1024)} %param.20) | copy-start | bytes 24580
  32.3 72.3 %copy-start.10 = (s32[2]{0:T(128)S(1)}, s32[2]{0:T(128)}, u32[]{:S(2)}) copy-start(s32[2]{0:T(128)} %pad_add_fusion.1.where_ref) | copy-start | bytes 28
  37.1 1.8 %collective-permute-start.9 = (bf16[64,1024]{1,0:T(8,128)(2,1)}, bf16[64,1024]{1,0:T(8,128)(2,1)S(1)}, u32[]{:S(2)}, u32[]{:S(2)}) collective-permute-start(bf16[64,1024]{1,0:T(8,128)(2,1)} %get-tuple-element.33), channel_id=1, source_target_pairs={{0,1},{1,0},{2,3},{3,2},{4,5},{5,4},{6,7},{7,6},{8,9},{9,8},{10,11... | collective-permute-start | bytes 393224 | tf_op jit(solution)/shard_map/ppermute | solution.py:23
  37.2 8.9 %collective-permute-start.12 = (bf16[128,128]{1,0:T(8,128)(2,1)S(1)}, bf16[128,128]{1,0:T(8,128)(2,1)S(1)}, u32[]{:S(2)}, u32[]{:S(2)}) collective-permute-start(bf16[128,128]{1,0:T(8,128)(2,1)S(1)} %get-tuple-element.61), channel_id=1, source_target_pairs={{0,0},{1,1},{2,2},{3,3},{4,8},{5,9},{6,10},{7,11},{8,16},{9,17},{1... | collective-permute-start | bytes 98312 | tf_op jit(solution)/shard_map/ppermute | solution.py:493
  37.9 10.7 %collective-permute-start.13 = (bf16[128,128]{1,0:T(8,128)(2,1)S(1)}, bf16[128,128]{1,0:T(8,128)(2,1)S(1)}, u32[]{:S(2)}, u32[]{:S(2)}) collective-permute-start(bf16[128,128]{1,0:T(8,128)(2,1)S(1)} %get-tuple-element.61), channel_id=1, source_target_pairs={{0,2},{1,3},{2,0},{3,1},{4,10},{5,11},{6,8},{7,9},{8,18},{9,19},{1... | collective-permute-start | bytes 98312 | tf_op jit(solution)/shard_map/ppermute | solution.py:493
  38.9 13.9 %collective-permute-start.16 = (bf16[128,8,128]{2,1,0:T(8,128)(2,1)}, bf16[128,8,128]{2,1,0:T(8,128)(2,1)S(1)}, u32[]{:S(2)}, u32[]{:S(2)}) collective-permute-start(bf16[128,8,128]{2,1,0:T(8,128)(2,1)} %bitcast.16), channel_id=1, source_target_pairs={{0,1},{1,0},{2,3},{3,2},{4,5},{5,4},{6,7},{7,6},{8,9},{9,8},{10,11... | collective-permute-start | bytes 786440 | tf_op jit(solution)/shard_map/ppermute | solution.py:23
  39.4 14.8 %copy-start.11 = (bf16[128,8,128]{2,1,0:T(8,128)(2,1)}, bf16[128,8,128]{2,1,0:T(8,128)(2,1)S(1)}, u32[]{:S(2)}) copy-start(bf16[128,8,128]{2,1,0:T(8,128)(2,1)S(1)} %collective-permute-done.17.refs_8_) | copy-start | bytes 786436
  39.4 14.1 %collective-permute-start.18 = (bf16[128,8,128]{2,1,0:T(8,128)(2,1)S(1)}, bf16[128,8,128]{2,1,0:T(8,128)(2,1)S(1)}, u32[]{:S(2)}, u32[]{:S(2)}) collective-permute-start(bf16[128,8,128]{2,1,0:T(8,128)(2,1)S(1)} %collective-permute-done.17.refs_8_), channel_id=1, source_target_pairs={{0,1},{1,0},{2,3},{3,2},{4,5},{5,4},{6,7},{7,6},{8,9},{9,8},{10,11... | collective-permute-start | bytes 786440 | tf_op jit(solution)/shard_map/ppermute | solution.py:23
  40.5 9.6 %collective-permute-start.14 = (bf16[128,128]{1,0:T(8,128)(2,1)S(1)}, bf16[128,128]{1,0:T(8,128)(2,1)S(1)}, u32[]{:S(2)}, u32[]{:S(2)}) collective-permute-start(bf16[128,128]{1,0:T(8,128)(2,1)S(1)} %get-tuple-element.60), channel_id=1, source_target_pairs={{0,4},{1,5},{2,6},{3,7},{4,12},{5,13},{6,14},{7,15},{8,20},{9,21},... | collective-permute-start | bytes 98312 | tf_op jit(solution)/shard_map/ppermute | solution.py:493
  46.1 5.7 %collective-permute-start.15 = (bf16[128,128]{1,0:T(8,128)(2,1)S(1)}, bf16[128,128]{1,0:T(8,128)(2,1)S(1)}, u32[]{:S(2)}, u32[]{:S(2)}) collective-permute-start(bf16[128,128]{1,0:T(8,128)(2,1)S(1)} %get-tuple-element.60), channel_id=1, source_target_pairs={{0,6},{1,7},{2,4},{3,5},{4,14},{5,15},{6,12},{7,13},{8,22},{9,23},... | collective-permute-start | bytes 98312 | tf_op jit(solution)/shard_map/ppermute | solution.py:493
  48.6 4.3 %collective-permute-start.10 = (bf16[32,1024]{1,0:T(8,128)(2,1)S(1)}, bf16[32,1024]{1,0:T(8,128)(2,1)S(1)}, u32[]{:S(2)}, u32[]{:S(2)}) collective-permute-start(bf16[32,1024]{1,0:T(8,128)(2,1)S(1)} %slice.101), channel_id=1, source_target_pairs={{0,2},{1,3},{2,0},{3,1},{4,6},{5,7},{6,4},{7,5},{8,10},{9,11},{10,... | collective-permute-start | bytes 196616 | tf_op jit(solution)/shard_map/ppermute | solution.py:23
  58.8 67.9 %slice-start = ((s8[7340032]{0:T(1024)(128)(4,1)}), s8[3145728]{0:T(1024)(128)(4,1)S(1)}, s32[]{:S(2)}) async-start(s8[7340032]{0:T(1024)(128)(4,1)} %bitcast.12), calls=%async_computation.1 | async-start | bytes 6291456
  61.0 5.6 %copy-start.7 = (bf16[32,1024]{1,0:T(8,128)(2,1)}, bf16[32,1024]{1,0:T(8,128)(2,1)S(1)}, u32[]{:S(2)}) copy-start(bf16[32,1024]{1,0:T(8,128)(2,1)S(1)} %shard_map.153.refs_0_) | copy-start | bytes 196612
  61.0 4.3 %collective-permute-start.20 = (bf16[32,1024]{1,0:T(8,128)(2,1)S(1)}, bf16[32,1024]{1,0:T(8,128)(2,1)S(1)}, u32[]{:S(2)}, u32[]{:S(2)}) collective-permute-start(bf16[32,1024]{1,0:T(8,128)(2,1)S(1)} %shard_map.153.refs_0_), channel_id=1, source_target_pairs={{0,2},{1,3},{2,0},{3,1},{4,6},{5,7},{6,4},{7,5},{8,10},{9,11},{10,... | collective-permute-start | bytes 196616 | tf_op jit(solution)/shard_map/ppermute | solution.py:23
  62.4 2.9 %collective-permute-start.19 = (bf16[32,1024]{1,0:T(8,128)(2,1)S(1)}, bf16[32,1024]{1,0:T(8,128)(2,1)S(1)}, u32[]{:S(2)}, u32[]{:S(2)}) collective-permute-start(bf16[32,1024]{1,0:T(8,128)(2,1)S(1)} %shard_map.153.refs_0_), channel_id=1, source_target_pairs={{0,1},{1,0},{2,3},{3,2},{4,5},{5,4},{6,7},{7,6},{8,9},{9,8},{10,11... | collective-permute-start | bytes 196616 | tf_op jit(solution)/shard_map/ppermute | solution.py:23
  65.3 1.3 copy-start.23
  65.3 1.3 collective-permute-start.21
  72.5 6.5 %collective-permute-start.22 = (bf16[32,2048]{1,0:T(8,128)(2,1)}, bf16[32,2048]{1,0:T(8,128)(2,1)S(1)}, u32[]{:S(2)}, u32[]{:S(2)}) collective-permute-start(bf16[32,2048]{1,0:T(8,128)(2,1)} %get-tuple-element.37), channel_id=1, source_target_pairs={{0,4},{4,0},{8,12},{12,8},{16,20},{20,16},{24,28},{28,24},{1,5},{5... | collective-permute-start | bytes 393224 | tf_op jit(solution)/shard_map/ppermute | solution.py:23
  73.7 12.1 %collective-permute-start.25 = (bf16[16,2048]{1,0:T(8,128)(2,1)}, bf16[16,2048]{1,0:T(8,128)(2,1)S(1)}, u32[]{:S(2)}, u32[]{:S(2)}) collective-permute-start(bf16[16,2048]{1,0:T(8,128)(2,1)} %get-tuple-element.40), channel_id=1, source_target_pairs={{0,4},{4,0},{8,12},{12,8},{16,20},{20,16},{24,28},{28,24},{1,5},{5... | collective-permute-start | bytes 196616 | tf_op jit(solution)/shard_map/ppermute | solution.py:23
  74.5 11.2 %collective-permute-start.26 = (bf16[16,2048]{1,0:T(8,128)(2,1)}, bf16[16,2048]{1,0:T(8,128)(2,1)S(1)}, u32[]{:S(2)}, u32[]{:S(2)}) collective-permute-start(bf16[16,2048]{1,0:T(8,128)(2,1)} %get-tuple-element.41), channel_id=1, source_target_pairs={{0,8},{4,12},{8,0},{12,4},{16,24},{20,28},{24,16},{28,20},{1,9},{5... | collective-permute-start | bytes 196616 | tf_op jit(solution)/shard_map/ppermute | solution.py:23
  76.5 9.3 %collective-permute-start.27 = (bf16[16,2048]{1,0:T(8,128)(2,1)}, bf16[16,2048]{1,0:T(8,128)(2,1)S(1)}, u32[]{:S(2)}, u32[]{:S(2)}) collective-permute-start(bf16[16,2048]{1,0:T(8,128)(2,1)} %get-tuple-element.42), channel_id=1, source_target_pairs={{0,12},{4,8},{8,4},{12,0},{16,28},{20,24},{24,20},{28,16},{1,13},{... | collective-permute-start | bytes 196616 | tf_op jit(solution)/shard_map/ppermute | solution.py:23
  80.0 5.9 %collective-permute-start.23 = (bf16[16,2048]{1,0:T(8,128)(2,1)S(1)}, bf16[16,2048]{1,0:T(8,128)(2,1)S(1)}, u32[]{:S(2)}, u32[]{:S(2)}) collective-permute-start(bf16[16,2048]{1,0:T(8,128)(2,1)S(1)} %get-tuple-element.38), channel_id=1, source_target_pairs={{0,16},{4,20},{8,24},{12,28},{16,0},{20,4},{24,8},{28,12},{1,17},{... | collective-permute-start | bytes 196616 | tf_op jit(solution)/shard_map/ppermute | solution.py:23
  81.5 7.3 %collective-permute-start.24 = (bf16[16,2048]{1,0:T(8,128)(2,1)S(1)}, bf16[16,2048]{1,0:T(8,128)(2,1)S(1)}, u32[]{:S(2)}, u32[]{:S(2)}) collective-permute-start(bf16[16,2048]{1,0:T(8,128)(2,1)S(1)} %get-tuple-element.39), channel_id=1, source_target_pairs={{0,24},{4,28},{8,16},{12,20},{16,8},{20,12},{24,0},{28,4},{1,25},{... | collective-permute-start | bytes 196616 | tf_op jit(solution)/shard_map/ppermute | solution.py:23
  90.4 6.0 %collective-permute-start.29 = (bf16[16,2048]{1,0:T(8,128)(2,1)S(1)}, bf16[16,2048]{1,0:T(8,128)(2,1)S(1)}, u32[]{:S(2)}, u32[]{:S(2)}) collective-permute-start(bf16[16,2048]{1,0:T(8,128)(2,1)S(1)} %get-tuple-element.44.refs_0_), channel_id=1, source_target_pairs={{0,8},{4,12},{8,0},{12,4},{16,24},{20,28},{24,16},{28,20},{1,9},{5... | collective-permute-start | bytes 196616 | tf_op jit(solution)/shard_map/ppermute | solution.py:23
  91.4 5.9 %collective-permute-start.31 = (bf16[16,2048]{1,0:T(8,128)(2,1)S(1)}, bf16[16,2048]{1,0:T(8,128)(2,1)S(1)}, u32[]{:S(2)}, u32[]{:S(2)}) collective-permute-start(bf16[16,2048]{1,0:T(8,128)(2,1)S(1)} %get-tuple-element.44.refs_0_), channel_id=1, source_target_pairs={{0,16},{4,20},{8,24},{12,28},{16,0},{20,4},{24,8},{28,12},{1,17},{... | collective-permute-start | bytes 196616 | tf_op jit(solution)/shard_map/ppermute | solution.py:23
  94.3 6.1 %collective-permute-start.33 = (bf16[16,2048]{1,0:T(8,128)(2,1)S(1)}, bf16[16,2048]{1,0:T(8,128)(2,1)S(1)}, u32[]{:S(2)}, u32[]{:S(2)}) collective-permute-start(bf16[16,2048]{1,0:T(8,128)(2,1)S(1)} %get-tuple-element.44.refs_0_), channel_id=1, source_target_pairs={{0,24},{4,28},{8,16},{12,20},{16,8},{20,12},{24,0},{28,4},{1,25},{... | collective-permute-start | bytes 196616 | tf_op jit(solution)/shard_map/ppermute | solution.py:23
  94.8 5.6 %collective-permute-start.28 = (bf16[16,2048]{1,0:T(8,128)(2,1)S(1)}, bf16[16,2048]{1,0:T(8,128)(2,1)S(1)}, u32[]{:S(2)}, u32[]{:S(2)}) collective-permute-start(bf16[16,2048]{1,0:T(8,128)(2,1)S(1)} %get-tuple-element.44.refs_0_), channel_id=1, source_target_pairs={{0,4},{4,0},{8,12},{12,8},{16,20},{20,16},{24,28},{28,24},{1,5},{5... | collective-permute-start | bytes 196616 | tf_op jit(solution)/shard_map/ppermute | solution.py:23
  96.4 4.3 %collective-permute-start.30 = (bf16[16,2048]{1,0:T(8,128)(2,1)S(1)}, bf16[16,2048]{1,0:T(8,128)(2,1)S(1)}, u32[]{:S(2)}, u32[]{:S(2)}) collective-permute-start(bf16[16,2048]{1,0:T(8,128)(2,1)S(1)} %collective-permute-done.29.refs_2_), channel_id=1, source_target_pairs={{0,4},{4,0},{8,12},{12,8},{16,20},{20,16},{24,28},{28,24},{1,5},{5... | collective-permute-start | bytes 196616 | tf_op jit(solution)/shard_map/ppermute | solution.py:23
  97.3 4.3 %collective-permute-start.32 = (bf16[16,2048]{1,0:T(8,128)(2,1)S(1)}, bf16[16,2048]{1,0:T(8,128)(2,1)S(1)}, u32[]{:S(2)}, u32[]{:S(2)}) collective-permute-start(bf16[16,2048]{1,0:T(8,128)(2,1)S(1)} %collective-permute-done.31.refs_4_), channel_id=1, source_target_pairs={{0,4},{4,0},{8,12},{12,8},{16,20},{20,16},{24,28},{28,24},{1,5},{5... | collective-permute-start | bytes 196616 | tf_op jit(solution)/shard_map/ppermute | solution.py:23
  100.4 4.3 %collective-permute-start.34 = (bf16[16,2048]{1,0:T(8,128)(2,1)S(1)}, bf16[16,2048]{1,0:T(8,128)(2,1)S(1)}, u32[]{:S(2)}, u32[]{:S(2)}) collective-permute-start(bf16[16,2048]{1,0:T(8,128)(2,1)S(1)} %collective-permute-done.33.refs_6_), channel_id=1, source_target_pairs={{0,4},{4,0},{8,12},{12,8},{16,20},{20,16},{24,28},{28,24},{1,5},{5... | collective-permute-start | bytes 196616 | tf_op jit(solution)/shard_map/ppermute | solution.py:23
  104.7 3.1 %copy-start = (bf16[2048,1792]{1,0:T(8,128)(2,1)S(1)}, bf16[2048,1792]{1,0:T(8,128)(2,1)}, u32[]{:S(2)}) copy-start(bf16[2048,1792]{1,0:T(8,128)(2,1)} %refs_8_.3) | copy-start | bytes 22020100
  107.8 3.1 %copy-start.1 = (bf16[2048,1792]{1,0:T(8,128)(2,1)S(1)}, bf16[2048,1792]{1,0:T(8,128)(2,1)}, u32[]{:S(2)}) copy-start(bf16[2048,1792]{1,0:T(8,128)(2,1)} %w_ref.3) | copy-start | bytes 22020100
  107.8 18.9 %slice-start.1 = ((s8[7340032]{0:T(1024)(128)(4,1)}), s8[4194304]{0:T(1024)(128)(4,1)S(1)}, s32[]{:S(2)}) async-start(s8[7340032]{0:T(1024)(128)(4,1)} %bitcast.12), calls=%async_computation.2 | async-start | bytes 8388608
  109.5 2.5 %collective-permute-start.35 = (bf16[64,1920]{1,0:T(8,128)(2,1)S(1)}, bf16[64,1920]{1,0:T(8,128)(2,1)S(1)}, u32[]{:S(2)}, u32[]{:S(2)}) collective-permute-start(bf16[64,1920]{1,0:T(8,128)(2,1)S(1)} %get-tuple-element.46), channel_id=1, source_target_pairs={{0,1},{1,0},{2,3},{3,2},{4,5},{5,4},{6,7},{7,6},{8,9},{9,8},{10,11... | collective-permute-start | bytes 737288 | tf_op jit(solution)/shard_map/ppermute | solution.py:23
  112.0 1.6 %collective-permute-start.37 = (bf16[64,1792]{1,0:T(8,128)(2,1)S(1)}, bf16[64,1792]{1,0:T(8,128)(2,1)S(1)}, u32[]{:S(2)}, u32[]{:S(2)}) collective-permute-start(bf16[64,1792]{1,0:T(8,128)(2,1)S(1)} %get-tuple-element.49), channel_id=1, source_target_pairs={{0,1},{1,0},{2,3},{3,2},{4,5},{5,4},{6,7},{7,6},{8,9},{9,8},{10,11... | collective-permute-start | bytes 688136 | tf_op jit(solution)/shard_map/ppermute | solution.py:23
  112.1 6.2 %collective-permute-start.36 = (bf16[32,1920]{1,0:T(8,128)(2,1)S(1)}, bf16[32,1920]{1,0:T(8,128)(2,1)S(1)}, u32[]{:S(2)}, u32[]{:S(2)}) collective-permute-start(bf16[32,1920]{1,0:T(8,128)(2,1)S(1)} %slice.99), channel_id=1, source_target_pairs={{0,2},{1,3},{2,0},{3,1},{4,6},{5,7},{6,4},{7,5},{8,10},{9,11},{10,... | collective-permute-start | bytes 368648 | tf_op jit(solution)/shard_map/ppermute | solution.py:23
  113.6 6.8 %collective-permute-start.38 = (bf16[32,1792]{1,0:T(8,128)(2,1)S(1)}, bf16[32,1792]{1,0:T(8,128)(2,1)S(1)}, u32[]{:S(2)}, u32[]{:S(2)}) collective-permute-start(bf16[32,1792]{1,0:T(8,128)(2,1)S(1)} %slice.100), channel_id=1, source_target_pairs={{0,2},{1,3},{2,0},{3,1},{4,6},{5,7},{6,4},{7,5},{8,10},{9,11},{10,... | collective-permute-start | bytes 344072 | tf_op jit(solution)/shard_map/ppermute | solution.py:23
  120.5 4.9 %collective-permute-start.40 = (bf16[32,1792]{1,0:T(8,128)(2,1)S(1)}, bf16[32,1792]{1,0:T(8,128)(2,1)S(1)}, u32[]{:S(2)}, u32[]{:S(2)}) collective-permute-start(bf16[32,1792]{1,0:T(8,128)(2,1)S(1)} %fusion.2.refs_0_), channel_id=1, source_target_pairs={{0,2},{1,3},{2,0},{3,1},{4,6},{5,7},{6,4},{7,5},{8,10},{9,11},{10,... | collective-permute-start | bytes 344072 | tf_op jit(solution)/shard_map/ppermute | solution.py:23
  120.9 4.5 %collective-permute-start.39 = (bf16[32,1792]{1,0:T(8,128)(2,1)S(1)}, bf16[32,1792]{1,0:T(8,128)(2,1)S(1)}, u32[]{:S(2)}, u32[]{:S(2)}) collective-permute-start(bf16[32,1792]{1,0:T(8,128)(2,1)S(1)} %fusion.2.refs_0_), channel_id=1, source_target_pairs={{0,1},{1,0},{2,3},{3,2},{4,5},{5,4},{6,7},{7,6},{8,9},{9,8},{10,11... | collective-permute-start | bytes 344072 | tf_op jit(solution)/shard_map/ppermute | solution.py:23
  125.4 1.3 collective-permute-start.41
  128.4 7.7 %collective-permute-start.42 = (bf16[32,2048]{1,0:T(8,128)(2,1)S(1)}, bf16[32,2048]{1,0:T(8,128)(2,1)S(1)}, u32[]{:S(2)}, u32[]{:S(2)}) collective-permute-start(bf16[32,2048]{1,0:T(8,128)(2,1)S(1)} %get-tuple-element.52), channel_id=1, source_target_pairs={{0,4},{4,0},{8,12},{12,8},{16,20},{20,16},{24,28},{28,24},{1,5},{5... | collective-permute-start | bytes 393224 | tf_op jit(solution)/shard_map/ppermute | solution.py:23
  128.5 8.3 %collective-permute-start.45 = (bf16[16,2048]{1,0:T(8,128)(2,1)S(1)}, bf16[16,2048]{1,0:T(8,128)(2,1)S(1)}, u32[]{:S(2)}, u32[]{:S(2)}) collective-permute-start(bf16[16,2048]{1,0:T(8,128)(2,1)S(1)} %get-tuple-element.55), channel_id=1, source_target_pairs={{0,4},{4,0},{8,12},{12,8},{16,20},{20,16},{24,28},{28,24},{1,5},{5... | collective-permute-start | bytes 196616 | tf_op jit(solution)/shard_map/ppermute | solution.py:23
  130.5 6.3 %collective-permute-start.46 = (bf16[16,2048]{1,0:T(8,128)(2,1)S(1)}, bf16[16,2048]{1,0:T(8,128)(2,1)S(1)}, u32[]{:S(2)}, u32[]{:S(2)}) collective-permute-start(bf16[16,2048]{1,0:T(8,128)(2,1)S(1)} %get-tuple-element.56), channel_id=1, source_target_pairs={{0,8},{4,12},{8,0},{12,4},{16,24},{20,28},{24,16},{28,20},{1,9},{5... | collective-permute-start | bytes 196616 | tf_op jit(solution)/shard_map/ppermute | solution.py:23
  130.5 6.3 %collective-permute-start.47 = (bf16[16,2048]{1,0:T(8,128)(2,1)S(1)}, bf16[16,2048]{1,0:T(8,128)(2,1)S(1)}, u32[]{:S(2)}, u32[]{:S(2)}) collective-permute-start(bf16[16,2048]{1,0:T(8,128)(2,1)S(1)} %get-tuple-element.57), channel_id=1, source_target_pairs={{0,12},{4,8},{8,4},{12,0},{16,28},{20,24},{24,20},{28,16},{1,13},{... | collective-permute-start | bytes 196616 | tf_op jit(solution)/shard_map/ppermute | solution.py:23
  136.2 5.2 %collective-permute-start.43 = (bf16[16,2048]{1,0:T(8,128)(2,1)S(1)}, bf16[16,2048]{1,0:T(8,128)(2,1)S(1)}, u32[]{:S(2)}, u32[]{:S(2)}) collective-permute-start(bf16[16,2048]{1,0:T(8,128)(2,1)S(1)} %get-tuple-element.53), channel_id=1, source_target_pairs={{0,16},{4,20},{8,24},{12,28},{16,0},{20,4},{24,8},{28,12},{1,17},{... | collective-permute-start | bytes 196616 | tf_op jit(solution)/shard_map/ppermute | solution.py:23
  136.2 6.2 %collective-permute-start.44 = (bf16[16,2048]{1,0:T(8,128)(2,1)S(1)}, bf16[16,2048]{1,0:T(8,128)(2,1)S(1)}, u32[]{:S(2)}, u32[]{:S(2)}) collective-permute-start(bf16[16,2048]{1,0:T(8,128)(2,1)S(1)} %get-tuple-element.54), channel_id=1, source_target_pairs={{0,24},{4,28},{8,16},{12,20},{16,8},{20,12},{24,0},{28,4},{1,25},{... | collective-permute-start | bytes 196616 | tf_op jit(solution)/shard_map/ppermute | solution.py:23
  (17 other events, 14.0 us)

commit v6 on v5

--- a/solution.py
+++ b/solution.py
@@ -14,6 +14,7 @@
 EPS = 1e-05
 ROPE_BASE = 500000.0
 MASKED = -1e30
+AROUND = 5 << 30
 BF16 = jnp.bfloat16
 F32 = jnp.float32
 
@@ -40,7 +41,7 @@
 HBM = pl.BlockSpec(memory_space=pltpu.HBM)
 
 
-def call(body, outs, ins, specs, scratch=(), limit=8 << 20, flops=0, moved=0):
+def call(body, outs, ins, specs, scratch=(), flops=0, moved=0, limit=8 << 20):
     return pl.pallas_call(
         body,
         out_shape=outs,
@@ -48,7 +49,7 @@
         out_specs=jax.tree.map(lambda _: VMEM, outs),
         scratch_shapes=scratch,
         compiler_params=pltpu.CompilerParams(vmem_limit_bytes=limit),
-        cost_estimate=pl.CostEstimate(flops=flops, bytes_accessed=moved, transcendentals=0),
+        cost_estimate=pl.CostEstimate(flops=flops + AROUND, bytes_accessed=moved, transcendentals=0),
     )(*ins)
 
 
@@ -103,28 +104,6 @@
         write(first, tile, jnp.dot(left, w_ref[:, first : first + tile], preferred_element_type=F32))
 
 
-def streamed(w_hbm, w_ref, sems):
-    columns = w_ref.shape[1]
-    tile = tiles(columns)
-    copies = [
-        pltpu.make_async_copy(w_hbm.at[:, pl.ds(first, tile)], w_ref.at[:, pl.ds(first, tile)], sems.at[i])
-        for i, first in enumerate(range(0, columns, tile))
-    ]
-    for copy in copies:
-        copy.start()
-
-    def run(left, write):
-        for i, first in enumerate(range(0, columns, tile)):
-            copies[i].wait()
-            write(first, tile, jnp.dot(left, w_ref[:, first : first + tile], preferred_element_type=F32))
-
-    return run
-
-
-def stream_scratch(w):
-    return [pltpu.VMEM(w.shape, BF16), pltpu.SemaphoreType.DMA((w.shape[1] // tiles(w.shape[1]),))]
-
-
 def stack_tokens(x_first, x_second):
     part_dev, features = x_first.shape
 
@@ -142,7 +121,6 @@
         (x_first, x_second),
         [HBM, HBM],
         [pltpu.VMEM(x_first.shape, BF16), pltpu.VMEM(x_first.shape, BF16), pltpu.SemaphoreType.DMA((2,))],
-        limit=None,
         moved=4 * x_first.size * 2,
     )
 
@@ -172,7 +150,6 @@
         (cache_keys, cache_values, *afters),
         [HBM, HBM] + [ANY] * len(afters),
         [pltpu.VMEM(cache_keys.shape, BF16), pltpu.VMEM(cache_keys.shape, BF16), pltpu.SemaphoreType.DMA((2,))],
-        limit=None,
         moved=8 * cache_keys.size,
     )
 
@@ -203,11 +180,8 @@
     columns = w.shape[1]
 
     def body(where_ref, gain_ref, *refs):
-        block_refs, (w_hbm, h_ref, ss_ref, kv_ref, product, w_ref, sem) = refs[: len(blocks)], refs[len(blocks) :]
-        copy = pltpu.make_async_copy(w_hbm, w_ref, sem)
-        copy.start()
+        block_refs, (w_ref, h_ref, ss_ref, kv_ref, product) = refs[: len(blocks)], refs[len(blocks) :]
         places = lift(where_ref, gain_ref, block_refs, h_ref, ss_ref, True)
-        copy.wait()
         product[...] = jnp.dot(h_ref[...], w_ref[...], preferred_element_type=F32)
         for to, place in places:
             kv_ref[pl.ds(to, pair), :] = product[pl.ds(place, pair), :].astype(BF16)
@@ -216,9 +190,8 @@
         body,
         (shaped((rows, features)), shaped((rows, 128), F32), shaped((rows, columns))),
         (where, gain[None], *blocks, w),
-        [SMEM] + [VMEM] * (1 + len(blocks)) + [HBM],
-        [pltpu.VMEM((rows, columns), F32), pltpu.VMEM(w.shape, BF16), pltpu.SemaphoreType.DMA],
-        limit=None,
+        [SMEM] + [VMEM] * (2 + len(blocks)),
+        [pltpu.VMEM((rows, columns), F32)],
         flops=2 * rows * w.size,
         moved=4 * rows * features + 2 * w.size,
     )
@@ -228,27 +201,20 @@
     half = h.shape[0] // 2
 
     def body(h_ref, w_ref, *refs):
-        run = None if after is None else streamed(w_ref, refs[-2], refs[-1])
-        keep_ref, send_ref = refs[:2] if after is None else refs[1:3]
-        left = h_ref[...]
+        keep_ref, send_ref = refs[-2:]
 
         def write(first, tile, product):
             keep_ref[:, first : first + tile] = product[:half]
             send_ref[:, first : first + tile] = product[half:].astype(BF16)
 
-        if run is None:
-            multiply(left, w_ref, write)
-        else:
-            run(left, write)
+        multiply(h_ref[...], w_ref, write)
 
     columns = w.shape[1]
     return call(
         body,
         (shaped((half, columns), F32), shaped((half, columns))),
         (h, w) if after is None else (h, w, after),
-        [VMEM] * 2 if after is None else [VMEM, HBM, ANY],
-        () if after is None else stream_scratch(w),
-        limit=None if after is not None else 8 << 20,
+        [VMEM] * 2 + [ANY] * (after is not None),
         flops=4 * half * w.size,
         moved=2 * w.size,
     )
@@ -287,7 +253,7 @@
     )
 
 
-def project_back(where, blocks, w, stream):
+def project_back(where, blocks, w):
     groups = lax.axis_size("dp")
     rows, depth = blocks[0].shape
     near = groups // len(blocks)
@@ -299,8 +265,7 @@
 
     def body(where_ref, *refs):
         block_refs, (w_ref, *out_refs) = refs[: len(blocks)], refs[len(blocks) :]
-        left = out_refs[close + 2]
-        run = streamed(w_ref, refs[-2], refs[-1]) if stream else None
+        left = out_refs[-1]
         d, t = where_ref[0], where_ref[1]
         for k, block_ref in enumerate(block_refs):
             for i in range(near):
@@ -317,10 +282,7 @@
             out_refs[close][:, lanes] = product[close * pair : middle]
             out_refs[close + 1][:, lanes] = product[middle:].astype(BF16)
 
-        if stream:
-            run(left[...], write)
-        else:
-            multiply(left[...], w_ref, write)
+        multiply(left[...], w_ref, write)
 
     outs = [shaped((pair, columns), F32)] + [shaped((pair, columns))] * (close - 1)
     outs += [shaped((far * pair, columns), F32), shaped((far * pair, columns))]
@@ -328,9 +290,8 @@
         body,
         tuple(outs),
         (where, *blocks, w),
-        [SMEM] + [VMEM] * len(blocks) + [HBM if stream else VMEM],
-        [pltpu.VMEM((total, depth), BF16)] + (stream_scratch(w) if stream else []),
-        limit=None if stream else 8 << 20,
+        [SMEM] + [VMEM] * (1 + len(blocks)),
+        [pltpu.VMEM((total, depth), BF16)],
         flops=2 * total * w.size,
         moved=2 * w.size,
     )
@@ -462,7 +423,7 @@
     rows, columns = queries[0].shape
     parts = rows // 2
     heads = columns // HD
-    limit = (8 << 20) + 4 * (3 * heads * parts * parts * tensor * span)
+    limit = (4 << 20) + 4 * (3 * heads * parts * parts * tensor * span)
     ins = (where, anc, rope, targets, scale, *queries, *new_kv, *cache)
     return call(
         functools.partial(attention_kernel, (tensor, groups, part_dev, span, len(queries), len(new_kv) // 2)),
@@ -555,7 +516,7 @@
     rope = jnp.asarray(np.stack(rope))
     mixed = attention(where, anc, rope, targets, scale, [queries] + queries_arrived, new_kv, caches, part_dev)
 
-    parts = project_back(where, gather_blocks(mixed), w_out, True)
+    parts = project_back(where, gather_blocks(mixed), w_out)
     attn_part, residual = finish(*sum_rows(parts, pair), x)
 
     hidden_cols = w_gate.shape[1]
@@ -568,7 +529,7 @@
         up = up + piece.astype(F32)
     scale = lax.rsqrt((gate[:, hidden_cols] + gate[:, hidden_cols + 1]) / width + EPS)[:, None]
     hidden = jax.nn.silu(gate[:, :hidden_cols] * scale) * (up * scale)
-    parts = project_back(where, gather_blocks(hidden.astype(BF16)), w_down, False)
+    parts = project_back(where, gather_blocks(hidden.astype(BF16)), w_down)
     (ffn_part,) = finish(*sum_rows(parts, pair))
     return (attn_part.reshape(2, part_dev, features), ffn_part.reshape(2, part_dev, features))
 

time: 144 us -> 117 us (0.81)
  Pallas kernels: 24.6 us -> 12.4 us
  local copies, waits for them, and re-layouts: 15.3 us -> 4.17 us
  starting transfers between devices: 54.4 us -> 58.2 us
  waiting for transfers between devices: 44 us -> 40.5 us
  other arithmetic: 3.76 us -> 0.73 us
    pallas_call x13, Pallas kernels: 24.6 us -> 12.4 us  [call(): pl.pallas_call(body, out_shape=outs, in_specs=specs, out_specs=jax.tree.m...]
    unnamed x64 -> x34, local copies, waits for them, and re-layouts: 14.1 us -> 3.81 us
    ppermute x44, waiting for transfers between devices: 42.3 us -> 34.5 us  [swap(): return lax.ppermute(x, axis, [(i, i ^ bits) for i in range(size)])]
    ppermute x44, starting transfers between devices: 40.1 us -> 46.8 us  [swap(): return lax.ppermute(x, axis, [(i, i ^ bits) for i in range(size)])]
    all_to_all x1, waiting for transfers between devices: 0.01 us -> 4.33 us  [local(): cache = lax.all_to_all(cache, 'dp', split_axis=0, concat_axis=0, tiled=True)]
    ppermute x4, starting transfers between devices: 9.72 us -> 6.88 us  [move(): return lax.ppermute(x, ('dp', 'tensor'), pairs)]
  transfers between devices with their start and end apart: 49 -> 49, of which waited for: 24 -> 22; matrix products, arithmetic and copies ran while one was open for 3% -> 1% of each run, Pallas kernels for 8% -> 3%
where the time goes in v6:
time: 117 us
  starting transfers between devices  58.2 us (50%)
  waiting for transfers between devices  40.5 us (35%)
  Pallas kernels  12.4 us (11%)
  local copies, waits for them, and re-layouts  4.17 us (4%)
    ppermute x44, starting transfers between devices, swap(): return lax.ppermute(x, axis, [(i, i ^ bits) for i in range(size)])  46.8 us
    ppermute x44, waiting for transfers between devices, swap(): return lax.ppermute(x, axis, [(i, i ^ bits) for i in range(size)])  34.5 us
    pallas_call x13, Pallas kernels, call(): pl.pallas_call(body, out_shape=outs, in_specs=specs, out_specs=jax.tree.m...  12.4 us
    ppermute x4, starting transfers between devices, move(): return lax.ppermute(x, ('dp', 'tensor'), pairs)  6.88 us
    all_to_all x1, starting transfers between devices, local(): cache = lax.all_to_all(cache, 'dp', split_axis=0, concat_axis=0, tiled=True)  4.53 us
    all_to_all x1, waiting for transfers between devices, local(): cache = lax.all_to_all(cache, 'dp', split_axis=0, concat_axis=0, tiled=True)  4.33 us
    unnamed x34, local copies, waits for them, and re-layouts  3.81 us
  transfers between devices with their start and end apart: 49, of which 22 were waited for; matrix products, arithmetic and copies ran while one was open for 1% of the time, Pallas kernels for 3%

profile of v6, /device:TPU:0, one launch (start us, length us, event | category | flops | bytes accessed | tf_op | source)
XLA Modules:
  0.0 117.0 jit_solution(3140949399966070997)
XLA Ops:
  0.7 0.8 copy-done.5
  1.5 0.8 copy-done.6
  2.3 3.1 %collective-permute-start.1 = (bf16[16,2048]{1,0:T(8,128)(2,1)S(1)}, bf16[16,2048]{1,0:T(8,128)(2,1)S(1)}, u32[]{:S(2)}, u32[]{:S(2)}) collective-permute-start(bf16[16,2048]{1,0:T(8,128)(2,1)S(1)} %shard_map.149.refs_0_.refs_5_), channel_id=1, source_target_pairs={{0,8},{4,12},{8,0},{12,4},{16,24},{20,28},{24,16},{28,20},{1,9},{5... | collective-permute-start | bytes 196616 | tf_op jit(solution)/shard_map/ppermute | solution.py:24
  5.4 2.6 %collective-permute-start.3 = (bf16[16,2048]{1,0:T(8,128)(2,1)S(1)}, bf16[16,2048]{1,0:T(8,128)(2,1)S(1)}, u32[]{:S(2)}, u32[]{:S(2)}) collective-permute-start(bf16[16,2048]{1,0:T(8,128)(2,1)S(1)} %shard_map.149.refs_0_.refs_5_), channel_id=1, source_target_pairs={{0,16},{4,20},{8,24},{12,28},{16,0},{20,4},{24,8},{28,12},{1,17},{... | collective-permute-start | bytes 196616 | tf_op jit(solution)/shard_map/ppermute | solution.py:24
  8.0 1.7 %collective-permute-start = (bf16[16,2048]{1,0:T(8,128)(2,1)S(1)}, bf16[16,2048]{1,0:T(8,128)(2,1)S(1)}, u32[]{:S(2)}, u32[]{:S(2)}) collective-permute-start(bf16[16,2048]{1,0:T(8,128)(2,1)S(1)} %shard_map.149.refs_0_.refs_5_), channel_id=1, source_target_pairs={{0,4},{4,0},{8,12},{12,8},{16,20},{20,16},{24,28},{28,24},{1,5},{5... | collective-permute-start | bytes 196616 | tf_op jit(solution)/shard_map/ppermute | solution.py:24
  10.3 2.4 %collective-permute-done.3.refs_4_.refs_1_ = bf16[16,2048]{1,0:T(8,128)(2,1)S(1)} collective-permute-done((bf16[16,2048]{1,0:T(8,128)(2,1)S(1)}, bf16[16,2048]{1,0:T(8,128)(2,1)S(1)}, u32[]{:S(2)}, u32[]{:S(2)}) %collective-permute-start.3) | collective-permute-done | bytes 65568 | tf_op jit(solution)/shard_map/ppermute | solution.py:24
  12.7 1.5 %collective-permute-start.4 = (bf16[16,2048]{1,0:T(8,128)(2,1)S(1)}, bf16[16,2048]{1,0:T(8,128)(2,1)S(1)}, u32[]{:S(2)}, u32[]{:S(2)}) collective-permute-start(bf16[16,2048]{1,0:T(8,128)(2,1)S(1)} %collective-permute-done.3.refs_4_.refs_1_), channel_id=1, source_target_pairs={{0,4},{4,0},{8,12},{12,8},{16,20},{20,16},{24,28},{28,24},{1,5},{5... | collective-permute-start | bytes 196616 | tf_op jit(solution)/shard_map/ppermute | solution.py:24
  14.1 1.4 %collective-permute-start.6 = (bf16[16,2048]{1,0:T(8,128)(2,1)S(1)}, bf16[16,2048]{1,0:T(8,128)(2,1)S(1)}, u32[]{:S(2)}, u32[]{:S(2)}) collective-permute-start(bf16[16,2048]{1,0:T(8,128)(2,1)S(1)} %collective-permute-done.5.refs_6_.refs_2_), channel_id=1, source_target_pairs={{0,4},{4,0},{8,12},{12,8},{16,20},{20,16},{24,28},{28,24},{1,5},{5... | collective-permute-start | bytes 196616 | tf_op jit(solution)/shard_map/ppermute | solution.py:24
  15.6 1.1 shard_map.151
  16.7 4.5 %all-to-all-start = ((bf16[8,2,8,8,128]{4,3,2,1,0:T(8,128)(2,1)}), bf16[8,2,8,8,128]{4,3,2,1,0:T(8,128)(2,1)S(1)}, u32[]{:S(2)}, u32[]{:S(2)}) async-start(bf16[8,2,8,8,128]{4,3,2,1,0:T(8,128)(2,1)} %shard_map.151), calls=%async_computation | async-start | bytes 524288 | tf_op jit(solution)/shard_map/all_to_all | solution.py:494
  21.3 1.0 shard_map.150
  23.0 0.5 collective-permute-done.7
  23.5 1.5 %collective-permute-start.8 = (f32[128]{0:T(128)S(1)}, f32[128]{0:T(128)S(1)}, u32[]{:S(2)}, u32[]{:S(2)}) collective-permute-start(f32[128]{0:T(128)S(1)} %add.143), channel_id=1, source_target_pairs={{0,2},{1,3},{2,0},{3,1},{4,6},{5,7},{6,4},{7,5},{8,10},{9,11},{10,... | collective-permute-start | bytes 1544 | tf_op jit(solution)/shard_map/ppermute | solution.py:24
  25.1 4.3 %all-to-all-done = bf16[8,2,8,8,128]{4,3,2,1,0:T(8,128)(2,1)S(1)} async-done(((bf16[8,2,8,8,128]{4,3,2,1,0:T(8,128)(2,1)}), bf16[8,2,8,8,128]{4,3,2,1,0:T(8,128)(2,1)S(1)}, u32[]{:S(2)}, u32[]{:S(2)}) %all-to-all-start) | async-done | bytes 262176 | tf_op jit(solution)/shard_map/all_to_all | solution.py:494
  29.4 1.5 %collective-permute-start.17 = (bf16[128,8,128]{2,1,0:T(8,128)(2,1)S(1)}, bf16[128,8,128]{2,1,0:T(8,128)(2,1)S(1)}, u32[]{:S(2)}, u32[]{:S(2)}) collective-permute-start(bf16[128,8,128]{2,1,0:T(8,128)(2,1)S(1)} %bitcast.12), channel_id=1, source_target_pairs={{0,2},{1,3},{2,0},{3,1},{4,6},{5,7},{6,4},{7,5},{8,10},{9,11},{10,... | collective-permute-start | bytes 786440 | tf_op jit(solution)/shard_map/ppermute | solution.py:24
  30.9 2.2 %copy-done = bf16[2048,1024]{1,0:T(8,128)(2,1)S(1)} copy-done((bf16[2048,1024]{1,0:T(8,128)(2,1)S(1)}, bf16[2048,1024]{1,0:T(8,128)(2,1)}, u32[]{:S(2)}) %copy-start) | copy-done | bytes 4194328
  33.1 0.7 shard_map.152
  34.0 0.7 collective-permute-start.12
  34.6 0.6 collective-permute-start.13
  35.9 3.2 %collective-permute-start.14 = (bf16[128,128]{1,0:T(8,128)(2,1)S(1)}, bf16[128,128]{1,0:T(8,128)(2,1)S(1)}, u32[]{:S(2)}, u32[]{:S(2)}) collective-permute-start(bf16[128,128]{1,0:T(8,128)(2,1)S(1)} %get-tuple-element.60), channel_id=1, source_target_pairs={{0,4},{1,5},{2,6},{3,7},{4,12},{5,13},{6,14},{7,15},{8,20},{9,21},... | collective-permute-start | bytes 98312 | tf_op jit(solution)/shard_map/ppermute | solution.py:454
  39.1 2.4 %collective-permute-start.15 = (bf16[128,128]{1,0:T(8,128)(2,1)S(1)}, bf16[128,128]{1,0:T(8,128)(2,1)S(1)}, u32[]{:S(2)}, u32[]{:S(2)}) collective-permute-start(bf16[128,128]{1,0:T(8,128)(2,1)S(1)} %get-tuple-element.60), channel_id=1, source_target_pairs={{0,6},{1,7},{2,4},{3,5},{4,14},{5,15},{6,12},{7,13},{8,22},{9,23},... | collective-permute-start | bytes 98312 | tf_op jit(solution)/shard_map/ppermute | solution.py:454
  41.5 1.5 %collective-permute-start.10 = (bf16[32,1024]{1,0:T(8,128)(2,1)S(1)}, bf16[32,1024]{1,0:T(8,128)(2,1)S(1)}, u32[]{:S(2)}, u32[]{:S(2)}) collective-permute-start(bf16[32,1024]{1,0:T(8,128)(2,1)S(1)} %slice.101), channel_id=1, source_target_pairs={{0,2},{1,3},{2,0},{3,1},{4,6},{5,7},{6,4},{7,5},{8,10},{9,11},{10,... | collective-permute-start | bytes 196616 | tf_op jit(solution)/shard_map/ppermute | solution.py:24
  43.2 1.6 %collective-permute-done.15.refs_5_ = bf16[128,128]{1,0:T(8,128)(2,1)S(1)} collective-permute-done((bf16[128,128]{1,0:T(8,128)(2,1)S(1)}, bf16[128,128]{1,0:T(8,128)(2,1)S(1)}, u32[]{:S(2)}, u32[]{:S(2)}) %collective-permute-start.15) | collective-permute-done | bytes 32800 | tf_op jit(solution)/shard_map/ppermute | solution.py:454
  44.8 1.0 collective-permute-done.10.refs_1_
  45.8 2.1 %shard_map.153.refs_0_ = bf16[32,1024]{1,0:T(8,128)(2,1)S(1)} custom-call(s32[2]{0:T(128)S(1)} %pad_add_fusion.1.where_ref, s32[16]{0:T(128)S(1)} %get-tuple-element.59.anc_ref, f32[4,128]{1,0:T(4,128)S(1)} %copy-done.9, s32[128,3]{1,0:T(8,128)S(1)} %bitcast.16, f32[128,1]{1,0:T(8,128)S(1)} %copy.19.scale_ref, f32[32,1024]{1,0:T(8,128)S(1)} %slice.59.refs_0_, ...), custom_call_target="tpu_custom_call" | custom-call | flops 6442450944 | bytes 4194304 | tf_op jit(solution)/shard_map/pallas_call | solution.py:45
  48.0 1.6 %collective-permute-start.20 = (bf16[32,1024]{1,0:T(8,128)(2,1)S(1)}, bf16[32,1024]{1,0:T(8,128)(2,1)S(1)}, u32[]{:S(2)}, u32[]{:S(2)}) collective-permute-start(bf16[32,1024]{1,0:T(8,128)(2,1)S(1)} %shard_map.153.refs_0_), channel_id=1, source_target_pairs={{0,2},{1,3},{2,0},{3,1},{4,6},{5,7},{6,4},{7,5},{8,10},{9,11},{10,... | collective-permute-start | bytes 196616 | tf_op jit(solution)/shard_map/ppermute | solution.py:24
  49.6 2.7 %collective-permute-done.20.refs_2_ = bf16[32,1024]{1,0:T(8,128)(2,1)S(1)} collective-permute-done((bf16[32,1024]{1,0:T(8,128)(2,1)S(1)}, bf16[32,1024]{1,0:T(8,128)(2,1)S(1)}, u32[]{:S(2)}, u32[]{:S(2)}) %collective-permute-start.20) | collective-permute-done | bytes 65568 | tf_op jit(solution)/shard_map/ppermute | solution.py:24
  52.3 1.2 %collective-permute-done.21.refs_3_ = bf16[32,1024]{1,0:T(8,128)(2,1)S(1)} collective-permute-done((bf16[32,1024]{1,0:T(8,128)(2,1)S(1)}, bf16[32,1024]{1,0:T(8,128)(2,1)S(1)}, u32[]{:S(2)}, u32[]{:S(2)}) %collective-permute-start.21) | collective-permute-done | bytes 65568 | tf_op jit(solution)/shard_map/ppermute | solution.py:24
  53.6 1.3 %shard_map.154 = (f32[16,2048]{1,0:T(8,128)S(1)}, bf16[16,2048]{1,0:T(8,128)(2,1)S(1)}, bf16[16,2048]{1,0:T(8,128)(2,1)S(1)}, bf16[16,2048]{1,0:T(8,128)(2,1)S(1...) custom-call(s32[2]{0:T(128)S(1)} %pad_add_fusion.1.where_ref, bf16[32,1024]{1,0:T(8,128)(2,1)S(1)} %shard_map.153.refs_0_, ...), custom_call_target="tpu_custom_call" | custom-call | flops 5905580032 | bytes 4194304 | tf_op jit(solution)/shard_map/pallas_call | solution.py:45
  54.8 2.9 %collective-permute-start.22 = (bf16[32,2048]{1,0:T(8,128)(2,1)S(1)}, bf16[32,2048]{1,0:T(8,128)(2,1)S(1)}, u32[]{:S(2)}, u32[]{:S(2)}) collective-permute-start(bf16[32,2048]{1,0:T(8,128)(2,1)S(1)} %get-tuple-element.37), channel_id=1, source_target_pairs={{0,4},{4,0},{8,12},{12,8},{16,20},{20,16},{24,28},{28,24},{1,5},{5... | collective-permute-start | bytes 393224 | tf_op jit(solution)/shard_map/ppermute | solution.py:24
  57.8 0.9 collective-permute-start.26
  58.8 2.5 %collective-permute-start.27 = (bf16[16,2048]{1,0:T(8,128)(2,1)S(1)}, bf16[16,2048]{1,0:T(8,128)(2,1)S(1)}, u32[]{:S(2)}, u32[]{:S(2)}) collective-permute-start(bf16[16,2048]{1,0:T(8,128)(2,1)S(1)} %get-tuple-element.42), channel_id=1, source_target_pairs={{0,12},{4,8},{8,4},{12,0},{16,28},{20,24},{24,20},{28,16},{1,13},{... | collective-permute-start | bytes 196616 | tf_op jit(solution)/shard_map/ppermute | solution.py:24
  61.2 1.7 %collective-permute-done.22.arrived_ref = bf16[32,2048]{1,0:T(8,128)(2,1)S(1)} collective-permute-done((bf16[32,2048]{1,0:T(8,128)(2,1)S(1)}, bf16[32,2048]{1,0:T(8,128)(2,1)S(1)}, u32[]{:S(2)}, u32[]{:S(2)}) %collective-permute-start.22) | collective-permute-done | bytes 131104 | tf_op jit(solution)/shard_map/ppermute | solution.py:24
  63.1 2.5 %collective-permute-start.24 = (bf16[16,2048]{1,0:T(8,128)(2,1)S(1)}, bf16[16,2048]{1,0:T(8,128)(2,1)S(1)}, u32[]{:S(2)}, u32[]{:S(2)}) collective-permute-start(bf16[16,2048]{1,0:T(8,128)(2,1)S(1)} %get-tuple-element.39), channel_id=1, source_target_pairs={{0,24},{4,28},{8,16},{12,20},{16,8},{20,12},{24,0},{28,4},{1,25},{... | collective-permute-start | bytes 196616 | tf_op jit(solution)/shard_map/ppermute | solution.py:24
  65.6 3.9 %collective-permute-done.23.refs_0_ = bf16[16,2048]{1,0:T(8,128)(2,1)S(1)} collective-permute-done((bf16[16,2048]{1,0:T(8,128)(2,1)S(1)}, bf16[16,2048]{1,0:T(8,128)(2,1)S(1)}, u32[]{:S(2)}, u32[]{:S(2)}) %collective-permute-start.23) | collective-permute-done | bytes 65568 | tf_op jit(solution)/shard_map/ppermute | solution.py:24
  69.6 0.7 shard_map.156
  70.2 1.3 %collective-permute-start.29 = (bf16[16,2048]{1,0:T(8,128)(2,1)S(1)}, bf16[16,2048]{1,0:T(8,128)(2,1)S(1)}, u32[]{:S(2)}, u32[]{:S(2)}) collective-permute-start(bf16[16,2048]{1,0:T(8,128)(2,1)S(1)} %get-tuple-element.44.refs_0_), channel_id=1, source_target_pairs={{0,8},{4,12},{8,0},{12,4},{16,24},{20,28},{24,16},{28,20},{1,9},{5... | collective-permute-start | bytes 196616 | tf_op jit(solution)/shard_map/ppermute | solution.py:24
  71.5 1.5 %collective-permute-start.31 = (bf16[16,2048]{1,0:T(8,128)(2,1)S(1)}, bf16[16,2048]{1,0:T(8,128)(2,1)S(1)}, u32[]{:S(2)}, u32[]{:S(2)}) collective-permute-start(bf16[16,2048]{1,0:T(8,128)(2,1)S(1)} %get-tuple-element.44.refs_0_), channel_id=1, source_target_pairs={{0,16},{4,20},{8,24},{12,28},{16,0},{20,4},{24,8},{28,12},{1,17},{... | collective-permute-start | bytes 196616 | tf_op jit(solution)/shard_map/ppermute | solution.py:24
  73.0 1.6 %collective-permute-start.33 = (bf16[16,2048]{1,0:T(8,128)(2,1)S(1)}, bf16[16,2048]{1,0:T(8,128)(2,1)S(1)}, u32[]{:S(2)}, u32[]{:S(2)}) collective-permute-start(bf16[16,2048]{1,0:T(8,128)(2,1)S(1)} %get-tuple-element.44.refs_0_), channel_id=1, source_target_pairs={{0,24},{4,28},{8,16},{12,20},{16,8},{20,12},{24,0},{28,4},{1,25},{... | collective-permute-start | bytes 196616 | tf_op jit(solution)/shard_map/ppermute | solution.py:24
  74.6 2.2 %collective-permute-start.28 = (bf16[16,2048]{1,0:T(8,128)(2,1)S(1)}, bf16[16,2048]{1,0:T(8,128)(2,1)S(1)}, u32[]{:S(2)}, u32[]{:S(2)}) collective-permute-start(bf16[16,2048]{1,0:T(8,128)(2,1)S(1)} %get-tuple-element.44.refs_0_), channel_id=1, source_target_pairs={{0,4},{4,0},{8,12},{12,8},{16,20},{20,16},{24,28},{28,24},{1,5},{5... | collective-permute-start | bytes 196616 | tf_op jit(solution)/shard_map/ppermute | solution.py:24
  77.4 1.5 %collective-permute-start.32 = (bf16[16,2048]{1,0:T(8,128)(2,1)S(1)}, bf16[16,2048]{1,0:T(8,128)(2,1)S(1)}, u32[]{:S(2)}, u32[]{:S(2)}) collective-permute-start(bf16[16,2048]{1,0:T(8,128)(2,1)S(1)} %collective-permute-done.31.refs_4_), channel_id=1, source_target_pairs={{0,4},{4,0},{8,12},{12,8},{16,20},{20,16},{24,28},{28,24},{1,5},{5... | collective-permute-start | bytes 196616 | tf_op jit(solution)/shard_map/ppermute | solution.py:24
  79.1 0.8 collective-permute-start.34
  79.9 1.2 %collective-permute-done.30.refs_3_ = bf16[16,2048]{1,0:T(8,128)(2,1)S(1)} collective-permute-done((bf16[16,2048]{1,0:T(8,128)(2,1)S(1)}, bf16[16,2048]{1,0:T(8,128)(2,1)S(1)}, u32[]{:S(2)}, u32[]{:S(2)}) %collective-permute-start.30) | collective-permute-done | bytes 65568 | tf_op jit(solution)/shard_map/ppermute | solution.py:24
  81.1 0.7 collective-permute-done.32.refs_5_
  81.8 1.5 %collective-permute-done.34.refs_7_ = bf16[16,2048]{1,0:T(8,128)(2,1)S(1)} collective-permute-done((bf16[16,2048]{1,0:T(8,128)(2,1)S(1)}, bf16[16,2048]{1,0:T(8,128)(2,1)S(1)}, u32[]{:S(2)}, u32[]{:S(2)}) %collective-permute-start.34) | collective-permute-done | bytes 65568 | tf_op jit(solution)/shard_map/ppermute | solution.py:24
  83.4 1.8 %shard_map.157 = (bf16[128,2048]{1,0:T(8,128)(2,1)S(1)}, f32[64,1920]{1,0:T(8,128)S(1)}, bf16[64,1920]{1,0:T(8,128)(2,1)S(1)}) custom-call(s32[2]{0:T(128)S(1)} %pad_add_fusion.1.where_ref, f32[1,2048]{1,0:T(1,128)S(1)} %bitcast.24, bf16[16,2048]{1,0:T(8,128)(2,1)S(1)} %get-tuple-element.44.refs_0_, bf16[16,2048]{1,0:T(8,128)(2,1)S(1)} %collective-permute-done.28.refs_1_, ...), custom_call_target="tpu_custom_call" | custom-call | flops 6308233216 | bytes 8388608 | tf_op jit(solution)/shard_map/pallas_call | solution.py:45
  85.3 1.1 shard_map.158
  86.5 0.5 collective-permute-start.37
  87.1 1.4 %collective-permute-start.36 = (bf16[32,1920]{1,0:T(8,128)(2,1)S(1)}, bf16[32,1920]{1,0:T(8,128)(2,1)S(1)}, u32[]{:S(2)}, u32[]{:S(2)}) collective-permute-start(bf16[32,1920]{1,0:T(8,128)(2,1)S(1)} %slice.99), channel_id=1, source_target_pairs={{0,2},{1,3},{2,0},{3,1},{4,6},{5,7},{6,4},{7,5},{8,10},{9,11},{10,... | collective-permute-start | bytes 368648 | tf_op jit(solution)/shard_map/ppermute | solution.py:24
  88.6 1.0 collective-permute-start.38
  89.6 3.7 %collective-permute-done.36 = bf16[32,1920]{1,0:T(8,128)(2,1)S(1)} collective-permute-done((bf16[32,1920]{1,0:T(8,128)(2,1)S(1)}, bf16[32,1920]{1,0:T(8,128)(2,1)S(1)}, u32[]{:S(2)}, u32[]{:S(2)}) %collective-permute-start.36) | collective-permute-done | bytes 122912 | tf_op jit(solution)/shard_map/ppermute | solution.py:24
  93.5 1.3 %collective-permute-done.38 = bf16[32,1792]{1,0:T(8,128)(2,1)S(1)} collective-permute-done((bf16[32,1792]{1,0:T(8,128)(2,1)S(1)}, bf16[32,1792]{1,0:T(8,128)(2,1)S(1)}, u32[]{:S(2)}, u32[]{:S(2)}) %collective-permute-start.38) | collective-permute-done | bytes 114720 | tf_op jit(solution)/shard_map/ppermute | solution.py:24
  95.0 1.4 %collective-permute-start.40 = (bf16[32,1792]{1,0:T(8,128)(2,1)S(1)}, bf16[32,1792]{1,0:T(8,128)(2,1)S(1)}, u32[]{:S(2)}, u32[]{:S(2)}) collective-permute-start(bf16[32,1792]{1,0:T(8,128)(2,1)S(1)} %fusion.2.refs_0_), channel_id=1, source_target_pairs={{0,2},{1,3},{2,0},{3,1},{4,6},{5,7},{6,4},{7,5},{8,10},{9,11},{10,... | collective-permute-start | bytes 344072 | tf_op jit(solution)/shard_map/ppermute | solution.py:24
  96.4 3.5 %collective-permute-done.40.refs_2_ = bf16[32,1792]{1,0:T(8,128)(2,1)S(1)} collective-permute-done((bf16[32,1792]{1,0:T(8,128)(2,1)S(1)}, bf16[32,1792]{1,0:T(8,128)(2,1)S(1)}, u32[]{:S(2)}, u32[]{:S(2)}) %collective-permute-start.40) | collective-permute-done | bytes 114720 | tf_op jit(solution)/shard_map/ppermute | solution.py:24
  99.9 1.3 %collective-permute-done.41.refs_3_ = bf16[32,1792]{1,0:T(8,128)(2,1)S(1)} collective-permute-done((bf16[32,1792]{1,0:T(8,128)(2,1)S(1)}, bf16[32,1792]{1,0:T(8,128)(2,1)S(1)}, u32[]{:S(2)}, u32[]{:S(2)}) %collective-permute-start.41) | collective-permute-done | bytes 114720 | tf_op jit(solution)/shard_map/ppermute | solution.py:24
  101.2 1.7 %shard_map.159 = (f32[16,2048]{1,0:T(8,128)S(1)}, bf16[16,2048]{1,0:T(8,128)(2,1)S(1)}, bf16[16,2048]{1,0:T(8,128)(2,1)S(1)}, bf16[16,2048]{1,0:T(8,128)(2,1)S(1...) custom-call(s32[2]{0:T(128)S(1)} %pad_add_fusion.1.where_ref, bf16[32,1792]{1,0:T(8,128)(2,1)S(1)} %fusion.2.refs_0_, ...), custom_call_target="tpu_custom_call" | custom-call | flops 6308233216 | bytes 7340032 | tf_op jit(solution)/shard_map/pallas_call | solution.py:45
  102.9 0.9 collective-permute-start.42
  103.8 1.2 %collective-permute-start.45 = (bf16[16,2048]{1,0:T(8,128)(2,1)S(1)}, bf16[16,2048]{1,0:T(8,128)(2,1)S(1)}, u32[]{:S(2)}, u32[]{:S(2)}) collective-permute-start(bf16[16,2048]{1,0:T(8,128)(2,1)S(1)} %get-tuple-element.55), channel_id=1, source_target_pairs={{0,4},{4,0},{8,12},{12,8},{16,20},{20,16},{24,28},{28,24},{1,5},{5... | collective-permute-start | bytes 196616 | tf_op jit(solution)/shard_map/ppermute | solution.py:24
  105.0 0.7 collective-permute-start.46
  105.7 1.6 %collective-permute-start.47 = (bf16[16,2048]{1,0:T(8,128)(2,1)S(1)}, bf16[16,2048]{1,0:T(8,128)(2,1)S(1)}, u32[]{:S(2)}, u32[]{:S(2)}) collective-permute-start(bf16[16,2048]{1,0:T(8,128)(2,1)S(1)} %get-tuple-element.57), channel_id=1, source_target_pairs={{0,12},{4,8},{8,4},{12,0},{16,28},{20,24},{24,20},{28,16},{1,13},{... | collective-permute-start | bytes 196616 | tf_op jit(solution)/shard_map/ppermute | solution.py:24
  107.3 2.6 %collective-permute-done.42.arrived_ref = bf16[32,2048]{1,0:T(8,128)(2,1)S(1)} collective-permute-done((bf16[32,2048]{1,0:T(8,128)(2,1)S(1)}, bf16[32,2048]{1,0:T(8,128)(2,1)S(1)}, u32[]{:S(2)}, u32[]{:S(2)}) %collective-permute-start.42) | collective-permute-done | bytes 131104 | tf_op jit(solution)/shard_map/ppermute | solution.py:24
  110.0 2.4 %collective-permute-start.44 = (bf16[16,2048]{1,0:T(8,128)(2,1)S(1)}, bf16[16,2048]{1,0:T(8,128)(2,1)S(1)}, u32[]{:S(2)}, u32[]{:S(2)}) collective-permute-start(bf16[16,2048]{1,0:T(8,128)(2,1)S(1)} %get-tuple-element.54), channel_id=1, source_target_pairs={{0,24},{4,28},{8,16},{12,20},{16,8},{20,12},{24,0},{28,4},{1,25},{... | collective-permute-start | bytes 196616 | tf_op jit(solution)/shard_map/ppermute | solution.py:24
  112.4 3.9 %collective-permute-done.43.refs_0_ = bf16[16,2048]{1,0:T(8,128)(2,1)S(1)} collective-permute-done((bf16[16,2048]{1,0:T(8,128)(2,1)S(1)}, bf16[16,2048]{1,0:T(8,128)(2,1)S(1)}, u32[]{:S(2)}, u32[]{:S(2)}) %collective-permute-start.43) | collective-permute-done | bytes 65568 | tf_op jit(solution)/shard_map/ppermute | solution.py:24
  116.4 0.7 shard_map.161
  (106 shorter events, 4.0 us)
Async XLA Ops:
  0.6 14.9 %copy-start.3 = (bf16[8,8,1024]{2,1,0:T(8,128)(2,1)S(1)}, bf16[8,8,1024]{2,1,0:T(8,128)(2,1)}, u32[]{:S(2)}) copy-start(bf16[8,8,1024]{2,1,0:T(8,128)(2,1)} %keys_hbm.1) | copy-start | bytes 393220
  0.6 14.9 %copy-start.4 = (bf16[8,8,1024]{2,1,0:T(8,128)(2,1)S(1)}, bf16[8,8,1024]{2,1,0:T(8,128)(2,1)}, u32[]{:S(2)}) copy-start(bf16[8,8,1024]{2,1,0:T(8,128)(2,1)} %values_hbm.1) | copy-start | bytes 393220
  2.2 7.6 %copy-start.10 = (s32[64]{0:T(128)S(1)}, s32[64]{0:T(128)}, u32[]{:S(2)}) copy-start(s32[64]{0:T(128)} %param.18) | copy-start | bytes 772
  2.3 7.6 %collective-permute-start.1 = (bf16[16,2048]{1,0:T(8,128)(2,1)S(1)}, bf16[16,2048]{1,0:T(8,128)(2,1)S(1)}, u32[]{:S(2)}, u32[]{:S(2)}) collective-permute-start(bf16[16,2048]{1,0:T(8,128)(2,1)S(1)} %shard_map.149.refs_0_.refs_5_), channel_id=1, source_target_pairs={{0,8},{4,12},{8,0},{12,4},{16,24},{20,28},{24,16},{28,20},{1,9},{5... | collective-permute-start | bytes 196616 | tf_op jit(solution)/shard_map/ppermute | solution.py:24
  5.4 7.3 %collective-permute-start.3 = (bf16[16,2048]{1,0:T(8,128)(2,1)S(1)}, bf16[16,2048]{1,0:T(8,128)(2,1)S(1)}, u32[]{:S(2)}, u32[]{:S(2)}) collective-permute-start(bf16[16,2048]{1,0:T(8,128)(2,1)S(1)} %shard_map.149.refs_0_.refs_5_), channel_id=1, source_target_pairs={{0,16},{4,20},{8,24},{12,28},{16,0},{20,4},{24,8},{28,12},{1,17},{... | collective-permute-start | bytes 196616 | tf_op jit(solution)/shard_map/ppermute | solution.py:24
  8.0 6.2 %collective-permute-start.5 = (bf16[16,2048]{1,0:T(8,128)(2,1)S(1)}, bf16[16,2048]{1,0:T(8,128)(2,1)S(1)}, u32[]{:S(2)}, u32[]{:S(2)}) collective-permute-start(bf16[16,2048]{1,0:T(8,128)(2,1)S(1)} %shard_map.149.refs_0_.refs_5_), channel_id=1, source_target_pairs={{0,24},{4,28},{8,16},{12,20},{16,8},{20,12},{24,0},{28,4},{1,25},{... | collective-permute-start | bytes 196616 | tf_op jit(solution)/shard_map/ppermute | solution.py:24
  8.0 13.2 %collective-permute-start = (bf16[16,2048]{1,0:T(8,128)(2,1)S(1)}, bf16[16,2048]{1,0:T(8,128)(2,1)S(1)}, u32[]{:S(2)}, u32[]{:S(2)}) collective-permute-start(bf16[16,2048]{1,0:T(8,128)(2,1)S(1)} %shard_map.149.refs_0_.refs_5_), channel_id=1, source_target_pairs={{0,4},{4,0},{8,12},{12,8},{16,20},{20,16},{24,28},{28,24},{1,5},{5... | collective-permute-start | bytes 196616 | tf_op jit(solution)/shard_map/ppermute | solution.py:24
  9.9 11.4 %copy-start.2 = (bf16[2048,256]{1,0:T(8,128)(2,1)S(1)}, bf16[2048,256]{1,0:T(8,128)(2,1)}, u32[]{:S(2)}) copy-start(bf16[2048,256]{1,0:T(8,128)(2,1)} %refs_8_.2) | copy-start | bytes 3145732
  9.9 11.4 %copy-start.7 = (f32[2048]{0:T(1024)S(1)}, f32[2048]{0:T(1024)}, u32[]{:S(2)}) copy-start(f32[2048]{0:T(1024)} %param.19) | copy-start | bytes 24580
  9.9 11.3 %collective-permute-start.2 = (bf16[16,2048]{1,0:T(8,128)(2,1)S(1)}, bf16[16,2048]{1,0:T(8,128)(2,1)S(1)}, u32[]{:S(2)}, u32[]{:S(2)}) collective-permute-start(bf16[16,2048]{1,0:T(8,128)(2,1)S(1)} %collective-permute-done.1.refs_2_.refs_0_), channel_id=1, source_target_pairs={{0,4},{4,0},{8,12},{12,8},{16,20},{20,16},{24,28},{28,24},{1,5},{5... | collective-permute-start | bytes 196616 | tf_op jit(solution)/shard_map/ppermute | solution.py:24
  12.7 8.6 %collective-permute-start.4 = (bf16[16,2048]{1,0:T(8,128)(2,1)S(1)}, bf16[16,2048]{1,0:T(8,128)(2,1)S(1)}, u32[]{:S(2)}, u32[]{:S(2)}) collective-permute-start(bf16[16,2048]{1,0:T(8,128)(2,1)S(1)} %collective-permute-done.3.refs_4_.refs_1_), channel_id=1, source_target_pairs={{0,4},{4,0},{8,12},{12,8},{16,20},{20,16},{24,28},{28,24},{1,5},{5... | collective-permute-start | bytes 196616 | tf_op jit(solution)/shard_map/ppermute | solution.py:24
  14.1 7.1 %collective-permute-start.6 = (bf16[16,2048]{1,0:T(8,128)(2,1)S(1)}, bf16[16,2048]{1,0:T(8,128)(2,1)S(1)}, u32[]{:S(2)}, u32[]{:S(2)}) collective-permute-start(bf16[16,2048]{1,0:T(8,128)(2,1)S(1)} %collective-permute-done.5.refs_6_.refs_2_), channel_id=1, source_target_pairs={{0,4},{4,0},{8,12},{12,8},{16,20},{20,16},{24,28},{28,24},{1,5},{5... | collective-permute-start | bytes 196616 | tf_op jit(solution)/shard_map/ppermute | solution.py:24
  16.7 12.7 %all-to-all-start = ((bf16[8,2,8,8,128]{4,3,2,1,0:T(8,128)(2,1)}), bf16[8,2,8,8,128]{4,3,2,1,0:T(8,128)(2,1)S(1)}, u32[]{:S(2)}, u32[]{:S(2)}) async-start(bf16[8,2,8,8,128]{4,3,2,1,0:T(8,128)(2,1)} %shard_map.151), calls=%async_computation | async-start | bytes 524288 | tf_op jit(solution)/shard_map/all_to_all | solution.py:494
  22.4 1.2 %collective-permute-start.7 = (f32[128]{0:T(128)S(1)}, f32[128]{0:T(128)S(1)}, u32[]{:S(2)}, u32[]{:S(2)}) collective-permute-start(f32[128]{0:T(128)S(1)} %slice_reduce_fusion), channel_id=1, source_target_pairs={{0,1},{1,0},{2,3},{3,2},{4,5},{5,4},{6,7},{7,6},{8,9},{9,8},{10,11... | collective-permute-start | bytes 1544 | tf_op jit(solution)/shard_map/ppermute | solution.py:24
  22.4 2.6 %collective-permute-start.11 = (bf16[128,256]{1,0:T(8,128)(2,1)S(1)}, bf16[128,256]{1,0:T(8,128)(2,1)S(1)}, u32[]{:S(2)}, u32[]{:S(2)}) collective-permute-start(bf16[128,256]{1,0:T(8,128)(2,1)S(1)} %get-tuple-element.34), channel_id=1, source_target_pairs={{0,1},{1,0},{2,3},{3,2},{4,5},{5,4},{6,7},{7,6},{8,9},{9,8},{10,11... | collective-permute-start | bytes 196616 | tf_op jit(solution)/shard_map/ppermute | solution.py:24
  23.5 12.3 %collective-permute-start.8 = (f32[128]{0:T(128)S(1)}, f32[128]{0:T(128)S(1)}, u32[]{:S(2)}, u32[]{:S(2)}) collective-permute-start(f32[128]{0:T(128)S(1)} %add.143), channel_id=1, source_target_pairs={{0,2},{1,3},{2,0},{3,1},{4,6},{5,7},{6,4},{7,5},{8,10},{9,11},{10,... | collective-permute-start | bytes 1544 | tf_op jit(solution)/shard_map/ppermute | solution.py:24
  29.4 6.4 %collective-permute-start.17 = (bf16[128,8,128]{2,1,0:T(8,128)(2,1)S(1)}, bf16[128,8,128]{2,1,0:T(8,128)(2,1)S(1)}, u32[]{:S(2)}, u32[]{:S(2)}) collective-permute-start(bf16[128,8,128]{2,1,0:T(8,128)(2,1)S(1)} %bitcast.12), channel_id=1, source_target_pairs={{0,2},{1,3},{2,0},{3,1},{4,6},{5,7},{6,4},{7,5},{8,10},{9,11},{10,... | collective-permute-start | bytes 786440 | tf_op jit(solution)/shard_map/ppermute | solution.py:24
  30.9 2.2 %copy-start = (bf16[2048,1024]{1,0:T(8,128)(2,1)S(1)}, bf16[2048,1024]{1,0:T(8,128)(2,1)}, u32[]{:S(2)}) copy-start(bf16[2048,1024]{1,0:T(8,128)(2,1)} %w_ref.2) | copy-start | bytes 12582916
  33.1 12.7 %copy-start.9 = (f32[4,128]{1,0:T(4,128)S(1)}, f32[4,128]{1,0:T(4,128)}, u32[]{:S(2)}) copy-start(f32[4,128]{1,0:T(4,128)} %constant.76.clone.rope_ref) | copy-start | bytes 6148
  33.9 1.4 %collective-permute-start.9 = (bf16[64,1024]{1,0:T(8,128)(2,1)S(1)}, bf16[64,1024]{1,0:T(8,128)(2,1)S(1)}, u32[]{:S(2)}, u32[]{:S(2)}) collective-permute-start(bf16[64,1024]{1,0:T(8,128)(2,1)S(1)} %get-tuple-element.33), channel_id=1, source_target_pairs={{0,1},{1,0},{2,3},{3,2},{4,5},{5,4},{6,7},{7,6},{8,9},{9,8},{10,11... | collective-permute-start | bytes 393224 | tf_op jit(solution)/shard_map/ppermute | solution.py:24
  34.0 5.1 %collective-permute-start.12 = (bf16[128,128]{1,0:T(8,128)(2,1)S(1)}, bf16[128,128]{1,0:T(8,128)(2,1)S(1)}, u32[]{:S(2)}, u32[]{:S(2)}) collective-permute-start(bf16[128,128]{1,0:T(8,128)(2,1)S(1)} %get-tuple-element.61), channel_id=1, source_target_pairs={{0,0},{1,1},{2,2},{3,3},{4,8},{5,9},{6,10},{7,11},{8,16},{9,17},{1... | collective-permute-start | bytes 98312 | tf_op jit(solution)/shard_map/ppermute | solution.py:454
  34.6 6.9 %collective-permute-start.13 = (bf16[128,128]{1,0:T(8,128)(2,1)S(1)}, bf16[128,128]{1,0:T(8,128)(2,1)S(1)}, u32[]{:S(2)}, u32[]{:S(2)}) collective-permute-start(bf16[128,128]{1,0:T(8,128)(2,1)S(1)} %get-tuple-element.61), channel_id=1, source_target_pairs={{0,2},{1,3},{2,0},{3,1},{4,10},{5,11},{6,8},{7,9},{8,18},{9,19},{1... | collective-permute-start | bytes 98312 | tf_op jit(solution)/shard_map/ppermute | solution.py:454
  35.3 10.5 %collective-permute-start.16 = (bf16[128,8,128]{2,1,0:T(8,128)(2,1)S(1)}, bf16[128,8,128]{2,1,0:T(8,128)(2,1)S(1)}, u32[]{:S(2)}, u32[]{:S(2)}) collective-permute-start(bf16[128,8,128]{2,1,0:T(8,128)(2,1)S(1)} %bitcast.14), channel_id=1, source_target_pairs={{0,1},{1,0},{2,3},{3,2},{4,5},{5,4},{6,7},{7,6},{8,9},{9,8},{10,11... | collective-permute-start | bytes 786440 | tf_op jit(solution)/shard_map/ppermute | solution.py:24
  35.8 10.0 %collective-permute-start.18 = (bf16[128,8,128]{2,1,0:T(8,128)(2,1)S(1)}, bf16[128,8,128]{2,1,0:T(8,128)(2,1)S(1)}, u32[]{:S(2)}, u32[]{:S(2)}) collective-permute-start(bf16[128,8,128]{2,1,0:T(8,128)(2,1)S(1)} %collective-permute-done.17.refs_8_), channel_id=1, source_target_pairs={{0,1},{1,0},{2,3},{3,2},{4,5},{5,4},{6,7},{7,6},{8,9},{9,8},{10,11... | collective-permute-start | bytes 786440 | tf_op jit(solution)/shard_map/ppermute | solution.py:24
  35.9 7.3 %collective-permute-start.14 = (bf16[128,128]{1,0:T(8,128)(2,1)S(1)}, bf16[128,128]{1,0:T(8,128)(2,1)S(1)}, u32[]{:S(2)}, u32[]{:S(2)}) collective-permute-start(bf16[128,128]{1,0:T(8,128)(2,1)S(1)} %get-tuple-element.60), channel_id=1, source_target_pairs={{0,4},{1,5},{2,6},{3,7},{4,12},{5,13},{6,14},{7,15},{8,20},{9,21},... | collective-permute-start | bytes 98312 | tf_op jit(solution)/shard_map/ppermute | solution.py:454
  39.1 5.7 %collective-permute-start.15 = (bf16[128,128]{1,0:T(8,128)(2,1)S(1)}, bf16[128,128]{1,0:T(8,128)(2,1)S(1)}, u32[]{:S(2)}, u32[]{:S(2)}) collective-permute-start(bf16[128,128]{1,0:T(8,128)(2,1)S(1)} %get-tuple-element.60), channel_id=1, source_target_pairs={{0,6},{1,7},{2,4},{3,5},{4,14},{5,15},{6,12},{7,13},{8,22},{9,23},... | collective-permute-start | bytes 98312 | tf_op jit(solution)/shard_map/ppermute | solution.py:454
  41.5 4.3 %collective-permute-start.10 = (bf16[32,1024]{1,0:T(8,128)(2,1)S(1)}, bf16[32,1024]{1,0:T(8,128)(2,1)S(1)}, u32[]{:S(2)}, u32[]{:S(2)}) collective-permute-start(bf16[32,1024]{1,0:T(8,128)(2,1)S(1)} %slice.101), channel_id=1, source_target_pairs={{0,2},{1,3},{2,0},{3,1},{4,6},{5,7},{6,4},{7,5},{8,10},{9,11},{10,... | collective-permute-start | bytes 196616 | tf_op jit(solution)/shard_map/ppermute | solution.py:24
  45.8 7.7 %copy-start.1 = (bf16[1024,2048]{1,0:T(8,128)(2,1)S(1)}, bf16[1024,2048]{1,0:T(8,128)(2,1)}, u32[]{:S(2)}) copy-start(bf16[1024,2048]{1,0:T(8,128)(2,1)} %refs_4_.2) | copy-start | bytes 12582916
  48.0 4.3 %collective-permute-start.20 = (bf16[32,1024]{1,0:T(8,128)(2,1)S(1)}, bf16[32,1024]{1,0:T(8,128)(2,1)S(1)}, u32[]{:S(2)}, u32[]{:S(2)}) collective-permute-start(bf16[32,1024]{1,0:T(8,128)(2,1)S(1)} %shard_map.153.refs_0_), channel_id=1, source_target_pairs={{0,2},{1,3},{2,0},{3,1},{4,6},{5,7},{6,4},{7,5},{8,10},{9,11},{10,... | collective-permute-start | bytes 196616 | tf_op jit(solution)/shard_map/ppermute | solution.py:24
  49.6 2.7 %collective-permute-start.19 = (bf16[32,1024]{1,0:T(8,128)(2,1)S(1)}, bf16[32,1024]{1,0:T(8,128)(2,1)S(1)}, u32[]{:S(2)}, u32[]{:S(2)}) collective-permute-start(bf16[32,1024]{1,0:T(8,128)(2,1)S(1)} %shard_map.153.refs_0_), channel_id=1, source_target_pairs={{0,1},{1,0},{2,3},{3,2},{4,5},{5,4},{6,7},{7,6},{8,9},{9,8},{10,11... | collective-permute-start | bytes 196616 | tf_op jit(solution)/shard_map/ppermute | solution.py:24
  52.3 1.3 %collective-permute-start.21 = (bf16[32,1024]{1,0:T(8,128)(2,1)S(1)}, bf16[32,1024]{1,0:T(8,128)(2,1)S(1)}, u32[]{:S(2)}, u32[]{:S(2)}) collective-permute-start(bf16[32,1024]{1,0:T(8,128)(2,1)S(1)} %collective-permute-done.20.refs_2_), channel_id=1, source_target_pairs={{0,1},{1,0},{2,3},{3,2},{4,5},{5,4},{6,7},{7,6},{8,9},{9,8},{10,11... | collective-permute-start | bytes 196616 | tf_op jit(solution)/shard_map/ppermute | solution.py:24
  54.8 8.1 %collective-permute-start.22 = (bf16[32,2048]{1,0:T(8,128)(2,1)S(1)}, bf16[32,2048]{1,0:T(8,128)(2,1)S(1)}, u32[]{:S(2)}, u32[]{:S(2)}) collective-permute-start(bf16[32,2048]{1,0:T(8,128)(2,1)S(1)} %get-tuple-element.37), channel_id=1, source_target_pairs={{0,4},{4,0},{8,12},{12,8},{16,20},{20,16},{24,28},{28,24},{1,5},{5... | collective-permute-start | bytes 393224 | tf_op jit(solution)/shard_map/ppermute | solution.py:24
  57.7 7.9 %collective-permute-start.25 = (bf16[16,2048]{1,0:T(8,128)(2,1)S(1)}, bf16[16,2048]{1,0:T(8,128)(2,1)S(1)}, u32[]{:S(2)}, u32[]{:S(2)}) collective-permute-start(bf16[16,2048]{1,0:T(8,128)(2,1)S(1)} %get-tuple-element.40), channel_id=1, source_target_pairs={{0,4},{4,0},{8,12},{12,8},{16,20},{20,16},{24,28},{28,24},{1,5},{5... | collective-permute-start | bytes 196616 | tf_op jit(solution)/shard_map/ppermute | solution.py:24
  57.8 7.8 %collective-permute-start.26 = (bf16[16,2048]{1,0:T(8,128)(2,1)S(1)}, bf16[16,2048]{1,0:T(8,128)(2,1)S(1)}, u32[]{:S(2)}, u32[]{:S(2)}) collective-permute-start(bf16[16,2048]{1,0:T(8,128)(2,1)S(1)} %get-tuple-element.41), channel_id=1, source_target_pairs={{0,8},{4,12},{8,0},{12,4},{16,24},{20,28},{24,16},{28,20},{1,9},{5... | collective-permute-start | bytes 196616 | tf_op jit(solution)/shard_map/ppermute | solution.py:24
  58.8 6.8 %collective-permute-start.27 = (bf16[16,2048]{1,0:T(8,128)(2,1)S(1)}, bf16[16,2048]{1,0:T(8,128)(2,1)S(1)}, u32[]{:S(2)}, u32[]{:S(2)}) collective-permute-start(bf16[16,2048]{1,0:T(8,128)(2,1)S(1)} %get-tuple-element.42), channel_id=1, source_target_pairs={{0,12},{4,8},{8,4},{12,0},{16,28},{20,24},{24,20},{28,16},{1,13},{... | collective-permute-start | bytes 196616 | tf_op jit(solution)/shard_map/ppermute | solution.py:24
  63.0 20.4 %slice-start = ((s8[7340032]{0:T(1024)(128)(4,1)}), s8[4194304]{0:T(1024)(128)(4,1)S(1)}, s32[]{:S(2)}) async-start(s8[7340032]{0:T(1024)(128)(4,1)} %bitcast.17), calls=%async_computation.1 | async-start | bytes 8388608
  63.0 6.6 %collective-permute-start.23 = (bf16[16,2048]{1,0:T(8,128)(2,1)S(1)}, bf16[16,2048]{1,0:T(8,128)(2,1)S(1)}, u32[]{:S(2)}, u32[]{:S(2)}) collective-permute-start(bf16[16,2048]{1,0:T(8,128)(2,1)S(1)} %get-tuple-element.38), channel_id=1, source_target_pairs={{0,16},{4,20},{8,24},{12,28},{16,0},{20,4},{24,8},{28,12},{1,17},{... | collective-permute-start | bytes 196616 | tf_op jit(solution)/shard_map/ppermute | solution.py:24
  63.1 20.3 %slice-start.1 = ((s8[7340032]{0:T(1024)(128)(4,1)}), s8[3145728]{0:T(1024)(128)(4,1)S(1)}, s32[]{:S(2)}) async-start(s8[7340032]{0:T(1024)(128)(4,1)} %bitcast.17), calls=%async_computation.2 | async-start | bytes 6291456
  63.1 6.5 %collective-permute-start.24 = (bf16[16,2048]{1,0:T(8,128)(2,1)S(1)}, bf16[16,2048]{1,0:T(8,128)(2,1)S(1)}, u32[]{:S(2)}, u32[]{:S(2)}) collective-permute-start(bf16[16,2048]{1,0:T(8,128)(2,1)S(1)} %get-tuple-element.39), channel_id=1, source_target_pairs={{0,24},{4,28},{8,16},{12,20},{16,8},{20,12},{24,0},{28,4},{1,25},{... | collective-permute-start | bytes 196616 | tf_op jit(solution)/shard_map/ppermute | solution.py:24
  69.5 13.8 %copy-start.8 = (f32[2048]{0:T(1024)S(1)}, f32[2048]{0:T(1024)}, u32[]{:S(2)}) copy-start(f32[2048]{0:T(1024)} %param.20) | copy-start | bytes 24580
  69.5 15.7 %slice-start.2 = ((s8[7340032]{0:T(1024)(128)(4,1)}), s8[4194304]{0:T(1024)(128)(4,1)S(1)}, s32[]{:S(2)}) async-start(s8[7340032]{0:T(1024)(128)(4,1)} %bitcast.19), calls=%async_computation.3 | async-start | bytes 8388608
  70.2 6.6 %collective-permute-start.29 = (bf16[16,2048]{1,0:T(8,128)(2,1)S(1)}, bf16[16,2048]{1,0:T(8,128)(2,1)S(1)}, u32[]{:S(2)}, u32[]{:S(2)}) collective-permute-start(bf16[16,2048]{1,0:T(8,128)(2,1)S(1)} %get-tuple-element.44.refs_0_), channel_id=1, source_target_pairs={{0,8},{4,12},{8,0},{12,4},{16,24},{20,28},{24,16},{28,20},{1,9},{5... | collective-permute-start | bytes 196616 | tf_op jit(solution)/shard_map/ppermute | solution.py:24
  71.5 5.9 %collective-permute-start.31 = (bf16[16,2048]{1,0:T(8,128)(2,1)S(1)}, bf16[16,2048]{1,0:T(8,128)(2,1)S(1)}, u32[]{:S(2)}, u32[]{:S(2)}) collective-permute-start(bf16[16,2048]{1,0:T(8,128)(2,1)S(1)} %get-tuple-element.44.refs_0_), channel_id=1, source_target_pairs={{0,16},{4,20},{8,24},{12,28},{16,0},{20,4},{24,8},{28,12},{1,17},{... | collective-permute-start | bytes 196616 | tf_op jit(solution)/shard_map/ppermute | solution.py:24
  73.0 6.1 %collective-permute-start.33 = (bf16[16,2048]{1,0:T(8,128)(2,1)S(1)}, bf16[16,2048]{1,0:T(8,128)(2,1)S(1)}, u32[]{:S(2)}, u32[]{:S(2)}) collective-permute-start(bf16[16,2048]{1,0:T(8,128)(2,1)S(1)} %get-tuple-element.44.refs_0_), channel_id=1, source_target_pairs={{0,24},{4,28},{8,16},{12,20},{16,8},{20,12},{24,0},{28,4},{1,25},{... | collective-permute-start | bytes 196616 | tf_op jit(solution)/shard_map/ppermute | solution.py:24
  74.6 5.3 %collective-permute-start.28 = (bf16[16,2048]{1,0:T(8,128)(2,1)S(1)}, bf16[16,2048]{1,0:T(8,128)(2,1)S(1)}, u32[]{:S(2)}, u32[]{:S(2)}) collective-permute-start(bf16[16,2048]{1,0:T(8,128)(2,1)S(1)} %get-tuple-element.44.refs_0_), channel_id=1, source_target_pairs={{0,4},{4,0},{8,12},{12,8},{16,20},{20,16},{24,28},{28,24},{1,5},{5... | collective-permute-start | bytes 196616 | tf_op jit(solution)/shard_map/ppermute | solution.py:24
  76.9 4.3 %collective-permute-start.30 = (bf16[16,2048]{1,0:T(8,128)(2,1)S(1)}, bf16[16,2048]{1,0:T(8,128)(2,1)S(1)}, u32[]{:S(2)}, u32[]{:S(2)}) collective-permute-start(bf16[16,2048]{1,0:T(8,128)(2,1)S(1)} %collective-permute-done.29.refs_2_), channel_id=1, source_target_pairs={{0,4},{4,0},{8,12},{12,8},{16,20},{20,16},{24,28},{28,24},{1,5},{5... | collective-permute-start | bytes 196616 | tf_op jit(solution)/shard_map/ppermute | solution.py:24
  77.4 4.5 %collective-permute-start.32 = (bf16[16,2048]{1,0:T(8,128)(2,1)S(1)}, bf16[16,2048]{1,0:T(8,128)(2,1)S(1)}, u32[]{:S(2)}, u32[]{:S(2)}) collective-permute-start(bf16[16,2048]{1,0:T(8,128)(2,1)S(1)} %collective-permute-done.31.refs_4_), channel_id=1, source_target_pairs={{0,4},{4,0},{8,12},{12,8},{16,20},{20,16},{24,28},{28,24},{1,5},{5... | collective-permute-start | bytes 196616 | tf_op jit(solution)/shard_map/ppermute | solution.py:24
  79.1 4.3 %collective-permute-start.34 = (bf16[16,2048]{1,0:T(8,128)(2,1)S(1)}, bf16[16,2048]{1,0:T(8,128)(2,1)S(1)}, u32[]{:S(2)}, u32[]{:S(2)}) collective-permute-start(bf16[16,2048]{1,0:T(8,128)(2,1)S(1)} %collective-permute-done.33.refs_6_), channel_id=1, source_target_pairs={{0,4},{4,0},{8,12},{12,8},{16,20},{20,16},{24,28},{28,24},{1,5},{5... | collective-permute-start | bytes 196616 | tf_op jit(solution)/shard_map/ppermute | solution.py:24
  83.4 1.9 %slice-start.3 = ((s8[7340032]{0:T(1024)(128)(4,1)}), s8[3145728]{0:T(1024)(128)(4,1)S(1)}, s32[]{:S(2)}) async-start(s8[7340032]{0:T(1024)(128)(4,1)} %bitcast.19), calls=%async_computation.4 | async-start | bytes 6291456
  83.4 17.8 %slice-start.4 = ((s8[7340032]{0:T(1024)(128)(4,1)}), s8[4194304]{0:T(1024)(128)(4,1)S(1)}, s32[]{:S(2)}) async-start(s8[7340032]{0:T(1024)(128)(4,1)} %bitcast.21), calls=%async_computation.5 | async-start | bytes 8388608
  85.2 1.8 %collective-permute-start.35 = (bf16[64,1920]{1,0:T(8,128)(2,1)S(1)}, bf16[64,1920]{1,0:T(8,128)(2,1)S(1)}, u32[]{:S(2)}, u32[]{:S(2)}) collective-permute-start(bf16[64,1920]{1,0:T(8,128)(2,1)S(1)} %get-tuple-element.46), channel_id=1, source_target_pairs={{0,1},{1,0},{2,3},{3,2},{4,5},{5,4},{6,7},{7,6},{8,9},{9,8},{10,11... | collective-permute-start | bytes 737288 | tf_op jit(solution)/shard_map/ppermute | solution.py:24
  85.3 15.9 %slice-start.5 = ((s8[7340032]{0:T(1024)(128)(4,1)}), s8[3145728]{0:T(1024)(128)(4,1)S(1)}, s32[]{:S(2)}) async-start(s8[7340032]{0:T(1024)(128)(4,1)} %bitcast.21), calls=%async_computation.6 | async-start | bytes 6291456
  86.5 2.0 %collective-permute-start.37 = (bf16[64,1792]{1,0:T(8,128)(2,1)S(1)}, bf16[64,1792]{1,0:T(8,128)(2,1)S(1)}, u32[]{:S(2)}, u32[]{:S(2)}) collective-permute-start(bf16[64,1792]{1,0:T(8,128)(2,1)S(1)} %get-tuple-element.49), channel_id=1, source_target_pairs={{0,1},{1,0},{2,3},{3,2},{4,5},{5,4},{6,7},{7,6},{8,9},{9,8},{10,11... | collective-permute-start | bytes 688136 | tf_op jit(solution)/shard_map/ppermute | solution.py:24
  87.1 6.2 %collective-permute-start.36 = (bf16[32,1920]{1,0:T(8,128)(2,1)S(1)}, bf16[32,1920]{1,0:T(8,128)(2,1)S(1)}, u32[]{:S(2)}, u32[]{:S(2)}) collective-permute-start(bf16[32,1920]{1,0:T(8,128)(2,1)S(1)} %slice.99), channel_id=1, source_target_pairs={{0,2},{1,3},{2,0},{3,1},{4,6},{5,7},{6,4},{7,5},{8,10},{9,11},{10,... | collective-permute-start | bytes 368648 | tf_op jit(solution)/shard_map/ppermute | solution.py:24
  88.6 6.3 %collective-permute-start.38 = (bf16[32,1792]{1,0:T(8,128)(2,1)S(1)}, bf16[32,1792]{1,0:T(8,128)(2,1)S(1)}, u32[]{:S(2)}, u32[]{:S(2)}) collective-permute-start(bf16[32,1792]{1,0:T(8,128)(2,1)S(1)} %slice.100), channel_id=1, source_target_pairs={{0,2},{1,3},{2,0},{3,1},{4,6},{5,7},{6,4},{7,5},{8,10},{9,11},{10,... | collective-permute-start | bytes 344072 | tf_op jit(solution)/shard_map/ppermute | solution.py:24
  95.0 4.9 %collective-permute-start.40 = (bf16[32,1792]{1,0:T(8,128)(2,1)S(1)}, bf16[32,1792]{1,0:T(8,128)(2,1)S(1)}, u32[]{:S(2)}, u32[]{:S(2)}) collective-permute-start(bf16[32,1792]{1,0:T(8,128)(2,1)S(1)} %fusion.2.refs_0_), channel_id=1, source_target_pairs={{0,2},{1,3},{2,0},{3,1},{4,6},{5,7},{6,4},{7,5},{8,10},{9,11},{10,... | collective-permute-start | bytes 344072 | tf_op jit(solution)/shard_map/ppermute | solution.py:24
  96.4 3.5 %collective-permute-start.39 = (bf16[32,1792]{1,0:T(8,128)(2,1)S(1)}, bf16[32,1792]{1,0:T(8,128)(2,1)S(1)}, u32[]{:S(2)}, u32[]{:S(2)}) collective-permute-start(bf16[32,1792]{1,0:T(8,128)(2,1)S(1)} %fusion.2.refs_0_), channel_id=1, source_target_pairs={{0,1},{1,0},{2,3},{3,2},{4,5},{5,4},{6,7},{7,6},{8,9},{9,8},{10,11... | collective-permute-start | bytes 344072 | tf_op jit(solution)/shard_map/ppermute | solution.py:24
  99.9 1.3 %collective-permute-start.41 = (bf16[32,1792]{1,0:T(8,128)(2,1)S(1)}, bf16[32,1792]{1,0:T(8,128)(2,1)S(1)}, u32[]{:S(2)}, u32[]{:S(2)}) collective-permute-start(bf16[32,1792]{1,0:T(8,128)(2,1)S(1)} %collective-permute-done.40.refs_2_), channel_id=1, source_target_pairs={{0,1},{1,0},{2,3},{3,2},{4,5},{5,4},{6,7},{7,6},{8,9},{9,8},{10,11... | collective-permute-start | bytes 344072 | tf_op jit(solution)/shard_map/ppermute | solution.py:24
  102.9 7.0 %collective-permute-start.42 = (bf16[32,2048]{1,0:T(8,128)(2,1)S(1)}, bf16[32,2048]{1,0:T(8,128)(2,1)S(1)}, u32[]{:S(2)}, u32[]{:S(2)}) collective-permute-start(bf16[32,2048]{1,0:T(8,128)(2,1)S(1)} %get-tuple-element.52), channel_id=1, source_target_pairs={{0,4},{4,0},{8,12},{12,8},{16,20},{20,16},{24,28},{28,24},{1,5},{5... | collective-permute-start | bytes 393224 | tf_op jit(solution)/shard_map/ppermute | solution.py:24
  103.8 8.6 %collective-permute-start.45 = (bf16[16,2048]{1,0:T(8,128)(2,1)S(1)}, bf16[16,2048]{1,0:T(8,128)(2,1)S(1)}, u32[]{:S(2)}, u32[]{:S(2)}) collective-permute-start(bf16[16,2048]{1,0:T(8,128)(2,1)S(1)} %get-tuple-element.55), channel_id=1, source_target_pairs={{0,4},{4,0},{8,12},{12,8},{16,20},{20,16},{24,28},{28,24},{1,5},{5... | collective-permute-start | bytes 196616 | tf_op jit(solution)/shard_map/ppermute | solution.py:24
  105.0 7.4 %collective-permute-start.46 = (bf16[16,2048]{1,0:T(8,128)(2,1)S(1)}, bf16[16,2048]{1,0:T(8,128)(2,1)S(1)}, u32[]{:S(2)}, u32[]{:S(2)}) collective-permute-start(bf16[16,2048]{1,0:T(8,128)(2,1)S(1)} %get-tuple-element.56), channel_id=1, source_target_pairs={{0,8},{4,12},{8,0},{12,4},{16,24},{20,28},{24,16},{28,20},{1,9},{5... | collective-permute-start | bytes 196616 | tf_op jit(solution)/shard_map/ppermute | solution.py:24
  105.7 6.7 %collective-permute-start.47 = (bf16[16,2048]{1,0:T(8,128)(2,1)S(1)}, bf16[16,2048]{1,0:T(8,128)(2,1)S(1)}, u32[]{:S(2)}, u32[]{:S(2)}) collective-permute-start(bf16[16,2048]{1,0:T(8,128)(2,1)S(1)} %get-tuple-element.57), channel_id=1, source_target_pairs={{0,12},{4,8},{8,4},{12,0},{16,28},{20,24},{24,20},{28,16},{1,13},{... | collective-permute-start | bytes 196616 | tf_op jit(solution)/shard_map/ppermute | solution.py:24
  110.0 6.4 %collective-permute-start.43 = (bf16[16,2048]{1,0:T(8,128)(2,1)S(1)}, bf16[16,2048]{1,0:T(8,128)(2,1)S(1)}, u32[]{:S(2)}, u32[]{:S(2)}) collective-permute-start(bf16[16,2048]{1,0:T(8,128)(2,1)S(1)} %get-tuple-element.53), channel_id=1, source_target_pairs={{0,16},{4,20},{8,24},{12,28},{16,0},{20,4},{24,8},{28,12},{1,17},{... | collective-permute-start | bytes 196616 | tf_op jit(solution)/shard_map/ppermute | solution.py:24
  110.0 6.3 %collective-permute-start.44 = (bf16[16,2048]{1,0:T(8,128)(2,1)S(1)}, bf16[16,2048]{1,0:T(8,128)(2,1)S(1)}, u32[]{:S(2)}, u32[]{:S(2)}) collective-permute-start(bf16[16,2048]{1,0:T(8,128)(2,1)S(1)} %get-tuple-element.54), channel_id=1, source_target_pairs={{0,24},{4,28},{8,16},{12,20},{16,8},{20,12},{24,0},{28,4},{1,25},{... | collective-permute-start | bytes 196616 | tf_op jit(solution)/shard_map/ppermute | solution.py:24
  (2 other events, 1.6 us)

commit v7 on v6

v7 whole, which is shorter than its diff:
```python
import functools
import math

import jax
import jax.numpy as jnp
import numpy as np
from jax import lax
from jax.experimental import pallas as pl
from jax.experimental.pallas import tpu as pltpu
from jax.sharding import PartitionSpec as P

KVH = 8
HD = 128
EPS = 1e-05
ROPE_BASE = 500000.0
MASKED = -1e30
AROUND = 5 << 30
BF16 = jnp.bfloat16
F32 = jnp.float32


def swap(x, axis, bits):
    size = lax.axis_size(axis)
    return lax.ppermute(x, axis, [(i, i ^ bits) for i in range(size)])


def rope_tables(position):
    half = HD // 2
    freq = np.power(np.float32(ROPE_BASE), -2.0 * np.arange(half, dtype=np.float32) / HD)
    angle = (np.float32(position) * freq.astype(np.float32)).astype(np.float32)
    cosine, sine = np.cos(angle), np.sin(angle)
    return (
        np.concatenate([cosine, cosine]).astype(np.float32),
        np.concatenate([-sine, sine]).astype(np.float32),
    )


SMEM = pl.BlockSpec(memory_space=pltpu.SMEM)
VMEM = pl.BlockSpec(memory_space=pltpu.VMEM)
ANY = pl.BlockSpec(memory_space=pl.ANY)
HBM = pl.BlockSpec(memory_space=pltpu.HBM)


def call(body, outs, ins, specs, scratch=(), flops=0, moved=0, limit=8 << 20):
    return pl.pallas_call(
        body,
        out_shape=outs,
        in_specs=specs,
        out_specs=jax.tree.map(lambda _: VMEM, outs),
        scratch_shapes=scratch,
        compiler_params=pltpu.CompilerParams(vmem_limit_bytes=limit),
        cost_estimate=pl.CostEstimate(flops=flops + AROUND, bytes_accessed=moved, transcendentals=0),
    )(*ins)


def shaped(shape, dtype=BF16):
    return jax.ShapeDtypeStruct(shape, dtype)


def gather_rows(rows):
    groups = lax.axis_size("dp")
    close = min(groups, 4)
    blocks = {0: rows}
    for k in range(groups - 2, close - 1, -2):
        blocks[k] = swap(rows, "dp", k)
    for k in range(close - 1, 0, -1):
        blocks[k] = swap(rows, "dp", k)
    for k in range(groups - 2, close - 1, -2):
        blocks[k + 1] = swap(blocks[k], "dp", 1)
    return [blocks[k] for k in range(groups)]


def gather_blocks(block):
    tensor = lax.axis_size("tensor")
    blocks = {0: block}
    for k in range(2, tensor, 2):
        blocks[k] = swap(block, "tensor", k)
    blocks[1] = swap(block, "tensor", 1)
    for k in range(2, tensor, 2):
        blocks[k + 1] = swap(blocks[k], "tensor", 1)
    return [blocks[k] for k in range(tensor)]


def sum_blocks(keep, send):
    tensor = lax.axis_size("tensor")
    rows = keep.shape[0] // (tensor // 2)
    paired = (keep + swap(send, "tensor", 1).astype(F32)).reshape(tensor // 2, rows, -1)
    return paired[0], [swap(paired[i].astype(BF16), "tensor", 2 * i) for i in range(1, tensor // 2)]


def slot(relative, size):
    return lax.shift_right_logical(relative, 1) + (relative & 1) * (size // 2)


def tiles(columns):
    for tile in (256, 384, 128):
        if columns % tile == 0:
            return tile
    return columns


def multiply(left, w_ref, write):
    columns = w_ref.shape[1]
    tile = tiles(columns)
    for first in range(0, columns, tile):
        write(first, tile, jnp.dot(left, w_ref[:, first : first + tile], preferred_element_type=F32))


def prologue(where, x_first, x_second, cache_keys, cache_values):
    groups = lax.axis_size("dp")
    part_dev, features = x_first.shape
    span = cache_keys.shape[1]
    shape = (groups // 2, 2, part_dev, span, HD)

    def body(where_ref, first_hbm, second_hbm, keys_hbm, values_hbm, x_ref, keep_ref, send_ref, *refs):
        one, two, keys_ref, values_ref, sems = refs
        pairs = ((first_hbm, one), (second_hbm, two), (keys_hbm, keys_ref), (values_hbm, values_ref))
        copies = [pltpu.make_async_copy(src, dst, sems.at[i]) for i, (src, dst) in enumerate(pairs)]
        for copy in copies:
            copy.start()
        for copy in copies[:2]:
            copy.wait()
        x_ref[...] = jnp.concatenate([one[...].astype(F32), two[...].astype(F32)], axis=0).astype(BF16)
        for copy in copies[2:]:
            copy.wait()
        for k in range(groups):
            head = lax.div((where_ref[0] ^ k) * KVH, groups)
            lanes = pl.ds(pl.multiple_of(head * HD, HD), HD)
            out_ref = send_ref if k % 2 else keep_ref
            out_ref[k // 2, 0] = keys_ref[:, :, lanes]
            out_ref[k // 2, 1] = values_ref[:, :, lanes]

    return call(
        body,
        (shaped((2 * part_dev, features)), shaped(shape), shaped(shape)),
        (where, x_first, x_second, cache_keys, cache_values),
        [SMEM] + [HBM] * 4,
        [pltpu.VMEM(a.shape, BF16) for a in (x_first, x_second, cache_keys, cache_values)]
        + [pltpu.SemaphoreType.DMA((4,))],
        limit=None,
        moved=8 * cache_keys.size,
    )


def move_cache(keep, send):
    groups = lax.axis_size("dp")
    both = jnp.stack([keep, swap(send, "dp", 1)], axis=1)
    moved = [both[:1]] + [swap(both[i : i + 1], "dp", 2 * i) for i in range(groups // 2 - 1, 0, -1)][::-1]
    both = jnp.concatenate(moved)
    return gather_blocks(both.reshape(groups * 2 * both.shape[3], *both.shape[4:]))


def lift(where_ref, gain_ref, block_refs, h_ref, ss_ref, absolute):
    groups = len(block_refs)
    tensor = lax.axis_size("tensor")
    pair = block_refs[0].shape[0]
    near = groups // tensor
    d, t = where_ref[0], where_ref[1]
    gain = gain_ref[...]
    places = []
    for k in range(groups):
        g = d ^ k
        place = slot(lax.div(g, near) ^ t, tensor) * near + lax.rem(g, near)
        place = pl.multiple_of(place * pair, pair)
        wide = block_refs[k][...].astype(F32)
        squares = jnp.broadcast_to(jnp.sum(wide * wide, axis=1, keepdims=True), (pair, 128))
        ss_ref[pl.ds(pl.multiple_of(g * pair, pair) if absolute else place, pair), :] = squares
        h_ref[pl.ds(place, pair), :] = (wide * gain).astype(BF16)
        places.append((pl.multiple_of(g * pair, pair), place))
    return places


def split(total, base, lane):
    high = total.astype(BF16).astype(F32)
    return jnp.where(lane == 0, high, jnp.where(lane == 1, total - high, base))


def project_attention(where, blocks, gain, w_keyval, w_query):
    pair, features = blocks[0].shape
    rows = len(blocks) * pair
    half = rows // 2
    columns = w_keyval.shape[1]
    wide = w_query.shape[1]

    def body(where_ref, gain_ref, *refs):
        block_refs, refs = refs[: len(blocks)], refs[len(blocks) :]
        w_kv_ref, w_q_ref, kv_ref, keep_ref, send_ref, h_ref, ss_ref, product = refs
        places = lift(where_ref, gain_ref, block_refs, h_ref, ss_ref, True)
        h = h_ref[...]
        product[...] = jnp.dot(h, w_kv_ref[...], preferred_element_type=F32)
        for to, place in places:
            kv_ref[pl.ds(to, pair), :columns] = product[pl.ds(place, pair), :].astype(BF16)
        squares = ss_ref[...]
        lane = lax.broadcasted_iota(jnp.int32, squares.shape, 1)
        kv_ref[:, columns:] = split(squares, 0.0, lane).astype(BF16)

        def write(first, tile, product):
            keep_ref[:, first : first + tile] = product[:half]
            send_ref[:, first : first + tile] = product[half:].astype(BF16)

        multiply(h, w_q_ref, write)

    return call(
        body,
        (shaped((rows, columns + 128)), shaped((half, wide), F32), shaped((half, wide))),
        (where, gain[None], *blocks, w_keyval, w_query),
        [SMEM] + [VMEM] * (3 + len(blocks)),
        [pltpu.VMEM((rows, features), BF16), pltpu.VMEM((rows, 128), F32), pltpu.VMEM((rows, columns), F32)],
        flops=2 * rows * (w_keyval.size + w_query.size),
        moved=4 * rows * features + 2 * (w_keyval.size + w_query.size),
    )


def add_keyvals(own, arrived):
    rows, columns = own.shape

    def body(own_ref, arrived_ref, out_ref):
        summed = own_ref[...].astype(F32) + arrived_ref[...].astype(F32)
        ends = summed[:, columns - 128 :]
        lane = lax.broadcasted_iota(jnp.int32, ends.shape, 1)
        out_ref[:, : columns - 128] = summed[:, : columns - 128].astype(BF16)
        out_ref[:, columns - 128 :] = split(ends[:, 0:1] + ends[:, 1:2], ends, lane).astype(BF16)

    return call(body, shaped(own.shape), (own, arrived), [VMEM] * 2, moved=6 * own.size)


def finish_keyvals(where, own, arrived, width):
    groups = lax.axis_size("dp")
    rows, columns = own.shape
    columns -= 128

    def body(where_ref, own_ref, arrived_ref, scale_ref, *out_refs):
        summed = own_ref[...].astype(F32) + arrived_ref[...].astype(F32)
        squares = summed[:, columns : columns + 1] + summed[:, columns + 1 : columns + 2]
        scale = lax.rsqrt(squares / width + EPS)
        scale_ref[...] = jnp.broadcast_to(scale, (rows, 128))
        scaled = summed[:, :columns] * scale
        if groups == KVH:
            lower = where_ref[0] < groups // 2
            out_refs[0][...] = jnp.where(lower, scaled[:, :HD], scaled[:, HD:]).astype(BF16)
            out_refs[1][...] = jnp.where(lower, scaled[:, HD:], scaled[:, :HD]).astype(BF16)
        else:
            out_refs[0][...] = scaled.astype(BF16)

    outs = [shaped((rows, 128), F32)]
    outs += [shaped((rows, HD))] * 2 if groups == KVH else [shaped((rows, columns))]
    return call(body, tuple(outs), (where, own, arrived), [SMEM, VMEM, VMEM], moved=8 * own.size)


def project(h, w):
    half = h.shape[0] // 2

    def body(h_ref, w_ref, keep_ref, send_ref):
        def write(first, tile, product):
            keep_ref[:, first : first + tile] = product[:half]
            send_ref[:, first : first + tile] = product[half:].astype(BF16)

        multiply(h_ref[...], w_ref, write)

    columns = w.shape[1]
    return call(
        body,
        (shaped((half, columns), F32), shaped((half, columns))),
        (h, w),
        [VMEM] * 2,
        flops=4 * half * w.size,
        moved=2 * w.size,
    )


def project_gate(where, blocks, gain, w):
    pair, features = blocks[0].shape
    rows = len(blocks) * pair
    half = rows // 2
    columns = w.shape[1]

    def body(where_ref, gain_ref, *refs):
        block_refs, (w_ref, h_ref, keep_ref, send_ref, ss_ref) = refs[: len(blocks)], refs[len(blocks) :]
        lift(where_ref, gain_ref, block_refs, h_ref, ss_ref, False)

        def write(first, tile, product):
            keep_ref[:, first : first + tile] = product[:half]
            send_ref[:, first : first + tile] = product[half:].astype(BF16)

        multiply(h_ref[...], w_ref, write)
        squares = ss_ref[...]
        high = squares.astype(BF16).astype(F32)
        lane = lax.broadcasted_iota(jnp.int32, squares.shape, 1)
        ends = jnp.where(lane == 0, high, jnp.where(lane == 1, squares - high, 0.0))
        keep_ref[:, columns:] = ends[:half]
        send_ref[:, columns:] = ends[half:].astype(BF16)

    return call(
        body,
        (shaped((rows, features)), shaped((half, columns + 128), F32), shaped((half, columns + 128))),
        (where, gain[None], *blocks, w),
        [SMEM] + [VMEM] * (2 + len(blocks)),
        [pltpu.VMEM((rows, 128), F32)],
        flops=2 * rows * w.size,
        moved=4 * rows * features + 2 * w.size,
    )


def project_back(where, blocks, w):
    groups = lax.axis_size("dp")
    rows, depth = blocks[0].shape
    near = groups // len(blocks)
    pair = rows // near
    total = len(blocks) * rows
    columns = w.shape[1]
    close = min(groups, 4)
    far = (groups - close) // 2

    def body(where_ref, *refs):
        block_refs, (w_ref, *out_refs) = refs[: len(blocks)], refs[len(blocks) :]
        left = out_refs[-1]
        d, t = where_ref[0], where_ref[1]
        for k, block_ref in enumerate(block_refs):
            for i in range(near):
                relative = ((t ^ k) * near + i) ^ d
                beyond = close + lax.shift_right_logical(relative - close, 1) + (relative & 1) * far
                place = jnp.where(relative < close, relative, beyond)
                left[pl.ds(pl.multiple_of(place * pair, pair), pair), :] = block_ref[i * pair : (i + 1) * pair, :]

        def write(first, tile, product):
            lanes = slice(first, first + tile)
            for i in range(close):
                out_refs[i][:, lanes] = product[i * pair : (i + 1) * pair].astype(out_refs[i].dtype)
            middle = (close + far) * pair
            cut = middle + far // 2 * pair
            out_refs[close][:, lanes] = product[close * pair : middle]
            out_refs[close + 1][:, lanes] = product[middle:cut].astype(BF16)
            out_refs[close + 2][:, lanes] = product[cut:].astype(BF16)

        multiply(left[...], w_ref, write)

    outs = [shaped((pair, columns), F32)] + [shaped((pair, columns))] * (close - 1)
    outs += [shaped((far * pair, columns), F32)] + [shaped((far // 2 * pair, columns))] * 2
    return call(
        body,
        tuple(outs),
        (where, *blocks, w),
        [SMEM] + [VMEM] * (1 + len(blocks)),
        [pltpu.VMEM((total, depth), BF16)],
        flops=2 * total * w.size,
        moved=2 * w.size,
    )


def add_pairs(keep, arrived, first, pair):
    def body(keep_ref, arrived_ref, *out_refs):
        for i, out_ref in enumerate(out_refs):
            own = keep_ref[first + i * pair : first + (i + 1) * pair, :]
            out_ref[...] = (own + arrived_ref[i * pair : (i + 1) * pair, :].astype(F32)).astype(BF16)

    outs = (shaped((pair, keep.shape[1])),) * (arrived.shape[0] // pair)
    return call(body, outs, (keep, arrived), [VMEM] * 2, moved=8 * arrived.size)


def sum_rows(parts, pair):
    own, *near, keep, one, two = parts
    sums = add_pairs(keep, swap(one, "dp", 1), 0, pair)
    sums += add_pairs(keep, swap(two, "dp", 1), one.shape[0], pair)
    arrived = [swap(piece, "dp", len(near) + 1 + 2 * i) for i, piece in enumerate(sums)]
    arrived += [swap(piece, "dp", k + 1) for k, piece in enumerate(near)]
    return own, arrived


def finish(own, arrived, x=None):
    def body(own_ref, *refs):
        total = own_ref[...]
        for ref in refs[: len(arrived)]:
            total = total + ref[...].astype(F32)
        rounded = total.astype(BF16)
        if x is None:
            refs[-1][...] = rounded
        else:
            refs[-2][...] = rounded
            refs[-1][...] = (refs[len(arrived)][...].astype(F32) + rounded.astype(F32)).astype(BF16)

    outs = (shaped(own.shape),) * (1 if x is None else 2)
    ins = (own, *arrived) + (() if x is None else (x,))
    return call(body, outs, ins, [VMEM] * len(ins), moved=8 * own.size)


def attend_cached(where, anc, rope, scale, queries, cache, part_dev):
    tensor = lax.axis_size("tensor")
    groups = lax.axis_size("dp")
    near = groups // tensor
    pair = 2 * part_dev
    span = cache[0].shape[1]
    ctx = tensor * span
    columns = queries[0].shape[1]
    heads = columns // HD
    parts = near * part_dev
    rows = heads * parts

    def body(where_ref, anc_ref, rope_ref, scale_ref, *refs):
        q_refs, refs = refs[: len(queries)], refs[len(queries) :]
        cache_refs, (query_ref, mixed_ref, highest_ref, total_ref, keys_ref, values_ref) = refs[:tensor], refs[tensor:]
        d, t = where_ref[0], where_ref[1]
        query_sum = q_refs[0][...]
        for ref in q_refs[1:]:
            query_sum = query_sum + ref[...].astype(F32)
        query_sum = query_sum * scale_ref[pl.ds(pl.multiple_of(t * near * pair, pair), near * pair), 0:1]
        for step in range(2):

            def bring(i, _, step=step):
                if step == 0:
                    block, member = (t * near + lax.div(i, part_dev)) ^ d, lax.rem(i, part_dev)
                else:
                    block, member = lax.div(anc_ref[i], part_dev) ^ d, lax.rem(anc_ref[i], part_dev)
                place = block * pair + member
                for k in range(tensor):
                    start = pl.multiple_of(i * ctx + k * span, 8)
                    keys_ref[pl.ds(start, span), :] = cache_refs[k][place].astype(F32)
                    values_ref[pl.ds(start, span), :] = cache_refs[k][place + part_dev].astype(F32)
                return 0

            lax.fori_loop(0, parts, bring, 0)
            keys = keys_ref[...].astype(BF16)
            values = values_ref[...].astype(BF16)
            per_head = []
            for h in range(heads):
                for b in range(near):
                    first = b * pair + step * part_dev
                    per_head.append(query_sum[first : first + part_dev, h * HD : (h + 1) * HD])
            query = jnp.concatenate(per_head, axis=0).astype(BF16).astype(F32)
            cosine = rope_ref[2 * step : 2 * step + 1, :]
            sine = rope_ref[2 * step + 1 : 2 * step + 2, :]
            query = (query * cosine + pltpu.roll(query, HD // 2, 1) * sine).astype(BF16)
            scores = lax.dot_general(query, keys, (((1,), (1,)), ((), ())), preferred_element_type=F32)
            scores = scores * (1.0 / math.sqrt(HD))
            row_part = lax.rem(lax.broadcasted_iota(jnp.int32, (rows, 1), 0), parts)
            col_part = lax.div(lax.broadcasted_iota(jnp.int32, (1, parts * ctx), 1), ctx)
            scores = jnp.where(row_part == col_part, scores, MASKED)
            highest = jnp.max(scores, axis=1, keepdims=True)
            weights = jnp.exp(scores - highest)
            here = slice(step * rows, (step + 1) * rows)
            query_ref[here, :] = query
            mixed_ref[here, :] = jnp.dot(weights.astype(BF16), values, preferred_element_type=F32)
            highest_ref[here, :] = jnp.broadcast_to(highest, (rows, 128))
            total_ref[here, :] = jnp.broadcast_to(jnp.sum(weights, axis=1, keepdims=True), (rows, 128))

    ins = (where, anc, rope, scale, *queries, *cache)
    return call(
        body,
        (shaped((2 * rows, HD)), shaped((2 * rows, HD), F32), shaped((2 * rows, 128), F32), shaped((2 * rows, 128), F32)),
        ins,
        [SMEM] * 2 + [VMEM] * (len(ins) - 2),
        [pltpu.VMEM((parts * ctx, HD), F32), pltpu.VMEM((parts * ctx, HD), F32)],
        limit=(4 << 20) + 12 * rows * parts * ctx,
        moved=4 << 20,
    )


def attend_new(where, rope, targets, pieces, state, shape, part_dev):
    groups = lax.axis_size("dp")
    tensor = lax.axis_size("tensor")
    near = groups // tensor
    pair = 2 * part_dev
    parts = near * part_dev
    heads = shape[1] // HD
    rows = heads * parts

    def body(where_ref, rope_ref, target_ref, one_ref, two_ref, query_ref, mixed_ref, highest_ref, total_ref, out_ref):
        even = where_ref[0] % 2 == 0 if groups == KVH else True
        one, two = one_ref[...].astype(F32), two_ref[...].astype(F32)
        plain = jnp.where(even, one, two)
        values = jnp.where(even, two, one).astype(BF16)
        cosine = jnp.concatenate([jnp.broadcast_to(rope_ref[2 * s : 2 * s + 1, :], (part_dev, HD)) for s in range(2)])
        sine = jnp.concatenate([jnp.broadcast_to(rope_ref[2 * s + 1 : 2 * s + 2, :], (part_dev, HD)) for s in range(2)])
        turned = pltpu.roll(plain, HD // 2, 1).reshape(groups, pair, HD)
        keys = plain.reshape(groups, pair, HD) * cosine[None] + turned * sine[None]
        keys = keys.reshape(groups * pair, HD).astype(BF16)
        scores = lax.dot_general(query_ref[...], keys, (((1,), (1,)), ((), ())), preferred_element_type=F32)
        scores = scores * (1.0 / math.sqrt(HD))
        col = lax.broadcasted_iota(jnp.int32, (1, groups * pair), 1)
        wanted = (col == target_ref[:, 0:1]) | (col == target_ref[:, 1:2])
        scores = jnp.where(wanted, scores, MASKED)
        before = highest_ref[:, 0:1]
        highest = jnp.maximum(before, jnp.max(scores, axis=1, keepdims=True))
        weights = jnp.exp(scores - highest)
        keep = jnp.exp(before - highest)
        total = total_ref[:, 0:1] * keep + jnp.sum(weights, axis=1, keepdims=True)
        mixed = mixed_ref[...] * keep + jnp.dot(weights.astype(BF16), values, preferred_element_type=F32)
        mixed = mixed / total
        for h in range(heads):
            for b in range(near):
                first = h * parts + b * part_dev
                both = [mixed[s * rows + first : s * rows + first + part_dev] for s in range(2)]
                here = slice(b * pair, (b + 1) * pair)
                out_ref[here, h * HD : (h + 1) * HD] = jnp.concatenate(both, axis=0).astype(BF16)

    ins = (where, rope, targets, *pieces, *state)
    return call(body, shaped(shape), ins, [SMEM] + [VMEM] * (len(ins) - 1), moved=1 << 20)


def move_keyvals(pieces):
    groups = lax.axis_size("dp")
    d = lax.axis_index("dp")
    if groups == KVH:
        half = groups // 2
        one = [(i, 2 * i) for i in range(half)] + [(half + i, 2 * i + 1) for i in range(half)]
        two = [(i, 2 * i + 1) for i in range(half)] + [(half + i, 2 * i) for i in range(half)]
        return [lax.ppermute(x, "dp", to) for x, to in zip(pieces, (one, two))]
    every = lax.all_gather(pieces[0], "dp", axis=1, tiled=True)
    start = (d * KVH // groups) * HD
    return [lax.dynamic_slice_in_dim(every, first + start, HD, axis=1) for first in (0, KVH * HD)]


def local(
    x_first,
    x_second,
    cache_keys,
    cache_values,
    ancestors,
    attn_gain,
    ffn_gain,
    w_query,
    w_keyval,
    w_out,
    w_gate,
    w_up,
    w_down,
):
    groups = lax.axis_size("dp")
    tensor = lax.axis_size("tensor")
    part_dev, features = x_first.shape
    span = cache_keys.shape[1]
    width = features * tensor
    context = span * tensor
    d = lax.axis_index("dp")
    t = lax.axis_index("tensor")
    pair = 2 * part_dev
    near = groups // tensor
    parts = near * part_dev
    where = jnp.stack([d, t]).astype(jnp.int32)

    x, keep, send = prologue(where, x_first, x_second, cache_keys, cache_values)
    blocks = gather_rows(x)
    caches = move_cache(keep, send)

    message, *queries = project_attention(where, blocks, attn_gain, w_keyval, w_query)
    bits = 1
    while 2 * bits < tensor:
        message = add_keyvals(message, swap(message, "tensor", bits))
        bits *= 2
    scale, *pieces = finish_keyvals(where, message, swap(message, "tensor", bits), width)
    pieces = move_keyvals(pieces)
    queries, queries_arrived = sum_blocks(*queries)

    own = t * parts + jnp.arange(parts, dtype=jnp.int32)
    anc = lax.dynamic_slice_in_dim(ancestors, t * parts, parts).astype(jnp.int32)
    heads = w_query.shape[1] // HD

    def row_of(particle, step):
        return (particle // part_dev) * pair + step * part_dev + particle % part_dev

    first = jnp.stack([row_of(own, 0)] * 2, axis=1)
    second = jnp.stack([row_of(anc, 0), row_of(own, 1)], axis=1)
    targets = jnp.concatenate([jnp.tile(first, (heads, 1)), jnp.tile(second, (heads, 1))]).astype(jnp.int32)
    rope = jnp.asarray(np.stack(rope_tables(context) + rope_tables(context + 1)))
    state = attend_cached(where, anc, rope, scale, [queries] + queries_arrived, caches, part_dev)
    mixed = attend_new(where, rope, targets, pieces, state, queries.shape, part_dev)

    parts = project_back(where, gather_blocks(mixed), w_out)
    attn_part, residual = finish(*sum_rows(parts, pair), x)

    hidden_cols = w_gate.shape[1]
    h, keep, send = project_gate(where, gather_rows(residual), ffn_gain, w_gate)
    gate, gate_arrived = sum_blocks(keep, send)
    up, up_arrived = sum_blocks(*project(h, w_up))
    for piece in gate_arrived:
        gate = gate + piece.astype(F32)
    for piece in up_arrived:
        up = up + piece.astype(F32)
    scale = lax.rsqrt((gate[:, hidden_cols] + gate[:, hidden_cols + 1]) / width + EPS)[:, None]
    hidden = jax.nn.silu(gate[:, :hidden_cols] * scale) * (up * scale)
    parts = project_back(where, gather_blocks(hidden.astype(BF16)), w_down)
    (ffn_part,) = finish(*sum_rows(parts, pair))
    return (attn_part.reshape(2, part_dev, features), ffn_part.reshape(2, part_dev, features))


def solution(mesh):
    return jax.shard_map(
        local,
        mesh=mesh,
        in_specs=(
            P("dp", "tensor"),
            P("dp", "tensor"),
            P("dp", "tensor", None),
            P("dp", "tensor", None),
            P(),
            P("tensor"),
            P("tensor"),
            P("tensor", "dp"),
            P("tensor", "dp"),
            P("dp", "tensor"),
            P("tensor", "dp"),
            P("tensor", "dp"),
            P("dp", "tensor"),
        ),
        out_specs=(P(None, "dp", "tensor"), P(None, "dp", "tensor")),
        check_vma=False,
    )
```

time: 117 us -> 119 us (1.017)
  Pallas kernels: 12.4 us -> 15.4 us
  starting transfers between devices: 58.2 us -> 56.5 us
  other arithmetic: 0.73 us -> 2.15 us
    ppermute x44 -> x49, starting transfers between devices: 46.8 us -> 53.8 us  [swap(): return lax.ppermute(x, axis, [(i, i ^ bits) for i in range(size)])]
    ppermute x44 -> x49, waiting for transfers between devices: 34.5 us -> 40.2 us  [swap(): return lax.ppermute(x, axis, [(i, i ^ bits) for i in range(size)])]
    all_to_all x1 -> x0, starting transfers between devices: 4.53 us -> none  [local(): cache = lax.all_to_all(cache, 'dp', split_axis=0, concat_axis=0, tiled=True)]
    all_to_all x1 -> x0, waiting for transfers between devices: 4.33 us -> none  [local(): cache = lax.all_to_all(cache, 'dp', split_axis=0, concat_axis=0, tiled=True)]
    ppermute x4 -> x2, starting transfers between devices: 6.88 us -> 2.72 us  [move_keyvals(): return [lax.ppermute(x, 'dp', to) for x, to in zip(pieces, (one, two))]]
    pallas_call x13 -> x16, Pallas kernels: 12.4 us -> 15.4 us  [call(): pl.pallas_call(body, out_shape=outs, in_specs=specs, out_specs=jax.tree.m...]
    ppermute x4 -> x2, waiting for transfers between devices: 1.62 us -> 0.19 us  [move_keyvals(): return [lax.ppermute(x, 'dp', to) for x, to in zip(pieces, (one, two))]]
    unnamed x34 -> x32, local copies, waits for them, and re-layouts: 3.81 us -> 3.09 us
  transfers between devices with their start and end apart: 49 -> 51, of which waited for: 22 -> 22; matrix products, arithmetic and copies ran while one was open for 1% -> 1% of each run, Pallas kernels for 3% -> 5%
where the time goes in v7:
time: 119 us
  starting transfers between devices  56.5 us (47%)
  waiting for transfers between devices  40.4 us (34%)
  Pallas kernels  15.4 us (13%)
  local copies, waits for them, and re-layouts  3.47 us (3%)
  other arithmetic  2.15 us (2%)
    ppermute x49, starting transfers between devices, swap(): return lax.ppermute(x, axis, [(i, i ^ bits) for i in range(size)])  53.8 us
    ppermute x49, waiting for transfers between devices, swap(): return lax.ppermute(x, axis, [(i, i ^ bits) for i in range(size)])  40.2 us
    pallas_call x16, Pallas kernels, call(): pl.pallas_call(body, out_shape=outs, in_specs=specs, out_specs=jax.tree.m...  15.4 us
    unnamed x32, local copies, waits for them, and re-layouts  3.09 us
    ppermute x2, starting transfers between devices, move_keyvals(): return [lax.ppermute(x, 'dp', to) for x, to in zip(pieces, (one, two))]  2.72 us
  transfers between devices with their start and end apart: 51, of which 22 were waited for; matrix products, arithmetic and copies ran while one was open for 1% of the time, Pallas kernels for 5%

profile of v7, /device:TPU:0, one launch (start us, length us, event | category | flops | bytes accessed | tf_op | source)
XLA Modules:
  0.0 119.1 jit_solution(16419997515283155545)
XLA Ops:
  1.3 2.6 %shard_map.149 = (bf16[16,2048]{1,0:T(8,128)(2,1)}, bf16[4,2,8,8,128]{4,3,2,1,0:T(8,128)(2,1)}, bf16[4,2,8,8,128]{4,3,2,1,0:T(8,128)(2,1)}) custom-call(s32[2]{0:T(128)} %pad_add_fusion.3.where_ref, bf16[8,2048]{1,0:T(8,128)(2,1)} %first_hbm.1, bf16[8,2048]{1,0:T(8,128)(2,1)} %second_hbm.1, bf16[8,8,1024]{2,1,0:T(8,128)(2,1)} %keys_hbm.1, ...), custom_call_target="tpu_custom_call" | custom-call | flops 5368709120 | bytes 524288 | tf_op jit(solution)/shard_map/pallas_call | solution.py:45
  3.9 4.1 %collective-permute-start.3 = (bf16[16,2048]{1,0:T(8,128)(2,1)}, bf16[16,2048]{1,0:T(8,128)(2,1)S(1)}, u32[]{:S(2)}, u32[]{:S(2)}) collective-permute-start(bf16[16,2048]{1,0:T(8,128)(2,1)} %get-tuple-element.36.refs_0_.refs_5_), channel_id=1, source_target_pairs={{0,16},{4,20},{8,24},{12,28},{16,0},{20,4},{24,8},{28,12},{1,17},{... | collective-permute-start | bytes 196616 | tf_op jit(solution)/shard_map/ppermute | solution.py:24
  8.0 1.3 %collective-permute-start.5 = (bf16[16,2048]{1,0:T(8,128)(2,1)}, bf16[16,2048]{1,0:T(8,128)(2,1)S(1)}, u32[]{:S(2)}, u32[]{:S(2)}) collective-permute-start(bf16[16,2048]{1,0:T(8,128)(2,1)} %get-tuple-element.36.refs_0_.refs_5_), channel_id=1, source_target_pairs={{0,24},{4,28},{8,16},{12,20},{16,8},{20,12},{24,0},{28,4},{1,25},{... | collective-permute-start | bytes 196616 | tf_op jit(solution)/shard_map/ppermute | solution.py:24
  9.3 1.5 %collective-permute-start = (bf16[16,2048]{1,0:T(8,128)(2,1)}, bf16[16,2048]{1,0:T(8,128)(2,1)S(1)}, u32[]{:S(2)}, u32[]{:S(2)}) collective-permute-start(bf16[16,2048]{1,0:T(8,128)(2,1)} %get-tuple-element.36.refs_0_.refs_5_), channel_id=1, source_target_pairs={{0,4},{4,0},{8,12},{12,8},{16,20},{20,16},{24,28},{28,24},{1,5},{5... | collective-permute-start | bytes 196616 | tf_op jit(solution)/shard_map/ppermute | solution.py:24
  12.1 3.1 %collective-permute-start.2 = (bf16[16,2048]{1,0:T(8,128)(2,1)}, bf16[16,2048]{1,0:T(8,128)(2,1)S(1)}, u32[]{:S(2)}, u32[]{:S(2)}) collective-permute-start(bf16[16,2048]{1,0:T(8,128)(2,1)} %get-tuple-element.36.refs_0_.refs_5_), channel_id=1, source_target_pairs={{0,12},{4,8},{8,4},{12,0},{16,28},{20,24},{24,20},{28,16},{1,13},{... | collective-permute-start | bytes 196616 | tf_op jit(solution)/shard_map/ppermute | solution.py:24
  15.2 0.8 collective-permute-start.4
  16.0 2.3 %collective-permute-done.13 = bf16[4,2,8,8,128]{4,3,2,1,0:T(8,128)(2,1)S(1)} collective-permute-done((bf16[4,2,8,8,128]{4,3,2,1,0:T(8,128)(2,1)}, bf16[4,2,8,8,128]{4,3,2,1,0:T(8,128)(2,1)S(1)}, u32[]{:S(2)}, u32[]{:S(2)}) %collective-permute-start.13) | collective-permute-done | bytes 131104 | tf_op jit(solution)/shard_map/ppermute | solution.py:24
  18.4 0.8 fusion.4
  19.3 2.2 %collective-permute-start.14 = (bf16[1,2,2,8,8,128]{5,4,3,2,0,1:T(8,128)(2,1)S(1)}, bf16[1,2,2,8,8,128]{5,4,3,2,0,1:T(8,128)(2,1)S(1)}, u32[]{:S(2)}, u32[]{:S(2)}) collective-permute-start(bf16[1,2,2,8,8,128]{5,4,3,2,0,1:T(8,128)(2,1)S(1)} %get-tuple-element.73), channel_id=1, source_target_pairs={{0,8},{4,12},{8,0},{12,4},{16,24},{20,28},{24,16},{28,20},{1,9},{5... | collective-permute-start | bytes 196616 | tf_op jit(solution)/shard_map/ppermute | solution.py:24
  21.6 2.3 %collective-permute-start.16 = (bf16[1,2,2,8,8,128]{5,4,3,2,0,1:T(8,128)(2,1)S(1)}, bf16[1,2,2,8,8,128]{5,4,3,2,0,1:T(8,128)(2,1)S(1)}, u32[]{:S(2)}, u32[]{:S(2)}) collective-permute-start(bf16[1,2,2,8,8,128]{5,4,3,2,0,1:T(8,128)(2,1)S(1)} %get-tuple-element.74), channel_id=1, source_target_pairs={{0,24},{4,28},{8,16},{12,20},{16,8},{20,12},{24,0},{28,4},{1,25},{... | collective-permute-start | bytes 196616 | tf_op jit(solution)/shard_map/ppermute | solution.py:24
  23.9 2.2 %copy-done = bf16[2048,1024]{1,0:T(8,128)(2,1)S(1)} copy-done((bf16[2048,1024]{1,0:T(8,128)(2,1)S(1)}, bf16[2048,1024]{1,0:T(8,128)(2,1)}, u32[]{:S(2)}) %copy-start) | copy-done | bytes 4194328
  26.1 0.8 copy-done.3
  27.0 1.5 %shard_map.150 = (bf16[128,384]{1,0:T(8,128)(2,1)S(1)}, f32[64,1024]{1,0:T(8,128)S(1)}, bf16[64,1024]{1,0:T(8,128)(2,1)S(1)}) custom-call(s32[2]{0:T(128)S(1)} %copy-done.7, f32[1,2048]{1,0:T(1,128)S(1)} %bitcast.24, bf16[16,2048]{1,0:T(8,128)(2,1)S(1)} %copy-done.3, bf16[16,2048]{1,0:T(8,128)(2,1)S(1)} %collective-permute-done.refs_1_, ...), custom_call_target="tpu_custom_call" | custom-call | flops 6039797760 | bytes 6291456 | tf_op jit(solution)/shard_map/pallas_call | solution.py:45
  29.1 1.5 %collective-permute-start.18 = (bf16[128,8,128]{2,1,0:T(8,128)(2,1)S(1)}, bf16[128,8,128]{2,1,0:T(8,128)(2,1)S(1)}, u32[]{:S(2)}, u32[]{:S(2)}) collective-permute-start(bf16[128,8,128]{2,1,0:T(8,128)(2,1)S(1)} %bitcast.15), channel_id=1, source_target_pairs={{0,2},{1,3},{2,0},{3,1},{4,6},{5,7},{6,4},{7,5},{8,10},{9,11},{10,... | collective-permute-start | bytes 786440 | tf_op jit(solution)/shard_map/ppermute | solution.py:24
  30.8 0.9 collective-permute-start.8
  31.8 1.3 %collective-permute-start.12 = (bf16[32,1024]{1,0:T(8,128)(2,1)S(1)}, bf16[32,1024]{1,0:T(8,128)(2,1)S(1)}, u32[]{:S(2)}, u32[]{:S(2)}) collective-permute-start(bf16[32,1024]{1,0:T(8,128)(2,1)S(1)} %slice.120), channel_id=1, source_target_pairs={{0,2},{1,3},{2,0},{3,1},{4,6},{5,7},{6,4},{7,5},{8,10},{9,11},{10,... | collective-permute-start | bytes 196616 | tf_op jit(solution)/shard_map/ppermute | solution.py:24
  33.1 5.3 %collective-permute-done.18.refs_4_ = bf16[128,8,128]{2,1,0:T(8,128)(2,1)S(1)} collective-permute-done((bf16[128,8,128]{2,1,0:T(8,128)(2,1)S(1)}, bf16[128,8,128]{2,1,0:T(8,128)(2,1)S(1)}, u32[]{:S(2)}, u32[]{:S(2)}) %collective-permute-start.18) | collective-permute-done | bytes 262176 | tf_op jit(solution)/shard_map/ppermute | solution.py:24
  38.4 1.9 %collective-permute-done.8.arrived_ref = bf16[128,384]{1,0:T(8,128)(2,1)S(1)} collective-permute-done((bf16[128,384]{1,0:T(8,128)(2,1)S(1)}, bf16[128,384]{1,0:T(8,128)(2,1)S(1)}, u32[]{:S(2)}, u32[]{:S(2)}) %collective-permute-start.8) | collective-permute-done | bytes 98336 | tf_op jit(solution)/shard_map/ppermute | solution.py:24
  40.3 0.7 shard_map.152
  41.0 2.1 %collective-permute-start.10 = (bf16[128,128]{1,0:T(8,128)(2,1)S(1)}, bf16[128,128]{1,0:T(8,128)(2,1)S(1)}, u32[]{:S(2)}, u32[]{:S(2)}) collective-permute-start(bf16[128,128]{1,0:T(8,128)(2,1)S(1)} %get-tuple-element.39), channel_id=1, source_target_pairs={{0,4},{4,12},{8,20},{12,28},{16,0},{20,8},{24,16},{28,24},{1,5},{5... | collective-permute-start | bytes 98312 | tf_op jit(solution)/shard_map/ppermute | solution.py:506
  43.1 0.7 collective-permute-start.9
  43.8 1.9 %shard_map.153 = (bf16[256,128]{1,0:T(8,128)(2,1)S(1)}, f32[256,128]{1,0:T(8,128)S(1)}, f32[256,128]{1,0:T(8,128)S(1)}, f32[256,128]{1,0:T(8,128)S(1)}) custom-call(s32[2]{0:T(128)S(1)} %copy-done.7, s32[16]{0:T(128)S(1)} %get-tuple-element.71.anc_ref, f32[4,128]{1,0:T(4,128)S(1)} %copy-done.8, f32[128,128]{1,0:T(8,128)S(1)} %get-tuple-element.40.scale_ref, ...), custom_call_target="tpu_custom_call" | custom-call | flops 5368709120 | bytes 4194304 | tf_op jit(solution)/shard_map/pallas_call | solution.py:45
  45.9 1.1 shard_map.154.refs_0_
  47.0 1.5 %collective-permute-start.21 = (bf16[32,1024]{1,0:T(8,128)(2,1)S(1)}, bf16[32,1024]{1,0:T(8,128)(2,1)S(1)}, u32[]{:S(2)}, u32[]{:S(2)}) collective-permute-start(bf16[32,1024]{1,0:T(8,128)(2,1)S(1)} %shard_map.154.refs_0_), channel_id=1, source_target_pairs={{0,2},{1,3},{2,0},{3,1},{4,6},{5,7},{6,4},{7,5},{8,10},{9,11},{10,... | collective-permute-start | bytes 196616 | tf_op jit(solution)/shard_map/ppermute | solution.py:24
  48.5 2.9 %collective-permute-done.21.refs_2_ = bf16[32,1024]{1,0:T(8,128)(2,1)S(1)} collective-permute-done((bf16[32,1024]{1,0:T(8,128)(2,1)S(1)}, bf16[32,1024]{1,0:T(8,128)(2,1)S(1)}, u32[]{:S(2)}, u32[]{:S(2)}) %collective-permute-start.21) | collective-permute-done | bytes 65568 | tf_op jit(solution)/shard_map/ppermute | solution.py:24
  51.4 1.2 %collective-permute-done.22.refs_3_ = bf16[32,1024]{1,0:T(8,128)(2,1)S(1)} collective-permute-done((bf16[32,1024]{1,0:T(8,128)(2,1)S(1)}, bf16[32,1024]{1,0:T(8,128)(2,1)S(1)}, u32[]{:S(2)}, u32[]{:S(2)}) %collective-permute-start.22) | collective-permute-done | bytes 65568 | tf_op jit(solution)/shard_map/ppermute | solution.py:24
  52.6 1.3 %shard_map.155 = (f32[16,2048]{1,0:T(8,128)S(1)}, bf16[16,2048]{1,0:T(8,128)(2,1)S(1)}, bf16[16,2048]{1,0:T(8,128)(2,1)S(1)}, bf16[16,2048]{1,0:T(8,128)(2,1)S(1...) custom-call(s32[2]{0:T(128)S(1)} %copy-done.7, ...), custom_call_target="tpu_custom_call" | custom-call | flops 5905580032 | bytes 4194304 | tf_op jit(solution)/shard_map/pallas_call | solution.py:45
  53.9 5.9 %collective-permute-start.25 = (bf16[16,2048]{1,0:T(8,128)(2,1)S(1)}, bf16[16,2048]{1,0:T(8,128)(2,1)S(1)}, u32[]{:S(2)}, u32[]{:S(2)}) collective-permute-start(bf16[16,2048]{1,0:T(8,128)(2,1)S(1)} %get-tuple-element.52), channel_id=1, source_target_pairs={{0,4},{4,0},{8,12},{12,8},{16,20},{20,16},{24,28},{28,24},{1,5},{5... | collective-permute-start | bytes 196616 | tf_op jit(solution)/shard_map/ppermute | solution.py:24
  59.9 1.9 %collective-permute-start.27 = (bf16[16,2048]{1,0:T(8,128)(2,1)S(1)}, bf16[16,2048]{1,0:T(8,128)(2,1)S(1)}, u32[]{:S(2)}, u32[]{:S(2)}) collective-permute-start(bf16[16,2048]{1,0:T(8,128)(2,1)S(1)} %get-tuple-element.53), channel_id=1, source_target_pairs={{0,4},{4,0},{8,12},{12,8},{16,20},{20,16},{24,28},{28,24},{1,5},{5... | collective-permute-start | bytes 196616 | tf_op jit(solution)/shard_map/ppermute | solution.py:24
  61.9 1.5 %collective-permute-start.29 = (bf16[16,2048]{1,0:T(8,128)(2,1)S(1)}, bf16[16,2048]{1,0:T(8,128)(2,1)S(1)}, u32[]{:S(2)}, u32[]{:S(2)}) collective-permute-start(bf16[16,2048]{1,0:T(8,128)(2,1)S(1)} %get-tuple-element.55), channel_id=1, source_target_pairs={{0,12},{4,8},{8,4},{12,0},{16,28},{20,24},{24,20},{28,16},{1,13},{... | collective-permute-start | bytes 196616 | tf_op jit(solution)/shard_map/ppermute | solution.py:24
  63.4 1.5 %collective-permute-start.26 = (bf16[16,2048]{1,0:T(8,128)(2,1)S(1)}, bf16[16,2048]{1,0:T(8,128)(2,1)S(1)}, u32[]{:S(2)}, u32[]{:S(2)}) collective-permute-start(bf16[16,2048]{1,0:T(8,128)(2,1)S(1)} %shard_map.157), channel_id=1, source_target_pairs={{0,24},{4,28},{8,16},{12,20},{16,8},{20,12},{24,0},{28,4},{1,25},{... | collective-permute-start | bytes 196616 | tf_op jit(solution)/shard_map/ppermute | solution.py:24
  66.1 0.9 collective-permute-done.29.refs_4_
  67.0 2.5 %collective-permute-done.26.refs_1_ = bf16[16,2048]{1,0:T(8,128)(2,1)S(1)} collective-permute-done((bf16[16,2048]{1,0:T(8,128)(2,1)S(1)}, bf16[16,2048]{1,0:T(8,128)(2,1)S(1)}, u32[]{:S(2)}, u32[]{:S(2)}) %collective-permute-start.26) | collective-permute-done | bytes 65568 | tf_op jit(solution)/shard_map/ppermute | solution.py:24
  69.6 2.3 %collective-permute-done.24.refs_0_ = bf16[16,2048]{1,0:T(8,128)(2,1)S(1)} collective-permute-done((bf16[16,2048]{1,0:T(8,128)(2,1)S(1)}, bf16[16,2048]{1,0:T(8,128)(2,1)S(1)}, u32[]{:S(2)}, u32[]{:S(2)}) %collective-permute-start.24) | collective-permute-done | bytes 65568 | tf_op jit(solution)/shard_map/ppermute | solution.py:24
  71.9 0.7 shard_map.158
  72.5 2.2 %collective-permute-start.35 = (bf16[16,2048]{1,0:T(8,128)(2,1)S(1)}, bf16[16,2048]{1,0:T(8,128)(2,1)S(1)}, u32[]{:S(2)}, u32[]{:S(2)}) collective-permute-start(bf16[16,2048]{1,0:T(8,128)(2,1)S(1)} %get-tuple-element.57.refs_0_), channel_id=1, source_target_pairs={{0,24},{4,28},{8,16},{12,20},{16,8},{20,12},{24,0},{28,4},{1,25},{... | collective-permute-start | bytes 196616 | tf_op jit(solution)/shard_map/ppermute | solution.py:24
  74.8 1.4 %collective-permute-start.30 = (bf16[16,2048]{1,0:T(8,128)(2,1)S(1)}, bf16[16,2048]{1,0:T(8,128)(2,1)S(1)}, u32[]{:S(2)}, u32[]{:S(2)}) collective-permute-start(bf16[16,2048]{1,0:T(8,128)(2,1)S(1)} %get-tuple-element.57.refs_0_), channel_id=1, source_target_pairs={{0,4},{4,0},{8,12},{12,8},{16,20},{20,16},{24,28},{28,24},{1,5},{5... | collective-permute-start | bytes 196616 | tf_op jit(solution)/shard_map/ppermute | solution.py:24
  76.2 1.2 %collective-permute-start.31 = (bf16[16,2048]{1,0:T(8,128)(2,1)S(1)}, bf16[16,2048]{1,0:T(8,128)(2,1)S(1)}, u32[]{:S(2)}, u32[]{:S(2)}) collective-permute-start(bf16[16,2048]{1,0:T(8,128)(2,1)S(1)} %get-tuple-element.57.refs_0_), channel_id=1, source_target_pairs={{0,8},{4,12},{8,0},{12,4},{16,24},{20,28},{24,16},{28,20},{1,9},{5... | collective-permute-start | bytes 196616 | tf_op jit(solution)/shard_map/ppermute | solution.py:24
  77.4 0.9 collective-permute-start.32
  78.3 1.5 %collective-permute-done.33.refs_4_ = bf16[16,2048]{1,0:T(8,128)(2,1)S(1)} collective-permute-done((bf16[16,2048]{1,0:T(8,128)(2,1)S(1)}, bf16[16,2048]{1,0:T(8,128)(2,1)S(1)}, u32[]{:S(2)}, u32[]{:S(2)}) %collective-permute-start.33) | collective-permute-done | bytes 65568 | tf_op jit(solution)/shard_map/ppermute | solution.py:24
  79.8 0.7 collective-permute-start.34
  80.5 1.4 %collective-permute-start.36 = (bf16[16,2048]{1,0:T(8,128)(2,1)S(1)}, bf16[16,2048]{1,0:T(8,128)(2,1)S(1)}, u32[]{:S(2)}, u32[]{:S(2)}) collective-permute-start(bf16[16,2048]{1,0:T(8,128)(2,1)S(1)} %collective-permute-done.35.refs_6_), channel_id=1, source_target_pairs={{0,4},{4,0},{8,12},{12,8},{16,20},{20,16},{24,28},{28,24},{1,5},{5... | collective-permute-start | bytes 196616 | tf_op jit(solution)/shard_map/ppermute | solution.py:24
  81.8 0.7 collective-permute-done.32.refs_3_
  82.6 1.5 %collective-permute-done.34.refs_5_ = bf16[16,2048]{1,0:T(8,128)(2,1)S(1)} collective-permute-done((bf16[16,2048]{1,0:T(8,128)(2,1)S(1)}, bf16[16,2048]{1,0:T(8,128)(2,1)S(1)}, u32[]{:S(2)}, u32[]{:S(2)}) %collective-permute-start.34) | collective-permute-done | bytes 65568 | tf_op jit(solution)/shard_map/ppermute | solution.py:24
  84.1 0.7 collective-permute-done.36.refs_7_
  84.8 1.8 %shard_map.159 = (bf16[128,2048]{1,0:T(8,128)(2,1)S(1)}, f32[64,1920]{1,0:T(8,128)S(1)}, bf16[64,1920]{1,0:T(8,128)(2,1)S(1)}) custom-call(s32[2]{0:T(128)S(1)} %copy-done.7, f32[1,2048]{1,0:T(1,128)S(1)} %bitcast.25, bf16[16,2048]{1,0:T(8,128)(2,1)S(1)} %get-tuple-element.57.refs_0_, bf16[16,2048]{1,0:T(8,128)(2,1)S(1)} %collective-permute-done.30.refs_1_, ...), custom_call_target="tpu_custom_call" | custom-call | flops 6308233216 | bytes 8388608 | tf_op jit(solution)/shard_map/pallas_call | solution.py:45
  86.8 1.2 shard_map.160
  88.5 1.5 %collective-permute-start.38 = (bf16[32,1920]{1,0:T(8,128)(2,1)S(1)}, bf16[32,1920]{1,0:T(8,128)(2,1)S(1)}, u32[]{:S(2)}, u32[]{:S(2)}) collective-permute-start(bf16[32,1920]{1,0:T(8,128)(2,1)S(1)} %slice.118), channel_id=1, source_target_pairs={{0,2},{1,3},{2,0},{3,1},{4,6},{5,7},{6,4},{7,5},{8,10},{9,11},{10,... | collective-permute-start | bytes 368648 | tf_op jit(solution)/shard_map/ppermute | solution.py:24
  90.1 1.0 collective-permute-start.40
  91.1 3.6 %collective-permute-done.38 = bf16[32,1920]{1,0:T(8,128)(2,1)S(1)} collective-permute-done((bf16[32,1920]{1,0:T(8,128)(2,1)S(1)}, bf16[32,1920]{1,0:T(8,128)(2,1)S(1)}, u32[]{:S(2)}, u32[]{:S(2)}) %collective-permute-start.38) | collective-permute-done | bytes 122912 | tf_op jit(solution)/shard_map/ppermute | solution.py:24
  95.0 1.3 %collective-permute-done.40 = bf16[32,1792]{1,0:T(8,128)(2,1)S(1)} collective-permute-done((bf16[32,1792]{1,0:T(8,128)(2,1)S(1)}, bf16[32,1792]{1,0:T(8,128)(2,1)S(1)}, u32[]{:S(2)}, u32[]{:S(2)}) %collective-permute-start.40) | collective-permute-done | bytes 114720 | tf_op jit(solution)/shard_map/ppermute | solution.py:24
  96.5 1.5 %collective-permute-start.42 = (bf16[32,1792]{1,0:T(8,128)(2,1)S(1)}, bf16[32,1792]{1,0:T(8,128)(2,1)S(1)}, u32[]{:S(2)}, u32[]{:S(2)}) collective-permute-start(bf16[32,1792]{1,0:T(8,128)(2,1)S(1)} %fusion.2.refs_0_), channel_id=1, source_target_pairs={{0,2},{1,3},{2,0},{3,1},{4,6},{5,7},{6,4},{7,5},{8,10},{9,11},{10,... | collective-permute-start | bytes 344072 | tf_op jit(solution)/shard_map/ppermute | solution.py:24
  98.0 3.4 %collective-permute-done.42.refs_2_ = bf16[32,1792]{1,0:T(8,128)(2,1)S(1)} collective-permute-done((bf16[32,1792]{1,0:T(8,128)(2,1)S(1)}, bf16[32,1792]{1,0:T(8,128)(2,1)S(1)}, u32[]{:S(2)}, u32[]{:S(2)}) %collective-permute-start.42) | collective-permute-done | bytes 114720 | tf_op jit(solution)/shard_map/ppermute | solution.py:24
  101.4 1.3 %collective-permute-done.43.refs_3_ = bf16[32,1792]{1,0:T(8,128)(2,1)S(1)} collective-permute-done((bf16[32,1792]{1,0:T(8,128)(2,1)S(1)}, bf16[32,1792]{1,0:T(8,128)(2,1)S(1)}, u32[]{:S(2)}, u32[]{:S(2)}) %collective-permute-start.43) | collective-permute-done | bytes 114720 | tf_op jit(solution)/shard_map/ppermute | solution.py:24
  102.7 1.7 %shard_map.161 = (f32[16,2048]{1,0:T(8,128)S(1)}, bf16[16,2048]{1,0:T(8,128)(2,1)S(1)}, bf16[16,2048]{1,0:T(8,128)(2,1)S(1)}, bf16[16,2048]{1,0:T(8,128)(2,1)S(1...) custom-call(s32[2]{0:T(128)S(1)} %copy-done.7, ...), custom_call_target="tpu_custom_call" | custom-call | flops 6308233216 | bytes 7340032 | tf_op jit(solution)/shard_map/pallas_call | solution.py:45
  104.4 1.4 %collective-permute-start.46 = (bf16[16,2048]{1,0:T(8,128)(2,1)S(1)}, bf16[16,2048]{1,0:T(8,128)(2,1)S(1)}, u32[]{:S(2)}, u32[]{:S(2)}) collective-permute-start(bf16[16,2048]{1,0:T(8,128)(2,1)S(1)} %get-tuple-element.66), channel_id=1, source_target_pairs={{0,4},{4,0},{8,12},{12,8},{16,20},{20,16},{24,28},{28,24},{1,5},{5... | collective-permute-start | bytes 196616 | tf_op jit(solution)/shard_map/ppermute | solution.py:24
  105.8 0.7 collective-permute-start.44
  106.5 1.3 %collective-permute-start.48 = (bf16[16,2048]{1,0:T(8,128)(2,1)S(1)}, bf16[16,2048]{1,0:T(8,128)(2,1)S(1)}, u32[]{:S(2)}, u32[]{:S(2)}) collective-permute-start(bf16[16,2048]{1,0:T(8,128)(2,1)S(1)} %get-tuple-element.67), channel_id=1, source_target_pairs={{0,4},{4,0},{8,12},{12,8},{16,20},{20,16},{24,28},{28,24},{1,5},{5... | collective-permute-start | bytes 196616 | tf_op jit(solution)/shard_map/ppermute | solution.py:24
  107.8 2.1 %collective-permute-start.50 = (bf16[16,2048]{1,0:T(8,128)(2,1)S(1)}, bf16[16,2048]{1,0:T(8,128)(2,1)S(1)}, u32[]{:S(2)}, u32[]{:S(2)}) collective-permute-start(bf16[16,2048]{1,0:T(8,128)(2,1)S(1)} %get-tuple-element.69), channel_id=1, source_target_pairs={{0,12},{4,8},{8,4},{12,0},{16,28},{20,24},{24,20},{28,16},{1,13},{... | collective-permute-start | bytes 196616 | tf_op jit(solution)/shard_map/ppermute | solution.py:24
  110.0 1.8 %collective-permute-start.47 = (bf16[16,2048]{1,0:T(8,128)(2,1)S(1)}, bf16[16,2048]{1,0:T(8,128)(2,1)S(1)}, u32[]{:S(2)}, u32[]{:S(2)}) collective-permute-start(bf16[16,2048]{1,0:T(8,128)(2,1)S(1)} %shard_map.163), channel_id=1, source_target_pairs={{0,24},{4,28},{8,16},{12,20},{16,8},{20,12},{24,0},{28,4},{1,25},{... | collective-permute-start | bytes 196616 | tf_op jit(solution)/shard_map/ppermute | solution.py:24
  112.3 0.7 collective-permute-done.50.refs_4_
  113.0 3.1 %collective-permute-done.47.refs_1_ = bf16[16,2048]{1,0:T(8,128)(2,1)S(1)} collective-permute-done((bf16[16,2048]{1,0:T(8,128)(2,1)S(1)}, bf16[16,2048]{1,0:T(8,128)(2,1)S(1)}, u32[]{:S(2)}, u32[]{:S(2)}) %collective-permute-start.47) | collective-permute-done | bytes 65568 | tf_op jit(solution)/shard_map/ppermute | solution.py:24
  116.1 2.3 %collective-permute-done.45.refs_0_ = bf16[16,2048]{1,0:T(8,128)(2,1)S(1)} collective-permute-done((bf16[16,2048]{1,0:T(8,128)(2,1)S(1)}, bf16[16,2048]{1,0:T(8,128)(2,1)S(1)}, u32[]{:S(2)}, u32[]{:S(2)}) %collective-permute-start.45) | collective-permute-done | bytes 65568 | tf_op jit(solution)/shard_map/ppermute | solution.py:24
  118.4 0.7 shard_map.164
  (113 shorter events, 6.3 us)
Async XLA Ops:
  1.3 10.3 %copy-start.9 = (s32[64]{0:T(128)S(1)}, s32[64]{0:T(128)}, u32[]{:S(2)}) copy-start(s32[64]{0:T(128)} %param.18) | copy-start | bytes 772
  1.3 22.6 %copy-start.2 = (bf16[2048,256]{1,0:T(8,128)(2,1)S(1)}, bf16[2048,256]{1,0:T(8,128)(2,1)}, u32[]{:S(2)}) copy-start(bf16[2048,256]{1,0:T(8,128)(2,1)} %refs_8_.2) | copy-start | bytes 3145732
  1.3 22.6 %copy-start.5 = (f32[2048]{0:T(1024)S(1)}, f32[2048]{0:T(1024)}, u32[]{:S(2)}) copy-start(f32[2048]{0:T(1024)} %param.19) | copy-start | bytes 24580
  1.3 22.6 %copy-start.7 = (s32[2]{0:T(128)S(1)}, s32[2]{0:T(128)}, u32[]{:S(2)}) copy-start(s32[2]{0:T(128)} %pad_add_fusion.3.where_ref) | copy-start | bytes 28
  3.9 8.2 %collective-permute-start.3 = (bf16[16,2048]{1,0:T(8,128)(2,1)}, bf16[16,2048]{1,0:T(8,128)(2,1)S(1)}, u32[]{:S(2)}, u32[]{:S(2)}) collective-permute-start(bf16[16,2048]{1,0:T(8,128)(2,1)} %get-tuple-element.36.refs_0_.refs_5_), channel_id=1, source_target_pairs={{0,16},{4,20},{8,24},{12,28},{16,0},{20,4},{24,8},{28,12},{1,17},{... | collective-permute-start | bytes 196616 | tf_op jit(solution)/shard_map/ppermute | solution.py:24
  8.0 7.2 %collective-permute-start.5 = (bf16[16,2048]{1,0:T(8,128)(2,1)}, bf16[16,2048]{1,0:T(8,128)(2,1)S(1)}, u32[]{:S(2)}, u32[]{:S(2)}) collective-permute-start(bf16[16,2048]{1,0:T(8,128)(2,1)} %get-tuple-element.36.refs_0_.refs_5_), channel_id=1, source_target_pairs={{0,24},{4,28},{8,16},{12,20},{16,8},{20,12},{24,0},{28,4},{1,25},{... | collective-permute-start | bytes 196616 | tf_op jit(solution)/shard_map/ppermute | solution.py:24
  9.3 9.9 %collective-permute-start = (bf16[16,2048]{1,0:T(8,128)(2,1)}, bf16[16,2048]{1,0:T(8,128)(2,1)S(1)}, u32[]{:S(2)}, u32[]{:S(2)}) collective-permute-start(bf16[16,2048]{1,0:T(8,128)(2,1)} %get-tuple-element.36.refs_0_.refs_5_), channel_id=1, source_target_pairs={{0,4},{4,0},{8,12},{12,8},{16,20},{20,16},{24,28},{28,24},{1,5},{5... | collective-permute-start | bytes 196616 | tf_op jit(solution)/shard_map/ppermute | solution.py:24
  10.8 10.6 %collective-permute-start.1 = (bf16[16,2048]{1,0:T(8,128)(2,1)}, bf16[16,2048]{1,0:T(8,128)(2,1)S(1)}, u32[]{:S(2)}, u32[]{:S(2)}) collective-permute-start(bf16[16,2048]{1,0:T(8,128)(2,1)} %get-tuple-element.36.refs_0_.refs_5_), channel_id=1, source_target_pairs={{0,8},{4,12},{8,0},{12,4},{16,24},{20,28},{24,16},{28,20},{1,9},{5... | collective-permute-start | bytes 196616 | tf_op jit(solution)/shard_map/ppermute | solution.py:24
  11.1 7.2 %collective-permute-start.13 = (bf16[4,2,8,8,128]{4,3,2,1,0:T(8,128)(2,1)}, bf16[4,2,8,8,128]{4,3,2,1,0:T(8,128)(2,1)S(1)}, u32[]{:S(2)}, u32[]{:S(2)}) collective-permute-start(bf16[4,2,8,8,128]{4,3,2,1,0:T(8,128)(2,1)} %get-tuple-element.44), channel_id=1, source_target_pairs={{0,4},{4,0},{8,12},{12,8},{16,20},{20,16},{24,28},{28,24},{1,5},{5... | collective-permute-start | bytes 393224 | tf_op jit(solution)/shard_map/ppermute | solution.py:24
  12.1 9.5 %collective-permute-start.2 = (bf16[16,2048]{1,0:T(8,128)(2,1)}, bf16[16,2048]{1,0:T(8,128)(2,1)S(1)}, u32[]{:S(2)}, u32[]{:S(2)}) collective-permute-start(bf16[16,2048]{1,0:T(8,128)(2,1)} %get-tuple-element.36.refs_0_.refs_5_), channel_id=1, source_target_pairs={{0,12},{4,8},{8,4},{12,0},{16,28},{20,24},{24,20},{28,16},{1,13},{... | collective-permute-start | bytes 196616 | tf_op jit(solution)/shard_map/ppermute | solution.py:24
  15.2 8.7 %collective-permute-start.4 = (bf16[16,2048]{1,0:T(8,128)(2,1)S(1)}, bf16[16,2048]{1,0:T(8,128)(2,1)S(1)}, u32[]{:S(2)}, u32[]{:S(2)}) collective-permute-start(bf16[16,2048]{1,0:T(8,128)(2,1)S(1)} %collective-permute-done.3.refs_4_), channel_id=1, source_target_pairs={{0,4},{4,0},{8,12},{12,8},{16,20},{20,16},{24,28},{28,24},{1,5},{5... | collective-permute-start | bytes 196616 | tf_op jit(solution)/shard_map/ppermute | solution.py:24
  18.3 5.6 %collective-permute-start.6 = (bf16[16,2048]{1,0:T(8,128)(2,1)S(1)}, bf16[16,2048]{1,0:T(8,128)(2,1)S(1)}, u32[]{:S(2)}, u32[]{:S(2)}) collective-permute-start(bf16[16,2048]{1,0:T(8,128)(2,1)S(1)} %collective-permute-done.5.refs_6_), channel_id=1, source_target_pairs={{0,4},{4,0},{8,12},{12,8},{16,20},{20,16},{24,28},{28,24},{1,5},{5... | collective-permute-start | bytes 196616 | tf_op jit(solution)/shard_map/ppermute | solution.py:24
  19.3 9.8 %collective-permute-start.14 = (bf16[1,2,2,8,8,128]{5,4,3,2,0,1:T(8,128)(2,1)S(1)}, bf16[1,2,2,8,8,128]{5,4,3,2,0,1:T(8,128)(2,1)S(1)}, u32[]{:S(2)}, u32[]{:S(2)}) collective-permute-start(bf16[1,2,2,8,8,128]{5,4,3,2,0,1:T(8,128)(2,1)S(1)} %get-tuple-element.73), channel_id=1, source_target_pairs={{0,8},{4,12},{8,0},{12,4},{16,24},{20,28},{24,16},{28,20},{1,9},{5... | collective-permute-start | bytes 196616 | tf_op jit(solution)/shard_map/ppermute | solution.py:24
  21.4 7.6 %collective-permute-start.15 = (bf16[1,2,2,8,8,128]{5,4,3,2,0,1:T(8,128)(2,1)S(1)}, bf16[1,2,2,8,8,128]{5,4,3,2,0,1:T(8,128)(2,1)S(1)}, u32[]{:S(2)}, u32[]{:S(2)}) collective-permute-start(bf16[1,2,2,8,8,128]{5,4,3,2,0,1:T(8,128)(2,1)S(1)} %get-tuple-element.75), channel_id=1, source_target_pairs={{0,16},{4,20},{8,24},{12,28},{16,0},{20,4},{24,8},{28,12},{1,17},{... | collective-permute-start | bytes 196616 | tf_op jit(solution)/shard_map/ppermute | solution.py:24
  21.6 7.5 %collective-permute-start.16 = (bf16[1,2,2,8,8,128]{5,4,3,2,0,1:T(8,128)(2,1)S(1)}, bf16[1,2,2,8,8,128]{5,4,3,2,0,1:T(8,128)(2,1)S(1)}, u32[]{:S(2)}, u32[]{:S(2)}) collective-permute-start(bf16[1,2,2,8,8,128]{5,4,3,2,0,1:T(8,128)(2,1)S(1)} %get-tuple-element.74), channel_id=1, source_target_pairs={{0,24},{4,28},{8,16},{12,20},{16,8},{20,12},{24,0},{28,4},{1,25},{... | collective-permute-start | bytes 196616 | tf_op jit(solution)/shard_map/ppermute | solution.py:24
  28.5 3.2 %collective-permute-start.11 = (bf16[64,1024]{1,0:T(8,128)(2,1)S(1)}, bf16[64,1024]{1,0:T(8,128)(2,1)S(1)}, u32[]{:S(2)}, u32[]{:S(2)}) collective-permute-start(bf16[64,1024]{1,0:T(8,128)(2,1)S(1)} %get-tuple-element.42), channel_id=1, source_target_pairs={{0,1},{1,0},{2,3},{3,2},{4,5},{5,4},{6,7},{7,6},{8,9},{9,8},{10,11... | collective-permute-start | bytes 393224 | tf_op jit(solution)/shard_map/ppermute | solution.py:24
  28.6 2.1 %collective-permute-start.7 = (bf16[128,384]{1,0:T(8,128)(2,1)S(1)}, bf16[128,384]{1,0:T(8,128)(2,1)S(1)}, u32[]{:S(2)}, u32[]{:S(2)}) collective-permute-start(bf16[128,384]{1,0:T(8,128)(2,1)S(1)} %get-tuple-element.37.own_ref), channel_id=1, source_target_pairs={{0,1},{1,0},{2,3},{3,2},{4,5},{5,4},{6,7},{7,6},{8,9},{9,8},{10,11... | collective-permute-start | bytes 294920 | tf_op jit(solution)/shard_map/ppermute | solution.py:24
  29.1 9.2 %collective-permute-start.18 = (bf16[128,8,128]{2,1,0:T(8,128)(2,1)S(1)}, bf16[128,8,128]{2,1,0:T(8,128)(2,1)S(1)}, u32[]{:S(2)}, u32[]{:S(2)}) collective-permute-start(bf16[128,8,128]{2,1,0:T(8,128)(2,1)S(1)} %bitcast.15), channel_id=1, source_target_pairs={{0,2},{1,3},{2,0},{3,1},{4,6},{5,7},{6,4},{7,5},{8,10},{9,11},{10,... | collective-permute-start | bytes 786440 | tf_op jit(solution)/shard_map/ppermute | solution.py:24
  30.6 13.1 %collective-permute-start.17 = (bf16[128,8,128]{2,1,0:T(8,128)(2,1)S(1)}, bf16[128,8,128]{2,1,0:T(8,128)(2,1)S(1)}, u32[]{:S(2)}, u32[]{:S(2)}) collective-permute-start(bf16[128,8,128]{2,1,0:T(8,128)(2,1)S(1)} %bitcast.16), channel_id=1, source_target_pairs={{0,1},{1,0},{2,3},{3,2},{4,5},{5,4},{6,7},{7,6},{8,9},{9,8},{10,11... | collective-permute-start | bytes 786440 | tf_op jit(solution)/shard_map/ppermute | solution.py:24
  30.8 9.5 %collective-permute-start.8 = (bf16[128,384]{1,0:T(8,128)(2,1)S(1)}, bf16[128,384]{1,0:T(8,128)(2,1)S(1)}, u32[]{:S(2)}, u32[]{:S(2)}) collective-permute-start(bf16[128,384]{1,0:T(8,128)(2,1)S(1)} %shard_map.151.own_ref), channel_id=1, source_target_pairs={{0,2},{1,3},{2,0},{3,1},{4,6},{5,7},{6,4},{7,5},{8,10},{9,11},{10,... | collective-permute-start | bytes 294920 | tf_op jit(solution)/shard_map/ppermute | solution.py:24
  31.8 12.0 %copy-start.8 = (f32[4,128]{1,0:T(4,128)S(1)}, f32[4,128]{1,0:T(4,128)}, u32[]{:S(2)}) copy-start(f32[4,128]{1,0:T(4,128)} %constant.71.clone.rope_ref) | copy-start | bytes 6148
  31.8 12.0 %collective-permute-start.12 = (bf16[32,1024]{1,0:T(8,128)(2,1)S(1)}, bf16[32,1024]{1,0:T(8,128)(2,1)S(1)}, u32[]{:S(2)}, u32[]{:S(2)}) collective-permute-start(bf16[32,1024]{1,0:T(8,128)(2,1)S(1)} %slice.120), channel_id=1, source_target_pairs={{0,2},{1,3},{2,0},{3,1},{4,6},{5,7},{6,4},{7,5},{8,10},{9,11},{10,... | collective-permute-start | bytes 196616 | tf_op jit(solution)/shard_map/ppermute | solution.py:24
  38.4 5.4 %collective-permute-start.19 = (bf16[128,8,128]{2,1,0:T(8,128)(2,1)S(1)}, bf16[128,8,128]{2,1,0:T(8,128)(2,1)S(1)}, u32[]{:S(2)}, u32[]{:S(2)}) collective-permute-start(bf16[128,8,128]{2,1,0:T(8,128)(2,1)S(1)} %collective-permute-done.18.refs_4_), channel_id=1, source_target_pairs={{0,1},{1,0},{2,3},{3,2},{4,5},{5,4},{6,7},{7,6},{8,9},{9,8},{10,11... | collective-permute-start | bytes 786440 | tf_op jit(solution)/shard_map/ppermute | solution.py:24
  41.0 4.9 %collective-permute-start.10 = (bf16[128,128]{1,0:T(8,128)(2,1)S(1)}, bf16[128,128]{1,0:T(8,128)(2,1)S(1)}, u32[]{:S(2)}, u32[]{:S(2)}) collective-permute-start(bf16[128,128]{1,0:T(8,128)(2,1)S(1)} %get-tuple-element.39), channel_id=1, source_target_pairs={{0,4},{4,12},{8,20},{12,28},{16,0},{20,8},{24,16},{28,24},{1,5},{5... | collective-permute-start | bytes 98312 | tf_op jit(solution)/shard_map/ppermute | solution.py:506
  43.1 2.8 %collective-permute-start.9 = (bf16[128,128]{1,0:T(8,128)(2,1)S(1)}, bf16[128,128]{1,0:T(8,128)(2,1)S(1)}, u32[]{:S(2)}, u32[]{:S(2)}) collective-permute-start(bf16[128,128]{1,0:T(8,128)(2,1)S(1)} %get-tuple-element.38), channel_id=1, source_target_pairs={{0,0},{4,8},{8,16},{12,24},{16,4},{20,12},{24,20},{28,28},{1,1},{5... | collective-permute-start | bytes 98312 | tf_op jit(solution)/shard_map/ppermute | solution.py:506
  45.9 6.7 %copy-start.1 = (bf16[1024,2048]{1,0:T(8,128)(2,1)S(1)}, bf16[1024,2048]{1,0:T(8,128)(2,1)}, u32[]{:S(2)}) copy-start(bf16[1024,2048]{1,0:T(8,128)(2,1)} %refs_4_.2) | copy-start | bytes 12582916
  47.0 4.3 %collective-permute-start.21 = (bf16[32,1024]{1,0:T(8,128)(2,1)S(1)}, bf16[32,1024]{1,0:T(8,128)(2,1)S(1)}, u32[]{:S(2)}, u32[]{:S(2)}) collective-permute-start(bf16[32,1024]{1,0:T(8,128)(2,1)S(1)} %shard_map.154.refs_0_), channel_id=1, source_target_pairs={{0,2},{1,3},{2,0},{3,1},{4,6},{5,7},{6,4},{7,5},{8,10},{9,11},{10,... | collective-permute-start | bytes 196616 | tf_op jit(solution)/shard_map/ppermute | solution.py:24
  48.5 2.9 %collective-permute-start.20 = (bf16[32,1024]{1,0:T(8,128)(2,1)S(1)}, bf16[32,1024]{1,0:T(8,128)(2,1)S(1)}, u32[]{:S(2)}, u32[]{:S(2)}) collective-permute-start(bf16[32,1024]{1,0:T(8,128)(2,1)S(1)} %shard_map.154.refs_0_), channel_id=1, source_target_pairs={{0,1},{1,0},{2,3},{3,2},{4,5},{5,4},{6,7},{7,6},{8,9},{9,8},{10,11... | collective-permute-start | bytes 196616 | tf_op jit(solution)/shard_map/ppermute | solution.py:24
  51.4 1.3 %collective-permute-start.22 = (bf16[32,1024]{1,0:T(8,128)(2,1)S(1)}, bf16[32,1024]{1,0:T(8,128)(2,1)S(1)}, u32[]{:S(2)}, u32[]{:S(2)}) collective-permute-start(bf16[32,1024]{1,0:T(8,128)(2,1)S(1)} %collective-permute-done.21.refs_2_), channel_id=1, source_target_pairs={{0,1},{1,0},{2,3},{3,2},{4,5},{5,4},{6,7},{7,6},{8,9},{9,8},{10,11... | collective-permute-start | bytes 196616 | tf_op jit(solution)/shard_map/ppermute | solution.py:24
  53.9 9.5 %collective-permute-start.25 = (bf16[16,2048]{1,0:T(8,128)(2,1)S(1)}, bf16[16,2048]{1,0:T(8,128)(2,1)S(1)}, u32[]{:S(2)}, u32[]{:S(2)}) collective-permute-start(bf16[16,2048]{1,0:T(8,128)(2,1)S(1)} %get-tuple-element.52), channel_id=1, source_target_pairs={{0,4},{4,0},{8,12},{12,8},{16,20},{20,16},{24,28},{28,24},{1,5},{5... | collective-permute-start | bytes 196616 | tf_op jit(solution)/shard_map/ppermute | solution.py:24
  59.8 5.1 %collective-permute-start.23 = (bf16[16,2048]{1,0:T(8,128)(2,1)S(1)}, bf16[16,2048]{1,0:T(8,128)(2,1)S(1)}, u32[]{:S(2)}, u32[]{:S(2)}) collective-permute-start(bf16[16,2048]{1,0:T(8,128)(2,1)S(1)} %get-tuple-element.51), channel_id=1, source_target_pairs={{0,4},{4,0},{8,12},{12,8},{16,20},{20,16},{24,28},{28,24},{1,5},{5... | collective-permute-start | bytes 196616 | tf_op jit(solution)/shard_map/ppermute | solution.py:24
  59.9 5.9 %collective-permute-start.27 = (bf16[16,2048]{1,0:T(8,128)(2,1)S(1)}, bf16[16,2048]{1,0:T(8,128)(2,1)S(1)}, u32[]{:S(2)}, u32[]{:S(2)}) collective-permute-start(bf16[16,2048]{1,0:T(8,128)(2,1)S(1)} %get-tuple-element.53), channel_id=1, source_target_pairs={{0,4},{4,0},{8,12},{12,8},{16,20},{20,16},{24,28},{28,24},{1,5},{5... | collective-permute-start | bytes 196616 | tf_op jit(solution)/shard_map/ppermute | solution.py:24
  61.8 4.3 %collective-permute-start.28 = (bf16[16,2048]{1,0:T(8,128)(2,1)S(1)}, bf16[16,2048]{1,0:T(8,128)(2,1)S(1)}, u32[]{:S(2)}, u32[]{:S(2)}) collective-permute-start(bf16[16,2048]{1,0:T(8,128)(2,1)S(1)} %get-tuple-element.54), channel_id=1, source_target_pairs={{0,8},{4,12},{8,0},{12,4},{16,24},{20,28},{24,16},{28,20},{1,9},{5... | collective-permute-start | bytes 196616 | tf_op jit(solution)/shard_map/ppermute | solution.py:24
  61.9 5.2 %collective-permute-start.29 = (bf16[16,2048]{1,0:T(8,128)(2,1)S(1)}, bf16[16,2048]{1,0:T(8,128)(2,1)S(1)}, u32[]{:S(2)}, u32[]{:S(2)}) collective-permute-start(bf16[16,2048]{1,0:T(8,128)(2,1)S(1)} %get-tuple-element.55), channel_id=1, source_target_pairs={{0,12},{4,8},{8,4},{12,0},{16,28},{20,24},{24,20},{28,16},{1,13},{... | collective-permute-start | bytes 196616 | tf_op jit(solution)/shard_map/ppermute | solution.py:24
  63.4 8.4 %copy-start.4 = (bf16[16,2048]{1,0:T(8,128)(2,1)S(1)}, bf16[16,2048]{1,0:T(8,128)(2,1)}, u32[]{:S(2)}) copy-start(bf16[16,2048]{1,0:T(8,128)(2,1)} %get-tuple-element.36.refs_0_.refs_5_) | copy-start | bytes 196612
  63.4 6.1 %collective-permute-start.26 = (bf16[16,2048]{1,0:T(8,128)(2,1)S(1)}, bf16[16,2048]{1,0:T(8,128)(2,1)S(1)}, u32[]{:S(2)}, u32[]{:S(2)}) collective-permute-start(bf16[16,2048]{1,0:T(8,128)(2,1)S(1)} %shard_map.157), channel_id=1, source_target_pairs={{0,24},{4,28},{8,16},{12,20},{16,8},{20,12},{24,0},{28,4},{1,25},{... | collective-permute-start | bytes 196616 | tf_op jit(solution)/shard_map/ppermute | solution.py:24
  65.0 19.8 %slice-start = ((s8[7340032]{0:T(1024)(128)(4,1)}), s8[4194304]{0:T(1024)(128)(4,1)S(1)}, s32[]{:S(2)}) async-start(s8[7340032]{0:T(1024)(128)(4,1)} %bitcast.18), calls=%async_computation | async-start | bytes 8388608
  65.0 6.8 %collective-permute-start.24 = (bf16[16,2048]{1,0:T(8,128)(2,1)S(1)}, bf16[16,2048]{1,0:T(8,128)(2,1)S(1)}, u32[]{:S(2)}, u32[]{:S(2)}) collective-permute-start(bf16[16,2048]{1,0:T(8,128)(2,1)S(1)} %shard_map.156), channel_id=1, source_target_pairs={{0,16},{4,20},{8,24},{12,28},{16,0},{20,4},{24,8},{28,12},{1,17},{... | collective-permute-start | bytes 196616 | tf_op jit(solution)/shard_map/ppermute | solution.py:24
  71.8 12.9 %slice-start.1 = ((s8[7340032]{0:T(1024)(128)(4,1)}), s8[3145728]{0:T(1024)(128)(4,1)S(1)}, s32[]{:S(2)}) async-start(s8[7340032]{0:T(1024)(128)(4,1)} %bitcast.18), calls=%async_computation.1 | async-start | bytes 6291456
  71.8 12.9 %copy-start.6 = (f32[2048]{0:T(1024)S(1)}, f32[2048]{0:T(1024)}, u32[]{:S(2)}) copy-start(f32[2048]{0:T(1024)} %param.20) | copy-start | bytes 24580
  71.8 14.9 %slice-start.2 = ((s8[7340032]{0:T(1024)(128)(4,1)}), s8[4194304]{0:T(1024)(128)(4,1)S(1)}, s32[]{:S(2)}) async-start(s8[7340032]{0:T(1024)(128)(4,1)} %bitcast.20), calls=%async_computation.2 | async-start | bytes 8388608
  72.5 7.2 %collective-permute-start.33 = (bf16[16,2048]{1,0:T(8,128)(2,1)S(1)}, bf16[16,2048]{1,0:T(8,128)(2,1)S(1)}, u32[]{:S(2)}, u32[]{:S(2)}) collective-permute-start(bf16[16,2048]{1,0:T(8,128)(2,1)S(1)} %get-tuple-element.57.refs_0_), channel_id=1, source_target_pairs={{0,16},{4,20},{8,24},{12,28},{16,0},{20,4},{24,8},{28,12},{1,17},{... | collective-permute-start | bytes 196616 | tf_op jit(solution)/shard_map/ppermute | solution.py:24
  72.5 7.9 %collective-permute-start.35 = (bf16[16,2048]{1,0:T(8,128)(2,1)S(1)}, bf16[16,2048]{1,0:T(8,128)(2,1)S(1)}, u32[]{:S(2)}, u32[]{:S(2)}) collective-permute-start(bf16[16,2048]{1,0:T(8,128)(2,1)S(1)} %get-tuple-element.57.refs_0_), channel_id=1, source_target_pairs={{0,24},{4,28},{8,16},{12,20},{16,8},{20,12},{24,0},{28,4},{1,25},{... | collective-permute-start | bytes 196616 | tf_op jit(solution)/shard_map/ppermute | solution.py:24
  74.8 7.1 %collective-permute-start.30 = (bf16[16,2048]{1,0:T(8,128)(2,1)S(1)}, bf16[16,2048]{1,0:T(8,128)(2,1)S(1)}, u32[]{:S(2)}, u32[]{:S(2)}) collective-permute-start(bf16[16,2048]{1,0:T(8,128)(2,1)S(1)} %get-tuple-element.57.refs_0_), channel_id=1, source_target_pairs={{0,4},{4,0},{8,12},{12,8},{16,20},{20,16},{24,28},{28,24},{1,5},{5... | collective-permute-start | bytes 196616 | tf_op jit(solution)/shard_map/ppermute | solution.py:24
  76.2 5.7 %collective-permute-start.31 = (bf16[16,2048]{1,0:T(8,128)(2,1)S(1)}, bf16[16,2048]{1,0:T(8,128)(2,1)S(1)}, u32[]{:S(2)}, u32[]{:S(2)}) collective-permute-start(bf16[16,2048]{1,0:T(8,128)(2,1)S(1)} %get-tuple-element.57.refs_0_), channel_id=1, source_target_pairs={{0,8},{4,12},{8,0},{12,4},{16,24},{20,28},{24,16},{28,20},{1,9},{5... | collective-permute-start | bytes 196616 | tf_op jit(solution)/shard_map/ppermute | solution.py:24
  77.4 5.2 %collective-permute-start.32 = (bf16[16,2048]{1,0:T(8,128)(2,1)S(1)}, bf16[16,2048]{1,0:T(8,128)(2,1)S(1)}, u32[]{:S(2)}, u32[]{:S(2)}) collective-permute-start(bf16[16,2048]{1,0:T(8,128)(2,1)S(1)} %get-tuple-element.57.refs_0_), channel_id=1, source_target_pairs={{0,12},{4,8},{8,4},{12,0},{16,28},{20,24},{24,20},{28,16},{1,13},{... | collective-permute-start | bytes 196616 | tf_op jit(solution)/shard_map/ppermute | solution.py:24
  79.8 4.3 %collective-permute-start.34 = (bf16[16,2048]{1,0:T(8,128)(2,1)S(1)}, bf16[16,2048]{1,0:T(8,128)(2,1)S(1)}, u32[]{:S(2)}, u32[]{:S(2)}) collective-permute-start(bf16[16,2048]{1,0:T(8,128)(2,1)S(1)} %collective-permute-done.33.refs_4_), channel_id=1, source_target_pairs={{0,4},{4,0},{8,12},{12,8},{16,20},{20,16},{24,28},{28,24},{1,5},{5... | collective-permute-start | bytes 196616 | tf_op jit(solution)/shard_map/ppermute | solution.py:24
  80.5 4.3 %collective-permute-start.36 = (bf16[16,2048]{1,0:T(8,128)(2,1)S(1)}, bf16[16,2048]{1,0:T(8,128)(2,1)S(1)}, u32[]{:S(2)}, u32[]{:S(2)}) collective-permute-start(bf16[16,2048]{1,0:T(8,128)(2,1)S(1)} %collective-permute-done.35.refs_6_), channel_id=1, source_target_pairs={{0,4},{4,0},{8,12},{12,8},{16,20},{20,16},{24,28},{28,24},{1,5},{5... | collective-permute-start | bytes 196616 | tf_op jit(solution)/shard_map/ppermute | solution.py:24
  84.8 17.9 %slice-start.4 = ((s8[7340032]{0:T(1024)(128)(4,1)}), s8[4194304]{0:T(1024)(128)(4,1)S(1)}, s32[]{:S(2)}) async-start(s8[7340032]{0:T(1024)(128)(4,1)} %bitcast.22), calls=%async_computation.4 | async-start | bytes 8388608
  86.6 1.8 %collective-permute-start.37 = (bf16[64,1920]{1,0:T(8,128)(2,1)S(1)}, bf16[64,1920]{1,0:T(8,128)(2,1)S(1)}, u32[]{:S(2)}, u32[]{:S(2)}) collective-permute-start(bf16[64,1920]{1,0:T(8,128)(2,1)S(1)} %get-tuple-element.59), channel_id=1, source_target_pairs={{0,1},{1,0},{2,3},{3,2},{4,5},{5,4},{6,7},{7,6},{8,9},{9,8},{10,11... | collective-permute-start | bytes 737288 | tf_op jit(solution)/shard_map/ppermute | solution.py:24
  86.7 15.9 %slice-start.5 = ((s8[7340032]{0:T(1024)(128)(4,1)}), s8[3145728]{0:T(1024)(128)(4,1)S(1)}, s32[]{:S(2)}) async-start(s8[7340032]{0:T(1024)(128)(4,1)} %bitcast.22), calls=%async_computation.5 | async-start | bytes 6291456
  87.9 2.1 %collective-permute-start.39 = (bf16[64,1792]{1,0:T(8,128)(2,1)S(1)}, bf16[64,1792]{1,0:T(8,128)(2,1)S(1)}, u32[]{:S(2)}, u32[]{:S(2)}) collective-permute-start(bf16[64,1792]{1,0:T(8,128)(2,1)S(1)} %get-tuple-element.62), channel_id=1, source_target_pairs={{0,1},{1,0},{2,3},{3,2},{4,5},{5,4},{6,7},{7,6},{8,9},{9,8},{10,11... | collective-permute-start | bytes 688136 | tf_op jit(solution)/shard_map/ppermute | solution.py:24
  88.5 6.2 %collective-permute-start.38 = (bf16[32,1920]{1,0:T(8,128)(2,1)S(1)}, bf16[32,1920]{1,0:T(8,128)(2,1)S(1)}, u32[]{:S(2)}, u32[]{:S(2)}) collective-permute-start(bf16[32,1920]{1,0:T(8,128)(2,1)S(1)} %slice.118), channel_id=1, source_target_pairs={{0,2},{1,3},{2,0},{3,1},{4,6},{5,7},{6,4},{7,5},{8,10},{9,11},{10,... | collective-permute-start | bytes 368648 | tf_op jit(solution)/shard_map/ppermute | solution.py:24
  90.1 6.2 %collective-permute-start.40 = (bf16[32,1792]{1,0:T(8,128)(2,1)S(1)}, bf16[32,1792]{1,0:T(8,128)(2,1)S(1)}, u32[]{:S(2)}, u32[]{:S(2)}) collective-permute-start(bf16[32,1792]{1,0:T(8,128)(2,1)S(1)} %slice.119), channel_id=1, source_target_pairs={{0,2},{1,3},{2,0},{3,1},{4,6},{5,7},{6,4},{7,5},{8,10},{9,11},{10,... | collective-permute-start | bytes 344072 | tf_op jit(solution)/shard_map/ppermute | solution.py:24
  96.5 4.9 %collective-permute-start.42 = (bf16[32,1792]{1,0:T(8,128)(2,1)S(1)}, bf16[32,1792]{1,0:T(8,128)(2,1)S(1)}, u32[]{:S(2)}, u32[]{:S(2)}) collective-permute-start(bf16[32,1792]{1,0:T(8,128)(2,1)S(1)} %fusion.2.refs_0_), channel_id=1, source_target_pairs={{0,2},{1,3},{2,0},{3,1},{4,6},{5,7},{6,4},{7,5},{8,10},{9,11},{10,... | collective-permute-start | bytes 344072 | tf_op jit(solution)/shard_map/ppermute | solution.py:24
  98.0 3.4 %collective-permute-start.41 = (bf16[32,1792]{1,0:T(8,128)(2,1)S(1)}, bf16[32,1792]{1,0:T(8,128)(2,1)S(1)}, u32[]{:S(2)}, u32[]{:S(2)}) collective-permute-start(bf16[32,1792]{1,0:T(8,128)(2,1)S(1)} %fusion.2.refs_0_), channel_id=1, source_target_pairs={{0,1},{1,0},{2,3},{3,2},{4,5},{5,4},{6,7},{7,6},{8,9},{9,8},{10,11... | collective-permute-start | bytes 344072 | tf_op jit(solution)/shard_map/ppermute | solution.py:24
  101.3 1.3 %collective-permute-start.43 = (bf16[32,1792]{1,0:T(8,128)(2,1)S(1)}, bf16[32,1792]{1,0:T(8,128)(2,1)S(1)}, u32[]{:S(2)}, u32[]{:S(2)}) collective-permute-start(bf16[32,1792]{1,0:T(8,128)(2,1)S(1)} %collective-permute-done.42.refs_2_), channel_id=1, source_target_pairs={{0,1},{1,0},{2,3},{3,2},{4,5},{5,4},{6,7},{7,6},{8,9},{9,8},{10,11... | collective-permute-start | bytes 344072 | tf_op jit(solution)/shard_map/ppermute | solution.py:24
  104.4 5.6 %collective-permute-start.46 = (bf16[16,2048]{1,0:T(8,128)(2,1)S(1)}, bf16[16,2048]{1,0:T(8,128)(2,1)S(1)}, u32[]{:S(2)}, u32[]{:S(2)}) collective-permute-start(bf16[16,2048]{1,0:T(8,128)(2,1)S(1)} %get-tuple-element.66), channel_id=1, source_target_pairs={{0,4},{4,0},{8,12},{12,8},{16,20},{20,16},{24,28},{28,24},{1,5},{5... | collective-permute-start | bytes 196616 | tf_op jit(solution)/shard_map/ppermute | solution.py:24
  105.8 6.0 %collective-permute-start.44 = (bf16[16,2048]{1,0:T(8,128)(2,1)S(1)}, bf16[16,2048]{1,0:T(8,128)(2,1)S(1)}, u32[]{:S(2)}, u32[]{:S(2)}) collective-permute-start(bf16[16,2048]{1,0:T(8,128)(2,1)S(1)} %get-tuple-element.65), channel_id=1, source_target_pairs={{0,4},{4,0},{8,12},{12,8},{16,20},{20,16},{24,28},{28,24},{1,5},{5... | collective-permute-start | bytes 196616 | tf_op jit(solution)/shard_map/ppermute | solution.py:24
  106.5 5.8 %collective-permute-start.48 = (bf16[16,2048]{1,0:T(8,128)(2,1)S(1)}, bf16[16,2048]{1,0:T(8,128)(2,1)S(1)}, u32[]{:S(2)}, u32[]{:S(2)}) collective-permute-start(bf16[16,2048]{1,0:T(8,128)(2,1)S(1)} %get-tuple-element.67), channel_id=1, source_target_pairs={{0,4},{4,0},{8,12},{12,8},{16,20},{20,16},{24,28},{28,24},{1,5},{5... | collective-permute-start | bytes 196616 | tf_op jit(solution)/shard_map/ppermute | solution.py:24
  107.8 4.5 %collective-permute-start.49 = (bf16[16,2048]{1,0:T(8,128)(2,1)S(1)}, bf16[16,2048]{1,0:T(8,128)(2,1)S(1)}, u32[]{:S(2)}, u32[]{:S(2)}) collective-permute-start(bf16[16,2048]{1,0:T(8,128)(2,1)S(1)} %get-tuple-element.68), channel_id=1, source_target_pairs={{0,8},{4,12},{8,0},{12,4},{16,24},{20,28},{24,16},{28,20},{1,9},{5... | collective-permute-start | bytes 196616 | tf_op jit(solution)/shard_map/ppermute | solution.py:24
  107.8 5.2 %collective-permute-start.50 = (bf16[16,2048]{1,0:T(8,128)(2,1)S(1)}, bf16[16,2048]{1,0:T(8,128)(2,1)S(1)}, u32[]{:S(2)}, u32[]{:S(2)}) collective-permute-start(bf16[16,2048]{1,0:T(8,128)(2,1)S(1)} %get-tuple-element.69), channel_id=1, source_target_pairs={{0,12},{4,8},{8,4},{12,0},{16,28},{20,24},{24,20},{28,16},{1,13},{... | collective-permute-start | bytes 196616 | tf_op jit(solution)/shard_map/ppermute | solution.py:24
  110.0 6.1 %collective-permute-start.47 = (bf16[16,2048]{1,0:T(8,128)(2,1)S(1)}, bf16[16,2048]{1,0:T(8,128)(2,1)S(1)}, u32[]{:S(2)}, u32[]{:S(2)}) collective-permute-start(bf16[16,2048]{1,0:T(8,128)(2,1)S(1)} %shard_map.163), channel_id=1, source_target_pairs={{0,24},{4,28},{8,16},{12,20},{16,8},{20,12},{24,0},{28,4},{1,25},{... | collective-permute-start | bytes 196616 | tf_op jit(solution)/shard_map/ppermute | solution.py:24
  111.8 6.6 %collective-permute-start.45 = (bf16[16,2048]{1,0:T(8,128)(2,1)S(1)}, bf16[16,2048]{1,0:T(8,128)(2,1)S(1)}, u32[]{:S(2)}, u32[]{:S(2)}) collective-permute-start(bf16[16,2048]{1,0:T(8,128)(2,1)S(1)} %shard_map.162), channel_id=1, source_target_pairs={{0,16},{4,20},{8,24},{12,28},{16,0},{20,4},{24,8},{28,12},{1,17},{... | collective-permute-start | bytes 196616 | tf_op jit(solution)/shard_map/ppermute | solution.py:24
  (3 other events, 5.0 us)

commit v8 on v7

--- a/solution.py
+++ b/solution.py
@@ -106,48 +106,44 @@
         write(first, tile, jnp.dot(left, w_ref[:, first : first + tile], preferred_element_type=F32))
 
 
-def prologue(where, x_first, x_second, cache_keys, cache_values):
-    groups = lax.axis_size("dp")
+def stack_tokens(x_first, x_second):
     part_dev, features = x_first.shape
-    span = cache_keys.shape[1]
-    shape = (groups // 2, 2, part_dev, span, HD)
-
-    def body(where_ref, first_hbm, second_hbm, keys_hbm, values_hbm, x_ref, keep_ref, send_ref, *refs):
-        one, two, keys_ref, values_ref, sems = refs
-        pairs = ((first_hbm, one), (second_hbm, two), (keys_hbm, keys_ref), (values_hbm, values_ref))
-        copies = [pltpu.make_async_copy(src, dst, sems.at[i]) for i, (src, dst) in enumerate(pairs)]
+
+    def body(first_ref, second_ref, out_ref, one, two, sems):
+        copies = [pltpu.make_async_copy(first_ref, one, sems.at[0]), pltpu.make_async_copy(second_ref, two, sems.at[1])]
         for copy in copies:
             copy.start()
-        for copy in copies[:2]:
+        for copy in copies:
             copy.wait()
-        x_ref[...] = jnp.concatenate([one[...].astype(F32), two[...].astype(F32)], axis=0).astype(BF16)
-        for copy in copies[2:]:
-            copy.wait()
-        for k in range(groups):
-            head = lax.div((where_ref[0] ^ k) * KVH, groups)
-            lanes = pl.ds(pl.multiple_of(head * HD, HD), HD)
-            out_ref = send_ref if k % 2 else keep_ref
-            out_ref[k // 2, 0] = keys_ref[:, :, lanes]
-            out_ref[k // 2, 1] = values_ref[:, :, lanes]
+        out_ref[...] = jnp.concatenate([one[...].astype(F32), two[...].astype(F32)], axis=0).astype(BF16)
 
     return call(
         body,
-        (shaped((2 * part_dev, features)), shaped(shape), shaped(shape)),
-        (where, x_first, x_second, cache_keys, cache_values),
-        [SMEM] + [HBM] * 4,
-        [pltpu.VMEM(a.shape, BF16) for a in (x_first, x_second, cache_keys, cache_values)]
-        + [pltpu.SemaphoreType.DMA((4,))],
+        shaped((2 * part_dev, features)),
+        (x_first, x_second),
+        [HBM, HBM],
+        [pltpu.VMEM(x_first.shape, BF16), pltpu.VMEM(x_first.shape, BF16), pltpu.SemaphoreType.DMA((2,))],
         limit=None,
-        moved=8 * cache_keys.size,
-    )
-
-
-def move_cache(keep, send):
-    groups = lax.axis_size("dp")
-    both = jnp.stack([keep, swap(send, "dp", 1)], axis=1)
-    moved = [both[:1]] + [swap(both[i : i + 1], "dp", 2 * i) for i in range(groups // 2 - 1, 0, -1)][::-1]
-    both = jnp.concatenate(moved)
-    return gather_blocks(both.reshape(groups * 2 * both.shape[3], *both.shape[4:]))
+    )
+
+
+def pack(cache_keys, cache_values, after):
+    groups = lax.axis_size("dp")
+    part_dev, span, _ = cache_keys.shape
+
+    def body(keys_ref, values_ref, after_ref, out_ref):
+        for g in range(groups):
+            first = g * KVH // groups * HD
+            out_ref[g, 0] = keys_ref[:, :, first : first + HD]
+            out_ref[g, 1] = values_ref[:, :, first : first + HD]
+
+    return call(
+        body,
+        shaped((groups, 2, part_dev, span, HD)),
+        (cache_keys, cache_values, after),
+        [VMEM, VMEM, ANY],
+        flops=4 * AROUND,
+    )
 
 
 def lift(where_ref, gain_ref, block_refs, h_ref, ss_ref, absolute):
@@ -398,7 +394,7 @@
     def body(where_ref, anc_ref, rope_ref, scale_ref, *refs):
         q_refs, refs = refs[: len(queries)], refs[len(queries) :]
         cache_refs, (query_ref, mixed_ref, highest_ref, total_ref, keys_ref, values_ref) = refs[:tensor], refs[tensor:]
-        d, t = where_ref[0], where_ref[1]
+        t = where_ref[1]
         query_sum = q_refs[0][...]
         for ref in q_refs[1:]:
             query_sum = query_sum + ref[...].astype(F32)
@@ -407,9 +403,9 @@
 
             def bring(i, _, step=step):
                 if step == 0:
-                    block, member = (t * near + lax.div(i, part_dev)) ^ d, lax.rem(i, part_dev)
+                    block, member = t * near + lax.div(i, part_dev), lax.rem(i, part_dev)
                 else:
-                    block, member = lax.div(anc_ref[i], part_dev) ^ d, lax.rem(anc_ref[i], part_dev)
+                    block, member = lax.div(anc_ref[i], part_dev), lax.rem(anc_ref[i], part_dev)
                 place = block * pair + member
                 for k in range(tensor):
                     start = pl.multiple_of(i * ctx + k * span, 8)
@@ -537,9 +533,10 @@
     parts = near * part_dev
     where = jnp.stack([d, t]).astype(jnp.int32)
 
-    x, keep, send = prologue(where, x_first, x_second, cache_keys, cache_values)
+    x = stack_tokens(x_first, x_second)
     blocks = gather_rows(x)
-    caches = move_cache(keep, send)
+    cache = lax.all_to_all(pack(cache_keys, cache_values, x), "dp", split_axis=0, concat_axis=0, tiled=True)
+    caches = gather_blocks(cache.reshape(groups * pair, span, HD))
 
     message, *queries = project_attention(where, blocks, attn_gain, w_keyval, w_query)
     bits = 1

time: 119 us -> 119 us (level)
  waiting for transfers between devices: 40.4 us -> 41.9 us
  other arithmetic: 2.15 us -> 0.67 us
    all_to_all x0 -> x1, starting transfers between devices: none -> 4.68 us  [local(): lax.all_to_all(pack(cache_keys, cache_values, x), 'dp', split_axis=0, con...]
    ppermute x49 -> x45, starting transfers between devices: 53.8 us -> 50 us  [swap(): return lax.ppermute(x, axis, [(i, i ^ bits) for i in range(size)])]
    ppermute x49 -> x45, waiting for transfers between devices: 40.2 us -> 40.8 us  [swap(): return lax.ppermute(x, axis, [(i, i ^ bits) for i in range(size)])]
    pallas_call x16 -> x17, Pallas kernels: 15.4 us -> 15 us  [call(): pl.pallas_call(body, out_shape=outs, in_specs=specs, out_specs=jax.tree.m...]
    unnamed x32 -> x34, local copies, waits for them, and re-layouts: 3.09 us -> 3.13 us
  transfers between devices with their start and end apart: 51 -> 48, of which waited for: 22 -> 21; matrix products, arithmetic and copies ran while one was open for 1% -> 1% of each run, Pallas kernels for 5% -> 5%
where the time goes in v8:
time: 119 us
  starting transfers between devices  56.5 us (47%)
  waiting for transfers between devices  41.9 us (35%)
  Pallas kernels  15 us (13%)
  local copies, waits for them, and re-layouts  3.48 us (3%)
    ppermute x45, starting transfers between devices, swap(): return lax.ppermute(x, axis, [(i, i ^ bits) for i in range(size)])  50 us
    ppermute x45, waiting for transfers between devices, swap(): return lax.ppermute(x, axis, [(i, i ^ bits) for i in range(size)])  40.8 us
    pallas_call x17, Pallas kernels, call(): pl.pallas_call(body, out_shape=outs, in_specs=specs, out_specs=jax.tree.m...  15 us
    all_to_all x1, starting transfers between devices, local(): lax.all_to_all(pack(cache_keys, cache_values, x), 'dp', split_axis=0, con...  4.68 us
    unnamed x34, local copies, waits for them, and re-layouts  3.13 us
  transfers between devices with their start and end apart: 48, of which 21 were waited for; matrix products, arithmetic and copies ran while one was open for 1% of the time, Pallas kernels for 5%

profile of v8, /device:TPU:0, one launch (start us, length us, event | category | flops | bytes accessed | tf_op | source)
XLA Modules:
  0.0 118.6 jit_solution(5107105401188410263)
XLA Ops:
  0.7 1.5 %shard_map.149.refs_0_.after_ref.refs_5_ = bf16[16,2048]{1,0:T(8,128)(2,1)} custom-call(bf16[8,2048]{1,0:T(8,128)(2,1)} %first_ref.1, bf16[8,2048]{1,0:T(8,128)(2,1)} %second_ref.1), custom_call_target="tpu_custom_call" | custom-call | flops 5368709120 | tf_op jit(solution)/shard_map/pallas_call | solution.py:45
  2.2 4.1 %collective-permute-start.3 = (bf16[16,2048]{1,0:T(8,128)(2,1)}, bf16[16,2048]{1,0:T(8,128)(2,1)S(1)}, u32[]{:S(2)}, u32[]{:S(2)}) collective-permute-start(bf16[16,2048]{1,0:T(8,128)(2,1)} %shard_map.149.refs_0_.after_ref.refs_5_), channel_id=1, source_target_pairs={{0,16},{4,20},{8,24},{12,28},{16,0},{20,4},{24,8},{28,12},{1,17},{... | collective-permute-start | bytes 196616 | tf_op jit(solution)/shard_map/ppermute | solution.py:24
  6.3 1.3 %collective-permute-start.5 = (bf16[16,2048]{1,0:T(8,128)(2,1)}, bf16[16,2048]{1,0:T(8,128)(2,1)S(1)}, u32[]{:S(2)}, u32[]{:S(2)}) collective-permute-start(bf16[16,2048]{1,0:T(8,128)(2,1)} %shard_map.149.refs_0_.after_ref.refs_5_), channel_id=1, source_target_pairs={{0,24},{4,28},{8,16},{12,20},{16,8},{20,12},{24,0},{28,4},{1,25},{... | collective-permute-start | bytes 196616 | tf_op jit(solution)/shard_map/ppermute | solution.py:24
  7.6 1.5 %collective-permute-start = (bf16[16,2048]{1,0:T(8,128)(2,1)}, bf16[16,2048]{1,0:T(8,128)(2,1)S(1)}, u32[]{:S(2)}, u32[]{:S(2)}) collective-permute-start(bf16[16,2048]{1,0:T(8,128)(2,1)} %shard_map.149.refs_0_.after_ref.refs_5_), channel_id=1, source_target_pairs={{0,4},{4,0},{8,12},{12,8},{16,20},{20,16},{24,28},{28,24},{1,5},{5... | collective-permute-start | bytes 196616 | tf_op jit(solution)/shard_map/ppermute | solution.py:24
  9.3 1.8 %collective-permute-start.2 = (bf16[16,2048]{1,0:T(8,128)(2,1)}, bf16[16,2048]{1,0:T(8,128)(2,1)S(1)}, u32[]{:S(2)}, u32[]{:S(2)}) collective-permute-start(bf16[16,2048]{1,0:T(8,128)(2,1)} %shard_map.149.refs_0_.after_ref.refs_5_), channel_id=1, source_target_pairs={{0,12},{4,8},{8,4},{12,0},{16,28},{20,24},{24,20},{28,16},{1,13},{... | collective-permute-start | bytes 196616 | tf_op jit(solution)/shard_map/ppermute | solution.py:24
  11.1 0.9 copy-done.5
  12.0 0.8 shard_map.153
  12.8 4.7 %all-to-all-start = ((bf16[8,2,8,8,128]{4,3,2,1,0:T(8,128)(2,1)}), bf16[8,2,8,8,128]{4,3,2,1,0:T(8,128)(2,1)S(1)}, u32[]{:S(2)}, u32[]{:S(2)}) async-start(bf16[8,2,8,8,128]{4,3,2,1,0:T(8,128)(2,1)} %shard_map.153), calls=%async_computation | async-start | bytes 524288 | tf_op jit(solution)/shard_map/all_to_all | solution.py:538
  17.7 2.1 %collective-permute-start.4 = (bf16[16,2048]{1,0:T(8,128)(2,1)S(1)}, bf16[16,2048]{1,0:T(8,128)(2,1)S(1)}, u32[]{:S(2)}, u32[]{:S(2)}) collective-permute-start(bf16[16,2048]{1,0:T(8,128)(2,1)S(1)} %collective-permute-done.3.refs_4_), channel_id=1, source_target_pairs={{0,4},{4,0},{8,12},{12,8},{16,20},{20,16},{24,28},{28,24},{1,5},{5... | collective-permute-start | bytes 196616 | tf_op jit(solution)/shard_map/ppermute | solution.py:24
  20.0 2.2 %collective-permute-done.4.refs_5_ = bf16[16,2048]{1,0:T(8,128)(2,1)S(1)} collective-permute-done((bf16[16,2048]{1,0:T(8,128)(2,1)S(1)}, bf16[16,2048]{1,0:T(8,128)(2,1)S(1)}, u32[]{:S(2)}, u32[]{:S(2)}) %collective-permute-start.4) | collective-permute-done | bytes 65568 | tf_op jit(solution)/shard_map/ppermute | solution.py:24
  22.2 2.1 %collective-permute-done.6.refs_7_ = bf16[16,2048]{1,0:T(8,128)(2,1)S(1)} collective-permute-done((bf16[16,2048]{1,0:T(8,128)(2,1)S(1)}, bf16[16,2048]{1,0:T(8,128)(2,1)S(1)}, u32[]{:S(2)}, u32[]{:S(2)}) %collective-permute-start.6) | collective-permute-done | bytes 65568 | tf_op jit(solution)/shard_map/ppermute | solution.py:24
  24.4 2.2 %copy-done = bf16[2048,1024]{1,0:T(8,128)(2,1)S(1)} copy-done((bf16[2048,1024]{1,0:T(8,128)(2,1)S(1)}, bf16[2048,1024]{1,0:T(8,128)(2,1)}, u32[]{:S(2)}) %copy-start) | copy-done | bytes 4194328
  26.6 1.5 %shard_map.150 = (bf16[128,384]{1,0:T(8,128)(2,1)S(1)}, f32[64,1024]{1,0:T(8,128)S(1)}, bf16[64,1024]{1,0:T(8,128)(2,1)S(1)}) custom-call(s32[2]{0:T(128)S(1)} %pad_add_fusion.3.where_ref, f32[1,2048]{1,0:T(1,128)S(1)} %bitcast.22, bf16[16,2048]{1,0:T(8,128)(2,1)S(1)} %copy-done.6, bf16[16,2048]{1,0:T(8,128)(2,1)S(1)} %collective-permute-done.refs_1_, ...), custom_call_target="tpu_custom_call" | custom-call | flops 6039797760 | bytes 6291456 | tf_op jit(solution)/shard_map/pallas_call | solution.py:45
  28.9 1.5 %collective-permute-start.14 = (bf16[128,8,128]{2,1,0:T(8,128)(2,1)S(1)}, bf16[128,8,128]{2,1,0:T(8,128)(2,1)S(1)}, u32[]{:S(2)}, u32[]{:S(2)}) collective-permute-start(bf16[128,8,128]{2,1,0:T(8,128)(2,1)S(1)} %bitcast.13), channel_id=1, source_target_pairs={{0,2},{1,3},{2,0},{3,1},{4,6},{5,7},{6,4},{7,5},{8,10},{9,11},{10,... | collective-permute-start | bytes 786440 | tf_op jit(solution)/shard_map/ppermute | solution.py:24
  30.6 0.6 collective-permute-start.8
  31.3 1.5 %collective-permute-start.12 = (bf16[32,1024]{1,0:T(8,128)(2,1)S(1)}, bf16[32,1024]{1,0:T(8,128)(2,1)S(1)}, u32[]{:S(2)}, u32[]{:S(2)}) collective-permute-start(bf16[32,1024]{1,0:T(8,128)(2,1)S(1)} %slice.80), channel_id=1, source_target_pairs={{0,2},{1,3},{2,0},{3,1},{4,6},{5,7},{6,4},{7,5},{8,10},{9,11},{10,... | collective-permute-start | bytes 196616 | tf_op jit(solution)/shard_map/ppermute | solution.py:24
  32.8 5.2 %collective-permute-done.14.refs_4_ = bf16[128,8,128]{2,1,0:T(8,128)(2,1)S(1)} collective-permute-done((bf16[128,8,128]{2,1,0:T(8,128)(2,1)S(1)}, bf16[128,8,128]{2,1,0:T(8,128)(2,1)S(1)}, u32[]{:S(2)}, u32[]{:S(2)}) %collective-permute-start.14) | collective-permute-done | bytes 262176 | tf_op jit(solution)/shard_map/ppermute | solution.py:24
  38.1 1.9 %collective-permute-done.8.arrived_ref = bf16[128,384]{1,0:T(8,128)(2,1)S(1)} collective-permute-done((bf16[128,384]{1,0:T(8,128)(2,1)S(1)}, bf16[128,384]{1,0:T(8,128)(2,1)S(1)}, u32[]{:S(2)}, u32[]{:S(2)}) %collective-permute-start.8) | collective-permute-done | bytes 98336 | tf_op jit(solution)/shard_map/ppermute | solution.py:24
  40.0 0.7 shard_map.152
  40.7 1.2 collective-permute-start.10
  41.9 0.7 collective-permute-start.9
  42.6 1.9 %shard_map.154 = (bf16[256,128]{1,0:T(8,128)(2,1)S(1)}, f32[256,128]{1,0:T(8,128)S(1)}, f32[256,128]{1,0:T(8,128)S(1)}, f32[256,128]{1,0:T(8,128)S(1)}) custom-call(s32[2]{0:T(128)S(1)} %pad_add_fusion.3.where_ref, s32[16]{0:T(128)S(1)} %get-tuple-element.65.anc_ref, f32[4,128]{1,0:T(4,128)S(1)} %copy-done.9, f32[128,128]{1,0:T(8,128)S(1)} %get-tuple-element.36.scale_ref, ...), custom_call_target="tpu_custom_call" | custom-call | flops 5368709120 | bytes 4194304 | tf_op jit(solution)/shard_map/pallas_call | solution.py:45
  44.5 1.1 collective-permute-done.10.two_ref
  45.6 1.1 shard_map.155.refs_0_
  46.7 1.6 %collective-permute-start.17 = (bf16[32,1024]{1,0:T(8,128)(2,1)S(1)}, bf16[32,1024]{1,0:T(8,128)(2,1)S(1)}, u32[]{:S(2)}, u32[]{:S(2)}) collective-permute-start(bf16[32,1024]{1,0:T(8,128)(2,1)S(1)} %shard_map.155.refs_0_), channel_id=1, source_target_pairs={{0,2},{1,3},{2,0},{3,1},{4,6},{5,7},{6,4},{7,5},{8,10},{9,11},{10,... | collective-permute-start | bytes 196616 | tf_op jit(solution)/shard_map/ppermute | solution.py:24
  48.3 2.7 %collective-permute-done.17.refs_2_ = bf16[32,1024]{1,0:T(8,128)(2,1)S(1)} collective-permute-done((bf16[32,1024]{1,0:T(8,128)(2,1)S(1)}, bf16[32,1024]{1,0:T(8,128)(2,1)S(1)}, u32[]{:S(2)}, u32[]{:S(2)}) %collective-permute-start.17) | collective-permute-done | bytes 65568 | tf_op jit(solution)/shard_map/ppermute | solution.py:24
  51.1 1.2 %collective-permute-done.18.refs_3_ = bf16[32,1024]{1,0:T(8,128)(2,1)S(1)} collective-permute-done((bf16[32,1024]{1,0:T(8,128)(2,1)S(1)}, bf16[32,1024]{1,0:T(8,128)(2,1)S(1)}, u32[]{:S(2)}, u32[]{:S(2)}) %collective-permute-start.18) | collective-permute-done | bytes 65568 | tf_op jit(solution)/shard_map/ppermute | solution.py:24
  52.3 1.3 %shard_map.156 = (f32[16,2048]{1,0:T(8,128)S(1)}, bf16[16,2048]{1,0:T(8,128)(2,1)S(1)}, bf16[16,2048]{1,0:T(8,128)(2,1)S(1)}, bf16[16,2048]{1,0:T(8,128)(2,1)S(1...) custom-call(s32[2]{0:T(128)S(1)} %pad_add_fusion.3.where_ref, ...), custom_call_target="tpu_custom_call" | custom-call | flops 5905580032 | bytes 4194304 | tf_op jit(solution)/shard_map/pallas_call | solution.py:45
  53.6 4.7 %collective-permute-start.21 = (bf16[16,2048]{1,0:T(8,128)(2,1)S(1)}, bf16[16,2048]{1,0:T(8,128)(2,1)S(1)}, u32[]{:S(2)}, u32[]{:S(2)}) collective-permute-start(bf16[16,2048]{1,0:T(8,128)(2,1)S(1)} %get-tuple-element.46), channel_id=1, source_target_pairs={{0,4},{4,0},{8,12},{12,8},{16,20},{20,16},{24,28},{28,24},{1,5},{5... | collective-permute-start | bytes 196616 | tf_op jit(solution)/shard_map/ppermute | solution.py:24
  58.4 1.9 %collective-permute-start.23 = (bf16[16,2048]{1,0:T(8,128)(2,1)S(1)}, bf16[16,2048]{1,0:T(8,128)(2,1)S(1)}, u32[]{:S(2)}, u32[]{:S(2)}) collective-permute-start(bf16[16,2048]{1,0:T(8,128)(2,1)S(1)} %get-tuple-element.47), channel_id=1, source_target_pairs={{0,4},{4,0},{8,12},{12,8},{16,20},{20,16},{24,28},{28,24},{1,5},{5... | collective-permute-start | bytes 196616 | tf_op jit(solution)/shard_map/ppermute | solution.py:24
  60.3 0.9 collective-permute-start.24
  61.2 0.6 collective-permute-start.25
  61.9 4.1 %collective-permute-start.22 = (bf16[16,2048]{1,0:T(8,128)(2,1)S(1)}, bf16[16,2048]{1,0:T(8,128)(2,1)S(1)}, u32[]{:S(2)}, u32[]{:S(2)}) collective-permute-start(bf16[16,2048]{1,0:T(8,128)(2,1)S(1)} %shard_map.158), channel_id=1, source_target_pairs={{0,24},{4,28},{8,16},{12,20},{16,8},{20,12},{24,0},{28,4},{1,25},{... | collective-permute-start | bytes 196616 | tf_op jit(solution)/shard_map/ppermute | solution.py:24
  66.4 2.8 %collective-permute-done.22.refs_1_ = bf16[16,2048]{1,0:T(8,128)(2,1)S(1)} collective-permute-done((bf16[16,2048]{1,0:T(8,128)(2,1)S(1)}, bf16[16,2048]{1,0:T(8,128)(2,1)S(1)}, u32[]{:S(2)}, u32[]{:S(2)}) %collective-permute-start.22) | collective-permute-done | bytes 65568 | tf_op jit(solution)/shard_map/ppermute | solution.py:24
  69.3 2.0 %collective-permute-done.20.refs_0_ = bf16[16,2048]{1,0:T(8,128)(2,1)S(1)} collective-permute-done((bf16[16,2048]{1,0:T(8,128)(2,1)S(1)}, bf16[16,2048]{1,0:T(8,128)(2,1)S(1)}, u32[]{:S(2)}, u32[]{:S(2)}) %collective-permute-start.20) | collective-permute-done | bytes 65568 | tf_op jit(solution)/shard_map/ppermute | solution.py:24
  71.3 0.7 shard_map.159
  72.0 0.9 collective-permute-start.29
  72.9 1.6 %collective-permute-start.31 = (bf16[16,2048]{1,0:T(8,128)(2,1)S(1)}, bf16[16,2048]{1,0:T(8,128)(2,1)S(1)}, u32[]{:S(2)}, u32[]{:S(2)}) collective-permute-start(bf16[16,2048]{1,0:T(8,128)(2,1)S(1)} %get-tuple-element.51.refs_0_), channel_id=1, source_target_pairs={{0,24},{4,28},{8,16},{12,20},{16,8},{20,12},{24,0},{28,4},{1,25},{... | collective-permute-start | bytes 196616 | tf_op jit(solution)/shard_map/ppermute | solution.py:24
  74.5 0.7 collective-permute-start.26
  75.2 1.3 %collective-permute-start.27 = (bf16[16,2048]{1,0:T(8,128)(2,1)S(1)}, bf16[16,2048]{1,0:T(8,128)(2,1)S(1)}, u32[]{:S(2)}, u32[]{:S(2)}) collective-permute-start(bf16[16,2048]{1,0:T(8,128)(2,1)S(1)} %get-tuple-element.51.refs_0_), channel_id=1, source_target_pairs={{0,8},{4,12},{8,0},{12,4},{16,24},{20,28},{24,16},{28,20},{1,9},{5... | collective-permute-start | bytes 196616 | tf_op jit(solution)/shard_map/ppermute | solution.py:24
  76.5 1.5 %collective-permute-start.28 = (bf16[16,2048]{1,0:T(8,128)(2,1)S(1)}, bf16[16,2048]{1,0:T(8,128)(2,1)S(1)}, u32[]{:S(2)}, u32[]{:S(2)}) collective-permute-start(bf16[16,2048]{1,0:T(8,128)(2,1)S(1)} %get-tuple-element.51.refs_0_), channel_id=1, source_target_pairs={{0,12},{4,8},{8,4},{12,0},{16,28},{20,24},{24,20},{28,16},{1,13},{... | collective-permute-start | bytes 196616 | tf_op jit(solution)/shard_map/ppermute | solution.py:24
  78.3 2.0 %collective-permute-start.30 = (bf16[16,2048]{1,0:T(8,128)(2,1)S(1)}, bf16[16,2048]{1,0:T(8,128)(2,1)S(1)}, u32[]{:S(2)}, u32[]{:S(2)}) collective-permute-start(bf16[16,2048]{1,0:T(8,128)(2,1)S(1)} %collective-permute-done.29.refs_4_), channel_id=1, source_target_pairs={{0,4},{4,0},{8,12},{12,8},{16,20},{20,16},{24,28},{28,24},{1,5},{5... | collective-permute-start | bytes 196616 | tf_op jit(solution)/shard_map/ppermute | solution.py:24
  80.4 1.4 %collective-permute-done.28.refs_3_ = bf16[16,2048]{1,0:T(8,128)(2,1)S(1)} collective-permute-done((bf16[16,2048]{1,0:T(8,128)(2,1)S(1)}, bf16[16,2048]{1,0:T(8,128)(2,1)S(1)}, u32[]{:S(2)}, u32[]{:S(2)}) %collective-permute-start.28) | collective-permute-done | bytes 65568 | tf_op jit(solution)/shard_map/ppermute | solution.py:24
  81.8 1.4 %collective-permute-done.30.refs_5_ = bf16[16,2048]{1,0:T(8,128)(2,1)S(1)} collective-permute-done((bf16[16,2048]{1,0:T(8,128)(2,1)S(1)}, bf16[16,2048]{1,0:T(8,128)(2,1)S(1)}, u32[]{:S(2)}, u32[]{:S(2)}) %collective-permute-start.30) | collective-permute-done | bytes 65568 | tf_op jit(solution)/shard_map/ppermute | solution.py:24
  83.2 1.4 %collective-permute-done.32.refs_7_ = bf16[16,2048]{1,0:T(8,128)(2,1)S(1)} collective-permute-done((bf16[16,2048]{1,0:T(8,128)(2,1)S(1)}, bf16[16,2048]{1,0:T(8,128)(2,1)S(1)}, u32[]{:S(2)}, u32[]{:S(2)}) %collective-permute-start.32) | collective-permute-done | bytes 65568 | tf_op jit(solution)/shard_map/ppermute | solution.py:24
  84.7 1.8 %shard_map.160 = (bf16[128,2048]{1,0:T(8,128)(2,1)S(1)}, f32[64,1920]{1,0:T(8,128)S(1)}, bf16[64,1920]{1,0:T(8,128)(2,1)S(1)}) custom-call(s32[2]{0:T(128)S(1)} %pad_add_fusion.3.where_ref, f32[1,2048]{1,0:T(1,128)S(1)} %bitcast.23, bf16[16,2048]{1,0:T(8,128)(2,1)S(1)} %get-tuple-element.51.refs_0_, bf16[16,2048]{1,0:T(8,128)(2,1)S(1)} %collective-permute-done.26.refs_1_, ...), custom_call_target="tpu_custom_call" | custom-call | flops 6308233216 | bytes 8388608 | tf_op jit(solution)/shard_map/pallas_call | solution.py:45
  86.6 1.1 shard_map.161
  88.4 1.6 %collective-permute-start.34 = (bf16[32,1920]{1,0:T(8,128)(2,1)S(1)}, bf16[32,1920]{1,0:T(8,128)(2,1)S(1)}, u32[]{:S(2)}, u32[]{:S(2)}) collective-permute-start(bf16[32,1920]{1,0:T(8,128)(2,1)S(1)} %slice.78), channel_id=1, source_target_pairs={{0,2},{1,3},{2,0},{3,1},{4,6},{5,7},{6,4},{7,5},{8,10},{9,11},{10,... | collective-permute-start | bytes 368648 | tf_op jit(solution)/shard_map/ppermute | solution.py:24
  90.0 1.1 collective-permute-start.36
  91.1 3.5 %collective-permute-done.34 = bf16[32,1920]{1,0:T(8,128)(2,1)S(1)} collective-permute-done((bf16[32,1920]{1,0:T(8,128)(2,1)S(1)}, bf16[32,1920]{1,0:T(8,128)(2,1)S(1)}, u32[]{:S(2)}, u32[]{:S(2)}) %collective-permute-start.34) | collective-permute-done | bytes 122912 | tf_op jit(solution)/shard_map/ppermute | solution.py:24
  94.8 1.3 %collective-permute-done.36 = bf16[32,1792]{1,0:T(8,128)(2,1)S(1)} collective-permute-done((bf16[32,1792]{1,0:T(8,128)(2,1)S(1)}, bf16[32,1792]{1,0:T(8,128)(2,1)S(1)}, u32[]{:S(2)}, u32[]{:S(2)}) %collective-permute-start.36) | collective-permute-done | bytes 114720 | tf_op jit(solution)/shard_map/ppermute | solution.py:24
  96.3 1.6 %collective-permute-start.38 = (bf16[32,1792]{1,0:T(8,128)(2,1)S(1)}, bf16[32,1792]{1,0:T(8,128)(2,1)S(1)}, u32[]{:S(2)}, u32[]{:S(2)}) collective-permute-start(bf16[32,1792]{1,0:T(8,128)(2,1)S(1)} %fusion.2.refs_0_), channel_id=1, source_target_pairs={{0,2},{1,3},{2,0},{3,1},{4,6},{5,7},{6,4},{7,5},{8,10},{9,11},{10,... | collective-permute-start | bytes 344072 | tf_op jit(solution)/shard_map/ppermute | solution.py:24
  97.9 3.3 %collective-permute-done.38.refs_2_ = bf16[32,1792]{1,0:T(8,128)(2,1)S(1)} collective-permute-done((bf16[32,1792]{1,0:T(8,128)(2,1)S(1)}, bf16[32,1792]{1,0:T(8,128)(2,1)S(1)}, u32[]{:S(2)}, u32[]{:S(2)}) %collective-permute-start.38) | collective-permute-done | bytes 114720 | tf_op jit(solution)/shard_map/ppermute | solution.py:24
  101.2 1.3 %collective-permute-done.39.refs_3_ = bf16[32,1792]{1,0:T(8,128)(2,1)S(1)} collective-permute-done((bf16[32,1792]{1,0:T(8,128)(2,1)S(1)}, bf16[32,1792]{1,0:T(8,128)(2,1)S(1)}, u32[]{:S(2)}, u32[]{:S(2)}) %collective-permute-start.39) | collective-permute-done | bytes 114720 | tf_op jit(solution)/shard_map/ppermute | solution.py:24
  102.5 1.7 %shard_map.162 = (f32[16,2048]{1,0:T(8,128)S(1)}, bf16[16,2048]{1,0:T(8,128)(2,1)S(1)}, bf16[16,2048]{1,0:T(8,128)(2,1)S(1)}, bf16[16,2048]{1,0:T(8,128)(2,1)S(1...) custom-call(s32[2]{0:T(128)S(1)} %pad_add_fusion.3.where_ref, ...), custom_call_target="tpu_custom_call" | custom-call | flops 6308233216 | bytes 7340032 | tf_op jit(solution)/shard_map/pallas_call | solution.py:45
  104.2 0.8 collective-permute-start.42
  105.0 1.3 %collective-permute-start.40 = (bf16[16,2048]{1,0:T(8,128)(2,1)S(1)}, bf16[16,2048]{1,0:T(8,128)(2,1)S(1)}, u32[]{:S(2)}, u32[]{:S(2)}) collective-permute-start(bf16[16,2048]{1,0:T(8,128)(2,1)S(1)} %get-tuple-element.59), channel_id=1, source_target_pairs={{0,4},{4,0},{8,12},{12,8},{16,20},{20,16},{24,28},{28,24},{1,5},{5... | collective-permute-start | bytes 196616 | tf_op jit(solution)/shard_map/ppermute | solution.py:24
  106.3 0.7 collective-permute-start.44
  107.6 2.2 %collective-permute-start.46 = (bf16[16,2048]{1,0:T(8,128)(2,1)S(1)}, bf16[16,2048]{1,0:T(8,128)(2,1)S(1)}, u32[]{:S(2)}, u32[]{:S(2)}) collective-permute-start(bf16[16,2048]{1,0:T(8,128)(2,1)S(1)} %get-tuple-element.63), channel_id=1, source_target_pairs={{0,12},{4,8},{8,4},{12,0},{16,28},{20,24},{24,20},{28,16},{1,13},{... | collective-permute-start | bytes 196616 | tf_op jit(solution)/shard_map/ppermute | solution.py:24
  109.8 2.0 %collective-permute-start.43 = (bf16[16,2048]{1,0:T(8,128)(2,1)S(1)}, bf16[16,2048]{1,0:T(8,128)(2,1)S(1)}, u32[]{:S(2)}, u32[]{:S(2)}) collective-permute-start(bf16[16,2048]{1,0:T(8,128)(2,1)S(1)} %shard_map.164), channel_id=1, source_target_pairs={{0,24},{4,28},{8,16},{12,20},{16,8},{20,12},{24,0},{28,4},{1,25},{... | collective-permute-start | bytes 196616 | tf_op jit(solution)/shard_map/ppermute | solution.py:24
  112.0 0.8 collective-permute-done.46.refs_4_
  112.8 3.2 %collective-permute-done.43.refs_1_ = bf16[16,2048]{1,0:T(8,128)(2,1)S(1)} collective-permute-done((bf16[16,2048]{1,0:T(8,128)(2,1)S(1)}, bf16[16,2048]{1,0:T(8,128)(2,1)S(1)}, u32[]{:S(2)}, u32[]{:S(2)}) %collective-permute-start.43) | collective-permute-done | bytes 65568 | tf_op jit(solution)/shard_map/ppermute | solution.py:24
  116.0 1.9 %collective-permute-done.41.refs_0_ = bf16[16,2048]{1,0:T(8,128)(2,1)S(1)} collective-permute-done((bf16[16,2048]{1,0:T(8,128)(2,1)S(1)}, bf16[16,2048]{1,0:T(8,128)(2,1)S(1)}, u32[]{:S(2)}, u32[]{:S(2)}) %collective-permute-start.41) | collective-permute-done | bytes 65568 | tf_op jit(solution)/shard_map/ppermute | solution.py:24
  117.9 0.7 shard_map.165
  (107 shorter events, 4.5 us)
Async XLA Ops:
  0.6 10.5 %copy-start.3 = (bf16[8,8,1024]{2,1,0:T(8,128)(2,1)S(1)}, bf16[8,8,1024]{2,1,0:T(8,128)(2,1)}, u32[]{:S(2)}) copy-start(bf16[8,8,1024]{2,1,0:T(8,128)(2,1)} %keys_ref.1) | copy-start | bytes 393220
  0.6 10.5 %copy-start.4 = (bf16[8,8,1024]{2,1,0:T(8,128)(2,1)S(1)}, bf16[8,8,1024]{2,1,0:T(8,128)(2,1)}, u32[]{:S(2)}) copy-start(bf16[8,8,1024]{2,1,0:T(8,128)(2,1)} %values_ref.1) | copy-start | bytes 393220
  0.7 16.8 %copy-start.10 = (s32[64]{0:T(128)S(1)}, s32[64]{0:T(128)}, u32[]{:S(2)}) copy-start(s32[64]{0:T(128)} %param.18) | copy-start | bytes 772
  0.7 23.7 %copy-start.7 = (f32[2048]{0:T(1024)S(1)}, f32[2048]{0:T(1024)}, u32[]{:S(2)}) copy-start(f32[2048]{0:T(1024)} %param.19) | copy-start | bytes 24580
  2.2 22.2 %copy-start.2 = (bf16[2048,256]{1,0:T(8,128)(2,1)S(1)}, bf16[2048,256]{1,0:T(8,128)(2,1)}, u32[]{:S(2)}) copy-start(bf16[2048,256]{1,0:T(8,128)(2,1)} %refs_8_.2) | copy-start | bytes 3145732
  2.2 15.6 %collective-permute-start.3 = (bf16[16,2048]{1,0:T(8,128)(2,1)}, bf16[16,2048]{1,0:T(8,128)(2,1)S(1)}, u32[]{:S(2)}, u32[]{:S(2)}) collective-permute-start(bf16[16,2048]{1,0:T(8,128)(2,1)} %shard_map.149.refs_0_.after_ref.refs_5_), channel_id=1, source_target_pairs={{0,16},{4,20},{8,24},{12,28},{16,0},{20,4},{24,8},{28,12},{1,17},{... | collective-permute-start | bytes 196616 | tf_op jit(solution)/shard_map/ppermute | solution.py:24
  6.3 13.6 %collective-permute-start.5 = (bf16[16,2048]{1,0:T(8,128)(2,1)}, bf16[16,2048]{1,0:T(8,128)(2,1)S(1)}, u32[]{:S(2)}, u32[]{:S(2)}) collective-permute-start(bf16[16,2048]{1,0:T(8,128)(2,1)} %shard_map.149.refs_0_.after_ref.refs_5_), channel_id=1, source_target_pairs={{0,24},{4,28},{8,16},{12,20},{16,8},{20,12},{24,0},{28,4},{1,25},{... | collective-permute-start | bytes 196616 | tf_op jit(solution)/shard_map/ppermute | solution.py:24
  7.6 12.4 %collective-permute-start = (bf16[16,2048]{1,0:T(8,128)(2,1)}, bf16[16,2048]{1,0:T(8,128)(2,1)S(1)}, u32[]{:S(2)}, u32[]{:S(2)}) collective-permute-start(bf16[16,2048]{1,0:T(8,128)(2,1)} %shard_map.149.refs_0_.after_ref.refs_5_), channel_id=1, source_target_pairs={{0,4},{4,0},{8,12},{12,8},{16,20},{20,16},{24,28},{28,24},{1,5},{5... | collective-permute-start | bytes 196616 | tf_op jit(solution)/shard_map/ppermute | solution.py:24
  9.1 10.9 %collective-permute-start.1 = (bf16[16,2048]{1,0:T(8,128)(2,1)}, bf16[16,2048]{1,0:T(8,128)(2,1)S(1)}, u32[]{:S(2)}, u32[]{:S(2)}) collective-permute-start(bf16[16,2048]{1,0:T(8,128)(2,1)} %shard_map.149.refs_0_.after_ref.refs_5_), channel_id=1, source_target_pairs={{0,8},{4,12},{8,0},{12,4},{16,24},{20,28},{24,16},{28,20},{1,9},{5... | collective-permute-start | bytes 196616 | tf_op jit(solution)/shard_map/ppermute | solution.py:24
  9.3 10.7 %collective-permute-start.2 = (bf16[16,2048]{1,0:T(8,128)(2,1)}, bf16[16,2048]{1,0:T(8,128)(2,1)S(1)}, u32[]{:S(2)}, u32[]{:S(2)}) collective-permute-start(bf16[16,2048]{1,0:T(8,128)(2,1)} %shard_map.149.refs_0_.after_ref.refs_5_), channel_id=1, source_target_pairs={{0,12},{4,8},{8,4},{12,0},{16,28},{20,24},{24,20},{28,16},{1,13},{... | collective-permute-start | bytes 196616 | tf_op jit(solution)/shard_map/ppermute | solution.py:24
  12.0 12.4 %copy-start.6 = (bf16[16,2048]{1,0:T(8,128)(2,1)S(1)}, bf16[16,2048]{1,0:T(8,128)(2,1)}, u32[]{:S(2)}) copy-start(bf16[16,2048]{1,0:T(8,128)(2,1)} %shard_map.149.refs_0_.after_ref.refs_5_) | copy-start | bytes 196612
  12.8 16.1 %all-to-all-start = ((bf16[8,2,8,8,128]{4,3,2,1,0:T(8,128)(2,1)}), bf16[8,2,8,8,128]{4,3,2,1,0:T(8,128)(2,1)S(1)}, u32[]{:S(2)}, u32[]{:S(2)}) async-start(bf16[8,2,8,8,128]{4,3,2,1,0:T(8,128)(2,1)} %shard_map.153), calls=%async_computation | async-start | bytes 524288 | tf_op jit(solution)/shard_map/all_to_all | solution.py:538
  17.7 4.5 %collective-permute-start.4 = (bf16[16,2048]{1,0:T(8,128)(2,1)S(1)}, bf16[16,2048]{1,0:T(8,128)(2,1)S(1)}, u32[]{:S(2)}, u32[]{:S(2)}) collective-permute-start(bf16[16,2048]{1,0:T(8,128)(2,1)S(1)} %collective-permute-done.3.refs_4_), channel_id=1, source_target_pairs={{0,4},{4,0},{8,12},{12,8},{16,20},{20,16},{24,28},{28,24},{1,5},{5... | collective-permute-start | bytes 196616 | tf_op jit(solution)/shard_map/ppermute | solution.py:24
  19.8 4.6 %collective-permute-start.6 = (bf16[16,2048]{1,0:T(8,128)(2,1)S(1)}, bf16[16,2048]{1,0:T(8,128)(2,1)S(1)}, u32[]{:S(2)}, u32[]{:S(2)}) collective-permute-start(bf16[16,2048]{1,0:T(8,128)(2,1)S(1)} %collective-permute-done.5.refs_6_), channel_id=1, source_target_pairs={{0,4},{4,0},{8,12},{12,8},{16,20},{20,16},{24,28},{28,24},{1,5},{5... | collective-permute-start | bytes 196616 | tf_op jit(solution)/shard_map/ppermute | solution.py:24
  24.4 2.2 %copy-start = (bf16[2048,1024]{1,0:T(8,128)(2,1)S(1)}, bf16[2048,1024]{1,0:T(8,128)(2,1)}, u32[]{:S(2)}) copy-start(bf16[2048,1024]{1,0:T(8,128)(2,1)} %refs_9_.1) | copy-start | bytes 12582916
  28.1 2.3 %collective-permute-start.7 = (bf16[128,384]{1,0:T(8,128)(2,1)S(1)}, bf16[128,384]{1,0:T(8,128)(2,1)S(1)}, u32[]{:S(2)}, u32[]{:S(2)}) collective-permute-start(bf16[128,384]{1,0:T(8,128)(2,1)S(1)} %get-tuple-element.33.own_ref), channel_id=1, source_target_pairs={{0,1},{1,0},{2,3},{3,2},{4,5},{5,4},{6,7},{7,6},{8,9},{9,8},{10,11... | collective-permute-start | bytes 294920 | tf_op jit(solution)/shard_map/ppermute | solution.py:24
  28.3 2.9 %collective-permute-start.11 = (bf16[64,1024]{1,0:T(8,128)(2,1)S(1)}, bf16[64,1024]{1,0:T(8,128)(2,1)S(1)}, u32[]{:S(2)}, u32[]{:S(2)}) collective-permute-start(bf16[64,1024]{1,0:T(8,128)(2,1)S(1)} %get-tuple-element.38), channel_id=1, source_target_pairs={{0,1},{1,0},{2,3},{3,2},{4,5},{5,4},{6,7},{7,6},{8,9},{9,8},{10,11... | collective-permute-start | bytes 393224 | tf_op jit(solution)/shard_map/ppermute | solution.py:24
  28.9 9.2 %collective-permute-start.14 = (bf16[128,8,128]{2,1,0:T(8,128)(2,1)S(1)}, bf16[128,8,128]{2,1,0:T(8,128)(2,1)S(1)}, u32[]{:S(2)}, u32[]{:S(2)}) collective-permute-start(bf16[128,8,128]{2,1,0:T(8,128)(2,1)S(1)} %bitcast.13), channel_id=1, source_target_pairs={{0,2},{1,3},{2,0},{3,1},{4,6},{5,7},{6,4},{7,5},{8,10},{9,11},{10,... | collective-permute-start | bytes 786440 | tf_op jit(solution)/shard_map/ppermute | solution.py:24
  30.6 9.4 %collective-permute-start.8 = (bf16[128,384]{1,0:T(8,128)(2,1)S(1)}, bf16[128,384]{1,0:T(8,128)(2,1)S(1)}, u32[]{:S(2)}, u32[]{:S(2)}) collective-permute-start(bf16[128,384]{1,0:T(8,128)(2,1)S(1)} %shard_map.151.own_ref), channel_id=1, source_target_pairs={{0,2},{1,3},{2,0},{3,1},{4,6},{5,7},{6,4},{7,5},{8,10},{9,11},{10,... | collective-permute-start | bytes 294920 | tf_op jit(solution)/shard_map/ppermute | solution.py:24
  31.3 11.3 %copy-start.9 = (f32[4,128]{1,0:T(4,128)S(1)}, f32[4,128]{1,0:T(4,128)}, u32[]{:S(2)}) copy-start(f32[4,128]{1,0:T(4,128)} %constant.71.clone.rope_ref) | copy-start | bytes 6148
  31.3 11.2 %collective-permute-start.12 = (bf16[32,1024]{1,0:T(8,128)(2,1)S(1)}, bf16[32,1024]{1,0:T(8,128)(2,1)S(1)}, u32[]{:S(2)}, u32[]{:S(2)}) collective-permute-start(bf16[32,1024]{1,0:T(8,128)(2,1)S(1)} %slice.80), channel_id=1, source_target_pairs={{0,2},{1,3},{2,0},{3,1},{4,6},{5,7},{6,4},{7,5},{8,10},{9,11},{10,... | collective-permute-start | bytes 196616 | tf_op jit(solution)/shard_map/ppermute | solution.py:24
  32.8 9.7 %collective-permute-start.13 = (bf16[128,8,128]{2,1,0:T(8,128)(2,1)S(1)}, bf16[128,8,128]{2,1,0:T(8,128)(2,1)S(1)}, u32[]{:S(2)}, u32[]{:S(2)}) collective-permute-start(bf16[128,8,128]{2,1,0:T(8,128)(2,1)S(1)} %bitcast.14), channel_id=1, source_target_pairs={{0,1},{1,0},{2,3},{3,2},{4,5},{5,4},{6,7},{7,6},{8,9},{9,8},{10,11... | collective-permute-start | bytes 786440 | tf_op jit(solution)/shard_map/ppermute | solution.py:24
  38.1 4.5 %collective-permute-start.15 = (bf16[128,8,128]{2,1,0:T(8,128)(2,1)S(1)}, bf16[128,8,128]{2,1,0:T(8,128)(2,1)S(1)}, u32[]{:S(2)}, u32[]{:S(2)}) collective-permute-start(bf16[128,8,128]{2,1,0:T(8,128)(2,1)S(1)} %collective-permute-done.14.refs_4_), channel_id=1, source_target_pairs={{0,1},{1,0},{2,3},{3,2},{4,5},{5,4},{6,7},{7,6},{8,9},{9,8},{10,11... | collective-permute-start | bytes 786440 | tf_op jit(solution)/shard_map/ppermute | solution.py:24
  40.7 4.9 %collective-permute-start.10 = (bf16[128,128]{1,0:T(8,128)(2,1)S(1)}, bf16[128,128]{1,0:T(8,128)(2,1)S(1)}, u32[]{:S(2)}, u32[]{:S(2)}) collective-permute-start(bf16[128,128]{1,0:T(8,128)(2,1)S(1)} %get-tuple-element.35), channel_id=1, source_target_pairs={{0,4},{4,12},{8,20},{12,28},{16,0},{20,8},{24,16},{28,24},{1,5},{5... | collective-permute-start | bytes 98312 | tf_op jit(solution)/shard_map/ppermute | solution.py:502
  41.9 3.7 %collective-permute-start.9 = (bf16[128,128]{1,0:T(8,128)(2,1)S(1)}, bf16[128,128]{1,0:T(8,128)(2,1)S(1)}, u32[]{:S(2)}, u32[]{:S(2)}) collective-permute-start(bf16[128,128]{1,0:T(8,128)(2,1)S(1)} %get-tuple-element.34), channel_id=1, source_target_pairs={{0,0},{4,8},{8,16},{12,24},{16,4},{20,12},{24,20},{28,28},{1,1},{5... | collective-permute-start | bytes 98312 | tf_op jit(solution)/shard_map/ppermute | solution.py:502
  45.6 6.7 %copy-start.1 = (bf16[1024,2048]{1,0:T(8,128)(2,1)S(1)}, bf16[1024,2048]{1,0:T(8,128)(2,1)}, u32[]{:S(2)}) copy-start(bf16[1024,2048]{1,0:T(8,128)(2,1)} %refs_4_.2) | copy-start | bytes 12582916
  46.7 4.3 %collective-permute-start.17 = (bf16[32,1024]{1,0:T(8,128)(2,1)S(1)}, bf16[32,1024]{1,0:T(8,128)(2,1)S(1)}, u32[]{:S(2)}, u32[]{:S(2)}) collective-permute-start(bf16[32,1024]{1,0:T(8,128)(2,1)S(1)} %shard_map.155.refs_0_), channel_id=1, source_target_pairs={{0,2},{1,3},{2,0},{3,1},{4,6},{5,7},{6,4},{7,5},{8,10},{9,11},{10,... | collective-permute-start | bytes 196616 | tf_op jit(solution)/shard_map/ppermute | solution.py:24
  48.3 2.8 %collective-permute-start.16 = (bf16[32,1024]{1,0:T(8,128)(2,1)S(1)}, bf16[32,1024]{1,0:T(8,128)(2,1)S(1)}, u32[]{:S(2)}, u32[]{:S(2)}) collective-permute-start(bf16[32,1024]{1,0:T(8,128)(2,1)S(1)} %shard_map.155.refs_0_), channel_id=1, source_target_pairs={{0,1},{1,0},{2,3},{3,2},{4,5},{5,4},{6,7},{7,6},{8,9},{9,8},{10,11... | collective-permute-start | bytes 196616 | tf_op jit(solution)/shard_map/ppermute | solution.py:24
  51.1 1.3 %collective-permute-start.18 = (bf16[32,1024]{1,0:T(8,128)(2,1)S(1)}, bf16[32,1024]{1,0:T(8,128)(2,1)S(1)}, u32[]{:S(2)}, u32[]{:S(2)}) collective-permute-start(bf16[32,1024]{1,0:T(8,128)(2,1)S(1)} %collective-permute-done.17.refs_2_), channel_id=1, source_target_pairs={{0,1},{1,0},{2,3},{3,2},{4,5},{5,4},{6,7},{7,6},{8,9},{9,8},{10,11... | collective-permute-start | bytes 196616 | tf_op jit(solution)/shard_map/ppermute | solution.py:24
  53.6 8.3 %collective-permute-start.21 = (bf16[16,2048]{1,0:T(8,128)(2,1)S(1)}, bf16[16,2048]{1,0:T(8,128)(2,1)S(1)}, u32[]{:S(2)}, u32[]{:S(2)}) collective-permute-start(bf16[16,2048]{1,0:T(8,128)(2,1)S(1)} %get-tuple-element.46), channel_id=1, source_target_pairs={{0,4},{4,0},{8,12},{12,8},{16,20},{20,16},{24,28},{28,24},{1,5},{5... | collective-permute-start | bytes 196616 | tf_op jit(solution)/shard_map/ppermute | solution.py:24
  58.3 7.7 %collective-permute-start.19 = (bf16[16,2048]{1,0:T(8,128)(2,1)S(1)}, bf16[16,2048]{1,0:T(8,128)(2,1)S(1)}, u32[]{:S(2)}, u32[]{:S(2)}) collective-permute-start(bf16[16,2048]{1,0:T(8,128)(2,1)S(1)} %get-tuple-element.45), channel_id=1, source_target_pairs={{0,4},{4,0},{8,12},{12,8},{16,20},{20,16},{24,28},{28,24},{1,5},{5... | collective-permute-start | bytes 196616 | tf_op jit(solution)/shard_map/ppermute | solution.py:24
  58.4 7.7 %collective-permute-start.23 = (bf16[16,2048]{1,0:T(8,128)(2,1)S(1)}, bf16[16,2048]{1,0:T(8,128)(2,1)S(1)}, u32[]{:S(2)}, u32[]{:S(2)}) collective-permute-start(bf16[16,2048]{1,0:T(8,128)(2,1)S(1)} %get-tuple-element.47), channel_id=1, source_target_pairs={{0,4},{4,0},{8,12},{12,8},{16,20},{20,16},{24,28},{28,24},{1,5},{5... | collective-permute-start | bytes 196616 | tf_op jit(solution)/shard_map/ppermute | solution.py:24
  60.3 5.8 %collective-permute-start.24 = (bf16[16,2048]{1,0:T(8,128)(2,1)S(1)}, bf16[16,2048]{1,0:T(8,128)(2,1)S(1)}, u32[]{:S(2)}, u32[]{:S(2)}) collective-permute-start(bf16[16,2048]{1,0:T(8,128)(2,1)S(1)} %get-tuple-element.48), channel_id=1, source_target_pairs={{0,8},{4,12},{8,0},{12,4},{16,24},{20,28},{24,16},{28,20},{1,9},{5... | collective-permute-start | bytes 196616 | tf_op jit(solution)/shard_map/ppermute | solution.py:24
  61.2 5.2 %collective-permute-start.25 = (bf16[16,2048]{1,0:T(8,128)(2,1)S(1)}, bf16[16,2048]{1,0:T(8,128)(2,1)S(1)}, u32[]{:S(2)}, u32[]{:S(2)}) collective-permute-start(bf16[16,2048]{1,0:T(8,128)(2,1)S(1)} %get-tuple-element.49), channel_id=1, source_target_pairs={{0,12},{4,8},{8,4},{12,0},{16,28},{20,24},{24,20},{28,16},{1,13},{... | collective-permute-start | bytes 196616 | tf_op jit(solution)/shard_map/ppermute | solution.py:24
  61.9 7.4 %collective-permute-start.22 = (bf16[16,2048]{1,0:T(8,128)(2,1)S(1)}, bf16[16,2048]{1,0:T(8,128)(2,1)S(1)}, u32[]{:S(2)}, u32[]{:S(2)}) collective-permute-start(bf16[16,2048]{1,0:T(8,128)(2,1)S(1)} %shard_map.158), channel_id=1, source_target_pairs={{0,24},{4,28},{8,16},{12,20},{16,8},{20,12},{24,0},{28,4},{1,25},{... | collective-permute-start | bytes 196616 | tf_op jit(solution)/shard_map/ppermute | solution.py:24
  66.0 18.6 %slice-start = ((s8[7340032]{0:T(1024)(128)(4,1)}), s8[4194304]{0:T(1024)(128)(4,1)S(1)}, s32[]{:S(2)}) async-start(s8[7340032]{0:T(1024)(128)(4,1)} %bitcast.16), calls=%async_computation.1 | async-start | bytes 8388608
  66.0 5.2 %collective-permute-start.20 = (bf16[16,2048]{1,0:T(8,128)(2,1)S(1)}, bf16[16,2048]{1,0:T(8,128)(2,1)S(1)}, u32[]{:S(2)}, u32[]{:S(2)}) collective-permute-start(bf16[16,2048]{1,0:T(8,128)(2,1)S(1)} %shard_map.157), channel_id=1, source_target_pairs={{0,16},{4,20},{8,24},{12,28},{16,0},{20,4},{24,8},{28,12},{1,17},{... | collective-permute-start | bytes 196616 | tf_op jit(solution)/shard_map/ppermute | solution.py:24
  71.3 13.4 %slice-start.1 = ((s8[7340032]{0:T(1024)(128)(4,1)}), s8[3145728]{0:T(1024)(128)(4,1)S(1)}, s32[]{:S(2)}) async-start(s8[7340032]{0:T(1024)(128)(4,1)} %bitcast.16), calls=%async_computation.2 | async-start | bytes 6291456
  71.3 13.4 %copy-start.8 = (f32[2048]{0:T(1024)S(1)}, f32[2048]{0:T(1024)}, u32[]{:S(2)}) copy-start(f32[2048]{0:T(1024)} %param.20) | copy-start | bytes 24580
  71.3 15.3 %slice-start.2 = ((s8[7340032]{0:T(1024)(128)(4,1)}), s8[4194304]{0:T(1024)(128)(4,1)S(1)}, s32[]{:S(2)}) async-start(s8[7340032]{0:T(1024)(128)(4,1)} %bitcast.18), calls=%async_computation.3 | async-start | bytes 8388608
  72.0 6.4 %collective-permute-start.29 = (bf16[16,2048]{1,0:T(8,128)(2,1)S(1)}, bf16[16,2048]{1,0:T(8,128)(2,1)S(1)}, u32[]{:S(2)}, u32[]{:S(2)}) collective-permute-start(bf16[16,2048]{1,0:T(8,128)(2,1)S(1)} %get-tuple-element.51.refs_0_), channel_id=1, source_target_pairs={{0,16},{4,20},{8,24},{12,28},{16,0},{20,4},{24,8},{28,12},{1,17},{... | collective-permute-start | bytes 196616 | tf_op jit(solution)/shard_map/ppermute | solution.py:24
  72.9 7.5 %collective-permute-start.31 = (bf16[16,2048]{1,0:T(8,128)(2,1)S(1)}, bf16[16,2048]{1,0:T(8,128)(2,1)S(1)}, u32[]{:S(2)}, u32[]{:S(2)}) collective-permute-start(bf16[16,2048]{1,0:T(8,128)(2,1)S(1)} %get-tuple-element.51.refs_0_), channel_id=1, source_target_pairs={{0,24},{4,28},{8,16},{12,20},{16,8},{20,12},{24,0},{28,4},{1,25},{... | collective-permute-start | bytes 196616 | tf_op jit(solution)/shard_map/ppermute | solution.py:24
  74.5 5.9 %collective-permute-start.26 = (bf16[16,2048]{1,0:T(8,128)(2,1)S(1)}, bf16[16,2048]{1,0:T(8,128)(2,1)S(1)}, u32[]{:S(2)}, u32[]{:S(2)}) collective-permute-start(bf16[16,2048]{1,0:T(8,128)(2,1)S(1)} %get-tuple-element.51.refs_0_), channel_id=1, source_target_pairs={{0,4},{4,0},{8,12},{12,8},{16,20},{20,16},{24,28},{28,24},{1,5},{5... | collective-permute-start | bytes 196616 | tf_op jit(solution)/shard_map/ppermute | solution.py:24
  75.2 5.2 %collective-permute-start.27 = (bf16[16,2048]{1,0:T(8,128)(2,1)S(1)}, bf16[16,2048]{1,0:T(8,128)(2,1)S(1)}, u32[]{:S(2)}, u32[]{:S(2)}) collective-permute-start(bf16[16,2048]{1,0:T(8,128)(2,1)S(1)} %get-tuple-element.51.refs_0_), channel_id=1, source_target_pairs={{0,8},{4,12},{8,0},{12,4},{16,24},{20,28},{24,16},{28,20},{1,9},{5... | collective-permute-start | bytes 196616 | tf_op jit(solution)/shard_map/ppermute | solution.py:24
  76.5 5.3 %collective-permute-start.28 = (bf16[16,2048]{1,0:T(8,128)(2,1)S(1)}, bf16[16,2048]{1,0:T(8,128)(2,1)S(1)}, u32[]{:S(2)}, u32[]{:S(2)}) collective-permute-start(bf16[16,2048]{1,0:T(8,128)(2,1)S(1)} %get-tuple-element.51.refs_0_), channel_id=1, source_target_pairs={{0,12},{4,8},{8,4},{12,0},{16,28},{20,24},{24,20},{28,16},{1,13},{... | collective-permute-start | bytes 196616 | tf_op jit(solution)/shard_map/ppermute | solution.py:24
  78.3 4.9 %collective-permute-start.30 = (bf16[16,2048]{1,0:T(8,128)(2,1)S(1)}, bf16[16,2048]{1,0:T(8,128)(2,1)S(1)}, u32[]{:S(2)}, u32[]{:S(2)}) collective-permute-start(bf16[16,2048]{1,0:T(8,128)(2,1)S(1)} %collective-permute-done.29.refs_4_), channel_id=1, source_target_pairs={{0,4},{4,0},{8,12},{12,8},{16,20},{20,16},{24,28},{28,24},{1,5},{5... | collective-permute-start | bytes 196616 | tf_op jit(solution)/shard_map/ppermute | solution.py:24
  80.4 4.3 %collective-permute-start.32 = (bf16[16,2048]{1,0:T(8,128)(2,1)S(1)}, bf16[16,2048]{1,0:T(8,128)(2,1)S(1)}, u32[]{:S(2)}, u32[]{:S(2)}) collective-permute-start(bf16[16,2048]{1,0:T(8,128)(2,1)S(1)} %collective-permute-done.31.refs_6_), channel_id=1, source_target_pairs={{0,4},{4,0},{8,12},{12,8},{16,20},{20,16},{24,28},{28,24},{1,5},{5... | collective-permute-start | bytes 196616 | tf_op jit(solution)/shard_map/ppermute | solution.py:24
  84.7 1.9 %slice-start.3 = ((s8[7340032]{0:T(1024)(128)(4,1)}), s8[3145728]{0:T(1024)(128)(4,1)S(1)}, s32[]{:S(2)}) async-start(s8[7340032]{0:T(1024)(128)(4,1)} %bitcast.18), calls=%async_computation.4 | async-start | bytes 6291456
  84.7 17.8 %slice-start.4 = ((s8[7340032]{0:T(1024)(128)(4,1)}), s8[4194304]{0:T(1024)(128)(4,1)S(1)}, s32[]{:S(2)}) async-start(s8[7340032]{0:T(1024)(128)(4,1)} %bitcast.20), calls=%async_computation.5 | async-start | bytes 8388608
  86.5 1.8 %collective-permute-start.33 = (bf16[64,1920]{1,0:T(8,128)(2,1)S(1)}, bf16[64,1920]{1,0:T(8,128)(2,1)S(1)}, u32[]{:S(2)}, u32[]{:S(2)}) collective-permute-start(bf16[64,1920]{1,0:T(8,128)(2,1)S(1)} %get-tuple-element.53), channel_id=1, source_target_pairs={{0,1},{1,0},{2,3},{3,2},{4,5},{5,4},{6,7},{7,6},{8,9},{9,8},{10,11... | collective-permute-start | bytes 737288 | tf_op jit(solution)/shard_map/ppermute | solution.py:24
  86.6 15.9 %slice-start.5 = ((s8[7340032]{0:T(1024)(128)(4,1)}), s8[3145728]{0:T(1024)(128)(4,1)S(1)}, s32[]{:S(2)}) async-start(s8[7340032]{0:T(1024)(128)(4,1)} %bitcast.20), calls=%async_computation.6 | async-start | bytes 6291456
  87.8 2.2 %collective-permute-start.35 = (bf16[64,1792]{1,0:T(8,128)(2,1)S(1)}, bf16[64,1792]{1,0:T(8,128)(2,1)S(1)}, u32[]{:S(2)}, u32[]{:S(2)}) collective-permute-start(bf16[64,1792]{1,0:T(8,128)(2,1)S(1)} %get-tuple-element.56), channel_id=1, source_target_pairs={{0,1},{1,0},{2,3},{3,2},{4,5},{5,4},{6,7},{7,6},{8,9},{9,8},{10,11... | collective-permute-start | bytes 688136 | tf_op jit(solution)/shard_map/ppermute | solution.py:24
  88.4 6.2 %collective-permute-start.34 = (bf16[32,1920]{1,0:T(8,128)(2,1)S(1)}, bf16[32,1920]{1,0:T(8,128)(2,1)S(1)}, u32[]{:S(2)}, u32[]{:S(2)}) collective-permute-start(bf16[32,1920]{1,0:T(8,128)(2,1)S(1)} %slice.78), channel_id=1, source_target_pairs={{0,2},{1,3},{2,0},{3,1},{4,6},{5,7},{6,4},{7,5},{8,10},{9,11},{10,... | collective-permute-start | bytes 368648 | tf_op jit(solution)/shard_map/ppermute | solution.py:24
  90.0 6.1 %collective-permute-start.36 = (bf16[32,1792]{1,0:T(8,128)(2,1)S(1)}, bf16[32,1792]{1,0:T(8,128)(2,1)S(1)}, u32[]{:S(2)}, u32[]{:S(2)}) collective-permute-start(bf16[32,1792]{1,0:T(8,128)(2,1)S(1)} %slice.79), channel_id=1, source_target_pairs={{0,2},{1,3},{2,0},{3,1},{4,6},{5,7},{6,4},{7,5},{8,10},{9,11},{10,... | collective-permute-start | bytes 344072 | tf_op jit(solution)/shard_map/ppermute | solution.py:24
  96.3 4.9 %collective-permute-start.38 = (bf16[32,1792]{1,0:T(8,128)(2,1)S(1)}, bf16[32,1792]{1,0:T(8,128)(2,1)S(1)}, u32[]{:S(2)}, u32[]{:S(2)}) collective-permute-start(bf16[32,1792]{1,0:T(8,128)(2,1)S(1)} %fusion.2.refs_0_), channel_id=1, source_target_pairs={{0,2},{1,3},{2,0},{3,1},{4,6},{5,7},{6,4},{7,5},{8,10},{9,11},{10,... | collective-permute-start | bytes 344072 | tf_op jit(solution)/shard_map/ppermute | solution.py:24
  97.9 3.3 %collective-permute-start.37 = (bf16[32,1792]{1,0:T(8,128)(2,1)S(1)}, bf16[32,1792]{1,0:T(8,128)(2,1)S(1)}, u32[]{:S(2)}, u32[]{:S(2)}) collective-permute-start(bf16[32,1792]{1,0:T(8,128)(2,1)S(1)} %fusion.2.refs_0_), channel_id=1, source_target_pairs={{0,1},{1,0},{2,3},{3,2},{4,5},{5,4},{6,7},{7,6},{8,9},{9,8},{10,11... | collective-permute-start | bytes 344072 | tf_op jit(solution)/shard_map/ppermute | solution.py:24
  101.2 1.3 %collective-permute-start.39 = (bf16[32,1792]{1,0:T(8,128)(2,1)S(1)}, bf16[32,1792]{1,0:T(8,128)(2,1)S(1)}, u32[]{:S(2)}, u32[]{:S(2)}) collective-permute-start(bf16[32,1792]{1,0:T(8,128)(2,1)S(1)} %collective-permute-done.38.refs_2_), channel_id=1, source_target_pairs={{0,1},{1,0},{2,3},{3,2},{4,5},{5,4},{6,7},{7,6},{8,9},{9,8},{10,11... | collective-permute-start | bytes 344072 | tf_op jit(solution)/shard_map/ppermute | solution.py:24
  104.2 5.6 %collective-permute-start.42 = (bf16[16,2048]{1,0:T(8,128)(2,1)S(1)}, bf16[16,2048]{1,0:T(8,128)(2,1)S(1)}, u32[]{:S(2)}, u32[]{:S(2)}) collective-permute-start(bf16[16,2048]{1,0:T(8,128)(2,1)S(1)} %get-tuple-element.60), channel_id=1, source_target_pairs={{0,4},{4,0},{8,12},{12,8},{16,20},{20,16},{24,28},{28,24},{1,5},{5... | collective-permute-start | bytes 196616 | tf_op jit(solution)/shard_map/ppermute | solution.py:24
  105.0 6.8 %collective-permute-start.40 = (bf16[16,2048]{1,0:T(8,128)(2,1)S(1)}, bf16[16,2048]{1,0:T(8,128)(2,1)S(1)}, u32[]{:S(2)}, u32[]{:S(2)}) collective-permute-start(bf16[16,2048]{1,0:T(8,128)(2,1)S(1)} %get-tuple-element.59), channel_id=1, source_target_pairs={{0,4},{4,0},{8,12},{12,8},{16,20},{20,16},{24,28},{28,24},{1,5},{5... | collective-permute-start | bytes 196616 | tf_op jit(solution)/shard_map/ppermute | solution.py:24
  106.3 5.6 %collective-permute-start.44 = (bf16[16,2048]{1,0:T(8,128)(2,1)S(1)}, bf16[16,2048]{1,0:T(8,128)(2,1)S(1)}, u32[]{:S(2)}, u32[]{:S(2)}) collective-permute-start(bf16[16,2048]{1,0:T(8,128)(2,1)S(1)} %get-tuple-element.61), channel_id=1, source_target_pairs={{0,4},{4,0},{8,12},{12,8},{16,20},{20,16},{24,28},{28,24},{1,5},{5... | collective-permute-start | bytes 196616 | tf_op jit(solution)/shard_map/ppermute | solution.py:24
  107.0 4.9 %collective-permute-start.45 = (bf16[16,2048]{1,0:T(8,128)(2,1)S(1)}, bf16[16,2048]{1,0:T(8,128)(2,1)S(1)}, u32[]{:S(2)}, u32[]{:S(2)}) collective-permute-start(bf16[16,2048]{1,0:T(8,128)(2,1)S(1)} %get-tuple-element.62), channel_id=1, source_target_pairs={{0,8},{4,12},{8,0},{12,4},{16,24},{20,28},{24,16},{28,20},{1,9},{5... | collective-permute-start | bytes 196616 | tf_op jit(solution)/shard_map/ppermute | solution.py:24
  107.6 5.2 %collective-permute-start.46 = (bf16[16,2048]{1,0:T(8,128)(2,1)S(1)}, bf16[16,2048]{1,0:T(8,128)(2,1)S(1)}, u32[]{:S(2)}, u32[]{:S(2)}) collective-permute-start(bf16[16,2048]{1,0:T(8,128)(2,1)S(1)} %get-tuple-element.63), channel_id=1, source_target_pairs={{0,12},{4,8},{8,4},{12,0},{16,28},{20,24},{24,20},{28,16},{1,13},{... | collective-permute-start | bytes 196616 | tf_op jit(solution)/shard_map/ppermute | solution.py:24
  109.8 6.1 %collective-permute-start.43 = (bf16[16,2048]{1,0:T(8,128)(2,1)S(1)}, bf16[16,2048]{1,0:T(8,128)(2,1)S(1)}, u32[]{:S(2)}, u32[]{:S(2)}) collective-permute-start(bf16[16,2048]{1,0:T(8,128)(2,1)S(1)} %shard_map.164), channel_id=1, source_target_pairs={{0,24},{4,28},{8,16},{12,20},{16,8},{20,12},{24,0},{28,4},{1,25},{... | collective-permute-start | bytes 196616 | tf_op jit(solution)/shard_map/ppermute | solution.py:24
  111.8 6.1 %collective-permute-start.41 = (bf16[16,2048]{1,0:T(8,128)(2,1)S(1)}, bf16[16,2048]{1,0:T(8,128)(2,1)S(1)}, u32[]{:S(2)}, u32[]{:S(2)}) collective-permute-start(bf16[16,2048]{1,0:T(8,128)(2,1)S(1)} %shard_map.163), channel_id=1, source_target_pairs={{0,16},{4,20},{8,24},{12,28},{16,0},{20,4},{24,8},{28,12},{1,17},{... | collective-permute-start | bytes 196616 | tf_op jit(solution)/shard_map/ppermute | solution.py:24
  (1 other events, 0.9 us)

commit v9 on v8

--- a/solution.py
+++ b/solution.py
@@ -107,24 +107,11 @@
 
 
 def stack_tokens(x_first, x_second):
+    def body(first_ref, second_ref, out_ref):
+        out_ref[...] = jnp.concatenate([first_ref[...].astype(F32), second_ref[...].astype(F32)], axis=0).astype(BF16)
+
     part_dev, features = x_first.shape
-
-    def body(first_ref, second_ref, out_ref, one, two, sems):
-        copies = [pltpu.make_async_copy(first_ref, one, sems.at[0]), pltpu.make_async_copy(second_ref, two, sems.at[1])]
-        for copy in copies:
-            copy.start()
-        for copy in copies:
-            copy.wait()
-        out_ref[...] = jnp.concatenate([one[...].astype(F32), two[...].astype(F32)], axis=0).astype(BF16)
-
-    return call(
-        body,
-        shaped((2 * part_dev, features)),
-        (x_first, x_second),
-        [HBM, HBM],
-        [pltpu.VMEM(x_first.shape, BF16), pltpu.VMEM(x_first.shape, BF16), pltpu.SemaphoreType.DMA((2,))],
-        limit=None,
-    )
+    return call(body, shaped((2 * part_dev, features)), (x_first, x_second), [VMEM] * 2)
 
 
 def pack(cache_keys, cache_values, after):
@@ -171,7 +158,7 @@
     return jnp.where(lane == 0, high, jnp.where(lane == 1, total - high, base))
 
 
-def project_attention(where, blocks, gain, w_keyval, w_query):
+def project_attention(where, blocks, gain, w_keyval, w_query, after):
     pair, features = blocks[0].shape
     rows = len(blocks) * pair
     half = rows // 2
@@ -180,7 +167,14 @@
 
     def body(where_ref, gain_ref, *refs):
         block_refs, refs = refs[: len(blocks)], refs[len(blocks) :]
-        w_kv_ref, w_q_ref, kv_ref, keep_ref, send_ref, h_ref, ss_ref, product = refs
+        w_kv_ref, w_q_hbm, after_ref, kv_ref, keep_ref, send_ref, h_ref, ss_ref, product, w_q_ref, sems = refs
+        tile = tiles(wide)
+        copies = [
+            pltpu.make_async_copy(w_q_hbm.at[:, pl.ds(i * tile, tile)], w_q_ref.at[:, pl.ds(i * tile, tile)], sems.at[i])
+            for i in range(wide // tile)
+        ]
+        for copy in copies:
+            copy.start()
         places = lift(where_ref, gain_ref, block_refs, h_ref, ss_ref, True)
         h = h_ref[...]
         product[...] = jnp.dot(h, w_kv_ref[...], preferred_element_type=F32)
@@ -190,18 +184,26 @@
         lane = lax.broadcasted_iota(jnp.int32, squares.shape, 1)
         kv_ref[:, columns:] = split(squares, 0.0, lane).astype(BF16)
 
-        def write(first, tile, product):
-            keep_ref[:, first : first + tile] = product[:half]
-            send_ref[:, first : first + tile] = product[half:].astype(BF16)
-
-        multiply(h, w_q_ref, write)
+        for i, copy in enumerate(copies):
+            copy.wait()
+            lanes = slice(i * tile, (i + 1) * tile)
+            queries = jnp.dot(h, w_q_ref[:, lanes], preferred_element_type=F32)
+            keep_ref[:, lanes] = queries[:half]
+            send_ref[:, lanes] = queries[half:].astype(BF16)
 
     return call(
         body,
         (shaped((rows, columns + 128)), shaped((half, wide), F32), shaped((half, wide))),
-        (where, gain[None], *blocks, w_keyval, w_query),
-        [SMEM] + [VMEM] * (3 + len(blocks)),
-        [pltpu.VMEM((rows, features), BF16), pltpu.VMEM((rows, 128), F32), pltpu.VMEM((rows, columns), F32)],
+        (where, gain[None], *blocks, w_keyval, w_query, after),
+        [SMEM] + [VMEM] * (2 + len(blocks)) + [HBM, ANY],
+        [
+            pltpu.VMEM((rows, features), BF16),
+            pltpu.VMEM((rows, 128), F32),
+            pltpu.VMEM((rows, columns), F32),
+            pltpu.VMEM(w_query.shape, BF16),
+            pltpu.SemaphoreType.DMA((wide // tiles(wide),)),
+        ],
+        limit=52 << 20,
         flops=2 * rows * (w_keyval.size + w_query.size),
         moved=4 * rows * features + 2 * (w_keyval.size + w_query.size),
     )
@@ -538,7 +540,7 @@
     cache = lax.all_to_all(pack(cache_keys, cache_values, x), "dp", split_axis=0, concat_axis=0, tiled=True)
     caches = gather_blocks(cache.reshape(groups * pair, span, HD))
 
-    message, *queries = project_attention(where, blocks, attn_gain, w_keyval, w_query)
+    message, *queries = project_attention(where, blocks, attn_gain, w_keyval, w_query, cache)
     bits = 1
     while 2 * bits < tensor:
         message = add_keyvals(message, swap(message, "tensor", bits))

time: 119 us -> 119 us (level)
  starting transfers between devices: 56.5 us -> 54.2 us
  waiting for transfers between devices: 41.9 us -> 44 us
  local copies, waits for them, and re-layouts: 3.48 us -> 1.96 us
  Pallas kernels: 15 us -> 16.5 us
    pallas_call x17, Pallas kernels: 15 us -> 16.5 us  [call(): pl.pallas_call(body, out_shape=outs, in_specs=specs, out_specs=jax.tree.m...]
    unnamed x34 -> x30, local copies, waits for them, and re-layouts: 3.13 us -> 1.61 us
    ppermute x45, starting transfers between devices: 50 us -> 48.6 us  [swap(): return lax.ppermute(x, axis, [(i, i ^ bits) for i in range(size)])]
    all_to_all x1, waiting for transfers between devices: 0.01 us -> 1.26 us  [local(): lax.all_to_all(pack(cache_keys, cache_values, x), 'dp', split_axis=0, con...]
  transfers between devices with their start and end apart: 48 -> 48, of which waited for: 21 -> 25; matrix products, arithmetic and copies ran while one was open for 1% -> 1% of each run, Pallas kernels for 5% -> 4%
where the time goes in v9:
time: 119 us; the launch traced here: 118 us
  starting transfers between devices  54.2 us (46%)
  waiting for transfers between devices  44 us (37%)
  Pallas kernels  16.5 us (14%)
  local copies, waits for them, and re-layouts  1.96 us (2%)
    ppermute x45, starting transfers between devices, swap(): return lax.ppermute(x, axis, [(i, i ^ bits) for i in range(size)])  48.6 us
    ppermute x45, waiting for transfers between devices, swap(): return lax.ppermute(x, axis, [(i, i ^ bits) for i in range(size)])  40.7 us
    pallas_call x17, Pallas kernels, call(): pl.pallas_call(body, out_shape=outs, in_specs=specs, out_specs=jax.tree.m...  16.5 us
    all_to_all x1, starting transfers between devices, local(): lax.all_to_all(pack(cache_keys, cache_values, x), 'dp', split_axis=0, con...  4.68 us
  transfers between devices with their start and end apart: 48, of which 25 were waited for; matrix products, arithmetic and copies ran while one was open for 1% of the time, Pallas kernels for 4%

profile of v9, /device:TPU:0, one launch (start us, length us, event | category | flops | bytes accessed | tf_op | source)
XLA Modules:
  0.0 118.4 jit_solution(1653746617691922562)
XLA Ops:
  0.7 0.8 copy-done.3
  1.5 0.8 copy-done.4
  2.2 4.1 %collective-permute-start.3 = (bf16[16,2048]{1,0:T(8,128)(2,1)S(1)}, bf16[16,2048]{1,0:T(8,128)(2,1)S(1)}, u32[]{:S(2)}, u32[]{:S(2)}) collective-permute-start(bf16[16,2048]{1,0:T(8,128)(2,1)S(1)} %shard_map.149.after_ref.refs_0_.refs_5_), channel_id=1, source_target_pairs={{0,16},{4,20},{8,24},{12,28},{16,0},{20,4},{24,8},{28,12},{1,17},{... | collective-permute-start | bytes 196616 | tf_op jit(solution)/shard_map/ppermute | solution.py:24
  6.3 1.3 %collective-permute-start.5 = (bf16[16,2048]{1,0:T(8,128)(2,1)S(1)}, bf16[16,2048]{1,0:T(8,128)(2,1)S(1)}, u32[]{:S(2)}, u32[]{:S(2)}) collective-permute-start(bf16[16,2048]{1,0:T(8,128)(2,1)S(1)} %shard_map.149.after_ref.refs_0_.refs_5_), channel_id=1, source_target_pairs={{0,24},{4,28},{8,16},{12,20},{16,8},{20,12},{24,0},{28,4},{1,25},{... | collective-permute-start | bytes 196616 | tf_op jit(solution)/shard_map/ppermute | solution.py:24
  7.7 1.5 %collective-permute-start = (bf16[16,2048]{1,0:T(8,128)(2,1)S(1)}, bf16[16,2048]{1,0:T(8,128)(2,1)S(1)}, u32[]{:S(2)}, u32[]{:S(2)}) collective-permute-start(bf16[16,2048]{1,0:T(8,128)(2,1)S(1)} %shard_map.149.after_ref.refs_0_.refs_5_), channel_id=1, source_target_pairs={{0,4},{4,0},{8,12},{12,8},{16,20},{20,16},{24,28},{28,24},{1,5},{5... | collective-permute-start | bytes 196616 | tf_op jit(solution)/shard_map/ppermute | solution.py:24
  9.4 1.8 %collective-permute-start.2 = (bf16[16,2048]{1,0:T(8,128)(2,1)S(1)}, bf16[16,2048]{1,0:T(8,128)(2,1)S(1)}, u32[]{:S(2)}, u32[]{:S(2)}) collective-permute-start(bf16[16,2048]{1,0:T(8,128)(2,1)S(1)} %shard_map.149.after_ref.refs_0_.refs_5_), channel_id=1, source_target_pairs={{0,12},{4,8},{8,4},{12,0},{16,28},{20,24},{24,20},{28,16},{1,13},{... | collective-permute-start | bytes 196616 | tf_op jit(solution)/shard_map/ppermute | solution.py:24
  11.2 0.8 shard_map.150
  11.9 4.7 %all-to-all-start = ((bf16[8,2,8,8,128]{4,3,2,1,0:T(8,128)(2,1)}), bf16[8,2,8,8,128]{4,3,2,1,0:T(8,128)(2,1)S(1)}, u32[]{:S(2)}, u32[]{:S(2)}) async-start(bf16[8,2,8,8,128]{4,3,2,1,0:T(8,128)(2,1)} %shard_map.150), calls=%async_computation | async-start | bytes 524288 | tf_op jit(solution)/shard_map/all_to_all | solution.py:540
  16.9 2.1 %collective-permute-start.4 = (bf16[16,2048]{1,0:T(8,128)(2,1)S(1)}, bf16[16,2048]{1,0:T(8,128)(2,1)S(1)}, u32[]{:S(2)}, u32[]{:S(2)}) collective-permute-start(bf16[16,2048]{1,0:T(8,128)(2,1)S(1)} %collective-permute-done.3.refs_4_), channel_id=1, source_target_pairs={{0,4},{4,0},{8,12},{12,8},{16,20},{20,16},{24,28},{28,24},{1,5},{5... | collective-permute-start | bytes 196616 | tf_op jit(solution)/shard_map/ppermute | solution.py:24
  19.2 2.2 %collective-permute-done.4.refs_5_ = bf16[16,2048]{1,0:T(8,128)(2,1)S(1)} collective-permute-done((bf16[16,2048]{1,0:T(8,128)(2,1)S(1)}, bf16[16,2048]{1,0:T(8,128)(2,1)S(1)}, u32[]{:S(2)}, u32[]{:S(2)}) %collective-permute-start.4) | collective-permute-done | bytes 65568 | tf_op jit(solution)/shard_map/ppermute | solution.py:24
  21.4 2.1 %collective-permute-done.6.refs_7_ = bf16[16,2048]{1,0:T(8,128)(2,1)S(1)} collective-permute-done((bf16[16,2048]{1,0:T(8,128)(2,1)S(1)}, bf16[16,2048]{1,0:T(8,128)(2,1)S(1)}, u32[]{:S(2)}, u32[]{:S(2)}) %collective-permute-start.6) | collective-permute-done | bytes 65568 | tf_op jit(solution)/shard_map/ppermute | solution.py:24
  23.6 1.3 %all-to-all-done.refs_10_ = bf16[8,2,8,8,128]{4,3,2,1,0:T(8,128)(2,1)S(1)} async-done(((bf16[8,2,8,8,128]{4,3,2,1,0:T(8,128)(2,1)}), bf16[8,2,8,8,128]{4,3,2,1,0:T(8,128)(2,1)S(1)}, u32[]{:S(2)}, u32[]{:S(2)}) %all-to-all-start) | async-done | bytes 262176 | tf_op jit(solution)/shard_map/all_to_all | solution.py:540
  24.8 4.5 %shard_map.151 = (bf16[128,384]{1,0:T(8,128)(2,1)S(1)}, f32[64,1024]{1,0:T(8,128)S(1)}, bf16[64,1024]{1,0:T(8,128)(2,1)S(1)}) custom-call(s32[2]{0:T(128)S(1)} %pad_add_fusion.3.where_ref, f32[1,2048]{1,0:T(1,128)S(1)} %bitcast.22, bf16[16,2048]{1,0:T(8,128)(2,1)S(1)} %shard_map.149.after_ref.refs_0_.refs_5_, ...), custom_call_target="tpu_custom_call" | custom-call | flops 6039797760 | bytes 6291456 | tf_op jit(solution)/shard_map/pallas_call | solution.py:45
  29.6 1.6 %collective-permute-start.14 = (bf16[128,8,128]{2,1,0:T(8,128)(2,1)S(1)}, bf16[128,8,128]{2,1,0:T(8,128)(2,1)S(1)}, u32[]{:S(2)}, u32[]{:S(2)}) collective-permute-start(bf16[128,8,128]{2,1,0:T(8,128)(2,1)S(1)} %bitcast.13), channel_id=1, source_target_pairs={{0,2},{1,3},{2,0},{3,1},{4,6},{5,7},{6,4},{7,5},{8,10},{9,11},{10,... | collective-permute-start | bytes 786440 | tf_op jit(solution)/shard_map/ppermute | solution.py:24
  31.9 0.6 collective-permute-start.8
  33.0 1.1 collective-permute-start.12
  34.1 4.6 %collective-permute-done.14.refs_4_ = bf16[128,8,128]{2,1,0:T(8,128)(2,1)S(1)} collective-permute-done((bf16[128,8,128]{2,1,0:T(8,128)(2,1)S(1)}, bf16[128,8,128]{2,1,0:T(8,128)(2,1)S(1)}, u32[]{:S(2)}, u32[]{:S(2)}) %collective-permute-start.14) | collective-permute-done | bytes 262176 | tf_op jit(solution)/shard_map/ppermute | solution.py:24
  38.8 2.1 %collective-permute-done.8.arrived_ref = bf16[128,384]{1,0:T(8,128)(2,1)S(1)} collective-permute-done((bf16[128,384]{1,0:T(8,128)(2,1)S(1)}, bf16[128,384]{1,0:T(8,128)(2,1)S(1)}, u32[]{:S(2)}, u32[]{:S(2)}) %collective-permute-start.8) | collective-permute-done | bytes 98336 | tf_op jit(solution)/shard_map/ppermute | solution.py:24
  40.9 0.7 shard_map.153
  41.8 0.7 collective-permute-start.9
  42.5 1.9 %shard_map.154 = (bf16[256,128]{1,0:T(8,128)(2,1)S(1)}, f32[256,128]{1,0:T(8,128)S(1)}, f32[256,128]{1,0:T(8,128)S(1)}, f32[256,128]{1,0:T(8,128)S(1)}) custom-call(s32[2]{0:T(128)S(1)} %pad_add_fusion.3.where_ref, s32[16]{0:T(128)S(1)} %get-tuple-element.65.anc_ref, f32[4,128]{1,0:T(4,128)S(1)} %copy-done.7, f32[128,128]{1,0:T(8,128)S(1)} %get-tuple-element.36.scale_ref, ...), custom_call_target="tpu_custom_call" | custom-call | flops 5368709120 | bytes 4194304 | tf_op jit(solution)/shard_map/pallas_call | solution.py:45
  44.4 2.0 %collective-permute-done.10.two_ref = bf16[128,128]{1,0:T(8,128)(2,1)S(1)} collective-permute-done((bf16[128,128]{1,0:T(8,128)(2,1)S(1)}, bf16[128,128]{1,0:T(8,128)(2,1)S(1)}, u32[]{:S(2)}, u32[]{:S(2)}) %collective-permute-start.10) | collective-permute-done | bytes 32800 | tf_op jit(solution)/shard_map/ppermute | solution.py:504
  46.4 1.1 shard_map.155.refs_0_
  47.6 1.6 %collective-permute-start.17 = (bf16[32,1024]{1,0:T(8,128)(2,1)S(1)}, bf16[32,1024]{1,0:T(8,128)(2,1)S(1)}, u32[]{:S(2)}, u32[]{:S(2)}) collective-permute-start(bf16[32,1024]{1,0:T(8,128)(2,1)S(1)} %shard_map.155.refs_0_), channel_id=1, source_target_pairs={{0,2},{1,3},{2,0},{3,1},{4,6},{5,7},{6,4},{7,5},{8,10},{9,11},{10,... | collective-permute-start | bytes 196616 | tf_op jit(solution)/shard_map/ppermute | solution.py:24
  49.2 2.7 %collective-permute-done.17.refs_2_ = bf16[32,1024]{1,0:T(8,128)(2,1)S(1)} collective-permute-done((bf16[32,1024]{1,0:T(8,128)(2,1)S(1)}, bf16[32,1024]{1,0:T(8,128)(2,1)S(1)}, u32[]{:S(2)}, u32[]{:S(2)}) %collective-permute-start.17) | collective-permute-done | bytes 65568 | tf_op jit(solution)/shard_map/ppermute | solution.py:24
  51.9 1.2 %collective-permute-done.18.refs_3_ = bf16[32,1024]{1,0:T(8,128)(2,1)S(1)} collective-permute-done((bf16[32,1024]{1,0:T(8,128)(2,1)S(1)}, bf16[32,1024]{1,0:T(8,128)(2,1)S(1)}, u32[]{:S(2)}, u32[]{:S(2)}) %collective-permute-start.18) | collective-permute-done | bytes 65568 | tf_op jit(solution)/shard_map/ppermute | solution.py:24
  53.2 1.3 %shard_map.156 = (f32[16,2048]{1,0:T(8,128)S(1)}, bf16[16,2048]{1,0:T(8,128)(2,1)S(1)}, bf16[16,2048]{1,0:T(8,128)(2,1)S(1)}, bf16[16,2048]{1,0:T(8,128)(2,1)S(1...) custom-call(s32[2]{0:T(128)S(1)} %pad_add_fusion.3.where_ref, ...), custom_call_target="tpu_custom_call" | custom-call | flops 5905580032 | bytes 4194304 | tf_op jit(solution)/shard_map/pallas_call | solution.py:45
  54.5 4.3 %collective-permute-start.21 = (bf16[16,2048]{1,0:T(8,128)(2,1)S(1)}, bf16[16,2048]{1,0:T(8,128)(2,1)S(1)}, u32[]{:S(2)}, u32[]{:S(2)}) collective-permute-start(bf16[16,2048]{1,0:T(8,128)(2,1)S(1)} %get-tuple-element.46), channel_id=1, source_target_pairs={{0,4},{4,0},{8,12},{12,8},{16,20},{20,16},{24,28},{28,24},{1,5},{5... | collective-permute-start | bytes 196616 | tf_op jit(solution)/shard_map/ppermute | solution.py:24
  58.9 1.9 %collective-permute-start.23 = (bf16[16,2048]{1,0:T(8,128)(2,1)S(1)}, bf16[16,2048]{1,0:T(8,128)(2,1)S(1)}, u32[]{:S(2)}, u32[]{:S(2)}) collective-permute-start(bf16[16,2048]{1,0:T(8,128)(2,1)S(1)} %get-tuple-element.47), channel_id=1, source_target_pairs={{0,4},{4,0},{8,12},{12,8},{16,20},{20,16},{24,28},{28,24},{1,5},{5... | collective-permute-start | bytes 196616 | tf_op jit(solution)/shard_map/ppermute | solution.py:24
  60.9 1.5 %collective-permute-start.25 = (bf16[16,2048]{1,0:T(8,128)(2,1)S(1)}, bf16[16,2048]{1,0:T(8,128)(2,1)S(1)}, u32[]{:S(2)}, u32[]{:S(2)}) collective-permute-start(bf16[16,2048]{1,0:T(8,128)(2,1)S(1)} %get-tuple-element.49), channel_id=1, source_target_pairs={{0,12},{4,8},{8,4},{12,0},{16,28},{20,24},{24,20},{28,16},{1,13},{... | collective-permute-start | bytes 196616 | tf_op jit(solution)/shard_map/ppermute | solution.py:24
  62.4 3.3 %collective-permute-start.22 = (bf16[16,2048]{1,0:T(8,128)(2,1)S(1)}, bf16[16,2048]{1,0:T(8,128)(2,1)S(1)}, u32[]{:S(2)}, u32[]{:S(2)}) collective-permute-start(bf16[16,2048]{1,0:T(8,128)(2,1)S(1)} %shard_map.158), channel_id=1, source_target_pairs={{0,24},{4,28},{8,16},{12,20},{16,8},{20,12},{24,0},{28,4},{1,25},{... | collective-permute-start | bytes 196616 | tf_op jit(solution)/shard_map/ppermute | solution.py:24
  66.0 2.9 %collective-permute-done.22.refs_1_ = bf16[16,2048]{1,0:T(8,128)(2,1)S(1)} collective-permute-done((bf16[16,2048]{1,0:T(8,128)(2,1)S(1)}, bf16[16,2048]{1,0:T(8,128)(2,1)S(1)}, u32[]{:S(2)}, u32[]{:S(2)}) %collective-permute-start.22) | collective-permute-done | bytes 65568 | tf_op jit(solution)/shard_map/ppermute | solution.py:24
  68.9 2.0 %collective-permute-done.20.refs_0_ = bf16[16,2048]{1,0:T(8,128)(2,1)S(1)} collective-permute-done((bf16[16,2048]{1,0:T(8,128)(2,1)S(1)}, bf16[16,2048]{1,0:T(8,128)(2,1)S(1)}, u32[]{:S(2)}, u32[]{:S(2)}) %collective-permute-start.20) | collective-permute-done | bytes 65568 | tf_op jit(solution)/shard_map/ppermute | solution.py:24
  70.9 0.7 shard_map.159
  71.6 1.0 collective-permute-start.29
  72.6 1.6 %collective-permute-start.31 = (bf16[16,2048]{1,0:T(8,128)(2,1)S(1)}, bf16[16,2048]{1,0:T(8,128)(2,1)S(1)}, u32[]{:S(2)}, u32[]{:S(2)}) collective-permute-start(bf16[16,2048]{1,0:T(8,128)(2,1)S(1)} %get-tuple-element.51.refs_0_), channel_id=1, source_target_pairs={{0,24},{4,28},{8,16},{12,20},{16,8},{20,12},{24,0},{28,4},{1,25},{... | collective-permute-start | bytes 196616 | tf_op jit(solution)/shard_map/ppermute | solution.py:24
  74.2 0.8 collective-permute-start.26
  75.0 1.6 %collective-permute-start.27 = (bf16[16,2048]{1,0:T(8,128)(2,1)S(1)}, bf16[16,2048]{1,0:T(8,128)(2,1)S(1)}, u32[]{:S(2)}, u32[]{:S(2)}) collective-permute-start(bf16[16,2048]{1,0:T(8,128)(2,1)S(1)} %get-tuple-element.51.refs_0_), channel_id=1, source_target_pairs={{0,8},{4,12},{8,0},{12,4},{16,24},{20,28},{24,16},{28,20},{1,9},{5... | collective-permute-start | bytes 196616 | tf_op jit(solution)/shard_map/ppermute | solution.py:24
  76.5 1.2 collective-permute-start.28
  77.9 2.3 %collective-permute-start.30 = (bf16[16,2048]{1,0:T(8,128)(2,1)S(1)}, bf16[16,2048]{1,0:T(8,128)(2,1)S(1)}, u32[]{:S(2)}, u32[]{:S(2)}) collective-permute-start(bf16[16,2048]{1,0:T(8,128)(2,1)S(1)} %collective-permute-done.29.refs_4_), channel_id=1, source_target_pairs={{0,4},{4,0},{8,12},{12,8},{16,20},{20,16},{24,28},{28,24},{1,5},{5... | collective-permute-start | bytes 196616 | tf_op jit(solution)/shard_map/ppermute | solution.py:24
  80.4 1.7 %collective-permute-done.28.refs_3_ = bf16[16,2048]{1,0:T(8,128)(2,1)S(1)} collective-permute-done((bf16[16,2048]{1,0:T(8,128)(2,1)S(1)}, bf16[16,2048]{1,0:T(8,128)(2,1)S(1)}, u32[]{:S(2)}, u32[]{:S(2)}) %collective-permute-start.28) | collective-permute-done | bytes 65568 | tf_op jit(solution)/shard_map/ppermute | solution.py:24
  82.1 1.5 %collective-permute-done.30.refs_5_ = bf16[16,2048]{1,0:T(8,128)(2,1)S(1)} collective-permute-done((bf16[16,2048]{1,0:T(8,128)(2,1)S(1)}, bf16[16,2048]{1,0:T(8,128)(2,1)S(1)}, u32[]{:S(2)}, u32[]{:S(2)}) %collective-permute-start.30) | collective-permute-done | bytes 65568 | tf_op jit(solution)/shard_map/ppermute | solution.py:24
  83.6 0.9 collective-permute-done.32.refs_7_
  84.5 1.8 %shard_map.160 = (bf16[128,2048]{1,0:T(8,128)(2,1)S(1)}, f32[64,1920]{1,0:T(8,128)S(1)}, bf16[64,1920]{1,0:T(8,128)(2,1)S(1)}) custom-call(s32[2]{0:T(128)S(1)} %pad_add_fusion.3.where_ref, f32[1,2048]{1,0:T(1,128)S(1)} %bitcast.23, bf16[16,2048]{1,0:T(8,128)(2,1)S(1)} %get-tuple-element.51.refs_0_, bf16[16,2048]{1,0:T(8,128)(2,1)S(1)} %collective-permute-done.26.refs_1_, ...), custom_call_target="tpu_custom_call" | custom-call | flops 6308233216 | bytes 8388608 | tf_op jit(solution)/shard_map/pallas_call | solution.py:45
  86.4 1.1 shard_map.161
  87.6 0.5 collective-permute-start.35
  88.2 1.6 %collective-permute-start.34 = (bf16[32,1920]{1,0:T(8,128)(2,1)S(1)}, bf16[32,1920]{1,0:T(8,128)(2,1)S(1)}, u32[]{:S(2)}, u32[]{:S(2)}) collective-permute-start(bf16[32,1920]{1,0:T(8,128)(2,1)S(1)} %slice.78), channel_id=1, source_target_pairs={{0,2},{1,3},{2,0},{3,1},{4,6},{5,7},{6,4},{7,5},{8,10},{9,11},{10,... | collective-permute-start | bytes 368648 | tf_op jit(solution)/shard_map/ppermute | solution.py:24
  89.9 1.0 collective-permute-start.36
  90.9 3.5 %collective-permute-done.34 = bf16[32,1920]{1,0:T(8,128)(2,1)S(1)} collective-permute-done((bf16[32,1920]{1,0:T(8,128)(2,1)S(1)}, bf16[32,1920]{1,0:T(8,128)(2,1)S(1)}, u32[]{:S(2)}, u32[]{:S(2)}) %collective-permute-start.34) | collective-permute-done | bytes 122912 | tf_op jit(solution)/shard_map/ppermute | solution.py:24
  94.7 1.3 %collective-permute-done.36 = bf16[32,1792]{1,0:T(8,128)(2,1)S(1)} collective-permute-done((bf16[32,1792]{1,0:T(8,128)(2,1)S(1)}, bf16[32,1792]{1,0:T(8,128)(2,1)S(1)}, u32[]{:S(2)}, u32[]{:S(2)}) %collective-permute-start.36) | collective-permute-done | bytes 114720 | tf_op jit(solution)/shard_map/ppermute | solution.py:24
  96.2 1.6 %collective-permute-start.38 = (bf16[32,1792]{1,0:T(8,128)(2,1)S(1)}, bf16[32,1792]{1,0:T(8,128)(2,1)S(1)}, u32[]{:S(2)}, u32[]{:S(2)}) collective-permute-start(bf16[32,1792]{1,0:T(8,128)(2,1)S(1)} %fusion.2.refs_0_), channel_id=1, source_target_pairs={{0,2},{1,3},{2,0},{3,1},{4,6},{5,7},{6,4},{7,5},{8,10},{9,11},{10,... | collective-permute-start | bytes 344072 | tf_op jit(solution)/shard_map/ppermute | solution.py:24
  97.8 3.2 %collective-permute-done.38.refs_2_ = bf16[32,1792]{1,0:T(8,128)(2,1)S(1)} collective-permute-done((bf16[32,1792]{1,0:T(8,128)(2,1)S(1)}, bf16[32,1792]{1,0:T(8,128)(2,1)S(1)}, u32[]{:S(2)}, u32[]{:S(2)}) %collective-permute-start.38) | collective-permute-done | bytes 114720 | tf_op jit(solution)/shard_map/ppermute | solution.py:24
  101.0 1.3 %collective-permute-done.39.refs_3_ = bf16[32,1792]{1,0:T(8,128)(2,1)S(1)} collective-permute-done((bf16[32,1792]{1,0:T(8,128)(2,1)S(1)}, bf16[32,1792]{1,0:T(8,128)(2,1)S(1)}, u32[]{:S(2)}, u32[]{:S(2)}) %collective-permute-start.39) | collective-permute-done | bytes 114720 | tf_op jit(solution)/shard_map/ppermute | solution.py:24
  102.3 1.7 %shard_map.162 = (f32[16,2048]{1,0:T(8,128)S(1)}, bf16[16,2048]{1,0:T(8,128)(2,1)S(1)}, bf16[16,2048]{1,0:T(8,128)(2,1)S(1)}, bf16[16,2048]{1,0:T(8,128)(2,1)S(1...) custom-call(s32[2]{0:T(128)S(1)} %pad_add_fusion.3.where_ref, ...), custom_call_target="tpu_custom_call" | custom-call | flops 6308233216 | bytes 7340032 | tf_op jit(solution)/shard_map/pallas_call | solution.py:45
  104.0 1.0 collective-permute-start.42
  105.0 1.1 collective-permute-start.40
  106.1 0.9 collective-permute-start.44
  107.1 0.7 collective-permute-start.45
  107.7 1.9 %collective-permute-start.46 = (bf16[16,2048]{1,0:T(8,128)(2,1)S(1)}, bf16[16,2048]{1,0:T(8,128)(2,1)S(1)}, u32[]{:S(2)}, u32[]{:S(2)}) collective-permute-start(bf16[16,2048]{1,0:T(8,128)(2,1)S(1)} %get-tuple-element.63), channel_id=1, source_target_pairs={{0,12},{4,8},{8,4},{12,0},{16,28},{20,24},{24,20},{28,16},{1,13},{... | collective-permute-start | bytes 196616 | tf_op jit(solution)/shard_map/ppermute | solution.py:24
  109.6 1.8 %collective-permute-start.43 = (bf16[16,2048]{1,0:T(8,128)(2,1)S(1)}, bf16[16,2048]{1,0:T(8,128)(2,1)S(1)}, u32[]{:S(2)}, u32[]{:S(2)}) collective-permute-start(bf16[16,2048]{1,0:T(8,128)(2,1)S(1)} %shard_map.164), channel_id=1, source_target_pairs={{0,24},{4,28},{8,16},{12,20},{16,8},{20,12},{24,0},{28,4},{1,25},{... | collective-permute-start | bytes 196616 | tf_op jit(solution)/shard_map/ppermute | solution.py:24
  111.8 1.1 collective-permute-done.46.refs_4_
  112.9 2.9 %collective-permute-done.43.refs_1_ = bf16[16,2048]{1,0:T(8,128)(2,1)S(1)} collective-permute-done((bf16[16,2048]{1,0:T(8,128)(2,1)S(1)}, bf16[16,2048]{1,0:T(8,128)(2,1)S(1)}, u32[]{:S(2)}, u32[]{:S(2)}) %collective-permute-start.43) | collective-permute-done | bytes 65568 | tf_op jit(solution)/shard_map/ppermute | solution.py:24
  115.8 2.0 %collective-permute-done.41.refs_0_ = bf16[16,2048]{1,0:T(8,128)(2,1)S(1)} collective-permute-done((bf16[16,2048]{1,0:T(8,128)(2,1)S(1)}, bf16[16,2048]{1,0:T(8,128)(2,1)S(1)}, u32[]{:S(2)}, u32[]{:S(2)}) %collective-permute-start.41) | collective-permute-done | bytes 65568 | tf_op jit(solution)/shard_map/ppermute | solution.py:24
  117.7 0.7 shard_map.165
  (103 shorter events, 4.3 us)
Async XLA Ops:
  0.6 10.5 %copy-start.1 = (bf16[8,8,1024]{2,1,0:T(8,128)(2,1)S(1)}, bf16[8,8,1024]{2,1,0:T(8,128)(2,1)}, u32[]{:S(2)}) copy-start(bf16[8,8,1024]{2,1,0:T(8,128)(2,1)} %keys_ref.1) | copy-start | bytes 393220
  0.6 10.5 %copy-start.2 = (bf16[8,8,1024]{2,1,0:T(8,128)(2,1)S(1)}, bf16[8,8,1024]{2,1,0:T(8,128)(2,1)}, u32[]{:S(2)}) copy-start(bf16[8,8,1024]{2,1,0:T(8,128)(2,1)} %values_ref.1) | copy-start | bytes 393220
  0.7 0.8 copy-start.3
  1.5 0.8 copy-start.4
  2.2 14.4 %copy-start.8 = (s32[64]{0:T(128)S(1)}, s32[64]{0:T(128)}, u32[]{:S(2)}) copy-start(s32[64]{0:T(128)} %param.18) | copy-start | bytes 772
  2.2 22.6 %copy-start.5 = (f32[2048]{0:T(1024)S(1)}, f32[2048]{0:T(1024)}, u32[]{:S(2)}) copy-start(f32[2048]{0:T(1024)} %param.19) | copy-start | bytes 24580
  2.2 14.7 %collective-permute-start.3 = (bf16[16,2048]{1,0:T(8,128)(2,1)S(1)}, bf16[16,2048]{1,0:T(8,128)(2,1)S(1)}, u32[]{:S(2)}, u32[]{:S(2)}) collective-permute-start(bf16[16,2048]{1,0:T(8,128)(2,1)S(1)} %shard_map.149.after_ref.refs_0_.refs_5_), channel_id=1, source_target_pairs={{0,16},{4,20},{8,24},{12,28},{16,0},{20,4},{24,8},{28,12},{1,17},{... | collective-permute-start | bytes 196616 | tf_op jit(solution)/shard_map/ppermute | solution.py:24
  6.3 12.7 %collective-permute-start.5 = (bf16[16,2048]{1,0:T(8,128)(2,1)S(1)}, bf16[16,2048]{1,0:T(8,128)(2,1)S(1)}, u32[]{:S(2)}, u32[]{:S(2)}) collective-permute-start(bf16[16,2048]{1,0:T(8,128)(2,1)S(1)} %shard_map.149.after_ref.refs_0_.refs_5_), channel_id=1, source_target_pairs={{0,24},{4,28},{8,16},{12,20},{16,8},{20,12},{24,0},{28,4},{1,25},{... | collective-permute-start | bytes 196616 | tf_op jit(solution)/shard_map/ppermute | solution.py:24
  7.7 11.5 %collective-permute-start = (bf16[16,2048]{1,0:T(8,128)(2,1)S(1)}, bf16[16,2048]{1,0:T(8,128)(2,1)S(1)}, u32[]{:S(2)}, u32[]{:S(2)}) collective-permute-start(bf16[16,2048]{1,0:T(8,128)(2,1)S(1)} %shard_map.149.after_ref.refs_0_.refs_5_), channel_id=1, source_target_pairs={{0,4},{4,0},{8,12},{12,8},{16,20},{20,16},{24,28},{28,24},{1,5},{5... | collective-permute-start | bytes 196616 | tf_op jit(solution)/shard_map/ppermute | solution.py:24
  9.2 10.0 %collective-permute-start.1 = (bf16[16,2048]{1,0:T(8,128)(2,1)S(1)}, bf16[16,2048]{1,0:T(8,128)(2,1)S(1)}, u32[]{:S(2)}, u32[]{:S(2)}) collective-permute-start(bf16[16,2048]{1,0:T(8,128)(2,1)S(1)} %shard_map.149.after_ref.refs_0_.refs_5_), channel_id=1, source_target_pairs={{0,8},{4,12},{8,0},{12,4},{16,24},{20,28},{24,16},{28,20},{1,9},{5... | collective-permute-start | bytes 196616 | tf_op jit(solution)/shard_map/ppermute | solution.py:24
  9.4 9.8 %collective-permute-start.2 = (bf16[16,2048]{1,0:T(8,128)(2,1)S(1)}, bf16[16,2048]{1,0:T(8,128)(2,1)S(1)}, u32[]{:S(2)}, u32[]{:S(2)}) collective-permute-start(bf16[16,2048]{1,0:T(8,128)(2,1)S(1)} %shard_map.149.after_ref.refs_0_.refs_5_), channel_id=1, source_target_pairs={{0,12},{4,8},{8,4},{12,0},{16,28},{20,24},{24,20},{28,16},{1,13},{... | collective-permute-start | bytes 196616 | tf_op jit(solution)/shard_map/ppermute | solution.py:24
  11.9 12.9 %all-to-all-start = ((bf16[8,2,8,8,128]{4,3,2,1,0:T(8,128)(2,1)}), bf16[8,2,8,8,128]{4,3,2,1,0:T(8,128)(2,1)S(1)}, u32[]{:S(2)}, u32[]{:S(2)}) async-start(bf16[8,2,8,8,128]{4,3,2,1,0:T(8,128)(2,1)} %shard_map.150), calls=%async_computation | async-start | bytes 524288 | tf_op jit(solution)/shard_map/all_to_all | solution.py:540
  16.9 4.5 %collective-permute-start.4 = (bf16[16,2048]{1,0:T(8,128)(2,1)S(1)}, bf16[16,2048]{1,0:T(8,128)(2,1)S(1)}, u32[]{:S(2)}, u32[]{:S(2)}) collective-permute-start(bf16[16,2048]{1,0:T(8,128)(2,1)S(1)} %collective-permute-done.3.refs_4_), channel_id=1, source_target_pairs={{0,4},{4,0},{8,12},{12,8},{16,20},{20,16},{24,28},{28,24},{1,5},{5... | collective-permute-start | bytes 196616 | tf_op jit(solution)/shard_map/ppermute | solution.py:24
  19.0 4.6 %collective-permute-start.6 = (bf16[16,2048]{1,0:T(8,128)(2,1)S(1)}, bf16[16,2048]{1,0:T(8,128)(2,1)S(1)}, u32[]{:S(2)}, u32[]{:S(2)}) collective-permute-start(bf16[16,2048]{1,0:T(8,128)(2,1)S(1)} %collective-permute-done.5.refs_6_), channel_id=1, source_target_pairs={{0,4},{4,0},{8,12},{12,8},{16,20},{20,16},{24,28},{28,24},{1,5},{5... | collective-permute-start | bytes 196616 | tf_op jit(solution)/shard_map/ppermute | solution.py:24
  29.4 2.3 %collective-permute-start.7 = (bf16[128,384]{1,0:T(8,128)(2,1)S(1)}, bf16[128,384]{1,0:T(8,128)(2,1)S(1)}, u32[]{:S(2)}, u32[]{:S(2)}) collective-permute-start(bf16[128,384]{1,0:T(8,128)(2,1)S(1)} %get-tuple-element.33.own_ref), channel_id=1, source_target_pairs={{0,1},{1,0},{2,3},{3,2},{4,5},{5,4},{6,7},{7,6},{8,9},{9,8},{10,11... | collective-permute-start | bytes 294920 | tf_op jit(solution)/shard_map/ppermute | solution.py:24
  29.6 9.2 %collective-permute-start.14 = (bf16[128,8,128]{2,1,0:T(8,128)(2,1)S(1)}, bf16[128,8,128]{2,1,0:T(8,128)(2,1)S(1)}, u32[]{:S(2)}, u32[]{:S(2)}) collective-permute-start(bf16[128,8,128]{2,1,0:T(8,128)(2,1)S(1)} %bitcast.13), channel_id=1, source_target_pairs={{0,2},{1,3},{2,0},{3,1},{4,6},{5,7},{6,4},{7,5},{8,10},{9,11},{10,... | collective-permute-start | bytes 786440 | tf_op jit(solution)/shard_map/ppermute | solution.py:24
  31.2 11.3 %collective-permute-start.13 = (bf16[128,8,128]{2,1,0:T(8,128)(2,1)S(1)}, bf16[128,8,128]{2,1,0:T(8,128)(2,1)S(1)}, u32[]{:S(2)}, u32[]{:S(2)}) collective-permute-start(bf16[128,8,128]{2,1,0:T(8,128)(2,1)S(1)} %bitcast.14), channel_id=1, source_target_pairs={{0,1},{1,0},{2,3},{3,2},{4,5},{5,4},{6,7},{7,6},{8,9},{9,8},{10,11... | collective-permute-start | bytes 786440 | tf_op jit(solution)/shard_map/ppermute | solution.py:24
  31.4 1.5 %collective-permute-start.11 = (bf16[64,1024]{1,0:T(8,128)(2,1)S(1)}, bf16[64,1024]{1,0:T(8,128)(2,1)S(1)}, u32[]{:S(2)}, u32[]{:S(2)}) collective-permute-start(bf16[64,1024]{1,0:T(8,128)(2,1)S(1)} %get-tuple-element.38), channel_id=1, source_target_pairs={{0,1},{1,0},{2,3},{3,2},{4,5},{5,4},{6,7},{7,6},{8,9},{9,8},{10,11... | collective-permute-start | bytes 393224 | tf_op jit(solution)/shard_map/ppermute | solution.py:24
  31.9 9.0 %collective-permute-start.8 = (bf16[128,384]{1,0:T(8,128)(2,1)S(1)}, bf16[128,384]{1,0:T(8,128)(2,1)S(1)}, u32[]{:S(2)}, u32[]{:S(2)}) collective-permute-start(bf16[128,384]{1,0:T(8,128)(2,1)S(1)} %shard_map.152.own_ref), channel_id=1, source_target_pairs={{0,2},{1,3},{2,0},{3,1},{4,6},{5,7},{6,4},{7,5},{8,10},{9,11},{10,... | collective-permute-start | bytes 294920 | tf_op jit(solution)/shard_map/ppermute | solution.py:24
  33.0 9.6 %copy-start.7 = (f32[4,128]{1,0:T(4,128)S(1)}, f32[4,128]{1,0:T(4,128)}, u32[]{:S(2)}) copy-start(f32[4,128]{1,0:T(4,128)} %constant.71.clone.rope_ref) | copy-start | bytes 6148
  33.0 9.5 %collective-permute-start.12 = (bf16[32,1024]{1,0:T(8,128)(2,1)S(1)}, bf16[32,1024]{1,0:T(8,128)(2,1)S(1)}, u32[]{:S(2)}, u32[]{:S(2)}) collective-permute-start(bf16[32,1024]{1,0:T(8,128)(2,1)S(1)} %slice.80), channel_id=1, source_target_pairs={{0,2},{1,3},{2,0},{3,1},{4,6},{5,7},{6,4},{7,5},{8,10},{9,11},{10,... | collective-permute-start | bytes 196616 | tf_op jit(solution)/shard_map/ppermute | solution.py:24
  38.8 3.8 %collective-permute-start.15 = (bf16[128,8,128]{2,1,0:T(8,128)(2,1)S(1)}, bf16[128,8,128]{2,1,0:T(8,128)(2,1)S(1)}, u32[]{:S(2)}, u32[]{:S(2)}) collective-permute-start(bf16[128,8,128]{2,1,0:T(8,128)(2,1)S(1)} %collective-permute-done.14.refs_4_), channel_id=1, source_target_pairs={{0,1},{1,0},{2,3},{3,2},{4,5},{5,4},{6,7},{7,6},{8,9},{9,8},{10,11... | collective-permute-start | bytes 786440 | tf_op jit(solution)/shard_map/ppermute | solution.py:24
  41.6 4.9 %collective-permute-start.10 = (bf16[128,128]{1,0:T(8,128)(2,1)S(1)}, bf16[128,128]{1,0:T(8,128)(2,1)S(1)}, u32[]{:S(2)}, u32[]{:S(2)}) collective-permute-start(bf16[128,128]{1,0:T(8,128)(2,1)S(1)} %get-tuple-element.35), channel_id=1, source_target_pairs={{0,4},{4,12},{8,20},{12,28},{16,0},{20,8},{24,16},{28,24},{1,5},{5... | collective-permute-start | bytes 98312 | tf_op jit(solution)/shard_map/ppermute | solution.py:504
  41.8 4.6 %collective-permute-start.9 = (bf16[128,128]{1,0:T(8,128)(2,1)S(1)}, bf16[128,128]{1,0:T(8,128)(2,1)S(1)}, u32[]{:S(2)}, u32[]{:S(2)}) collective-permute-start(bf16[128,128]{1,0:T(8,128)(2,1)S(1)} %get-tuple-element.34), channel_id=1, source_target_pairs={{0,0},{4,8},{8,16},{12,24},{16,4},{20,12},{24,20},{28,28},{1,1},{5... | collective-permute-start | bytes 98312 | tf_op jit(solution)/shard_map/ppermute | solution.py:504
  46.4 6.7 %copy-start = (bf16[1024,2048]{1,0:T(8,128)(2,1)S(1)}, bf16[1024,2048]{1,0:T(8,128)(2,1)}, u32[]{:S(2)}) copy-start(bf16[1024,2048]{1,0:T(8,128)(2,1)} %refs_4_.2) | copy-start | bytes 12582916
  47.6 4.3 %collective-permute-start.17 = (bf16[32,1024]{1,0:T(8,128)(2,1)S(1)}, bf16[32,1024]{1,0:T(8,128)(2,1)S(1)}, u32[]{:S(2)}, u32[]{:S(2)}) collective-permute-start(bf16[32,1024]{1,0:T(8,128)(2,1)S(1)} %shard_map.155.refs_0_), channel_id=1, source_target_pairs={{0,2},{1,3},{2,0},{3,1},{4,6},{5,7},{6,4},{7,5},{8,10},{9,11},{10,... | collective-permute-start | bytes 196616 | tf_op jit(solution)/shard_map/ppermute | solution.py:24
  49.2 2.8 %collective-permute-start.16 = (bf16[32,1024]{1,0:T(8,128)(2,1)S(1)}, bf16[32,1024]{1,0:T(8,128)(2,1)S(1)}, u32[]{:S(2)}, u32[]{:S(2)}) collective-permute-start(bf16[32,1024]{1,0:T(8,128)(2,1)S(1)} %shard_map.155.refs_0_), channel_id=1, source_target_pairs={{0,1},{1,0},{2,3},{3,2},{4,5},{5,4},{6,7},{7,6},{8,9},{9,8},{10,11... | collective-permute-start | bytes 196616 | tf_op jit(solution)/shard_map/ppermute | solution.py:24
  51.9 1.3 %collective-permute-start.18 = (bf16[32,1024]{1,0:T(8,128)(2,1)S(1)}, bf16[32,1024]{1,0:T(8,128)(2,1)S(1)}, u32[]{:S(2)}, u32[]{:S(2)}) collective-permute-start(bf16[32,1024]{1,0:T(8,128)(2,1)S(1)} %collective-permute-done.17.refs_2_), channel_id=1, source_target_pairs={{0,1},{1,0},{2,3},{3,2},{4,5},{5,4},{6,7},{7,6},{8,9},{9,8},{10,11... | collective-permute-start | bytes 196616 | tf_op jit(solution)/shard_map/ppermute | solution.py:24
  54.5 7.9 %collective-permute-start.21 = (bf16[16,2048]{1,0:T(8,128)(2,1)S(1)}, bf16[16,2048]{1,0:T(8,128)(2,1)S(1)}, u32[]{:S(2)}, u32[]{:S(2)}) collective-permute-start(bf16[16,2048]{1,0:T(8,128)(2,1)S(1)} %get-tuple-element.46), channel_id=1, source_target_pairs={{0,4},{4,0},{8,12},{12,8},{16,20},{20,16},{24,28},{28,24},{1,5},{5... | collective-permute-start | bytes 196616 | tf_op jit(solution)/shard_map/ppermute | solution.py:24
  58.8 6.9 %collective-permute-start.19 = (bf16[16,2048]{1,0:T(8,128)(2,1)S(1)}, bf16[16,2048]{1,0:T(8,128)(2,1)S(1)}, u32[]{:S(2)}, u32[]{:S(2)}) collective-permute-start(bf16[16,2048]{1,0:T(8,128)(2,1)S(1)} %get-tuple-element.45), channel_id=1, source_target_pairs={{0,4},{4,0},{8,12},{12,8},{16,20},{20,16},{24,28},{28,24},{1,5},{5... | collective-permute-start | bytes 196616 | tf_op jit(solution)/shard_map/ppermute | solution.py:24
  58.9 6.9 %collective-permute-start.23 = (bf16[16,2048]{1,0:T(8,128)(2,1)S(1)}, bf16[16,2048]{1,0:T(8,128)(2,1)S(1)}, u32[]{:S(2)}, u32[]{:S(2)}) collective-permute-start(bf16[16,2048]{1,0:T(8,128)(2,1)S(1)} %get-tuple-element.47), channel_id=1, source_target_pairs={{0,4},{4,0},{8,12},{12,8},{16,20},{20,16},{24,28},{28,24},{1,5},{5... | collective-permute-start | bytes 196616 | tf_op jit(solution)/shard_map/ppermute | solution.py:24
  60.8 5.0 %collective-permute-start.24 = (bf16[16,2048]{1,0:T(8,128)(2,1)S(1)}, bf16[16,2048]{1,0:T(8,128)(2,1)S(1)}, u32[]{:S(2)}, u32[]{:S(2)}) collective-permute-start(bf16[16,2048]{1,0:T(8,128)(2,1)S(1)} %get-tuple-element.48), channel_id=1, source_target_pairs={{0,8},{4,12},{8,0},{12,4},{16,24},{20,28},{24,16},{28,20},{1,9},{5... | collective-permute-start | bytes 196616 | tf_op jit(solution)/shard_map/ppermute | solution.py:24
  60.9 5.2 %collective-permute-start.25 = (bf16[16,2048]{1,0:T(8,128)(2,1)S(1)}, bf16[16,2048]{1,0:T(8,128)(2,1)S(1)}, u32[]{:S(2)}, u32[]{:S(2)}) collective-permute-start(bf16[16,2048]{1,0:T(8,128)(2,1)S(1)} %get-tuple-element.49), channel_id=1, source_target_pairs={{0,12},{4,8},{8,4},{12,0},{16,28},{20,24},{24,20},{28,16},{1,13},{... | collective-permute-start | bytes 196616 | tf_op jit(solution)/shard_map/ppermute | solution.py:24
  62.4 6.5 %collective-permute-start.22 = (bf16[16,2048]{1,0:T(8,128)(2,1)S(1)}, bf16[16,2048]{1,0:T(8,128)(2,1)S(1)}, u32[]{:S(2)}, u32[]{:S(2)}) collective-permute-start(bf16[16,2048]{1,0:T(8,128)(2,1)S(1)} %shard_map.158), channel_id=1, source_target_pairs={{0,24},{4,28},{8,16},{12,20},{16,8},{20,12},{24,0},{28,4},{1,25},{... | collective-permute-start | bytes 196616 | tf_op jit(solution)/shard_map/ppermute | solution.py:24
  65.6 18.8 %slice-start = ((s8[7340032]{0:T(1024)(128)(4,1)}), s8[4194304]{0:T(1024)(128)(4,1)S(1)}, s32[]{:S(2)}) async-start(s8[7340032]{0:T(1024)(128)(4,1)} %bitcast.16), calls=%async_computation.1 | async-start | bytes 8388608
  65.7 5.2 %collective-permute-start.20 = (bf16[16,2048]{1,0:T(8,128)(2,1)S(1)}, bf16[16,2048]{1,0:T(8,128)(2,1)S(1)}, u32[]{:S(2)}, u32[]{:S(2)}) collective-permute-start(bf16[16,2048]{1,0:T(8,128)(2,1)S(1)} %shard_map.157), channel_id=1, source_target_pairs={{0,16},{4,20},{8,24},{12,28},{16,0},{20,4},{24,8},{28,12},{1,17},{... | collective-permute-start | bytes 196616 | tf_op jit(solution)/shard_map/ppermute | solution.py:24
  70.9 13.6 %slice-start.1 = ((s8[7340032]{0:T(1024)(128)(4,1)}), s8[3145728]{0:T(1024)(128)(4,1)S(1)}, s32[]{:S(2)}) async-start(s8[7340032]{0:T(1024)(128)(4,1)} %bitcast.16), calls=%async_computation.2 | async-start | bytes 6291456
  70.9 13.6 %copy-start.6 = (f32[2048]{0:T(1024)S(1)}, f32[2048]{0:T(1024)}, u32[]{:S(2)}) copy-start(f32[2048]{0:T(1024)} %param.20) | copy-start | bytes 24580
  70.9 15.5 %slice-start.2 = ((s8[7340032]{0:T(1024)(128)(4,1)}), s8[4194304]{0:T(1024)(128)(4,1)S(1)}, s32[]{:S(2)}) async-start(s8[7340032]{0:T(1024)(128)(4,1)} %bitcast.18), calls=%async_computation.3 | async-start | bytes 8388608
  71.6 6.3 %collective-permute-start.29 = (bf16[16,2048]{1,0:T(8,128)(2,1)S(1)}, bf16[16,2048]{1,0:T(8,128)(2,1)S(1)}, u32[]{:S(2)}, u32[]{:S(2)}) collective-permute-start(bf16[16,2048]{1,0:T(8,128)(2,1)S(1)} %get-tuple-element.51.refs_0_), channel_id=1, source_target_pairs={{0,16},{4,20},{8,24},{12,28},{16,0},{20,4},{24,8},{28,12},{1,17},{... | collective-permute-start | bytes 196616 | tf_op jit(solution)/shard_map/ppermute | solution.py:24
  72.6 7.6 %collective-permute-start.31 = (bf16[16,2048]{1,0:T(8,128)(2,1)S(1)}, bf16[16,2048]{1,0:T(8,128)(2,1)S(1)}, u32[]{:S(2)}, u32[]{:S(2)}) collective-permute-start(bf16[16,2048]{1,0:T(8,128)(2,1)S(1)} %get-tuple-element.51.refs_0_), channel_id=1, source_target_pairs={{0,24},{4,28},{8,16},{12,20},{16,8},{20,12},{24,0},{28,4},{1,25},{... | collective-permute-start | bytes 196616 | tf_op jit(solution)/shard_map/ppermute | solution.py:24
  74.2 6.0 %collective-permute-start.26 = (bf16[16,2048]{1,0:T(8,128)(2,1)S(1)}, bf16[16,2048]{1,0:T(8,128)(2,1)S(1)}, u32[]{:S(2)}, u32[]{:S(2)}) collective-permute-start(bf16[16,2048]{1,0:T(8,128)(2,1)S(1)} %get-tuple-element.51.refs_0_), channel_id=1, source_target_pairs={{0,4},{4,0},{8,12},{12,8},{16,20},{20,16},{24,28},{28,24},{1,5},{5... | collective-permute-start | bytes 196616 | tf_op jit(solution)/shard_map/ppermute | solution.py:24
  75.0 5.5 %collective-permute-start.27 = (bf16[16,2048]{1,0:T(8,128)(2,1)S(1)}, bf16[16,2048]{1,0:T(8,128)(2,1)S(1)}, u32[]{:S(2)}, u32[]{:S(2)}) collective-permute-start(bf16[16,2048]{1,0:T(8,128)(2,1)S(1)} %get-tuple-element.51.refs_0_), channel_id=1, source_target_pairs={{0,8},{4,12},{8,0},{12,4},{16,24},{20,28},{24,16},{28,20},{1,9},{5... | collective-permute-start | bytes 196616 | tf_op jit(solution)/shard_map/ppermute | solution.py:24
  76.5 5.6 %collective-permute-start.28 = (bf16[16,2048]{1,0:T(8,128)(2,1)S(1)}, bf16[16,2048]{1,0:T(8,128)(2,1)S(1)}, u32[]{:S(2)}, u32[]{:S(2)}) collective-permute-start(bf16[16,2048]{1,0:T(8,128)(2,1)S(1)} %get-tuple-element.51.refs_0_), channel_id=1, source_target_pairs={{0,12},{4,8},{8,4},{12,0},{16,28},{20,24},{24,20},{28,16},{1,13},{... | collective-permute-start | bytes 196616 | tf_op jit(solution)/shard_map/ppermute | solution.py:24
  77.9 5.6 %collective-permute-start.30 = (bf16[16,2048]{1,0:T(8,128)(2,1)S(1)}, bf16[16,2048]{1,0:T(8,128)(2,1)S(1)}, u32[]{:S(2)}, u32[]{:S(2)}) collective-permute-start(bf16[16,2048]{1,0:T(8,128)(2,1)S(1)} %collective-permute-done.29.refs_4_), channel_id=1, source_target_pairs={{0,4},{4,0},{8,12},{12,8},{16,20},{20,16},{24,28},{28,24},{1,5},{5... | collective-permute-start | bytes 196616 | tf_op jit(solution)/shard_map/ppermute | solution.py:24
  80.2 4.3 %collective-permute-start.32 = (bf16[16,2048]{1,0:T(8,128)(2,1)S(1)}, bf16[16,2048]{1,0:T(8,128)(2,1)S(1)}, u32[]{:S(2)}, u32[]{:S(2)}) collective-permute-start(bf16[16,2048]{1,0:T(8,128)(2,1)S(1)} %collective-permute-done.31.refs_6_), channel_id=1, source_target_pairs={{0,4},{4,0},{8,12},{12,8},{16,20},{20,16},{24,28},{28,24},{1,5},{5... | collective-permute-start | bytes 196616 | tf_op jit(solution)/shard_map/ppermute | solution.py:24
  84.5 1.9 %slice-start.3 = ((s8[7340032]{0:T(1024)(128)(4,1)}), s8[3145728]{0:T(1024)(128)(4,1)S(1)}, s32[]{:S(2)}) async-start(s8[7340032]{0:T(1024)(128)(4,1)} %bitcast.18), calls=%async_computation.4 | async-start | bytes 6291456
  84.5 17.8 %slice-start.4 = ((s8[7340032]{0:T(1024)(128)(4,1)}), s8[4194304]{0:T(1024)(128)(4,1)S(1)}, s32[]{:S(2)}) async-start(s8[7340032]{0:T(1024)(128)(4,1)} %bitcast.20), calls=%async_computation.5 | async-start | bytes 8388608
  86.3 1.8 %collective-permute-start.33 = (bf16[64,1920]{1,0:T(8,128)(2,1)S(1)}, bf16[64,1920]{1,0:T(8,128)(2,1)S(1)}, u32[]{:S(2)}, u32[]{:S(2)}) collective-permute-start(bf16[64,1920]{1,0:T(8,128)(2,1)S(1)} %get-tuple-element.53), channel_id=1, source_target_pairs={{0,1},{1,0},{2,3},{3,2},{4,5},{5,4},{6,7},{7,6},{8,9},{9,8},{10,11... | collective-permute-start | bytes 737288 | tf_op jit(solution)/shard_map/ppermute | solution.py:24
  86.4 15.9 %slice-start.5 = ((s8[7340032]{0:T(1024)(128)(4,1)}), s8[3145728]{0:T(1024)(128)(4,1)S(1)}, s32[]{:S(2)}) async-start(s8[7340032]{0:T(1024)(128)(4,1)} %bitcast.20), calls=%async_computation.6 | async-start | bytes 6291456
  87.6 2.2 %collective-permute-start.35 = (bf16[64,1792]{1,0:T(8,128)(2,1)S(1)}, bf16[64,1792]{1,0:T(8,128)(2,1)S(1)}, u32[]{:S(2)}, u32[]{:S(2)}) collective-permute-start(bf16[64,1792]{1,0:T(8,128)(2,1)S(1)} %get-tuple-element.56), channel_id=1, source_target_pairs={{0,1},{1,0},{2,3},{3,2},{4,5},{5,4},{6,7},{7,6},{8,9},{9,8},{10,11... | collective-permute-start | bytes 688136 | tf_op jit(solution)/shard_map/ppermute | solution.py:24
  88.2 6.2 %collective-permute-start.34 = (bf16[32,1920]{1,0:T(8,128)(2,1)S(1)}, bf16[32,1920]{1,0:T(8,128)(2,1)S(1)}, u32[]{:S(2)}, u32[]{:S(2)}) collective-permute-start(bf16[32,1920]{1,0:T(8,128)(2,1)S(1)} %slice.78), channel_id=1, source_target_pairs={{0,2},{1,3},{2,0},{3,1},{4,6},{5,7},{6,4},{7,5},{8,10},{9,11},{10,... | collective-permute-start | bytes 368648 | tf_op jit(solution)/shard_map/ppermute | solution.py:24
  89.9 6.1 %collective-permute-start.36 = (bf16[32,1792]{1,0:T(8,128)(2,1)S(1)}, bf16[32,1792]{1,0:T(8,128)(2,1)S(1)}, u32[]{:S(2)}, u32[]{:S(2)}) collective-permute-start(bf16[32,1792]{1,0:T(8,128)(2,1)S(1)} %slice.79), channel_id=1, source_target_pairs={{0,2},{1,3},{2,0},{3,1},{4,6},{5,7},{6,4},{7,5},{8,10},{9,11},{10,... | collective-permute-start | bytes 344072 | tf_op jit(solution)/shard_map/ppermute | solution.py:24
  96.2 4.9 %collective-permute-start.38 = (bf16[32,1792]{1,0:T(8,128)(2,1)S(1)}, bf16[32,1792]{1,0:T(8,128)(2,1)S(1)}, u32[]{:S(2)}, u32[]{:S(2)}) collective-permute-start(bf16[32,1792]{1,0:T(8,128)(2,1)S(1)} %fusion.2.refs_0_), channel_id=1, source_target_pairs={{0,2},{1,3},{2,0},{3,1},{4,6},{5,7},{6,4},{7,5},{8,10},{9,11},{10,... | collective-permute-start | bytes 344072 | tf_op jit(solution)/shard_map/ppermute | solution.py:24
  97.8 3.3 %collective-permute-start.37 = (bf16[32,1792]{1,0:T(8,128)(2,1)S(1)}, bf16[32,1792]{1,0:T(8,128)(2,1)S(1)}, u32[]{:S(2)}, u32[]{:S(2)}) collective-permute-start(bf16[32,1792]{1,0:T(8,128)(2,1)S(1)} %fusion.2.refs_0_), channel_id=1, source_target_pairs={{0,1},{1,0},{2,3},{3,2},{4,5},{5,4},{6,7},{7,6},{8,9},{9,8},{10,11... | collective-permute-start | bytes 344072 | tf_op jit(solution)/shard_map/ppermute | solution.py:24
  101.0 1.3 %collective-permute-start.39 = (bf16[32,1792]{1,0:T(8,128)(2,1)S(1)}, bf16[32,1792]{1,0:T(8,128)(2,1)S(1)}, u32[]{:S(2)}, u32[]{:S(2)}) collective-permute-start(bf16[32,1792]{1,0:T(8,128)(2,1)S(1)} %collective-permute-done.38.refs_2_), channel_id=1, source_target_pairs={{0,1},{1,0},{2,3},{3,2},{4,5},{5,4},{6,7},{7,6},{8,9},{9,8},{10,11... | collective-permute-start | bytes 344072 | tf_op jit(solution)/shard_map/ppermute | solution.py:24
  104.0 5.6 %collective-permute-start.42 = (bf16[16,2048]{1,0:T(8,128)(2,1)S(1)}, bf16[16,2048]{1,0:T(8,128)(2,1)S(1)}, u32[]{:S(2)}, u32[]{:S(2)}) collective-permute-start(bf16[16,2048]{1,0:T(8,128)(2,1)S(1)} %get-tuple-element.60), channel_id=1, source_target_pairs={{0,4},{4,0},{8,12},{12,8},{16,20},{20,16},{24,28},{28,24},{1,5},{5... | collective-permute-start | bytes 196616 | tf_op jit(solution)/shard_map/ppermute | solution.py:24
  105.0 6.4 %collective-permute-start.40 = (bf16[16,2048]{1,0:T(8,128)(2,1)S(1)}, bf16[16,2048]{1,0:T(8,128)(2,1)S(1)}, u32[]{:S(2)}, u32[]{:S(2)}) collective-permute-start(bf16[16,2048]{1,0:T(8,128)(2,1)S(1)} %get-tuple-element.59), channel_id=1, source_target_pairs={{0,4},{4,0},{8,12},{12,8},{16,20},{20,16},{24,28},{28,24},{1,5},{5... | collective-permute-start | bytes 196616 | tf_op jit(solution)/shard_map/ppermute | solution.py:24
  106.1 5.6 %collective-permute-start.44 = (bf16[16,2048]{1,0:T(8,128)(2,1)S(1)}, bf16[16,2048]{1,0:T(8,128)(2,1)S(1)}, u32[]{:S(2)}, u32[]{:S(2)}) collective-permute-start(bf16[16,2048]{1,0:T(8,128)(2,1)S(1)} %get-tuple-element.61), channel_id=1, source_target_pairs={{0,4},{4,0},{8,12},{12,8},{16,20},{20,16},{24,28},{28,24},{1,5},{5... | collective-permute-start | bytes 196616 | tf_op jit(solution)/shard_map/ppermute | solution.py:24
  107.1 4.7 %collective-permute-start.45 = (bf16[16,2048]{1,0:T(8,128)(2,1)S(1)}, bf16[16,2048]{1,0:T(8,128)(2,1)S(1)}, u32[]{:S(2)}, u32[]{:S(2)}) collective-permute-start(bf16[16,2048]{1,0:T(8,128)(2,1)S(1)} %get-tuple-element.62), channel_id=1, source_target_pairs={{0,8},{4,12},{8,0},{12,4},{16,24},{20,28},{24,16},{28,20},{1,9},{5... | collective-permute-start | bytes 196616 | tf_op jit(solution)/shard_map/ppermute | solution.py:24
  107.7 5.2 %collective-permute-start.46 = (bf16[16,2048]{1,0:T(8,128)(2,1)S(1)}, bf16[16,2048]{1,0:T(8,128)(2,1)S(1)}, u32[]{:S(2)}, u32[]{:S(2)}) collective-permute-start(bf16[16,2048]{1,0:T(8,128)(2,1)S(1)} %get-tuple-element.63), channel_id=1, source_target_pairs={{0,12},{4,8},{8,4},{12,0},{16,28},{20,24},{24,20},{28,16},{1,13},{... | collective-permute-start | bytes 196616 | tf_op jit(solution)/shard_map/ppermute | solution.py:24
  109.6 6.1 %collective-permute-start.43 = (bf16[16,2048]{1,0:T(8,128)(2,1)S(1)}, bf16[16,2048]{1,0:T(8,128)(2,1)S(1)}, u32[]{:S(2)}, u32[]{:S(2)}) collective-permute-start(bf16[16,2048]{1,0:T(8,128)(2,1)S(1)} %shard_map.164), channel_id=1, source_target_pairs={{0,24},{4,28},{8,16},{12,20},{16,8},{20,12},{24,0},{28,4},{1,25},{... | collective-permute-start | bytes 196616 | tf_op jit(solution)/shard_map/ppermute | solution.py:24
  111.5 6.3 %collective-permute-start.41 = (bf16[16,2048]{1,0:T(8,128)(2,1)S(1)}, bf16[16,2048]{1,0:T(8,128)(2,1)S(1)}, u32[]{:S(2)}, u32[]{:S(2)}) collective-permute-start(bf16[16,2048]{1,0:T(8,128)(2,1)S(1)} %shard_map.163), channel_id=1, source_target_pairs={{0,16},{4,20},{8,24},{12,28},{16,0},{20,4},{24,8},{28,12},{1,17},{... | collective-permute-start | bytes 196616 | tf_op jit(solution)/shard_map/ppermute | solution.py:24

commit v10 on v8

--- a/solution.py
+++ b/solution.py
@@ -57,14 +57,14 @@
     return jax.ShapeDtypeStruct(shape, dtype)
 
 
-def gather_rows(rows):
+def gather_rows(rows, near=None):
     groups = lax.axis_size("dp")
     close = min(groups, 4)
     blocks = {0: rows}
     for k in range(groups - 2, close - 1, -2):
         blocks[k] = swap(rows, "dp", k)
     for k in range(close - 1, 0, -1):
-        blocks[k] = swap(rows, "dp", k)
+        blocks[k] = swap(rows if near is None else near[k - 1], "dp", k)
     for k in range(groups - 2, close - 1, -2):
         blocks[k + 1] = swap(blocks[k], "dp", 1)
     return [blocks[k] for k in range(groups)]
@@ -107,43 +107,91 @@
 
 
 def stack_tokens(x_first, x_second):
+    def body(first_ref, second_ref, out_ref):
+        out_ref[...] = jnp.concatenate([first_ref[...].astype(F32), second_ref[...].astype(F32)], axis=0).astype(BF16)
+
     part_dev, features = x_first.shape
-
-    def body(first_ref, second_ref, out_ref, one, two, sems):
-        copies = [pltpu.make_async_copy(first_ref, one, sems.at[0]), pltpu.make_async_copy(second_ref, two, sems.at[1])]
-        for copy in copies:
-            copy.start()
-        for copy in copies:
-            copy.wait()
-        out_ref[...] = jnp.concatenate([one[...].astype(F32), two[...].astype(F32)], axis=0).astype(BF16)
+    return call(body, shaped((2 * part_dev, features)), (x_first, x_second), [VMEM] * 2)
+
+
+def cache_piece(where_ref, keys_ref, values_ref, k):
+    groups = lax.axis_size("dp")
+    head = lax.div((where_ref[0] ^ k) * KVH, groups)
+    lanes = pl.ds(pl.multiple_of(head * HD, HD), HD)
+    tiles_of = [ref[p, :, lanes].astype(F32) for ref in (keys_ref, values_ref) for p in range(keys_ref.shape[0])]
+    return jnp.concatenate(tiles_of, axis=1)
+
+
+def pack_near(where, x, cache_keys, cache_values):
+    part_dev, span, _ = cache_keys.shape
+    close = min(lax.axis_size("dp"), 4)
+    wide = 2 * part_dev * HD
+    joined = x.shape[1] == wide
+
+    def body(where_ref, x_ref, keys_ref, values_ref, own_ref, *out_refs):
+        own_ref[...] = cache_piece(where_ref, keys_ref, values_ref, 0).astype(BF16)
+        for k, out_ref in enumerate(out_refs, 1):
+            piece = cache_piece(where_ref, keys_ref, values_ref, k)
+            if joined:
+                piece = jnp.concatenate([x_ref[...].astype(F32), piece], axis=0)
+            out_ref[...] = piece.astype(BF16)
+
+    height = span + (x.shape[0] if joined else 0)
+    own, *near = call(
+        body,
+        (shaped((span, wide)),) + (shaped((height, wide)),) * (close - 1),
+        (where, x, cache_keys, cache_values),
+        [SMEM] + [VMEM] * 3,
+        flops=2 * AROUND,
+    )
+    return own, near, joined
+
+
+def pack_far(where, cache_keys, cache_values, afters):
+    groups = lax.axis_size("dp")
+    part_dev, span, _ = cache_keys.shape
+    wide = 2 * part_dev * HD
+    close = min(groups, 4)
+
+    def body(where_ref, keys_ref, values_ref, *refs):
+        for i, out_ref in enumerate(refs[len(afters) :]):
+            for odd in range(2):
+                out_ref[odd] = cache_piece(where_ref, keys_ref, values_ref, close + 2 * i + odd).astype(BF16)
 
     return call(
         body,
-        shaped((2 * part_dev, features)),
-        (x_first, x_second),
-        [HBM, HBM],
-        [pltpu.VMEM(x_first.shape, BF16), pltpu.VMEM(x_first.shape, BF16), pltpu.SemaphoreType.DMA((2,))],
-        limit=None,
-    )
-
-
-def pack(cache_keys, cache_values, after):
-    groups = lax.axis_size("dp")
-    part_dev, span, _ = cache_keys.shape
-
-    def body(keys_ref, values_ref, after_ref, out_ref):
-        for g in range(groups):
-            first = g * KVH // groups * HD
-            out_ref[g, 0] = keys_ref[:, :, first : first + HD]
-            out_ref[g, 1] = values_ref[:, :, first : first + HD]
-
-    return call(
-        body,
-        shaped((groups, 2, part_dev, span, HD)),
-        (cache_keys, cache_values, after),
-        [VMEM, VMEM, ANY],
-        flops=4 * AROUND,
-    )
+        (shaped((2, span, wide)),) * ((groups - close) // 2),
+        (where, cache_keys, cache_values, *afters),
+        [SMEM, VMEM, VMEM] + [ANY] * len(afters),
+        flops=AROUND,
+    )
+
+
+def collect_near(own, near, span):
+    def body(own_ref, *refs):
+        refs[-1][0] = own_ref[...]
+        for k, ref in enumerate(refs[:-1], 1):
+            refs[-1][k] = ref[...].astype(F32)[ref.shape[0] - span :].astype(BF16)
+
+    return call(body, shaped((1 + len(near),) + own.shape), (own, *near), [VMEM] * (1 + len(near)))
+
+
+def first_entries(pieces, entry):
+    def body(*refs):
+        for i, ref in enumerate(refs[:-1]):
+            refs[-1][i] = ref[entry]
+
+    return call(body, shaped((len(pieces),) + pieces[0].shape[1:]), pieces, [VMEM] * len(pieces))
+
+
+def collect_far(pieces, passed):
+    def body(*refs):
+        for i, ref in enumerate(refs[:-2]):
+            refs[-1][2 * i] = ref[0]
+            refs[-1][2 * i + 1] = refs[-2][i]
+
+    shape = (2 * len(pieces),) + pieces[0].shape[1:]
+    return call(body, shaped(shape), (*pieces, passed), [VMEM] * (1 + len(pieces)))
 
 
 def lift(where_ref, gain_ref, block_refs, h_ref, ss_ref, absolute):
@@ -158,7 +206,7 @@
         g = d ^ k
         place = slot(lax.div(g, near) ^ t, tensor) * near + lax.rem(g, near)
         place = pl.multiple_of(place * pair, pair)
-        wide = block_refs[k][...].astype(F32)
+        wide = block_refs[k][...].astype(F32)[:pair]
         squares = jnp.broadcast_to(jnp.sum(wide * wide, axis=1, keepdims=True), (pair, 128))
         ss_ref[pl.ds(pl.multiple_of(g * pair, pair) if absolute else place, pair), :] = squares
         h_ref[pl.ds(place, pair), :] = (wide * gain).astype(BF16)
@@ -379,12 +427,12 @@
     return call(body, outs, ins, [VMEM] * len(ins), moved=8 * own.size)
 
 
-def attend_cached(where, anc, rope, scale, queries, cache, part_dev):
+def attend_cached(where, anc, rope, scale, queries, near_cache, far_cache, part_dev):
     tensor = lax.axis_size("tensor")
     groups = lax.axis_size("dp")
     near = groups // tensor
     pair = 2 * part_dev
-    span = cache[0].shape[1]
+    close, span, _ = near_cache[0].shape
     ctx = tensor * span
     columns = queries[0].shape[1]
     heads = columns // HD
@@ -393,8 +441,9 @@
 
     def body(where_ref, anc_ref, rope_ref, scale_ref, *refs):
         q_refs, refs = refs[: len(queries)], refs[len(queries) :]
-        cache_refs, (query_ref, mixed_ref, highest_ref, total_ref, keys_ref, values_ref) = refs[:tensor], refs[tensor:]
-        t = where_ref[1]
+        near_refs, far_refs = refs[:tensor], refs[tensor : 2 * tensor]
+        query_ref, mixed_ref, highest_ref, total_ref, keys_ref, values_ref = refs[2 * tensor :]
+        d, t = where_ref[0], where_ref[1]
         query_sum = q_refs[0][...]
         for ref in q_refs[1:]:
             query_sum = query_sum + ref[...].astype(F32)
@@ -402,15 +451,25 @@
         for step in range(2):
 
             def bring(i, _, step=step):
-                if step == 0:
-                    block, member = t * near + lax.div(i, part_dev), lax.rem(i, part_dev)
-                else:
-                    block, member = lax.div(anc_ref[i], part_dev), lax.rem(anc_ref[i], part_dev)
-                place = block * pair + member
-                for k in range(tensor):
-                    start = pl.multiple_of(i * ctx + k * span, 8)
-                    keys_ref[pl.ds(start, span), :] = cache_refs[k][place].astype(F32)
-                    values_ref[pl.ds(start, span), :] = cache_refs[k][place + part_dev].astype(F32)
+                particle = t * parts + i if step == 0 else anc_ref[i]
+                block, member = lax.div(particle, part_dev) ^ d, lax.rem(particle, part_dev)
+
+                def load(cache_refs, entry):
+                    for k, cache_ref in enumerate(cache_refs):
+                        to = pl.ds(pl.multiple_of(i * ctx + k * span, 8), span)
+                        lanes = pl.ds(pl.multiple_of(member * HD, HD), HD)
+                        keys_ref[to, :] = cache_ref[entry, :, lanes].astype(F32)
+                        lanes = pl.ds(pl.multiple_of((part_dev + member) * HD, HD), HD)
+                        values_ref[to, :] = cache_ref[entry, :, lanes].astype(F32)
+
+                @pl.when(block < close)
+                def _():
+                    load(near_refs, block)
+
+                @pl.when(block >= close)
+                def _():
+                    load(far_refs, block - close)
+
                 return 0
 
             lax.fori_loop(0, parts, bring, 0)
@@ -438,7 +497,7 @@
             highest_ref[here, :] = jnp.broadcast_to(highest, (rows, 128))
             total_ref[here, :] = jnp.broadcast_to(jnp.sum(weights, axis=1, keepdims=True), (rows, 128))
 
-    ins = (where, anc, rope, scale, *queries, *cache)
+    ins = (where, anc, rope, scale, *queries, *near_cache, *far_cache)
     return call(
         body,
         (shaped((2 * rows, HD)), shaped((2 * rows, HD), F32), shaped((2 * rows, 128), F32), shaped((2 * rows, 128), F32)),
@@ -534,9 +593,14 @@
     where = jnp.stack([d, t]).astype(jnp.int32)
 
     x = stack_tokens(x_first, x_second)
-    blocks = gather_rows(x)
-    cache = lax.all_to_all(pack(cache_keys, cache_values, x), "dp", split_axis=0, concat_axis=0, tiled=True)
-    caches = gather_blocks(cache.reshape(groups * pair, span, HD))
+    own_piece, near_pieces, joined = pack_near(where, x, cache_keys, cache_values)
+    blocks = gather_rows(x, near_pieces if joined else None)
+    close = min(groups, 4)
+    near_moved = blocks[1:close] if joined else [swap(piece, "dp", k) for k, piece in enumerate(near_pieces, 1)]
+    near_cache = gather_blocks(collect_near(own_piece, near_moved, span))
+    far_pieces = pack_far(where, cache_keys, cache_values, blocks[close::2])
+    far_pieces = [swap(piece, "dp", close + 2 * i) for i, piece in enumerate(far_pieces)]
+    far_cache = gather_blocks(collect_far(far_pieces, swap(first_entries(far_pieces, 1), "dp", 1)))
 
     message, *queries = project_attention(where, blocks, attn_gain, w_keyval, w_query)
     bits = 1
@@ -558,7 +622,7 @@
     second = jnp.stack([row_of(anc, 0), row_of(own, 1)], axis=1)
     targets = jnp.concatenate([jnp.tile(first, (heads, 1)), jnp.tile(second, (heads, 1))]).astype(jnp.int32)
     rope = jnp.asarray(np.stack(rope_tables(context) + rope_tables(context + 1)))
-    state = attend_cached(where, anc, rope, scale, [queries] + queries_arrived, caches, part_dev)
+    state = attend_cached(where, anc, rope, scale, [queries] + queries_arrived, near_cache, far_cache, part_dev)
     mixed = attend_new(where, rope, targets, pieces, state, queries.shape, part_dev)
 
     parts = project_back(where, gather_blocks(mixed), w_out)

time: 119 us -> 115 us (0.966)
  waiting for transfers between devices: 41.9 us -> 37.8 us
  starting transfers between devices: 56.5 us -> 58.2 us
  local copies, waits for them, and re-layouts: 3.48 us -> 1.99 us
    ppermute x45 -> x51, starting transfers between devices: 50 us -> 56 us  [swap(): return lax.ppermute(x, axis, [(i, i ^ bits) for i in range(size)])]
    all_to_all x1 -> x0, starting transfers between devices: 4.68 us -> none  [local(): lax.all_to_all(pack(cache_keys, cache_values, x), 'dp', split_axis=0, con...]
    ppermute x45 -> x51, waiting for transfers between devices: 40.8 us -> 37.8 us  [swap(): return lax.ppermute(x, axis, [(i, i ^ bits) for i in range(size)])]
    unnamed x34, local copies, waits for them, and re-layouts: 3.13 us -> 1.63 us
    pallas_call x17 -> x21, Pallas kernels: 15 us -> 14.5 us  [call(): pl.pallas_call(body, out_shape=outs, in_specs=specs, out_specs=jax.tree.m...]
  transfers between devices with their start and end apart: 48 -> 53, of which waited for: 21 -> 22; matrix products, arithmetic and copies ran while one was open for 1% -> 1% of each run, Pallas kernels for 5% -> 6%
where the time goes in v10:
time: 115 us; the launch traced here: 114 us
  starting transfers between devices  58.2 us (51%)
  waiting for transfers between devices  37.8 us (33%)
  Pallas kernels  14.5 us (13%)
  local copies, waits for them, and re-layouts  1.99 us (2%)
    ppermute x51, starting transfers between devices, swap(): return lax.ppermute(x, axis, [(i, i ^ bits) for i in range(size)])  56 us
    ppermute x51, waiting for transfers between devices, swap(): return lax.ppermute(x, axis, [(i, i ^ bits) for i in range(size)])  37.8 us
    pallas_call x21, Pallas kernels, call(): pl.pallas_call(body, out_shape=outs, in_specs=specs, out_specs=jax.tree.m...  14.5 us
  transfers between devices with their start and end apart: 53, of which 22 were waited for; matrix products, arithmetic and copies ran while one was open for 1% of the time, Pallas kernels for 6%

profile of v10, /device:TPU:0, one launch (start us, length us, event | category | flops | bytes accessed | tf_op | source)
XLA Modules:
  0.0 114.3 jit_solution(1240845147418742589)
XLA Ops:
  0.7 0.8 copy-done.5
  1.5 0.8 copy-done.6
  2.2 4.0 %collective-permute-start.3 = (bf16[16,2048]{1,0:T(8,128)(2,1)S(1)}, bf16[16,2048]{1,0:T(8,128)(2,1)S(1)}, u32[]{:S(2)}, u32[]{:S(2)}) collective-permute-start(bf16[16,2048]{1,0:T(8,128)(2,1)S(1)} %shard_map.149.x_ref.refs_0_.refs_5_), channel_id=1, source_target_pairs={{0,16},{4,20},{8,24},{12,28},{16,0},{20,4},{24,8},{28,12},{1,17},{... | collective-permute-start | bytes 196616 | tf_op jit(solution)/shard_map/ppermute | solution.py:24
  6.3 1.3 %collective-permute-start.5 = (bf16[16,2048]{1,0:T(8,128)(2,1)S(1)}, bf16[16,2048]{1,0:T(8,128)(2,1)S(1)}, u32[]{:S(2)}, u32[]{:S(2)}) collective-permute-start(bf16[16,2048]{1,0:T(8,128)(2,1)S(1)} %shard_map.149.x_ref.refs_0_.refs_5_), channel_id=1, source_target_pairs={{0,24},{4,28},{8,16},{12,20},{16,8},{20,12},{24,0},{28,4},{1,25},{... | collective-permute-start | bytes 196616 | tf_op jit(solution)/shard_map/ppermute | solution.py:24
  7.7 0.6 shard_map.150
  8.3 1.6 %collective-permute-start = (bf16[24,2048]{1,0:T(8,128)(2,1)S(1)}, bf16[24,2048]{1,0:T(8,128)(2,1)S(1)}, u32[]{:S(2)}, u32[]{:S(2)}) collective-permute-start(bf16[24,2048]{1,0:T(8,128)(2,1)S(1)} %get-tuple-element.39), channel_id=1, source_target_pairs={{0,4},{4,0},{8,12},{12,8},{16,20},{20,16},{24,28},{28,24},{1,5},{5... | collective-permute-start | bytes 294920 | tf_op jit(solution)/shard_map/ppermute | solution.py:24
  10.1 1.8 %collective-permute-start.2 = (bf16[24,2048]{1,0:T(8,128)(2,1)S(1)}, bf16[24,2048]{1,0:T(8,128)(2,1)S(1)}, u32[]{:S(2)}, u32[]{:S(2)}) collective-permute-start(bf16[24,2048]{1,0:T(8,128)(2,1)S(1)} %get-tuple-element.41), channel_id=1, source_target_pairs={{0,12},{4,8},{8,4},{12,0},{16,28},{20,24},{24,20},{28,16},{1,13},{... | collective-permute-start | bytes 294920 | tf_op jit(solution)/shard_map/ppermute | solution.py:24
  12.5 0.6 shard_map.155
  13.1 2.8 %collective-permute-start.16 = (bf16[2,8,2048]{2,1,0:T(8,128)(2,1)S(1)}, bf16[2,8,2048]{2,1,0:T(8,128)(2,1)S(1)}, u32[]{:S(2)}, u32[]{:S(2)}) collective-permute-start(bf16[2,8,2048]{2,1,0:T(8,128)(2,1)S(1)} %get-tuple-element.49), channel_id=1, source_target_pairs={{0,16},{4,20},{8,24},{12,28},{16,0},{20,4},{24,8},{28,12},{1,17},{... | collective-permute-start | bytes 196616 | tf_op jit(solution)/shard_map/ppermute | solution.py:24
  16.3 1.6 %collective-permute-start.4 = (bf16[16,2048]{1,0:T(8,128)(2,1)S(1)}, bf16[16,2048]{1,0:T(8,128)(2,1)S(1)}, u32[]{:S(2)}, u32[]{:S(2)}) collective-permute-start(bf16[16,2048]{1,0:T(8,128)(2,1)S(1)} %collective-permute-done.3.refs_4_.refs_0_), channel_id=1, source_target_pairs={{0,4},{4,0},{8,12},{12,8},{16,20},{20,16},{24,28},{28,24},{1,5},{5... | collective-permute-start | bytes 196616 | tf_op jit(solution)/shard_map/ppermute | solution.py:24
  18.4 1.8 %collective-permute-start.14 = (bf16[4,8,2048]{2,1,0:T(8,128)(2,1)S(1)}, bf16[4,8,2048]{2,1,0:T(8,128)(2,1)S(1)}, u32[]{:S(2)}, u32[]{:S(2)}) collective-permute-start(bf16[4,8,2048]{2,1,0:T(8,128)(2,1)S(1)} %shard_map.154.refs_2_), channel_id=1, source_target_pairs={{0,2},{1,3},{2,0},{3,1},{4,6},{5,7},{6,4},{7,5},{8,10},{9,11},{10,... | collective-permute-start | bytes 393224 | tf_op jit(solution)/shard_map/ppermute | solution.py:24
  20.2 1.8 %collective-permute-done.17.refs_1_ = bf16[2,8,2048]{2,1,0:T(8,128)(2,1)S(1)} collective-permute-done((bf16[2,8,2048]{2,1,0:T(8,128)(2,1)S(1)}, bf16[2,8,2048]{2,1,0:T(8,128)(2,1)S(1)}, u32[]{:S(2)}, u32[]{:S(2)}) %collective-permute-start.17) | collective-permute-done | bytes 65568 | tf_op jit(solution)/shard_map/ppermute | solution.py:24
  22.0 1.5 %collective-permute-start.18 = (bf16[2,8,2048]{2,1,0:T(8,128)(2,1)S(1)}, bf16[2,8,2048]{2,1,0:T(8,128)(2,1)S(1)}, u32[]{:S(2)}, u32[]{:S(2)}) collective-permute-start(bf16[2,8,2048]{2,1,0:T(8,128)(2,1)S(1)} %shard_map.156), channel_id=1, source_target_pairs={{0,4},{4,0},{8,12},{12,8},{16,20},{20,16},{24,28},{28,24},{1,5},{5... | collective-permute-start | bytes 196616 | tf_op jit(solution)/shard_map/ppermute | solution.py:24
  23.6 1.5 %shard_map.151 = (bf16[128,384]{1,0:T(8,128)(2,1)S(1)}, f32[64,1024]{1,0:T(8,128)S(1)}, bf16[64,1024]{1,0:T(8,128)(2,1)S(1)}) custom-call(s32[2]{0:T(128)S(1)} %pad_add_fusion.3.where_ref, f32[1,2048]{1,0:T(1,128)S(1)} %bitcast.18, bf16[16,2048]{1,0:T(8,128)(2,1)S(1)} %shard_map.149.x_ref.refs_0_.refs_5_, ...), custom_call_target="tpu_custom_call" | custom-call | flops 6039797760 | bytes 6291456 | tf_op jit(solution)/shard_map/pallas_call | solution.py:45
  25.7 0.6 collective-permute-done.18.refs_2_
  26.3 1.6 %collective-permute-start.20 = (bf16[4,8,2048]{2,1,0:T(8,128)(2,1)S(1)}, bf16[4,8,2048]{2,1,0:T(8,128)(2,1)S(1)}, u32[]{:S(2)}, u32[]{:S(2)}) collective-permute-start(bf16[4,8,2048]{2,1,0:T(8,128)(2,1)S(1)} %shard_map.157.refs_6_), channel_id=1, source_target_pairs={{0,2},{1,3},{2,0},{3,1},{4,6},{5,7},{6,4},{7,5},{8,10},{9,11},{10,... | collective-permute-start | bytes 393224 | tf_op jit(solution)/shard_map/ppermute | solution.py:24
  29.0 4.5 %collective-permute-done.8.arrived_ref = bf16[128,384]{1,0:T(8,128)(2,1)S(1)} collective-permute-done((bf16[128,384]{1,0:T(8,128)(2,1)S(1)}, bf16[128,384]{1,0:T(8,128)(2,1)S(1)}, u32[]{:S(2)}, u32[]{:S(2)}) %collective-permute-start.8) | collective-permute-done | bytes 98336 | tf_op jit(solution)/shard_map/ppermute | solution.py:24
  33.4 1.5 %collective-permute-start.12 = (bf16[32,1024]{1,0:T(8,128)(2,1)S(1)}, bf16[32,1024]{1,0:T(8,128)(2,1)S(1)}, u32[]{:S(2)}, u32[]{:S(2)}) collective-permute-start(bf16[32,1024]{1,0:T(8,128)(2,1)S(1)} %slice.80), channel_id=1, source_target_pairs={{0,2},{1,3},{2,0},{3,1},{4,6},{5,7},{6,4},{7,5},{8,10},{9,11},{10,... | collective-permute-start | bytes 196616 | tf_op jit(solution)/shard_map/ppermute | solution.py:24
  35.0 0.7 shard_map.153
  35.7 1.6 %collective-permute-start.10 = (bf16[128,128]{1,0:T(8,128)(2,1)S(1)}, bf16[128,128]{1,0:T(8,128)(2,1)S(1)}, u32[]{:S(2)}, u32[]{:S(2)}) collective-permute-start(bf16[128,128]{1,0:T(8,128)(2,1)S(1)} %get-tuple-element.44), channel_id=1, source_target_pairs={{0,4},{4,12},{8,20},{12,28},{16,0},{20,8},{24,16},{28,24},{1,5},{5... | collective-permute-start | bytes 98312 | tf_op jit(solution)/shard_map/ppermute | solution.py:561
  37.7 0.7 collective-permute-start.9
  38.4 2.4 %shard_map.158 = (bf16[256,128]{1,0:T(8,128)(2,1)S(1)}, f32[256,128]{1,0:T(8,128)S(1)}, f32[256,128]{1,0:T(8,128)S(1)}, f32[256,128]{1,0:T(8,128)S(1)}) custom-call(s32[2]{0:T(128)S(1)} %pad_add_fusion.3.where_ref, s32[16]{0:T(128)S(1)} %get-tuple-element.77.anc_ref, f32[4,128]{1,0:T(4,128)S(1)} %copy-done.9, f32[128,128]{1,0:T(8,128)S(1)} %get-tuple-element.45.scale_ref, ...), custom_call_target="tpu_custom_call" | custom-call | flops 5368709120 | bytes 4194304 | tf_op jit(solution)/shard_map/pallas_call | solution.py:45
  40.8 1.1 shard_map.159.refs_0_
  42.0 1.6 %collective-permute-start.23 = (bf16[32,1024]{1,0:T(8,128)(2,1)S(1)}, bf16[32,1024]{1,0:T(8,128)(2,1)S(1)}, u32[]{:S(2)}, u32[]{:S(2)}) collective-permute-start(bf16[32,1024]{1,0:T(8,128)(2,1)S(1)} %shard_map.159.refs_0_), channel_id=1, source_target_pairs={{0,2},{1,3},{2,0},{3,1},{4,6},{5,7},{6,4},{7,5},{8,10},{9,11},{10,... | collective-permute-start | bytes 196616 | tf_op jit(solution)/shard_map/ppermute | solution.py:24
  43.6 2.7 %collective-permute-done.23.refs_2_ = bf16[32,1024]{1,0:T(8,128)(2,1)S(1)} collective-permute-done((bf16[32,1024]{1,0:T(8,128)(2,1)S(1)}, bf16[32,1024]{1,0:T(8,128)(2,1)S(1)}, u32[]{:S(2)}, u32[]{:S(2)}) %collective-permute-start.23) | collective-permute-done | bytes 65568 | tf_op jit(solution)/shard_map/ppermute | solution.py:24
  46.3 1.2 %collective-permute-done.24.refs_3_ = bf16[32,1024]{1,0:T(8,128)(2,1)S(1)} collective-permute-done((bf16[32,1024]{1,0:T(8,128)(2,1)S(1)}, bf16[32,1024]{1,0:T(8,128)(2,1)S(1)}, u32[]{:S(2)}, u32[]{:S(2)}) %collective-permute-start.24) | collective-permute-done | bytes 65568 | tf_op jit(solution)/shard_map/ppermute | solution.py:24
  47.6 1.3 %shard_map.160 = (f32[16,2048]{1,0:T(8,128)S(1)}, bf16[16,2048]{1,0:T(8,128)(2,1)S(1)}, bf16[16,2048]{1,0:T(8,128)(2,1)S(1)}, bf16[16,2048]{1,0:T(8,128)(2,1)S(1...) custom-call(s32[2]{0:T(128)S(1)} %pad_add_fusion.3.where_ref, ...), custom_call_target="tpu_custom_call" | custom-call | flops 5905580032 | bytes 4194304 | tf_op jit(solution)/shard_map/pallas_call | solution.py:45
  48.9 6.1 %collective-permute-start.27 = (bf16[16,2048]{1,0:T(8,128)(2,1)S(1)}, bf16[16,2048]{1,0:T(8,128)(2,1)S(1)}, u32[]{:S(2)}, u32[]{:S(2)}) collective-permute-start(bf16[16,2048]{1,0:T(8,128)(2,1)S(1)} %get-tuple-element.58), channel_id=1, source_target_pairs={{0,4},{4,0},{8,12},{12,8},{16,20},{20,16},{24,28},{28,24},{1,5},{5... | collective-permute-start | bytes 196616 | tf_op jit(solution)/shard_map/ppermute | solution.py:24
  55.0 1.9 %collective-permute-start.29 = (bf16[16,2048]{1,0:T(8,128)(2,1)S(1)}, bf16[16,2048]{1,0:T(8,128)(2,1)S(1)}, u32[]{:S(2)}, u32[]{:S(2)}) collective-permute-start(bf16[16,2048]{1,0:T(8,128)(2,1)S(1)} %get-tuple-element.59), channel_id=1, source_target_pairs={{0,4},{4,0},{8,12},{12,8},{16,20},{20,16},{24,28},{28,24},{1,5},{5... | collective-permute-start | bytes 196616 | tf_op jit(solution)/shard_map/ppermute | solution.py:24
  57.0 1.5 %collective-permute-start.31 = (bf16[16,2048]{1,0:T(8,128)(2,1)S(1)}, bf16[16,2048]{1,0:T(8,128)(2,1)S(1)}, u32[]{:S(2)}, u32[]{:S(2)}) collective-permute-start(bf16[16,2048]{1,0:T(8,128)(2,1)S(1)} %get-tuple-element.61), channel_id=1, source_target_pairs={{0,12},{4,8},{8,4},{12,0},{16,28},{20,24},{24,20},{28,16},{1,13},{... | collective-permute-start | bytes 196616 | tf_op jit(solution)/shard_map/ppermute | solution.py:24
  58.5 2.4 %collective-permute-start.28 = (bf16[16,2048]{1,0:T(8,128)(2,1)S(1)}, bf16[16,2048]{1,0:T(8,128)(2,1)S(1)}, u32[]{:S(2)}, u32[]{:S(2)}) collective-permute-start(bf16[16,2048]{1,0:T(8,128)(2,1)S(1)} %shard_map.162), channel_id=1, source_target_pairs={{0,24},{4,28},{8,16},{12,20},{16,8},{20,12},{24,0},{28,4},{1,25},{... | collective-permute-start | bytes 196616 | tf_op jit(solution)/shard_map/ppermute | solution.py:24
  61.2 0.9 collective-permute-done.31.refs_4_
  62.1 2.7 %collective-permute-done.28.refs_1_ = bf16[16,2048]{1,0:T(8,128)(2,1)S(1)} collective-permute-done((bf16[16,2048]{1,0:T(8,128)(2,1)S(1)}, bf16[16,2048]{1,0:T(8,128)(2,1)S(1)}, u32[]{:S(2)}, u32[]{:S(2)}) %collective-permute-start.28) | collective-permute-done | bytes 65568 | tf_op jit(solution)/shard_map/ppermute | solution.py:24
  64.8 2.1 %collective-permute-done.26.refs_0_ = bf16[16,2048]{1,0:T(8,128)(2,1)S(1)} collective-permute-done((bf16[16,2048]{1,0:T(8,128)(2,1)S(1)}, bf16[16,2048]{1,0:T(8,128)(2,1)S(1)}, u32[]{:S(2)}, u32[]{:S(2)}) %collective-permute-start.26) | collective-permute-done | bytes 65568 | tf_op jit(solution)/shard_map/ppermute | solution.py:24
  66.9 0.7 shard_map.163
  67.8 1.9 %collective-permute-start.37 = (bf16[16,2048]{1,0:T(8,128)(2,1)S(1)}, bf16[16,2048]{1,0:T(8,128)(2,1)S(1)}, u32[]{:S(2)}, u32[]{:S(2)}) collective-permute-start(bf16[16,2048]{1,0:T(8,128)(2,1)S(1)} %get-tuple-element.63.refs_0_), channel_id=1, source_target_pairs={{0,24},{4,28},{8,16},{12,20},{16,8},{20,12},{24,0},{28,4},{1,25},{... | collective-permute-start | bytes 196616 | tf_op jit(solution)/shard_map/ppermute | solution.py:24
  69.7 1.5 %collective-permute-start.32 = (bf16[16,2048]{1,0:T(8,128)(2,1)S(1)}, bf16[16,2048]{1,0:T(8,128)(2,1)S(1)}, u32[]{:S(2)}, u32[]{:S(2)}) collective-permute-start(bf16[16,2048]{1,0:T(8,128)(2,1)S(1)} %get-tuple-element.63.refs_0_), channel_id=1, source_target_pairs={{0,4},{4,0},{8,12},{12,8},{16,20},{20,16},{24,28},{28,24},{1,5},{5... | collective-permute-start | bytes 196616 | tf_op jit(solution)/shard_map/ppermute | solution.py:24
  71.3 1.3 %collective-permute-start.33 = (bf16[16,2048]{1,0:T(8,128)(2,1)S(1)}, bf16[16,2048]{1,0:T(8,128)(2,1)S(1)}, u32[]{:S(2)}, u32[]{:S(2)}) collective-permute-start(bf16[16,2048]{1,0:T(8,128)(2,1)S(1)} %get-tuple-element.63.refs_0_), channel_id=1, source_target_pairs={{0,8},{4,12},{8,0},{12,4},{16,24},{20,28},{24,16},{28,20},{1,9},{5... | collective-permute-start | bytes 196616 | tf_op jit(solution)/shard_map/ppermute | solution.py:24
  72.5 0.7 collective-permute-start.34
  73.2 1.6 %collective-permute-done.35.refs_4_ = bf16[16,2048]{1,0:T(8,128)(2,1)S(1)} collective-permute-done((bf16[16,2048]{1,0:T(8,128)(2,1)S(1)}, bf16[16,2048]{1,0:T(8,128)(2,1)S(1)}, u32[]{:S(2)}, u32[]{:S(2)}) %collective-permute-start.35) | collective-permute-done | bytes 65568 | tf_op jit(solution)/shard_map/ppermute | solution.py:24
  74.8 0.9 collective-permute-start.36
  75.7 1.1 collective-permute-start.38
  76.8 1.0 collective-permute-done.34.refs_3_
  77.8 1.6 %collective-permute-done.36.refs_5_ = bf16[16,2048]{1,0:T(8,128)(2,1)S(1)} collective-permute-done((bf16[16,2048]{1,0:T(8,128)(2,1)S(1)}, bf16[16,2048]{1,0:T(8,128)(2,1)S(1)}, u32[]{:S(2)}, u32[]{:S(2)}) %collective-permute-start.36) | collective-permute-done | bytes 65568 | tf_op jit(solution)/shard_map/ppermute | solution.py:24
  79.4 0.7 collective-permute-done.38.refs_7_
  80.1 1.8 %shard_map.164 = (bf16[128,2048]{1,0:T(8,128)(2,1)S(1)}, f32[64,1920]{1,0:T(8,128)S(1)}, bf16[64,1920]{1,0:T(8,128)(2,1)S(1)}) custom-call(s32[2]{0:T(128)S(1)} %pad_add_fusion.3.where_ref, f32[1,2048]{1,0:T(1,128)S(1)} %bitcast.19, bf16[16,2048]{1,0:T(8,128)(2,1)S(1)} %get-tuple-element.63.refs_0_, bf16[16,2048]{1,0:T(8,128)(2,1)S(1)} %collective-permute-done.32.refs_1_, ...), custom_call_target="tpu_custom_call" | custom-call | flops 6308233216 | bytes 8388608 | tf_op jit(solution)/shard_map/pallas_call | solution.py:45
  82.1 1.1 shard_map.165
  83.8 1.6 %collective-permute-start.40 = (bf16[32,1920]{1,0:T(8,128)(2,1)S(1)}, bf16[32,1920]{1,0:T(8,128)(2,1)S(1)}, u32[]{:S(2)}, u32[]{:S(2)}) collective-permute-start(bf16[32,1920]{1,0:T(8,128)(2,1)S(1)} %slice.78), channel_id=1, source_target_pairs={{0,2},{1,3},{2,0},{3,1},{4,6},{5,7},{6,4},{7,5},{8,10},{9,11},{10,... | collective-permute-start | bytes 368648 | tf_op jit(solution)/shard_map/ppermute | solution.py:24
  85.5 1.0 collective-permute-start.42
  86.6 3.5 %collective-permute-done.40 = bf16[32,1920]{1,0:T(8,128)(2,1)S(1)} collective-permute-done((bf16[32,1920]{1,0:T(8,128)(2,1)S(1)}, bf16[32,1920]{1,0:T(8,128)(2,1)S(1)}, u32[]{:S(2)}, u32[]{:S(2)}) %collective-permute-start.40) | collective-permute-done | bytes 122912 | tf_op jit(solution)/shard_map/ppermute | solution.py:24
  90.3 1.3 %collective-permute-done.42 = bf16[32,1792]{1,0:T(8,128)(2,1)S(1)} collective-permute-done((bf16[32,1792]{1,0:T(8,128)(2,1)S(1)}, bf16[32,1792]{1,0:T(8,128)(2,1)S(1)}, u32[]{:S(2)}, u32[]{:S(2)}) %collective-permute-start.42) | collective-permute-done | bytes 114720 | tf_op jit(solution)/shard_map/ppermute | solution.py:24
  91.8 1.6 %collective-permute-start.44 = (bf16[32,1792]{1,0:T(8,128)(2,1)S(1)}, bf16[32,1792]{1,0:T(8,128)(2,1)S(1)}, u32[]{:S(2)}, u32[]{:S(2)}) collective-permute-start(bf16[32,1792]{1,0:T(8,128)(2,1)S(1)} %fusion.2.refs_0_), channel_id=1, source_target_pairs={{0,2},{1,3},{2,0},{3,1},{4,6},{5,7},{6,4},{7,5},{8,10},{9,11},{10,... | collective-permute-start | bytes 344072 | tf_op jit(solution)/shard_map/ppermute | solution.py:24
  93.4 3.3 %collective-permute-done.44.refs_2_ = bf16[32,1792]{1,0:T(8,128)(2,1)S(1)} collective-permute-done((bf16[32,1792]{1,0:T(8,128)(2,1)S(1)}, bf16[32,1792]{1,0:T(8,128)(2,1)S(1)}, u32[]{:S(2)}, u32[]{:S(2)}) %collective-permute-start.44) | collective-permute-done | bytes 114720 | tf_op jit(solution)/shard_map/ppermute | solution.py:24
  96.6 1.3 %collective-permute-done.45.refs_3_ = bf16[32,1792]{1,0:T(8,128)(2,1)S(1)} collective-permute-done((bf16[32,1792]{1,0:T(8,128)(2,1)S(1)}, bf16[32,1792]{1,0:T(8,128)(2,1)S(1)}, u32[]{:S(2)}, u32[]{:S(2)}) %collective-permute-start.45) | collective-permute-done | bytes 114720 | tf_op jit(solution)/shard_map/ppermute | solution.py:24
  98.0 1.7 %shard_map.166 = (f32[16,2048]{1,0:T(8,128)S(1)}, bf16[16,2048]{1,0:T(8,128)(2,1)S(1)}, bf16[16,2048]{1,0:T(8,128)(2,1)S(1)}, bf16[16,2048]{1,0:T(8,128)(2,1)S(1...) custom-call(s32[2]{0:T(128)S(1)} %pad_add_fusion.3.where_ref, ...), custom_call_target="tpu_custom_call" | custom-call | flops 6308233216 | bytes 7340032 | tf_op jit(solution)/shard_map/pallas_call | solution.py:45
  99.7 1.0 collective-permute-start.48
  100.7 1.1 collective-permute-start.46
  101.8 0.9 collective-permute-start.50
  103.0 2.3 %collective-permute-start.52 = (bf16[16,2048]{1,0:T(8,128)(2,1)S(1)}, bf16[16,2048]{1,0:T(8,128)(2,1)S(1)}, u32[]{:S(2)}, u32[]{:S(2)}) collective-permute-start(bf16[16,2048]{1,0:T(8,128)(2,1)S(1)} %get-tuple-element.75), channel_id=1, source_target_pairs={{0,12},{4,8},{8,4},{12,0},{16,28},{20,24},{24,20},{28,16},{1,13},{... | collective-permute-start | bytes 196616 | tf_op jit(solution)/shard_map/ppermute | solution.py:24
  105.3 1.8 %collective-permute-start.49 = (bf16[16,2048]{1,0:T(8,128)(2,1)S(1)}, bf16[16,2048]{1,0:T(8,128)(2,1)S(1)}, u32[]{:S(2)}, u32[]{:S(2)}) collective-permute-start(bf16[16,2048]{1,0:T(8,128)(2,1)S(1)} %shard_map.168), channel_id=1, source_target_pairs={{0,24},{4,28},{8,16},{12,20},{16,8},{20,12},{24,0},{28,4},{1,25},{... | collective-permute-start | bytes 196616 | tf_op jit(solution)/shard_map/ppermute | solution.py:24
  107.5 0.7 collective-permute-done.52.refs_4_
  108.2 3.2 %collective-permute-done.49.refs_1_ = bf16[16,2048]{1,0:T(8,128)(2,1)S(1)} collective-permute-done((bf16[16,2048]{1,0:T(8,128)(2,1)S(1)}, bf16[16,2048]{1,0:T(8,128)(2,1)S(1)}, u32[]{:S(2)}, u32[]{:S(2)}) %collective-permute-start.49) | collective-permute-done | bytes 65568 | tf_op jit(solution)/shard_map/ppermute | solution.py:24
  111.4 2.2 %collective-permute-done.47.refs_0_ = bf16[16,2048]{1,0:T(8,128)(2,1)S(1)} collective-permute-done((bf16[16,2048]{1,0:T(8,128)(2,1)S(1)}, bf16[16,2048]{1,0:T(8,128)(2,1)S(1)}, u32[]{:S(2)}, u32[]{:S(2)}) %collective-permute-start.47) | collective-permute-done | bytes 65568 | tf_op jit(solution)/shard_map/ppermute | solution.py:24
  113.6 0.7 shard_map.169
  (121 shorter events, 6.4 us)
Async XLA Ops:
  0.6 7.0 %copy-start.3 = (bf16[8,8,1024]{2,1,0:T(8,128)(2,1)S(1)}, bf16[8,8,1024]{2,1,0:T(8,128)(2,1)}, u32[]{:S(2)}) copy-start(bf16[8,8,1024]{2,1,0:T(8,128)(2,1)} %keys_ref.3) | copy-start | bytes 393220
  0.6 7.0 %copy-start.4 = (bf16[8,8,1024]{2,1,0:T(8,128)(2,1)S(1)}, bf16[8,8,1024]{2,1,0:T(8,128)(2,1)}, u32[]{:S(2)}) copy-start(bf16[8,8,1024]{2,1,0:T(8,128)(2,1)} %values_ref.3) | copy-start | bytes 393220
  2.2 10.1 %collective-permute-start.3 = (bf16[16,2048]{1,0:T(8,128)(2,1)S(1)}, bf16[16,2048]{1,0:T(8,128)(2,1)S(1)}, u32[]{:S(2)}, u32[]{:S(2)}) collective-permute-start(bf16[16,2048]{1,0:T(8,128)(2,1)S(1)} %shard_map.149.x_ref.refs_0_.refs_5_), channel_id=1, source_target_pairs={{0,16},{4,20},{8,24},{12,28},{16,0},{20,4},{24,8},{28,12},{1,17},{... | collective-permute-start | bytes 196616 | tf_op jit(solution)/shard_map/ppermute | solution.py:24
  6.3 6.2 %collective-permute-start.5 = (bf16[16,2048]{1,0:T(8,128)(2,1)S(1)}, bf16[16,2048]{1,0:T(8,128)(2,1)S(1)}, u32[]{:S(2)}, u32[]{:S(2)}) collective-permute-start(bf16[16,2048]{1,0:T(8,128)(2,1)S(1)} %shard_map.149.x_ref.refs_0_.refs_5_), channel_id=1, source_target_pairs={{0,24},{4,28},{8,16},{12,20},{16,8},{20,12},{24,0},{28,4},{1,25},{... | collective-permute-start | bytes 196616 | tf_op jit(solution)/shard_map/ppermute | solution.py:24
  8.3 8.0 %collective-permute-start = (bf16[24,2048]{1,0:T(8,128)(2,1)S(1)}, bf16[24,2048]{1,0:T(8,128)(2,1)S(1)}, u32[]{:S(2)}, u32[]{:S(2)}) collective-permute-start(bf16[24,2048]{1,0:T(8,128)(2,1)S(1)} %get-tuple-element.39), channel_id=1, source_target_pairs={{0,4},{4,0},{8,12},{12,8},{16,20},{20,16},{24,28},{28,24},{1,5},{5... | collective-permute-start | bytes 294920 | tf_op jit(solution)/shard_map/ppermute | solution.py:24
  9.8 8.1 %collective-permute-start.1 = (bf16[24,2048]{1,0:T(8,128)(2,1)S(1)}, bf16[24,2048]{1,0:T(8,128)(2,1)S(1)}, u32[]{:S(2)}, u32[]{:S(2)}) collective-permute-start(bf16[24,2048]{1,0:T(8,128)(2,1)S(1)} %get-tuple-element.40), channel_id=1, source_target_pairs={{0,8},{4,12},{8,0},{12,4},{16,24},{20,28},{24,16},{28,20},{1,9},{5... | collective-permute-start | bytes 294920 | tf_op jit(solution)/shard_map/ppermute | solution.py:24
  10.1 8.3 %collective-permute-start.2 = (bf16[24,2048]{1,0:T(8,128)(2,1)S(1)}, bf16[24,2048]{1,0:T(8,128)(2,1)S(1)}, u32[]{:S(2)}, u32[]{:S(2)}) collective-permute-start(bf16[24,2048]{1,0:T(8,128)(2,1)S(1)} %get-tuple-element.41), channel_id=1, source_target_pairs={{0,12},{4,8},{8,4},{12,0},{16,28},{20,24},{24,20},{28,16},{1,13},{... | collective-permute-start | bytes 294920 | tf_op jit(solution)/shard_map/ppermute | solution.py:24
  13.1 7.1 %collective-permute-start.16 = (bf16[2,8,2048]{2,1,0:T(8,128)(2,1)S(1)}, bf16[2,8,2048]{2,1,0:T(8,128)(2,1)S(1)}, u32[]{:S(2)}, u32[]{:S(2)}) collective-permute-start(bf16[2,8,2048]{2,1,0:T(8,128)(2,1)S(1)} %get-tuple-element.49), channel_id=1, source_target_pairs={{0,16},{4,20},{8,24},{12,28},{16,0},{20,4},{24,8},{28,12},{1,17},{... | collective-permute-start | bytes 196616 | tf_op jit(solution)/shard_map/ppermute | solution.py:24
  15.9 6.2 %collective-permute-start.17 = (bf16[2,8,2048]{2,1,0:T(8,128)(2,1)S(1)}, bf16[2,8,2048]{2,1,0:T(8,128)(2,1)S(1)}, u32[]{:S(2)}, u32[]{:S(2)}) collective-permute-start(bf16[2,8,2048]{2,1,0:T(8,128)(2,1)S(1)} %get-tuple-element.50), channel_id=1, source_target_pairs={{0,24},{4,28},{8,16},{12,20},{16,8},{20,12},{24,0},{28,4},{1,25},{... | collective-permute-start | bytes 196616 | tf_op jit(solution)/shard_map/ppermute | solution.py:24
  16.3 7.3 %collective-permute-start.4 = (bf16[16,2048]{1,0:T(8,128)(2,1)S(1)}, bf16[16,2048]{1,0:T(8,128)(2,1)S(1)}, u32[]{:S(2)}, u32[]{:S(2)}) collective-permute-start(bf16[16,2048]{1,0:T(8,128)(2,1)S(1)} %collective-permute-done.3.refs_4_.refs_0_), channel_id=1, source_target_pairs={{0,4},{4,0},{8,12},{12,8},{16,20},{20,16},{24,28},{28,24},{1,5},{5... | collective-permute-start | bytes 196616 | tf_op jit(solution)/shard_map/ppermute | solution.py:24
  17.9 5.7 %collective-permute-start.6 = (bf16[16,2048]{1,0:T(8,128)(2,1)S(1)}, bf16[16,2048]{1,0:T(8,128)(2,1)S(1)}, u32[]{:S(2)}, u32[]{:S(2)}) collective-permute-start(bf16[16,2048]{1,0:T(8,128)(2,1)S(1)} %collective-permute-done.5.refs_6_.refs_1_), channel_id=1, source_target_pairs={{0,4},{4,0},{8,12},{12,8},{16,20},{20,16},{24,28},{28,24},{1,5},{5... | collective-permute-start | bytes 196616 | tf_op jit(solution)/shard_map/ppermute | solution.py:24
  18.3 5.2 %copy-start = (bf16[2048,1024]{1,0:T(8,128)(2,1)S(1)}, bf16[2048,1024]{1,0:T(8,128)(2,1)}, u32[]{:S(2)}) copy-start(bf16[2048,1024]{1,0:T(8,128)(2,1)} %refs_9_.1) | copy-start | bytes 12582916
  18.4 9.7 %collective-permute-start.14 = (bf16[4,8,2048]{2,1,0:T(8,128)(2,1)S(1)}, bf16[4,8,2048]{2,1,0:T(8,128)(2,1)S(1)}, u32[]{:S(2)}, u32[]{:S(2)}) collective-permute-start(bf16[4,8,2048]{2,1,0:T(8,128)(2,1)S(1)} %shard_map.154.refs_2_), channel_id=1, source_target_pairs={{0,2},{1,3},{2,0},{3,1},{4,6},{5,7},{6,4},{7,5},{8,10},{9,11},{10,... | collective-permute-start | bytes 393224 | tf_op jit(solution)/shard_map/ppermute | solution.py:24
  20.2 15.5 %collective-permute-start.13 = (bf16[4,8,2048]{2,1,0:T(8,128)(2,1)S(1)}, bf16[4,8,2048]{2,1,0:T(8,128)(2,1)S(1)}, u32[]{:S(2)}, u32[]{:S(2)}) collective-permute-start(bf16[4,8,2048]{2,1,0:T(8,128)(2,1)S(1)} %shard_map.154.refs_2_), channel_id=1, source_target_pairs={{0,1},{1,0},{2,3},{3,2},{4,5},{5,4},{6,7},{7,6},{8,9},{9,8},{10,11... | collective-permute-start | bytes 393224 | tf_op jit(solution)/shard_map/ppermute | solution.py:24
  22.0 4.3 %collective-permute-start.18 = (bf16[2,8,2048]{2,1,0:T(8,128)(2,1)S(1)}, bf16[2,8,2048]{2,1,0:T(8,128)(2,1)S(1)}, u32[]{:S(2)}, u32[]{:S(2)}) collective-permute-start(bf16[2,8,2048]{2,1,0:T(8,128)(2,1)S(1)} %shard_map.156), channel_id=1, source_target_pairs={{0,4},{4,0},{8,12},{12,8},{16,20},{20,16},{24,28},{28,24},{1,5},{5... | collective-permute-start | bytes 196616 | tf_op jit(solution)/shard_map/ppermute | solution.py:24
  25.1 2.8 %collective-permute-start.7 = (bf16[128,384]{1,0:T(8,128)(2,1)S(1)}, bf16[128,384]{1,0:T(8,128)(2,1)S(1)}, u32[]{:S(2)}, u32[]{:S(2)}) collective-permute-start(bf16[128,384]{1,0:T(8,128)(2,1)S(1)} %get-tuple-element.42.own_ref), channel_id=1, source_target_pairs={{0,1},{1,0},{2,3},{3,2},{4,5},{5,4},{6,7},{7,6},{8,9},{9,8},{10,11... | collective-permute-start | bytes 294920 | tf_op jit(solution)/shard_map/ppermute | solution.py:24
  25.2 3.5 %collective-permute-start.11 = (bf16[64,1024]{1,0:T(8,128)(2,1)S(1)}, bf16[64,1024]{1,0:T(8,128)(2,1)S(1)}, u32[]{:S(2)}, u32[]{:S(2)}) collective-permute-start(bf16[64,1024]{1,0:T(8,128)(2,1)S(1)} %get-tuple-element.47), channel_id=1, source_target_pairs={{0,1},{1,0},{2,3},{3,2},{4,5},{5,4},{6,7},{7,6},{8,9},{9,8},{10,11... | collective-permute-start | bytes 393224 | tf_op jit(solution)/shard_map/ppermute | solution.py:24
  26.3 8.7 %collective-permute-start.20 = (bf16[4,8,2048]{2,1,0:T(8,128)(2,1)S(1)}, bf16[4,8,2048]{2,1,0:T(8,128)(2,1)S(1)}, u32[]{:S(2)}, u32[]{:S(2)}) collective-permute-start(bf16[4,8,2048]{2,1,0:T(8,128)(2,1)S(1)} %shard_map.157.refs_6_), channel_id=1, source_target_pairs={{0,2},{1,3},{2,0},{3,1},{4,6},{5,7},{6,4},{7,5},{8,10},{9,11},{10,... | collective-permute-start | bytes 393224 | tf_op jit(solution)/shard_map/ppermute | solution.py:24
  27.9 10.5 %collective-permute-start.19 = (bf16[4,8,2048]{2,1,0:T(8,128)(2,1)S(1)}, bf16[4,8,2048]{2,1,0:T(8,128)(2,1)S(1)}, u32[]{:S(2)}, u32[]{:S(2)}) collective-permute-start(bf16[4,8,2048]{2,1,0:T(8,128)(2,1)S(1)} %shard_map.157.refs_6_), channel_id=1, source_target_pairs={{0,1},{1,0},{2,3},{3,2},{4,5},{5,4},{6,7},{7,6},{8,9},{9,8},{10,11... | collective-permute-start | bytes 393224 | tf_op jit(solution)/shard_map/ppermute | solution.py:24
  28.1 5.3 %collective-permute-start.8 = (bf16[128,384]{1,0:T(8,128)(2,1)S(1)}, bf16[128,384]{1,0:T(8,128)(2,1)S(1)}, u32[]{:S(2)}, u32[]{:S(2)}) collective-permute-start(bf16[128,384]{1,0:T(8,128)(2,1)S(1)} %shard_map.152.own_ref), channel_id=1, source_target_pairs={{0,2},{1,3},{2,0},{3,1},{4,6},{5,7},{6,4},{7,5},{8,10},{9,11},{10,... | collective-permute-start | bytes 294920 | tf_op jit(solution)/shard_map/ppermute | solution.py:24
  28.7 9.7 %collective-permute-start.15 = (bf16[4,8,2048]{2,1,0:T(8,128)(2,1)S(1)}, bf16[4,8,2048]{2,1,0:T(8,128)(2,1)S(1)}, u32[]{:S(2)}, u32[]{:S(2)}) collective-permute-start(bf16[4,8,2048]{2,1,0:T(8,128)(2,1)S(1)} %collective-permute-done.14.refs_4_), channel_id=1, source_target_pairs={{0,1},{1,0},{2,3},{3,2},{4,5},{5,4},{6,7},{7,6},{8,9},{9,8},{10,11... | collective-permute-start | bytes 393224 | tf_op jit(solution)/shard_map/ppermute | solution.py:24
  29.0 9.4 %copy-start.9 = (f32[4,128]{1,0:T(4,128)S(1)}, f32[4,128]{1,0:T(4,128)}, u32[]{:S(2)}) copy-start(f32[4,128]{1,0:T(4,128)} %constant.71.clone.rope_ref) | copy-start | bytes 6148
  33.4 4.3 %collective-permute-start.12 = (bf16[32,1024]{1,0:T(8,128)(2,1)S(1)}, bf16[32,1024]{1,0:T(8,128)(2,1)S(1)}, u32[]{:S(2)}, u32[]{:S(2)}) collective-permute-start(bf16[32,1024]{1,0:T(8,128)(2,1)S(1)} %slice.80), channel_id=1, source_target_pairs={{0,2},{1,3},{2,0},{3,1},{4,6},{5,7},{6,4},{7,5},{8,10},{9,11},{10,... | collective-permute-start | bytes 196616 | tf_op jit(solution)/shard_map/ppermute | solution.py:24
  35.0 3.4 %collective-permute-start.21 = (bf16[4,8,2048]{2,1,0:T(8,128)(2,1)S(1)}, bf16[4,8,2048]{2,1,0:T(8,128)(2,1)S(1)}, u32[]{:S(2)}, u32[]{:S(2)}) collective-permute-start(bf16[4,8,2048]{2,1,0:T(8,128)(2,1)S(1)} %collective-permute-done.20.refs_8_), channel_id=1, source_target_pairs={{0,1},{1,0},{2,3},{3,2},{4,5},{5,4},{6,7},{7,6},{8,9},{9,8},{10,11... | collective-permute-start | bytes 393224 | tf_op jit(solution)/shard_map/ppermute | solution.py:24
  35.7 5.1 %collective-permute-start.10 = (bf16[128,128]{1,0:T(8,128)(2,1)S(1)}, bf16[128,128]{1,0:T(8,128)(2,1)S(1)}, u32[]{:S(2)}, u32[]{:S(2)}) collective-permute-start(bf16[128,128]{1,0:T(8,128)(2,1)S(1)} %get-tuple-element.44), channel_id=1, source_target_pairs={{0,4},{4,12},{8,20},{12,28},{16,0},{20,8},{24,16},{28,24},{1,5},{5... | collective-permute-start | bytes 98312 | tf_op jit(solution)/shard_map/ppermute | solution.py:561
  37.7 3.1 %collective-permute-start.9 = (bf16[128,128]{1,0:T(8,128)(2,1)S(1)}, bf16[128,128]{1,0:T(8,128)(2,1)S(1)}, u32[]{:S(2)}, u32[]{:S(2)}) collective-permute-start(bf16[128,128]{1,0:T(8,128)(2,1)S(1)} %get-tuple-element.43), channel_id=1, source_target_pairs={{0,0},{4,8},{8,16},{12,24},{16,4},{20,12},{24,20},{28,28},{1,1},{5... | collective-permute-start | bytes 98312 | tf_op jit(solution)/shard_map/ppermute | solution.py:561
  40.8 6.7 %copy-start.1 = (bf16[1024,2048]{1,0:T(8,128)(2,1)S(1)}, bf16[1024,2048]{1,0:T(8,128)(2,1)}, u32[]{:S(2)}) copy-start(bf16[1024,2048]{1,0:T(8,128)(2,1)} %refs_4_.2) | copy-start | bytes 12582916
  42.0 4.3 %collective-permute-start.23 = (bf16[32,1024]{1,0:T(8,128)(2,1)S(1)}, bf16[32,1024]{1,0:T(8,128)(2,1)S(1)}, u32[]{:S(2)}, u32[]{:S(2)}) collective-permute-start(bf16[32,1024]{1,0:T(8,128)(2,1)S(1)} %shard_map.159.refs_0_), channel_id=1, source_target_pairs={{0,2},{1,3},{2,0},{3,1},{4,6},{5,7},{6,4},{7,5},{8,10},{9,11},{10,... | collective-permute-start | bytes 196616 | tf_op jit(solution)/shard_map/ppermute | solution.py:24
  43.6 2.8 %collective-permute-start.22 = (bf16[32,1024]{1,0:T(8,128)(2,1)S(1)}, bf16[32,1024]{1,0:T(8,128)(2,1)S(1)}, u32[]{:S(2)}, u32[]{:S(2)}) collective-permute-start(bf16[32,1024]{1,0:T(8,128)(2,1)S(1)} %shard_map.159.refs_0_), channel_id=1, source_target_pairs={{0,1},{1,0},{2,3},{3,2},{4,5},{5,4},{6,7},{7,6},{8,9},{9,8},{10,11... | collective-permute-start | bytes 196616 | tf_op jit(solution)/shard_map/ppermute | solution.py:24
  46.3 1.3 %collective-permute-start.24 = (bf16[32,1024]{1,0:T(8,128)(2,1)S(1)}, bf16[32,1024]{1,0:T(8,128)(2,1)S(1)}, u32[]{:S(2)}, u32[]{:S(2)}) collective-permute-start(bf16[32,1024]{1,0:T(8,128)(2,1)S(1)} %collective-permute-done.23.refs_2_), channel_id=1, source_target_pairs={{0,1},{1,0},{2,3},{3,2},{4,5},{5,4},{6,7},{7,6},{8,9},{9,8},{10,11... | collective-permute-start | bytes 196616 | tf_op jit(solution)/shard_map/ppermute | solution.py:24
  48.9 9.6 %collective-permute-start.27 = (bf16[16,2048]{1,0:T(8,128)(2,1)S(1)}, bf16[16,2048]{1,0:T(8,128)(2,1)S(1)}, u32[]{:S(2)}, u32[]{:S(2)}) collective-permute-start(bf16[16,2048]{1,0:T(8,128)(2,1)S(1)} %get-tuple-element.58), channel_id=1, source_target_pairs={{0,4},{4,0},{8,12},{12,8},{16,20},{20,16},{24,28},{28,24},{1,5},{5... | collective-permute-start | bytes 196616 | tf_op jit(solution)/shard_map/ppermute | solution.py:24
  54.9 6.0 %collective-permute-start.25 = (bf16[16,2048]{1,0:T(8,128)(2,1)S(1)}, bf16[16,2048]{1,0:T(8,128)(2,1)S(1)}, u32[]{:S(2)}, u32[]{:S(2)}) collective-permute-start(bf16[16,2048]{1,0:T(8,128)(2,1)S(1)} %get-tuple-element.57), channel_id=1, source_target_pairs={{0,4},{4,0},{8,12},{12,8},{16,20},{20,16},{24,28},{28,24},{1,5},{5... | collective-permute-start | bytes 196616 | tf_op jit(solution)/shard_map/ppermute | solution.py:24
  55.0 6.0 %collective-permute-start.29 = (bf16[16,2048]{1,0:T(8,128)(2,1)S(1)}, bf16[16,2048]{1,0:T(8,128)(2,1)S(1)}, u32[]{:S(2)}, u32[]{:S(2)}) collective-permute-start(bf16[16,2048]{1,0:T(8,128)(2,1)S(1)} %get-tuple-element.59), channel_id=1, source_target_pairs={{0,4},{4,0},{8,12},{12,8},{16,20},{20,16},{24,28},{28,24},{1,5},{5... | collective-permute-start | bytes 196616 | tf_op jit(solution)/shard_map/ppermute | solution.py:24
  57.0 4.3 %collective-permute-start.30 = (bf16[16,2048]{1,0:T(8,128)(2,1)S(1)}, bf16[16,2048]{1,0:T(8,128)(2,1)S(1)}, u32[]{:S(2)}, u32[]{:S(2)}) collective-permute-start(bf16[16,2048]{1,0:T(8,128)(2,1)S(1)} %get-tuple-element.60), channel_id=1, source_target_pairs={{0,8},{4,12},{8,0},{12,4},{16,24},{20,28},{24,16},{28,20},{1,9},{5... | collective-permute-start | bytes 196616 | tf_op jit(solution)/shard_map/ppermute | solution.py:24
  57.0 5.2 %collective-permute-start.31 = (bf16[16,2048]{1,0:T(8,128)(2,1)S(1)}, bf16[16,2048]{1,0:T(8,128)(2,1)S(1)}, u32[]{:S(2)}, u32[]{:S(2)}) collective-permute-start(bf16[16,2048]{1,0:T(8,128)(2,1)S(1)} %get-tuple-element.61), channel_id=1, source_target_pairs={{0,12},{4,8},{8,4},{12,0},{16,28},{20,24},{24,20},{28,16},{1,13},{... | collective-permute-start | bytes 196616 | tf_op jit(solution)/shard_map/ppermute | solution.py:24
  58.5 6.3 %collective-permute-start.28 = (bf16[16,2048]{1,0:T(8,128)(2,1)S(1)}, bf16[16,2048]{1,0:T(8,128)(2,1)S(1)}, u32[]{:S(2)}, u32[]{:S(2)}) collective-permute-start(bf16[16,2048]{1,0:T(8,128)(2,1)S(1)} %shard_map.162), channel_id=1, source_target_pairs={{0,24},{4,28},{8,16},{12,20},{16,8},{20,12},{24,0},{28,4},{1,25},{... | collective-permute-start | bytes 196616 | tf_op jit(solution)/shard_map/ppermute | solution.py:24
  60.9 19.2 %slice-start = ((s8[7340032]{0:T(1024)(128)(4,1)}), s8[4194304]{0:T(1024)(128)(4,1)S(1)}, s32[]{:S(2)}) async-start(s8[7340032]{0:T(1024)(128)(4,1)} %bitcast.12), calls=%async_computation | async-start | bytes 8388608
  61.0 6.0 %collective-permute-start.26 = (bf16[16,2048]{1,0:T(8,128)(2,1)S(1)}, bf16[16,2048]{1,0:T(8,128)(2,1)S(1)}, u32[]{:S(2)}, u32[]{:S(2)}) collective-permute-start(bf16[16,2048]{1,0:T(8,128)(2,1)S(1)} %shard_map.161), channel_id=1, source_target_pairs={{0,16},{4,20},{8,24},{12,28},{16,0},{20,4},{24,8},{28,12},{1,17},{... | collective-permute-start | bytes 196616 | tf_op jit(solution)/shard_map/ppermute | solution.py:24
  66.9 13.2 %slice-start.1 = ((s8[7340032]{0:T(1024)(128)(4,1)}), s8[3145728]{0:T(1024)(128)(4,1)S(1)}, s32[]{:S(2)}) async-start(s8[7340032]{0:T(1024)(128)(4,1)} %bitcast.12), calls=%async_computation.1 | async-start | bytes 6291456
  66.9 13.2 %copy-start.8 = (f32[2048]{0:T(1024)S(1)}, f32[2048]{0:T(1024)}, u32[]{:S(2)}) copy-start(f32[2048]{0:T(1024)} %param.20) | copy-start | bytes 24580
  66.9 15.1 %slice-start.2 = ((s8[7340032]{0:T(1024)(128)(4,1)}), s8[4194304]{0:T(1024)(128)(4,1)S(1)}, s32[]{:S(2)}) async-start(s8[7340032]{0:T(1024)(128)(4,1)} %bitcast.14), calls=%async_computation.2 | async-start | bytes 8388608
  67.6 7.1 %collective-permute-start.35 = (bf16[16,2048]{1,0:T(8,128)(2,1)S(1)}, bf16[16,2048]{1,0:T(8,128)(2,1)S(1)}, u32[]{:S(2)}, u32[]{:S(2)}) collective-permute-start(bf16[16,2048]{1,0:T(8,128)(2,1)S(1)} %get-tuple-element.63.refs_0_), channel_id=1, source_target_pairs={{0,16},{4,20},{8,24},{12,28},{16,0},{20,4},{24,8},{28,12},{1,17},{... | collective-permute-start | bytes 196616 | tf_op jit(solution)/shard_map/ppermute | solution.py:24
  67.8 7.9 %collective-permute-start.37 = (bf16[16,2048]{1,0:T(8,128)(2,1)S(1)}, bf16[16,2048]{1,0:T(8,128)(2,1)S(1)}, u32[]{:S(2)}, u32[]{:S(2)}) collective-permute-start(bf16[16,2048]{1,0:T(8,128)(2,1)S(1)} %get-tuple-element.63.refs_0_), channel_id=1, source_target_pairs={{0,24},{4,28},{8,16},{12,20},{16,8},{20,12},{24,0},{28,4},{1,25},{... | collective-permute-start | bytes 196616 | tf_op jit(solution)/shard_map/ppermute | solution.py:24
  69.7 7.1 %collective-permute-start.32 = (bf16[16,2048]{1,0:T(8,128)(2,1)S(1)}, bf16[16,2048]{1,0:T(8,128)(2,1)S(1)}, u32[]{:S(2)}, u32[]{:S(2)}) collective-permute-start(bf16[16,2048]{1,0:T(8,128)(2,1)S(1)} %get-tuple-element.63.refs_0_), channel_id=1, source_target_pairs={{0,4},{4,0},{8,12},{12,8},{16,20},{20,16},{24,28},{28,24},{1,5},{5... | collective-permute-start | bytes 196616 | tf_op jit(solution)/shard_map/ppermute | solution.py:24
  71.3 5.6 %collective-permute-start.33 = (bf16[16,2048]{1,0:T(8,128)(2,1)S(1)}, bf16[16,2048]{1,0:T(8,128)(2,1)S(1)}, u32[]{:S(2)}, u32[]{:S(2)}) collective-permute-start(bf16[16,2048]{1,0:T(8,128)(2,1)S(1)} %get-tuple-element.63.refs_0_), channel_id=1, source_target_pairs={{0,8},{4,12},{8,0},{12,4},{16,24},{20,28},{24,16},{28,20},{1,9},{5... | collective-permute-start | bytes 196616 | tf_op jit(solution)/shard_map/ppermute | solution.py:24
  72.5 5.3 %collective-permute-start.34 = (bf16[16,2048]{1,0:T(8,128)(2,1)S(1)}, bf16[16,2048]{1,0:T(8,128)(2,1)S(1)}, u32[]{:S(2)}, u32[]{:S(2)}) collective-permute-start(bf16[16,2048]{1,0:T(8,128)(2,1)S(1)} %get-tuple-element.63.refs_0_), channel_id=1, source_target_pairs={{0,12},{4,8},{8,4},{12,0},{16,28},{20,24},{24,20},{28,16},{1,13},{... | collective-permute-start | bytes 196616 | tf_op jit(solution)/shard_map/ppermute | solution.py:24
  74.8 4.6 %collective-permute-start.36 = (bf16[16,2048]{1,0:T(8,128)(2,1)S(1)}, bf16[16,2048]{1,0:T(8,128)(2,1)S(1)}, u32[]{:S(2)}, u32[]{:S(2)}) collective-permute-start(bf16[16,2048]{1,0:T(8,128)(2,1)S(1)} %collective-permute-done.35.refs_4_), channel_id=1, source_target_pairs={{0,4},{4,0},{8,12},{12,8},{16,20},{20,16},{24,28},{28,24},{1,5},{5... | collective-permute-start | bytes 196616 | tf_op jit(solution)/shard_map/ppermute | solution.py:24
  75.7 4.4 %collective-permute-start.38 = (bf16[16,2048]{1,0:T(8,128)(2,1)S(1)}, bf16[16,2048]{1,0:T(8,128)(2,1)S(1)}, u32[]{:S(2)}, u32[]{:S(2)}) collective-permute-start(bf16[16,2048]{1,0:T(8,128)(2,1)S(1)} %collective-permute-done.37.refs_6_), channel_id=1, source_target_pairs={{0,4},{4,0},{8,12},{12,8},{16,20},{20,16},{24,28},{28,24},{1,5},{5... | collective-permute-start | bytes 196616 | tf_op jit(solution)/shard_map/ppermute | solution.py:24
  80.1 17.8 %slice-start.4 = ((s8[7340032]{0:T(1024)(128)(4,1)}), s8[4194304]{0:T(1024)(128)(4,1)S(1)}, s32[]{:S(2)}) async-start(s8[7340032]{0:T(1024)(128)(4,1)} %bitcast.16), calls=%async_computation.4 | async-start | bytes 8388608
  82.0 1.8 %collective-permute-start.39 = (bf16[64,1920]{1,0:T(8,128)(2,1)S(1)}, bf16[64,1920]{1,0:T(8,128)(2,1)S(1)}, u32[]{:S(2)}, u32[]{:S(2)}) collective-permute-start(bf16[64,1920]{1,0:T(8,128)(2,1)S(1)} %get-tuple-element.65), channel_id=1, source_target_pairs={{0,1},{1,0},{2,3},{3,2},{4,5},{5,4},{6,7},{7,6},{8,9},{9,8},{10,11... | collective-permute-start | bytes 737288 | tf_op jit(solution)/shard_map/ppermute | solution.py:24
  82.1 15.9 %slice-start.5 = ((s8[7340032]{0:T(1024)(128)(4,1)}), s8[3145728]{0:T(1024)(128)(4,1)S(1)}, s32[]{:S(2)}) async-start(s8[7340032]{0:T(1024)(128)(4,1)} %bitcast.16), calls=%async_computation.5 | async-start | bytes 6291456
  83.2 2.2 %collective-permute-start.41 = (bf16[64,1792]{1,0:T(8,128)(2,1)S(1)}, bf16[64,1792]{1,0:T(8,128)(2,1)S(1)}, u32[]{:S(2)}, u32[]{:S(2)}) collective-permute-start(bf16[64,1792]{1,0:T(8,128)(2,1)S(1)} %get-tuple-element.68), channel_id=1, source_target_pairs={{0,1},{1,0},{2,3},{3,2},{4,5},{5,4},{6,7},{7,6},{8,9},{9,8},{10,11... | collective-permute-start | bytes 688136 | tf_op jit(solution)/shard_map/ppermute | solution.py:24
  83.8 6.2 %collective-permute-start.40 = (bf16[32,1920]{1,0:T(8,128)(2,1)S(1)}, bf16[32,1920]{1,0:T(8,128)(2,1)S(1)}, u32[]{:S(2)}, u32[]{:S(2)}) collective-permute-start(bf16[32,1920]{1,0:T(8,128)(2,1)S(1)} %slice.78), channel_id=1, source_target_pairs={{0,2},{1,3},{2,0},{3,1},{4,6},{5,7},{6,4},{7,5},{8,10},{9,11},{10,... | collective-permute-start | bytes 368648 | tf_op jit(solution)/shard_map/ppermute | solution.py:24
  85.5 6.1 %collective-permute-start.42 = (bf16[32,1792]{1,0:T(8,128)(2,1)S(1)}, bf16[32,1792]{1,0:T(8,128)(2,1)S(1)}, u32[]{:S(2)}, u32[]{:S(2)}) collective-permute-start(bf16[32,1792]{1,0:T(8,128)(2,1)S(1)} %slice.79), channel_id=1, source_target_pairs={{0,2},{1,3},{2,0},{3,1},{4,6},{5,7},{6,4},{7,5},{8,10},{9,11},{10,... | collective-permute-start | bytes 344072 | tf_op jit(solution)/shard_map/ppermute | solution.py:24
  91.8 4.9 %collective-permute-start.44 = (bf16[32,1792]{1,0:T(8,128)(2,1)S(1)}, bf16[32,1792]{1,0:T(8,128)(2,1)S(1)}, u32[]{:S(2)}, u32[]{:S(2)}) collective-permute-start(bf16[32,1792]{1,0:T(8,128)(2,1)S(1)} %fusion.2.refs_0_), channel_id=1, source_target_pairs={{0,2},{1,3},{2,0},{3,1},{4,6},{5,7},{6,4},{7,5},{8,10},{9,11},{10,... | collective-permute-start | bytes 344072 | tf_op jit(solution)/shard_map/ppermute | solution.py:24
  93.4 3.3 %collective-permute-start.43 = (bf16[32,1792]{1,0:T(8,128)(2,1)S(1)}, bf16[32,1792]{1,0:T(8,128)(2,1)S(1)}, u32[]{:S(2)}, u32[]{:S(2)}) collective-permute-start(bf16[32,1792]{1,0:T(8,128)(2,1)S(1)} %fusion.2.refs_0_), channel_id=1, source_target_pairs={{0,1},{1,0},{2,3},{3,2},{4,5},{5,4},{6,7},{7,6},{8,9},{9,8},{10,11... | collective-permute-start | bytes 344072 | tf_op jit(solution)/shard_map/ppermute | solution.py:24
  96.6 1.3 %collective-permute-start.45 = (bf16[32,1792]{1,0:T(8,128)(2,1)S(1)}, bf16[32,1792]{1,0:T(8,128)(2,1)S(1)}, u32[]{:S(2)}, u32[]{:S(2)}) collective-permute-start(bf16[32,1792]{1,0:T(8,128)(2,1)S(1)} %collective-permute-done.44.refs_2_), channel_id=1, source_target_pairs={{0,1},{1,0},{2,3},{3,2},{4,5},{5,4},{6,7},{7,6},{8,9},{9,8},{10,11... | collective-permute-start | bytes 344072 | tf_op jit(solution)/shard_map/ppermute | solution.py:24
  99.7 5.6 %collective-permute-start.48 = (bf16[16,2048]{1,0:T(8,128)(2,1)S(1)}, bf16[16,2048]{1,0:T(8,128)(2,1)S(1)}, u32[]{:S(2)}, u32[]{:S(2)}) collective-permute-start(bf16[16,2048]{1,0:T(8,128)(2,1)S(1)} %get-tuple-element.72), channel_id=1, source_target_pairs={{0,4},{4,0},{8,12},{12,8},{16,20},{20,16},{24,28},{28,24},{1,5},{5... | collective-permute-start | bytes 196616 | tf_op jit(solution)/shard_map/ppermute | solution.py:24
  100.7 6.4 %collective-permute-start.46 = (bf16[16,2048]{1,0:T(8,128)(2,1)S(1)}, bf16[16,2048]{1,0:T(8,128)(2,1)S(1)}, u32[]{:S(2)}, u32[]{:S(2)}) collective-permute-start(bf16[16,2048]{1,0:T(8,128)(2,1)S(1)} %get-tuple-element.71), channel_id=1, source_target_pairs={{0,4},{4,0},{8,12},{12,8},{16,20},{20,16},{24,28},{28,24},{1,5},{5... | collective-permute-start | bytes 196616 | tf_op jit(solution)/shard_map/ppermute | solution.py:24
  101.8 5.8 %collective-permute-start.50 = (bf16[16,2048]{1,0:T(8,128)(2,1)S(1)}, bf16[16,2048]{1,0:T(8,128)(2,1)S(1)}, u32[]{:S(2)}, u32[]{:S(2)}) collective-permute-start(bf16[16,2048]{1,0:T(8,128)(2,1)S(1)} %get-tuple-element.73), channel_id=1, source_target_pairs={{0,4},{4,0},{8,12},{12,8},{16,20},{20,16},{24,28},{28,24},{1,5},{5... | collective-permute-start | bytes 196616 | tf_op jit(solution)/shard_map/ppermute | solution.py:24
  102.7 4.8 %collective-permute-start.51 = (bf16[16,2048]{1,0:T(8,128)(2,1)S(1)}, bf16[16,2048]{1,0:T(8,128)(2,1)S(1)}, u32[]{:S(2)}, u32[]{:S(2)}) collective-permute-start(bf16[16,2048]{1,0:T(8,128)(2,1)S(1)} %get-tuple-element.74), channel_id=1, source_target_pairs={{0,8},{4,12},{8,0},{12,4},{16,24},{20,28},{24,16},{28,20},{1,9},{5... | collective-permute-start | bytes 196616 | tf_op jit(solution)/shard_map/ppermute | solution.py:24
  103.0 5.2 %collective-permute-start.52 = (bf16[16,2048]{1,0:T(8,128)(2,1)S(1)}, bf16[16,2048]{1,0:T(8,128)(2,1)S(1)}, u32[]{:S(2)}, u32[]{:S(2)}) collective-permute-start(bf16[16,2048]{1,0:T(8,128)(2,1)S(1)} %get-tuple-element.75), channel_id=1, source_target_pairs={{0,12},{4,8},{8,4},{12,0},{16,28},{20,24},{24,20},{28,16},{1,13},{... | collective-permute-start | bytes 196616 | tf_op jit(solution)/shard_map/ppermute | solution.py:24
  105.3 6.1 %collective-permute-start.49 = (bf16[16,2048]{1,0:T(8,128)(2,1)S(1)}, bf16[16,2048]{1,0:T(8,128)(2,1)S(1)}, u32[]{:S(2)}, u32[]{:S(2)}) collective-permute-start(bf16[16,2048]{1,0:T(8,128)(2,1)S(1)} %shard_map.168), channel_id=1, source_target_pairs={{0,24},{4,28},{8,16},{12,20},{16,8},{20,12},{24,0},{28,4},{1,25},{... | collective-permute-start | bytes 196616 | tf_op jit(solution)/shard_map/ppermute | solution.py:24
  107.1 6.5 %collective-permute-start.47 = (bf16[16,2048]{1,0:T(8,128)(2,1)S(1)}, bf16[16,2048]{1,0:T(8,128)(2,1)S(1)}, u32[]{:S(2)}, u32[]{:S(2)}) collective-permute-start(bf16[16,2048]{1,0:T(8,128)(2,1)S(1)} %shard_map.167), channel_id=1, source_target_pairs={{0,16},{4,20},{8,24},{12,28},{16,0},{20,4},{24,8},{28,12},{1,17},{... | collective-permute-start | bytes 196616 | tf_op jit(solution)/shard_map/ppermute | solution.py:24
  (6 other events, 18.1 us)

commit v11 on v10

--- a/solution.py
+++ b/solution.py
@@ -41,7 +41,7 @@
 HBM = pl.BlockSpec(memory_space=pltpu.HBM)
 
 
-def call(body, outs, ins, specs, scratch=(), flops=0, moved=0, limit=8 << 20):
+def call(body, outs, ins, specs, scratch=(), flops=0, moved=0, limit=8 << 20, around=1):
     return pl.pallas_call(
         body,
         out_shape=outs,
@@ -49,7 +49,7 @@
         out_specs=jax.tree.map(lambda _: VMEM, outs),
         scratch_shapes=scratch,
         compiler_params=pltpu.CompilerParams(vmem_limit_bytes=limit),
-        cost_estimate=pl.CostEstimate(flops=flops + AROUND, bytes_accessed=moved, transcendentals=0),
+        cost_estimate=pl.CostEstimate(flops=flops + around * AROUND, bytes_accessed=moved, transcendentals=0),
     )(*ins)
 
 
@@ -173,15 +173,16 @@
         for k, ref in enumerate(refs[:-1], 1):
             refs[-1][k] = ref[...].astype(F32)[ref.shape[0] - span :].astype(BF16)
 
-    return call(body, shaped((1 + len(near),) + own.shape), (own, *near), [VMEM] * (1 + len(near)))
-
-
-def first_entries(pieces, entry):
-    def body(*refs):
+    return call(body, shaped((1 + len(near),) + own.shape), (own, *near), [VMEM] * (1 + len(near)), around=1)
+
+
+def last_entries(pieces, after):
+    def body(after_ref, *refs):
         for i, ref in enumerate(refs[:-1]):
-            refs[-1][i] = ref[entry]
-
-    return call(body, shaped((len(pieces),) + pieces[0].shape[1:]), pieces, [VMEM] * len(pieces))
+            refs[-1][i] = ref[1]
+
+    ins = (after, *pieces)
+    return call(body, shaped((len(pieces),) + pieces[0].shape[1:]), ins, [ANY] + [VMEM] * len(pieces), around=1)
 
 
 def collect_far(pieces, passed):
@@ -191,7 +192,7 @@
             refs[-1][2 * i + 1] = refs[-2][i]
 
     shape = (2 * len(pieces),) + pieces[0].shape[1:]
-    return call(body, shaped(shape), (*pieces, passed), [VMEM] * (1 + len(pieces)))
+    return call(body, shaped(shape), (*pieces, passed), [VMEM] * (1 + len(pieces)), around=1)
 
 
 def lift(where_ref, gain_ref, block_refs, h_ref, ss_ref, absolute):
@@ -219,40 +220,78 @@
     return jnp.where(lane == 0, high, jnp.where(lane == 1, total - high, base))
 
 
-def project_attention(where, blocks, gain, w_keyval, w_query):
+def stacked(rows, parts):
+    width = rows.shape[1] // parts
+    return jnp.concatenate([rows[:, i * width : (i + 1) * width] for i in range(parts)], axis=0)
+
+
+def unstacked(rows, parts):
+    height = rows.shape[0] // parts
+    return jnp.concatenate([rows[i * height : (i + 1) * height] for i in range(parts)], axis=1)
+
+
+def project_attention(where, blocks, gain, w_keyval, w_query, after):
     pair, features = blocks[0].shape
     rows = len(blocks) * pair
     half = rows // 2
     columns = w_keyval.shape[1]
     wide = w_query.shape[1]
+    base = columns + 128
 
     def body(where_ref, gain_ref, *refs):
         block_refs, refs = refs[: len(blocks)], refs[len(blocks) :]
-        w_kv_ref, w_q_ref, kv_ref, keep_ref, send_ref, h_ref, ss_ref, product = refs
+        w_kv_ref, w_q_ref, after_ref, message_ref, keep_ref, h_ref, ss_ref, product = refs
         places = lift(where_ref, gain_ref, block_refs, h_ref, ss_ref, True)
         h = h_ref[...]
         product[...] = jnp.dot(h, w_kv_ref[...], preferred_element_type=F32)
         for to, place in places:
-            kv_ref[pl.ds(to, pair), :columns] = product[pl.ds(place, pair), :].astype(BF16)
+            message_ref[pl.ds(to, pair), :columns] = product[pl.ds(place, pair), :].astype(BF16)
         squares = ss_ref[...]
         lane = lax.broadcasted_iota(jnp.int32, squares.shape, 1)
-        kv_ref[:, columns:] = split(squares, 0.0, lane).astype(BF16)
-
-        def write(first, tile, product):
-            keep_ref[:, first : first + tile] = product[:half]
-            send_ref[:, first : first + tile] = product[half:].astype(BF16)
-
-        multiply(h, w_q_ref, write)
+        message_ref[:, columns:base] = split(squares, 0.0, lane).astype(BF16)
+        tile = tiles(wide // 2)
+        for first in range(0, wide, tile):
+            queries = jnp.dot(h, w_q_ref[:, first : first + tile], preferred_element_type=F32)
+            keep_ref[:, first : first + tile] = queries[:half]
+            below, lanes = divmod(first, wide // 2)
+            lanes += base
+            message_ref[below * half : (below + 1) * half, lanes : lanes + tile] = queries[half:].astype(BF16)
 
     return call(
         body,
-        (shaped((rows, columns + 128)), shaped((half, wide), F32), shaped((half, wide))),
-        (where, gain[None], *blocks, w_keyval, w_query),
-        [SMEM] + [VMEM] * (3 + len(blocks)),
+        (shaped((rows, base + wide // 2)), shaped((half, wide), F32)),
+        (where, gain[None], *blocks, w_keyval, w_query, after),
+        [SMEM] + [VMEM] * (3 + len(blocks)) + [ANY],
         [pltpu.VMEM((rows, features), BF16), pltpu.VMEM((rows, 128), F32), pltpu.VMEM((rows, columns), F32)],
         flops=2 * rows * (w_keyval.size + w_query.size),
         moved=4 * rows * features + 2 * (w_keyval.size + w_query.size),
     )
+
+
+def add_cores(own, keep, arrived):
+    tensor = lax.axis_size("tensor")
+    rows, total = own.shape
+    half, wide = keep.shape
+    base = total - wide // 2
+    height = 2 * half // tensor
+    joined = tensor == 4
+
+    def body(own_ref, keep_ref, arrived_ref, first_ref, message_ref, *out_refs):
+        summed = own_ref[:, :base].astype(F32) + arrived_ref[:, :base].astype(F32)
+        ends = summed[:, base - 128 :]
+        lane = lax.broadcasted_iota(jnp.int32, ends.shape, 1)
+        message_ref[:, : base - 128] = summed[:, : base - 128].astype(BF16)
+        message_ref[:, base - 128 : base] = split(ends[:, 0:1] + ends[:, 1:2], ends, lane).astype(BF16)
+        queries = keep_ref[...] + unstacked(arrived_ref[:, base:].astype(F32), 2)
+        first_ref[...] = queries[:height]
+        if joined:
+            message_ref[:, base:] = stacked(queries[height:], 4).astype(BF16)
+        for i, out_ref in enumerate(out_refs, 1):
+            out_ref[...] = queries[i * height : (i + 1) * height].astype(BF16)
+
+    outs = [shaped((height, wide), F32), shaped((rows, base + (wide // 4 if joined else 0)))]
+    outs += [] if joined else [shaped((height, wide))] * (tensor // 2 - 1)
+    return call(body, tuple(outs), (own, keep, arrived), [VMEM] * 3, moved=6 * own.size, around=1)
 
 
 def add_keyvals(own, arrived):
@@ -268,13 +307,13 @@
     return call(body, shaped(own.shape), (own, arrived), [VMEM] * 2, moved=6 * own.size)
 
 
-def finish_keyvals(where, own, arrived, width):
-    groups = lax.axis_size("dp")
-    rows, columns = own.shape
-    columns -= 128
+def finish_keyvals(where, own, arrived, columns, width):
+    groups = lax.axis_size("dp")
+    rows = own.shape[0]
+    lanes = slice(0, columns + 128)
 
     def body(where_ref, own_ref, arrived_ref, scale_ref, *out_refs):
-        summed = own_ref[...].astype(F32) + arrived_ref[...].astype(F32)
+        summed = own_ref[:, lanes].astype(F32) + arrived_ref[:, lanes].astype(F32)
         squares = summed[:, columns : columns + 1] + summed[:, columns + 1 : columns + 2]
         scale = lax.rsqrt(squares / width + EPS)
         scale_ref[...] = jnp.broadcast_to(scale, (rows, 128))
@@ -288,7 +327,7 @@
 
     outs = [shaped((rows, 128), F32)]
     outs += [shaped((rows, HD))] * 2 if groups == KVH else [shaped((rows, columns))]
-    return call(body, tuple(outs), (where, own, arrived), [SMEM, VMEM, VMEM], moved=8 * own.size)
+    return call(body, tuple(outs), (where, own, arrived), [SMEM, VMEM, VMEM], moved=8 * own.size, around=1)
 
 
 def project(h, w):
@@ -391,19 +430,26 @@
     )
 
 
-def add_pairs(keep, arrived, first, pair):
-    def body(keep_ref, arrived_ref, *out_refs):
-        for i, out_ref in enumerate(out_refs):
+def add_pairs(keep, arrived, first, pair, passed=()):
+    count = arrived.shape[0] // pair
+
+    def body(keep_ref, arrived_ref, *refs):
+        for i, out_ref in enumerate(refs[len(passed) : len(passed) + count]):
             own = keep_ref[first + i * pair : first + (i + 1) * pair, :]
             out_ref[...] = (own + arrived_ref[i * pair : (i + 1) * pair, :].astype(F32)).astype(BF16)
-
-    outs = (shaped((pair, keep.shape[1])),) * (arrived.shape[0] // pair)
-    return call(body, outs, (keep, arrived), [VMEM] * 2, moved=8 * arrived.size)
+        for ref, out_ref in zip(refs[: len(passed)], refs[len(passed) + count :]):
+            out_ref[...] = ref[...]
+
+    outs = (shaped((pair, keep.shape[1])),) * (count + len(passed))
+    ins = (keep, arrived, *passed)
+    return call(body, outs, ins, [VMEM] * len(ins), moved=8 * arrived.size)
 
 
 def sum_rows(parts, pair):
     own, *near, keep, one, two = parts
-    sums = add_pairs(keep, swap(one, "dp", 1), 0, pair)
+    count = one.shape[0] // pair
+    sums = add_pairs(keep, swap(one, "dp", 1), 0, pair, near[:2])
+    sums, near = list(sums[:count]), [*sums[count:], *near[2:]]
     sums += add_pairs(keep, swap(two, "dp", 1), one.shape[0], pair)
     arrived = [swap(piece, "dp", len(near) + 1 + 2 * i) for i, piece in enumerate(sums)]
     arrived += [swap(piece, "dp", k + 1) for k, piece in enumerate(near)]
@@ -434,7 +480,7 @@
     pair = 2 * part_dev
     close, span, _ = near_cache[0].shape
     ctx = tensor * span
-    columns = queries[0].shape[1]
+    height, columns = queries[0].shape
     heads = columns // HD
     parts = near * part_dev
     rows = heads * parts
@@ -446,7 +492,11 @@
         d, t = where_ref[0], where_ref[1]
         query_sum = q_refs[0][...]
         for ref in q_refs[1:]:
-            query_sum = query_sum + ref[...].astype(F32)
+            if ref.shape[0] == height:
+                query_sum = query_sum + ref[...].astype(F32)
+            else:
+                lanes = slice(ref.shape[1] - columns // 4, ref.shape[1])
+                query_sum = query_sum + unstacked(ref[:, lanes].astype(F32), 4)
         query_sum = query_sum * scale_ref[pl.ds(pl.multiple_of(t * near * pair, pair), near * pair), 0:1]
         for step in range(2):
 
@@ -598,18 +648,21 @@
     close = min(groups, 4)
     near_moved = blocks[1:close] if joined else [swap(piece, "dp", k) for k, piece in enumerate(near_pieces, 1)]
     near_cache = gather_blocks(collect_near(own_piece, near_moved, span))
-    far_pieces = pack_far(where, cache_keys, cache_values, blocks[close::2])
-    far_pieces = [swap(piece, "dp", close + 2 * i) for i, piece in enumerate(far_pieces)]
-    far_cache = gather_blocks(collect_far(far_pieces, swap(first_entries(far_pieces, 1), "dp", 1)))
-
-    message, *queries = project_attention(where, blocks, attn_gain, w_keyval, w_query)
-    bits = 1
+    packed = pack_far(where, cache_keys, cache_values, blocks[close::2])
+    far_pieces = [swap(piece, "dp", close + 2 * i) for i, piece in enumerate(packed)]
+
+    message, keep = project_attention(where, blocks, attn_gain, w_keyval, w_query, x)
+    queries, message, *leaving = add_cores(message, keep, swap(message, "tensor", 1))
+    passed = swap(last_entries(far_pieces, x), "dp", 1)
+    far_cache = gather_blocks(collect_far(far_pieces, passed))
+    bits = 2
     while 2 * bits < tensor:
         message = add_keyvals(message, swap(message, "tensor", bits))
         bits *= 2
-    scale, *pieces = finish_keyvals(where, message, swap(message, "tensor", bits), width)
+    arrived = swap(message, "tensor", bits)
+    scale, *pieces = finish_keyvals(where, message, arrived, w_keyval.shape[1], width)
     pieces = move_keyvals(pieces)
-    queries, queries_arrived = sum_blocks(*queries)
+    queries = [queries] + ([swap(x, "tensor", 2 * i) for i, x in enumerate(leaving, 1)] if leaving else [arrived])
 
     own = t * parts + jnp.arange(parts, dtype=jnp.int32)
     anc = lax.dynamic_slice_in_dim(ancestors, t * parts, parts).astype(jnp.int32)
@@ -622,8 +675,8 @@
     second = jnp.stack([row_of(anc, 0), row_of(own, 1)], axis=1)
     targets = jnp.concatenate([jnp.tile(first, (heads, 1)), jnp.tile(second, (heads, 1))]).astype(jnp.int32)
     rope = jnp.asarray(np.stack(rope_tables(context) + rope_tables(context + 1)))
-    state = attend_cached(where, anc, rope, scale, [queries] + queries_arrived, near_cache, far_cache, part_dev)
-    mixed = attend_new(where, rope, targets, pieces, state, queries.shape, part_dev)
+    state = attend_cached(where, anc, rope, scale, queries, near_cache, far_cache, part_dev)
+    mixed = attend_new(where, rope, targets, pieces, state, queries[0].shape, part_dev)
 
     parts = project_back(where, gather_blocks(mixed), w_out)
     attn_part, residual = finish(*sum_rows(parts, pair), x)

time: 115 us -> 112 us (0.974)
  waiting for transfers between devices: 37.8 us -> 34.4 us
    ppermute x51 -> x49, waiting for transfers between devices: 37.8 us -> 33 us  [swap(): return lax.ppermute(x, axis, [(i, i ^ bits) for i in range(size)])]
    ppermute x51 -> x49, starting transfers between devices: 56 us -> 58.1 us  [swap(): return lax.ppermute(x, axis, [(i, i ^ bits) for i in range(size)])]
    ppermute x2, waiting for transfers between devices: 0.01 us -> 1.48 us  [move_keyvals(): return [lax.ppermute(x, 'dp', to) for x, to in zip(pieces, (one, two))]]
  transfers between devices with their start and end apart: 53 -> 51, of which waited for: 22 -> 22; matrix products, arithmetic and copies ran while one was open for 1% -> 1% of each run, Pallas kernels for 6% -> 6%
where the time goes in v11:
time: 112 us
  starting transfers between devices  59.3 us (53%)
  waiting for transfers between devices  34.4 us (31%)
  Pallas kernels  14.5 us (13%)
  local copies, waits for them, and re-layouts  1.97 us (2%)
    ppermute x49, starting transfers between devices, swap(): return lax.ppermute(x, axis, [(i, i ^ bits) for i in range(size)])  58.1 us
    ppermute x49, waiting for transfers between devices, swap(): return lax.ppermute(x, axis, [(i, i ^ bits) for i in range(size)])  33 us
    pallas_call x21, Pallas kernels, call(): pl.pallas_call(body, out_shape=outs, in_specs=specs, out_specs=jax.tree.m...  14.5 us
  transfers between devices with their start and end apart: 51, of which 22 were waited for; matrix products, arithmetic and copies ran while one was open for 1% of the time, Pallas kernels for 6%

profile of v11, /device:TPU:0, one launch (start us, length us, event | category | flops | bytes accessed | tf_op | source)
XLA Modules:
  0.0 112.0 jit_solution(316481134509962005)
XLA Ops:
  0.7 0.8 copy-done.5
  1.5 0.8 copy-done.6
  2.2 4.0 %collective-permute-start.3 = (bf16[16,2048]{1,0:T(8,128)(2,1)S(1)}, bf16[16,2048]{1,0:T(8,128)(2,1)S(1)}, u32[]{:S(2)}, u32[]{:S(2)}) collective-permute-start(bf16[16,2048]{1,0:T(8,128)(2,1)S(1)} %shard_map.149.x_ref.refs_0_.refs_10_.after_ref.refs_5_), channel_id=1, source_target_pairs={{0,16},{4,20},{8,24},{12,28},{16,0},{20,4},{24,8},{28,12},{1,17},{... | collective-permute-start | bytes 196616 | tf_op jit(solution)/shard_map/ppermute | solution.py:24
  6.3 1.3 %collective-permute-start.5 = (bf16[16,2048]{1,0:T(8,128)(2,1)S(1)}, bf16[16,2048]{1,0:T(8,128)(2,1)S(1)}, u32[]{:S(2)}, u32[]{:S(2)}) collective-permute-start(bf16[16,2048]{1,0:T(8,128)(2,1)S(1)} %shard_map.149.x_ref.refs_0_.refs_10_.after_ref.refs_5_), channel_id=1, source_target_pairs={{0,24},{4,28},{8,16},{12,20},{16,8},{20,12},{24,0},{28,4},{1,25},{... | collective-permute-start | bytes 196616 | tf_op jit(solution)/shard_map/ppermute | solution.py:24
  7.7 0.6 shard_map.150
  8.3 1.6 %collective-permute-start = (bf16[24,2048]{1,0:T(8,128)(2,1)S(1)}, bf16[24,2048]{1,0:T(8,128)(2,1)S(1)}, u32[]{:S(2)}, u32[]{:S(2)}) collective-permute-start(bf16[24,2048]{1,0:T(8,128)(2,1)S(1)} %get-tuple-element.46), channel_id=1, source_target_pairs={{0,4},{4,0},{8,12},{12,8},{16,20},{20,16},{24,28},{28,24},{1,5},{5... | collective-permute-start | bytes 294920 | tf_op jit(solution)/shard_map/ppermute | solution.py:24
  10.1 1.8 %collective-permute-start.2 = (bf16[24,2048]{1,0:T(8,128)(2,1)S(1)}, bf16[24,2048]{1,0:T(8,128)(2,1)S(1)}, u32[]{:S(2)}, u32[]{:S(2)}) collective-permute-start(bf16[24,2048]{1,0:T(8,128)(2,1)S(1)} %get-tuple-element.48), channel_id=1, source_target_pairs={{0,12},{4,8},{8,4},{12,0},{16,28},{20,24},{24,20},{28,16},{1,13},{... | collective-permute-start | bytes 294920 | tf_op jit(solution)/shard_map/ppermute | solution.py:24
  12.5 0.6 shard_map.155
  13.1 2.8 %collective-permute-start.14 = (bf16[2,8,2048]{2,1,0:T(8,128)(2,1)S(1)}, bf16[2,8,2048]{2,1,0:T(8,128)(2,1)S(1)}, u32[]{:S(2)}, u32[]{:S(2)}) collective-permute-start(bf16[2,8,2048]{2,1,0:T(8,128)(2,1)S(1)} %get-tuple-element.57), channel_id=1, source_target_pairs={{0,16},{4,20},{8,24},{12,28},{16,0},{20,4},{24,8},{28,12},{1,17},{... | collective-permute-start | bytes 196616 | tf_op jit(solution)/shard_map/ppermute | solution.py:24
  16.3 1.6 %collective-permute-start.4 = (bf16[16,2048]{1,0:T(8,128)(2,1)S(1)}, bf16[16,2048]{1,0:T(8,128)(2,1)S(1)}, u32[]{:S(2)}, u32[]{:S(2)}) collective-permute-start(bf16[16,2048]{1,0:T(8,128)(2,1)S(1)} %collective-permute-done.3.refs_4_.refs_0_), channel_id=1, source_target_pairs={{0,4},{4,0},{8,12},{12,8},{16,20},{20,16},{24,28},{28,24},{1,5},{5... | collective-permute-start | bytes 196616 | tf_op jit(solution)/shard_map/ppermute | solution.py:24
  18.4 1.8 %collective-permute-start.12 = (bf16[4,8,2048]{2,1,0:T(8,128)(2,1)S(1)}, bf16[4,8,2048]{2,1,0:T(8,128)(2,1)S(1)}, u32[]{:S(2)}, u32[]{:S(2)}) collective-permute-start(bf16[4,8,2048]{2,1,0:T(8,128)(2,1)S(1)} %shard_map.154.refs_2_), channel_id=1, source_target_pairs={{0,2},{1,3},{2,0},{3,1},{4,6},{5,7},{6,4},{7,5},{8,10},{9,11},{10,... | collective-permute-start | bytes 393224 | tf_op jit(solution)/shard_map/ppermute | solution.py:24
  20.2 1.8 %collective-permute-done.15.refs_1_ = bf16[2,8,2048]{2,1,0:T(8,128)(2,1)S(1)} collective-permute-done((bf16[2,8,2048]{2,1,0:T(8,128)(2,1)S(1)}, bf16[2,8,2048]{2,1,0:T(8,128)(2,1)S(1)}, u32[]{:S(2)}, u32[]{:S(2)}) %collective-permute-start.15) | collective-permute-done | bytes 65568 | tf_op jit(solution)/shard_map/ppermute | solution.py:24
  22.0 1.5 %collective-permute-start.16 = (bf16[2,8,2048]{2,1,0:T(8,128)(2,1)S(1)}, bf16[2,8,2048]{2,1,0:T(8,128)(2,1)S(1)}, u32[]{:S(2)}, u32[]{:S(2)}) collective-permute-start(bf16[2,8,2048]{2,1,0:T(8,128)(2,1)S(1)} %shard_map.156), channel_id=1, source_target_pairs={{0,4},{4,0},{8,12},{12,8},{16,20},{20,16},{24,28},{28,24},{1,5},{5... | collective-permute-start | bytes 196616 | tf_op jit(solution)/shard_map/ppermute | solution.py:24
  23.6 1.5 %shard_map.151 = (bf16[128,896]{1,0:T(8,128)(2,1)S(1)}, f32[64,1024]{1,0:T(8,128)S(1)}) custom-call(s32[2]{0:T(128)S(1)} %pad_add_fusion.3.where_ref, f32[1,2048]{1,0:T(1,128)S(1)} %bitcast.18, bf16[16,2048]{1,0:T(8,128)(2,1)S(1)} %shard_map.149.x_ref.refs_0_.refs_10_.after_ref.refs_5_, bf16[24,2048]{1,0:T(8,128)(2,1)S(1)} %collective-permute-done.refs_1_.refs_0_, ...), custom_call_target="tpu_custom_call" | custom-call | flops 6039797760 | bytes 6291456 | tf_op jit(solution)/shard_map/pallas_call | solution.py:45
  25.2 1.1 collective-permute-done.16.refs_2_
  26.3 1.6 %collective-permute-start.18 = (bf16[4,8,2048]{2,1,0:T(8,128)(2,1)S(1)}, bf16[4,8,2048]{2,1,0:T(8,128)(2,1)S(1)}, u32[]{:S(2)}, u32[]{:S(2)}) collective-permute-start(bf16[4,8,2048]{2,1,0:T(8,128)(2,1)S(1)} %shard_map.157.refs_6_), channel_id=1, source_target_pairs={{0,2},{1,3},{2,0},{3,1},{4,6},{5,7},{6,4},{7,5},{8,10},{9,11},{10,... | collective-permute-start | bytes 393224 | tf_op jit(solution)/shard_map/ppermute | solution.py:24
  29.7 3.1 %collective-permute-done.18.refs_8_ = bf16[4,8,2048]{2,1,0:T(8,128)(2,1)S(1)} collective-permute-done((bf16[4,8,2048]{2,1,0:T(8,128)(2,1)S(1)}, bf16[4,8,2048]{2,1,0:T(8,128)(2,1)S(1)}, u32[]{:S(2)}, u32[]{:S(2)}) %collective-permute-start.18) | collective-permute-done | bytes 131104 | tf_op jit(solution)/shard_map/ppermute | solution.py:24
  32.7 2.0 %collective-permute-done.8.arrived_ref.refs_1_ = bf16[128,640]{1,0:T(8,128)(2,1)S(1)} collective-permute-done((bf16[128,640]{1,0:T(8,128)(2,1)S(1)}, bf16[128,640]{1,0:T(8,128)(2,1)S(1)}, u32[]{:S(2)}, u32[]{:S(2)}) %collective-permute-start.8) | collective-permute-done | bytes 163872 | tf_op jit(solution)/shard_map/ppermute | solution.py:24
  34.8 0.7 shard_map.153
  36.1 0.7 collective-permute-start.9
  36.8 2.4 %shard_map.158 = (bf16[256,128]{1,0:T(8,128)(2,1)S(1)}, f32[256,128]{1,0:T(8,128)S(1)}, f32[256,128]{1,0:T(8,128)S(1)}, f32[256,128]{1,0:T(8,128)S(1)}) custom-call(s32[2]{0:T(128)S(1)} %pad_add_fusion.3.where_ref, s32[16]{0:T(128)S(1)} %get-tuple-element.91.anc_ref, f32[4,128]{1,0:T(4,128)S(1)} %copy-done.9, f32[128,128]{1,0:T(8,128)S(1)} %get-tuple-element.54.scale_ref, ...), custom_call_target="tpu_custom_call" | custom-call | flops 5368709120 | bytes 4194304 | tf_op jit(solution)/shard_map/pallas_call | solution.py:45
  39.1 1.5 %collective-permute-done.10.two_ref = bf16[128,128]{1,0:T(8,128)(2,1)S(1)} collective-permute-done((bf16[128,128]{1,0:T(8,128)(2,1)S(1)}, bf16[128,128]{1,0:T(8,128)(2,1)S(1)}, u32[]{:S(2)}, u32[]{:S(2)}) %collective-permute-start.10) | collective-permute-done | bytes 32800 | tf_op jit(solution)/shard_map/ppermute | solution.py:611
  40.6 1.1 %shard_map.159.refs_0_ = bf16[32,1024]{1,0:T(8,128)(2,1)S(1)} custom-call(s32[2]{0:T(128)S(1)} %pad_add_fusion.3.where_ref, f32[4,128]{1,0:T(4,128)S(1)} %copy-done.9, s32[256,2]{1,0:T(8,128)S(1)} %copy.20.target_ref, bf16[128,128]{1,0:T(8,128)(2,1)S(1)} %collective-permute-done.9.one_ref, bf16[128,128]{1,0:T(8,128)(2,1)S(1)} %collective-permute-done.10.two_ref, ...), custom_call_target="tpu_custom_call" | custom-call | flops 5368709120 | bytes 1048576 | tf_op jit(solution)/shard_map/pallas_call | solution.py:45
  41.8 1.5 %collective-permute-start.21 = (bf16[32,1024]{1,0:T(8,128)(2,1)S(1)}, bf16[32,1024]{1,0:T(8,128)(2,1)S(1)}, u32[]{:S(2)}, u32[]{:S(2)}) collective-permute-start(bf16[32,1024]{1,0:T(8,128)(2,1)S(1)} %shard_map.159.refs_0_), channel_id=1, source_target_pairs={{0,2},{1,3},{2,0},{3,1},{4,6},{5,7},{6,4},{7,5},{8,10},{9,11},{10,... | collective-permute-start | bytes 196616 | tf_op jit(solution)/shard_map/ppermute | solution.py:24
  43.3 2.8 %collective-permute-done.21.refs_2_ = bf16[32,1024]{1,0:T(8,128)(2,1)S(1)} collective-permute-done((bf16[32,1024]{1,0:T(8,128)(2,1)S(1)}, bf16[32,1024]{1,0:T(8,128)(2,1)S(1)}, u32[]{:S(2)}, u32[]{:S(2)}) %collective-permute-start.21) | collective-permute-done | bytes 65568 | tf_op jit(solution)/shard_map/ppermute | solution.py:24
  46.1 1.2 %collective-permute-done.22.refs_3_ = bf16[32,1024]{1,0:T(8,128)(2,1)S(1)} collective-permute-done((bf16[32,1024]{1,0:T(8,128)(2,1)S(1)}, bf16[32,1024]{1,0:T(8,128)(2,1)S(1)}, u32[]{:S(2)}, u32[]{:S(2)}) %collective-permute-start.22) | collective-permute-done | bytes 65568 | tf_op jit(solution)/shard_map/ppermute | solution.py:24
  47.4 1.3 %shard_map.160 = (f32[16,2048]{1,0:T(8,128)S(1)}, bf16[16,2048]{1,0:T(8,128)(2,1)S(1)}, bf16[16,2048]{1,0:T(8,128)(2,1)S(1)}, bf16[16,2048]{1,0:T(8,128)(2,1)S(1...) custom-call(s32[2]{0:T(128)S(1)} %pad_add_fusion.3.where_ref, ...), custom_call_target="tpu_custom_call" | custom-call | flops 5905580032 | bytes 4194304 | tf_op jit(solution)/shard_map/pallas_call | solution.py:45
  48.7 3.7 %collective-permute-start.25 = (bf16[16,2048]{1,0:T(8,128)(2,1)S(1)}, bf16[16,2048]{1,0:T(8,128)(2,1)S(1)}, u32[]{:S(2)}, u32[]{:S(2)}) collective-permute-start(bf16[16,2048]{1,0:T(8,128)(2,1)S(1)} %get-tuple-element.69), channel_id=1, source_target_pairs={{0,4},{4,0},{8,12},{12,8},{16,20},{20,16},{24,28},{28,24},{1,5},{5... | collective-permute-start | bytes 196616 | tf_op jit(solution)/shard_map/ppermute | solution.py:24
  52.4 2.2 %collective-permute-start.29 = (bf16[16,2048]{1,0:T(8,128)(2,1)S(1)}, bf16[16,2048]{1,0:T(8,128)(2,1)S(1)}, u32[]{:S(2)}, u32[]{:S(2)}) collective-permute-start(bf16[16,2048]{1,0:T(8,128)(2,1)S(1)} %get-tuple-element.72), channel_id=1, source_target_pairs={{0,12},{4,8},{8,4},{12,0},{16,28},{20,24},{24,20},{28,16},{1,13},{... | collective-permute-start | bytes 196616 | tf_op jit(solution)/shard_map/ppermute | solution.py:24
  54.8 4.2 %collective-permute-start.26 = (bf16[16,2048]{1,0:T(8,128)(2,1)S(1)}, bf16[16,2048]{1,0:T(8,128)(2,1)S(1)}, u32[]{:S(2)}, u32[]{:S(2)}) collective-permute-start(bf16[16,2048]{1,0:T(8,128)(2,1)S(1)} %shard_map.162), channel_id=1, source_target_pairs={{0,24},{4,28},{8,16},{12,20},{16,8},{20,12},{24,0},{28,4},{1,25},{... | collective-permute-start | bytes 196616 | tf_op jit(solution)/shard_map/ppermute | solution.py:24
  59.0 1.2 %collective-permute-start.27 = (bf16[16,2048]{1,0:T(8,128)(2,1)S(1)}, bf16[16,2048]{1,0:T(8,128)(2,1)S(1)}, u32[]{:S(2)}, u32[]{:S(2)}) collective-permute-start(bf16[16,2048]{1,0:T(8,128)(2,1)S(1)} %get-tuple-element.70), channel_id=1, source_target_pairs={{0,4},{4,0},{8,12},{12,8},{16,20},{20,16},{24,28},{28,24},{1,5},{5... | collective-permute-start | bytes 196616 | tf_op jit(solution)/shard_map/ppermute | solution.py:24
  60.2 2.0 %collective-permute-start.28 = (bf16[16,2048]{1,0:T(8,128)(2,1)S(1)}, bf16[16,2048]{1,0:T(8,128)(2,1)S(1)}, u32[]{:S(2)}, u32[]{:S(2)}) collective-permute-start(bf16[16,2048]{1,0:T(8,128)(2,1)S(1)} %get-tuple-element.71), channel_id=1, source_target_pairs={{0,8},{4,12},{8,0},{12,4},{16,24},{20,28},{24,16},{28,20},{1,9},{5... | collective-permute-start | bytes 196616 | tf_op jit(solution)/shard_map/ppermute | solution.py:24
  62.2 2.2 %collective-permute-done.24.refs_0_ = bf16[16,2048]{1,0:T(8,128)(2,1)S(1)} collective-permute-done((bf16[16,2048]{1,0:T(8,128)(2,1)S(1)}, bf16[16,2048]{1,0:T(8,128)(2,1)S(1)}, u32[]{:S(2)}, u32[]{:S(2)}) %collective-permute-start.24) | collective-permute-done | bytes 65568 | tf_op jit(solution)/shard_map/ppermute | solution.py:24
  64.4 0.6 collective-permute-done.28.refs_3_
  65.0 0.7 shard_map.163
  65.7 1.2 %collective-permute-start.33 = (bf16[16,2048]{1,0:T(8,128)(2,1)S(1)}, bf16[16,2048]{1,0:T(8,128)(2,1)S(1)}, u32[]{:S(2)}, u32[]{:S(2)}) collective-permute-start(bf16[16,2048]{1,0:T(8,128)(2,1)S(1)} %get-tuple-element.74.refs_0_), channel_id=1, source_target_pairs={{0,16},{4,20},{8,24},{12,28},{16,0},{20,4},{24,8},{28,12},{1,17},{... | collective-permute-start | bytes 196616 | tf_op jit(solution)/shard_map/ppermute | solution.py:24
  66.9 2.6 %collective-permute-start.35 = (bf16[16,2048]{1,0:T(8,128)(2,1)S(1)}, bf16[16,2048]{1,0:T(8,128)(2,1)S(1)}, u32[]{:S(2)}, u32[]{:S(2)}) collective-permute-start(bf16[16,2048]{1,0:T(8,128)(2,1)S(1)} %get-tuple-element.74.refs_0_), channel_id=1, source_target_pairs={{0,24},{4,28},{8,16},{12,20},{16,8},{20,12},{24,0},{28,4},{1,25},{... | collective-permute-start | bytes 196616 | tf_op jit(solution)/shard_map/ppermute | solution.py:24
  69.5 0.7 collective-permute-start.30
  70.2 2.8 %collective-permute-start.32 = (bf16[16,2048]{1,0:T(8,128)(2,1)S(1)}, bf16[16,2048]{1,0:T(8,128)(2,1)S(1)}, u32[]{:S(2)}, u32[]{:S(2)}) collective-permute-start(bf16[16,2048]{1,0:T(8,128)(2,1)S(1)} %get-tuple-element.74.refs_0_), channel_id=1, source_target_pairs={{0,12},{4,8},{8,4},{12,0},{16,28},{20,24},{24,20},{28,16},{1,13},{... | collective-permute-start | bytes 196616 | tf_op jit(solution)/shard_map/ppermute | solution.py:24
  73.0 0.7 collective-permute-start.34
  73.7 1.3 %collective-permute-start.36 = (bf16[16,2048]{1,0:T(8,128)(2,1)S(1)}, bf16[16,2048]{1,0:T(8,128)(2,1)S(1)}, u32[]{:S(2)}, u32[]{:S(2)}) collective-permute-start(bf16[16,2048]{1,0:T(8,128)(2,1)S(1)} %collective-permute-done.35.refs_6_), channel_id=1, source_target_pairs={{0,4},{4,0},{8,12},{12,8},{16,20},{20,16},{24,28},{28,24},{1,5},{5... | collective-permute-start | bytes 196616 | tf_op jit(solution)/shard_map/ppermute | solution.py:24
  75.1 0.9 collective-permute-done.32.refs_3_
  76.0 1.3 %collective-permute-done.34.refs_5_ = bf16[16,2048]{1,0:T(8,128)(2,1)S(1)} collective-permute-done((bf16[16,2048]{1,0:T(8,128)(2,1)S(1)}, bf16[16,2048]{1,0:T(8,128)(2,1)S(1)}, u32[]{:S(2)}, u32[]{:S(2)}) %collective-permute-start.34) | collective-permute-done | bytes 65568 | tf_op jit(solution)/shard_map/ppermute | solution.py:24
  77.3 0.7 collective-permute-done.36.refs_7_
  78.0 1.8 %shard_map.164 = (bf16[128,2048]{1,0:T(8,128)(2,1)S(1)}, f32[64,1920]{1,0:T(8,128)S(1)}, bf16[64,1920]{1,0:T(8,128)(2,1)S(1)}) custom-call(s32[2]{0:T(128)S(1)} %pad_add_fusion.3.where_ref, f32[1,2048]{1,0:T(1,128)S(1)} %bitcast.19, bf16[16,2048]{1,0:T(8,128)(2,1)S(1)} %get-tuple-element.74.refs_0_, bf16[16,2048]{1,0:T(8,128)(2,1)S(1)} %collective-permute-done.30.refs_1_, ...), custom_call_target="tpu_custom_call" | custom-call | flops 6308233216 | bytes 8388608 | tf_op jit(solution)/shard_map/pallas_call | solution.py:45
  80.0 1.1 %shard_map.165 = (f32[64,1792]{1,0:T(8,128)S(1)}, bf16[64,1792]{1,0:T(8,128)(2,1)S(1)}) custom-call(bf16[128,2048]{1,0:T(8,128)(2,1)S(1)} %get-tuple-element.77.h_ref, bf16[2048,1792]{1,0:T(8,128)(2,1)S(1)} %bitcast.15), custom_call_target="tpu_custom_call" | custom-call | flops 6308233216 | bytes 7340032 | tf_op jit(solution)/shard_map/pallas_call | solution.py:45
  81.7 1.5 %collective-permute-start.38 = (bf16[32,1920]{1,0:T(8,128)(2,1)S(1)}, bf16[32,1920]{1,0:T(8,128)(2,1)S(1)}, u32[]{:S(2)}, u32[]{:S(2)}) collective-permute-start(bf16[32,1920]{1,0:T(8,128)(2,1)S(1)} %slice.64), channel_id=1, source_target_pairs={{0,2},{1,3},{2,0},{3,1},{4,6},{5,7},{6,4},{7,5},{8,10},{9,11},{10,... | collective-permute-start | bytes 368648 | tf_op jit(solution)/shard_map/ppermute | solution.py:24
  83.3 1.0 collective-permute-start.40
  84.3 3.6 %collective-permute-done.38 = bf16[32,1920]{1,0:T(8,128)(2,1)S(1)} collective-permute-done((bf16[32,1920]{1,0:T(8,128)(2,1)S(1)}, bf16[32,1920]{1,0:T(8,128)(2,1)S(1)}, u32[]{:S(2)}, u32[]{:S(2)}) %collective-permute-start.38) | collective-permute-done | bytes 122912 | tf_op jit(solution)/shard_map/ppermute | solution.py:24
  88.2 1.3 %collective-permute-done.40 = bf16[32,1792]{1,0:T(8,128)(2,1)S(1)} collective-permute-done((bf16[32,1792]{1,0:T(8,128)(2,1)S(1)}, bf16[32,1792]{1,0:T(8,128)(2,1)S(1)}, u32[]{:S(2)}, u32[]{:S(2)}) %collective-permute-start.40) | collective-permute-done | bytes 114720 | tf_op jit(solution)/shard_map/ppermute | solution.py:24
  89.7 1.5 %collective-permute-start.42 = (bf16[32,1792]{1,0:T(8,128)(2,1)S(1)}, bf16[32,1792]{1,0:T(8,128)(2,1)S(1)}, u32[]{:S(2)}, u32[]{:S(2)}) collective-permute-start(bf16[32,1792]{1,0:T(8,128)(2,1)S(1)} %fusion.2.refs_0_), channel_id=1, source_target_pairs={{0,2},{1,3},{2,0},{3,1},{4,6},{5,7},{6,4},{7,5},{8,10},{9,11},{10,... | collective-permute-start | bytes 344072 | tf_op jit(solution)/shard_map/ppermute | solution.py:24
  91.2 3.4 %collective-permute-done.42.refs_2_ = bf16[32,1792]{1,0:T(8,128)(2,1)S(1)} collective-permute-done((bf16[32,1792]{1,0:T(8,128)(2,1)S(1)}, bf16[32,1792]{1,0:T(8,128)(2,1)S(1)}, u32[]{:S(2)}, u32[]{:S(2)}) %collective-permute-start.42) | collective-permute-done | bytes 114720 | tf_op jit(solution)/shard_map/ppermute | solution.py:24
  94.5 1.3 %collective-permute-done.43.refs_3_ = bf16[32,1792]{1,0:T(8,128)(2,1)S(1)} collective-permute-done((bf16[32,1792]{1,0:T(8,128)(2,1)S(1)}, bf16[32,1792]{1,0:T(8,128)(2,1)S(1)}, u32[]{:S(2)}, u32[]{:S(2)}) %collective-permute-start.43) | collective-permute-done | bytes 114720 | tf_op jit(solution)/shard_map/ppermute | solution.py:24
  95.9 1.7 %shard_map.166 = (f32[16,2048]{1,0:T(8,128)S(1)}, bf16[16,2048]{1,0:T(8,128)(2,1)S(1)}, bf16[16,2048]{1,0:T(8,128)(2,1)S(1)}, bf16[16,2048]{1,0:T(8,128)(2,1)S(1...) custom-call(s32[2]{0:T(128)S(1)} %pad_add_fusion.3.where_ref, ...), custom_call_target="tpu_custom_call" | custom-call | flops 6308233216 | bytes 7340032 | tf_op jit(solution)/shard_map/pallas_call | solution.py:45
  97.6 1.4 %collective-permute-start.46 = (bf16[16,2048]{1,0:T(8,128)(2,1)S(1)}, bf16[16,2048]{1,0:T(8,128)(2,1)S(1)}, u32[]{:S(2)}, u32[]{:S(2)}) collective-permute-start(bf16[16,2048]{1,0:T(8,128)(2,1)S(1)} %get-tuple-element.86), channel_id=1, source_target_pairs={{0,4},{4,0},{8,12},{12,8},{16,20},{20,16},{24,28},{28,24},{1,5},{5... | collective-permute-start | bytes 196616 | tf_op jit(solution)/shard_map/ppermute | solution.py:24
  99.0 0.7 collective-permute-start.44
  99.7 0.9 collective-permute-start.50
  100.6 1.8 %collective-permute-done.46.arrived_ref = bf16[16,2048]{1,0:T(8,128)(2,1)S(1)} collective-permute-done((bf16[16,2048]{1,0:T(8,128)(2,1)S(1)}, bf16[16,2048]{1,0:T(8,128)(2,1)S(1)}, u32[]{:S(2)}, u32[]{:S(2)}) %collective-permute-start.46) | collective-permute-done | bytes 65568 | tf_op jit(solution)/shard_map/ppermute | solution.py:24
  102.4 2.7 %collective-permute-start.47 = (bf16[16,2048]{1,0:T(8,128)(2,1)S(1)}, bf16[16,2048]{1,0:T(8,128)(2,1)S(1)}, u32[]{:S(2)}, u32[]{:S(2)}) collective-permute-start(bf16[16,2048]{1,0:T(8,128)(2,1)S(1)} %shard_map.168), channel_id=1, source_target_pairs={{0,24},{4,28},{8,16},{12,20},{16,8},{20,12},{24,0},{28,4},{1,25},{... | collective-permute-start | bytes 196616 | tf_op jit(solution)/shard_map/ppermute | solution.py:24
  105.2 0.8 collective-permute-start.48
  106.0 2.4 %collective-permute-start.49 = (bf16[16,2048]{1,0:T(8,128)(2,1)S(1)}, bf16[16,2048]{1,0:T(8,128)(2,1)S(1)}, u32[]{:S(2)}, u32[]{:S(2)}) collective-permute-start(bf16[16,2048]{1,0:T(8,128)(2,1)S(1)} %get-tuple-element.88), channel_id=1, source_target_pairs={{0,8},{4,12},{8,0},{12,4},{16,24},{20,28},{24,16},{28,20},{1,9},{5... | collective-permute-start | bytes 196616 | tf_op jit(solution)/shard_map/ppermute | solution.py:24
  108.8 1.9 %collective-permute-done.45.refs_0_ = bf16[16,2048]{1,0:T(8,128)(2,1)S(1)} collective-permute-done((bf16[16,2048]{1,0:T(8,128)(2,1)S(1)}, bf16[16,2048]{1,0:T(8,128)(2,1)S(1)}, u32[]{:S(2)}, u32[]{:S(2)}) %collective-permute-start.45) | collective-permute-done | bytes 65568 | tf_op jit(solution)/shard_map/ppermute | solution.py:24
  110.7 0.6 collective-permute-done.49.refs_3_
  111.3 0.7 shard_map.169
  (114 shorter events, 6.3 us)
Async XLA Ops:
  0.6 7.0 %copy-start.3 = (bf16[8,8,1024]{2,1,0:T(8,128)(2,1)S(1)}, bf16[8,8,1024]{2,1,0:T(8,128)(2,1)}, u32[]{:S(2)}) copy-start(bf16[8,8,1024]{2,1,0:T(8,128)(2,1)} %keys_ref.3) | copy-start | bytes 393220
  0.6 7.0 %copy-start.4 = (bf16[8,8,1024]{2,1,0:T(8,128)(2,1)S(1)}, bf16[8,8,1024]{2,1,0:T(8,128)(2,1)}, u32[]{:S(2)}) copy-start(bf16[8,8,1024]{2,1,0:T(8,128)(2,1)} %values_ref.3) | copy-start | bytes 393220
  2.2 9.7 %collective-permute-start.3 = (bf16[16,2048]{1,0:T(8,128)(2,1)S(1)}, bf16[16,2048]{1,0:T(8,128)(2,1)S(1)}, u32[]{:S(2)}, u32[]{:S(2)}) collective-permute-start(bf16[16,2048]{1,0:T(8,128)(2,1)S(1)} %shard_map.149.x_ref.refs_0_.refs_10_.after_ref.refs_5_), channel_id=1, source_target_pairs={{0,16},{4,20},{8,24},{12,28},{16,0},{20,4},{24,8},{28,12},{1,17},{... | collective-permute-start | bytes 196616 | tf_op jit(solution)/shard_map/ppermute | solution.py:24
  6.3 6.2 %collective-permute-start.5 = (bf16[16,2048]{1,0:T(8,128)(2,1)S(1)}, bf16[16,2048]{1,0:T(8,128)(2,1)S(1)}, u32[]{:S(2)}, u32[]{:S(2)}) collective-permute-start(bf16[16,2048]{1,0:T(8,128)(2,1)S(1)} %shard_map.149.x_ref.refs_0_.refs_10_.after_ref.refs_5_), channel_id=1, source_target_pairs={{0,24},{4,28},{8,16},{12,20},{16,8},{20,12},{24,0},{28,4},{1,25},{... | collective-permute-start | bytes 196616 | tf_op jit(solution)/shard_map/ppermute | solution.py:24
  8.3 8.0 %collective-permute-start = (bf16[24,2048]{1,0:T(8,128)(2,1)S(1)}, bf16[24,2048]{1,0:T(8,128)(2,1)S(1)}, u32[]{:S(2)}, u32[]{:S(2)}) collective-permute-start(bf16[24,2048]{1,0:T(8,128)(2,1)S(1)} %get-tuple-element.46), channel_id=1, source_target_pairs={{0,4},{4,0},{8,12},{12,8},{16,20},{20,16},{24,28},{28,24},{1,5},{5... | collective-permute-start | bytes 294920 | tf_op jit(solution)/shard_map/ppermute | solution.py:24
  9.8 8.1 %collective-permute-start.1 = (bf16[24,2048]{1,0:T(8,128)(2,1)S(1)}, bf16[24,2048]{1,0:T(8,128)(2,1)S(1)}, u32[]{:S(2)}, u32[]{:S(2)}) collective-permute-start(bf16[24,2048]{1,0:T(8,128)(2,1)S(1)} %get-tuple-element.47), channel_id=1, source_target_pairs={{0,8},{4,12},{8,0},{12,4},{16,24},{20,28},{24,16},{28,20},{1,9},{5... | collective-permute-start | bytes 294920 | tf_op jit(solution)/shard_map/ppermute | solution.py:24
  10.1 8.3 %collective-permute-start.2 = (bf16[24,2048]{1,0:T(8,128)(2,1)S(1)}, bf16[24,2048]{1,0:T(8,128)(2,1)S(1)}, u32[]{:S(2)}, u32[]{:S(2)}) collective-permute-start(bf16[24,2048]{1,0:T(8,128)(2,1)S(1)} %get-tuple-element.48), channel_id=1, source_target_pairs={{0,12},{4,8},{8,4},{12,0},{16,28},{20,24},{24,20},{28,16},{1,13},{... | collective-permute-start | bytes 294920 | tf_op jit(solution)/shard_map/ppermute | solution.py:24
  13.1 7.1 %collective-permute-start.14 = (bf16[2,8,2048]{2,1,0:T(8,128)(2,1)S(1)}, bf16[2,8,2048]{2,1,0:T(8,128)(2,1)S(1)}, u32[]{:S(2)}, u32[]{:S(2)}) collective-permute-start(bf16[2,8,2048]{2,1,0:T(8,128)(2,1)S(1)} %get-tuple-element.57), channel_id=1, source_target_pairs={{0,16},{4,20},{8,24},{12,28},{16,0},{20,4},{24,8},{28,12},{1,17},{... | collective-permute-start | bytes 196616 | tf_op jit(solution)/shard_map/ppermute | solution.py:24
  15.9 6.2 %collective-permute-start.15 = (bf16[2,8,2048]{2,1,0:T(8,128)(2,1)S(1)}, bf16[2,8,2048]{2,1,0:T(8,128)(2,1)S(1)}, u32[]{:S(2)}, u32[]{:S(2)}) collective-permute-start(bf16[2,8,2048]{2,1,0:T(8,128)(2,1)S(1)} %get-tuple-element.58), channel_id=1, source_target_pairs={{0,24},{4,28},{8,16},{12,20},{16,8},{20,12},{24,0},{28,4},{1,25},{... | collective-permute-start | bytes 196616 | tf_op jit(solution)/shard_map/ppermute | solution.py:24
  16.3 7.3 %collective-permute-start.4 = (bf16[16,2048]{1,0:T(8,128)(2,1)S(1)}, bf16[16,2048]{1,0:T(8,128)(2,1)S(1)}, u32[]{:S(2)}, u32[]{:S(2)}) collective-permute-start(bf16[16,2048]{1,0:T(8,128)(2,1)S(1)} %collective-permute-done.3.refs_4_.refs_0_), channel_id=1, source_target_pairs={{0,4},{4,0},{8,12},{12,8},{16,20},{20,16},{24,28},{28,24},{1,5},{5... | collective-permute-start | bytes 196616 | tf_op jit(solution)/shard_map/ppermute | solution.py:24
  17.9 5.7 %collective-permute-start.6 = (bf16[16,2048]{1,0:T(8,128)(2,1)S(1)}, bf16[16,2048]{1,0:T(8,128)(2,1)S(1)}, u32[]{:S(2)}, u32[]{:S(2)}) collective-permute-start(bf16[16,2048]{1,0:T(8,128)(2,1)S(1)} %collective-permute-done.5.refs_6_.refs_1_), channel_id=1, source_target_pairs={{0,4},{4,0},{8,12},{12,8},{16,20},{20,16},{24,28},{28,24},{1,5},{5... | collective-permute-start | bytes 196616 | tf_op jit(solution)/shard_map/ppermute | solution.py:24
  18.3 5.2 %copy-start = (bf16[2048,1024]{1,0:T(8,128)(2,1)S(1)}, bf16[2048,1024]{1,0:T(8,128)(2,1)}, u32[]{:S(2)}) copy-start(bf16[2048,1024]{1,0:T(8,128)(2,1)} %refs_9_.1) | copy-start | bytes 12582916
  18.4 5.2 %copy-start.2 = (bf16[2048,256]{1,0:T(8,128)(2,1)S(1)}, bf16[2048,256]{1,0:T(8,128)(2,1)}, u32[]{:S(2)}) copy-start(bf16[2048,256]{1,0:T(8,128)(2,1)} %refs_8_.2) | copy-start | bytes 3145732
  18.4 5.2 %copy-start.7 = (f32[2048]{0:T(1024)S(1)}, f32[2048]{0:T(1024)}, u32[]{:S(2)}) copy-start(f32[2048]{0:T(1024)} %param.19) | copy-start | bytes 24580
  18.4 11.2 %collective-permute-start.12 = (bf16[4,8,2048]{2,1,0:T(8,128)(2,1)S(1)}, bf16[4,8,2048]{2,1,0:T(8,128)(2,1)S(1)}, u32[]{:S(2)}, u32[]{:S(2)}) collective-permute-start(bf16[4,8,2048]{2,1,0:T(8,128)(2,1)S(1)} %shard_map.154.refs_2_), channel_id=1, source_target_pairs={{0,2},{1,3},{2,0},{3,1},{4,6},{5,7},{6,4},{7,5},{8,10},{9,11},{10,... | collective-permute-start | bytes 393224 | tf_op jit(solution)/shard_map/ppermute | solution.py:24
  22.0 4.3 %collective-permute-start.16 = (bf16[2,8,2048]{2,1,0:T(8,128)(2,1)S(1)}, bf16[2,8,2048]{2,1,0:T(8,128)(2,1)S(1)}, u32[]{:S(2)}, u32[]{:S(2)}) collective-permute-start(bf16[2,8,2048]{2,1,0:T(8,128)(2,1)S(1)} %shard_map.156), channel_id=1, source_target_pairs={{0,4},{4,0},{8,12},{12,8},{16,20},{20,16},{24,28},{28,24},{1,5},{5... | collective-permute-start | bytes 196616 | tf_op jit(solution)/shard_map/ppermute | solution.py:24
  25.1 2.8 %collective-permute-start.7 = (bf16[128,896]{1,0:T(8,128)(2,1)S(1)}, bf16[128,896]{1,0:T(8,128)(2,1)S(1)}, u32[]{:S(2)}, u32[]{:S(2)}) collective-permute-start(bf16[128,896]{1,0:T(8,128)(2,1)S(1)} %get-tuple-element.49.own_ref), channel_id=1, source_target_pairs={{0,1},{1,0},{2,3},{3,2},{4,5},{5,4},{6,7},{7,6},{8,9},{9,8},{10,11... | collective-permute-start | bytes 688136 | tf_op jit(solution)/shard_map/ppermute | solution.py:24
  26.3 6.4 %collective-permute-start.18 = (bf16[4,8,2048]{2,1,0:T(8,128)(2,1)S(1)}, bf16[4,8,2048]{2,1,0:T(8,128)(2,1)S(1)}, u32[]{:S(2)}, u32[]{:S(2)}) collective-permute-start(bf16[4,8,2048]{2,1,0:T(8,128)(2,1)S(1)} %shard_map.157.refs_6_), channel_id=1, source_target_pairs={{0,2},{1,3},{2,0},{3,1},{4,6},{5,7},{6,4},{7,5},{8,10},{9,11},{10,... | collective-permute-start | bytes 393224 | tf_op jit(solution)/shard_map/ppermute | solution.py:24
  28.1 6.7 %collective-permute-start.8 = (bf16[128,640]{1,0:T(8,128)(2,1)S(1)}, bf16[128,640]{1,0:T(8,128)(2,1)S(1)}, u32[]{:S(2)}, u32[]{:S(2)}) collective-permute-start(bf16[128,640]{1,0:T(8,128)(2,1)S(1)} %get-tuple-element.51.own_ref), channel_id=1, source_target_pairs={{0,2},{1,3},{2,0},{3,1},{4,6},{5,7},{6,4},{7,5},{8,10},{9,11},{10,... | collective-permute-start | bytes 491528 | tf_op jit(solution)/shard_map/ppermute | solution.py:24
  29.0 7.8 %copy-start.9 = (f32[4,128]{1,0:T(4,128)S(1)}, f32[4,128]{1,0:T(4,128)}, u32[]{:S(2)}) copy-start(f32[4,128]{1,0:T(4,128)} %constant.71.clone.rope_ref) | copy-start | bytes 6148
  29.0 7.0 %collective-permute-start.11 = (bf16[4,8,2048]{2,1,0:T(8,128)(2,1)S(1)}, bf16[4,8,2048]{2,1,0:T(8,128)(2,1)S(1)}, u32[]{:S(2)}, u32[]{:S(2)}) collective-permute-start(bf16[4,8,2048]{2,1,0:T(8,128)(2,1)S(1)} %shard_map.154.refs_2_), channel_id=1, source_target_pairs={{0,1},{1,0},{2,3},{3,2},{4,5},{5,4},{6,7},{7,6},{8,9},{9,8},{10,11... | collective-permute-start | bytes 393224 | tf_op jit(solution)/shard_map/ppermute | solution.py:24
  29.1 7.6 %collective-permute-start.17 = (bf16[4,8,2048]{2,1,0:T(8,128)(2,1)S(1)}, bf16[4,8,2048]{2,1,0:T(8,128)(2,1)S(1)}, u32[]{:S(2)}, u32[]{:S(2)}) collective-permute-start(bf16[4,8,2048]{2,1,0:T(8,128)(2,1)S(1)} %shard_map.157.refs_6_), channel_id=1, source_target_pairs={{0,1},{1,0},{2,3},{3,2},{4,5},{5,4},{6,7},{7,6},{8,9},{9,8},{10,11... | collective-permute-start | bytes 393224 | tf_op jit(solution)/shard_map/ppermute | solution.py:24
  29.6 7.1 %collective-permute-start.13 = (bf16[4,8,2048]{2,1,0:T(8,128)(2,1)S(1)}, bf16[4,8,2048]{2,1,0:T(8,128)(2,1)S(1)}, u32[]{:S(2)}, u32[]{:S(2)}) collective-permute-start(bf16[4,8,2048]{2,1,0:T(8,128)(2,1)S(1)} %collective-permute-done.12.refs_4_), channel_id=1, source_target_pairs={{0,1},{1,0},{2,3},{3,2},{4,5},{5,4},{6,7},{7,6},{8,9},{9,8},{10,11... | collective-permute-start | bytes 393224 | tf_op jit(solution)/shard_map/ppermute | solution.py:24
  32.7 4.0 %collective-permute-start.19 = (bf16[4,8,2048]{2,1,0:T(8,128)(2,1)S(1)}, bf16[4,8,2048]{2,1,0:T(8,128)(2,1)S(1)}, u32[]{:S(2)}, u32[]{:S(2)}) collective-permute-start(bf16[4,8,2048]{2,1,0:T(8,128)(2,1)S(1)} %collective-permute-done.18.refs_8_), channel_id=1, source_target_pairs={{0,1},{1,0},{2,3},{3,2},{4,5},{5,4},{6,7},{7,6},{8,9},{9,8},{10,11... | collective-permute-start | bytes 393224 | tf_op jit(solution)/shard_map/ppermute | solution.py:24
  35.5 5.1 %collective-permute-start.10 = (bf16[128,128]{1,0:T(8,128)(2,1)S(1)}, bf16[128,128]{1,0:T(8,128)(2,1)S(1)}, u32[]{:S(2)}, u32[]{:S(2)}) collective-permute-start(bf16[128,128]{1,0:T(8,128)(2,1)S(1)} %get-tuple-element.53), channel_id=1, source_target_pairs={{0,4},{4,12},{8,20},{12,28},{16,0},{20,8},{24,16},{28,24},{1,5},{5... | collective-permute-start | bytes 98312 | tf_op jit(solution)/shard_map/ppermute | solution.py:611
  36.1 4.6 %collective-permute-start.9 = (bf16[128,128]{1,0:T(8,128)(2,1)S(1)}, bf16[128,128]{1,0:T(8,128)(2,1)S(1)}, u32[]{:S(2)}, u32[]{:S(2)}) collective-permute-start(bf16[128,128]{1,0:T(8,128)(2,1)S(1)} %get-tuple-element.52), channel_id=1, source_target_pairs={{0,0},{4,8},{8,16},{12,24},{16,4},{20,12},{24,20},{28,28},{1,1},{5... | collective-permute-start | bytes 98312 | tf_op jit(solution)/shard_map/ppermute | solution.py:611
  40.6 6.7 %copy-start.1 = (bf16[1024,2048]{1,0:T(8,128)(2,1)S(1)}, bf16[1024,2048]{1,0:T(8,128)(2,1)}, u32[]{:S(2)}) copy-start(bf16[1024,2048]{1,0:T(8,128)(2,1)} %refs_4_.2) | copy-start | bytes 12582916
  41.8 4.3 %collective-permute-start.21 = (bf16[32,1024]{1,0:T(8,128)(2,1)S(1)}, bf16[32,1024]{1,0:T(8,128)(2,1)S(1)}, u32[]{:S(2)}, u32[]{:S(2)}) collective-permute-start(bf16[32,1024]{1,0:T(8,128)(2,1)S(1)} %shard_map.159.refs_0_), channel_id=1, source_target_pairs={{0,2},{1,3},{2,0},{3,1},{4,6},{5,7},{6,4},{7,5},{8,10},{9,11},{10,... | collective-permute-start | bytes 196616 | tf_op jit(solution)/shard_map/ppermute | solution.py:24
  43.3 2.8 %collective-permute-start.20 = (bf16[32,1024]{1,0:T(8,128)(2,1)S(1)}, bf16[32,1024]{1,0:T(8,128)(2,1)S(1)}, u32[]{:S(2)}, u32[]{:S(2)}) collective-permute-start(bf16[32,1024]{1,0:T(8,128)(2,1)S(1)} %shard_map.159.refs_0_), channel_id=1, source_target_pairs={{0,1},{1,0},{2,3},{3,2},{4,5},{5,4},{6,7},{7,6},{8,9},{9,8},{10,11... | collective-permute-start | bytes 196616 | tf_op jit(solution)/shard_map/ppermute | solution.py:24
  46.1 1.3 %collective-permute-start.22 = (bf16[32,1024]{1,0:T(8,128)(2,1)S(1)}, bf16[32,1024]{1,0:T(8,128)(2,1)S(1)}, u32[]{:S(2)}, u32[]{:S(2)}) collective-permute-start(bf16[32,1024]{1,0:T(8,128)(2,1)S(1)} %collective-permute-done.21.refs_2_), channel_id=1, source_target_pairs={{0,1},{1,0},{2,3},{3,2},{4,5},{5,4},{6,7},{7,6},{8,9},{9,8},{10,11... | collective-permute-start | bytes 196616 | tf_op jit(solution)/shard_map/ppermute | solution.py:24
  48.7 6.1 %collective-permute-start.25 = (bf16[16,2048]{1,0:T(8,128)(2,1)S(1)}, bf16[16,2048]{1,0:T(8,128)(2,1)S(1)}, u32[]{:S(2)}, u32[]{:S(2)}) collective-permute-start(bf16[16,2048]{1,0:T(8,128)(2,1)S(1)} %get-tuple-element.69), channel_id=1, source_target_pairs={{0,4},{4,0},{8,12},{12,8},{16,20},{20,16},{24,28},{28,24},{1,5},{5... | collective-permute-start | bytes 196616 | tf_op jit(solution)/shard_map/ppermute | solution.py:24
  52.3 6.6 %collective-permute-start.23 = (bf16[16,2048]{1,0:T(8,128)(2,1)S(1)}, bf16[16,2048]{1,0:T(8,128)(2,1)S(1)}, u32[]{:S(2)}, u32[]{:S(2)}) collective-permute-start(bf16[16,2048]{1,0:T(8,128)(2,1)S(1)} %get-tuple-element.65), channel_id=1, source_target_pairs={{0,4},{4,0},{8,12},{12,8},{16,20},{20,16},{24,28},{28,24},{1,5},{5... | collective-permute-start | bytes 196616 | tf_op jit(solution)/shard_map/ppermute | solution.py:24
  52.4 9.8 %collective-permute-start.29 = (bf16[16,2048]{1,0:T(8,128)(2,1)S(1)}, bf16[16,2048]{1,0:T(8,128)(2,1)S(1)}, u32[]{:S(2)}, u32[]{:S(2)}) collective-permute-start(bf16[16,2048]{1,0:T(8,128)(2,1)S(1)} %get-tuple-element.72), channel_id=1, source_target_pairs={{0,12},{4,8},{8,4},{12,0},{16,28},{20,24},{24,20},{28,16},{1,13},{... | collective-permute-start | bytes 196616 | tf_op jit(solution)/shard_map/ppermute | solution.py:24
  54.8 7.5 %collective-permute-start.26 = (bf16[16,2048]{1,0:T(8,128)(2,1)S(1)}, bf16[16,2048]{1,0:T(8,128)(2,1)S(1)}, u32[]{:S(2)}, u32[]{:S(2)}) collective-permute-start(bf16[16,2048]{1,0:T(8,128)(2,1)S(1)} %shard_map.162), channel_id=1, source_target_pairs={{0,24},{4,28},{8,16},{12,20},{16,8},{20,12},{24,0},{28,4},{1,25},{... | collective-permute-start | bytes 196616 | tf_op jit(solution)/shard_map/ppermute | solution.py:24
  58.9 19.1 %slice-start = ((s8[7340032]{0:T(1024)(128)(4,1)}), s8[4194304]{0:T(1024)(128)(4,1)S(1)}, s32[]{:S(2)}) async-start(s8[7340032]{0:T(1024)(128)(4,1)} %bitcast.12), calls=%async_computation | async-start | bytes 8388608
  58.9 5.4 %collective-permute-start.24 = (bf16[16,2048]{1,0:T(8,128)(2,1)S(1)}, bf16[16,2048]{1,0:T(8,128)(2,1)S(1)}, u32[]{:S(2)}, u32[]{:S(2)}) collective-permute-start(bf16[16,2048]{1,0:T(8,128)(2,1)S(1)} %get-tuple-element.68), channel_id=1, source_target_pairs={{0,16},{4,20},{8,24},{12,28},{16,0},{20,4},{24,8},{28,12},{1,17},{... | collective-permute-start | bytes 196616 | tf_op jit(solution)/shard_map/ppermute | solution.py:24
  59.0 5.4 %collective-permute-start.27 = (bf16[16,2048]{1,0:T(8,128)(2,1)S(1)}, bf16[16,2048]{1,0:T(8,128)(2,1)S(1)}, u32[]{:S(2)}, u32[]{:S(2)}) collective-permute-start(bf16[16,2048]{1,0:T(8,128)(2,1)S(1)} %get-tuple-element.70), channel_id=1, source_target_pairs={{0,4},{4,0},{8,12},{12,8},{16,20},{20,16},{24,28},{28,24},{1,5},{5... | collective-permute-start | bytes 196616 | tf_op jit(solution)/shard_map/ppermute | solution.py:24
  60.2 17.8 %slice-start.1 = ((s8[7340032]{0:T(1024)(128)(4,1)}), s8[3145728]{0:T(1024)(128)(4,1)S(1)}, s32[]{:S(2)}) async-start(s8[7340032]{0:T(1024)(128)(4,1)} %bitcast.12), calls=%async_computation.1 | async-start | bytes 6291456
  60.2 4.8 %collective-permute-start.28 = (bf16[16,2048]{1,0:T(8,128)(2,1)S(1)}, bf16[16,2048]{1,0:T(8,128)(2,1)S(1)}, u32[]{:S(2)}, u32[]{:S(2)}) collective-permute-start(bf16[16,2048]{1,0:T(8,128)(2,1)S(1)} %get-tuple-element.71), channel_id=1, source_target_pairs={{0,8},{4,12},{8,0},{12,4},{16,24},{20,28},{24,16},{28,20},{1,9},{5... | collective-permute-start | bytes 196616 | tf_op jit(solution)/shard_map/ppermute | solution.py:24
  65.0 13.0 %copy-start.8 = (f32[2048]{0:T(1024)S(1)}, f32[2048]{0:T(1024)}, u32[]{:S(2)}) copy-start(f32[2048]{0:T(1024)} %param.20) | copy-start | bytes 24580
  65.0 14.9 %slice-start.2 = ((s8[7340032]{0:T(1024)(128)(4,1)}), s8[4194304]{0:T(1024)(128)(4,1)S(1)}, s32[]{:S(2)}) async-start(s8[7340032]{0:T(1024)(128)(4,1)} %bitcast.14), calls=%async_computation.2 | async-start | bytes 8388608
  65.7 7.3 %collective-permute-start.33 = (bf16[16,2048]{1,0:T(8,128)(2,1)S(1)}, bf16[16,2048]{1,0:T(8,128)(2,1)S(1)}, u32[]{:S(2)}, u32[]{:S(2)}) collective-permute-start(bf16[16,2048]{1,0:T(8,128)(2,1)S(1)} %get-tuple-element.74.refs_0_), channel_id=1, source_target_pairs={{0,16},{4,20},{8,24},{12,28},{16,0},{20,4},{24,8},{28,12},{1,17},{... | collective-permute-start | bytes 196616 | tf_op jit(solution)/shard_map/ppermute | solution.py:24
  66.9 6.8 %collective-permute-start.35 = (bf16[16,2048]{1,0:T(8,128)(2,1)S(1)}, bf16[16,2048]{1,0:T(8,128)(2,1)S(1)}, u32[]{:S(2)}, u32[]{:S(2)}) collective-permute-start(bf16[16,2048]{1,0:T(8,128)(2,1)S(1)} %get-tuple-element.74.refs_0_), channel_id=1, source_target_pairs={{0,24},{4,28},{8,16},{12,20},{16,8},{20,12},{24,0},{28,4},{1,25},{... | collective-permute-start | bytes 196616 | tf_op jit(solution)/shard_map/ppermute | solution.py:24
  69.5 5.5 %collective-permute-start.30 = (bf16[16,2048]{1,0:T(8,128)(2,1)S(1)}, bf16[16,2048]{1,0:T(8,128)(2,1)S(1)}, u32[]{:S(2)}, u32[]{:S(2)}) collective-permute-start(bf16[16,2048]{1,0:T(8,128)(2,1)S(1)} %get-tuple-element.74.refs_0_), channel_id=1, source_target_pairs={{0,4},{4,0},{8,12},{12,8},{16,20},{20,16},{24,28},{28,24},{1,5},{5... | collective-permute-start | bytes 196616 | tf_op jit(solution)/shard_map/ppermute | solution.py:24
  70.2 4.8 %collective-permute-start.31 = (bf16[16,2048]{1,0:T(8,128)(2,1)S(1)}, bf16[16,2048]{1,0:T(8,128)(2,1)S(1)}, u32[]{:S(2)}, u32[]{:S(2)}) collective-permute-start(bf16[16,2048]{1,0:T(8,128)(2,1)S(1)} %get-tuple-element.74.refs_0_), channel_id=1, source_target_pairs={{0,8},{4,12},{8,0},{12,4},{16,24},{20,28},{24,16},{28,20},{1,9},{5... | collective-permute-start | bytes 196616 | tf_op jit(solution)/shard_map/ppermute | solution.py:24
  70.2 5.7 %collective-permute-start.32 = (bf16[16,2048]{1,0:T(8,128)(2,1)S(1)}, bf16[16,2048]{1,0:T(8,128)(2,1)S(1)}, u32[]{:S(2)}, u32[]{:S(2)}) collective-permute-start(bf16[16,2048]{1,0:T(8,128)(2,1)S(1)} %get-tuple-element.74.refs_0_), channel_id=1, source_target_pairs={{0,12},{4,8},{8,4},{12,0},{16,28},{20,24},{24,20},{28,16},{1,13},{... | collective-permute-start | bytes 196616 | tf_op jit(solution)/shard_map/ppermute | solution.py:24
  73.0 4.3 %collective-permute-start.34 = (bf16[16,2048]{1,0:T(8,128)(2,1)S(1)}, bf16[16,2048]{1,0:T(8,128)(2,1)S(1)}, u32[]{:S(2)}, u32[]{:S(2)}) collective-permute-start(bf16[16,2048]{1,0:T(8,128)(2,1)S(1)} %collective-permute-done.33.refs_4_), channel_id=1, source_target_pairs={{0,4},{4,0},{8,12},{12,8},{16,20},{20,16},{24,28},{28,24},{1,5},{5... | collective-permute-start | bytes 196616 | tf_op jit(solution)/shard_map/ppermute | solution.py:24
  73.7 4.3 %collective-permute-start.36 = (bf16[16,2048]{1,0:T(8,128)(2,1)S(1)}, bf16[16,2048]{1,0:T(8,128)(2,1)S(1)}, u32[]{:S(2)}, u32[]{:S(2)}) collective-permute-start(bf16[16,2048]{1,0:T(8,128)(2,1)S(1)} %collective-permute-done.35.refs_6_), channel_id=1, source_target_pairs={{0,4},{4,0},{8,12},{12,8},{16,20},{20,16},{24,28},{28,24},{1,5},{5... | collective-permute-start | bytes 196616 | tf_op jit(solution)/shard_map/ppermute | solution.py:24
  78.0 17.8 %slice-start.4 = ((s8[7340032]{0:T(1024)(128)(4,1)}), s8[4194304]{0:T(1024)(128)(4,1)S(1)}, s32[]{:S(2)}) async-start(s8[7340032]{0:T(1024)(128)(4,1)} %bitcast.16), calls=%async_computation.4 | async-start | bytes 8388608
  79.9 1.8 %collective-permute-start.37 = (bf16[64,1920]{1,0:T(8,128)(2,1)S(1)}, bf16[64,1920]{1,0:T(8,128)(2,1)S(1)}, u32[]{:S(2)}, u32[]{:S(2)}) collective-permute-start(bf16[64,1920]{1,0:T(8,128)(2,1)S(1)} %get-tuple-element.76), channel_id=1, source_target_pairs={{0,1},{1,0},{2,3},{3,2},{4,5},{5,4},{6,7},{7,6},{8,9},{9,8},{10,11... | collective-permute-start | bytes 737288 | tf_op jit(solution)/shard_map/ppermute | solution.py:24
  80.0 15.9 %slice-start.5 = ((s8[7340032]{0:T(1024)(128)(4,1)}), s8[3145728]{0:T(1024)(128)(4,1)S(1)}, s32[]{:S(2)}) async-start(s8[7340032]{0:T(1024)(128)(4,1)} %bitcast.16), calls=%async_computation.5 | async-start | bytes 6291456
  81.1 2.1 %collective-permute-start.39 = (bf16[64,1792]{1,0:T(8,128)(2,1)S(1)}, bf16[64,1792]{1,0:T(8,128)(2,1)S(1)}, u32[]{:S(2)}, u32[]{:S(2)}) collective-permute-start(bf16[64,1792]{1,0:T(8,128)(2,1)S(1)} %get-tuple-element.79), channel_id=1, source_target_pairs={{0,1},{1,0},{2,3},{3,2},{4,5},{5,4},{6,7},{7,6},{8,9},{9,8},{10,11... | collective-permute-start | bytes 688136 | tf_op jit(solution)/shard_map/ppermute | solution.py:24
  81.7 6.2 %collective-permute-start.38 = (bf16[32,1920]{1,0:T(8,128)(2,1)S(1)}, bf16[32,1920]{1,0:T(8,128)(2,1)S(1)}, u32[]{:S(2)}, u32[]{:S(2)}) collective-permute-start(bf16[32,1920]{1,0:T(8,128)(2,1)S(1)} %slice.64), channel_id=1, source_target_pairs={{0,2},{1,3},{2,0},{3,1},{4,6},{5,7},{6,4},{7,5},{8,10},{9,11},{10,... | collective-permute-start | bytes 368648 | tf_op jit(solution)/shard_map/ppermute | solution.py:24
  83.3 6.2 %collective-permute-start.40 = (bf16[32,1792]{1,0:T(8,128)(2,1)S(1)}, bf16[32,1792]{1,0:T(8,128)(2,1)S(1)}, u32[]{:S(2)}, u32[]{:S(2)}) collective-permute-start(bf16[32,1792]{1,0:T(8,128)(2,1)S(1)} %slice.65), channel_id=1, source_target_pairs={{0,2},{1,3},{2,0},{3,1},{4,6},{5,7},{6,4},{7,5},{8,10},{9,11},{10,... | collective-permute-start | bytes 344072 | tf_op jit(solution)/shard_map/ppermute | solution.py:24
  89.7 4.9 %collective-permute-start.42 = (bf16[32,1792]{1,0:T(8,128)(2,1)S(1)}, bf16[32,1792]{1,0:T(8,128)(2,1)S(1)}, u32[]{:S(2)}, u32[]{:S(2)}) collective-permute-start(bf16[32,1792]{1,0:T(8,128)(2,1)S(1)} %fusion.2.refs_0_), channel_id=1, source_target_pairs={{0,2},{1,3},{2,0},{3,1},{4,6},{5,7},{6,4},{7,5},{8,10},{9,11},{10,... | collective-permute-start | bytes 344072 | tf_op jit(solution)/shard_map/ppermute | solution.py:24
  91.2 3.4 %collective-permute-start.41 = (bf16[32,1792]{1,0:T(8,128)(2,1)S(1)}, bf16[32,1792]{1,0:T(8,128)(2,1)S(1)}, u32[]{:S(2)}, u32[]{:S(2)}) collective-permute-start(bf16[32,1792]{1,0:T(8,128)(2,1)S(1)} %fusion.2.refs_0_), channel_id=1, source_target_pairs={{0,1},{1,0},{2,3},{3,2},{4,5},{5,4},{6,7},{7,6},{8,9},{9,8},{10,11... | collective-permute-start | bytes 344072 | tf_op jit(solution)/shard_map/ppermute | solution.py:24
  94.5 1.3 %collective-permute-start.43 = (bf16[32,1792]{1,0:T(8,128)(2,1)S(1)}, bf16[32,1792]{1,0:T(8,128)(2,1)S(1)}, u32[]{:S(2)}, u32[]{:S(2)}) collective-permute-start(bf16[32,1792]{1,0:T(8,128)(2,1)S(1)} %collective-permute-done.42.refs_2_), channel_id=1, source_target_pairs={{0,1},{1,0},{2,3},{3,2},{4,5},{5,4},{6,7},{7,6},{8,9},{9,8},{10,11... | collective-permute-start | bytes 344072 | tf_op jit(solution)/shard_map/ppermute | solution.py:24
  97.6 4.8 %collective-permute-start.46 = (bf16[16,2048]{1,0:T(8,128)(2,1)S(1)}, bf16[16,2048]{1,0:T(8,128)(2,1)S(1)}, u32[]{:S(2)}, u32[]{:S(2)}) collective-permute-start(bf16[16,2048]{1,0:T(8,128)(2,1)S(1)} %get-tuple-element.86), channel_id=1, source_target_pairs={{0,4},{4,0},{8,12},{12,8},{16,20},{20,16},{24,28},{28,24},{1,5},{5... | collective-permute-start | bytes 196616 | tf_op jit(solution)/shard_map/ppermute | solution.py:24
  99.0 6.1 %collective-permute-start.44 = (bf16[16,2048]{1,0:T(8,128)(2,1)S(1)}, bf16[16,2048]{1,0:T(8,128)(2,1)S(1)}, u32[]{:S(2)}, u32[]{:S(2)}) collective-permute-start(bf16[16,2048]{1,0:T(8,128)(2,1)S(1)} %get-tuple-element.82), channel_id=1, source_target_pairs={{0,4},{4,0},{8,12},{12,8},{16,20},{20,16},{24,28},{28,24},{1,5},{5... | collective-permute-start | bytes 196616 | tf_op jit(solution)/shard_map/ppermute | solution.py:24
  99.7 8.7 %collective-permute-start.50 = (bf16[16,2048]{1,0:T(8,128)(2,1)S(1)}, bf16[16,2048]{1,0:T(8,128)(2,1)S(1)}, u32[]{:S(2)}, u32[]{:S(2)}) collective-permute-start(bf16[16,2048]{1,0:T(8,128)(2,1)S(1)} %get-tuple-element.89), channel_id=1, source_target_pairs={{0,12},{4,8},{8,4},{12,0},{16,28},{20,24},{24,20},{28,16},{1,13},{... | collective-permute-start | bytes 196616 | tf_op jit(solution)/shard_map/ppermute | solution.py:24
  102.4 6.3 %collective-permute-start.47 = (bf16[16,2048]{1,0:T(8,128)(2,1)S(1)}, bf16[16,2048]{1,0:T(8,128)(2,1)S(1)}, u32[]{:S(2)}, u32[]{:S(2)}) collective-permute-start(bf16[16,2048]{1,0:T(8,128)(2,1)S(1)} %shard_map.168), channel_id=1, source_target_pairs={{0,24},{4,28},{8,16},{12,20},{16,8},{20,12},{24,0},{28,4},{1,25},{... | collective-permute-start | bytes 196616 | tf_op jit(solution)/shard_map/ppermute | solution.py:24
  105.1 5.5 %collective-permute-start.45 = (bf16[16,2048]{1,0:T(8,128)(2,1)S(1)}, bf16[16,2048]{1,0:T(8,128)(2,1)S(1)}, u32[]{:S(2)}, u32[]{:S(2)}) collective-permute-start(bf16[16,2048]{1,0:T(8,128)(2,1)S(1)} %get-tuple-element.85), channel_id=1, source_target_pairs={{0,16},{4,20},{8,24},{12,28},{16,0},{20,4},{24,8},{28,12},{1,17},{... | collective-permute-start | bytes 196616 | tf_op jit(solution)/shard_map/ppermute | solution.py:24
  105.2 5.4 %collective-permute-start.48 = (bf16[16,2048]{1,0:T(8,128)(2,1)S(1)}, bf16[16,2048]{1,0:T(8,128)(2,1)S(1)}, u32[]{:S(2)}, u32[]{:S(2)}) collective-permute-start(bf16[16,2048]{1,0:T(8,128)(2,1)S(1)} %get-tuple-element.87), channel_id=1, source_target_pairs={{0,4},{4,0},{8,12},{12,8},{16,20},{20,16},{24,28},{28,24},{1,5},{5... | collective-permute-start | bytes 196616 | tf_op jit(solution)/shard_map/ppermute | solution.py:24
  106.0 5.3 %collective-permute-start.49 = (bf16[16,2048]{1,0:T(8,128)(2,1)S(1)}, bf16[16,2048]{1,0:T(8,128)(2,1)S(1)}, u32[]{:S(2)}, u32[]{:S(2)}) collective-permute-start(bf16[16,2048]{1,0:T(8,128)(2,1)S(1)} %get-tuple-element.88), channel_id=1, source_target_pairs={{0,8},{4,12},{8,0},{12,4},{16,24},{20,28},{24,16},{28,20},{1,9},{5... | collective-permute-start | bytes 196616 | tf_op jit(solution)/shard_map/ppermute | solution.py:24
  (4 other events, 7.7 us)

commit v12 on v11

--- a/solution.py
+++ b/solution.py
@@ -57,15 +57,26 @@
     return jax.ShapeDtypeStruct(shape, dtype)
 
 
-def gather_rows(rows, near=None):
-    groups = lax.axis_size("dp")
+def far_split(groups):
     close = min(groups, 4)
+    return close, close + (groups - close) // 4 * 2
+
+
+def arrival_order(groups, passing):
+    close, _ = far_split(groups)
+    far = [*range(close, passing, 2), *range(close - 1, 1, -1), *range(groups - 1, passing - 1, -1)]
+    return [0, *far, *range(close + 1, passing, 2), 1]
+
+
+def gather_rows(rows, passing, near=None):
+    groups = lax.axis_size("dp")
+    close, _ = far_split(groups)
     blocks = {0: rows}
-    for k in range(groups - 2, close - 1, -2):
+    for k in [*range(close, passing, 2), *range(passing, groups)]:
         blocks[k] = swap(rows, "dp", k)
     for k in range(close - 1, 0, -1):
         blocks[k] = swap(rows if near is None else near[k - 1], "dp", k)
-    for k in range(groups - 2, close - 1, -2):
+    for k in range(close, passing, 2):
         blocks[k + 1] = swap(blocks[k], "dp", 1)
     return [blocks[k] for k in range(groups)]
 
@@ -195,7 +206,7 @@
     return call(body, shaped(shape), (*pieces, passed), [VMEM] * (1 + len(pieces)), around=1)
 
 
-def lift(where_ref, gain_ref, block_refs, h_ref, ss_ref, absolute):
+def lift(where_ref, gain_ref, order, block_refs, h_ref, ss_ref, absolute):
     groups = len(block_refs)
     tensor = lax.axis_size("tensor")
     pair = block_refs[0].shape[0]
@@ -203,11 +214,11 @@
     d, t = where_ref[0], where_ref[1]
     gain = gain_ref[...]
     places = []
-    for k in range(groups):
+    for ref, k in zip(block_refs, order):
         g = d ^ k
         place = slot(lax.div(g, near) ^ t, tensor) * near + lax.rem(g, near)
         place = pl.multiple_of(place * pair, pair)
-        wide = block_refs[k][...].astype(F32)[:pair]
+        wide = ref[...].astype(F32)[:pair]
         squares = jnp.broadcast_to(jnp.sum(wide * wide, axis=1, keepdims=True), (pair, 128))
         ss_ref[pl.ds(pl.multiple_of(g * pair, pair) if absolute else place, pair), :] = squares
         h_ref[pl.ds(place, pair), :] = (wide * gain).astype(BF16)
@@ -230,7 +241,7 @@
     return jnp.concatenate([rows[i * height : (i + 1) * height] for i in range(parts)], axis=1)
 
 
-def project_attention(where, blocks, gain, w_keyval, w_query, after):
+def project_attention(where, blocks, order, gain, w_keyval, w_query, after):
     pair, features = blocks[0].shape
     rows = len(blocks) * pair
     half = rows // 2
@@ -241,7 +252,7 @@
     def body(where_ref, gain_ref, *refs):
         block_refs, refs = refs[: len(blocks)], refs[len(blocks) :]
         w_kv_ref, w_q_ref, after_ref, message_ref, keep_ref, h_ref, ss_ref, product = refs
-        places = lift(where_ref, gain_ref, block_refs, h_ref, ss_ref, True)
+        places = lift(where_ref, gain_ref, order, block_refs, h_ref, ss_ref, True)
         h = h_ref[...]
         product[...] = jnp.dot(h, w_kv_ref[...], preferred_element_type=F32)
         for to, place in places:
@@ -260,7 +271,7 @@
     return call(
         body,
         (shaped((rows, base + wide // 2)), shaped((half, wide), F32)),
-        (where, gain[None], *blocks, w_keyval, w_query, after),
+        (where, gain[None], *[blocks[k] for k in order], w_keyval, w_query, after),
         [SMEM] + [VMEM] * (3 + len(blocks)) + [ANY],
         [pltpu.VMEM((rows, features), BF16), pltpu.VMEM((rows, 128), F32), pltpu.VMEM((rows, columns), F32)],
         flops=2 * rows * (w_keyval.size + w_query.size),
@@ -351,7 +362,7 @@
     )
 
 
-def project_gate(where, blocks, gain, w):
+def project_gate(where, blocks, order, gain, w):
     pair, features = blocks[0].shape
     rows = len(blocks) * pair
     half = rows // 2
@@ -359,7 +370,7 @@
 
     def body(where_ref, gain_ref, *refs):
         block_refs, (w_ref, h_ref, keep_ref, send_ref, ss_ref) = refs[: len(blocks)], refs[len(blocks) :]
-        lift(where_ref, gain_ref, block_refs, h_ref, ss_ref, False)
+        lift(where_ref, gain_ref, order, block_refs, h_ref, ss_ref, False)
 
         def write(first, tile, product):
             keep_ref[:, first : first + tile] = product[:half]
@@ -376,7 +387,7 @@
     return call(
         body,
         (shaped((rows, features)), shaped((half, columns + 128), F32), shaped((half, columns + 128))),
-        (where, gain[None], *blocks, w),
+        (where, gain[None], *[blocks[k] for k in order], w),
         [SMEM] + [VMEM] * (2 + len(blocks)),
         [pltpu.VMEM((rows, 128), F32)],
         flops=2 * rows * w.size,
@@ -391,8 +402,9 @@
     pair = rows // near
     total = len(blocks) * rows
     columns = w.shape[1]
-    close = min(groups, 4)
-    far = (groups - close) // 2
+    close, passing = far_split(groups)
+    single = groups - (passing - close)
+    joint = (passing - close) // 2
 
     def body(where_ref, *refs):
         block_refs, (w_ref, *out_refs) = refs[: len(blocks)], refs[len(blocks) :]
@@ -401,24 +413,23 @@
         for k, block_ref in enumerate(block_refs):
             for i in range(near):
                 relative = ((t ^ k) * near + i) ^ d
-                beyond = close + lax.shift_right_logical(relative - close, 1) + (relative & 1) * far
-                place = jnp.where(relative < close, relative, beyond)
+                by_x = single + lax.shift_right_logical(relative - close, 1) + (relative & 1) * joint
+                place = jnp.where(relative < passing, by_x, relative - (passing - close))
+                place = jnp.where(relative < close, relative, place)
                 left[pl.ds(pl.multiple_of(place * pair, pair), pair), :] = block_ref[i * pair : (i + 1) * pair, :]
 
         def write(first, tile, product):
             lanes = slice(first, first + tile)
-            for i in range(close):
+            for i in range(single):
                 out_refs[i][:, lanes] = product[i * pair : (i + 1) * pair].astype(out_refs[i].dtype)
-            middle = (close + far) * pair
-            cut = middle + far // 2 * pair
-            out_refs[close][:, lanes] = product[close * pair : middle]
-            out_refs[close + 1][:, lanes] = product[middle:cut].astype(BF16)
-            out_refs[close + 2][:, lanes] = product[cut:].astype(BF16)
+            middle = (single + joint) * pair
+            out_refs[single][:, lanes] = product[single * pair : middle]
+            out_refs[single + 1][:, lanes] = product[middle:].astype(BF16)
 
         multiply(left[...], w_ref, write)
 
-    outs = [shaped((pair, columns), F32)] + [shaped((pair, columns))] * (close - 1)
-    outs += [shaped((far * pair, columns), F32)] + [shaped((far // 2 * pair, columns))] * 2
+    outs = [shaped((pair, columns), F32)] + [shaped((pair, columns))] * (single - 1)
+    outs += [shaped((joint * pair, columns), F32), shaped((joint * pair, columns))]
     return call(
         body,
         tuple(outs),
@@ -430,29 +441,27 @@
     )
 
 
-def add_pairs(keep, arrived, first, pair, passed=()):
+def add_pairs(keep, arrived, pair, passed):
     count = arrived.shape[0] // pair
 
-    def body(keep_ref, arrived_ref, *refs):
-        for i, out_ref in enumerate(refs[len(passed) : len(passed) + count]):
-            own = keep_ref[first + i * pair : first + (i + 1) * pair, :]
-            out_ref[...] = (own + arrived_ref[i * pair : (i + 1) * pair, :].astype(F32)).astype(BF16)
-        for ref, out_ref in zip(refs[: len(passed)], refs[len(passed) + count :]):
-            out_ref[...] = ref[...]
-
-    outs = (shaped((pair, keep.shape[1])),) * (count + len(passed))
-    ins = (keep, arrived, *passed)
-    return call(body, outs, ins, [VMEM] * len(ins), moved=8 * arrived.size)
+    def body(keep_ref, arrived_ref, passed_ref, *out_refs):
+        for i, out_ref in enumerate(out_refs[:-1]):
+            rows = slice(i * pair, (i + 1) * pair)
+            out_ref[...] = (keep_ref[rows, :] + arrived_ref[rows, :].astype(F32)).astype(BF16)
+        out_refs[-1][...] = passed_ref[...]
+
+    outs = (shaped((pair, keep.shape[1])),) * (count + 1)
+    return call(body, outs, (keep, arrived, passed), [VMEM] * 3, moved=8 * arrived.size)
 
 
 def sum_rows(parts, pair):
-    own, *near, keep, one, two = parts
-    count = one.shape[0] // pair
-    sums = add_pairs(keep, swap(one, "dp", 1), 0, pair, near[:2])
-    sums, near = list(sums[:count]), [*sums[count:], *near[2:]]
-    sums += add_pairs(keep, swap(two, "dp", 1), one.shape[0], pair)
-    arrived = [swap(piece, "dp", len(near) + 1 + 2 * i) for i, piece in enumerate(sums)]
-    arrived += [swap(piece, "dp", k + 1) for k, piece in enumerate(near)]
+    groups = lax.axis_size("dp")
+    close, passing = far_split(groups)
+    own, *direct, keep, send = parts
+    *sums, direct[0] = add_pairs(keep, swap(send, "dp", 1), pair, direct[0])
+    arrived = [swap(piece, "dp", close + 2 * i) for i, piece in enumerate(sums)]
+    places = [*range(1, close), *range(passing, groups)]
+    arrived += [swap(piece, "dp", k) for k, piece in sorted(zip(places, direct), key=lambda item: -item[0])]
     return own, arrived
 
 
@@ -644,14 +653,14 @@
 
     x = stack_tokens(x_first, x_second)
     own_piece, near_pieces, joined = pack_near(where, x, cache_keys, cache_values)
-    blocks = gather_rows(x, near_pieces if joined else None)
+    blocks = gather_rows(x, groups, near_pieces if joined else None)
     close = min(groups, 4)
     near_moved = blocks[1:close] if joined else [swap(piece, "dp", k) for k, piece in enumerate(near_pieces, 1)]
     near_cache = gather_blocks(collect_near(own_piece, near_moved, span))
     packed = pack_far(where, cache_keys, cache_values, blocks[close::2])
     far_pieces = [swap(piece, "dp", close + 2 * i) for i, piece in enumerate(packed)]
 
-    message, keep = project_attention(where, blocks, attn_gain, w_keyval, w_query, x)
+    message, keep = project_attention(where, blocks, range(groups), attn_gain, w_keyval, w_query, x)
     queries, message, *leaving = add_cores(message, keep, swap(message, "tensor", 1))
     passed = swap(last_entries(far_pieces, x), "dp", 1)
     far_cache = gather_blocks(collect_far(far_pieces, passed))
@@ -682,7 +691,9 @@
     attn_part, residual = finish(*sum_rows(parts, pair), x)
 
     hidden_cols = w_gate.shape[1]
-    h, keep, send = project_gate(where, gather_rows(residual), ffn_gain, w_gate)
+    passing = far_split(groups)[1]
+    order = arrival_order(groups, passing)
+    h, keep, send = project_gate(where, gather_rows(residual, passing), order, ffn_gain, w_gate)
     gate, gate_arrived = sum_blocks(keep, send)
     up, up_arrived = sum_blocks(*project(h, w_up))
     for piece in gate_arrived:

time: 112 us -> 113 us (level)
  starting transfers between devices: 59.3 us -> 61.4 us
    ppermute x49, starting transfers between devices: 58.1 us -> 60.2 us  [swap(): return lax.ppermute(x, axis, [(i, i ^ bits) for i in range(size)])]
    pallas_call x21 -> x19, Pallas kernels: 14.5 us -> 14.5 us  [call(): pl.pallas_call(body, out_shape=outs, in_specs=specs, out_specs=jax.tree.m...]
  transfers between devices with their start and end apart: 51 -> 51, of which waited for: 22 -> 23; matrix products, arithmetic and copies ran while one was open for 1% -> 1% of each run, Pallas kernels for 6% -> 6%
where the time goes in v12:
time: 113 us
  starting transfers between devices  61.4 us (54%)
  waiting for transfers between devices  33.7 us (30%)
  Pallas kernels  14.5 us (13%)
  local copies, waits for them, and re-layouts  1.97 us (2%)
    ppermute x49, starting transfers between devices, swap(): return lax.ppermute(x, axis, [(i, i ^ bits) for i in range(size)])  60.2 us
    ppermute x49, waiting for transfers between devices, swap(): return lax.ppermute(x, axis, [(i, i ^ bits) for i in range(size)])  32.2 us
    pallas_call x19, Pallas kernels, call(): pl.pallas_call(body, out_shape=outs, in_specs=specs, out_specs=jax.tree.m...  14.5 us
  transfers between devices with their start and end apart: 51, of which 23 were waited for; matrix products, arithmetic and copies ran while one was open for 1% of the time, Pallas kernels for 6%

profile of v12, /device:TPU:0, one launch (start us, length us, event | category | flops | bytes accessed | tf_op | source)
XLA Modules:
  0.0 113.3 jit_solution(13021457078949779448)
XLA Ops:
  0.7 0.8 copy-done.5
  1.5 0.8 copy-done.6
  2.2 4.0 %collective-permute-start.3 = (bf16[16,2048]{1,0:T(8,128)(2,1)S(1)}, bf16[16,2048]{1,0:T(8,128)(2,1)S(1)}, u32[]{:S(2)}, u32[]{:S(2)}) collective-permute-start(bf16[16,2048]{1,0:T(8,128)(2,1)S(1)} %shard_map.149.x_ref.refs_0_.refs_10_.after_ref.refs_6_), channel_id=1, source_target_pairs={{0,16},{4,20},{8,24},{12,28},{16,0},{20,4},{24,8},{28,12},{1,17},{... | collective-permute-start | bytes 196616 | tf_op jit(solution)/shard_map/ppermute | solution.py:24
  6.3 1.3 %collective-permute-start.5 = (bf16[16,2048]{1,0:T(8,128)(2,1)S(1)}, bf16[16,2048]{1,0:T(8,128)(2,1)S(1)}, u32[]{:S(2)}, u32[]{:S(2)}) collective-permute-start(bf16[16,2048]{1,0:T(8,128)(2,1)S(1)} %shard_map.149.x_ref.refs_0_.refs_10_.after_ref.refs_6_), channel_id=1, source_target_pairs={{0,24},{4,28},{8,16},{12,20},{16,8},{20,12},{24,0},{28,4},{1,25},{... | collective-permute-start | bytes 196616 | tf_op jit(solution)/shard_map/ppermute | solution.py:24
  7.7 0.6 shard_map.150
  8.3 1.6 %collective-permute-start = (bf16[24,2048]{1,0:T(8,128)(2,1)S(1)}, bf16[24,2048]{1,0:T(8,128)(2,1)S(1)}, u32[]{:S(2)}, u32[]{:S(2)}) collective-permute-start(bf16[24,2048]{1,0:T(8,128)(2,1)S(1)} %get-tuple-element.46), channel_id=1, source_target_pairs={{0,4},{4,0},{8,12},{12,8},{16,20},{20,16},{24,28},{28,24},{1,5},{5... | collective-permute-start | bytes 294920 | tf_op jit(solution)/shard_map/ppermute | solution.py:24
  10.1 1.8 %collective-permute-start.2 = (bf16[24,2048]{1,0:T(8,128)(2,1)S(1)}, bf16[24,2048]{1,0:T(8,128)(2,1)S(1)}, u32[]{:S(2)}, u32[]{:S(2)}) collective-permute-start(bf16[24,2048]{1,0:T(8,128)(2,1)S(1)} %get-tuple-element.48), channel_id=1, source_target_pairs={{0,12},{4,8},{8,4},{12,0},{16,28},{20,24},{24,20},{28,16},{1,13},{... | collective-permute-start | bytes 294920 | tf_op jit(solution)/shard_map/ppermute | solution.py:24
  12.5 0.6 shard_map.155
  13.1 2.8 %collective-permute-start.14 = (bf16[2,8,2048]{2,1,0:T(8,128)(2,1)S(1)}, bf16[2,8,2048]{2,1,0:T(8,128)(2,1)S(1)}, u32[]{:S(2)}, u32[]{:S(2)}) collective-permute-start(bf16[2,8,2048]{2,1,0:T(8,128)(2,1)S(1)} %get-tuple-element.57), channel_id=1, source_target_pairs={{0,16},{4,20},{8,24},{12,28},{16,0},{20,4},{24,8},{28,12},{1,17},{... | collective-permute-start | bytes 196616 | tf_op jit(solution)/shard_map/ppermute | solution.py:24
  16.3 1.6 %collective-permute-start.4 = (bf16[16,2048]{1,0:T(8,128)(2,1)S(1)}, bf16[16,2048]{1,0:T(8,128)(2,1)S(1)}, u32[]{:S(2)}, u32[]{:S(2)}) collective-permute-start(bf16[16,2048]{1,0:T(8,128)(2,1)S(1)} %collective-permute-done.3.refs_4_.refs_0_), channel_id=1, source_target_pairs={{0,4},{4,0},{8,12},{12,8},{16,20},{20,16},{24,28},{28,24},{1,5},{5... | collective-permute-start | bytes 196616 | tf_op jit(solution)/shard_map/ppermute | solution.py:24
  18.4 1.8 %collective-permute-start.12 = (bf16[4,8,2048]{2,1,0:T(8,128)(2,1)S(1)}, bf16[4,8,2048]{2,1,0:T(8,128)(2,1)S(1)}, u32[]{:S(2)}, u32[]{:S(2)}) collective-permute-start(bf16[4,8,2048]{2,1,0:T(8,128)(2,1)S(1)} %shard_map.154.refs_2_), channel_id=1, source_target_pairs={{0,2},{1,3},{2,0},{3,1},{4,6},{5,7},{6,4},{7,5},{8,10},{9,11},{10,... | collective-permute-start | bytes 393224 | tf_op jit(solution)/shard_map/ppermute | solution.py:24
  20.2 1.8 %collective-permute-done.15.refs_1_ = bf16[2,8,2048]{2,1,0:T(8,128)(2,1)S(1)} collective-permute-done((bf16[2,8,2048]{2,1,0:T(8,128)(2,1)S(1)}, bf16[2,8,2048]{2,1,0:T(8,128)(2,1)S(1)}, u32[]{:S(2)}, u32[]{:S(2)}) %collective-permute-start.15) | collective-permute-done | bytes 65568 | tf_op jit(solution)/shard_map/ppermute | solution.py:24
  22.0 1.5 %collective-permute-start.16 = (bf16[2,8,2048]{2,1,0:T(8,128)(2,1)S(1)}, bf16[2,8,2048]{2,1,0:T(8,128)(2,1)S(1)}, u32[]{:S(2)}, u32[]{:S(2)}) collective-permute-start(bf16[2,8,2048]{2,1,0:T(8,128)(2,1)S(1)} %shard_map.156), channel_id=1, source_target_pairs={{0,4},{4,0},{8,12},{12,8},{16,20},{20,16},{24,28},{28,24},{1,5},{5... | collective-permute-start | bytes 196616 | tf_op jit(solution)/shard_map/ppermute | solution.py:24
  23.6 1.5 %shard_map.151 = (bf16[128,896]{1,0:T(8,128)(2,1)S(1)}, f32[64,1024]{1,0:T(8,128)S(1)}) custom-call(s32[2]{0:T(128)S(1)} %pad_add_fusion.3.where_ref, f32[1,2048]{1,0:T(1,128)S(1)} %bitcast.18, bf16[16,2048]{1,0:T(8,128)(2,1)S(1)} %shard_map.149.x_ref.refs_0_.refs_10_.after_ref.refs_6_, bf16[24,2048]{1,0:T(8,128)(2,1)S(1)} %collective-permute-done.refs_1_.refs_0_, ...), custom_call_target="tpu_custom_call" | custom-call | flops 6039797760 | bytes 6291456 | tf_op jit(solution)/shard_map/pallas_call | solution.py:45
  25.2 1.1 collective-permute-done.16.refs_2_
  26.3 1.6 %collective-permute-start.18 = (bf16[4,8,2048]{2,1,0:T(8,128)(2,1)S(1)}, bf16[4,8,2048]{2,1,0:T(8,128)(2,1)S(1)}, u32[]{:S(2)}, u32[]{:S(2)}) collective-permute-start(bf16[4,8,2048]{2,1,0:T(8,128)(2,1)S(1)} %shard_map.157.refs_6_), channel_id=1, source_target_pairs={{0,2},{1,3},{2,0},{3,1},{4,6},{5,7},{6,4},{7,5},{8,10},{9,11},{10,... | collective-permute-start | bytes 393224 | tf_op jit(solution)/shard_map/ppermute | solution.py:24
  28.1 0.6 collective-permute-start.8
  29.7 3.1 %collective-permute-done.18.refs_8_ = bf16[4,8,2048]{2,1,0:T(8,128)(2,1)S(1)} collective-permute-done((bf16[4,8,2048]{2,1,0:T(8,128)(2,1)S(1)}, bf16[4,8,2048]{2,1,0:T(8,128)(2,1)S(1)}, u32[]{:S(2)}, u32[]{:S(2)}) %collective-permute-start.18) | collective-permute-done | bytes 131104 | tf_op jit(solution)/shard_map/ppermute | solution.py:24
  32.7 2.0 %collective-permute-done.8.arrived_ref.refs_1_ = bf16[128,640]{1,0:T(8,128)(2,1)S(1)} collective-permute-done((bf16[128,640]{1,0:T(8,128)(2,1)S(1)}, bf16[128,640]{1,0:T(8,128)(2,1)S(1)}, u32[]{:S(2)}, u32[]{:S(2)}) %collective-permute-start.8) | collective-permute-done | bytes 163872 | tf_op jit(solution)/shard_map/ppermute | solution.py:24
  34.8 0.7 shard_map.153
  36.1 0.7 collective-permute-start.9
  36.8 2.4 %shard_map.158 = (bf16[256,128]{1,0:T(8,128)(2,1)S(1)}, f32[256,128]{1,0:T(8,128)S(1)}, f32[256,128]{1,0:T(8,128)S(1)}, f32[256,128]{1,0:T(8,128)S(1)}) custom-call(s32[2]{0:T(128)S(1)} %pad_add_fusion.3.where_ref, s32[16]{0:T(128)S(1)} %get-tuple-element.91.anc_ref, f32[4,128]{1,0:T(4,128)S(1)} %copy-done.9, f32[128,128]{1,0:T(8,128)S(1)} %get-tuple-element.54.scale_ref, ...), custom_call_target="tpu_custom_call" | custom-call | flops 5368709120 | bytes 4194304 | tf_op jit(solution)/shard_map/pallas_call | solution.py:45
  39.1 1.5 %collective-permute-done.10.two_ref = bf16[128,128]{1,0:T(8,128)(2,1)S(1)} collective-permute-done((bf16[128,128]{1,0:T(8,128)(2,1)S(1)}, bf16[128,128]{1,0:T(8,128)(2,1)S(1)}, u32[]{:S(2)}, u32[]{:S(2)}) %collective-permute-start.10) | collective-permute-done | bytes 32800 | tf_op jit(solution)/shard_map/ppermute | solution.py:620
  40.6 1.1 shard_map.159.refs_0_
  41.8 1.5 %collective-permute-start.21 = (bf16[32,1024]{1,0:T(8,128)(2,1)S(1)}, bf16[32,1024]{1,0:T(8,128)(2,1)S(1)}, u32[]{:S(2)}, u32[]{:S(2)}) collective-permute-start(bf16[32,1024]{1,0:T(8,128)(2,1)S(1)} %shard_map.159.refs_0_), channel_id=1, source_target_pairs={{0,2},{1,3},{2,0},{3,1},{4,6},{5,7},{6,4},{7,5},{8,10},{9,11},{10,... | collective-permute-start | bytes 196616 | tf_op jit(solution)/shard_map/ppermute | solution.py:24
  43.3 2.8 %collective-permute-done.21.refs_2_ = bf16[32,1024]{1,0:T(8,128)(2,1)S(1)} collective-permute-done((bf16[32,1024]{1,0:T(8,128)(2,1)S(1)}, bf16[32,1024]{1,0:T(8,128)(2,1)S(1)}, u32[]{:S(2)}, u32[]{:S(2)}) %collective-permute-start.21) | collective-permute-done | bytes 65568 | tf_op jit(solution)/shard_map/ppermute | solution.py:24
  46.1 1.2 %collective-permute-done.22.refs_3_ = bf16[32,1024]{1,0:T(8,128)(2,1)S(1)} collective-permute-done((bf16[32,1024]{1,0:T(8,128)(2,1)S(1)}, bf16[32,1024]{1,0:T(8,128)(2,1)S(1)}, u32[]{:S(2)}, u32[]{:S(2)}) %collective-permute-start.22) | collective-permute-done | bytes 65568 | tf_op jit(solution)/shard_map/ppermute | solution.py:24
  47.4 1.3 %shard_map.160 = (f32[16,2048]{1,0:T(8,128)S(1)}, bf16[16,2048]{1,0:T(8,128)(2,1)S(1)}, bf16[16,2048]{1,0:T(8,128)(2,1)S(1)}, bf16[16,2048]{1,0:T(8,128)(2,1)S(1...) custom-call(s32[2]{0:T(128)S(1)} %pad_add_fusion.3.where_ref, ...), custom_call_target="tpu_custom_call" | custom-call | flops 5905580032 | bytes 4194304 | tf_op jit(solution)/shard_map/pallas_call | solution.py:45
  48.7 3.7 %collective-permute-start.23 = (bf16[16,2048]{1,0:T(8,128)(2,1)S(1)}, bf16[16,2048]{1,0:T(8,128)(2,1)S(1)}, u32[]{:S(2)}, u32[]{:S(2)}) collective-permute-start(bf16[16,2048]{1,0:T(8,128)(2,1)S(1)} %get-tuple-element.65), channel_id=1, source_target_pairs={{0,4},{4,0},{8,12},{12,8},{16,20},{20,16},{24,28},{28,24},{1,5},{5... | collective-permute-start | bytes 196616 | tf_op jit(solution)/shard_map/ppermute | solution.py:24
  52.3 3.1 %collective-permute-start.25 = (bf16[16,2048]{1,0:T(8,128)(2,1)S(1)}, bf16[16,2048]{1,0:T(8,128)(2,1)S(1)}, u32[]{:S(2)}, u32[]{:S(2)}) collective-permute-start(bf16[16,2048]{1,0:T(8,128)(2,1)S(1)} %get-tuple-element.68), channel_id=1, source_target_pairs={{0,28},{4,24},{8,20},{12,16},{16,12},{20,8},{24,4},{28,0},{1,29},{... | collective-permute-start | bytes 196616 | tf_op jit(solution)/shard_map/ppermute | solution.py:24
  56.1 3.0 %collective-permute-start.28 = (bf16[16,2048]{1,0:T(8,128)(2,1)S(1)}, bf16[16,2048]{1,0:T(8,128)(2,1)S(1)}, u32[]{:S(2)}, u32[]{:S(2)}) collective-permute-start(bf16[16,2048]{1,0:T(8,128)(2,1)S(1)} %get-tuple-element.71), channel_id=1, source_target_pairs={{0,8},{4,12},{8,0},{12,4},{16,24},{20,28},{24,16},{28,20},{1,9},{5... | collective-permute-start | bytes 196616 | tf_op jit(solution)/shard_map/ppermute | solution.py:24
  59.1 0.8 collective-permute-start.24
  59.9 1.5 %collective-permute-start.29 = (bf16[16,2048]{1,0:T(8,128)(2,1)S(1)}, bf16[16,2048]{1,0:T(8,128)(2,1)S(1)}, u32[]{:S(2)}, u32[]{:S(2)}) collective-permute-start(bf16[16,2048]{1,0:T(8,128)(2,1)S(1)} %get-tuple-element.72), channel_id=1, source_target_pairs={{0,4},{4,0},{8,12},{12,8},{16,20},{20,16},{24,28},{28,24},{1,5},{5... | collective-permute-start | bytes 196616 | tf_op jit(solution)/shard_map/ppermute | solution.py:24
  61.4 1.0 collective-permute-done.26.refs_2_
  62.9 1.6 %collective-permute-done.28.refs_4_ = bf16[16,2048]{1,0:T(8,128)(2,1)S(1)} collective-permute-done((bf16[16,2048]{1,0:T(8,128)(2,1)S(1)}, bf16[16,2048]{1,0:T(8,128)(2,1)S(1)}, u32[]{:S(2)}, u32[]{:S(2)}) %collective-permute-start.28) | collective-permute-done | bytes 65568 | tf_op jit(solution)/shard_map/ppermute | solution.py:24
  64.6 0.7 shard_map.162
  65.3 1.8 %collective-permute-start.30 = (bf16[16,2048]{1,0:T(8,128)(2,1)S(1)}, bf16[16,2048]{1,0:T(8,128)(2,1)S(1)}, u32[]{:S(2)}, u32[]{:S(2)}) collective-permute-start(bf16[16,2048]{1,0:T(8,128)(2,1)S(1)} %get-tuple-element.74.refs_0_), channel_id=1, source_target_pairs={{0,16},{4,20},{8,24},{12,28},{16,0},{20,4},{24,8},{28,12},{1,17},{... | collective-permute-start | bytes 196616 | tf_op jit(solution)/shard_map/ppermute | solution.py:24
  67.1 1.8 %collective-permute-start.31 = (bf16[16,2048]{1,0:T(8,128)(2,1)S(1)}, bf16[16,2048]{1,0:T(8,128)(2,1)S(1)}, u32[]{:S(2)}, u32[]{:S(2)}) collective-permute-start(bf16[16,2048]{1,0:T(8,128)(2,1)S(1)} %get-tuple-element.74.refs_0_), channel_id=1, source_target_pairs={{0,12},{4,8},{8,4},{12,0},{16,28},{20,24},{24,20},{28,16},{1,13},{... | collective-permute-start | bytes 196616 | tf_op jit(solution)/shard_map/ppermute | solution.py:24
  68.9 2.9 %collective-permute-start.33 = (bf16[16,2048]{1,0:T(8,128)(2,1)S(1)}, bf16[16,2048]{1,0:T(8,128)(2,1)S(1)}, u32[]{:S(2)}, u32[]{:S(2)}) collective-permute-start(bf16[16,2048]{1,0:T(8,128)(2,1)S(1)} %get-tuple-element.74.refs_0_), channel_id=1, source_target_pairs={{0,28},{4,24},{8,20},{12,16},{16,12},{20,8},{24,4},{28,0},{1,29},{... | collective-permute-start | bytes 196616 | tf_op jit(solution)/shard_map/ppermute | solution.py:24
  71.7 2.1 %collective-permute-start.34 = (bf16[16,2048]{1,0:T(8,128)(2,1)S(1)}, bf16[16,2048]{1,0:T(8,128)(2,1)S(1)}, u32[]{:S(2)}, u32[]{:S(2)}) collective-permute-start(bf16[16,2048]{1,0:T(8,128)(2,1)S(1)} %get-tuple-element.74.refs_0_), channel_id=1, source_target_pairs={{0,24},{4,28},{8,16},{12,20},{16,8},{20,12},{24,0},{28,4},{1,25},{... | collective-permute-start | bytes 196616 | tf_op jit(solution)/shard_map/ppermute | solution.py:24
  74.2 1.7 %collective-permute-start.35 = (bf16[16,2048]{1,0:T(8,128)(2,1)S(1)}, bf16[16,2048]{1,0:T(8,128)(2,1)S(1)}, u32[]{:S(2)}, u32[]{:S(2)}) collective-permute-start(bf16[16,2048]{1,0:T(8,128)(2,1)S(1)} %collective-permute-done.30.refs_1_), channel_id=1, source_target_pairs={{0,4},{4,0},{8,12},{12,8},{16,20},{20,16},{24,28},{28,24},{1,5},{5... | collective-permute-start | bytes 196616 | tf_op jit(solution)/shard_map/ppermute | solution.py:24
  76.0 1.7 %collective-permute-done.34.refs_5_ = bf16[16,2048]{1,0:T(8,128)(2,1)S(1)} collective-permute-done((bf16[16,2048]{1,0:T(8,128)(2,1)S(1)}, bf16[16,2048]{1,0:T(8,128)(2,1)S(1)}, u32[]{:S(2)}, u32[]{:S(2)}) %collective-permute-start.34) | collective-permute-done | bytes 65568 | tf_op jit(solution)/shard_map/ppermute | solution.py:24
  78.1 0.7 collective-permute-done.35.refs_6_
  78.8 1.8 %shard_map.163 = (bf16[128,2048]{1,0:T(8,128)(2,1)S(1)}, f32[64,1920]{1,0:T(8,128)S(1)}, bf16[64,1920]{1,0:T(8,128)(2,1)S(1)}) custom-call(s32[2]{0:T(128)S(1)} %pad_add_fusion.3.where_ref, f32[1,2048]{1,0:T(1,128)S(1)} %bitcast.19, bf16[16,2048]{1,0:T(8,128)(2,1)S(1)} %get-tuple-element.74.refs_0_, bf16[16,2048]{1,0:T(8,128)(2,1)S(1)} %collective-permute-done.30.refs_1_, ...), custom_call_target="tpu_custom_call" | custom-call | flops 6308233216 | bytes 8388608 | tf_op jit(solution)/shard_map/pallas_call | solution.py:45
  80.8 1.1 %shard_map.164 = (f32[64,1792]{1,0:T(8,128)S(1)}, bf16[64,1792]{1,0:T(8,128)(2,1)S(1)}) custom-call(bf16[128,2048]{1,0:T(8,128)(2,1)S(1)} %get-tuple-element.77.h_ref, bf16[2048,1792]{1,0:T(8,128)(2,1)S(1)} %bitcast.15), custom_call_target="tpu_custom_call" | custom-call | flops 6308233216 | bytes 7340032 | tf_op jit(solution)/shard_map/pallas_call | solution.py:45
  82.5 1.5 %collective-permute-start.38 = (bf16[32,1920]{1,0:T(8,128)(2,1)S(1)}, bf16[32,1920]{1,0:T(8,128)(2,1)S(1)}, u32[]{:S(2)}, u32[]{:S(2)}) collective-permute-start(bf16[32,1920]{1,0:T(8,128)(2,1)S(1)} %slice.64), channel_id=1, source_target_pairs={{0,2},{1,3},{2,0},{3,1},{4,6},{5,7},{6,4},{7,5},{8,10},{9,11},{10,... | collective-permute-start | bytes 368648 | tf_op jit(solution)/shard_map/ppermute | solution.py:24
  84.1 1.0 collective-permute-start.40
  85.1 3.6 %collective-permute-done.38 = bf16[32,1920]{1,0:T(8,128)(2,1)S(1)} collective-permute-done((bf16[32,1920]{1,0:T(8,128)(2,1)S(1)}, bf16[32,1920]{1,0:T(8,128)(2,1)S(1)}, u32[]{:S(2)}, u32[]{:S(2)}) %collective-permute-start.38) | collective-permute-done | bytes 122912 | tf_op jit(solution)/shard_map/ppermute | solution.py:24
  89.0 1.3 %collective-permute-done.40 = bf16[32,1792]{1,0:T(8,128)(2,1)S(1)} collective-permute-done((bf16[32,1792]{1,0:T(8,128)(2,1)S(1)}, bf16[32,1792]{1,0:T(8,128)(2,1)S(1)}, u32[]{:S(2)}, u32[]{:S(2)}) %collective-permute-start.40) | collective-permute-done | bytes 114720 | tf_op jit(solution)/shard_map/ppermute | solution.py:24
  90.5 1.5 %collective-permute-start.42 = (bf16[32,1792]{1,0:T(8,128)(2,1)S(1)}, bf16[32,1792]{1,0:T(8,128)(2,1)S(1)}, u32[]{:S(2)}, u32[]{:S(2)}) collective-permute-start(bf16[32,1792]{1,0:T(8,128)(2,1)S(1)} %fusion.2.refs_0_), channel_id=1, source_target_pairs={{0,2},{1,3},{2,0},{3,1},{4,6},{5,7},{6,4},{7,5},{8,10},{9,11},{10,... | collective-permute-start | bytes 344072 | tf_op jit(solution)/shard_map/ppermute | solution.py:24
  92.0 3.3 %collective-permute-done.42.refs_2_ = bf16[32,1792]{1,0:T(8,128)(2,1)S(1)} collective-permute-done((bf16[32,1792]{1,0:T(8,128)(2,1)S(1)}, bf16[32,1792]{1,0:T(8,128)(2,1)S(1)}, u32[]{:S(2)}, u32[]{:S(2)}) %collective-permute-start.42) | collective-permute-done | bytes 114720 | tf_op jit(solution)/shard_map/ppermute | solution.py:24
  95.3 1.3 %collective-permute-done.43.refs_3_ = bf16[32,1792]{1,0:T(8,128)(2,1)S(1)} collective-permute-done((bf16[32,1792]{1,0:T(8,128)(2,1)S(1)}, bf16[32,1792]{1,0:T(8,128)(2,1)S(1)}, u32[]{:S(2)}, u32[]{:S(2)}) %collective-permute-start.43) | collective-permute-done | bytes 114720 | tf_op jit(solution)/shard_map/ppermute | solution.py:24
  96.7 1.7 %shard_map.165 = (f32[16,2048]{1,0:T(8,128)S(1)}, bf16[16,2048]{1,0:T(8,128)(2,1)S(1)}, bf16[16,2048]{1,0:T(8,128)(2,1)S(1)}, bf16[16,2048]{1,0:T(8,128)(2,1)S(1...) custom-call(s32[2]{0:T(128)S(1)} %pad_add_fusion.3.where_ref, ...), custom_call_target="tpu_custom_call" | custom-call | flops 6308233216 | bytes 7340032 | tf_op jit(solution)/shard_map/pallas_call | solution.py:45
  98.4 1.4 %collective-permute-start.44 = (bf16[16,2048]{1,0:T(8,128)(2,1)S(1)}, bf16[16,2048]{1,0:T(8,128)(2,1)S(1)}, u32[]{:S(2)}, u32[]{:S(2)}) collective-permute-start(bf16[16,2048]{1,0:T(8,128)(2,1)S(1)} %get-tuple-element.82), channel_id=1, source_target_pairs={{0,4},{4,0},{8,12},{12,8},{16,20},{20,16},{24,28},{28,24},{1,5},{5... | collective-permute-start | bytes 196616 | tf_op jit(solution)/shard_map/ppermute | solution.py:24
  99.8 3.1 %collective-permute-start.46 = (bf16[16,2048]{1,0:T(8,128)(2,1)S(1)}, bf16[16,2048]{1,0:T(8,128)(2,1)S(1)}, u32[]{:S(2)}, u32[]{:S(2)}) collective-permute-start(bf16[16,2048]{1,0:T(8,128)(2,1)S(1)} %get-tuple-element.85), channel_id=1, source_target_pairs={{0,28},{4,24},{8,20},{12,16},{16,12},{20,8},{24,4},{28,0},{1,29},{... | collective-permute-start | bytes 196616 | tf_op jit(solution)/shard_map/ppermute | solution.py:24
  102.9 0.9 collective-permute-start.47
  103.7 2.8 %collective-permute-start.49 = (bf16[16,2048]{1,0:T(8,128)(2,1)S(1)}, bf16[16,2048]{1,0:T(8,128)(2,1)S(1)}, u32[]{:S(2)}, u32[]{:S(2)}) collective-permute-start(bf16[16,2048]{1,0:T(8,128)(2,1)S(1)} %get-tuple-element.88), channel_id=1, source_target_pairs={{0,8},{4,12},{8,0},{12,4},{16,24},{20,28},{24,16},{28,20},{1,9},{5... | collective-permute-start | bytes 196616 | tf_op jit(solution)/shard_map/ppermute | solution.py:24
  106.5 1.0 collective-permute-start.45
  107.5 1.3 %collective-permute-start.50 = (bf16[16,2048]{1,0:T(8,128)(2,1)S(1)}, bf16[16,2048]{1,0:T(8,128)(2,1)S(1)}, u32[]{:S(2)}, u32[]{:S(2)}) collective-permute-start(bf16[16,2048]{1,0:T(8,128)(2,1)S(1)} %get-tuple-element.89), channel_id=1, source_target_pairs={{0,4},{4,0},{8,12},{12,8},{16,20},{20,16},{24,28},{28,24},{1,5},{5... | collective-permute-start | bytes 196616 | tf_op jit(solution)/shard_map/ppermute | solution.py:24
  108.8 0.6 collective-permute-done.47.refs_2_
  109.4 1.5 %collective-permute-done.48.refs_3_ = bf16[16,2048]{1,0:T(8,128)(2,1)S(1)} collective-permute-done((bf16[16,2048]{1,0:T(8,128)(2,1)S(1)}, bf16[16,2048]{1,0:T(8,128)(2,1)S(1)}, u32[]{:S(2)}, u32[]{:S(2)}) %collective-permute-start.48) | collective-permute-done | bytes 65568 | tf_op jit(solution)/shard_map/ppermute | solution.py:24
  110.9 1.1 collective-permute-done.49.refs_4_
  112.0 0.6 collective-permute-done.45.refs_0_
  112.6 0.7 shard_map.167
  (112 shorter events, 6.9 us)
Async XLA Ops:
  0.6 7.0 %copy-start.3 = (bf16[8,8,1024]{2,1,0:T(8,128)(2,1)S(1)}, bf16[8,8,1024]{2,1,0:T(8,128)(2,1)}, u32[]{:S(2)}) copy-start(bf16[8,8,1024]{2,1,0:T(8,128)(2,1)} %keys_ref.3) | copy-start | bytes 393220
  0.6 7.0 %copy-start.4 = (bf16[8,8,1024]{2,1,0:T(8,128)(2,1)S(1)}, bf16[8,8,1024]{2,1,0:T(8,128)(2,1)}, u32[]{:S(2)}) copy-start(bf16[8,8,1024]{2,1,0:T(8,128)(2,1)} %values_ref.3) | copy-start | bytes 393220
  2.2 9.7 %collective-permute-start.3 = (bf16[16,2048]{1,0:T(8,128)(2,1)S(1)}, bf16[16,2048]{1,0:T(8,128)(2,1)S(1)}, u32[]{:S(2)}, u32[]{:S(2)}) collective-permute-start(bf16[16,2048]{1,0:T(8,128)(2,1)S(1)} %shard_map.149.x_ref.refs_0_.refs_10_.after_ref.refs_6_), channel_id=1, source_target_pairs={{0,16},{4,20},{8,24},{12,28},{16,0},{20,4},{24,8},{28,12},{1,17},{... | collective-permute-start | bytes 196616 | tf_op jit(solution)/shard_map/ppermute | solution.py:24
  6.3 6.2 %collective-permute-start.5 = (bf16[16,2048]{1,0:T(8,128)(2,1)S(1)}, bf16[16,2048]{1,0:T(8,128)(2,1)S(1)}, u32[]{:S(2)}, u32[]{:S(2)}) collective-permute-start(bf16[16,2048]{1,0:T(8,128)(2,1)S(1)} %shard_map.149.x_ref.refs_0_.refs_10_.after_ref.refs_6_), channel_id=1, source_target_pairs={{0,24},{4,28},{8,16},{12,20},{16,8},{20,12},{24,0},{28,4},{1,25},{... | collective-permute-start | bytes 196616 | tf_op jit(solution)/shard_map/ppermute | solution.py:24
  8.3 8.0 %collective-permute-start = (bf16[24,2048]{1,0:T(8,128)(2,1)S(1)}, bf16[24,2048]{1,0:T(8,128)(2,1)S(1)}, u32[]{:S(2)}, u32[]{:S(2)}) collective-permute-start(bf16[24,2048]{1,0:T(8,128)(2,1)S(1)} %get-tuple-element.46), channel_id=1, source_target_pairs={{0,4},{4,0},{8,12},{12,8},{16,20},{20,16},{24,28},{28,24},{1,5},{5... | collective-permute-start | bytes 294920 | tf_op jit(solution)/shard_map/ppermute | solution.py:24
  9.8 8.1 %collective-permute-start.1 = (bf16[24,2048]{1,0:T(8,128)(2,1)S(1)}, bf16[24,2048]{1,0:T(8,128)(2,1)S(1)}, u32[]{:S(2)}, u32[]{:S(2)}) collective-permute-start(bf16[24,2048]{1,0:T(8,128)(2,1)S(1)} %get-tuple-element.47), channel_id=1, source_target_pairs={{0,8},{4,12},{8,0},{12,4},{16,24},{20,28},{24,16},{28,20},{1,9},{5... | collective-permute-start | bytes 294920 | tf_op jit(solution)/shard_map/ppermute | solution.py:24
  10.1 8.3 %collective-permute-start.2 = (bf16[24,2048]{1,0:T(8,128)(2,1)S(1)}, bf16[24,2048]{1,0:T(8,128)(2,1)S(1)}, u32[]{:S(2)}, u32[]{:S(2)}) collective-permute-start(bf16[24,2048]{1,0:T(8,128)(2,1)S(1)} %get-tuple-element.48), channel_id=1, source_target_pairs={{0,12},{4,8},{8,4},{12,0},{16,28},{20,24},{24,20},{28,16},{1,13},{... | collective-permute-start | bytes 294920 | tf_op jit(solution)/shard_map/ppermute | solution.py:24
  13.1 7.1 %collective-permute-start.14 = (bf16[2,8,2048]{2,1,0:T(8,128)(2,1)S(1)}, bf16[2,8,2048]{2,1,0:T(8,128)(2,1)S(1)}, u32[]{:S(2)}, u32[]{:S(2)}) collective-permute-start(bf16[2,8,2048]{2,1,0:T(8,128)(2,1)S(1)} %get-tuple-element.57), channel_id=1, source_target_pairs={{0,16},{4,20},{8,24},{12,28},{16,0},{20,4},{24,8},{28,12},{1,17},{... | collective-permute-start | bytes 196616 | tf_op jit(solution)/shard_map/ppermute | solution.py:24
  15.9 6.2 %collective-permute-start.15 = (bf16[2,8,2048]{2,1,0:T(8,128)(2,1)S(1)}, bf16[2,8,2048]{2,1,0:T(8,128)(2,1)S(1)}, u32[]{:S(2)}, u32[]{:S(2)}) collective-permute-start(bf16[2,8,2048]{2,1,0:T(8,128)(2,1)S(1)} %get-tuple-element.58), channel_id=1, source_target_pairs={{0,24},{4,28},{8,16},{12,20},{16,8},{20,12},{24,0},{28,4},{1,25},{... | collective-permute-start | bytes 196616 | tf_op jit(solution)/shard_map/ppermute | solution.py:24
  16.3 7.3 %collective-permute-start.4 = (bf16[16,2048]{1,0:T(8,128)(2,1)S(1)}, bf16[16,2048]{1,0:T(8,128)(2,1)S(1)}, u32[]{:S(2)}, u32[]{:S(2)}) collective-permute-start(bf16[16,2048]{1,0:T(8,128)(2,1)S(1)} %collective-permute-done.3.refs_4_.refs_0_), channel_id=1, source_target_pairs={{0,4},{4,0},{8,12},{12,8},{16,20},{20,16},{24,28},{28,24},{1,5},{5... | collective-permute-start | bytes 196616 | tf_op jit(solution)/shard_map/ppermute | solution.py:24
  17.9 5.7 %collective-permute-start.6 = (bf16[16,2048]{1,0:T(8,128)(2,1)S(1)}, bf16[16,2048]{1,0:T(8,128)(2,1)S(1)}, u32[]{:S(2)}, u32[]{:S(2)}) collective-permute-start(bf16[16,2048]{1,0:T(8,128)(2,1)S(1)} %collective-permute-done.5.refs_6_.refs_1_), channel_id=1, source_target_pairs={{0,4},{4,0},{8,12},{12,8},{16,20},{20,16},{24,28},{28,24},{1,5},{5... | collective-permute-start | bytes 196616 | tf_op jit(solution)/shard_map/ppermute | solution.py:24
  18.3 5.2 %copy-start = (bf16[2048,1024]{1,0:T(8,128)(2,1)S(1)}, bf16[2048,1024]{1,0:T(8,128)(2,1)}, u32[]{:S(2)}) copy-start(bf16[2048,1024]{1,0:T(8,128)(2,1)} %refs_9_.1) | copy-start | bytes 12582916
  18.4 5.2 %copy-start.2 = (bf16[2048,256]{1,0:T(8,128)(2,1)S(1)}, bf16[2048,256]{1,0:T(8,128)(2,1)}, u32[]{:S(2)}) copy-start(bf16[2048,256]{1,0:T(8,128)(2,1)} %refs_8_.2) | copy-start | bytes 3145732
  18.4 5.2 %copy-start.7 = (f32[2048]{0:T(1024)S(1)}, f32[2048]{0:T(1024)}, u32[]{:S(2)}) copy-start(f32[2048]{0:T(1024)} %param.19) | copy-start | bytes 24580
  18.4 11.2 %collective-permute-start.12 = (bf16[4,8,2048]{2,1,0:T(8,128)(2,1)S(1)}, bf16[4,8,2048]{2,1,0:T(8,128)(2,1)S(1)}, u32[]{:S(2)}, u32[]{:S(2)}) collective-permute-start(bf16[4,8,2048]{2,1,0:T(8,128)(2,1)S(1)} %shard_map.154.refs_2_), channel_id=1, source_target_pairs={{0,2},{1,3},{2,0},{3,1},{4,6},{5,7},{6,4},{7,5},{8,10},{9,11},{10,... | collective-permute-start | bytes 393224 | tf_op jit(solution)/shard_map/ppermute | solution.py:24
  22.0 4.3 %collective-permute-start.16 = (bf16[2,8,2048]{2,1,0:T(8,128)(2,1)S(1)}, bf16[2,8,2048]{2,1,0:T(8,128)(2,1)S(1)}, u32[]{:S(2)}, u32[]{:S(2)}) collective-permute-start(bf16[2,8,2048]{2,1,0:T(8,128)(2,1)S(1)} %shard_map.156), channel_id=1, source_target_pairs={{0,4},{4,0},{8,12},{12,8},{16,20},{20,16},{24,28},{28,24},{1,5},{5... | collective-permute-start | bytes 196616 | tf_op jit(solution)/shard_map/ppermute | solution.py:24
  25.1 2.8 %collective-permute-start.7 = (bf16[128,896]{1,0:T(8,128)(2,1)S(1)}, bf16[128,896]{1,0:T(8,128)(2,1)S(1)}, u32[]{:S(2)}, u32[]{:S(2)}) collective-permute-start(bf16[128,896]{1,0:T(8,128)(2,1)S(1)} %get-tuple-element.49.own_ref), channel_id=1, source_target_pairs={{0,1},{1,0},{2,3},{3,2},{4,5},{5,4},{6,7},{7,6},{8,9},{9,8},{10,11... | collective-permute-start | bytes 688136 | tf_op jit(solution)/shard_map/ppermute | solution.py:24
  26.3 6.4 %collective-permute-start.18 = (bf16[4,8,2048]{2,1,0:T(8,128)(2,1)S(1)}, bf16[4,8,2048]{2,1,0:T(8,128)(2,1)S(1)}, u32[]{:S(2)}, u32[]{:S(2)}) collective-permute-start(bf16[4,8,2048]{2,1,0:T(8,128)(2,1)S(1)} %shard_map.157.refs_6_), channel_id=1, source_target_pairs={{0,2},{1,3},{2,0},{3,1},{4,6},{5,7},{6,4},{7,5},{8,10},{9,11},{10,... | collective-permute-start | bytes 393224 | tf_op jit(solution)/shard_map/ppermute | solution.py:24
  28.1 6.7 %collective-permute-start.8 = (bf16[128,640]{1,0:T(8,128)(2,1)S(1)}, bf16[128,640]{1,0:T(8,128)(2,1)S(1)}, u32[]{:S(2)}, u32[]{:S(2)}) collective-permute-start(bf16[128,640]{1,0:T(8,128)(2,1)S(1)} %get-tuple-element.51.own_ref), channel_id=1, source_target_pairs={{0,2},{1,3},{2,0},{3,1},{4,6},{5,7},{6,4},{7,5},{8,10},{9,11},{10,... | collective-permute-start | bytes 491528 | tf_op jit(solution)/shard_map/ppermute | solution.py:24
  29.0 7.8 %copy-start.9 = (f32[4,128]{1,0:T(4,128)S(1)}, f32[4,128]{1,0:T(4,128)}, u32[]{:S(2)}) copy-start(f32[4,128]{1,0:T(4,128)} %constant.71.clone.rope_ref) | copy-start | bytes 6148
  29.0 7.0 %collective-permute-start.11 = (bf16[4,8,2048]{2,1,0:T(8,128)(2,1)S(1)}, bf16[4,8,2048]{2,1,0:T(8,128)(2,1)S(1)}, u32[]{:S(2)}, u32[]{:S(2)}) collective-permute-start(bf16[4,8,2048]{2,1,0:T(8,128)(2,1)S(1)} %shard_map.154.refs_2_), channel_id=1, source_target_pairs={{0,1},{1,0},{2,3},{3,2},{4,5},{5,4},{6,7},{7,6},{8,9},{9,8},{10,11... | collective-permute-start | bytes 393224 | tf_op jit(solution)/shard_map/ppermute | solution.py:24
  29.1 7.6 %collective-permute-start.17 = (bf16[4,8,2048]{2,1,0:T(8,128)(2,1)S(1)}, bf16[4,8,2048]{2,1,0:T(8,128)(2,1)S(1)}, u32[]{:S(2)}, u32[]{:S(2)}) collective-permute-start(bf16[4,8,2048]{2,1,0:T(8,128)(2,1)S(1)} %shard_map.157.refs_6_), channel_id=1, source_target_pairs={{0,1},{1,0},{2,3},{3,2},{4,5},{5,4},{6,7},{7,6},{8,9},{9,8},{10,11... | collective-permute-start | bytes 393224 | tf_op jit(solution)/shard_map/ppermute | solution.py:24
  29.6 7.1 %collective-permute-start.13 = (bf16[4,8,2048]{2,1,0:T(8,128)(2,1)S(1)}, bf16[4,8,2048]{2,1,0:T(8,128)(2,1)S(1)}, u32[]{:S(2)}, u32[]{:S(2)}) collective-permute-start(bf16[4,8,2048]{2,1,0:T(8,128)(2,1)S(1)} %collective-permute-done.12.refs_4_), channel_id=1, source_target_pairs={{0,1},{1,0},{2,3},{3,2},{4,5},{5,4},{6,7},{7,6},{8,9},{9,8},{10,11... | collective-permute-start | bytes 393224 | tf_op jit(solution)/shard_map/ppermute | solution.py:24
  32.7 4.0 %collective-permute-start.19 = (bf16[4,8,2048]{2,1,0:T(8,128)(2,1)S(1)}, bf16[4,8,2048]{2,1,0:T(8,128)(2,1)S(1)}, u32[]{:S(2)}, u32[]{:S(2)}) collective-permute-start(bf16[4,8,2048]{2,1,0:T(8,128)(2,1)S(1)} %collective-permute-done.18.refs_8_), channel_id=1, source_target_pairs={{0,1},{1,0},{2,3},{3,2},{4,5},{5,4},{6,7},{7,6},{8,9},{9,8},{10,11... | collective-permute-start | bytes 393224 | tf_op jit(solution)/shard_map/ppermute | solution.py:24
  35.5 5.1 %collective-permute-start.10 = (bf16[128,128]{1,0:T(8,128)(2,1)S(1)}, bf16[128,128]{1,0:T(8,128)(2,1)S(1)}, u32[]{:S(2)}, u32[]{:S(2)}) collective-permute-start(bf16[128,128]{1,0:T(8,128)(2,1)S(1)} %get-tuple-element.53), channel_id=1, source_target_pairs={{0,4},{4,12},{8,20},{12,28},{16,0},{20,8},{24,16},{28,24},{1,5},{5... | collective-permute-start | bytes 98312 | tf_op jit(solution)/shard_map/ppermute | solution.py:620
  36.1 4.6 %collective-permute-start.9 = (bf16[128,128]{1,0:T(8,128)(2,1)S(1)}, bf16[128,128]{1,0:T(8,128)(2,1)S(1)}, u32[]{:S(2)}, u32[]{:S(2)}) collective-permute-start(bf16[128,128]{1,0:T(8,128)(2,1)S(1)} %get-tuple-element.52), channel_id=1, source_target_pairs={{0,0},{4,8},{8,16},{12,24},{16,4},{20,12},{24,20},{28,28},{1,1},{5... | collective-permute-start | bytes 98312 | tf_op jit(solution)/shard_map/ppermute | solution.py:620
  40.6 6.7 %copy-start.1 = (bf16[1024,2048]{1,0:T(8,128)(2,1)S(1)}, bf16[1024,2048]{1,0:T(8,128)(2,1)}, u32[]{:S(2)}) copy-start(bf16[1024,2048]{1,0:T(8,128)(2,1)} %refs_4_.2) | copy-start | bytes 12582916
  41.8 4.3 %collective-permute-start.21 = (bf16[32,1024]{1,0:T(8,128)(2,1)S(1)}, bf16[32,1024]{1,0:T(8,128)(2,1)S(1)}, u32[]{:S(2)}, u32[]{:S(2)}) collective-permute-start(bf16[32,1024]{1,0:T(8,128)(2,1)S(1)} %shard_map.159.refs_0_), channel_id=1, source_target_pairs={{0,2},{1,3},{2,0},{3,1},{4,6},{5,7},{6,4},{7,5},{8,10},{9,11},{10,... | collective-permute-start | bytes 196616 | tf_op jit(solution)/shard_map/ppermute | solution.py:24
  43.3 2.8 %collective-permute-start.20 = (bf16[32,1024]{1,0:T(8,128)(2,1)S(1)}, bf16[32,1024]{1,0:T(8,128)(2,1)S(1)}, u32[]{:S(2)}, u32[]{:S(2)}) collective-permute-start(bf16[32,1024]{1,0:T(8,128)(2,1)S(1)} %shard_map.159.refs_0_), channel_id=1, source_target_pairs={{0,1},{1,0},{2,3},{3,2},{4,5},{5,4},{6,7},{7,6},{8,9},{9,8},{10,11... | collective-permute-start | bytes 196616 | tf_op jit(solution)/shard_map/ppermute | solution.py:24
  46.1 1.3 %collective-permute-start.22 = (bf16[32,1024]{1,0:T(8,128)(2,1)S(1)}, bf16[32,1024]{1,0:T(8,128)(2,1)S(1)}, u32[]{:S(2)}, u32[]{:S(2)}) collective-permute-start(bf16[32,1024]{1,0:T(8,128)(2,1)S(1)} %collective-permute-done.21.refs_2_), channel_id=1, source_target_pairs={{0,1},{1,0},{2,3},{3,2},{4,5},{5,4},{6,7},{7,6},{8,9},{9,8},{10,11... | collective-permute-start | bytes 196616 | tf_op jit(solution)/shard_map/ppermute | solution.py:24
  48.7 10.4 %collective-permute-start.23 = (bf16[16,2048]{1,0:T(8,128)(2,1)S(1)}, bf16[16,2048]{1,0:T(8,128)(2,1)S(1)}, u32[]{:S(2)}, u32[]{:S(2)}) collective-permute-start(bf16[16,2048]{1,0:T(8,128)(2,1)S(1)} %get-tuple-element.65), channel_id=1, source_target_pairs={{0,4},{4,0},{8,12},{12,8},{16,20},{20,16},{24,28},{28,24},{1,5},{5... | collective-permute-start | bytes 196616 | tf_op jit(solution)/shard_map/ppermute | solution.py:24
  52.3 7.6 %collective-permute-start.25 = (bf16[16,2048]{1,0:T(8,128)(2,1)S(1)}, bf16[16,2048]{1,0:T(8,128)(2,1)S(1)}, u32[]{:S(2)}, u32[]{:S(2)}) collective-permute-start(bf16[16,2048]{1,0:T(8,128)(2,1)S(1)} %get-tuple-element.68), channel_id=1, source_target_pairs={{0,28},{4,24},{8,20},{12,16},{16,12},{20,8},{24,4},{28,0},{1,29},{... | collective-permute-start | bytes 196616 | tf_op jit(solution)/shard_map/ppermute | solution.py:24
  55.4 7.0 %collective-permute-start.26 = (bf16[16,2048]{1,0:T(8,128)(2,1)S(1)}, bf16[16,2048]{1,0:T(8,128)(2,1)S(1)}, u32[]{:S(2)}, u32[]{:S(2)}) collective-permute-start(bf16[16,2048]{1,0:T(8,128)(2,1)S(1)} %get-tuple-element.69), channel_id=1, source_target_pairs={{0,24},{4,28},{8,16},{12,20},{16,8},{20,12},{24,0},{28,4},{1,25},{... | collective-permute-start | bytes 196616 | tf_op jit(solution)/shard_map/ppermute | solution.py:24
  55.7 7.3 %collective-permute-start.27 = (bf16[16,2048]{1,0:T(8,128)(2,1)S(1)}, bf16[16,2048]{1,0:T(8,128)(2,1)S(1)}, u32[]{:S(2)}, u32[]{:S(2)}) collective-permute-start(bf16[16,2048]{1,0:T(8,128)(2,1)S(1)} %get-tuple-element.70), channel_id=1, source_target_pairs={{0,12},{4,8},{8,4},{12,0},{16,28},{20,24},{24,20},{28,16},{1,13},{... | collective-permute-start | bytes 196616 | tf_op jit(solution)/shard_map/ppermute | solution.py:24
  56.1 8.5 %collective-permute-start.28 = (bf16[16,2048]{1,0:T(8,128)(2,1)S(1)}, bf16[16,2048]{1,0:T(8,128)(2,1)S(1)}, u32[]{:S(2)}, u32[]{:S(2)}) collective-permute-start(bf16[16,2048]{1,0:T(8,128)(2,1)S(1)} %get-tuple-element.71), channel_id=1, source_target_pairs={{0,8},{4,12},{8,0},{12,4},{16,24},{20,28},{24,16},{28,20},{1,9},{5... | collective-permute-start | bytes 196616 | tf_op jit(solution)/shard_map/ppermute | solution.py:24
  59.1 19.7 %slice-start = ((s8[7340032]{0:T(1024)(128)(4,1)}), s8[4194304]{0:T(1024)(128)(4,1)S(1)}, s32[]{:S(2)}) async-start(s8[7340032]{0:T(1024)(128)(4,1)} %bitcast.12), calls=%async_computation | async-start | bytes 8388608
  59.1 5.5 %collective-permute-start.24 = (bf16[16,2048]{1,0:T(8,128)(2,1)S(1)}, bf16[16,2048]{1,0:T(8,128)(2,1)S(1)}, u32[]{:S(2)}, u32[]{:S(2)}) collective-permute-start(bf16[16,2048]{1,0:T(8,128)(2,1)S(1)} %get-tuple-element.67), channel_id=1, source_target_pairs={{0,16},{4,20},{8,24},{12,28},{16,0},{20,4},{24,8},{28,12},{1,17},{... | collective-permute-start | bytes 196616 | tf_op jit(solution)/shard_map/ppermute | solution.py:24
  59.9 18.9 %slice-start.1 = ((s8[7340032]{0:T(1024)(128)(4,1)}), s8[3145728]{0:T(1024)(128)(4,1)S(1)}, s32[]{:S(2)}) async-start(s8[7340032]{0:T(1024)(128)(4,1)} %bitcast.12), calls=%async_computation.1 | async-start | bytes 6291456
  59.9 4.7 %collective-permute-start.29 = (bf16[16,2048]{1,0:T(8,128)(2,1)S(1)}, bf16[16,2048]{1,0:T(8,128)(2,1)S(1)}, u32[]{:S(2)}, u32[]{:S(2)}) collective-permute-start(bf16[16,2048]{1,0:T(8,128)(2,1)S(1)} %get-tuple-element.72), channel_id=1, source_target_pairs={{0,4},{4,0},{8,12},{12,8},{16,20},{20,16},{24,28},{28,24},{1,5},{5... | collective-permute-start | bytes 196616 | tf_op jit(solution)/shard_map/ppermute | solution.py:24
  64.6 14.2 %copy-start.8 = (f32[2048]{0:T(1024)S(1)}, f32[2048]{0:T(1024)}, u32[]{:S(2)}) copy-start(f32[2048]{0:T(1024)} %param.20) | copy-start | bytes 24580
  64.6 16.1 %slice-start.2 = ((s8[7340032]{0:T(1024)(128)(4,1)}), s8[4194304]{0:T(1024)(128)(4,1)S(1)}, s32[]{:S(2)}) async-start(s8[7340032]{0:T(1024)(128)(4,1)} %bitcast.14), calls=%async_computation.2 | async-start | bytes 8388608
  65.3 8.5 %collective-permute-start.30 = (bf16[16,2048]{1,0:T(8,128)(2,1)S(1)}, bf16[16,2048]{1,0:T(8,128)(2,1)S(1)}, u32[]{:S(2)}, u32[]{:S(2)}) collective-permute-start(bf16[16,2048]{1,0:T(8,128)(2,1)S(1)} %get-tuple-element.74.refs_0_), channel_id=1, source_target_pairs={{0,16},{4,20},{8,24},{12,28},{16,0},{20,4},{24,8},{28,12},{1,17},{... | collective-permute-start | bytes 196616 | tf_op jit(solution)/shard_map/ppermute | solution.py:24
  67.1 7.1 %collective-permute-start.31 = (bf16[16,2048]{1,0:T(8,128)(2,1)S(1)}, bf16[16,2048]{1,0:T(8,128)(2,1)S(1)}, u32[]{:S(2)}, u32[]{:S(2)}) collective-permute-start(bf16[16,2048]{1,0:T(8,128)(2,1)S(1)} %get-tuple-element.74.refs_0_), channel_id=1, source_target_pairs={{0,12},{4,8},{8,4},{12,0},{16,28},{20,24},{24,20},{28,16},{1,13},{... | collective-permute-start | bytes 196616 | tf_op jit(solution)/shard_map/ppermute | solution.py:24
  68.9 7.0 %collective-permute-start.32 = (bf16[16,2048]{1,0:T(8,128)(2,1)S(1)}, bf16[16,2048]{1,0:T(8,128)(2,1)S(1)}, u32[]{:S(2)}, u32[]{:S(2)}) collective-permute-start(bf16[16,2048]{1,0:T(8,128)(2,1)S(1)} %get-tuple-element.74.refs_0_), channel_id=1, source_target_pairs={{0,8},{4,12},{8,0},{12,4},{16,24},{20,28},{24,16},{28,20},{1,9},{5... | collective-permute-start | bytes 196616 | tf_op jit(solution)/shard_map/ppermute | solution.py:24
  68.9 7.2 %collective-permute-start.33 = (bf16[16,2048]{1,0:T(8,128)(2,1)S(1)}, bf16[16,2048]{1,0:T(8,128)(2,1)S(1)}, u32[]{:S(2)}, u32[]{:S(2)}) collective-permute-start(bf16[16,2048]{1,0:T(8,128)(2,1)S(1)} %get-tuple-element.74.refs_0_), channel_id=1, source_target_pairs={{0,28},{4,24},{8,20},{12,16},{16,12},{20,8},{24,4},{28,0},{1,29},{... | collective-permute-start | bytes 196616 | tf_op jit(solution)/shard_map/ppermute | solution.py:24
  71.7 6.1 %collective-permute-start.34 = (bf16[16,2048]{1,0:T(8,128)(2,1)S(1)}, bf16[16,2048]{1,0:T(8,128)(2,1)S(1)}, u32[]{:S(2)}, u32[]{:S(2)}) collective-permute-start(bf16[16,2048]{1,0:T(8,128)(2,1)S(1)} %get-tuple-element.74.refs_0_), channel_id=1, source_target_pairs={{0,24},{4,28},{8,16},{12,20},{16,8},{20,12},{24,0},{28,4},{1,25},{... | collective-permute-start | bytes 196616 | tf_op jit(solution)/shard_map/ppermute | solution.py:24
  73.8 4.3 %collective-permute-start.36 = (bf16[16,2048]{1,0:T(8,128)(2,1)S(1)}, bf16[16,2048]{1,0:T(8,128)(2,1)S(1)}, u32[]{:S(2)}, u32[]{:S(2)}) collective-permute-start(bf16[16,2048]{1,0:T(8,128)(2,1)S(1)} %get-tuple-element.74.refs_0_), channel_id=1, source_target_pairs={{0,4},{4,0},{8,12},{12,8},{16,20},{20,16},{24,28},{28,24},{1,5},{5... | collective-permute-start | bytes 196616 | tf_op jit(solution)/shard_map/ppermute | solution.py:24
  74.2 4.6 %collective-permute-start.35 = (bf16[16,2048]{1,0:T(8,128)(2,1)S(1)}, bf16[16,2048]{1,0:T(8,128)(2,1)S(1)}, u32[]{:S(2)}, u32[]{:S(2)}) collective-permute-start(bf16[16,2048]{1,0:T(8,128)(2,1)S(1)} %collective-permute-done.30.refs_1_), channel_id=1, source_target_pairs={{0,4},{4,0},{8,12},{12,8},{16,20},{20,16},{24,28},{28,24},{1,5},{5... | collective-permute-start | bytes 196616 | tf_op jit(solution)/shard_map/ppermute | solution.py:24
  78.8 17.8 %slice-start.4 = ((s8[7340032]{0:T(1024)(128)(4,1)}), s8[4194304]{0:T(1024)(128)(4,1)S(1)}, s32[]{:S(2)}) async-start(s8[7340032]{0:T(1024)(128)(4,1)} %bitcast.16), calls=%async_computation.4 | async-start | bytes 8388608
  80.6 1.8 %collective-permute-start.37 = (bf16[64,1920]{1,0:T(8,128)(2,1)S(1)}, bf16[64,1920]{1,0:T(8,128)(2,1)S(1)}, u32[]{:S(2)}, u32[]{:S(2)}) collective-permute-start(bf16[64,1920]{1,0:T(8,128)(2,1)S(1)} %get-tuple-element.76), channel_id=1, source_target_pairs={{0,1},{1,0},{2,3},{3,2},{4,5},{5,4},{6,7},{7,6},{8,9},{9,8},{10,11... | collective-permute-start | bytes 737288 | tf_op jit(solution)/shard_map/ppermute | solution.py:24
  80.7 15.9 %slice-start.5 = ((s8[7340032]{0:T(1024)(128)(4,1)}), s8[3145728]{0:T(1024)(128)(4,1)S(1)}, s32[]{:S(2)}) async-start(s8[7340032]{0:T(1024)(128)(4,1)} %bitcast.16), calls=%async_computation.5 | async-start | bytes 6291456
  81.9 2.1 %collective-permute-start.39 = (bf16[64,1792]{1,0:T(8,128)(2,1)S(1)}, bf16[64,1792]{1,0:T(8,128)(2,1)S(1)}, u32[]{:S(2)}, u32[]{:S(2)}) collective-permute-start(bf16[64,1792]{1,0:T(8,128)(2,1)S(1)} %get-tuple-element.79), channel_id=1, source_target_pairs={{0,1},{1,0},{2,3},{3,2},{4,5},{5,4},{6,7},{7,6},{8,9},{9,8},{10,11... | collective-permute-start | bytes 688136 | tf_op jit(solution)/shard_map/ppermute | solution.py:24
  82.5 6.2 %collective-permute-start.38 = (bf16[32,1920]{1,0:T(8,128)(2,1)S(1)}, bf16[32,1920]{1,0:T(8,128)(2,1)S(1)}, u32[]{:S(2)}, u32[]{:S(2)}) collective-permute-start(bf16[32,1920]{1,0:T(8,128)(2,1)S(1)} %slice.64), channel_id=1, source_target_pairs={{0,2},{1,3},{2,0},{3,1},{4,6},{5,7},{6,4},{7,5},{8,10},{9,11},{10,... | collective-permute-start | bytes 368648 | tf_op jit(solution)/shard_map/ppermute | solution.py:24
  84.1 6.2 %collective-permute-start.40 = (bf16[32,1792]{1,0:T(8,128)(2,1)S(1)}, bf16[32,1792]{1,0:T(8,128)(2,1)S(1)}, u32[]{:S(2)}, u32[]{:S(2)}) collective-permute-start(bf16[32,1792]{1,0:T(8,128)(2,1)S(1)} %slice.65), channel_id=1, source_target_pairs={{0,2},{1,3},{2,0},{3,1},{4,6},{5,7},{6,4},{7,5},{8,10},{9,11},{10,... | collective-permute-start | bytes 344072 | tf_op jit(solution)/shard_map/ppermute | solution.py:24
  90.5 4.9 %collective-permute-start.42 = (bf16[32,1792]{1,0:T(8,128)(2,1)S(1)}, bf16[32,1792]{1,0:T(8,128)(2,1)S(1)}, u32[]{:S(2)}, u32[]{:S(2)}) collective-permute-start(bf16[32,1792]{1,0:T(8,128)(2,1)S(1)} %fusion.2.refs_0_), channel_id=1, source_target_pairs={{0,2},{1,3},{2,0},{3,1},{4,6},{5,7},{6,4},{7,5},{8,10},{9,11},{10,... | collective-permute-start | bytes 344072 | tf_op jit(solution)/shard_map/ppermute | solution.py:24
  92.0 3.4 %collective-permute-start.41 = (bf16[32,1792]{1,0:T(8,128)(2,1)S(1)}, bf16[32,1792]{1,0:T(8,128)(2,1)S(1)}, u32[]{:S(2)}, u32[]{:S(2)}) collective-permute-start(bf16[32,1792]{1,0:T(8,128)(2,1)S(1)} %fusion.2.refs_0_), channel_id=1, source_target_pairs={{0,1},{1,0},{2,3},{3,2},{4,5},{5,4},{6,7},{7,6},{8,9},{9,8},{10,11... | collective-permute-start | bytes 344072 | tf_op jit(solution)/shard_map/ppermute | solution.py:24
  95.3 1.3 %collective-permute-start.43 = (bf16[32,1792]{1,0:T(8,128)(2,1)S(1)}, bf16[32,1792]{1,0:T(8,128)(2,1)S(1)}, u32[]{:S(2)}, u32[]{:S(2)}) collective-permute-start(bf16[32,1792]{1,0:T(8,128)(2,1)S(1)} %collective-permute-done.42.refs_2_), channel_id=1, source_target_pairs={{0,1},{1,0},{2,3},{3,2},{4,5},{5,4},{6,7},{7,6},{8,9},{9,8},{10,11... | collective-permute-start | bytes 344072 | tf_op jit(solution)/shard_map/ppermute | solution.py:24
  98.4 8.2 %collective-permute-start.44 = (bf16[16,2048]{1,0:T(8,128)(2,1)S(1)}, bf16[16,2048]{1,0:T(8,128)(2,1)S(1)}, u32[]{:S(2)}, u32[]{:S(2)}) collective-permute-start(bf16[16,2048]{1,0:T(8,128)(2,1)S(1)} %get-tuple-element.82), channel_id=1, source_target_pairs={{0,4},{4,0},{8,12},{12,8},{16,20},{20,16},{24,28},{28,24},{1,5},{5... | collective-permute-start | bytes 196616 | tf_op jit(solution)/shard_map/ppermute | solution.py:24
  99.8 7.7 %collective-permute-start.46 = (bf16[16,2048]{1,0:T(8,128)(2,1)S(1)}, bf16[16,2048]{1,0:T(8,128)(2,1)S(1)}, u32[]{:S(2)}, u32[]{:S(2)}) collective-permute-start(bf16[16,2048]{1,0:T(8,128)(2,1)S(1)} %get-tuple-element.85), channel_id=1, source_target_pairs={{0,28},{4,24},{8,20},{12,16},{16,12},{20,8},{24,4},{28,0},{1,29},{... | collective-permute-start | bytes 196616 | tf_op jit(solution)/shard_map/ppermute | solution.py:24
  102.9 6.6 %collective-permute-start.47 = (bf16[16,2048]{1,0:T(8,128)(2,1)S(1)}, bf16[16,2048]{1,0:T(8,128)(2,1)S(1)}, u32[]{:S(2)}, u32[]{:S(2)}) collective-permute-start(bf16[16,2048]{1,0:T(8,128)(2,1)S(1)} %get-tuple-element.86), channel_id=1, source_target_pairs={{0,24},{4,28},{8,16},{12,20},{16,8},{20,12},{24,0},{28,4},{1,25},{... | collective-permute-start | bytes 196616 | tf_op jit(solution)/shard_map/ppermute | solution.py:24
  103.7 7.2 %collective-permute-start.48 = (bf16[16,2048]{1,0:T(8,128)(2,1)S(1)}, bf16[16,2048]{1,0:T(8,128)(2,1)S(1)}, u32[]{:S(2)}, u32[]{:S(2)}) collective-permute-start(bf16[16,2048]{1,0:T(8,128)(2,1)S(1)} %get-tuple-element.87), channel_id=1, source_target_pairs={{0,12},{4,8},{8,4},{12,0},{16,28},{20,24},{24,20},{28,16},{1,13},{... | collective-permute-start | bytes 196616 | tf_op jit(solution)/shard_map/ppermute | solution.py:24
  103.7 8.3 %collective-permute-start.49 = (bf16[16,2048]{1,0:T(8,128)(2,1)S(1)}, bf16[16,2048]{1,0:T(8,128)(2,1)S(1)}, u32[]{:S(2)}, u32[]{:S(2)}) collective-permute-start(bf16[16,2048]{1,0:T(8,128)(2,1)S(1)} %get-tuple-element.88), channel_id=1, source_target_pairs={{0,8},{4,12},{8,0},{12,4},{16,24},{20,28},{24,16},{28,20},{1,9},{5... | collective-permute-start | bytes 196616 | tf_op jit(solution)/shard_map/ppermute | solution.py:24
  106.5 6.0 %collective-permute-start.45 = (bf16[16,2048]{1,0:T(8,128)(2,1)S(1)}, bf16[16,2048]{1,0:T(8,128)(2,1)S(1)}, u32[]{:S(2)}, u32[]{:S(2)}) collective-permute-start(bf16[16,2048]{1,0:T(8,128)(2,1)S(1)} %get-tuple-element.84), channel_id=1, source_target_pairs={{0,16},{4,20},{8,24},{12,28},{16,0},{20,4},{24,8},{28,12},{1,17},{... | collective-permute-start | bytes 196616 | tf_op jit(solution)/shard_map/ppermute | solution.py:24
  107.5 5.1 %collective-permute-start.50 = (bf16[16,2048]{1,0:T(8,128)(2,1)S(1)}, bf16[16,2048]{1,0:T(8,128)(2,1)S(1)}, u32[]{:S(2)}, u32[]{:S(2)}) collective-permute-start(bf16[16,2048]{1,0:T(8,128)(2,1)S(1)} %get-tuple-element.89), channel_id=1, source_target_pairs={{0,4},{4,0},{8,12},{12,8},{16,20},{20,16},{24,28},{28,24},{1,5},{5... | collective-permute-start | bytes 196616 | tf_op jit(solution)/shard_map/ppermute | solution.py:24
  (4 other events, 7.7 us)

commit v13 on v11

--- a/solution.py
+++ b/solution.py
@@ -174,6 +174,18 @@
             refs[-1][k] = ref[...].astype(F32)[ref.shape[0] - span :].astype(BF16)
 
     return call(body, shaped((1 + len(near),) + own.shape), (own, *near), [VMEM] * (1 + len(near)), around=1)
+
+
+def gather_cache(block, after):
+    blocks = [block] + [swap(block, "tensor", k) for k in range(2, lax.axis_size("tensor"), 2)]
+
+    def body(after_ref, *refs):
+        for i, ref in enumerate(refs[:-1]):
+            refs[-1][i] = ref[...]
+
+    ins = (after, *blocks)
+    both = call(body, shaped((len(blocks),) + block.shape), ins, [ANY] + [VMEM] * len(blocks), around=0)
+    return blocks + [swap(both, "tensor", 1)]
 
 
 def last_entries(pieces, after):
@@ -268,30 +280,51 @@
     )
 
 
-def add_cores(own, keep, arrived):
+def direct_keyvals():
+    return lax.axis_size("dp") == KVH and lax.axis_size("tensor") == 4
+
+
+def add_cores(where, own, keep, arrived):
     tensor = lax.axis_size("tensor")
+    groups = lax.axis_size("dp")
     rows, total = own.shape
     half, wide = keep.shape
     base = total - wide // 2
     height = 2 * half // tensor
-    joined = tensor == 4
-
-    def body(own_ref, keep_ref, arrived_ref, first_ref, message_ref, *out_refs):
+    direct = direct_keyvals()
+
+    def body(where_ref, own_ref, keep_ref, arrived_ref, first_ref, message_ref, *out_refs):
         summed = own_ref[:, :base].astype(F32) + arrived_ref[:, :base].astype(F32)
         ends = summed[:, base - 128 :]
         lane = lax.broadcasted_iota(jnp.int32, ends.shape, 1)
-        message_ref[:, : base - 128] = summed[:, : base - 128].astype(BF16)
-        message_ref[:, base - 128 : base] = split(ends[:, 0:1] + ends[:, 1:2], ends, lane).astype(BF16)
+        ends = split(ends[:, 0:1] + ends[:, 1:2], ends, lane).astype(BF16)
         queries = keep_ref[...] + unstacked(arrived_ref[:, base:].astype(F32), 2)
         first_ref[...] = queries[:height]
-        if joined:
-            message_ref[:, base:] = stacked(queries[height:], 4).astype(BF16)
-        for i, out_ref in enumerate(out_refs, 1):
-            out_ref[...] = queries[i * height : (i + 1) * height].astype(BF16)
-
-    outs = [shaped((height, wide), F32), shaped((rows, base + (wide // 4 if joined else 0)))]
-    outs += [] if joined else [shaped((height, wide))] * (tensor // 2 - 1)
-    return call(body, tuple(outs), (own, keep, arrived), [VMEM] * 3, moved=6 * own.size, around=1)
+        if direct:
+            message_ref[:, :128] = ends
+            message_ref[:, 128:] = stacked(queries[height:], 4).astype(BF16)
+            lower = where_ref[0] < groups // 2
+            one, two = summed[:, :HD], summed[:, HD : 2 * HD]
+            out_refs[0][...] = jnp.where(lower, one, two).astype(BF16)
+            out_refs[1][...] = jnp.where(lower, two, one).astype(BF16)
+        else:
+            message_ref[:, : base - 128] = summed[:, : base - 128].astype(BF16)
+            message_ref[:, base - 128 :] = ends
+            for i, out_ref in enumerate(out_refs, 1):
+                out_ref[...] = queries[i * height : (i + 1) * height].astype(BF16)
+
+    outs = [shaped((height, wide), F32), shaped((rows, 128 + wide // 4 if direct else base))]
+    outs += [shaped((rows, HD))] * 2 if direct else [shaped((height, wide))] * (tensor // 2 - 1)
+    return call(body, tuple(outs), (where, own, keep, arrived), [SMEM] + [VMEM] * 3, moved=6 * own.size)
+
+
+def row_scale(own, arrived, width):
+    def body(own_ref, arrived_ref, out_ref):
+        squares = own_ref[:, :128].astype(F32) + arrived_ref[:, :128].astype(F32)
+        scale = lax.rsqrt((squares[:, 0:1] + squares[:, 1:2]) / width + EPS)
+        out_ref[...] = jnp.broadcast_to(scale, squares.shape)
+
+    return call(body, shaped((own.shape[0], 128), F32), (own, arrived), [VMEM] * 2)
 
 
 def add_keyvals(own, arrived):
@@ -487,8 +520,10 @@
 
     def body(where_ref, anc_ref, rope_ref, scale_ref, *refs):
         q_refs, refs = refs[: len(queries)], refs[len(queries) :]
-        near_refs, far_refs = refs[:tensor], refs[tensor : 2 * tensor]
-        query_ref, mixed_ref, highest_ref, total_ref, keys_ref, values_ref = refs[2 * tensor :]
+        count = tensor // 2 + 1
+        near_refs, far_refs = refs[:count], refs[count : 2 * count]
+        near_refs, far_refs = [(*part[:-1], *[part[-1].at[i] for i in range(count - 1)]) for part in (near_refs, far_refs)]
+        query_ref, mixed_ref, highest_ref, total_ref, keys_ref, values_ref = refs[2 * count :]
         d, t = where_ref[0], where_ref[1]
         query_sum = q_refs[0][...]
         for ref in q_refs[1:]:
@@ -559,7 +594,7 @@
     )
 
 
-def attend_new(where, rope, targets, pieces, state, shape, part_dev):
+def attend_new(where, rope, targets, scale, pieces, state, shape, part_dev):
     groups = lax.axis_size("dp")
     tensor = lax.axis_size("tensor")
     near = groups // tensor
@@ -568,9 +603,14 @@
     heads = shape[1] // HD
     rows = heads * parts
 
-    def body(where_ref, rope_ref, target_ref, one_ref, two_ref, query_ref, mixed_ref, highest_ref, total_ref, out_ref):
+    def body(where_ref, rope_ref, target_ref, scale_ref, *refs):
+        piece_refs, (query_ref, mixed_ref, highest_ref, total_ref, out_ref) = refs[: len(pieces)], refs[len(pieces) :]
         even = where_ref[0] % 2 == 0 if groups == KVH else True
-        one, two = one_ref[...].astype(F32), two_ref[...].astype(F32)
+        if len(pieces) == 2:
+            one, two = [ref[...].astype(F32) for ref in piece_refs]
+        else:
+            one, two = [piece_refs[i][...].astype(F32) + piece_refs[i + 1][...].astype(F32) for i in (0, 2)]
+            one, two = [(x * scale_ref[...]).astype(BF16).astype(F32) for x in (one, two)]
         plain = jnp.where(even, one, two)
         values = jnp.where(even, two, one).astype(BF16)
         cosine = jnp.concatenate([jnp.broadcast_to(rope_ref[2 * s : 2 * s + 1, :], (part_dev, HD)) for s in range(2)])
@@ -597,8 +637,21 @@
                 here = slice(b * pair, (b + 1) * pair)
                 out_ref[here, h * HD : (h + 1) * HD] = jnp.concatenate(both, axis=0).astype(BF16)
 
-    ins = (where, rope, targets, *pieces, *state)
+    ins = (where, rope, targets, scale, *pieces, *state)
     return call(body, shaped(shape), ins, [SMEM] + [VMEM] * (len(ins) - 1), moved=1 << 20)
+
+
+def send_keyvals(pieces):
+    groups = lax.axis_size("dp")
+    tensor = lax.axis_size("tensor")
+    half = groups // 2
+    moved = []
+    for flip, piece in enumerate(pieces):
+        to = [2 * i + flip for i in range(half)] + [2 * i + 1 - flip for i in range(half)]
+        for k in (0, 2):
+            pairs = [(i * tensor + t, to[i] * tensor + (t ^ k)) for i in range(groups) for t in range(tensor)]
+            moved.append(lax.ppermute(piece, ("dp", "tensor"), pairs))
+    return moved
 
 
 def move_keyvals(pieces):
@@ -647,22 +700,31 @@
     blocks = gather_rows(x, near_pieces if joined else None)
     close = min(groups, 4)
     near_moved = blocks[1:close] if joined else [swap(piece, "dp", k) for k, piece in enumerate(near_pieces, 1)]
-    near_cache = gather_blocks(collect_near(own_piece, near_moved, span))
+    near_pieces = collect_near(own_piece, near_moved, span)
     packed = pack_far(where, cache_keys, cache_values, blocks[close::2])
     far_pieces = [swap(piece, "dp", close + 2 * i) for i, piece in enumerate(packed)]
 
     message, keep = project_attention(where, blocks, attn_gain, w_keyval, w_query, x)
-    queries, message, *leaving = add_cores(message, keep, swap(message, "tensor", 1))
+    queries, message, *leaving = add_cores(where, message, keep, swap(message, "tensor", 1))
     passed = swap(last_entries(far_pieces, x), "dp", 1)
-    far_cache = gather_blocks(collect_far(far_pieces, passed))
-    bits = 2
-    while 2 * bits < tensor:
-        message = add_keyvals(message, swap(message, "tensor", bits))
-        bits *= 2
-    arrived = swap(message, "tensor", bits)
-    scale, *pieces = finish_keyvals(where, message, arrived, w_keyval.shape[1], width)
-    pieces = move_keyvals(pieces)
-    queries = [queries] + ([swap(x, "tensor", 2 * i) for i, x in enumerate(leaving, 1)] if leaving else [arrived])
+    far_pieces = collect_far(far_pieces, passed)
+    if direct_keyvals():
+        pieces = send_keyvals(leaving)
+        arrived = swap(message, "tensor", 2)
+        scale = row_scale(message, arrived, width)
+        queries = [queries, arrived]
+    else:
+        bits = 2
+        while 2 * bits < tensor:
+            message = add_keyvals(message, swap(message, "tensor", bits))
+            bits *= 2
+        arrived = swap(message, "tensor", bits)
+        scale, *pieces = finish_keyvals(where, message, arrived, w_keyval.shape[1], width)
+        pieces = move_keyvals(pieces)
+        queries = [queries] + [swap(piece, "tensor", 2 * i) for i, piece in enumerate(leaving, 1)]
+
+    near_cache = gather_cache(near_pieces, arrived)
+    far_cache = gather_cache(far_pieces, arrived)
 
     own = t * parts + jnp.arange(parts, dtype=jnp.int32)
     anc = lax.dynamic_slice_in_dim(ancestors, t * parts, parts).astype(jnp.int32)
@@ -676,7 +738,7 @@
     targets = jnp.concatenate([jnp.tile(first, (heads, 1)), jnp.tile(second, (heads, 1))]).astype(jnp.int32)
     rope = jnp.asarray(np.stack(rope_tables(context) + rope_tables(context + 1)))
     state = attend_cached(where, anc, rope, scale, queries, near_cache, far_cache, part_dev)
-    mixed = attend_new(where, rope, targets, pieces, state, queries[0].shape, part_dev)
+    mixed = attend_new(where, rope, targets, scale, pieces, state, queries[0].shape, part_dev)
 
     parts = project_back(where, gather_blocks(mixed), w_out)
     attn_part, residual = finish(*sum_rows(parts, pair), x)

time: 112 us -> 112 us (level)
  starting transfers between devices: 59.3 us -> 65.3 us
  waiting for transfers between devices: 34.4 us -> 28.7 us
    ppermute x49 -> x47, waiting for transfers between devices: 33 us -> 28.7 us  [swap(): return lax.ppermute(x, axis, [(i, i ^ bits) for i in range(size)])]
    ppermute x2 -> x4, starting transfers between devices: 1.19 us -> 5.32 us  [send_keyvals(): moved.append(lax.ppermute(piece, ('dp', 'tensor'), pairs))]
    ppermute x49 -> x47, starting transfers between devices: 58.1 us -> 60 us  [swap(): return lax.ppermute(x, axis, [(i, i ^ bits) for i in range(size)])]
    ppermute x2 -> x4, waiting for transfers between devices: 1.48 us -> 0.01 us  [send_keyvals(): moved.append(lax.ppermute(piece, ('dp', 'tensor'), pairs))]
    pallas_call x21 -> x23, Pallas kernels: 14.5 us -> 14.5 us  [call(): pl.pallas_call(body, out_shape=outs, in_specs=specs, out_specs=jax.tree.m...]
  transfers between devices with their start and end apart: 51 -> 51, of which waited for: 22 -> 21; matrix products, arithmetic and copies ran while one was open for 1% -> 1% of each run, Pallas kernels for 6% -> 6%
where the time goes in v13:
time: 112 us
  starting transfers between devices  65.3 us (58%)
  waiting for transfers between devices  28.7 us (26%)
  Pallas kernels  14.5 us (13%)
  local copies, waits for them, and re-layouts  1.97 us (2%)
    ppermute x47, starting transfers between devices, swap(): return lax.ppermute(x, axis, [(i, i ^ bits) for i in range(size)])  60 us
    ppermute x47, waiting for transfers between devices, swap(): return lax.ppermute(x, axis, [(i, i ^ bits) for i in range(size)])  28.7 us
    pallas_call x23, Pallas kernels, call(): pl.pallas_call(body, out_shape=outs, in_specs=specs, out_specs=jax.tree.m...  14.5 us
    ppermute x4, starting transfers between devices, send_keyvals(): moved.append(lax.ppermute(piece, ('dp', 'tensor'), pairs))  5.32 us
  transfers between devices with their start and end apart: 51, of which 21 were waited for; matrix products, arithmetic and copies ran while one was open for 1% of the time, Pallas kernels for 6%

profile of v13, /device:TPU:0, one launch (start us, length us, event | category | flops | bytes accessed | tf_op | source)
XLA Modules:
  0.0 112.2 jit_solution(5302695886737070555)
XLA Ops:
  0.7 0.8 copy-done.5
  1.5 0.8 copy-done.6
  2.2 4.0 %collective-permute-start.3 = (bf16[16,2048]{1,0:T(8,128)(2,1)S(1)}, bf16[16,2048]{1,0:T(8,128)(2,1)S(1)}, u32[]{:S(2)}, u32[]{:S(2)}) collective-permute-start(bf16[16,2048]{1,0:T(8,128)(2,1)S(1)} %shard_map.149.x_ref.refs_0_.refs_10_.after_ref.refs_5_), channel_id=1, source_target_pairs={{0,16},{4,20},{8,24},{12,28},{16,0},{20,4},{24,8},{28,12},{1,17},{... | collective-permute-start | bytes 196616 | tf_op jit(solution)/shard_map/ppermute | solution.py:24
  6.3 1.3 %collective-permute-start.5 = (bf16[16,2048]{1,0:T(8,128)(2,1)S(1)}, bf16[16,2048]{1,0:T(8,128)(2,1)S(1)}, u32[]{:S(2)}, u32[]{:S(2)}) collective-permute-start(bf16[16,2048]{1,0:T(8,128)(2,1)S(1)} %shard_map.149.x_ref.refs_0_.refs_10_.after_ref.refs_5_), channel_id=1, source_target_pairs={{0,24},{4,28},{8,16},{12,20},{16,8},{20,12},{24,0},{28,4},{1,25},{... | collective-permute-start | bytes 196616 | tf_op jit(solution)/shard_map/ppermute | solution.py:24
  7.7 0.6 shard_map.150
  8.3 1.6 %collective-permute-start = (bf16[24,2048]{1,0:T(8,128)(2,1)S(1)}, bf16[24,2048]{1,0:T(8,128)(2,1)S(1)}, u32[]{:S(2)}, u32[]{:S(2)}) collective-permute-start(bf16[24,2048]{1,0:T(8,128)(2,1)S(1)} %get-tuple-element.45), channel_id=1, source_target_pairs={{0,4},{4,0},{8,12},{12,8},{16,20},{20,16},{24,28},{28,24},{1,5},{5... | collective-permute-start | bytes 294920 | tf_op jit(solution)/shard_map/ppermute | solution.py:24
  10.1 1.8 %collective-permute-start.2 = (bf16[24,2048]{1,0:T(8,128)(2,1)S(1)}, bf16[24,2048]{1,0:T(8,128)(2,1)S(1)}, u32[]{:S(2)}, u32[]{:S(2)}) collective-permute-start(bf16[24,2048]{1,0:T(8,128)(2,1)S(1)} %get-tuple-element.47), channel_id=1, source_target_pairs={{0,12},{4,8},{8,4},{12,0},{16,28},{20,24},{24,20},{28,16},{1,13},{... | collective-permute-start | bytes 294920 | tf_op jit(solution)/shard_map/ppermute | solution.py:24
  13.1 2.8 %collective-permute-start.15 = (bf16[2,8,2048]{2,1,0:T(8,128)(2,1)S(1)}, bf16[2,8,2048]{2,1,0:T(8,128)(2,1)S(1)}, u32[]{:S(2)}, u32[]{:S(2)}) collective-permute-start(bf16[2,8,2048]{2,1,0:T(8,128)(2,1)S(1)} %get-tuple-element.55), channel_id=1, source_target_pairs={{0,16},{4,20},{8,24},{12,28},{16,0},{20,4},{24,8},{28,12},{1,17},{... | collective-permute-start | bytes 196616 | tf_op jit(solution)/shard_map/ppermute | solution.py:24
  16.3 1.6 %collective-permute-start.4 = (bf16[16,2048]{1,0:T(8,128)(2,1)S(1)}, bf16[16,2048]{1,0:T(8,128)(2,1)S(1)}, u32[]{:S(2)}, u32[]{:S(2)}) collective-permute-start(bf16[16,2048]{1,0:T(8,128)(2,1)S(1)} %collective-permute-done.3.refs_4_.refs_0_), channel_id=1, source_target_pairs={{0,4},{4,0},{8,12},{12,8},{16,20},{20,16},{24,28},{28,24},{1,5},{5... | collective-permute-start | bytes 196616 | tf_op jit(solution)/shard_map/ppermute | solution.py:24
  18.4 1.8 %collective-permute-start.13 = (bf16[4,8,2048]{2,1,0:T(8,128)(2,1)S(1)}, bf16[4,8,2048]{2,1,0:T(8,128)(2,1)S(1)}, u32[]{:S(2)}, u32[]{:S(2)}) collective-permute-start(bf16[4,8,2048]{2,1,0:T(8,128)(2,1)S(1)} %shard_map.154.refs_0_.refs_2_), channel_id=1, source_target_pairs={{0,2},{1,3},{2,0},{3,1},{4,6},{5,7},{6,4},{7,5},{8,10},{9,11},{10,... | collective-permute-start | bytes 393224 | tf_op jit(solution)/shard_map/ppermute | solution.py:24
  20.2 1.8 %collective-permute-done.16.refs_1_ = bf16[2,8,2048]{2,1,0:T(8,128)(2,1)S(1)} collective-permute-done((bf16[2,8,2048]{2,1,0:T(8,128)(2,1)S(1)}, bf16[2,8,2048]{2,1,0:T(8,128)(2,1)S(1)}, u32[]{:S(2)}, u32[]{:S(2)}) %collective-permute-start.16) | collective-permute-done | bytes 65568 | tf_op jit(solution)/shard_map/ppermute | solution.py:24
  22.0 1.5 %collective-permute-start.17 = (bf16[2,8,2048]{2,1,0:T(8,128)(2,1)S(1)}, bf16[2,8,2048]{2,1,0:T(8,128)(2,1)S(1)}, u32[]{:S(2)}, u32[]{:S(2)}) collective-permute-start(bf16[2,8,2048]{2,1,0:T(8,128)(2,1)S(1)} %shard_map.157), channel_id=1, source_target_pairs={{0,4},{4,0},{8,12},{12,8},{16,20},{20,16},{24,28},{28,24},{1,5},{5... | collective-permute-start | bytes 196616 | tf_op jit(solution)/shard_map/ppermute | solution.py:24
  23.6 1.5 %shard_map.151 = (bf16[128,896]{1,0:T(8,128)(2,1)S(1)}, f32[64,1024]{1,0:T(8,128)S(1)}) custom-call(s32[2]{0:T(128)S(1)} %pad_add_fusion.3.where_ref, f32[1,2048]{1,0:T(1,128)S(1)} %bitcast.18, bf16[16,2048]{1,0:T(8,128)(2,1)S(1)} %shard_map.149.x_ref.refs_0_.refs_10_.after_ref.refs_5_, bf16[24,2048]{1,0:T(8,128)(2,1)S(1)} %collective-permute-done.refs_1_.refs_0_, ...), custom_call_target="tpu_custom_call" | custom-call | flops 6039797760 | bytes 6291456 | tf_op jit(solution)/shard_map/pallas_call | solution.py:45
  25.2 1.1 collective-permute-done.17.refs_2_
  26.3 1.6 %collective-permute-start.18 = (bf16[4,8,2048]{2,1,0:T(8,128)(2,1)S(1)}, bf16[4,8,2048]{2,1,0:T(8,128)(2,1)S(1)}, u32[]{:S(2)}, u32[]{:S(2)}) collective-permute-start(bf16[4,8,2048]{2,1,0:T(8,128)(2,1)S(1)} %shard_map.158.refs_0_.refs_5_), channel_id=1, source_target_pairs={{0,2},{1,3},{2,0},{3,1},{4,6},{5,7},{6,4},{7,5},{8,10},{9,11},{10,... | collective-permute-start | bytes 393224 | tf_op jit(solution)/shard_map/ppermute | solution.py:24
  27.9 0.7 shard_map.152
  29.3 1.6 %collective-permute-start.11 = (bf16[128,128]{1,0:T(8,128)(2,1)S(1)}, bf16[128,128]{1,0:T(8,128)(2,1)S(1)}, u32[]{:S(2)}, u32[]{:S(2)}) collective-permute-start(bf16[128,128]{1,0:T(8,128)(2,1)S(1)} %get-tuple-element.52), channel_id=1, source_target_pairs={{0,4},{1,5},{2,6},{3,7},{4,12},{5,13},{6,14},{7,15},{8,20},{9,21},... | collective-permute-start | bytes 98312 | tf_op jit(solution)/shard_map/ppermute | solution.py:653
  30.9 1.5 %collective-permute-start.12 = (bf16[128,128]{1,0:T(8,128)(2,1)S(1)}, bf16[128,128]{1,0:T(8,128)(2,1)S(1)}, u32[]{:S(2)}, u32[]{:S(2)}) collective-permute-start(bf16[128,128]{1,0:T(8,128)(2,1)S(1)} %get-tuple-element.52), channel_id=1, source_target_pairs={{0,6},{1,7},{2,4},{3,5},{4,14},{5,15},{6,12},{7,13},{8,22},{9,23},... | collective-permute-start | bytes 98312 | tf_op jit(solution)/shard_map/ppermute | solution.py:653
  32.5 1.5 %collective-permute-start.10 = (bf16[128,128]{1,0:T(8,128)(2,1)S(1)}, bf16[128,128]{1,0:T(8,128)(2,1)S(1)}, u32[]{:S(2)}, u32[]{:S(2)}) collective-permute-start(bf16[128,128]{1,0:T(8,128)(2,1)S(1)} %get-tuple-element.51), channel_id=1, source_target_pairs={{0,2},{1,3},{2,0},{3,1},{4,10},{5,11},{6,8},{7,9},{8,18},{9,19},{1... | collective-permute-start | bytes 98312 | tf_op jit(solution)/shard_map/ppermute | solution.py:653
  35.0 0.8 collective-permute-done.19.refs_7_
  35.8 0.7 collective-permute-start.9
  36.5 2.4 %shard_map.160 = (bf16[256,128]{1,0:T(8,128)(2,1)S(1)}, f32[256,128]{1,0:T(8,128)S(1)}, f32[256,128]{1,0:T(8,128)S(1)}, f32[256,128]{1,0:T(8,128)S(1)}) custom-call(s32[2]{0:T(128)S(1)} %pad_add_fusion.3.where_ref, s32[16]{0:T(128)S(1)} %get-tuple-element.89.anc_ref, f32[4,128]{1,0:T(4,128)S(1)} %copy-done.9, f32[128,128]{1,0:T(8,128)S(1)} %shard_map.153.scale_ref, ...), custom_call_target="tpu_custom_call" | custom-call | flops 5368709120 | bytes 4194304 | tf_op jit(solution)/shard_map/pallas_call | solution.py:45
  38.9 1.1 %shard_map.161.refs_0_ = bf16[32,1024]{1,0:T(8,128)(2,1)S(1)} custom-call(s32[2]{0:T(128)S(1)} %pad_add_fusion.3.where_ref, f32[4,128]{1,0:T(4,128)S(1)} %copy-done.9, s32[256,2]{1,0:T(8,128)S(1)} %copy.20.target_ref, f32[128,128]{1,0:T(8,128)S(1)} %shard_map.153.scale_ref, bf16[128,128]{1,0:T(8,128)(2,1)S(1)} %collective-permute-done.9.refs_0_, ...), custom_call_target="tpu_custom_call" | custom-call | flops 5368709120 | bytes 1048576 | tf_op jit(solution)/shard_map/pallas_call | solution.py:45
  40.0 1.6 %collective-permute-start.21 = (bf16[32,1024]{1,0:T(8,128)(2,1)S(1)}, bf16[32,1024]{1,0:T(8,128)(2,1)S(1)}, u32[]{:S(2)}, u32[]{:S(2)}) collective-permute-start(bf16[32,1024]{1,0:T(8,128)(2,1)S(1)} %shard_map.161.refs_0_), channel_id=1, source_target_pairs={{0,2},{1,3},{2,0},{3,1},{4,6},{5,7},{6,4},{7,5},{8,10},{9,11},{10,... | collective-permute-start | bytes 196616 | tf_op jit(solution)/shard_map/ppermute | solution.py:24
  41.6 2.7 %collective-permute-done.21.refs_2_ = bf16[32,1024]{1,0:T(8,128)(2,1)S(1)} collective-permute-done((bf16[32,1024]{1,0:T(8,128)(2,1)S(1)}, bf16[32,1024]{1,0:T(8,128)(2,1)S(1)}, u32[]{:S(2)}, u32[]{:S(2)}) %collective-permute-start.21) | collective-permute-done | bytes 65568 | tf_op jit(solution)/shard_map/ppermute | solution.py:24
  44.4 1.2 %collective-permute-done.22.refs_3_ = bf16[32,1024]{1,0:T(8,128)(2,1)S(1)} collective-permute-done((bf16[32,1024]{1,0:T(8,128)(2,1)S(1)}, bf16[32,1024]{1,0:T(8,128)(2,1)S(1)}, u32[]{:S(2)}, u32[]{:S(2)}) %collective-permute-start.22) | collective-permute-done | bytes 65568 | tf_op jit(solution)/shard_map/ppermute | solution.py:24
  45.6 1.3 %shard_map.162 = (f32[16,2048]{1,0:T(8,128)S(1)}, bf16[16,2048]{1,0:T(8,128)(2,1)S(1)}, bf16[16,2048]{1,0:T(8,128)(2,1)S(1)}, bf16[16,2048]{1,0:T(8,128)(2,1)S(1...) custom-call(s32[2]{0:T(128)S(1)} %pad_add_fusion.3.where_ref, ...), custom_call_target="tpu_custom_call" | custom-call | flops 5905580032 | bytes 4194304 | tf_op jit(solution)/shard_map/pallas_call | solution.py:45
  46.9 5.8 %collective-permute-start.25 = (bf16[16,2048]{1,0:T(8,128)(2,1)S(1)}, bf16[16,2048]{1,0:T(8,128)(2,1)S(1)}, u32[]{:S(2)}, u32[]{:S(2)}) collective-permute-start(bf16[16,2048]{1,0:T(8,128)(2,1)S(1)} %get-tuple-element.67), channel_id=1, source_target_pairs={{0,4},{4,0},{8,12},{12,8},{16,20},{20,16},{24,28},{28,24},{1,5},{5... | collective-permute-start | bytes 196616 | tf_op jit(solution)/shard_map/ppermute | solution.py:24
  52.8 1.7 %collective-permute-start.29 = (bf16[16,2048]{1,0:T(8,128)(2,1)S(1)}, bf16[16,2048]{1,0:T(8,128)(2,1)S(1)}, u32[]{:S(2)}, u32[]{:S(2)}) collective-permute-start(bf16[16,2048]{1,0:T(8,128)(2,1)S(1)} %get-tuple-element.70), channel_id=1, source_target_pairs={{0,12},{4,8},{8,4},{12,0},{16,28},{20,24},{24,20},{28,16},{1,13},{... | collective-permute-start | bytes 196616 | tf_op jit(solution)/shard_map/ppermute | solution.py:24
  54.5 0.6 collective-permute-done.25.arrived_ref
  55.1 4.0 %collective-permute-start.26 = (bf16[16,2048]{1,0:T(8,128)(2,1)S(1)}, bf16[16,2048]{1,0:T(8,128)(2,1)S(1)}, u32[]{:S(2)}, u32[]{:S(2)}) collective-permute-start(bf16[16,2048]{1,0:T(8,128)(2,1)S(1)} %shard_map.164), channel_id=1, source_target_pairs={{0,24},{4,28},{8,16},{12,20},{16,8},{20,12},{24,0},{28,4},{1,25},{... | collective-permute-start | bytes 196616 | tf_op jit(solution)/shard_map/ppermute | solution.py:24
  59.5 2.9 %collective-permute-start.28 = (bf16[16,2048]{1,0:T(8,128)(2,1)S(1)}, bf16[16,2048]{1,0:T(8,128)(2,1)S(1)}, u32[]{:S(2)}, u32[]{:S(2)}) collective-permute-start(bf16[16,2048]{1,0:T(8,128)(2,1)S(1)} %get-tuple-element.69), channel_id=1, source_target_pairs={{0,8},{4,12},{8,0},{12,4},{16,24},{20,28},{24,16},{28,20},{1,9},{5... | collective-permute-start | bytes 196616 | tf_op jit(solution)/shard_map/ppermute | solution.py:24
  62.5 2.0 %collective-permute-done.24.refs_0_ = bf16[16,2048]{1,0:T(8,128)(2,1)S(1)} collective-permute-done((bf16[16,2048]{1,0:T(8,128)(2,1)S(1)}, bf16[16,2048]{1,0:T(8,128)(2,1)S(1)}, u32[]{:S(2)}, u32[]{:S(2)}) %collective-permute-start.24) | collective-permute-done | bytes 65568 | tf_op jit(solution)/shard_map/ppermute | solution.py:24
  64.5 0.7 collective-permute-done.28.refs_3_
  65.2 0.7 shard_map.165
  65.8 1.3 %collective-permute-start.33 = (bf16[16,2048]{1,0:T(8,128)(2,1)S(1)}, bf16[16,2048]{1,0:T(8,128)(2,1)S(1)}, u32[]{:S(2)}, u32[]{:S(2)}) collective-permute-start(bf16[16,2048]{1,0:T(8,128)(2,1)S(1)} %get-tuple-element.72.refs_0_), channel_id=1, source_target_pairs={{0,16},{4,20},{8,24},{12,28},{16,0},{20,4},{24,8},{28,12},{1,17},{... | collective-permute-start | bytes 196616 | tf_op jit(solution)/shard_map/ppermute | solution.py:24
  67.2 2.6 %collective-permute-start.35 = (bf16[16,2048]{1,0:T(8,128)(2,1)S(1)}, bf16[16,2048]{1,0:T(8,128)(2,1)S(1)}, u32[]{:S(2)}, u32[]{:S(2)}) collective-permute-start(bf16[16,2048]{1,0:T(8,128)(2,1)S(1)} %get-tuple-element.72.refs_0_), channel_id=1, source_target_pairs={{0,24},{4,28},{8,16},{12,20},{16,8},{20,12},{24,0},{28,4},{1,25},{... | collective-permute-start | bytes 196616 | tf_op jit(solution)/shard_map/ppermute | solution.py:24
  69.8 0.7 collective-permute-start.30
  70.5 2.8 %collective-permute-start.32 = (bf16[16,2048]{1,0:T(8,128)(2,1)S(1)}, bf16[16,2048]{1,0:T(8,128)(2,1)S(1)}, u32[]{:S(2)}, u32[]{:S(2)}) collective-permute-start(bf16[16,2048]{1,0:T(8,128)(2,1)S(1)} %get-tuple-element.72.refs_0_), channel_id=1, source_target_pairs={{0,12},{4,8},{8,4},{12,0},{16,28},{20,24},{24,20},{28,16},{1,13},{... | collective-permute-start | bytes 196616 | tf_op jit(solution)/shard_map/ppermute | solution.py:24
  73.3 0.7 collective-permute-start.34
  74.0 1.3 %collective-permute-start.36 = (bf16[16,2048]{1,0:T(8,128)(2,1)S(1)}, bf16[16,2048]{1,0:T(8,128)(2,1)S(1)}, u32[]{:S(2)}, u32[]{:S(2)}) collective-permute-start(bf16[16,2048]{1,0:T(8,128)(2,1)S(1)} %collective-permute-done.35.refs_6_), channel_id=1, source_target_pairs={{0,4},{4,0},{8,12},{12,8},{16,20},{20,16},{24,28},{28,24},{1,5},{5... | collective-permute-start | bytes 196616 | tf_op jit(solution)/shard_map/ppermute | solution.py:24
  75.3 0.9 collective-permute-done.32.refs_3_
  76.2 1.3 %collective-permute-done.34.refs_5_ = bf16[16,2048]{1,0:T(8,128)(2,1)S(1)} collective-permute-done((bf16[16,2048]{1,0:T(8,128)(2,1)S(1)}, bf16[16,2048]{1,0:T(8,128)(2,1)S(1)}, u32[]{:S(2)}, u32[]{:S(2)}) %collective-permute-start.34) | collective-permute-done | bytes 65568 | tf_op jit(solution)/shard_map/ppermute | solution.py:24
  77.6 0.7 collective-permute-done.36.refs_7_
  78.3 1.8 %shard_map.166 = (bf16[128,2048]{1,0:T(8,128)(2,1)S(1)}, f32[64,1920]{1,0:T(8,128)S(1)}, bf16[64,1920]{1,0:T(8,128)(2,1)S(1)}) custom-call(s32[2]{0:T(128)S(1)} %pad_add_fusion.3.where_ref, f32[1,2048]{1,0:T(1,128)S(1)} %bitcast.19, bf16[16,2048]{1,0:T(8,128)(2,1)S(1)} %get-tuple-element.72.refs_0_, bf16[16,2048]{1,0:T(8,128)(2,1)S(1)} %collective-permute-done.30.refs_1_, ...), custom_call_target="tpu_custom_call" | custom-call | flops 6308233216 | bytes 8388608 | tf_op jit(solution)/shard_map/pallas_call | solution.py:45
  80.3 1.1 %shard_map.167 = (f32[64,1792]{1,0:T(8,128)S(1)}, bf16[64,1792]{1,0:T(8,128)(2,1)S(1)}) custom-call(bf16[128,2048]{1,0:T(8,128)(2,1)S(1)} %get-tuple-element.75.h_ref, bf16[2048,1792]{1,0:T(8,128)(2,1)S(1)} %bitcast.15), custom_call_target="tpu_custom_call" | custom-call | flops 6308233216 | bytes 7340032 | tf_op jit(solution)/shard_map/pallas_call | solution.py:45
  82.0 1.6 %collective-permute-start.38 = (bf16[32,1920]{1,0:T(8,128)(2,1)S(1)}, bf16[32,1920]{1,0:T(8,128)(2,1)S(1)}, u32[]{:S(2)}, u32[]{:S(2)}) collective-permute-start(bf16[32,1920]{1,0:T(8,128)(2,1)S(1)} %slice.64), channel_id=1, source_target_pairs={{0,2},{1,3},{2,0},{3,1},{4,6},{5,7},{6,4},{7,5},{8,10},{9,11},{10,... | collective-permute-start | bytes 368648 | tf_op jit(solution)/shard_map/ppermute | solution.py:24
  83.6 1.0 collective-permute-start.40
  84.7 3.6 %collective-permute-done.38 = bf16[32,1920]{1,0:T(8,128)(2,1)S(1)} collective-permute-done((bf16[32,1920]{1,0:T(8,128)(2,1)S(1)}, bf16[32,1920]{1,0:T(8,128)(2,1)S(1)}, u32[]{:S(2)}, u32[]{:S(2)}) %collective-permute-start.38) | collective-permute-done | bytes 122912 | tf_op jit(solution)/shard_map/ppermute | solution.py:24
  88.5 1.3 %collective-permute-done.40 = bf16[32,1792]{1,0:T(8,128)(2,1)S(1)} collective-permute-done((bf16[32,1792]{1,0:T(8,128)(2,1)S(1)}, bf16[32,1792]{1,0:T(8,128)(2,1)S(1)}, u32[]{:S(2)}, u32[]{:S(2)}) %collective-permute-start.40) | collective-permute-done | bytes 114720 | tf_op jit(solution)/shard_map/ppermute | solution.py:24
  90.0 1.5 %collective-permute-start.42 = (bf16[32,1792]{1,0:T(8,128)(2,1)S(1)}, bf16[32,1792]{1,0:T(8,128)(2,1)S(1)}, u32[]{:S(2)}, u32[]{:S(2)}) collective-permute-start(bf16[32,1792]{1,0:T(8,128)(2,1)S(1)} %fusion.2.refs_0_), channel_id=1, source_target_pairs={{0,2},{1,3},{2,0},{3,1},{4,6},{5,7},{6,4},{7,5},{8,10},{9,11},{10,... | collective-permute-start | bytes 344072 | tf_op jit(solution)/shard_map/ppermute | solution.py:24
  91.5 3.3 %collective-permute-done.42.refs_2_ = bf16[32,1792]{1,0:T(8,128)(2,1)S(1)} collective-permute-done((bf16[32,1792]{1,0:T(8,128)(2,1)S(1)}, bf16[32,1792]{1,0:T(8,128)(2,1)S(1)}, u32[]{:S(2)}, u32[]{:S(2)}) %collective-permute-start.42) | collective-permute-done | bytes 114720 | tf_op jit(solution)/shard_map/ppermute | solution.py:24
  94.8 1.3 %collective-permute-done.43.refs_3_ = bf16[32,1792]{1,0:T(8,128)(2,1)S(1)} collective-permute-done((bf16[32,1792]{1,0:T(8,128)(2,1)S(1)}, bf16[32,1792]{1,0:T(8,128)(2,1)S(1)}, u32[]{:S(2)}, u32[]{:S(2)}) %collective-permute-start.43) | collective-permute-done | bytes 114720 | tf_op jit(solution)/shard_map/ppermute | solution.py:24
  96.1 1.7 %shard_map.168 = (f32[16,2048]{1,0:T(8,128)S(1)}, bf16[16,2048]{1,0:T(8,128)(2,1)S(1)}, bf16[16,2048]{1,0:T(8,128)(2,1)S(1)}, bf16[16,2048]{1,0:T(8,128)(2,1)S(1...) custom-call(s32[2]{0:T(128)S(1)} %pad_add_fusion.3.where_ref, ...), custom_call_target="tpu_custom_call" | custom-call | flops 6308233216 | bytes 7340032 | tf_op jit(solution)/shard_map/pallas_call | solution.py:45
  97.9 1.4 %collective-permute-start.46 = (bf16[16,2048]{1,0:T(8,128)(2,1)S(1)}, bf16[16,2048]{1,0:T(8,128)(2,1)S(1)}, u32[]{:S(2)}, u32[]{:S(2)}) collective-permute-start(bf16[16,2048]{1,0:T(8,128)(2,1)S(1)} %get-tuple-element.84), channel_id=1, source_target_pairs={{0,4},{4,0},{8,12},{12,8},{16,20},{20,16},{24,28},{28,24},{1,5},{5... | collective-permute-start | bytes 196616 | tf_op jit(solution)/shard_map/ppermute | solution.py:24
  99.2 0.7 collective-permute-start.44
  100.0 0.9 collective-permute-start.50
  100.8 1.8 %collective-permute-done.46.arrived_ref = bf16[16,2048]{1,0:T(8,128)(2,1)S(1)} collective-permute-done((bf16[16,2048]{1,0:T(8,128)(2,1)S(1)}, bf16[16,2048]{1,0:T(8,128)(2,1)S(1)}, u32[]{:S(2)}, u32[]{:S(2)}) %collective-permute-start.46) | collective-permute-done | bytes 65568 | tf_op jit(solution)/shard_map/ppermute | solution.py:24
  102.7 2.7 %collective-permute-start.47 = (bf16[16,2048]{1,0:T(8,128)(2,1)S(1)}, bf16[16,2048]{1,0:T(8,128)(2,1)S(1)}, u32[]{:S(2)}, u32[]{:S(2)}) collective-permute-start(bf16[16,2048]{1,0:T(8,128)(2,1)S(1)} %shard_map.170), channel_id=1, source_target_pairs={{0,24},{4,28},{8,16},{12,20},{16,8},{20,12},{24,0},{28,4},{1,25},{... | collective-permute-start | bytes 196616 | tf_op jit(solution)/shard_map/ppermute | solution.py:24
  105.5 0.8 collective-permute-start.48
  106.3 2.4 %collective-permute-start.49 = (bf16[16,2048]{1,0:T(8,128)(2,1)S(1)}, bf16[16,2048]{1,0:T(8,128)(2,1)S(1)}, u32[]{:S(2)}, u32[]{:S(2)}) collective-permute-start(bf16[16,2048]{1,0:T(8,128)(2,1)S(1)} %get-tuple-element.86), channel_id=1, source_target_pairs={{0,8},{4,12},{8,0},{12,4},{16,24},{20,28},{24,16},{28,20},{1,9},{5... | collective-permute-start | bytes 196616 | tf_op jit(solution)/shard_map/ppermute | solution.py:24
  109.0 1.9 %collective-permute-done.45.refs_0_ = bf16[16,2048]{1,0:T(8,128)(2,1)S(1)} collective-permute-done((bf16[16,2048]{1,0:T(8,128)(2,1)S(1)}, bf16[16,2048]{1,0:T(8,128)(2,1)S(1)}, u32[]{:S(2)}, u32[]{:S(2)}) %collective-permute-start.45) | collective-permute-done | bytes 65568 | tf_op jit(solution)/shard_map/ppermute | solution.py:24
  110.9 0.6 collective-permute-done.49.refs_3_
  111.5 0.7 shard_map.171
  (116 shorter events, 6.4 us)
Async XLA Ops:
  0.6 7.0 %copy-start.3 = (bf16[8,8,1024]{2,1,0:T(8,128)(2,1)S(1)}, bf16[8,8,1024]{2,1,0:T(8,128)(2,1)}, u32[]{:S(2)}) copy-start(bf16[8,8,1024]{2,1,0:T(8,128)(2,1)} %keys_ref.3) | copy-start | bytes 393220
  0.6 7.0 %copy-start.4 = (bf16[8,8,1024]{2,1,0:T(8,128)(2,1)S(1)}, bf16[8,8,1024]{2,1,0:T(8,128)(2,1)}, u32[]{:S(2)}) copy-start(bf16[8,8,1024]{2,1,0:T(8,128)(2,1)} %values_ref.3) | copy-start | bytes 393220
  2.2 9.9 %collective-permute-start.3 = (bf16[16,2048]{1,0:T(8,128)(2,1)S(1)}, bf16[16,2048]{1,0:T(8,128)(2,1)S(1)}, u32[]{:S(2)}, u32[]{:S(2)}) collective-permute-start(bf16[16,2048]{1,0:T(8,128)(2,1)S(1)} %shard_map.149.x_ref.refs_0_.refs_10_.after_ref.refs_5_), channel_id=1, source_target_pairs={{0,16},{4,20},{8,24},{12,28},{16,0},{20,4},{24,8},{28,12},{1,17},{... | collective-permute-start | bytes 196616 | tf_op jit(solution)/shard_map/ppermute | solution.py:24
  6.3 6.2 %collective-permute-start.5 = (bf16[16,2048]{1,0:T(8,128)(2,1)S(1)}, bf16[16,2048]{1,0:T(8,128)(2,1)S(1)}, u32[]{:S(2)}, u32[]{:S(2)}) collective-permute-start(bf16[16,2048]{1,0:T(8,128)(2,1)S(1)} %shard_map.149.x_ref.refs_0_.refs_10_.after_ref.refs_5_), channel_id=1, source_target_pairs={{0,24},{4,28},{8,16},{12,20},{16,8},{20,12},{24,0},{28,4},{1,25},{... | collective-permute-start | bytes 196616 | tf_op jit(solution)/shard_map/ppermute | solution.py:24
  7.7 4.2 %copy-start.10 = (s32[64]{0:T(128)S(1)}, s32[64]{0:T(128)}, u32[]{:S(2)}) copy-start(s32[64]{0:T(128)} %param.18) | copy-start | bytes 772
  8.3 8.0 %collective-permute-start = (bf16[24,2048]{1,0:T(8,128)(2,1)S(1)}, bf16[24,2048]{1,0:T(8,128)(2,1)S(1)}, u32[]{:S(2)}, u32[]{:S(2)}) collective-permute-start(bf16[24,2048]{1,0:T(8,128)(2,1)S(1)} %get-tuple-element.45), channel_id=1, source_target_pairs={{0,4},{4,0},{8,12},{12,8},{16,20},{20,16},{24,28},{28,24},{1,5},{5... | collective-permute-start | bytes 294920 | tf_op jit(solution)/shard_map/ppermute | solution.py:24
  9.8 8.1 %collective-permute-start.1 = (bf16[24,2048]{1,0:T(8,128)(2,1)S(1)}, bf16[24,2048]{1,0:T(8,128)(2,1)S(1)}, u32[]{:S(2)}, u32[]{:S(2)}) collective-permute-start(bf16[24,2048]{1,0:T(8,128)(2,1)S(1)} %get-tuple-element.46), channel_id=1, source_target_pairs={{0,8},{4,12},{8,0},{12,4},{16,24},{20,28},{24,16},{28,20},{1,9},{5... | collective-permute-start | bytes 294920 | tf_op jit(solution)/shard_map/ppermute | solution.py:24
  10.1 8.3 %collective-permute-start.2 = (bf16[24,2048]{1,0:T(8,128)(2,1)S(1)}, bf16[24,2048]{1,0:T(8,128)(2,1)S(1)}, u32[]{:S(2)}, u32[]{:S(2)}) collective-permute-start(bf16[24,2048]{1,0:T(8,128)(2,1)S(1)} %get-tuple-element.47), channel_id=1, source_target_pairs={{0,12},{4,8},{8,4},{12,0},{16,28},{20,24},{24,20},{28,16},{1,13},{... | collective-permute-start | bytes 294920 | tf_op jit(solution)/shard_map/ppermute | solution.py:24
  13.1 7.1 %collective-permute-start.15 = (bf16[2,8,2048]{2,1,0:T(8,128)(2,1)S(1)}, bf16[2,8,2048]{2,1,0:T(8,128)(2,1)S(1)}, u32[]{:S(2)}, u32[]{:S(2)}) collective-permute-start(bf16[2,8,2048]{2,1,0:T(8,128)(2,1)S(1)} %get-tuple-element.55), channel_id=1, source_target_pairs={{0,16},{4,20},{8,24},{12,28},{16,0},{20,4},{24,8},{28,12},{1,17},{... | collective-permute-start | bytes 196616 | tf_op jit(solution)/shard_map/ppermute | solution.py:24
  15.9 6.2 %collective-permute-start.16 = (bf16[2,8,2048]{2,1,0:T(8,128)(2,1)S(1)}, bf16[2,8,2048]{2,1,0:T(8,128)(2,1)S(1)}, u32[]{:S(2)}, u32[]{:S(2)}) collective-permute-start(bf16[2,8,2048]{2,1,0:T(8,128)(2,1)S(1)} %get-tuple-element.56), channel_id=1, source_target_pairs={{0,24},{4,28},{8,16},{12,20},{16,8},{20,12},{24,0},{28,4},{1,25},{... | collective-permute-start | bytes 196616 | tf_op jit(solution)/shard_map/ppermute | solution.py:24
  16.3 7.3 %collective-permute-start.4 = (bf16[16,2048]{1,0:T(8,128)(2,1)S(1)}, bf16[16,2048]{1,0:T(8,128)(2,1)S(1)}, u32[]{:S(2)}, u32[]{:S(2)}) collective-permute-start(bf16[16,2048]{1,0:T(8,128)(2,1)S(1)} %collective-permute-done.3.refs_4_.refs_0_), channel_id=1, source_target_pairs={{0,4},{4,0},{8,12},{12,8},{16,20},{20,16},{24,28},{28,24},{1,5},{5... | collective-permute-start | bytes 196616 | tf_op jit(solution)/shard_map/ppermute | solution.py:24
  17.9 5.7 %collective-permute-start.6 = (bf16[16,2048]{1,0:T(8,128)(2,1)S(1)}, bf16[16,2048]{1,0:T(8,128)(2,1)S(1)}, u32[]{:S(2)}, u32[]{:S(2)}) collective-permute-start(bf16[16,2048]{1,0:T(8,128)(2,1)S(1)} %collective-permute-done.5.refs_6_.refs_1_), channel_id=1, source_target_pairs={{0,4},{4,0},{8,12},{12,8},{16,20},{20,16},{24,28},{28,24},{1,5},{5... | collective-permute-start | bytes 196616 | tf_op jit(solution)/shard_map/ppermute | solution.py:24
  18.3 5.2 %copy-start = (bf16[2048,1024]{1,0:T(8,128)(2,1)S(1)}, bf16[2048,1024]{1,0:T(8,128)(2,1)}, u32[]{:S(2)}) copy-start(bf16[2048,1024]{1,0:T(8,128)(2,1)} %refs_9_.1) | copy-start | bytes 12582916
  18.4 5.2 %copy-start.2 = (bf16[2048,256]{1,0:T(8,128)(2,1)S(1)}, bf16[2048,256]{1,0:T(8,128)(2,1)}, u32[]{:S(2)}) copy-start(bf16[2048,256]{1,0:T(8,128)(2,1)} %refs_8_.2) | copy-start | bytes 3145732
  18.4 5.2 %copy-start.7 = (f32[2048]{0:T(1024)S(1)}, f32[2048]{0:T(1024)}, u32[]{:S(2)}) copy-start(f32[2048]{0:T(1024)} %param.19) | copy-start | bytes 24580
  18.4 15.9 %collective-permute-start.13 = (bf16[4,8,2048]{2,1,0:T(8,128)(2,1)S(1)}, bf16[4,8,2048]{2,1,0:T(8,128)(2,1)S(1)}, u32[]{:S(2)}, u32[]{:S(2)}) collective-permute-start(bf16[4,8,2048]{2,1,0:T(8,128)(2,1)S(1)} %shard_map.154.refs_0_.refs_2_), channel_id=1, source_target_pairs={{0,2},{1,3},{2,0},{3,1},{4,6},{5,7},{6,4},{7,5},{8,10},{9,11},{10,... | collective-permute-start | bytes 393224 | tf_op jit(solution)/shard_map/ppermute | solution.py:24
  22.0 4.3 %collective-permute-start.17 = (bf16[2,8,2048]{2,1,0:T(8,128)(2,1)S(1)}, bf16[2,8,2048]{2,1,0:T(8,128)(2,1)S(1)}, u32[]{:S(2)}, u32[]{:S(2)}) collective-permute-start(bf16[2,8,2048]{2,1,0:T(8,128)(2,1)S(1)} %shard_map.157), channel_id=1, source_target_pairs={{0,4},{4,0},{8,12},{12,8},{16,20},{20,16},{24,28},{28,24},{1,5},{5... | collective-permute-start | bytes 196616 | tf_op jit(solution)/shard_map/ppermute | solution.py:24
  25.1 2.8 %collective-permute-start.7 = (bf16[128,896]{1,0:T(8,128)(2,1)S(1)}, bf16[128,896]{1,0:T(8,128)(2,1)S(1)}, u32[]{:S(2)}, u32[]{:S(2)}) collective-permute-start(bf16[128,896]{1,0:T(8,128)(2,1)S(1)} %get-tuple-element.48.own_ref), channel_id=1, source_target_pairs={{0,1},{1,0},{2,3},{3,2},{4,5},{5,4},{6,7},{7,6},{8,9},{9,8},{10,11... | collective-permute-start | bytes 688136 | tf_op jit(solution)/shard_map/ppermute | solution.py:24
  26.3 6.1 %collective-permute-start.18 = (bf16[4,8,2048]{2,1,0:T(8,128)(2,1)S(1)}, bf16[4,8,2048]{2,1,0:T(8,128)(2,1)S(1)}, u32[]{:S(2)}, u32[]{:S(2)}) collective-permute-start(bf16[4,8,2048]{2,1,0:T(8,128)(2,1)S(1)} %shard_map.158.refs_0_.refs_5_), channel_id=1, source_target_pairs={{0,2},{1,3},{2,0},{3,1},{4,6},{5,7},{6,4},{7,5},{8,10},{9,11},{10,... | collective-permute-start | bytes 393224 | tf_op jit(solution)/shard_map/ppermute | solution.py:24
  28.6 5.5 %collective-permute-start.8 = (bf16[128,384]{1,0:T(8,128)(2,1)S(1)}, bf16[128,384]{1,0:T(8,128)(2,1)S(1)}, u32[]{:S(2)}, u32[]{:S(2)}) collective-permute-start(bf16[128,384]{1,0:T(8,128)(2,1)S(1)} %get-tuple-element.50.own_ref), channel_id=1, source_target_pairs={{0,2},{1,3},{2,0},{3,1},{4,6},{5,7},{6,4},{7,5},{8,10},{9,11},{10,... | collective-permute-start | bytes 294920 | tf_op jit(solution)/shard_map/ppermute | solution.py:24
  29.3 9.5 %collective-permute-start.11 = (bf16[128,128]{1,0:T(8,128)(2,1)S(1)}, bf16[128,128]{1,0:T(8,128)(2,1)S(1)}, u32[]{:S(2)}, u32[]{:S(2)}) collective-permute-start(bf16[128,128]{1,0:T(8,128)(2,1)S(1)} %get-tuple-element.52), channel_id=1, source_target_pairs={{0,4},{1,5},{2,6},{3,7},{4,12},{5,13},{6,14},{7,15},{8,20},{9,21},... | collective-permute-start | bytes 98312 | tf_op jit(solution)/shard_map/ppermute | solution.py:653
  30.9 7.9 %collective-permute-start.12 = (bf16[128,128]{1,0:T(8,128)(2,1)S(1)}, bf16[128,128]{1,0:T(8,128)(2,1)S(1)}, u32[]{:S(2)}, u32[]{:S(2)}) collective-permute-start(bf16[128,128]{1,0:T(8,128)(2,1)S(1)} %get-tuple-element.52), channel_id=1, source_target_pairs={{0,6},{1,7},{2,4},{3,5},{4,14},{5,15},{6,12},{7,13},{8,22},{9,23},... | collective-permute-start | bytes 98312 | tf_op jit(solution)/shard_map/ppermute | solution.py:653
  32.5 6.4 %collective-permute-start.10 = (bf16[128,128]{1,0:T(8,128)(2,1)S(1)}, bf16[128,128]{1,0:T(8,128)(2,1)S(1)}, u32[]{:S(2)}, u32[]{:S(2)}) collective-permute-start(bf16[128,128]{1,0:T(8,128)(2,1)S(1)} %get-tuple-element.51), channel_id=1, source_target_pairs={{0,2},{1,3},{2,0},{3,1},{4,10},{5,11},{6,8},{7,9},{8,18},{9,19},{1... | collective-permute-start | bytes 98312 | tf_op jit(solution)/shard_map/ppermute | solution.py:653
  34.2 1.6 %collective-permute-start.19 = (bf16[2,4,8,2048]{3,2,1,0:T(8,128)(2,1)S(1)}, bf16[2,4,8,2048]{3,2,1,0:T(8,128)(2,1)S(1)}, u32[]{:S(2)}, u32[]{:S(2)}) collective-permute-start(bf16[2,4,8,2048]{3,2,1,0:T(8,128)(2,1)S(1)} %shard_map.159), channel_id=1, source_target_pairs={{0,1},{1,0},{2,3},{3,2},{4,5},{5,4},{6,7},{7,6},{8,9},{9,8},{10,11... | collective-permute-start | bytes 786440 | tf_op jit(solution)/shard_map/ppermute | solution.py:24
  34.3 2.1 %collective-permute-start.14 = (bf16[2,4,8,2048]{3,2,1,0:T(8,128)(2,1)S(1)}, bf16[2,4,8,2048]{3,2,1,0:T(8,128)(2,1)S(1)}, u32[]{:S(2)}, u32[]{:S(2)}) collective-permute-start(bf16[2,4,8,2048]{3,2,1,0:T(8,128)(2,1)S(1)} %shard_map.155), channel_id=1, source_target_pairs={{0,1},{1,0},{2,3},{3,2},{4,5},{5,4},{6,7},{7,6},{8,9},{9,8},{10,11... | collective-permute-start | bytes 786440 | tf_op jit(solution)/shard_map/ppermute | solution.py:24
  35.8 3.1 %collective-permute-start.9 = (bf16[128,128]{1,0:T(8,128)(2,1)S(1)}, bf16[128,128]{1,0:T(8,128)(2,1)S(1)}, u32[]{:S(2)}, u32[]{:S(2)}) collective-permute-start(bf16[128,128]{1,0:T(8,128)(2,1)S(1)} %get-tuple-element.51), channel_id=1, source_target_pairs={{0,0},{1,1},{2,2},{3,3},{4,8},{5,9},{6,10},{7,11},{8,16},{9,17},{1... | collective-permute-start | bytes 98312 | tf_op jit(solution)/shard_map/ppermute | solution.py:653
  38.9 6.7 %copy-start.1 = (bf16[1024,2048]{1,0:T(8,128)(2,1)S(1)}, bf16[1024,2048]{1,0:T(8,128)(2,1)}, u32[]{:S(2)}) copy-start(bf16[1024,2048]{1,0:T(8,128)(2,1)} %refs_4_.2) | copy-start | bytes 12582916
  40.0 4.3 %collective-permute-start.21 = (bf16[32,1024]{1,0:T(8,128)(2,1)S(1)}, bf16[32,1024]{1,0:T(8,128)(2,1)S(1)}, u32[]{:S(2)}, u32[]{:S(2)}) collective-permute-start(bf16[32,1024]{1,0:T(8,128)(2,1)S(1)} %shard_map.161.refs_0_), channel_id=1, source_target_pairs={{0,2},{1,3},{2,0},{3,1},{4,6},{5,7},{6,4},{7,5},{8,10},{9,11},{10,... | collective-permute-start | bytes 196616 | tf_op jit(solution)/shard_map/ppermute | solution.py:24
  41.6 2.7 %collective-permute-start.20 = (bf16[32,1024]{1,0:T(8,128)(2,1)S(1)}, bf16[32,1024]{1,0:T(8,128)(2,1)S(1)}, u32[]{:S(2)}, u32[]{:S(2)}) collective-permute-start(bf16[32,1024]{1,0:T(8,128)(2,1)S(1)} %shard_map.161.refs_0_), channel_id=1, source_target_pairs={{0,1},{1,0},{2,3},{3,2},{4,5},{5,4},{6,7},{7,6},{8,9},{9,8},{10,11... | collective-permute-start | bytes 196616 | tf_op jit(solution)/shard_map/ppermute | solution.py:24
  44.4 1.3 %collective-permute-start.22 = (bf16[32,1024]{1,0:T(8,128)(2,1)S(1)}, bf16[32,1024]{1,0:T(8,128)(2,1)S(1)}, u32[]{:S(2)}, u32[]{:S(2)}) collective-permute-start(bf16[32,1024]{1,0:T(8,128)(2,1)S(1)} %collective-permute-done.21.refs_2_), channel_id=1, source_target_pairs={{0,1},{1,0},{2,3},{3,2},{4,5},{5,4},{6,7},{7,6},{8,9},{9,8},{10,11... | collective-permute-start | bytes 196616 | tf_op jit(solution)/shard_map/ppermute | solution.py:24
  46.9 8.2 %collective-permute-start.25 = (bf16[16,2048]{1,0:T(8,128)(2,1)S(1)}, bf16[16,2048]{1,0:T(8,128)(2,1)S(1)}, u32[]{:S(2)}, u32[]{:S(2)}) collective-permute-start(bf16[16,2048]{1,0:T(8,128)(2,1)S(1)} %get-tuple-element.67), channel_id=1, source_target_pairs={{0,4},{4,0},{8,12},{12,8},{16,20},{20,16},{24,28},{28,24},{1,5},{5... | collective-permute-start | bytes 196616 | tf_op jit(solution)/shard_map/ppermute | solution.py:24
  52.7 6.5 %collective-permute-start.23 = (bf16[16,2048]{1,0:T(8,128)(2,1)S(1)}, bf16[16,2048]{1,0:T(8,128)(2,1)S(1)}, u32[]{:S(2)}, u32[]{:S(2)}) collective-permute-start(bf16[16,2048]{1,0:T(8,128)(2,1)S(1)} %get-tuple-element.63), channel_id=1, source_target_pairs={{0,4},{4,0},{8,12},{12,8},{16,20},{20,16},{24,28},{28,24},{1,5},{5... | collective-permute-start | bytes 196616 | tf_op jit(solution)/shard_map/ppermute | solution.py:24
  52.8 9.7 %collective-permute-start.29 = (bf16[16,2048]{1,0:T(8,128)(2,1)S(1)}, bf16[16,2048]{1,0:T(8,128)(2,1)S(1)}, u32[]{:S(2)}, u32[]{:S(2)}) collective-permute-start(bf16[16,2048]{1,0:T(8,128)(2,1)S(1)} %get-tuple-element.70), channel_id=1, source_target_pairs={{0,12},{4,8},{8,4},{12,0},{16,28},{20,24},{24,20},{28,16},{1,13},{... | collective-permute-start | bytes 196616 | tf_op jit(solution)/shard_map/ppermute | solution.py:24
  55.1 7.3 %collective-permute-start.26 = (bf16[16,2048]{1,0:T(8,128)(2,1)S(1)}, bf16[16,2048]{1,0:T(8,128)(2,1)S(1)}, u32[]{:S(2)}, u32[]{:S(2)}) collective-permute-start(bf16[16,2048]{1,0:T(8,128)(2,1)S(1)} %shard_map.164), channel_id=1, source_target_pairs={{0,24},{4,28},{8,16},{12,20},{16,8},{20,12},{24,0},{28,4},{1,25},{... | collective-permute-start | bytes 196616 | tf_op jit(solution)/shard_map/ppermute | solution.py:24
  59.2 19.1 %slice-start = ((s8[7340032]{0:T(1024)(128)(4,1)}), s8[4194304]{0:T(1024)(128)(4,1)S(1)}, s32[]{:S(2)}) async-start(s8[7340032]{0:T(1024)(128)(4,1)} %bitcast.12), calls=%async_computation | async-start | bytes 8388608
  59.2 5.3 %collective-permute-start.24 = (bf16[16,2048]{1,0:T(8,128)(2,1)S(1)}, bf16[16,2048]{1,0:T(8,128)(2,1)S(1)}, u32[]{:S(2)}, u32[]{:S(2)}) collective-permute-start(bf16[16,2048]{1,0:T(8,128)(2,1)S(1)} %get-tuple-element.66), channel_id=1, source_target_pairs={{0,16},{4,20},{8,24},{12,28},{16,0},{20,4},{24,8},{28,12},{1,17},{... | collective-permute-start | bytes 196616 | tf_op jit(solution)/shard_map/ppermute | solution.py:24
  59.3 5.2 %collective-permute-start.27 = (bf16[16,2048]{1,0:T(8,128)(2,1)S(1)}, bf16[16,2048]{1,0:T(8,128)(2,1)S(1)}, u32[]{:S(2)}, u32[]{:S(2)}) collective-permute-start(bf16[16,2048]{1,0:T(8,128)(2,1)S(1)} %get-tuple-element.68), channel_id=1, source_target_pairs={{0,4},{4,0},{8,12},{12,8},{16,20},{20,16},{24,28},{28,24},{1,5},{5... | collective-permute-start | bytes 196616 | tf_op jit(solution)/shard_map/ppermute | solution.py:24
  59.5 18.7 %slice-start.1 = ((s8[7340032]{0:T(1024)(128)(4,1)}), s8[3145728]{0:T(1024)(128)(4,1)S(1)}, s32[]{:S(2)}) async-start(s8[7340032]{0:T(1024)(128)(4,1)} %bitcast.12), calls=%async_computation.1 | async-start | bytes 6291456
  59.5 5.6 %collective-permute-start.28 = (bf16[16,2048]{1,0:T(8,128)(2,1)S(1)}, bf16[16,2048]{1,0:T(8,128)(2,1)S(1)}, u32[]{:S(2)}, u32[]{:S(2)}) collective-permute-start(bf16[16,2048]{1,0:T(8,128)(2,1)S(1)} %get-tuple-element.69), channel_id=1, source_target_pairs={{0,8},{4,12},{8,0},{12,4},{16,24},{20,28},{24,16},{28,20},{1,9},{5... | collective-permute-start | bytes 196616 | tf_op jit(solution)/shard_map/ppermute | solution.py:24
  65.2 13.1 %copy-start.8 = (f32[2048]{0:T(1024)S(1)}, f32[2048]{0:T(1024)}, u32[]{:S(2)}) copy-start(f32[2048]{0:T(1024)} %param.20) | copy-start | bytes 24580
  65.2 15.1 %slice-start.2 = ((s8[7340032]{0:T(1024)(128)(4,1)}), s8[4194304]{0:T(1024)(128)(4,1)S(1)}, s32[]{:S(2)}) async-start(s8[7340032]{0:T(1024)(128)(4,1)} %bitcast.14), calls=%async_computation.2 | async-start | bytes 8388608
  65.8 7.5 %collective-permute-start.33 = (bf16[16,2048]{1,0:T(8,128)(2,1)S(1)}, bf16[16,2048]{1,0:T(8,128)(2,1)S(1)}, u32[]{:S(2)}, u32[]{:S(2)}) collective-permute-start(bf16[16,2048]{1,0:T(8,128)(2,1)S(1)} %get-tuple-element.72.refs_0_), channel_id=1, source_target_pairs={{0,16},{4,20},{8,24},{12,28},{16,0},{20,4},{24,8},{28,12},{1,17},{... | collective-permute-start | bytes 196616 | tf_op jit(solution)/shard_map/ppermute | solution.py:24
  67.2 6.8 %collective-permute-start.35 = (bf16[16,2048]{1,0:T(8,128)(2,1)S(1)}, bf16[16,2048]{1,0:T(8,128)(2,1)S(1)}, u32[]{:S(2)}, u32[]{:S(2)}) collective-permute-start(bf16[16,2048]{1,0:T(8,128)(2,1)S(1)} %get-tuple-element.72.refs_0_), channel_id=1, source_target_pairs={{0,24},{4,28},{8,16},{12,20},{16,8},{20,12},{24,0},{28,4},{1,25},{... | collective-permute-start | bytes 196616 | tf_op jit(solution)/shard_map/ppermute | solution.py:24
  69.8 5.5 %collective-permute-start.30 = (bf16[16,2048]{1,0:T(8,128)(2,1)S(1)}, bf16[16,2048]{1,0:T(8,128)(2,1)S(1)}, u32[]{:S(2)}, u32[]{:S(2)}) collective-permute-start(bf16[16,2048]{1,0:T(8,128)(2,1)S(1)} %get-tuple-element.72.refs_0_), channel_id=1, source_target_pairs={{0,4},{4,0},{8,12},{12,8},{16,20},{20,16},{24,28},{28,24},{1,5},{5... | collective-permute-start | bytes 196616 | tf_op jit(solution)/shard_map/ppermute | solution.py:24
  70.5 4.8 %collective-permute-start.31 = (bf16[16,2048]{1,0:T(8,128)(2,1)S(1)}, bf16[16,2048]{1,0:T(8,128)(2,1)S(1)}, u32[]{:S(2)}, u32[]{:S(2)}) collective-permute-start(bf16[16,2048]{1,0:T(8,128)(2,1)S(1)} %get-tuple-element.72.refs_0_), channel_id=1, source_target_pairs={{0,8},{4,12},{8,0},{12,4},{16,24},{20,28},{24,16},{28,20},{1,9},{5... | collective-permute-start | bytes 196616 | tf_op jit(solution)/shard_map/ppermute | solution.py:24
  70.5 5.7 %collective-permute-start.32 = (bf16[16,2048]{1,0:T(8,128)(2,1)S(1)}, bf16[16,2048]{1,0:T(8,128)(2,1)S(1)}, u32[]{:S(2)}, u32[]{:S(2)}) collective-permute-start(bf16[16,2048]{1,0:T(8,128)(2,1)S(1)} %get-tuple-element.72.refs_0_), channel_id=1, source_target_pairs={{0,12},{4,8},{8,4},{12,0},{16,28},{20,24},{24,20},{28,16},{1,13},{... | collective-permute-start | bytes 196616 | tf_op jit(solution)/shard_map/ppermute | solution.py:24
  73.3 4.3 %collective-permute-start.34 = (bf16[16,2048]{1,0:T(8,128)(2,1)S(1)}, bf16[16,2048]{1,0:T(8,128)(2,1)S(1)}, u32[]{:S(2)}, u32[]{:S(2)}) collective-permute-start(bf16[16,2048]{1,0:T(8,128)(2,1)S(1)} %collective-permute-done.33.refs_4_), channel_id=1, source_target_pairs={{0,4},{4,0},{8,12},{12,8},{16,20},{20,16},{24,28},{28,24},{1,5},{5... | collective-permute-start | bytes 196616 | tf_op jit(solution)/shard_map/ppermute | solution.py:24
  74.0 4.3 %collective-permute-start.36 = (bf16[16,2048]{1,0:T(8,128)(2,1)S(1)}, bf16[16,2048]{1,0:T(8,128)(2,1)S(1)}, u32[]{:S(2)}, u32[]{:S(2)}) collective-permute-start(bf16[16,2048]{1,0:T(8,128)(2,1)S(1)} %collective-permute-done.35.refs_6_), channel_id=1, source_target_pairs={{0,4},{4,0},{8,12},{12,8},{16,20},{20,16},{24,28},{28,24},{1,5},{5... | collective-permute-start | bytes 196616 | tf_op jit(solution)/shard_map/ppermute | solution.py:24
  78.3 17.8 %slice-start.4 = ((s8[7340032]{0:T(1024)(128)(4,1)}), s8[4194304]{0:T(1024)(128)(4,1)S(1)}, s32[]{:S(2)}) async-start(s8[7340032]{0:T(1024)(128)(4,1)} %bitcast.16), calls=%async_computation.4 | async-start | bytes 8388608
  80.1 1.8 %collective-permute-start.37 = (bf16[64,1920]{1,0:T(8,128)(2,1)S(1)}, bf16[64,1920]{1,0:T(8,128)(2,1)S(1)}, u32[]{:S(2)}, u32[]{:S(2)}) collective-permute-start(bf16[64,1920]{1,0:T(8,128)(2,1)S(1)} %get-tuple-element.74), channel_id=1, source_target_pairs={{0,1},{1,0},{2,3},{3,2},{4,5},{5,4},{6,7},{7,6},{8,9},{9,8},{10,11... | collective-permute-start | bytes 737288 | tf_op jit(solution)/shard_map/ppermute | solution.py:24
  80.2 15.9 %slice-start.5 = ((s8[7340032]{0:T(1024)(128)(4,1)}), s8[3145728]{0:T(1024)(128)(4,1)S(1)}, s32[]{:S(2)}) async-start(s8[7340032]{0:T(1024)(128)(4,1)} %bitcast.16), calls=%async_computation.5 | async-start | bytes 6291456
  81.4 2.2 %collective-permute-start.39 = (bf16[64,1792]{1,0:T(8,128)(2,1)S(1)}, bf16[64,1792]{1,0:T(8,128)(2,1)S(1)}, u32[]{:S(2)}, u32[]{:S(2)}) collective-permute-start(bf16[64,1792]{1,0:T(8,128)(2,1)S(1)} %get-tuple-element.77), channel_id=1, source_target_pairs={{0,1},{1,0},{2,3},{3,2},{4,5},{5,4},{6,7},{7,6},{8,9},{9,8},{10,11... | collective-permute-start | bytes 688136 | tf_op jit(solution)/shard_map/ppermute | solution.py:24
  82.0 6.2 %collective-permute-start.38 = (bf16[32,1920]{1,0:T(8,128)(2,1)S(1)}, bf16[32,1920]{1,0:T(8,128)(2,1)S(1)}, u32[]{:S(2)}, u32[]{:S(2)}) collective-permute-start(bf16[32,1920]{1,0:T(8,128)(2,1)S(1)} %slice.64), channel_id=1, source_target_pairs={{0,2},{1,3},{2,0},{3,1},{4,6},{5,7},{6,4},{7,5},{8,10},{9,11},{10,... | collective-permute-start | bytes 368648 | tf_op jit(solution)/shard_map/ppermute | solution.py:24
  83.6 6.2 %collective-permute-start.40 = (bf16[32,1792]{1,0:T(8,128)(2,1)S(1)}, bf16[32,1792]{1,0:T(8,128)(2,1)S(1)}, u32[]{:S(2)}, u32[]{:S(2)}) collective-permute-start(bf16[32,1792]{1,0:T(8,128)(2,1)S(1)} %slice.65), channel_id=1, source_target_pairs={{0,2},{1,3},{2,0},{3,1},{4,6},{5,7},{6,4},{7,5},{8,10},{9,11},{10,... | collective-permute-start | bytes 344072 | tf_op jit(solution)/shard_map/ppermute | solution.py:24
  90.0 4.9 %collective-permute-start.42 = (bf16[32,1792]{1,0:T(8,128)(2,1)S(1)}, bf16[32,1792]{1,0:T(8,128)(2,1)S(1)}, u32[]{:S(2)}, u32[]{:S(2)}) collective-permute-start(bf16[32,1792]{1,0:T(8,128)(2,1)S(1)} %fusion.2.refs_0_), channel_id=1, source_target_pairs={{0,2},{1,3},{2,0},{3,1},{4,6},{5,7},{6,4},{7,5},{8,10},{9,11},{10,... | collective-permute-start | bytes 344072 | tf_op jit(solution)/shard_map/ppermute | solution.py:24
  91.5 3.3 %collective-permute-start.41 = (bf16[32,1792]{1,0:T(8,128)(2,1)S(1)}, bf16[32,1792]{1,0:T(8,128)(2,1)S(1)}, u32[]{:S(2)}, u32[]{:S(2)}) collective-permute-start(bf16[32,1792]{1,0:T(8,128)(2,1)S(1)} %fusion.2.refs_0_), channel_id=1, source_target_pairs={{0,1},{1,0},{2,3},{3,2},{4,5},{5,4},{6,7},{7,6},{8,9},{9,8},{10,11... | collective-permute-start | bytes 344072 | tf_op jit(solution)/shard_map/ppermute | solution.py:24
  94.8 1.3 %collective-permute-start.43 = (bf16[32,1792]{1,0:T(8,128)(2,1)S(1)}, bf16[32,1792]{1,0:T(8,128)(2,1)S(1)}, u32[]{:S(2)}, u32[]{:S(2)}) collective-permute-start(bf16[32,1792]{1,0:T(8,128)(2,1)S(1)} %collective-permute-done.42.refs_2_), channel_id=1, source_target_pairs={{0,1},{1,0},{2,3},{3,2},{4,5},{5,4},{6,7},{7,6},{8,9},{9,8},{10,11... | collective-permute-start | bytes 344072 | tf_op jit(solution)/shard_map/ppermute | solution.py:24
  97.9 4.8 %collective-permute-start.46 = (bf16[16,2048]{1,0:T(8,128)(2,1)S(1)}, bf16[16,2048]{1,0:T(8,128)(2,1)S(1)}, u32[]{:S(2)}, u32[]{:S(2)}) collective-permute-start(bf16[16,2048]{1,0:T(8,128)(2,1)S(1)} %get-tuple-element.84), channel_id=1, source_target_pairs={{0,4},{4,0},{8,12},{12,8},{16,20},{20,16},{24,28},{28,24},{1,5},{5... | collective-permute-start | bytes 196616 | tf_op jit(solution)/shard_map/ppermute | solution.py:24
  99.2 6.1 %collective-permute-start.44 = (bf16[16,2048]{1,0:T(8,128)(2,1)S(1)}, bf16[16,2048]{1,0:T(8,128)(2,1)S(1)}, u32[]{:S(2)}, u32[]{:S(2)}) collective-permute-start(bf16[16,2048]{1,0:T(8,128)(2,1)S(1)} %get-tuple-element.80), channel_id=1, source_target_pairs={{0,4},{4,0},{8,12},{12,8},{16,20},{20,16},{24,28},{28,24},{1,5},{5... | collective-permute-start | bytes 196616 | tf_op jit(solution)/shard_map/ppermute | solution.py:24
  100.0 8.7 %collective-permute-start.50 = (bf16[16,2048]{1,0:T(8,128)(2,1)S(1)}, bf16[16,2048]{1,0:T(8,128)(2,1)S(1)}, u32[]{:S(2)}, u32[]{:S(2)}) collective-permute-start(bf16[16,2048]{1,0:T(8,128)(2,1)S(1)} %get-tuple-element.87), channel_id=1, source_target_pairs={{0,12},{4,8},{8,4},{12,0},{16,28},{20,24},{24,20},{28,16},{1,13},{... | collective-permute-start | bytes 196616 | tf_op jit(solution)/shard_map/ppermute | solution.py:24
  102.7 6.3 %collective-permute-start.47 = (bf16[16,2048]{1,0:T(8,128)(2,1)S(1)}, bf16[16,2048]{1,0:T(8,128)(2,1)S(1)}, u32[]{:S(2)}, u32[]{:S(2)}) collective-permute-start(bf16[16,2048]{1,0:T(8,128)(2,1)S(1)} %shard_map.170), channel_id=1, source_target_pairs={{0,24},{4,28},{8,16},{12,20},{16,8},{20,12},{24,0},{28,4},{1,25},{... | collective-permute-start | bytes 196616 | tf_op jit(solution)/shard_map/ppermute | solution.py:24
  105.4 5.5 %collective-permute-start.45 = (bf16[16,2048]{1,0:T(8,128)(2,1)S(1)}, bf16[16,2048]{1,0:T(8,128)(2,1)S(1)}, u32[]{:S(2)}, u32[]{:S(2)}) collective-permute-start(bf16[16,2048]{1,0:T(8,128)(2,1)S(1)} %get-tuple-element.83), channel_id=1, source_target_pairs={{0,16},{4,20},{8,24},{12,28},{16,0},{20,4},{24,8},{28,12},{1,17},{... | collective-permute-start | bytes 196616 | tf_op jit(solution)/shard_map/ppermute | solution.py:24
  105.5 5.5 %collective-permute-start.48 = (bf16[16,2048]{1,0:T(8,128)(2,1)S(1)}, bf16[16,2048]{1,0:T(8,128)(2,1)S(1)}, u32[]{:S(2)}, u32[]{:S(2)}) collective-permute-start(bf16[16,2048]{1,0:T(8,128)(2,1)S(1)} %get-tuple-element.85), channel_id=1, source_target_pairs={{0,4},{4,0},{8,12},{12,8},{16,20},{20,16},{24,28},{28,24},{1,5},{5... | collective-permute-start | bytes 196616 | tf_op jit(solution)/shard_map/ppermute | solution.py:24
  106.3 5.3 %collective-permute-start.49 = (bf16[16,2048]{1,0:T(8,128)(2,1)S(1)}, bf16[16,2048]{1,0:T(8,128)(2,1)S(1)}, u32[]{:S(2)}, u32[]{:S(2)}) collective-permute-start(bf16[16,2048]{1,0:T(8,128)(2,1)S(1)} %get-tuple-element.86), channel_id=1, source_target_pairs={{0,8},{4,12},{8,0},{12,4},{16,24},{20,28},{24,16},{28,20},{1,9},{5... | collective-permute-start | bytes 196616 | tf_op jit(solution)/shard_map/ppermute | solution.py:24
  (4 other events, 5.6 us)

commit v14 on v13

--- a/solution.py
+++ b/solution.py
@@ -176,16 +176,19 @@
     return call(body, shaped((1 + len(near),) + own.shape), (own, *near), [VMEM] * (1 + len(near)), around=1)
 
 
-def gather_cache(block, after):
-    blocks = [block] + [swap(block, "tensor", k) for k in range(2, lax.axis_size("tensor"), 2)]
-
+def cross_chips(block):
+    return [block] + [swap(block, "tensor", k) for k in range(2, lax.axis_size("tensor"), 2)]
+
+
+def cross_cores(blocks, after):
     def body(after_ref, *refs):
         for i, ref in enumerate(refs[:-1]):
             refs[-1][i] = ref[...]
 
     ins = (after, *blocks)
-    both = call(body, shaped((len(blocks),) + block.shape), ins, [ANY] + [VMEM] * len(blocks), around=0)
-    return blocks + [swap(both, "tensor", 1)]
+    shape = (len(blocks),) + blocks[0].shape
+    both = call(body, shaped(shape), ins, [ANY] + [VMEM] * len(blocks), around=0)
+    return [*blocks, swap(both, "tensor", 1)]
 
 
 def last_entries(pieces, after):
@@ -284,7 +287,7 @@
     return lax.axis_size("dp") == KVH and lax.axis_size("tensor") == 4
 
 
-def add_cores(where, own, keep, arrived):
+def add_cores(where, own, keep, arrived, after):
     tensor = lax.axis_size("tensor")
     groups = lax.axis_size("dp")
     rows, total = own.shape
@@ -293,7 +296,7 @@
     height = 2 * half // tensor
     direct = direct_keyvals()
 
-    def body(where_ref, own_ref, keep_ref, arrived_ref, first_ref, message_ref, *out_refs):
+    def body(where_ref, own_ref, keep_ref, arrived_ref, after_ref, first_ref, message_ref, *out_refs):
         summed = own_ref[:, :base].astype(F32) + arrived_ref[:, :base].astype(F32)
         ends = summed[:, base - 128 :]
         lane = lax.broadcasted_iota(jnp.int32, ends.shape, 1)
@@ -315,7 +318,8 @@
 
     outs = [shaped((height, wide), F32), shaped((rows, 128 + wide // 4 if direct else base))]
     outs += [shaped((rows, HD))] * 2 if direct else [shaped((height, wide))] * (tensor // 2 - 1)
-    return call(body, tuple(outs), (where, own, keep, arrived), [SMEM] + [VMEM] * 3, moved=6 * own.size)
+    ins = (where, own, keep, arrived, after)
+    return call(body, tuple(outs), ins, [SMEM] + [VMEM] * 3 + [ANY], moved=6 * own.size)
 
 
 def row_scale(own, arrived, width):
@@ -481,8 +485,8 @@
 def sum_rows(parts, pair):
     own, *near, keep, one, two = parts
     count = one.shape[0] // pair
-    sums = add_pairs(keep, swap(one, "dp", 1), 0, pair, near[:2])
-    sums, near = list(sums[:count]), [*sums[count:], *near[2:]]
+    sums = add_pairs(keep, swap(one, "dp", 1), 0, pair, near[:1])
+    sums, near = list(sums[:count]), [*sums[count:], *near[1:]]
     sums += add_pairs(keep, swap(two, "dp", 1), one.shape[0], pair)
     arrived = [swap(piece, "dp", len(near) + 1 + 2 * i) for i, piece in enumerate(sums)]
     arrived += [swap(piece, "dp", k + 1) for k, piece in enumerate(near)]
@@ -700,14 +704,14 @@
     blocks = gather_rows(x, near_pieces if joined else None)
     close = min(groups, 4)
     near_moved = blocks[1:close] if joined else [swap(piece, "dp", k) for k, piece in enumerate(near_pieces, 1)]
-    near_pieces = collect_near(own_piece, near_moved, span)
+    near_cache = cross_chips(collect_near(own_piece, near_moved, span))
     packed = pack_far(where, cache_keys, cache_values, blocks[close::2])
     far_pieces = [swap(piece, "dp", close + 2 * i) for i, piece in enumerate(packed)]
 
     message, keep = project_attention(where, blocks, attn_gain, w_keyval, w_query, x)
-    queries, message, *leaving = add_cores(where, message, keep, swap(message, "tensor", 1))
+    queries, message, *leaving = add_cores(where, message, keep, swap(message, "tensor", 1), near_cache[-1])
     passed = swap(last_entries(far_pieces, x), "dp", 1)
-    far_pieces = collect_far(far_pieces, passed)
+    far_cache = cross_chips(collect_far(far_pieces, passed))
     if direct_keyvals():
         pieces = send_keyvals(leaving)
         arrived = swap(message, "tensor", 2)
@@ -723,8 +727,8 @@
         pieces = move_keyvals(pieces)
         queries = [queries] + [swap(piece, "tensor", 2 * i) for i, piece in enumerate(leaving, 1)]
 
-    near_cache = gather_cache(near_pieces, arrived)
-    far_cache = gather_cache(far_pieces, arrived)
+    near_cache = cross_cores(near_cache, arrived)
+    far_cache = cross_cores(far_cache, arrived)
 
     own = t * parts + jnp.arange(parts, dtype=jnp.int32)
     anc = lax.dynamic_slice_in_dim(ancestors, t * parts, parts).astype(jnp.int32)

time: 112 us -> 112 us (level)
  starting transfers between devices: 65.3 us -> 58.3 us
  waiting for transfers between devices: 28.7 us -> 35.1 us
    ppermute x47, starting transfers between devices: 60 us -> 49.7 us  [swap(): return lax.ppermute(x, axis, [(i, i ^ bits) for i in range(size)])]
    ppermute x47, waiting for transfers between devices: 28.7 us -> 34.2 us  [swap(): return lax.ppermute(x, axis, [(i, i ^ bits) for i in range(size)])]
    ppermute x4, starting transfers between devices: 5.32 us -> 8.57 us  [send_keyvals(): moved.append(lax.ppermute(piece, ('dp', 'tensor'), pairs))]
  transfers between devices with their start and end apart: 51 -> 51, of which waited for: 21 -> 20; matrix products, arithmetic and copies ran while one was open for 1% -> 1% of each run, Pallas kernels for 6% -> 6%
where the time goes in v14:
time: 112 us
  starting transfers between devices  58.3 us (52%)
  waiting for transfers between devices  35.1 us (31%)
  Pallas kernels  14.5 us (13%)
  local copies, waits for them, and re-layouts  1.96 us (2%)
    ppermute x47, starting transfers between devices, swap(): return lax.ppermute(x, axis, [(i, i ^ bits) for i in range(size)])  49.7 us
    ppermute x47, waiting for transfers between devices, swap(): return lax.ppermute(x, axis, [(i, i ^ bits) for i in range(size)])  34.2 us
    pallas_call x23, Pallas kernels, call(): pl.pallas_call(body, out_shape=outs, in_specs=specs, out_specs=jax.tree.m...  14.5 us
    ppermute x4, starting transfers between devices, send_keyvals(): moved.append(lax.ppermute(piece, ('dp', 'tensor'), pairs))  8.57 us
  transfers between devices with their start and end apart: 51, of which 20 were waited for; matrix products, arithmetic and copies ran while one was open for 1% of the time, Pallas kernels for 6%

profile of v14, /device:TPU:0, one launch (start us, length us, event | category | flops | bytes accessed | tf_op | source)
XLA Modules:
  0.0 111.6 jit_solution(10033299782508829062)
XLA Ops:
  0.7 0.8 copy-done.5
  1.5 0.8 copy-done.6
  2.2 4.0 %collective-permute-start.3 = (bf16[16,2048]{1,0:T(8,128)(2,1)S(1)}, bf16[16,2048]{1,0:T(8,128)(2,1)S(1)}, u32[]{:S(2)}, u32[]{:S(2)}) collective-permute-start(bf16[16,2048]{1,0:T(8,128)(2,1)S(1)} %shard_map.149.x_ref.refs_0_.refs_10_.after_ref.refs_5_), channel_id=1, source_target_pairs={{0,16},{4,20},{8,24},{12,28},{16,0},{20,4},{24,8},{28,12},{1,17},{... | collective-permute-start | bytes 196616 | tf_op jit(solution)/shard_map/ppermute | solution.py:24
  6.3 1.3 %collective-permute-start.5 = (bf16[16,2048]{1,0:T(8,128)(2,1)S(1)}, bf16[16,2048]{1,0:T(8,128)(2,1)S(1)}, u32[]{:S(2)}, u32[]{:S(2)}) collective-permute-start(bf16[16,2048]{1,0:T(8,128)(2,1)S(1)} %shard_map.149.x_ref.refs_0_.refs_10_.after_ref.refs_5_), channel_id=1, source_target_pairs={{0,24},{4,28},{8,16},{12,20},{16,8},{20,12},{24,0},{28,4},{1,25},{... | collective-permute-start | bytes 196616 | tf_op jit(solution)/shard_map/ppermute | solution.py:24
  7.7 0.6 shard_map.150
  8.3 1.6 %collective-permute-start = (bf16[24,2048]{1,0:T(8,128)(2,1)S(1)}, bf16[24,2048]{1,0:T(8,128)(2,1)S(1)}, u32[]{:S(2)}, u32[]{:S(2)}) collective-permute-start(bf16[24,2048]{1,0:T(8,128)(2,1)S(1)} %get-tuple-element.43), channel_id=1, source_target_pairs={{0,4},{4,0},{8,12},{12,8},{16,20},{20,16},{24,28},{28,24},{1,5},{5... | collective-permute-start | bytes 294920 | tf_op jit(solution)/shard_map/ppermute | solution.py:24
  10.1 1.8 %collective-permute-start.2 = (bf16[24,2048]{1,0:T(8,128)(2,1)S(1)}, bf16[24,2048]{1,0:T(8,128)(2,1)S(1)}, u32[]{:S(2)}, u32[]{:S(2)}) collective-permute-start(bf16[24,2048]{1,0:T(8,128)(2,1)S(1)} %get-tuple-element.45), channel_id=1, source_target_pairs={{0,12},{4,8},{8,4},{12,0},{16,28},{20,24},{24,20},{28,16},{1,13},{... | collective-permute-start | bytes 294920 | tf_op jit(solution)/shard_map/ppermute | solution.py:24
  12.5 0.6 shard_map.156
  13.1 2.8 %collective-permute-start.15 = (bf16[2,8,2048]{2,1,0:T(8,128)(2,1)S(1)}, bf16[2,8,2048]{2,1,0:T(8,128)(2,1)S(1)}, u32[]{:S(2)}, u32[]{:S(2)}) collective-permute-start(bf16[2,8,2048]{2,1,0:T(8,128)(2,1)S(1)} %get-tuple-element.53), channel_id=1, source_target_pairs={{0,16},{4,20},{8,24},{12,28},{16,0},{20,4},{24,8},{28,12},{1,17},{... | collective-permute-start | bytes 196616 | tf_op jit(solution)/shard_map/ppermute | solution.py:24
  16.3 1.6 %collective-permute-start.4 = (bf16[16,2048]{1,0:T(8,128)(2,1)S(1)}, bf16[16,2048]{1,0:T(8,128)(2,1)S(1)}, u32[]{:S(2)}, u32[]{:S(2)}) collective-permute-start(bf16[16,2048]{1,0:T(8,128)(2,1)S(1)} %collective-permute-done.3.refs_4_.refs_0_), channel_id=1, source_target_pairs={{0,4},{4,0},{8,12},{12,8},{16,20},{20,16},{24,28},{28,24},{1,5},{5... | collective-permute-start | bytes 196616 | tf_op jit(solution)/shard_map/ppermute | solution.py:24
  18.4 1.8 %collective-permute-start.8 = (bf16[4,8,2048]{2,1,0:T(8,128)(2,1)S(1)}, bf16[4,8,2048]{2,1,0:T(8,128)(2,1)S(1)}, u32[]{:S(2)}, u32[]{:S(2)}) collective-permute-start(bf16[4,8,2048]{2,1,0:T(8,128)(2,1)S(1)} %shard_map.152.refs_0_.refs_2_), channel_id=1, source_target_pairs={{0,2},{1,3},{2,0},{3,1},{4,6},{5,7},{6,4},{7,5},{8,10},{9,11},{10,... | collective-permute-start | bytes 393224 | tf_op jit(solution)/shard_map/ppermute | solution.py:24
  20.2 1.8 %collective-permute-done.16.refs_1_ = bf16[2,8,2048]{2,1,0:T(8,128)(2,1)S(1)} collective-permute-done((bf16[2,8,2048]{2,1,0:T(8,128)(2,1)S(1)}, bf16[2,8,2048]{2,1,0:T(8,128)(2,1)S(1)}, u32[]{:S(2)}, u32[]{:S(2)}) %collective-permute-start.16) | collective-permute-done | bytes 65568 | tf_op jit(solution)/shard_map/ppermute | solution.py:24
  22.0 1.5 %collective-permute-start.17 = (bf16[2,8,2048]{2,1,0:T(8,128)(2,1)S(1)}, bf16[2,8,2048]{2,1,0:T(8,128)(2,1)S(1)}, u32[]{:S(2)}, u32[]{:S(2)}) collective-permute-start(bf16[2,8,2048]{2,1,0:T(8,128)(2,1)S(1)} %shard_map.157), channel_id=1, source_target_pairs={{0,4},{4,0},{8,12},{12,8},{16,20},{20,16},{24,28},{28,24},{1,5},{5... | collective-permute-start | bytes 196616 | tf_op jit(solution)/shard_map/ppermute | solution.py:24
  23.6 1.5 %shard_map.151 = (bf16[128,896]{1,0:T(8,128)(2,1)S(1)}, f32[64,1024]{1,0:T(8,128)S(1)}) custom-call(s32[2]{0:T(128)S(1)} %pad_add_fusion.3.where_ref, f32[1,2048]{1,0:T(1,128)S(1)} %bitcast.18, bf16[16,2048]{1,0:T(8,128)(2,1)S(1)} %shard_map.149.x_ref.refs_0_.refs_10_.after_ref.refs_5_, bf16[24,2048]{1,0:T(8,128)(2,1)S(1)} %collective-permute-done.refs_1_.refs_0_, ...), custom_call_target="tpu_custom_call" | custom-call | flops 6039797760 | bytes 6291456 | tf_op jit(solution)/shard_map/pallas_call | solution.py:45
  25.2 1.1 collective-permute-done.17.refs_2_
  26.3 1.6 %collective-permute-start.18 = (bf16[4,8,2048]{2,1,0:T(8,128)(2,1)S(1)}, bf16[4,8,2048]{2,1,0:T(8,128)(2,1)S(1)}, u32[]{:S(2)}, u32[]{:S(2)}) collective-permute-start(bf16[4,8,2048]{2,1,0:T(8,128)(2,1)S(1)} %shard_map.158.refs_0_.refs_5_), channel_id=1, source_target_pairs={{0,2},{1,3},{2,0},{3,1},{4,6},{5,7},{6,4},{7,5},{8,10},{9,11},{10,... | collective-permute-start | bytes 393224 | tf_op jit(solution)/shard_map/ppermute | solution.py:24
  27.9 0.7 shard_map.153
  29.3 0.7 collective-permute-start.10
  30.0 1.6 %collective-permute-start.11 = (bf16[128,128]{1,0:T(8,128)(2,1)S(1)}, bf16[128,128]{1,0:T(8,128)(2,1)S(1)}, u32[]{:S(2)}, u32[]{:S(2)}) collective-permute-start(bf16[128,128]{1,0:T(8,128)(2,1)S(1)} %get-tuple-element.50), channel_id=1, source_target_pairs={{0,2},{1,3},{2,0},{3,1},{4,10},{5,11},{6,8},{7,9},{8,18},{9,19},{1... | collective-permute-start | bytes 98312 | tf_op jit(solution)/shard_map/ppermute | solution.py:657
  31.6 4.0 %collective-permute-start.12 = (bf16[128,128]{1,0:T(8,128)(2,1)S(1)}, bf16[128,128]{1,0:T(8,128)(2,1)S(1)}, u32[]{:S(2)}, u32[]{:S(2)}) collective-permute-start(bf16[128,128]{1,0:T(8,128)(2,1)S(1)} %get-tuple-element.51), channel_id=1, source_target_pairs={{0,4},{1,5},{2,6},{3,7},{4,12},{5,13},{6,14},{7,15},{8,20},{9,21},... | collective-permute-start | bytes 98312 | tf_op jit(solution)/shard_map/ppermute | solution.py:657
  36.4 0.8 collective-permute-done.19.refs_7_
  37.2 2.4 %collective-permute-start.13 = (bf16[128,128]{1,0:T(8,128)(2,1)S(1)}, bf16[128,128]{1,0:T(8,128)(2,1)S(1)}, u32[]{:S(2)}, u32[]{:S(2)}) collective-permute-start(bf16[128,128]{1,0:T(8,128)(2,1)S(1)} %get-tuple-element.51), channel_id=1, source_target_pairs={{0,6},{1,7},{2,4},{3,5},{4,14},{5,15},{6,12},{7,13},{8,22},{9,23},... | collective-permute-start | bytes 98312 | tf_op jit(solution)/shard_map/ppermute | solution.py:657
  39.6 2.4 %shard_map.160 = (bf16[256,128]{1,0:T(8,128)(2,1)S(1)}, f32[256,128]{1,0:T(8,128)S(1)}, f32[256,128]{1,0:T(8,128)S(1)}, f32[256,128]{1,0:T(8,128)S(1)}) custom-call(s32[2]{0:T(128)S(1)} %pad_add_fusion.3.where_ref, s32[16]{0:T(128)S(1)} %get-tuple-element.85.anc_ref, f32[4,128]{1,0:T(4,128)S(1)} %copy-done.9, f32[128,128]{1,0:T(8,128)S(1)} %shard_map.154.scale_ref, ...), custom_call_target="tpu_custom_call" | custom-call | flops 5368709120 | bytes 4194304 | tf_op jit(solution)/shard_map/pallas_call | solution.py:45
  42.0 0.9 collective-permute-done.13.refs_3_
  42.9 1.1 %shard_map.161.refs_0_ = bf16[32,1024]{1,0:T(8,128)(2,1)S(1)} custom-call(s32[2]{0:T(128)S(1)} %pad_add_fusion.3.where_ref, f32[4,128]{1,0:T(4,128)S(1)} %copy-done.9, s32[256,2]{1,0:T(8,128)S(1)} %copy.20.target_ref, f32[128,128]{1,0:T(8,128)S(1)} %shard_map.154.scale_ref, bf16[128,128]{1,0:T(8,128)(2,1)S(1)} %collective-permute-done.10.refs_0_, ...), custom_call_target="tpu_custom_call" | custom-call | flops 5368709120 | bytes 1048576 | tf_op jit(solution)/shard_map/pallas_call | solution.py:45
  44.0 0.7 collective-permute-start.21
  44.7 3.6 %collective-permute-done.21.refs_2_ = bf16[32,1024]{1,0:T(8,128)(2,1)S(1)} collective-permute-done((bf16[32,1024]{1,0:T(8,128)(2,1)S(1)}, bf16[32,1024]{1,0:T(8,128)(2,1)S(1)}, u32[]{:S(2)}, u32[]{:S(2)}) %collective-permute-start.21) | collective-permute-done | bytes 65568 | tf_op jit(solution)/shard_map/ppermute | solution.py:24
  48.4 1.2 %collective-permute-done.22.refs_3_ = bf16[32,1024]{1,0:T(8,128)(2,1)S(1)} collective-permute-done((bf16[32,1024]{1,0:T(8,128)(2,1)S(1)}, bf16[32,1024]{1,0:T(8,128)(2,1)S(1)}, u32[]{:S(2)}, u32[]{:S(2)}) %collective-permute-start.22) | collective-permute-done | bytes 65568 | tf_op jit(solution)/shard_map/ppermute | solution.py:24
  49.6 1.3 %shard_map.162 = (f32[16,2048]{1,0:T(8,128)S(1)}, bf16[16,2048]{1,0:T(8,128)(2,1)S(1)}, bf16[16,2048]{1,0:T(8,128)(2,1)S(1)}, bf16[16,2048]{1,0:T(8,128)(2,1)S(1...) custom-call(s32[2]{0:T(128)S(1)} %pad_add_fusion.3.where_ref, ...), custom_call_target="tpu_custom_call" | custom-call | flops 5905580032 | bytes 4194304 | tf_op jit(solution)/shard_map/pallas_call | solution.py:45
  50.9 1.6 %collective-permute-start.25 = (bf16[16,2048]{1,0:T(8,128)(2,1)S(1)}, bf16[16,2048]{1,0:T(8,128)(2,1)S(1)}, u32[]{:S(2)}, u32[]{:S(2)}) collective-permute-start(bf16[16,2048]{1,0:T(8,128)(2,1)S(1)} %get-tuple-element.64), channel_id=1, source_target_pairs={{0,4},{4,0},{8,12},{12,8},{16,20},{20,16},{24,28},{28,24},{1,5},{5... | collective-permute-start | bytes 196616 | tf_op jit(solution)/shard_map/ppermute | solution.py:24
  53.0 1.7 %collective-permute-start.28 = (bf16[16,2048]{1,0:T(8,128)(2,1)S(1)}, bf16[16,2048]{1,0:T(8,128)(2,1)S(1)}, u32[]{:S(2)}, u32[]{:S(2)}) collective-permute-start(bf16[16,2048]{1,0:T(8,128)(2,1)S(1)} %get-tuple-element.66), channel_id=1, source_target_pairs={{0,8},{4,12},{8,0},{12,4},{16,24},{20,28},{24,16},{28,20},{1,9},{5... | collective-permute-start | bytes 196616 | tf_op jit(solution)/shard_map/ppermute | solution.py:24
  54.7 1.3 %collective-permute-start.29 = (bf16[16,2048]{1,0:T(8,128)(2,1)S(1)}, bf16[16,2048]{1,0:T(8,128)(2,1)S(1)}, u32[]{:S(2)}, u32[]{:S(2)}) collective-permute-start(bf16[16,2048]{1,0:T(8,128)(2,1)S(1)} %get-tuple-element.67), channel_id=1, source_target_pairs={{0,12},{4,8},{8,4},{12,0},{16,28},{20,24},{24,20},{28,16},{1,13},{... | collective-permute-start | bytes 196616 | tf_op jit(solution)/shard_map/ppermute | solution.py:24
  56.0 2.1 %collective-permute-start.26 = (bf16[16,2048]{1,0:T(8,128)(2,1)S(1)}, bf16[16,2048]{1,0:T(8,128)(2,1)S(1)}, u32[]{:S(2)}, u32[]{:S(2)}) collective-permute-start(bf16[16,2048]{1,0:T(8,128)(2,1)S(1)} %shard_map.164), channel_id=1, source_target_pairs={{0,24},{4,28},{8,16},{12,20},{16,8},{20,12},{24,0},{28,4},{1,25},{... | collective-permute-start | bytes 196616 | tf_op jit(solution)/shard_map/ppermute | solution.py:24
  58.1 1.3 %collective-permute-start.24 = (bf16[16,2048]{1,0:T(8,128)(2,1)S(1)}, bf16[16,2048]{1,0:T(8,128)(2,1)S(1)}, u32[]{:S(2)}, u32[]{:S(2)}) collective-permute-start(bf16[16,2048]{1,0:T(8,128)(2,1)S(1)} %get-tuple-element.63), channel_id=1, source_target_pairs={{0,16},{4,20},{8,24},{12,28},{16,0},{20,4},{24,8},{28,12},{1,17},{... | collective-permute-start | bytes 196616 | tf_op jit(solution)/shard_map/ppermute | solution.py:24
  59.4 1.7 %collective-permute-start.27 = (bf16[16,2048]{1,0:T(8,128)(2,1)S(1)}, bf16[16,2048]{1,0:T(8,128)(2,1)S(1)}, u32[]{:S(2)}, u32[]{:S(2)}) collective-permute-start(bf16[16,2048]{1,0:T(8,128)(2,1)S(1)} %get-tuple-element.65), channel_id=1, source_target_pairs={{0,4},{4,0},{8,12},{12,8},{16,20},{20,16},{24,28},{28,24},{1,5},{5... | collective-permute-start | bytes 196616 | tf_op jit(solution)/shard_map/ppermute | solution.py:24
  61.2 1.3 %collective-permute-done.26.refs_1_ = bf16[16,2048]{1,0:T(8,128)(2,1)S(1)} collective-permute-done((bf16[16,2048]{1,0:T(8,128)(2,1)S(1)}, bf16[16,2048]{1,0:T(8,128)(2,1)S(1)}, u32[]{:S(2)}, u32[]{:S(2)}) %collective-permute-start.26) | collective-permute-done | bytes 65568 | tf_op jit(solution)/shard_map/ppermute | solution.py:24
  62.5 2.5 %collective-permute-done.24.refs_0_ = bf16[16,2048]{1,0:T(8,128)(2,1)S(1)} collective-permute-done((bf16[16,2048]{1,0:T(8,128)(2,1)S(1)}, bf16[16,2048]{1,0:T(8,128)(2,1)S(1)}, u32[]{:S(2)}, u32[]{:S(2)}) %collective-permute-start.24) | collective-permute-done | bytes 65568 | tf_op jit(solution)/shard_map/ppermute | solution.py:24
  65.0 0.7 shard_map.165
  66.1 1.8 %collective-permute-start.35 = (bf16[16,2048]{1,0:T(8,128)(2,1)S(1)}, bf16[16,2048]{1,0:T(8,128)(2,1)S(1)}, u32[]{:S(2)}, u32[]{:S(2)}) collective-permute-start(bf16[16,2048]{1,0:T(8,128)(2,1)S(1)} %get-tuple-element.69.refs_0_), channel_id=1, source_target_pairs={{0,24},{4,28},{8,16},{12,20},{16,8},{20,12},{24,0},{28,4},{1,25},{... | collective-permute-start | bytes 196616 | tf_op jit(solution)/shard_map/ppermute | solution.py:24
  67.9 1.3 %collective-permute-start.30 = (bf16[16,2048]{1,0:T(8,128)(2,1)S(1)}, bf16[16,2048]{1,0:T(8,128)(2,1)S(1)}, u32[]{:S(2)}, u32[]{:S(2)}) collective-permute-start(bf16[16,2048]{1,0:T(8,128)(2,1)S(1)} %get-tuple-element.69.refs_0_), channel_id=1, source_target_pairs={{0,4},{4,0},{8,12},{12,8},{16,20},{20,16},{24,28},{28,24},{1,5},{5... | collective-permute-start | bytes 196616 | tf_op jit(solution)/shard_map/ppermute | solution.py:24
  69.3 0.6 collective-permute-start.31
  69.9 1.5 %collective-permute-start.32 = (bf16[16,2048]{1,0:T(8,128)(2,1)S(1)}, bf16[16,2048]{1,0:T(8,128)(2,1)S(1)}, u32[]{:S(2)}, u32[]{:S(2)}) collective-permute-start(bf16[16,2048]{1,0:T(8,128)(2,1)S(1)} %get-tuple-element.69.refs_0_), channel_id=1, source_target_pairs={{0,12},{4,8},{8,4},{12,0},{16,28},{20,24},{24,20},{28,16},{1,13},{... | collective-permute-start | bytes 196616 | tf_op jit(solution)/shard_map/ppermute | solution.py:24
  71.4 1.5 %collective-permute-done.33.refs_4_ = bf16[16,2048]{1,0:T(8,128)(2,1)S(1)} collective-permute-done((bf16[16,2048]{1,0:T(8,128)(2,1)S(1)}, bf16[16,2048]{1,0:T(8,128)(2,1)S(1)}, u32[]{:S(2)}, u32[]{:S(2)}) %collective-permute-start.33) | collective-permute-done | bytes 65568 | tf_op jit(solution)/shard_map/ppermute | solution.py:24
  72.9 2.0 %collective-permute-start.36 = (bf16[16,2048]{1,0:T(8,128)(2,1)S(1)}, bf16[16,2048]{1,0:T(8,128)(2,1)S(1)}, u32[]{:S(2)}, u32[]{:S(2)}) collective-permute-start(bf16[16,2048]{1,0:T(8,128)(2,1)S(1)} %collective-permute-done.35.refs_6_), channel_id=1, source_target_pairs={{0,4},{4,0},{8,12},{12,8},{16,20},{20,16},{24,28},{28,24},{1,5},{5... | collective-permute-start | bytes 196616 | tf_op jit(solution)/shard_map/ppermute | solution.py:24
  75.0 2.1 %collective-permute-done.34.refs_5_ = bf16[16,2048]{1,0:T(8,128)(2,1)S(1)} collective-permute-done((bf16[16,2048]{1,0:T(8,128)(2,1)S(1)}, bf16[16,2048]{1,0:T(8,128)(2,1)S(1)}, u32[]{:S(2)}, u32[]{:S(2)}) %collective-permute-start.34) | collective-permute-done | bytes 65568 | tf_op jit(solution)/shard_map/ppermute | solution.py:24
  77.1 0.7 collective-permute-done.36.refs_7_
  77.9 1.8 %shard_map.166 = (bf16[128,2048]{1,0:T(8,128)(2,1)S(1)}, f32[64,1920]{1,0:T(8,128)S(1)}, bf16[64,1920]{1,0:T(8,128)(2,1)S(1)}) custom-call(s32[2]{0:T(128)S(1)} %pad_add_fusion.3.where_ref, f32[1,2048]{1,0:T(1,128)S(1)} %bitcast.19, bf16[16,2048]{1,0:T(8,128)(2,1)S(1)} %get-tuple-element.69.refs_0_, bf16[16,2048]{1,0:T(8,128)(2,1)S(1)} %collective-permute-done.30.refs_1_, ...), custom_call_target="tpu_custom_call" | custom-call | flops 6308233216 | bytes 8388608 | tf_op jit(solution)/shard_map/pallas_call | solution.py:45
  79.8 1.1 %shard_map.167 = (f32[64,1792]{1,0:T(8,128)S(1)}, bf16[64,1792]{1,0:T(8,128)(2,1)S(1)}) custom-call(bf16[128,2048]{1,0:T(8,128)(2,1)S(1)} %get-tuple-element.72.h_ref, bf16[2048,1792]{1,0:T(8,128)(2,1)S(1)} %bitcast.15), custom_call_target="tpu_custom_call" | custom-call | flops 6308233216 | bytes 7340032 | tf_op jit(solution)/shard_map/pallas_call | solution.py:45
  81.8 0.7 collective-permute-done.39
  82.7 1.1 %collective-permute-start.40 = (bf16[32,1792]{1,0:T(8,128)(2,1)S(1)}, bf16[32,1792]{1,0:T(8,128)(2,1)S(1)}, u32[]{:S(2)}, u32[]{:S(2)}) collective-permute-start(bf16[32,1792]{1,0:T(8,128)(2,1)S(1)} %slice.65), channel_id=1, source_target_pairs={{0,2},{1,3},{2,0},{3,1},{4,6},{5,7},{6,4},{7,5},{8,10},{9,11},{10,... | collective-permute-start | bytes 344072 | tf_op jit(solution)/shard_map/ppermute | solution.py:24
  83.8 4.0 %collective-permute-done.38 = bf16[32,1920]{1,0:T(8,128)(2,1)S(1)} collective-permute-done((bf16[32,1920]{1,0:T(8,128)(2,1)S(1)}, bf16[32,1920]{1,0:T(8,128)(2,1)S(1)}, u32[]{:S(2)}, u32[]{:S(2)}) %collective-permute-start.38) | collective-permute-done | bytes 122912 | tf_op jit(solution)/shard_map/ppermute | solution.py:24
  88.0 1.3 %collective-permute-done.40 = bf16[32,1792]{1,0:T(8,128)(2,1)S(1)} collective-permute-done((bf16[32,1792]{1,0:T(8,128)(2,1)S(1)}, bf16[32,1792]{1,0:T(8,128)(2,1)S(1)}, u32[]{:S(2)}, u32[]{:S(2)}) %collective-permute-start.40) | collective-permute-done | bytes 114720 | tf_op jit(solution)/shard_map/ppermute | solution.py:24
  89.9 4.5 %collective-permute-done.42.refs_2_ = bf16[32,1792]{1,0:T(8,128)(2,1)S(1)} collective-permute-done((bf16[32,1792]{1,0:T(8,128)(2,1)S(1)}, bf16[32,1792]{1,0:T(8,128)(2,1)S(1)}, u32[]{:S(2)}, u32[]{:S(2)}) %collective-permute-start.42) | collective-permute-done | bytes 114720 | tf_op jit(solution)/shard_map/ppermute | solution.py:24
  94.4 1.3 %collective-permute-done.43.refs_3_ = bf16[32,1792]{1,0:T(8,128)(2,1)S(1)} collective-permute-done((bf16[32,1792]{1,0:T(8,128)(2,1)S(1)}, bf16[32,1792]{1,0:T(8,128)(2,1)S(1)}, u32[]{:S(2)}, u32[]{:S(2)}) %collective-permute-start.43) | collective-permute-done | bytes 114720 | tf_op jit(solution)/shard_map/ppermute | solution.py:24
  95.7 1.7 %shard_map.168 = (f32[16,2048]{1,0:T(8,128)S(1)}, bf16[16,2048]{1,0:T(8,128)(2,1)S(1)}, bf16[16,2048]{1,0:T(8,128)(2,1)S(1)}, bf16[16,2048]{1,0:T(8,128)(2,1)S(1...) custom-call(s32[2]{0:T(128)S(1)} %pad_add_fusion.3.where_ref, ...), custom_call_target="tpu_custom_call" | custom-call | flops 6308233216 | bytes 7340032 | tf_op jit(solution)/shard_map/pallas_call | solution.py:45
  97.4 1.4 %collective-permute-start.46 = (bf16[16,2048]{1,0:T(8,128)(2,1)S(1)}, bf16[16,2048]{1,0:T(8,128)(2,1)S(1)}, u32[]{:S(2)}, u32[]{:S(2)}) collective-permute-start(bf16[16,2048]{1,0:T(8,128)(2,1)S(1)} %get-tuple-element.80), channel_id=1, source_target_pairs={{0,4},{4,0},{8,12},{12,8},{16,20},{20,16},{24,28},{28,24},{1,5},{5... | collective-permute-start | bytes 196616 | tf_op jit(solution)/shard_map/ppermute | solution.py:24
  98.8 0.7 collective-permute-start.44
  99.5 0.7 collective-permute-start.49
  100.2 2.1 %collective-permute-start.50 = (bf16[16,2048]{1,0:T(8,128)(2,1)S(1)}, bf16[16,2048]{1,0:T(8,128)(2,1)S(1)}, u32[]{:S(2)}, u32[]{:S(2)}) collective-permute-start(bf16[16,2048]{1,0:T(8,128)(2,1)S(1)} %get-tuple-element.83), channel_id=1, source_target_pairs={{0,12},{4,8},{8,4},{12,0},{16,28},{20,24},{24,20},{28,16},{1,13},{... | collective-permute-start | bytes 196616 | tf_op jit(solution)/shard_map/ppermute | solution.py:24
  102.3 1.9 %collective-permute-start.47 = (bf16[16,2048]{1,0:T(8,128)(2,1)S(1)}, bf16[16,2048]{1,0:T(8,128)(2,1)S(1)}, u32[]{:S(2)}, u32[]{:S(2)}) collective-permute-start(bf16[16,2048]{1,0:T(8,128)(2,1)S(1)} %shard_map.170), channel_id=1, source_target_pairs={{0,24},{4,28},{8,16},{12,20},{16,8},{20,12},{24,0},{28,4},{1,25},{... | collective-permute-start | bytes 196616 | tf_op jit(solution)/shard_map/ppermute | solution.py:24
  104.7 1.1 collective-permute-start.48
  105.8 2.8 %collective-permute-done.47.refs_1_ = bf16[16,2048]{1,0:T(8,128)(2,1)S(1)} collective-permute-done((bf16[16,2048]{1,0:T(8,128)(2,1)S(1)}, bf16[16,2048]{1,0:T(8,128)(2,1)S(1)}, u32[]{:S(2)}, u32[]{:S(2)}) %collective-permute-start.47) | collective-permute-done | bytes 65568 | tf_op jit(solution)/shard_map/ppermute | solution.py:24
  108.6 2.3 %collective-permute-done.45.refs_0_ = bf16[16,2048]{1,0:T(8,128)(2,1)S(1)} collective-permute-done((bf16[16,2048]{1,0:T(8,128)(2,1)S(1)}, bf16[16,2048]{1,0:T(8,128)(2,1)S(1)}, u32[]{:S(2)}, u32[]{:S(2)}) %collective-permute-start.45) | collective-permute-done | bytes 65568 | tf_op jit(solution)/shard_map/ppermute | solution.py:24
  110.9 0.7 shard_map.171
  (116 shorter events, 6.9 us)
Async XLA Ops:
  0.6 7.0 %copy-start.3 = (bf16[8,8,1024]{2,1,0:T(8,128)(2,1)S(1)}, bf16[8,8,1024]{2,1,0:T(8,128)(2,1)}, u32[]{:S(2)}) copy-start(bf16[8,8,1024]{2,1,0:T(8,128)(2,1)} %keys_ref.3) | copy-start | bytes 393220
  0.6 7.0 %copy-start.4 = (bf16[8,8,1024]{2,1,0:T(8,128)(2,1)S(1)}, bf16[8,8,1024]{2,1,0:T(8,128)(2,1)}, u32[]{:S(2)}) copy-start(bf16[8,8,1024]{2,1,0:T(8,128)(2,1)} %values_ref.3) | copy-start | bytes 393220
  2.2 9.9 %collective-permute-start.3 = (bf16[16,2048]{1,0:T(8,128)(2,1)S(1)}, bf16[16,2048]{1,0:T(8,128)(2,1)S(1)}, u32[]{:S(2)}, u32[]{:S(2)}) collective-permute-start(bf16[16,2048]{1,0:T(8,128)(2,1)S(1)} %shard_map.149.x_ref.refs_0_.refs_10_.after_ref.refs_5_), channel_id=1, source_target_pairs={{0,16},{4,20},{8,24},{12,28},{16,0},{20,4},{24,8},{28,12},{1,17},{... | collective-permute-start | bytes 196616 | tf_op jit(solution)/shard_map/ppermute | solution.py:24
  6.3 6.2 %collective-permute-start.5 = (bf16[16,2048]{1,0:T(8,128)(2,1)S(1)}, bf16[16,2048]{1,0:T(8,128)(2,1)S(1)}, u32[]{:S(2)}, u32[]{:S(2)}) collective-permute-start(bf16[16,2048]{1,0:T(8,128)(2,1)S(1)} %shard_map.149.x_ref.refs_0_.refs_10_.after_ref.refs_5_), channel_id=1, source_target_pairs={{0,24},{4,28},{8,16},{12,20},{16,8},{20,12},{24,0},{28,4},{1,25},{... | collective-permute-start | bytes 196616 | tf_op jit(solution)/shard_map/ppermute | solution.py:24
  7.7 4.2 %copy-start.10 = (s32[64]{0:T(128)S(1)}, s32[64]{0:T(128)}, u32[]{:S(2)}) copy-start(s32[64]{0:T(128)} %param.18) | copy-start | bytes 772
  8.3 8.0 %collective-permute-start = (bf16[24,2048]{1,0:T(8,128)(2,1)S(1)}, bf16[24,2048]{1,0:T(8,128)(2,1)S(1)}, u32[]{:S(2)}, u32[]{:S(2)}) collective-permute-start(bf16[24,2048]{1,0:T(8,128)(2,1)S(1)} %get-tuple-element.43), channel_id=1, source_target_pairs={{0,4},{4,0},{8,12},{12,8},{16,20},{20,16},{24,28},{28,24},{1,5},{5... | collective-permute-start | bytes 294920 | tf_op jit(solution)/shard_map/ppermute | solution.py:24
  9.8 8.1 %collective-permute-start.1 = (bf16[24,2048]{1,0:T(8,128)(2,1)S(1)}, bf16[24,2048]{1,0:T(8,128)(2,1)S(1)}, u32[]{:S(2)}, u32[]{:S(2)}) collective-permute-start(bf16[24,2048]{1,0:T(8,128)(2,1)S(1)} %get-tuple-element.44), channel_id=1, source_target_pairs={{0,8},{4,12},{8,0},{12,4},{16,24},{20,28},{24,16},{28,20},{1,9},{5... | collective-permute-start | bytes 294920 | tf_op jit(solution)/shard_map/ppermute | solution.py:24
  10.1 8.3 %collective-permute-start.2 = (bf16[24,2048]{1,0:T(8,128)(2,1)S(1)}, bf16[24,2048]{1,0:T(8,128)(2,1)S(1)}, u32[]{:S(2)}, u32[]{:S(2)}) collective-permute-start(bf16[24,2048]{1,0:T(8,128)(2,1)S(1)} %get-tuple-element.45), channel_id=1, source_target_pairs={{0,12},{4,8},{8,4},{12,0},{16,28},{20,24},{24,20},{28,16},{1,13},{... | collective-permute-start | bytes 294920 | tf_op jit(solution)/shard_map/ppermute | solution.py:24
  13.1 7.1 %collective-permute-start.15 = (bf16[2,8,2048]{2,1,0:T(8,128)(2,1)S(1)}, bf16[2,8,2048]{2,1,0:T(8,128)(2,1)S(1)}, u32[]{:S(2)}, u32[]{:S(2)}) collective-permute-start(bf16[2,8,2048]{2,1,0:T(8,128)(2,1)S(1)} %get-tuple-element.53), channel_id=1, source_target_pairs={{0,16},{4,20},{8,24},{12,28},{16,0},{20,4},{24,8},{28,12},{1,17},{... | collective-permute-start | bytes 196616 | tf_op jit(solution)/shard_map/ppermute | solution.py:24
  15.9 6.2 %collective-permute-start.16 = (bf16[2,8,2048]{2,1,0:T(8,128)(2,1)S(1)}, bf16[2,8,2048]{2,1,0:T(8,128)(2,1)S(1)}, u32[]{:S(2)}, u32[]{:S(2)}) collective-permute-start(bf16[2,8,2048]{2,1,0:T(8,128)(2,1)S(1)} %get-tuple-element.54), channel_id=1, source_target_pairs={{0,24},{4,28},{8,16},{12,20},{16,8},{20,12},{24,0},{28,4},{1,25},{... | collective-permute-start | bytes 196616 | tf_op jit(solution)/shard_map/ppermute | solution.py:24
  16.3 7.3 %collective-permute-start.4 = (bf16[16,2048]{1,0:T(8,128)(2,1)S(1)}, bf16[16,2048]{1,0:T(8,128)(2,1)S(1)}, u32[]{:S(2)}, u32[]{:S(2)}) collective-permute-start(bf16[16,2048]{1,0:T(8,128)(2,1)S(1)} %collective-permute-done.3.refs_4_.refs_0_), channel_id=1, source_target_pairs={{0,4},{4,0},{8,12},{12,8},{16,20},{20,16},{24,28},{28,24},{1,5},{5... | collective-permute-start | bytes 196616 | tf_op jit(solution)/shard_map/ppermute | solution.py:24
  17.9 5.7 %collective-permute-start.6 = (bf16[16,2048]{1,0:T(8,128)(2,1)S(1)}, bf16[16,2048]{1,0:T(8,128)(2,1)S(1)}, u32[]{:S(2)}, u32[]{:S(2)}) collective-permute-start(bf16[16,2048]{1,0:T(8,128)(2,1)S(1)} %collective-permute-done.5.refs_6_.refs_1_), channel_id=1, source_target_pairs={{0,4},{4,0},{8,12},{12,8},{16,20},{20,16},{24,28},{28,24},{1,5},{5... | collective-permute-start | bytes 196616 | tf_op jit(solution)/shard_map/ppermute | solution.py:24
  18.3 5.2 %copy-start = (bf16[2048,1024]{1,0:T(8,128)(2,1)S(1)}, bf16[2048,1024]{1,0:T(8,128)(2,1)}, u32[]{:S(2)}) copy-start(bf16[2048,1024]{1,0:T(8,128)(2,1)} %refs_9_.1) | copy-start | bytes 12582916
  18.4 5.2 %copy-start.2 = (bf16[2048,256]{1,0:T(8,128)(2,1)S(1)}, bf16[2048,256]{1,0:T(8,128)(2,1)}, u32[]{:S(2)}) copy-start(bf16[2048,256]{1,0:T(8,128)(2,1)} %refs_8_.2) | copy-start | bytes 3145732
  18.4 5.2 %copy-start.7 = (f32[2048]{0:T(1024)S(1)}, f32[2048]{0:T(1024)}, u32[]{:S(2)}) copy-start(f32[2048]{0:T(1024)} %param.19) | copy-start | bytes 24580
  18.4 9.5 %collective-permute-start.8 = (bf16[4,8,2048]{2,1,0:T(8,128)(2,1)S(1)}, bf16[4,8,2048]{2,1,0:T(8,128)(2,1)S(1)}, u32[]{:S(2)}, u32[]{:S(2)}) collective-permute-start(bf16[4,8,2048]{2,1,0:T(8,128)(2,1)S(1)} %shard_map.152.refs_0_.refs_2_), channel_id=1, source_target_pairs={{0,2},{1,3},{2,0},{3,1},{4,6},{5,7},{6,4},{7,5},{8,10},{9,11},{10,... | collective-permute-start | bytes 393224 | tf_op jit(solution)/shard_map/ppermute | solution.py:24
  22.0 4.3 %collective-permute-start.17 = (bf16[2,8,2048]{2,1,0:T(8,128)(2,1)S(1)}, bf16[2,8,2048]{2,1,0:T(8,128)(2,1)S(1)}, u32[]{:S(2)}, u32[]{:S(2)}) collective-permute-start(bf16[2,8,2048]{2,1,0:T(8,128)(2,1)S(1)} %shard_map.157), channel_id=1, source_target_pairs={{0,4},{4,0},{8,12},{12,8},{16,20},{20,16},{24,28},{28,24},{1,5},{5... | collective-permute-start | bytes 196616 | tf_op jit(solution)/shard_map/ppermute | solution.py:24
  25.1 2.8 %collective-permute-start.7 = (bf16[128,896]{1,0:T(8,128)(2,1)S(1)}, bf16[128,896]{1,0:T(8,128)(2,1)S(1)}, u32[]{:S(2)}, u32[]{:S(2)}) collective-permute-start(bf16[128,896]{1,0:T(8,128)(2,1)S(1)} %get-tuple-element.46.own_ref), channel_id=1, source_target_pairs={{0,1},{1,0},{2,3},{3,2},{4,5},{5,4},{6,7},{7,6},{8,9},{9,8},{10,11... | collective-permute-start | bytes 688136 | tf_op jit(solution)/shard_map/ppermute | solution.py:24
  26.3 9.2 %collective-permute-start.18 = (bf16[4,8,2048]{2,1,0:T(8,128)(2,1)S(1)}, bf16[4,8,2048]{2,1,0:T(8,128)(2,1)S(1)}, u32[]{:S(2)}, u32[]{:S(2)}) collective-permute-start(bf16[4,8,2048]{2,1,0:T(8,128)(2,1)S(1)} %shard_map.158.refs_0_.refs_5_), channel_id=1, source_target_pairs={{0,2},{1,3},{2,0},{3,1},{4,6},{5,7},{6,4},{7,5},{8,10},{9,11},{10,... | collective-permute-start | bytes 393224 | tf_op jit(solution)/shard_map/ppermute | solution.py:24
  28.6 6.9 %collective-permute-start.9 = (bf16[128,384]{1,0:T(8,128)(2,1)S(1)}, bf16[128,384]{1,0:T(8,128)(2,1)S(1)}, u32[]{:S(2)}, u32[]{:S(2)}) collective-permute-start(bf16[128,384]{1,0:T(8,128)(2,1)S(1)} %get-tuple-element.49.own_ref), channel_id=1, source_target_pairs={{0,2},{1,3},{2,0},{3,1},{4,6},{5,7},{6,4},{7,5},{8,10},{9,11},{10,... | collective-permute-start | bytes 294920 | tf_op jit(solution)/shard_map/ppermute | solution.py:24
  29.3 12.6 %collective-permute-start.10 = (bf16[128,128]{1,0:T(8,128)(2,1)S(1)}, bf16[128,128]{1,0:T(8,128)(2,1)S(1)}, u32[]{:S(2)}, u32[]{:S(2)}) collective-permute-start(bf16[128,128]{1,0:T(8,128)(2,1)S(1)} %get-tuple-element.50), channel_id=1, source_target_pairs={{0,0},{1,1},{2,2},{3,3},{4,8},{5,9},{6,10},{7,11},{8,16},{9,17},{1... | collective-permute-start | bytes 98312 | tf_op jit(solution)/shard_map/ppermute | solution.py:657
  30.0 11.9 %collective-permute-start.11 = (bf16[128,128]{1,0:T(8,128)(2,1)S(1)}, bf16[128,128]{1,0:T(8,128)(2,1)S(1)}, u32[]{:S(2)}, u32[]{:S(2)}) collective-permute-start(bf16[128,128]{1,0:T(8,128)(2,1)S(1)} %get-tuple-element.50), channel_id=1, source_target_pairs={{0,2},{1,3},{2,0},{3,1},{4,10},{5,11},{6,8},{7,9},{8,18},{9,19},{1... | collective-permute-start | bytes 98312 | tf_op jit(solution)/shard_map/ppermute | solution.py:657
  31.6 10.4 %collective-permute-start.12 = (bf16[128,128]{1,0:T(8,128)(2,1)S(1)}, bf16[128,128]{1,0:T(8,128)(2,1)S(1)}, u32[]{:S(2)}, u32[]{:S(2)}) collective-permute-start(bf16[128,128]{1,0:T(8,128)(2,1)S(1)} %get-tuple-element.51), channel_id=1, source_target_pairs={{0,4},{1,5},{2,6},{3,7},{4,12},{5,13},{6,14},{7,15},{8,20},{9,21},... | collective-permute-start | bytes 98312 | tf_op jit(solution)/shard_map/ppermute | solution.py:657
  35.6 1.6 %collective-permute-start.19 = (bf16[2,4,8,2048]{3,2,1,0:T(8,128)(2,1)S(1)}, bf16[2,4,8,2048]{3,2,1,0:T(8,128)(2,1)S(1)}, u32[]{:S(2)}, u32[]{:S(2)}) collective-permute-start(bf16[2,4,8,2048]{3,2,1,0:T(8,128)(2,1)S(1)} %shard_map.159), channel_id=1, source_target_pairs={{0,1},{1,0},{2,3},{3,2},{4,5},{5,4},{6,7},{7,6},{8,9},{9,8},{10,11... | collective-permute-start | bytes 786440 | tf_op jit(solution)/shard_map/ppermute | solution.py:24
  35.7 3.9 %collective-permute-start.14 = (bf16[2,4,8,2048]{3,2,1,0:T(8,128)(2,1)S(1)}, bf16[2,4,8,2048]{3,2,1,0:T(8,128)(2,1)S(1)}, u32[]{:S(2)}, u32[]{:S(2)}) collective-permute-start(bf16[2,4,8,2048]{3,2,1,0:T(8,128)(2,1)S(1)} %shard_map.155), channel_id=1, source_target_pairs={{0,1},{1,0},{2,3},{3,2},{4,5},{5,4},{6,7},{7,6},{8,9},{9,8},{10,11... | collective-permute-start | bytes 786440 | tf_op jit(solution)/shard_map/ppermute | solution.py:24
  37.2 5.7 %collective-permute-start.13 = (bf16[128,128]{1,0:T(8,128)(2,1)S(1)}, bf16[128,128]{1,0:T(8,128)(2,1)S(1)}, u32[]{:S(2)}, u32[]{:S(2)}) collective-permute-start(bf16[128,128]{1,0:T(8,128)(2,1)S(1)} %get-tuple-element.51), channel_id=1, source_target_pairs={{0,6},{1,7},{2,4},{3,5},{4,14},{5,15},{6,12},{7,13},{8,22},{9,23},... | collective-permute-start | bytes 98312 | tf_op jit(solution)/shard_map/ppermute | solution.py:657
  42.9 6.7 %copy-start.1 = (bf16[1024,2048]{1,0:T(8,128)(2,1)S(1)}, bf16[1024,2048]{1,0:T(8,128)(2,1)}, u32[]{:S(2)}) copy-start(bf16[1024,2048]{1,0:T(8,128)(2,1)} %refs_4_.2) | copy-start | bytes 12582916
  44.0 4.3 %collective-permute-start.21 = (bf16[32,1024]{1,0:T(8,128)(2,1)S(1)}, bf16[32,1024]{1,0:T(8,128)(2,1)S(1)}, u32[]{:S(2)}, u32[]{:S(2)}) collective-permute-start(bf16[32,1024]{1,0:T(8,128)(2,1)S(1)} %shard_map.161.refs_0_), channel_id=1, source_target_pairs={{0,2},{1,3},{2,0},{3,1},{4,6},{5,7},{6,4},{7,5},{8,10},{9,11},{10,... | collective-permute-start | bytes 196616 | tf_op jit(solution)/shard_map/ppermute | solution.py:24
  44.7 3.6 %collective-permute-start.20 = (bf16[32,1024]{1,0:T(8,128)(2,1)S(1)}, bf16[32,1024]{1,0:T(8,128)(2,1)S(1)}, u32[]{:S(2)}, u32[]{:S(2)}) collective-permute-start(bf16[32,1024]{1,0:T(8,128)(2,1)S(1)} %shard_map.161.refs_0_), channel_id=1, source_target_pairs={{0,1},{1,0},{2,3},{3,2},{4,5},{5,4},{6,7},{7,6},{8,9},{9,8},{10,11... | collective-permute-start | bytes 196616 | tf_op jit(solution)/shard_map/ppermute | solution.py:24
  48.4 1.3 %collective-permute-start.22 = (bf16[32,1024]{1,0:T(8,128)(2,1)S(1)}, bf16[32,1024]{1,0:T(8,128)(2,1)S(1)}, u32[]{:S(2)}, u32[]{:S(2)}) collective-permute-start(bf16[32,1024]{1,0:T(8,128)(2,1)S(1)} %collective-permute-done.21.refs_2_), channel_id=1, source_target_pairs={{0,1},{1,0},{2,3},{3,2},{4,5},{5,4},{6,7},{7,6},{8,9},{9,8},{10,11... | collective-permute-start | bytes 196616 | tf_op jit(solution)/shard_map/ppermute | solution.py:24
  50.9 5.1 %collective-permute-start.25 = (bf16[16,2048]{1,0:T(8,128)(2,1)S(1)}, bf16[16,2048]{1,0:T(8,128)(2,1)S(1)}, u32[]{:S(2)}, u32[]{:S(2)}) collective-permute-start(bf16[16,2048]{1,0:T(8,128)(2,1)S(1)} %get-tuple-element.64), channel_id=1, source_target_pairs={{0,4},{4,0},{8,12},{12,8},{16,20},{20,16},{24,28},{28,24},{1,5},{5... | collective-permute-start | bytes 196616 | tf_op jit(solution)/shard_map/ppermute | solution.py:24
  52.5 5.6 %collective-permute-start.23 = (bf16[16,2048]{1,0:T(8,128)(2,1)S(1)}, bf16[16,2048]{1,0:T(8,128)(2,1)S(1)}, u32[]{:S(2)}, u32[]{:S(2)}) collective-permute-start(bf16[16,2048]{1,0:T(8,128)(2,1)S(1)} %get-tuple-element.61), channel_id=1, source_target_pairs={{0,4},{4,0},{8,12},{12,8},{16,20},{20,16},{24,28},{28,24},{1,5},{5... | collective-permute-start | bytes 196616 | tf_op jit(solution)/shard_map/ppermute | solution.py:24
  53.0 8.2 %collective-permute-start.28 = (bf16[16,2048]{1,0:T(8,128)(2,1)S(1)}, bf16[16,2048]{1,0:T(8,128)(2,1)S(1)}, u32[]{:S(2)}, u32[]{:S(2)}) collective-permute-start(bf16[16,2048]{1,0:T(8,128)(2,1)S(1)} %get-tuple-element.66), channel_id=1, source_target_pairs={{0,8},{4,12},{8,0},{12,4},{16,24},{20,28},{24,16},{28,20},{1,9},{5... | collective-permute-start | bytes 196616 | tf_op jit(solution)/shard_map/ppermute | solution.py:24
  54.7 6.4 %collective-permute-start.29 = (bf16[16,2048]{1,0:T(8,128)(2,1)S(1)}, bf16[16,2048]{1,0:T(8,128)(2,1)S(1)}, u32[]{:S(2)}, u32[]{:S(2)}) collective-permute-start(bf16[16,2048]{1,0:T(8,128)(2,1)S(1)} %get-tuple-element.67), channel_id=1, source_target_pairs={{0,12},{4,8},{8,4},{12,0},{16,28},{20,24},{24,20},{28,16},{1,13},{... | collective-permute-start | bytes 196616 | tf_op jit(solution)/shard_map/ppermute | solution.py:24
  56.0 6.5 %collective-permute-start.26 = (bf16[16,2048]{1,0:T(8,128)(2,1)S(1)}, bf16[16,2048]{1,0:T(8,128)(2,1)S(1)}, u32[]{:S(2)}, u32[]{:S(2)}) collective-permute-start(bf16[16,2048]{1,0:T(8,128)(2,1)S(1)} %shard_map.164), channel_id=1, source_target_pairs={{0,24},{4,28},{8,16},{12,20},{16,8},{20,12},{24,0},{28,4},{1,25},{... | collective-permute-start | bytes 196616 | tf_op jit(solution)/shard_map/ppermute | solution.py:24
  58.1 19.7 %slice-start = ((s8[7340032]{0:T(1024)(128)(4,1)}), s8[4194304]{0:T(1024)(128)(4,1)S(1)}, s32[]{:S(2)}) async-start(s8[7340032]{0:T(1024)(128)(4,1)} %bitcast.12), calls=%async_computation | async-start | bytes 8388608
  58.1 6.9 %collective-permute-start.24 = (bf16[16,2048]{1,0:T(8,128)(2,1)S(1)}, bf16[16,2048]{1,0:T(8,128)(2,1)S(1)}, u32[]{:S(2)}, u32[]{:S(2)}) collective-permute-start(bf16[16,2048]{1,0:T(8,128)(2,1)S(1)} %get-tuple-element.63), channel_id=1, source_target_pairs={{0,16},{4,20},{8,24},{12,28},{16,0},{20,4},{24,8},{28,12},{1,17},{... | collective-permute-start | bytes 196616 | tf_op jit(solution)/shard_map/ppermute | solution.py:24
  59.4 18.4 %slice-start.1 = ((s8[7340032]{0:T(1024)(128)(4,1)}), s8[3145728]{0:T(1024)(128)(4,1)S(1)}, s32[]{:S(2)}) async-start(s8[7340032]{0:T(1024)(128)(4,1)} %bitcast.12), calls=%async_computation.1 | async-start | bytes 6291456
  59.4 5.6 %collective-permute-start.27 = (bf16[16,2048]{1,0:T(8,128)(2,1)S(1)}, bf16[16,2048]{1,0:T(8,128)(2,1)S(1)}, u32[]{:S(2)}, u32[]{:S(2)}) collective-permute-start(bf16[16,2048]{1,0:T(8,128)(2,1)S(1)} %get-tuple-element.65), channel_id=1, source_target_pairs={{0,4},{4,0},{8,12},{12,8},{16,20},{20,16},{24,28},{28,24},{1,5},{5... | collective-permute-start | bytes 196616 | tf_op jit(solution)/shard_map/ppermute | solution.py:24
  65.0 12.8 %copy-start.8 = (f32[2048]{0:T(1024)S(1)}, f32[2048]{0:T(1024)}, u32[]{:S(2)}) copy-start(f32[2048]{0:T(1024)} %param.20) | copy-start | bytes 24580
  65.0 14.7 %slice-start.2 = ((s8[7340032]{0:T(1024)(128)(4,1)}), s8[4194304]{0:T(1024)(128)(4,1)S(1)}, s32[]{:S(2)}) async-start(s8[7340032]{0:T(1024)(128)(4,1)} %bitcast.14), calls=%async_computation.2 | async-start | bytes 8388608
  65.7 7.2 %collective-permute-start.33 = (bf16[16,2048]{1,0:T(8,128)(2,1)S(1)}, bf16[16,2048]{1,0:T(8,128)(2,1)S(1)}, u32[]{:S(2)}, u32[]{:S(2)}) collective-permute-start(bf16[16,2048]{1,0:T(8,128)(2,1)S(1)} %get-tuple-element.69.refs_0_), channel_id=1, source_target_pairs={{0,16},{4,20},{8,24},{12,28},{16,0},{20,4},{24,8},{28,12},{1,17},{... | collective-permute-start | bytes 196616 | tf_op jit(solution)/shard_map/ppermute | solution.py:24
  66.1 6.8 %collective-permute-start.35 = (bf16[16,2048]{1,0:T(8,128)(2,1)S(1)}, bf16[16,2048]{1,0:T(8,128)(2,1)S(1)}, u32[]{:S(2)}, u32[]{:S(2)}) collective-permute-start(bf16[16,2048]{1,0:T(8,128)(2,1)S(1)} %get-tuple-element.69.refs_0_), channel_id=1, source_target_pairs={{0,24},{4,28},{8,16},{12,20},{16,8},{20,12},{24,0},{28,4},{1,25},{... | collective-permute-start | bytes 196616 | tf_op jit(solution)/shard_map/ppermute | solution.py:24
  67.9 7.0 %collective-permute-start.30 = (bf16[16,2048]{1,0:T(8,128)(2,1)S(1)}, bf16[16,2048]{1,0:T(8,128)(2,1)S(1)}, u32[]{:S(2)}, u32[]{:S(2)}) collective-permute-start(bf16[16,2048]{1,0:T(8,128)(2,1)S(1)} %get-tuple-element.69.refs_0_), channel_id=1, source_target_pairs={{0,4},{4,0},{8,12},{12,8},{16,20},{20,16},{24,28},{28,24},{1,5},{5... | collective-permute-start | bytes 196616 | tf_op jit(solution)/shard_map/ppermute | solution.py:24
  69.3 5.6 %collective-permute-start.31 = (bf16[16,2048]{1,0:T(8,128)(2,1)S(1)}, bf16[16,2048]{1,0:T(8,128)(2,1)S(1)}, u32[]{:S(2)}, u32[]{:S(2)}) collective-permute-start(bf16[16,2048]{1,0:T(8,128)(2,1)S(1)} %get-tuple-element.69.refs_0_), channel_id=1, source_target_pairs={{0,8},{4,12},{8,0},{12,4},{16,24},{20,28},{24,16},{28,20},{1,9},{5... | collective-permute-start | bytes 196616 | tf_op jit(solution)/shard_map/ppermute | solution.py:24
  69.9 5.2 %collective-permute-start.32 = (bf16[16,2048]{1,0:T(8,128)(2,1)S(1)}, bf16[16,2048]{1,0:T(8,128)(2,1)S(1)}, u32[]{:S(2)}, u32[]{:S(2)}) collective-permute-start(bf16[16,2048]{1,0:T(8,128)(2,1)S(1)} %get-tuple-element.69.refs_0_), channel_id=1, source_target_pairs={{0,12},{4,8},{8,4},{12,0},{16,28},{20,24},{24,20},{28,16},{1,13},{... | collective-permute-start | bytes 196616 | tf_op jit(solution)/shard_map/ppermute | solution.py:24
  72.9 4.3 %collective-permute-start.34 = (bf16[16,2048]{1,0:T(8,128)(2,1)S(1)}, bf16[16,2048]{1,0:T(8,128)(2,1)S(1)}, u32[]{:S(2)}, u32[]{:S(2)}) collective-permute-start(bf16[16,2048]{1,0:T(8,128)(2,1)S(1)} %collective-permute-done.33.refs_4_), channel_id=1, source_target_pairs={{0,4},{4,0},{8,12},{12,8},{16,20},{20,16},{24,28},{28,24},{1,5},{5... | collective-permute-start | bytes 196616 | tf_op jit(solution)/shard_map/ppermute | solution.py:24
  72.9 5.0 %collective-permute-start.36 = (bf16[16,2048]{1,0:T(8,128)(2,1)S(1)}, bf16[16,2048]{1,0:T(8,128)(2,1)S(1)}, u32[]{:S(2)}, u32[]{:S(2)}) collective-permute-start(bf16[16,2048]{1,0:T(8,128)(2,1)S(1)} %collective-permute-done.35.refs_6_), channel_id=1, source_target_pairs={{0,4},{4,0},{8,12},{12,8},{16,20},{20,16},{24,28},{28,24},{1,5},{5... | collective-permute-start | bytes 196616 | tf_op jit(solution)/shard_map/ppermute | solution.py:24
  77.9 17.8 %slice-start.4 = ((s8[7340032]{0:T(1024)(128)(4,1)}), s8[4194304]{0:T(1024)(128)(4,1)S(1)}, s32[]{:S(2)}) async-start(s8[7340032]{0:T(1024)(128)(4,1)} %bitcast.16), calls=%async_computation.4 | async-start | bytes 8388608
  79.7 1.8 %collective-permute-start.37 = (bf16[64,1920]{1,0:T(8,128)(2,1)S(1)}, bf16[64,1920]{1,0:T(8,128)(2,1)S(1)}, u32[]{:S(2)}, u32[]{:S(2)}) collective-permute-start(bf16[64,1920]{1,0:T(8,128)(2,1)S(1)} %get-tuple-element.71), channel_id=1, source_target_pairs={{0,1},{1,0},{2,3},{3,2},{4,5},{5,4},{6,7},{7,6},{8,9},{9,8},{10,11... | collective-permute-start | bytes 737288 | tf_op jit(solution)/shard_map/ppermute | solution.py:24
  79.8 15.9 %slice-start.5 = ((s8[7340032]{0:T(1024)(128)(4,1)}), s8[3145728]{0:T(1024)(128)(4,1)S(1)}, s32[]{:S(2)}) async-start(s8[7340032]{0:T(1024)(128)(4,1)} %bitcast.16), calls=%async_computation.5 | async-start | bytes 6291456
  80.9 1.6 %collective-permute-start.39 = (bf16[64,1792]{1,0:T(8,128)(2,1)S(1)}, bf16[64,1792]{1,0:T(8,128)(2,1)S(1)}, u32[]{:S(2)}, u32[]{:S(2)}) collective-permute-start(bf16[64,1792]{1,0:T(8,128)(2,1)S(1)} %get-tuple-element.74), channel_id=1, source_target_pairs={{0,1},{1,0},{2,3},{3,2},{4,5},{5,4},{6,7},{7,6},{8,9},{9,8},{10,11... | collective-permute-start | bytes 688136 | tf_op jit(solution)/shard_map/ppermute | solution.py:24
  81.6 6.2 %collective-permute-start.38 = (bf16[32,1920]{1,0:T(8,128)(2,1)S(1)}, bf16[32,1920]{1,0:T(8,128)(2,1)S(1)}, u32[]{:S(2)}, u32[]{:S(2)}) collective-permute-start(bf16[32,1920]{1,0:T(8,128)(2,1)S(1)} %slice.64), channel_id=1, source_target_pairs={{0,2},{1,3},{2,0},{3,1},{4,6},{5,7},{6,4},{7,5},{8,10},{9,11},{10,... | collective-permute-start | bytes 368648 | tf_op jit(solution)/shard_map/ppermute | solution.py:24
  82.7 6.7 %collective-permute-start.40 = (bf16[32,1792]{1,0:T(8,128)(2,1)S(1)}, bf16[32,1792]{1,0:T(8,128)(2,1)S(1)}, u32[]{:S(2)}, u32[]{:S(2)}) collective-permute-start(bf16[32,1792]{1,0:T(8,128)(2,1)S(1)} %slice.65), channel_id=1, source_target_pairs={{0,2},{1,3},{2,0},{3,1},{4,6},{5,7},{6,4},{7,5},{8,10},{9,11},{10,... | collective-permute-start | bytes 344072 | tf_op jit(solution)/shard_map/ppermute | solution.py:24
  89.5 4.9 %collective-permute-start.42 = (bf16[32,1792]{1,0:T(8,128)(2,1)S(1)}, bf16[32,1792]{1,0:T(8,128)(2,1)S(1)}, u32[]{:S(2)}, u32[]{:S(2)}) collective-permute-start(bf16[32,1792]{1,0:T(8,128)(2,1)S(1)} %fusion.2.refs_0_), channel_id=1, source_target_pairs={{0,2},{1,3},{2,0},{3,1},{4,6},{5,7},{6,4},{7,5},{8,10},{9,11},{10,... | collective-permute-start | bytes 344072 | tf_op jit(solution)/shard_map/ppermute | solution.py:24
  89.8 4.5 %collective-permute-start.41 = (bf16[32,1792]{1,0:T(8,128)(2,1)S(1)}, bf16[32,1792]{1,0:T(8,128)(2,1)S(1)}, u32[]{:S(2)}, u32[]{:S(2)}) collective-permute-start(bf16[32,1792]{1,0:T(8,128)(2,1)S(1)} %fusion.2.refs_0_), channel_id=1, source_target_pairs={{0,1},{1,0},{2,3},{3,2},{4,5},{5,4},{6,7},{7,6},{8,9},{9,8},{10,11... | collective-permute-start | bytes 344072 | tf_op jit(solution)/shard_map/ppermute | solution.py:24
  94.4 1.3 %collective-permute-start.43 = (bf16[32,1792]{1,0:T(8,128)(2,1)S(1)}, bf16[32,1792]{1,0:T(8,128)(2,1)S(1)}, u32[]{:S(2)}, u32[]{:S(2)}) collective-permute-start(bf16[32,1792]{1,0:T(8,128)(2,1)S(1)} %collective-permute-done.42.refs_2_), channel_id=1, source_target_pairs={{0,1},{1,0},{2,3},{3,2},{4,5},{5,4},{6,7},{7,6},{8,9},{9,8},{10,11... | collective-permute-start | bytes 344072 | tf_op jit(solution)/shard_map/ppermute | solution.py:24
  97.4 4.9 %collective-permute-start.46 = (bf16[16,2048]{1,0:T(8,128)(2,1)S(1)}, bf16[16,2048]{1,0:T(8,128)(2,1)S(1)}, u32[]{:S(2)}, u32[]{:S(2)}) collective-permute-start(bf16[16,2048]{1,0:T(8,128)(2,1)S(1)} %get-tuple-element.80), channel_id=1, source_target_pairs={{0,4},{4,0},{8,12},{12,8},{16,20},{20,16},{24,28},{28,24},{1,5},{5... | collective-permute-start | bytes 196616 | tf_op jit(solution)/shard_map/ppermute | solution.py:24
  98.8 5.4 %collective-permute-start.44 = (bf16[16,2048]{1,0:T(8,128)(2,1)S(1)}, bf16[16,2048]{1,0:T(8,128)(2,1)S(1)}, u32[]{:S(2)}, u32[]{:S(2)}) collective-permute-start(bf16[16,2048]{1,0:T(8,128)(2,1)S(1)} %get-tuple-element.77), channel_id=1, source_target_pairs={{0,4},{4,0},{8,12},{12,8},{16,20},{20,16},{24,28},{28,24},{1,5},{5... | collective-permute-start | bytes 196616 | tf_op jit(solution)/shard_map/ppermute | solution.py:24
  99.5 6.3 %collective-permute-start.49 = (bf16[16,2048]{1,0:T(8,128)(2,1)S(1)}, bf16[16,2048]{1,0:T(8,128)(2,1)S(1)}, u32[]{:S(2)}, u32[]{:S(2)}) collective-permute-start(bf16[16,2048]{1,0:T(8,128)(2,1)S(1)} %get-tuple-element.82), channel_id=1, source_target_pairs={{0,8},{4,12},{8,0},{12,4},{16,24},{20,28},{24,16},{28,20},{1,9},{5... | collective-permute-start | bytes 196616 | tf_op jit(solution)/shard_map/ppermute | solution.py:24
  100.2 5.5 %collective-permute-start.50 = (bf16[16,2048]{1,0:T(8,128)(2,1)S(1)}, bf16[16,2048]{1,0:T(8,128)(2,1)S(1)}, u32[]{:S(2)}, u32[]{:S(2)}) collective-permute-start(bf16[16,2048]{1,0:T(8,128)(2,1)S(1)} %get-tuple-element.83), channel_id=1, source_target_pairs={{0,12},{4,8},{8,4},{12,0},{16,28},{20,24},{24,20},{28,16},{1,13},{... | collective-permute-start | bytes 196616 | tf_op jit(solution)/shard_map/ppermute | solution.py:24
  102.3 6.3 %collective-permute-start.47 = (bf16[16,2048]{1,0:T(8,128)(2,1)S(1)}, bf16[16,2048]{1,0:T(8,128)(2,1)S(1)}, u32[]{:S(2)}, u32[]{:S(2)}) collective-permute-start(bf16[16,2048]{1,0:T(8,128)(2,1)S(1)} %shard_map.170), channel_id=1, source_target_pairs={{0,24},{4,28},{8,16},{12,20},{16,8},{20,12},{24,0},{28,4},{1,25},{... | collective-permute-start | bytes 196616 | tf_op jit(solution)/shard_map/ppermute | solution.py:24
  104.2 6.6 %collective-permute-start.45 = (bf16[16,2048]{1,0:T(8,128)(2,1)S(1)}, bf16[16,2048]{1,0:T(8,128)(2,1)S(1)}, u32[]{:S(2)}, u32[]{:S(2)}) collective-permute-start(bf16[16,2048]{1,0:T(8,128)(2,1)S(1)} %get-tuple-element.79), channel_id=1, source_target_pairs={{0,16},{4,20},{8,24},{12,28},{16,0},{20,4},{24,8},{28,12},{1,17},{... | collective-permute-start | bytes 196616 | tf_op jit(solution)/shard_map/ppermute | solution.py:24
  104.7 6.2 %collective-permute-start.48 = (bf16[16,2048]{1,0:T(8,128)(2,1)S(1)}, bf16[16,2048]{1,0:T(8,128)(2,1)S(1)}, u32[]{:S(2)}, u32[]{:S(2)}) collective-permute-start(bf16[16,2048]{1,0:T(8,128)(2,1)S(1)} %get-tuple-element.81), channel_id=1, source_target_pairs={{0,4},{4,0},{8,12},{12,8},{16,20},{20,16},{24,28},{28,24},{1,5},{5... | collective-permute-start | bytes 196616 | tf_op jit(solution)/shard_map/ppermute | solution.py:24
  (4 other events, 7.4 us)

commit v15 on v14

--- a/solution.py
+++ b/solution.py
@@ -180,15 +180,18 @@
     return [block] + [swap(block, "tensor", k) for k in range(2, lax.axis_size("tensor"), 2)]
 
 
-def cross_cores(blocks, after):
+def cross_cores(near, far, after):
+    close, span, wide = near[0].shape
+    total = close + far[0].shape[0]
+
     def body(after_ref, *refs):
-        for i, ref in enumerate(refs[:-1]):
-            refs[-1][i] = ref[...]
-
-    ins = (after, *blocks)
-    shape = (len(blocks),) + blocks[0].shape
-    both = call(body, shaped(shape), ins, [ANY] + [VMEM] * len(blocks), around=0)
-    return [*blocks, swap(both, "tensor", 1)]
+        for i in range(len(near)):
+            refs[-1][i, :close] = refs[i][...]
+            refs[-1][i, close:] = refs[len(near) + i][...]
+
+    ins = (after, *near, *far)
+    even = call(body, shaped((len(near), total, span, wide)), ins, [ANY] + [VMEM] * (2 * len(near)), around=0)
+    return even, swap(even, "tensor", 1)
 
 
 def last_entries(pieces, after):
@@ -510,12 +513,12 @@
     return call(body, outs, ins, [VMEM] * len(ins), moved=8 * own.size)
 
 
-def attend_cached(where, anc, rope, scale, queries, near_cache, far_cache, part_dev):
+def attend_cached(where, anc, rope, scale, queries, cache, part_dev):
     tensor = lax.axis_size("tensor")
     groups = lax.axis_size("dp")
     near = groups // tensor
     pair = 2 * part_dev
-    close, span, _ = near_cache[0].shape
+    span = cache[0].shape[2]
     ctx = tensor * span
     height, columns = queries[0].shape
     heads = columns // HD
@@ -524,10 +527,8 @@
 
     def body(where_ref, anc_ref, rope_ref, scale_ref, *refs):
         q_refs, refs = refs[: len(queries)], refs[len(queries) :]
-        count = tensor // 2 + 1
-        near_refs, far_refs = refs[:count], refs[count : 2 * count]
-        near_refs, far_refs = [(*part[:-1], *[part[-1].at[i] for i in range(count - 1)]) for part in (near_refs, far_refs)]
-        query_ref, mixed_ref, highest_ref, total_ref, keys_ref, values_ref = refs[2 * count :]
+        cache_refs = [ref.at[i] for ref in refs[:2] for i in range(tensor // 2)]
+        query_ref, mixed_ref, highest_ref, total_ref, keys_ref, values_ref = refs[2:]
         d, t = where_ref[0], where_ref[1]
         query_sum = q_refs[0][...]
         for ref in q_refs[1:]:
@@ -543,22 +544,12 @@
                 particle = t * parts + i if step == 0 else anc_ref[i]
                 block, member = lax.div(particle, part_dev) ^ d, lax.rem(particle, part_dev)
 
-                def load(cache_refs, entry):
-                    for k, cache_ref in enumerate(cache_refs):
-                        to = pl.ds(pl.multiple_of(i * ctx + k * span, 8), span)
-                        lanes = pl.ds(pl.multiple_of(member * HD, HD), HD)
-                        keys_ref[to, :] = cache_ref[entry, :, lanes].astype(F32)
-                        lanes = pl.ds(pl.multiple_of((part_dev + member) * HD, HD), HD)
-                        values_ref[to, :] = cache_ref[entry, :, lanes].astype(F32)
-
-                @pl.when(block < close)
-                def _():
-                    load(near_refs, block)
-
-                @pl.when(block >= close)
-                def _():
-                    load(far_refs, block - close)
-
+                for k, cache_ref in enumerate(cache_refs):
+                    to = pl.ds(pl.multiple_of(i * ctx + k * span, 8), span)
+                    lanes = pl.ds(pl.multiple_of(member * HD, HD), HD)
+                    keys_ref[to, :] = cache_ref[block, :, lanes].astype(F32)
+                    lanes = pl.ds(pl.multiple_of((part_dev + member) * HD, HD), HD)
+                    values_ref[to, :] = cache_ref[block, :, lanes].astype(F32)
                 return 0
 
             lax.fori_loop(0, parts, bring, 0)
@@ -586,7 +577,7 @@
             highest_ref[here, :] = jnp.broadcast_to(highest, (rows, 128))
             total_ref[here, :] = jnp.broadcast_to(jnp.sum(weights, axis=1, keepdims=True), (rows, 128))
 
-    ins = (where, anc, rope, scale, *queries, *near_cache, *far_cache)
+    ins = (where, anc, rope, scale, *queries, *cache)
     return call(
         body,
         (shaped((2 * rows, HD)), shaped((2 * rows, HD), F32), shaped((2 * rows, 128), F32), shaped((2 * rows, 128), F32)),
@@ -727,8 +718,7 @@
         pieces = move_keyvals(pieces)
         queries = [queries] + [swap(piece, "tensor", 2 * i) for i, piece in enumerate(leaving, 1)]
 
-    near_cache = cross_cores(near_cache, arrived)
-    far_cache = cross_cores(far_cache, arrived)
+    cache = cross_cores(near_cache, far_cache, pieces[1] if direct_keyvals() else arrived)
 
     own = t * parts + jnp.arange(parts, dtype=jnp.int32)
     anc = lax.dynamic_slice_in_dim(ancestors, t * parts, parts).astype(jnp.int32)
@@ -741,7 +731,7 @@
     second = jnp.stack([row_of(anc, 0), row_of(own, 1)], axis=1)
     targets = jnp.concatenate([jnp.tile(first, (heads, 1)), jnp.tile(second, (heads, 1))]).astype(jnp.int32)
     rope = jnp.asarray(np.stack(rope_tables(context) + rope_tables(context + 1)))
-    state = attend_cached(where, anc, rope, scale, queries, near_cache, far_cache, part_dev)
+    state = attend_cached(where, anc, rope, scale, queries, cache, part_dev)
     mixed = attend_new(where, rope, targets, scale, pieces, state, queries[0].shape, part_dev)
 
     parts = project_back(where, gather_blocks(mixed), w_out)

time: 112 us -> 113 us (level)
  starting transfers between devices: 58.3 us -> 59.8 us
    ppermute x4, waiting for transfers between devices: 0.93 us -> 2.62 us  [send_keyvals(): moved.append(lax.ppermute(piece, ('dp', 'tensor'), pairs))]
    ppermute x47 -> x46, waiting for transfers between devices: 34.2 us -> 32.7 us  [swap(): return lax.ppermute(x, axis, [(i, i ^ bits) for i in range(size)])]
    ppermute x47 -> x46, starting transfers between devices: 49.7 us -> 51.1 us  [swap(): return lax.ppermute(x, axis, [(i, i ^ bits) for i in range(size)])]
    pallas_call x23 -> x22, Pallas kernels: 14.5 us -> 14 us  [call(): pl.pallas_call(body, out_shape=outs, in_specs=specs, out_specs=jax.tree.m...]
  transfers between devices with their start and end apart: 51 -> 50, of which waited for: 20 -> 23; matrix products, arithmetic and copies ran while one was open for 1% -> 1% of each run, Pallas kernels for 6% -> 6%
where the time goes in v15:
time: 113 us
  starting transfers between devices  59.8 us (53%)
  waiting for transfers between devices  35.3 us (31%)
  Pallas kernels  14 us (12%)
  local copies, waits for them, and re-layouts  1.97 us (2%)
    ppermute x46, starting transfers between devices, swap(): return lax.ppermute(x, axis, [(i, i ^ bits) for i in range(size)])  51.1 us
    ppermute x46, waiting for transfers between devices, swap(): return lax.ppermute(x, axis, [(i, i ^ bits) for i in range(size)])  32.7 us
    pallas_call x22, Pallas kernels, call(): pl.pallas_call(body, out_shape=outs, in_specs=specs, out_specs=jax.tree.m...  14 us
    ppermute x4, starting transfers between devices, send_keyvals(): moved.append(lax.ppermute(piece, ('dp', 'tensor'), pairs))  8.62 us
    ppermute x4, waiting for transfers between devices, send_keyvals(): moved.append(lax.ppermute(piece, ('dp', 'tensor'), pairs))  2.62 us
  transfers between devices with their start and end apart: 50, of which 23 were waited for; matrix products, arithmetic and copies ran while one was open for 1% of the time, Pallas kernels for 6%

profile of v15, /device:TPU:0, one launch (start us, length us, event | category | flops | bytes accessed | tf_op | source)
XLA Modules:
  0.0 112.8 jit_solution(2628265952865203133)
XLA Ops:
  0.7 0.8 copy-done.5
  1.5 0.8 copy-done.6
  2.2 4.0 %collective-permute-start.3 = (bf16[16,2048]{1,0:T(8,128)(2,1)S(1)}, bf16[16,2048]{1,0:T(8,128)(2,1)S(1)}, u32[]{:S(2)}, u32[]{:S(2)}) collective-permute-start(bf16[16,2048]{1,0:T(8,128)(2,1)S(1)} %shard_map.149.x_ref.refs_0_.refs_10_.after_ref.refs_5_), channel_id=1, source_target_pairs={{0,16},{4,20},{8,24},{12,28},{16,0},{20,4},{24,8},{28,12},{1,17},{... | collective-permute-start | bytes 196616 | tf_op jit(solution)/shard_map/ppermute | solution.py:24
  6.3 1.3 %collective-permute-start.5 = (bf16[16,2048]{1,0:T(8,128)(2,1)S(1)}, bf16[16,2048]{1,0:T(8,128)(2,1)S(1)}, u32[]{:S(2)}, u32[]{:S(2)}) collective-permute-start(bf16[16,2048]{1,0:T(8,128)(2,1)S(1)} %shard_map.149.x_ref.refs_0_.refs_10_.after_ref.refs_5_), channel_id=1, source_target_pairs={{0,24},{4,28},{8,16},{12,20},{16,8},{20,12},{24,0},{28,4},{1,25},{... | collective-permute-start | bytes 196616 | tf_op jit(solution)/shard_map/ppermute | solution.py:24
  8.3 1.6 %collective-permute-start = (bf16[24,2048]{1,0:T(8,128)(2,1)S(1)}, bf16[24,2048]{1,0:T(8,128)(2,1)S(1)}, u32[]{:S(2)}, u32[]{:S(2)}) collective-permute-start(bf16[24,2048]{1,0:T(8,128)(2,1)S(1)} %get-tuple-element.43), channel_id=1, source_target_pairs={{0,4},{4,0},{8,12},{12,8},{16,20},{20,16},{24,28},{28,24},{1,5},{5... | collective-permute-start | bytes 294920 | tf_op jit(solution)/shard_map/ppermute | solution.py:24
  10.1 1.8 %collective-permute-start.2 = (bf16[24,2048]{1,0:T(8,128)(2,1)S(1)}, bf16[24,2048]{1,0:T(8,128)(2,1)S(1)}, u32[]{:S(2)}, u32[]{:S(2)}) collective-permute-start(bf16[24,2048]{1,0:T(8,128)(2,1)S(1)} %get-tuple-element.45), channel_id=1, source_target_pairs={{0,12},{4,8},{8,4},{12,0},{16,28},{20,24},{24,20},{28,16},{1,13},{... | collective-permute-start | bytes 294920 | tf_op jit(solution)/shard_map/ppermute | solution.py:24
  13.1 2.8 %collective-permute-start.14 = (bf16[2,8,2048]{2,1,0:T(8,128)(2,1)S(1)}, bf16[2,8,2048]{2,1,0:T(8,128)(2,1)S(1)}, u32[]{:S(2)}, u32[]{:S(2)}) collective-permute-start(bf16[2,8,2048]{2,1,0:T(8,128)(2,1)S(1)} %get-tuple-element.53), channel_id=1, source_target_pairs={{0,16},{4,20},{8,24},{12,28},{16,0},{20,4},{24,8},{28,12},{1,17},{... | collective-permute-start | bytes 196616 | tf_op jit(solution)/shard_map/ppermute | solution.py:24
  16.3 1.6 %collective-permute-start.4 = (bf16[16,2048]{1,0:T(8,128)(2,1)S(1)}, bf16[16,2048]{1,0:T(8,128)(2,1)S(1)}, u32[]{:S(2)}, u32[]{:S(2)}) collective-permute-start(bf16[16,2048]{1,0:T(8,128)(2,1)S(1)} %collective-permute-done.3.refs_4_.refs_0_), channel_id=1, source_target_pairs={{0,4},{4,0},{8,12},{12,8},{16,20},{20,16},{24,28},{28,24},{1,5},{5... | collective-permute-start | bytes 196616 | tf_op jit(solution)/shard_map/ppermute | solution.py:24
  18.4 1.8 %collective-permute-start.8 = (bf16[4,8,2048]{2,1,0:T(8,128)(2,1)S(1)}, bf16[4,8,2048]{2,1,0:T(8,128)(2,1)S(1)}, u32[]{:S(2)}, u32[]{:S(2)}) collective-permute-start(bf16[4,8,2048]{2,1,0:T(8,128)(2,1)S(1)} %shard_map.152.refs_0_), channel_id=1, source_target_pairs={{0,2},{1,3},{2,0},{3,1},{4,6},{5,7},{6,4},{7,5},{8,10},{9,11},{10,... | collective-permute-start | bytes 393224 | tf_op jit(solution)/shard_map/ppermute | solution.py:24
  20.2 1.8 %collective-permute-done.15.refs_1_ = bf16[2,8,2048]{2,1,0:T(8,128)(2,1)S(1)} collective-permute-done((bf16[2,8,2048]{2,1,0:T(8,128)(2,1)S(1)}, bf16[2,8,2048]{2,1,0:T(8,128)(2,1)S(1)}, u32[]{:S(2)}, u32[]{:S(2)}) %collective-permute-start.15) | collective-permute-done | bytes 65568 | tf_op jit(solution)/shard_map/ppermute | solution.py:24
  22.0 1.5 %collective-permute-start.16 = (bf16[2,8,2048]{2,1,0:T(8,128)(2,1)S(1)}, bf16[2,8,2048]{2,1,0:T(8,128)(2,1)S(1)}, u32[]{:S(2)}, u32[]{:S(2)}) collective-permute-start(bf16[2,8,2048]{2,1,0:T(8,128)(2,1)S(1)} %shard_map.156), channel_id=1, source_target_pairs={{0,4},{4,0},{8,12},{12,8},{16,20},{20,16},{24,28},{28,24},{1,5},{5... | collective-permute-start | bytes 196616 | tf_op jit(solution)/shard_map/ppermute | solution.py:24
  23.6 1.5 %shard_map.151 = (bf16[128,896]{1,0:T(8,128)(2,1)S(1)}, f32[64,1024]{1,0:T(8,128)S(1)}) custom-call(s32[2]{0:T(128)S(1)} %pad_add_fusion.3.where_ref, f32[1,2048]{1,0:T(1,128)S(1)} %bitcast.18, bf16[16,2048]{1,0:T(8,128)(2,1)S(1)} %shard_map.149.x_ref.refs_0_.refs_10_.after_ref.refs_5_, bf16[24,2048]{1,0:T(8,128)(2,1)S(1)} %collective-permute-done.refs_1_.refs_0_, ...), custom_call_target="tpu_custom_call" | custom-call | flops 6039797760 | bytes 6291456 | tf_op jit(solution)/shard_map/pallas_call | solution.py:45
  25.2 1.1 collective-permute-done.16.refs_2_
  26.3 1.6 %collective-permute-start.17 = (bf16[4,8,2048]{2,1,0:T(8,128)(2,1)S(1)}, bf16[4,8,2048]{2,1,0:T(8,128)(2,1)S(1)}, u32[]{:S(2)}, u32[]{:S(2)}) collective-permute-start(bf16[4,8,2048]{2,1,0:T(8,128)(2,1)S(1)} %shard_map.157.refs_2_), channel_id=1, source_target_pairs={{0,2},{1,3},{2,0},{3,1},{4,6},{5,7},{6,4},{7,5},{8,10},{9,11},{10,... | collective-permute-start | bytes 393224 | tf_op jit(solution)/shard_map/ppermute | solution.py:24
  27.9 0.7 shard_map.153
  29.4 1.5 %collective-permute-start.9 = (bf16[128,384]{1,0:T(8,128)(2,1)S(1)}, bf16[128,384]{1,0:T(8,128)(2,1)S(1)}, u32[]{:S(2)}, u32[]{:S(2)}) collective-permute-start(bf16[128,384]{1,0:T(8,128)(2,1)S(1)} %get-tuple-element.49.own_ref), channel_id=1, source_target_pairs={{0,2},{1,3},{2,0},{3,1},{4,6},{5,7},{6,4},{7,5},{8,10},{9,11},{10,... | collective-permute-start | bytes 294920 | tf_op jit(solution)/shard_map/ppermute | solution.py:24
  30.9 0.8 collective-permute-done.17.refs_3_
  31.7 1.2 %collective-permute-done.11.after_ref.refs_1_ = bf16[128,128]{1,0:T(8,128)(2,1)S(1)} collective-permute-done((bf16[128,128]{1,0:T(8,128)(2,1)S(1)}, bf16[128,128]{1,0:T(8,128)(2,1)S(1)}, u32[]{:S(2)}, u32[]{:S(2)}) %collective-permute-start.11) | collective-permute-done | bytes 32800 | tf_op jit(solution)/shard_map/ppermute | solution.py:648
  33.8 5.3 %collective-permute-start.12 = (bf16[128,128]{1,0:T(8,128)(2,1)S(1)}, bf16[128,128]{1,0:T(8,128)(2,1)S(1)}, u32[]{:S(2)}, u32[]{:S(2)}) collective-permute-start(bf16[128,128]{1,0:T(8,128)(2,1)S(1)} %get-tuple-element.51), channel_id=1, source_target_pairs={{0,4},{1,5},{2,6},{3,7},{4,12},{5,13},{6,14},{7,15},{8,20},{9,21},... | collective-permute-start | bytes 98312 | tf_op jit(solution)/shard_map/ppermute | solution.py:648
  39.1 2.1 %collective-permute-start.13 = (bf16[128,128]{1,0:T(8,128)(2,1)S(1)}, bf16[128,128]{1,0:T(8,128)(2,1)S(1)}, u32[]{:S(2)}, u32[]{:S(2)}) collective-permute-start(bf16[128,128]{1,0:T(8,128)(2,1)S(1)} %get-tuple-element.51), channel_id=1, source_target_pairs={{0,6},{1,7},{2,4},{3,5},{4,14},{5,15},{6,12},{7,13},{8,22},{9,23},... | collective-permute-start | bytes 98312 | tf_op jit(solution)/shard_map/ppermute | solution.py:648
  41.4 1.9 %shard_map.159 = (bf16[256,128]{1,0:T(8,128)(2,1)S(1)}, f32[256,128]{1,0:T(8,128)S(1)}, f32[256,128]{1,0:T(8,128)S(1)}, f32[256,128]{1,0:T(8,128)S(1)}) custom-call(s32[2]{0:T(128)S(1)} %pad_add_fusion.3.where_ref, s32[16]{0:T(128)S(1)} %get-tuple-element.85.anc_ref, f32[4,128]{1,0:T(4,128)S(1)} %copy-done.9, f32[128,128]{1,0:T(8,128)S(1)} %shard_map.154.scale_ref, ...), custom_call_target="tpu_custom_call" | custom-call | flops 5368709120 | bytes 4194304 | tf_op jit(solution)/shard_map/pallas_call | solution.py:45
  43.3 0.8 collective-permute-done.12.refs_2_
  44.8 1.1 %shard_map.160.refs_0_ = bf16[32,1024]{1,0:T(8,128)(2,1)S(1)} custom-call(s32[2]{0:T(128)S(1)} %pad_add_fusion.3.where_ref, f32[4,128]{1,0:T(4,128)S(1)} %copy-done.9, s32[256,2]{1,0:T(8,128)S(1)} %copy.20.target_ref, f32[128,128]{1,0:T(8,128)S(1)} %shard_map.154.scale_ref, bf16[128,128]{1,0:T(8,128)(2,1)S(1)} %collective-permute-done.10.refs_0_, ...), custom_call_target="tpu_custom_call" | custom-call | flops 5368709120 | bytes 1048576 | tf_op jit(solution)/shard_map/pallas_call | solution.py:45
  45.9 1.2 %collective-permute-start.20 = (bf16[32,1024]{1,0:T(8,128)(2,1)S(1)}, bf16[32,1024]{1,0:T(8,128)(2,1)S(1)}, u32[]{:S(2)}, u32[]{:S(2)}) collective-permute-start(bf16[32,1024]{1,0:T(8,128)(2,1)S(1)} %shard_map.160.refs_0_), channel_id=1, source_target_pairs={{0,2},{1,3},{2,0},{3,1},{4,6},{5,7},{6,4},{7,5},{8,10},{9,11},{10,... | collective-permute-start | bytes 196616 | tf_op jit(solution)/shard_map/ppermute | solution.py:24
  47.2 3.1 %collective-permute-done.20.refs_2_ = bf16[32,1024]{1,0:T(8,128)(2,1)S(1)} collective-permute-done((bf16[32,1024]{1,0:T(8,128)(2,1)S(1)}, bf16[32,1024]{1,0:T(8,128)(2,1)S(1)}, u32[]{:S(2)}, u32[]{:S(2)}) %collective-permute-start.20) | collective-permute-done | bytes 65568 | tf_op jit(solution)/shard_map/ppermute | solution.py:24
  50.3 1.2 %collective-permute-done.21.refs_3_ = bf16[32,1024]{1,0:T(8,128)(2,1)S(1)} collective-permute-done((bf16[32,1024]{1,0:T(8,128)(2,1)S(1)}, bf16[32,1024]{1,0:T(8,128)(2,1)S(1)}, u32[]{:S(2)}, u32[]{:S(2)}) %collective-permute-start.21) | collective-permute-done | bytes 65568 | tf_op jit(solution)/shard_map/ppermute | solution.py:24
  51.5 1.3 %shard_map.161 = (f32[16,2048]{1,0:T(8,128)S(1)}, bf16[16,2048]{1,0:T(8,128)(2,1)S(1)}, bf16[16,2048]{1,0:T(8,128)(2,1)S(1)}, bf16[16,2048]{1,0:T(8,128)(2,1)S(1...) custom-call(s32[2]{0:T(128)S(1)} %pad_add_fusion.3.where_ref, ...), custom_call_target="tpu_custom_call" | custom-call | flops 5905580032 | bytes 4194304 | tf_op jit(solution)/shard_map/pallas_call | solution.py:45
  52.8 1.3 %collective-permute-start.24 = (bf16[16,2048]{1,0:T(8,128)(2,1)S(1)}, bf16[16,2048]{1,0:T(8,128)(2,1)S(1)}, u32[]{:S(2)}, u32[]{:S(2)}) collective-permute-start(bf16[16,2048]{1,0:T(8,128)(2,1)S(1)} %get-tuple-element.64), channel_id=1, source_target_pairs={{0,4},{4,0},{8,12},{12,8},{16,20},{20,16},{24,28},{28,24},{1,5},{5... | collective-permute-start | bytes 196616 | tf_op jit(solution)/shard_map/ppermute | solution.py:24
  54.1 0.8 collective-permute-start.22
  55.4 2.2 %collective-permute-start.28 = (bf16[16,2048]{1,0:T(8,128)(2,1)S(1)}, bf16[16,2048]{1,0:T(8,128)(2,1)S(1)}, u32[]{:S(2)}, u32[]{:S(2)}) collective-permute-start(bf16[16,2048]{1,0:T(8,128)(2,1)S(1)} %get-tuple-element.67), channel_id=1, source_target_pairs={{0,12},{4,8},{8,4},{12,0},{16,28},{20,24},{24,20},{28,16},{1,13},{... | collective-permute-start | bytes 196616 | tf_op jit(solution)/shard_map/ppermute | solution.py:24
  57.8 3.0 %collective-permute-start.25 = (bf16[16,2048]{1,0:T(8,128)(2,1)S(1)}, bf16[16,2048]{1,0:T(8,128)(2,1)S(1)}, u32[]{:S(2)}, u32[]{:S(2)}) collective-permute-start(bf16[16,2048]{1,0:T(8,128)(2,1)S(1)} %shard_map.163), channel_id=1, source_target_pairs={{0,24},{4,28},{8,16},{12,20},{16,8},{20,12},{24,0},{28,4},{1,25},{... | collective-permute-start | bytes 196616 | tf_op jit(solution)/shard_map/ppermute | solution.py:24
  60.9 0.7 collective-permute-start.26
  61.6 2.4 %collective-permute-done.25.refs_1_ = bf16[16,2048]{1,0:T(8,128)(2,1)S(1)} collective-permute-done((bf16[16,2048]{1,0:T(8,128)(2,1)S(1)}, bf16[16,2048]{1,0:T(8,128)(2,1)S(1)}, u32[]{:S(2)}, u32[]{:S(2)}) %collective-permute-start.25) | collective-permute-done | bytes 65568 | tf_op jit(solution)/shard_map/ppermute | solution.py:24
  64.0 2.0 %collective-permute-done.23.refs_0_ = bf16[16,2048]{1,0:T(8,128)(2,1)S(1)} collective-permute-done((bf16[16,2048]{1,0:T(8,128)(2,1)S(1)}, bf16[16,2048]{1,0:T(8,128)(2,1)S(1)}, u32[]{:S(2)}, u32[]{:S(2)}) %collective-permute-start.23) | collective-permute-done | bytes 65568 | tf_op jit(solution)/shard_map/ppermute | solution.py:24
  66.0 0.7 shard_map.164
  66.7 2.0 %collective-permute-start.32 = (bf16[16,2048]{1,0:T(8,128)(2,1)S(1)}, bf16[16,2048]{1,0:T(8,128)(2,1)S(1)}, u32[]{:S(2)}, u32[]{:S(2)}) collective-permute-start(bf16[16,2048]{1,0:T(8,128)(2,1)S(1)} %get-tuple-element.69.refs_0_), channel_id=1, source_target_pairs={{0,16},{4,20},{8,24},{12,28},{16,0},{20,4},{24,8},{28,12},{1,17},{... | collective-permute-start | bytes 196616 | tf_op jit(solution)/shard_map/ppermute | solution.py:24
  68.7 1.3 %collective-permute-start.34 = (bf16[16,2048]{1,0:T(8,128)(2,1)S(1)}, bf16[16,2048]{1,0:T(8,128)(2,1)S(1)}, u32[]{:S(2)}, u32[]{:S(2)}) collective-permute-start(bf16[16,2048]{1,0:T(8,128)(2,1)S(1)} %get-tuple-element.69.refs_0_), channel_id=1, source_target_pairs={{0,24},{4,28},{8,16},{12,20},{16,8},{20,12},{24,0},{28,4},{1,25},{... | collective-permute-start | bytes 196616 | tf_op jit(solution)/shard_map/ppermute | solution.py:24
  70.0 0.8 collective-permute-start.29
  71.0 2.5 %collective-permute-start.31 = (bf16[16,2048]{1,0:T(8,128)(2,1)S(1)}, bf16[16,2048]{1,0:T(8,128)(2,1)S(1)}, u32[]{:S(2)}, u32[]{:S(2)}) collective-permute-start(bf16[16,2048]{1,0:T(8,128)(2,1)S(1)} %get-tuple-element.69.refs_0_), channel_id=1, source_target_pairs={{0,12},{4,8},{8,4},{12,0},{16,28},{20,24},{24,20},{28,16},{1,13},{... | collective-permute-start | bytes 196616 | tf_op jit(solution)/shard_map/ppermute | solution.py:24
  73.5 0.8 collective-permute-start.33
  74.3 0.8 collective-permute-done.34.refs_6_
  75.1 1.0 collective-permute-start.35
  76.1 0.7 collective-permute-done.31.refs_3_
  76.8 1.4 %collective-permute-done.33.refs_5_ = bf16[16,2048]{1,0:T(8,128)(2,1)S(1)} collective-permute-done((bf16[16,2048]{1,0:T(8,128)(2,1)S(1)}, bf16[16,2048]{1,0:T(8,128)(2,1)S(1)}, u32[]{:S(2)}, u32[]{:S(2)}) %collective-permute-start.33) | collective-permute-done | bytes 65568 | tf_op jit(solution)/shard_map/ppermute | solution.py:24
  78.1 1.3 %collective-permute-done.35.refs_7_ = bf16[16,2048]{1,0:T(8,128)(2,1)S(1)} collective-permute-done((bf16[16,2048]{1,0:T(8,128)(2,1)S(1)}, bf16[16,2048]{1,0:T(8,128)(2,1)S(1)}, u32[]{:S(2)}, u32[]{:S(2)}) %collective-permute-start.35) | collective-permute-done | bytes 65568 | tf_op jit(solution)/shard_map/ppermute | solution.py:24
  79.4 1.8 %shard_map.165 = (bf16[128,2048]{1,0:T(8,128)(2,1)S(1)}, f32[64,1920]{1,0:T(8,128)S(1)}, bf16[64,1920]{1,0:T(8,128)(2,1)S(1)}) custom-call(s32[2]{0:T(128)S(1)} %pad_add_fusion.3.where_ref, f32[1,2048]{1,0:T(1,128)S(1)} %bitcast.19, bf16[16,2048]{1,0:T(8,128)(2,1)S(1)} %get-tuple-element.69.refs_0_, bf16[16,2048]{1,0:T(8,128)(2,1)S(1)} %collective-permute-done.29.refs_1_, ...), custom_call_target="tpu_custom_call" | custom-call | flops 6308233216 | bytes 8388608 | tf_op jit(solution)/shard_map/pallas_call | solution.py:45
  81.4 1.1 %shard_map.166 = (f32[64,1792]{1,0:T(8,128)S(1)}, bf16[64,1792]{1,0:T(8,128)(2,1)S(1)}) custom-call(bf16[128,2048]{1,0:T(8,128)(2,1)S(1)} %get-tuple-element.72.h_ref, bf16[2048,1792]{1,0:T(8,128)(2,1)S(1)} %bitcast.15), custom_call_target="tpu_custom_call" | custom-call | flops 6308233216 | bytes 7340032 | tf_op jit(solution)/shard_map/pallas_call | solution.py:45
  83.1 1.2 %collective-permute-start.37 = (bf16[32,1920]{1,0:T(8,128)(2,1)S(1)}, bf16[32,1920]{1,0:T(8,128)(2,1)S(1)}, u32[]{:S(2)}, u32[]{:S(2)}) collective-permute-start(bf16[32,1920]{1,0:T(8,128)(2,1)S(1)} %slice.64), channel_id=1, source_target_pairs={{0,2},{1,3},{2,0},{3,1},{4,6},{5,7},{6,4},{7,5},{8,10},{9,11},{10,... | collective-permute-start | bytes 368648 | tf_op jit(solution)/shard_map/ppermute | solution.py:24
  84.4 1.0 collective-permute-start.39
  85.4 4.0 %collective-permute-done.37 = bf16[32,1920]{1,0:T(8,128)(2,1)S(1)} collective-permute-done((bf16[32,1920]{1,0:T(8,128)(2,1)S(1)}, bf16[32,1920]{1,0:T(8,128)(2,1)S(1)}, u32[]{:S(2)}, u32[]{:S(2)}) %collective-permute-start.37) | collective-permute-done | bytes 122912 | tf_op jit(solution)/shard_map/ppermute | solution.py:24
  89.6 1.3 %collective-permute-done.39 = bf16[32,1792]{1,0:T(8,128)(2,1)S(1)} collective-permute-done((bf16[32,1792]{1,0:T(8,128)(2,1)S(1)}, bf16[32,1792]{1,0:T(8,128)(2,1)S(1)}, u32[]{:S(2)}, u32[]{:S(2)}) %collective-permute-start.39) | collective-permute-done | bytes 114720 | tf_op jit(solution)/shard_map/ppermute | solution.py:24
  91.1 1.2 %collective-permute-start.41 = (bf16[32,1792]{1,0:T(8,128)(2,1)S(1)}, bf16[32,1792]{1,0:T(8,128)(2,1)S(1)}, u32[]{:S(2)}, u32[]{:S(2)}) collective-permute-start(bf16[32,1792]{1,0:T(8,128)(2,1)S(1)} %fusion.2.refs_0_), channel_id=1, source_target_pairs={{0,2},{1,3},{2,0},{3,1},{4,6},{5,7},{6,4},{7,5},{8,10},{9,11},{10,... | collective-permute-start | bytes 344072 | tf_op jit(solution)/shard_map/ppermute | solution.py:24
  92.2 3.7 %collective-permute-done.41.refs_2_ = bf16[32,1792]{1,0:T(8,128)(2,1)S(1)} collective-permute-done((bf16[32,1792]{1,0:T(8,128)(2,1)S(1)}, bf16[32,1792]{1,0:T(8,128)(2,1)S(1)}, u32[]{:S(2)}, u32[]{:S(2)}) %collective-permute-start.41) | collective-permute-done | bytes 114720 | tf_op jit(solution)/shard_map/ppermute | solution.py:24
  95.9 1.3 %collective-permute-done.42.refs_3_ = bf16[32,1792]{1,0:T(8,128)(2,1)S(1)} collective-permute-done((bf16[32,1792]{1,0:T(8,128)(2,1)S(1)}, bf16[32,1792]{1,0:T(8,128)(2,1)S(1)}, u32[]{:S(2)}, u32[]{:S(2)}) %collective-permute-start.42) | collective-permute-done | bytes 114720 | tf_op jit(solution)/shard_map/ppermute | solution.py:24
  97.3 1.7 %shard_map.167 = (f32[16,2048]{1,0:T(8,128)S(1)}, bf16[16,2048]{1,0:T(8,128)(2,1)S(1)}, bf16[16,2048]{1,0:T(8,128)(2,1)S(1)}, bf16[16,2048]{1,0:T(8,128)(2,1)S(1...) custom-call(s32[2]{0:T(128)S(1)} %pad_add_fusion.3.where_ref, ...), custom_call_target="tpu_custom_call" | custom-call | flops 6308233216 | bytes 7340032 | tf_op jit(solution)/shard_map/pallas_call | solution.py:45
  99.0 1.0 collective-permute-start.45
  100.0 1.1 collective-permute-start.43
  101.0 0.7 collective-permute-start.48
  101.8 1.7 %collective-permute-start.49 = (bf16[16,2048]{1,0:T(8,128)(2,1)S(1)}, bf16[16,2048]{1,0:T(8,128)(2,1)S(1)}, u32[]{:S(2)}, u32[]{:S(2)}) collective-permute-start(bf16[16,2048]{1,0:T(8,128)(2,1)S(1)} %get-tuple-element.83), channel_id=1, source_target_pairs={{0,12},{4,8},{8,4},{12,0},{16,28},{20,24},{24,20},{28,16},{1,13},{... | collective-permute-start | bytes 196616 | tf_op jit(solution)/shard_map/ppermute | solution.py:24
  103.9 2.3 %collective-permute-start.46 = (bf16[16,2048]{1,0:T(8,128)(2,1)S(1)}, bf16[16,2048]{1,0:T(8,128)(2,1)S(1)}, u32[]{:S(2)}, u32[]{:S(2)}) collective-permute-start(bf16[16,2048]{1,0:T(8,128)(2,1)S(1)} %shard_map.169), channel_id=1, source_target_pairs={{0,24},{4,28},{8,16},{12,20},{16,8},{20,12},{24,0},{28,4},{1,25},{... | collective-permute-start | bytes 196616 | tf_op jit(solution)/shard_map/ppermute | solution.py:24
  106.4 1.1 collective-permute-start.47
  107.5 2.6 %collective-permute-done.46.refs_1_ = bf16[16,2048]{1,0:T(8,128)(2,1)S(1)} collective-permute-done((bf16[16,2048]{1,0:T(8,128)(2,1)S(1)}, bf16[16,2048]{1,0:T(8,128)(2,1)S(1)}, u32[]{:S(2)}, u32[]{:S(2)}) %collective-permute-start.46) | collective-permute-done | bytes 65568 | tf_op jit(solution)/shard_map/ppermute | solution.py:24
  110.0 2.1 %collective-permute-done.44.refs_0_ = bf16[16,2048]{1,0:T(8,128)(2,1)S(1)} collective-permute-done((bf16[16,2048]{1,0:T(8,128)(2,1)S(1)}, bf16[16,2048]{1,0:T(8,128)(2,1)S(1)}, u32[]{:S(2)}, u32[]{:S(2)}) %collective-permute-start.44) | collective-permute-done | bytes 65568 | tf_op jit(solution)/shard_map/ppermute | solution.py:24
  112.1 0.7 shard_map.170
  (113 shorter events, 8.2 us)
Async XLA Ops:
  0.6 7.0 %copy-start.3 = (bf16[8,8,1024]{2,1,0:T(8,128)(2,1)S(1)}, bf16[8,8,1024]{2,1,0:T(8,128)(2,1)}, u32[]{:S(2)}) copy-start(bf16[8,8,1024]{2,1,0:T(8,128)(2,1)} %keys_ref.3) | copy-start | bytes 393220
  0.6 7.0 %copy-start.4 = (bf16[8,8,1024]{2,1,0:T(8,128)(2,1)S(1)}, bf16[8,8,1024]{2,1,0:T(8,128)(2,1)}, u32[]{:S(2)}) copy-start(bf16[8,8,1024]{2,1,0:T(8,128)(2,1)} %values_ref.3) | copy-start | bytes 393220
  2.2 9.7 %collective-permute-start.3 = (bf16[16,2048]{1,0:T(8,128)(2,1)S(1)}, bf16[16,2048]{1,0:T(8,128)(2,1)S(1)}, u32[]{:S(2)}, u32[]{:S(2)}) collective-permute-start(bf16[16,2048]{1,0:T(8,128)(2,1)S(1)} %shard_map.149.x_ref.refs_0_.refs_10_.after_ref.refs_5_), channel_id=1, source_target_pairs={{0,16},{4,20},{8,24},{12,28},{16,0},{20,4},{24,8},{28,12},{1,17},{... | collective-permute-start | bytes 196616 | tf_op jit(solution)/shard_map/ppermute | solution.py:24
  6.3 6.2 %collective-permute-start.5 = (bf16[16,2048]{1,0:T(8,128)(2,1)S(1)}, bf16[16,2048]{1,0:T(8,128)(2,1)S(1)}, u32[]{:S(2)}, u32[]{:S(2)}) collective-permute-start(bf16[16,2048]{1,0:T(8,128)(2,1)S(1)} %shard_map.149.x_ref.refs_0_.refs_10_.after_ref.refs_5_), channel_id=1, source_target_pairs={{0,24},{4,28},{8,16},{12,20},{16,8},{20,12},{24,0},{28,4},{1,25},{... | collective-permute-start | bytes 196616 | tf_op jit(solution)/shard_map/ppermute | solution.py:24
  7.7 4.2 %copy-start.10 = (s32[64]{0:T(128)S(1)}, s32[64]{0:T(128)}, u32[]{:S(2)}) copy-start(s32[64]{0:T(128)} %param.18) | copy-start | bytes 772
  8.3 8.0 %collective-permute-start = (bf16[24,2048]{1,0:T(8,128)(2,1)S(1)}, bf16[24,2048]{1,0:T(8,128)(2,1)S(1)}, u32[]{:S(2)}, u32[]{:S(2)}) collective-permute-start(bf16[24,2048]{1,0:T(8,128)(2,1)S(1)} %get-tuple-element.43), channel_id=1, source_target_pairs={{0,4},{4,0},{8,12},{12,8},{16,20},{20,16},{24,28},{28,24},{1,5},{5... | collective-permute-start | bytes 294920 | tf_op jit(solution)/shard_map/ppermute | solution.py:24
  9.8 8.1 %collective-permute-start.1 = (bf16[24,2048]{1,0:T(8,128)(2,1)S(1)}, bf16[24,2048]{1,0:T(8,128)(2,1)S(1)}, u32[]{:S(2)}, u32[]{:S(2)}) collective-permute-start(bf16[24,2048]{1,0:T(8,128)(2,1)S(1)} %get-tuple-element.44), channel_id=1, source_target_pairs={{0,8},{4,12},{8,0},{12,4},{16,24},{20,28},{24,16},{28,20},{1,9},{5... | collective-permute-start | bytes 294920 | tf_op jit(solution)/shard_map/ppermute | solution.py:24
  10.1 8.3 %collective-permute-start.2 = (bf16[24,2048]{1,0:T(8,128)(2,1)S(1)}, bf16[24,2048]{1,0:T(8,128)(2,1)S(1)}, u32[]{:S(2)}, u32[]{:S(2)}) collective-permute-start(bf16[24,2048]{1,0:T(8,128)(2,1)S(1)} %get-tuple-element.45), channel_id=1, source_target_pairs={{0,12},{4,8},{8,4},{12,0},{16,28},{20,24},{24,20},{28,16},{1,13},{... | collective-permute-start | bytes 294920 | tf_op jit(solution)/shard_map/ppermute | solution.py:24
  13.1 7.1 %collective-permute-start.14 = (bf16[2,8,2048]{2,1,0:T(8,128)(2,1)S(1)}, bf16[2,8,2048]{2,1,0:T(8,128)(2,1)S(1)}, u32[]{:S(2)}, u32[]{:S(2)}) collective-permute-start(bf16[2,8,2048]{2,1,0:T(8,128)(2,1)S(1)} %get-tuple-element.53), channel_id=1, source_target_pairs={{0,16},{4,20},{8,24},{12,28},{16,0},{20,4},{24,8},{28,12},{1,17},{... | collective-permute-start | bytes 196616 | tf_op jit(solution)/shard_map/ppermute | solution.py:24
  15.9 6.2 %collective-permute-start.15 = (bf16[2,8,2048]{2,1,0:T(8,128)(2,1)S(1)}, bf16[2,8,2048]{2,1,0:T(8,128)(2,1)S(1)}, u32[]{:S(2)}, u32[]{:S(2)}) collective-permute-start(bf16[2,8,2048]{2,1,0:T(8,128)(2,1)S(1)} %get-tuple-element.54), channel_id=1, source_target_pairs={{0,24},{4,28},{8,16},{12,20},{16,8},{20,12},{24,0},{28,4},{1,25},{... | collective-permute-start | bytes 196616 | tf_op jit(solution)/shard_map/ppermute | solution.py:24
  16.3 7.3 %collective-permute-start.4 = (bf16[16,2048]{1,0:T(8,128)(2,1)S(1)}, bf16[16,2048]{1,0:T(8,128)(2,1)S(1)}, u32[]{:S(2)}, u32[]{:S(2)}) collective-permute-start(bf16[16,2048]{1,0:T(8,128)(2,1)S(1)} %collective-permute-done.3.refs_4_.refs_0_), channel_id=1, source_target_pairs={{0,4},{4,0},{8,12},{12,8},{16,20},{20,16},{24,28},{28,24},{1,5},{5... | collective-permute-start | bytes 196616 | tf_op jit(solution)/shard_map/ppermute | solution.py:24
  17.9 5.7 %collective-permute-start.6 = (bf16[16,2048]{1,0:T(8,128)(2,1)S(1)}, bf16[16,2048]{1,0:T(8,128)(2,1)S(1)}, u32[]{:S(2)}, u32[]{:S(2)}) collective-permute-start(bf16[16,2048]{1,0:T(8,128)(2,1)S(1)} %collective-permute-done.5.refs_6_.refs_1_), channel_id=1, source_target_pairs={{0,4},{4,0},{8,12},{12,8},{16,20},{20,16},{24,28},{28,24},{1,5},{5... | collective-permute-start | bytes 196616 | tf_op jit(solution)/shard_map/ppermute | solution.py:24
  18.3 5.2 %copy-start = (bf16[2048,1024]{1,0:T(8,128)(2,1)S(1)}, bf16[2048,1024]{1,0:T(8,128)(2,1)}, u32[]{:S(2)}) copy-start(bf16[2048,1024]{1,0:T(8,128)(2,1)} %refs_9_.1) | copy-start | bytes 12582916
  18.4 5.2 %copy-start.2 = (bf16[2048,256]{1,0:T(8,128)(2,1)S(1)}, bf16[2048,256]{1,0:T(8,128)(2,1)}, u32[]{:S(2)}) copy-start(bf16[2048,256]{1,0:T(8,128)(2,1)} %refs_8_.2) | copy-start | bytes 3145732
  18.4 5.2 %copy-start.7 = (f32[2048]{0:T(1024)S(1)}, f32[2048]{0:T(1024)}, u32[]{:S(2)}) copy-start(f32[2048]{0:T(1024)} %param.19) | copy-start | bytes 24580
  18.4 9.5 %collective-permute-start.8 = (bf16[4,8,2048]{2,1,0:T(8,128)(2,1)S(1)}, bf16[4,8,2048]{2,1,0:T(8,128)(2,1)S(1)}, u32[]{:S(2)}, u32[]{:S(2)}) collective-permute-start(bf16[4,8,2048]{2,1,0:T(8,128)(2,1)S(1)} %shard_map.152.refs_0_), channel_id=1, source_target_pairs={{0,2},{1,3},{2,0},{3,1},{4,6},{5,7},{6,4},{7,5},{8,10},{9,11},{10,... | collective-permute-start | bytes 393224 | tf_op jit(solution)/shard_map/ppermute | solution.py:24
  22.0 4.3 %collective-permute-start.16 = (bf16[2,8,2048]{2,1,0:T(8,128)(2,1)S(1)}, bf16[2,8,2048]{2,1,0:T(8,128)(2,1)S(1)}, u32[]{:S(2)}, u32[]{:S(2)}) collective-permute-start(bf16[2,8,2048]{2,1,0:T(8,128)(2,1)S(1)} %shard_map.156), channel_id=1, source_target_pairs={{0,4},{4,0},{8,12},{12,8},{16,20},{20,16},{24,28},{28,24},{1,5},{5... | collective-permute-start | bytes 196616 | tf_op jit(solution)/shard_map/ppermute | solution.py:24
  25.1 2.8 %collective-permute-start.7 = (bf16[128,896]{1,0:T(8,128)(2,1)S(1)}, bf16[128,896]{1,0:T(8,128)(2,1)S(1)}, u32[]{:S(2)}, u32[]{:S(2)}) collective-permute-start(bf16[128,896]{1,0:T(8,128)(2,1)S(1)} %get-tuple-element.46.own_ref), channel_id=1, source_target_pairs={{0,1},{1,0},{2,3},{3,2},{4,5},{5,4},{6,7},{7,6},{8,9},{9,8},{10,11... | collective-permute-start | bytes 688136 | tf_op jit(solution)/shard_map/ppermute | solution.py:24
  26.3 5.4 %collective-permute-start.17 = (bf16[4,8,2048]{2,1,0:T(8,128)(2,1)S(1)}, bf16[4,8,2048]{2,1,0:T(8,128)(2,1)S(1)}, u32[]{:S(2)}, u32[]{:S(2)}) collective-permute-start(bf16[4,8,2048]{2,1,0:T(8,128)(2,1)S(1)} %shard_map.157.refs_2_), channel_id=1, source_target_pairs={{0,2},{1,3},{2,0},{3,1},{4,6},{5,7},{6,4},{7,5},{8,10},{9,11},{10,... | collective-permute-start | bytes 393224 | tf_op jit(solution)/shard_map/ppermute | solution.py:24
  28.6 4.3 %collective-permute-start.11 = (bf16[128,128]{1,0:T(8,128)(2,1)S(1)}, bf16[128,128]{1,0:T(8,128)(2,1)S(1)}, u32[]{:S(2)}, u32[]{:S(2)}) collective-permute-start(bf16[128,128]{1,0:T(8,128)(2,1)S(1)} %get-tuple-element.50), channel_id=1, source_target_pairs={{0,2},{1,3},{2,0},{3,1},{4,10},{5,11},{6,8},{7,9},{8,18},{9,19},{1... | collective-permute-start | bytes 98312 | tf_op jit(solution)/shard_map/ppermute | solution.py:648
  29.4 11.9 %collective-permute-start.9 = (bf16[128,384]{1,0:T(8,128)(2,1)S(1)}, bf16[128,384]{1,0:T(8,128)(2,1)S(1)}, u32[]{:S(2)}, u32[]{:S(2)}) collective-permute-start(bf16[128,384]{1,0:T(8,128)(2,1)S(1)} %get-tuple-element.49.own_ref), channel_id=1, source_target_pairs={{0,2},{1,3},{2,0},{3,1},{4,6},{5,7},{6,4},{7,5},{8,10},{9,11},{10,... | collective-permute-start | bytes 294920 | tf_op jit(solution)/shard_map/ppermute | solution.py:24
  32.9 8.5 %collective-permute-start.18 = (bf16[2,8,8,2048]{3,2,1,0:T(8,128)(2,1)S(1)}, bf16[2,8,8,2048]{3,2,1,0:T(8,128)(2,1)S(1)}, u32[]{:S(2)}, u32[]{:S(2)}) collective-permute-start(bf16[2,8,8,2048]{3,2,1,0:T(8,128)(2,1)S(1)} %shard_map.158.refs_2_), channel_id=1, source_target_pairs={{0,1},{1,0},{2,3},{3,2},{4,5},{5,4},{6,7},{7,6},{8,9},{9,8},{10,11... | collective-permute-start | bytes 1572872 | tf_op jit(solution)/shard_map/ppermute | solution.py:24
  33.1 10.2 %collective-permute-start.10 = (bf16[128,128]{1,0:T(8,128)(2,1)S(1)}, bf16[128,128]{1,0:T(8,128)(2,1)S(1)}, u32[]{:S(2)}, u32[]{:S(2)}) collective-permute-start(bf16[128,128]{1,0:T(8,128)(2,1)S(1)} %get-tuple-element.50), channel_id=1, source_target_pairs={{0,0},{1,1},{2,2},{3,3},{4,8},{5,9},{6,10},{7,11},{8,16},{9,17},{1... | collective-permute-start | bytes 98312 | tf_op jit(solution)/shard_map/ppermute | solution.py:648
  33.8 7.6 %copy-start.9 = (f32[4,128]{1,0:T(4,128)S(1)}, f32[4,128]{1,0:T(4,128)}, u32[]{:S(2)}) copy-start(f32[4,128]{1,0:T(4,128)} %constant.71.clone.rope_ref) | copy-start | bytes 6148
  33.8 10.3 %collective-permute-start.12 = (bf16[128,128]{1,0:T(8,128)(2,1)S(1)}, bf16[128,128]{1,0:T(8,128)(2,1)S(1)}, u32[]{:S(2)}, u32[]{:S(2)}) collective-permute-start(bf16[128,128]{1,0:T(8,128)(2,1)S(1)} %get-tuple-element.51), channel_id=1, source_target_pairs={{0,4},{1,5},{2,6},{3,7},{4,12},{5,13},{6,14},{7,15},{8,20},{9,21},... | collective-permute-start | bytes 98312 | tf_op jit(solution)/shard_map/ppermute | solution.py:648
  39.1 5.7 %collective-permute-start.13 = (bf16[128,128]{1,0:T(8,128)(2,1)S(1)}, bf16[128,128]{1,0:T(8,128)(2,1)S(1)}, u32[]{:S(2)}, u32[]{:S(2)}) collective-permute-start(bf16[128,128]{1,0:T(8,128)(2,1)S(1)} %get-tuple-element.51), channel_id=1, source_target_pairs={{0,6},{1,7},{2,4},{3,5},{4,14},{5,15},{6,12},{7,13},{8,22},{9,23},... | collective-permute-start | bytes 98312 | tf_op jit(solution)/shard_map/ppermute | solution.py:648
  44.8 6.7 %copy-start.1 = (bf16[1024,2048]{1,0:T(8,128)(2,1)S(1)}, bf16[1024,2048]{1,0:T(8,128)(2,1)}, u32[]{:S(2)}) copy-start(bf16[1024,2048]{1,0:T(8,128)(2,1)} %refs_4_.2) | copy-start | bytes 12582916
  45.9 4.3 %collective-permute-start.20 = (bf16[32,1024]{1,0:T(8,128)(2,1)S(1)}, bf16[32,1024]{1,0:T(8,128)(2,1)S(1)}, u32[]{:S(2)}, u32[]{:S(2)}) collective-permute-start(bf16[32,1024]{1,0:T(8,128)(2,1)S(1)} %shard_map.160.refs_0_), channel_id=1, source_target_pairs={{0,2},{1,3},{2,0},{3,1},{4,6},{5,7},{6,4},{7,5},{8,10},{9,11},{10,... | collective-permute-start | bytes 196616 | tf_op jit(solution)/shard_map/ppermute | solution.py:24
  47.2 3.1 %collective-permute-start.19 = (bf16[32,1024]{1,0:T(8,128)(2,1)S(1)}, bf16[32,1024]{1,0:T(8,128)(2,1)S(1)}, u32[]{:S(2)}, u32[]{:S(2)}) collective-permute-start(bf16[32,1024]{1,0:T(8,128)(2,1)S(1)} %shard_map.160.refs_0_), channel_id=1, source_target_pairs={{0,1},{1,0},{2,3},{3,2},{4,5},{5,4},{6,7},{7,6},{8,9},{9,8},{10,11... | collective-permute-start | bytes 196616 | tf_op jit(solution)/shard_map/ppermute | solution.py:24
  50.3 1.3 %collective-permute-start.21 = (bf16[32,1024]{1,0:T(8,128)(2,1)S(1)}, bf16[32,1024]{1,0:T(8,128)(2,1)S(1)}, u32[]{:S(2)}, u32[]{:S(2)}) collective-permute-start(bf16[32,1024]{1,0:T(8,128)(2,1)S(1)} %collective-permute-done.20.refs_2_), channel_id=1, source_target_pairs={{0,1},{1,0},{2,3},{3,2},{4,5},{5,4},{6,7},{7,6},{8,9},{9,8},{10,11... | collective-permute-start | bytes 196616 | tf_op jit(solution)/shard_map/ppermute | solution.py:24
  52.8 4.9 %collective-permute-start.24 = (bf16[16,2048]{1,0:T(8,128)(2,1)S(1)}, bf16[16,2048]{1,0:T(8,128)(2,1)S(1)}, u32[]{:S(2)}, u32[]{:S(2)}) collective-permute-start(bf16[16,2048]{1,0:T(8,128)(2,1)S(1)} %get-tuple-element.64), channel_id=1, source_target_pairs={{0,4},{4,0},{8,12},{12,8},{16,20},{20,16},{24,28},{28,24},{1,5},{5... | collective-permute-start | bytes 196616 | tf_op jit(solution)/shard_map/ppermute | solution.py:24
  54.1 6.6 %collective-permute-start.22 = (bf16[16,2048]{1,0:T(8,128)(2,1)S(1)}, bf16[16,2048]{1,0:T(8,128)(2,1)S(1)}, u32[]{:S(2)}, u32[]{:S(2)}) collective-permute-start(bf16[16,2048]{1,0:T(8,128)(2,1)S(1)} %get-tuple-element.61), channel_id=1, source_target_pairs={{0,4},{4,0},{8,12},{12,8},{16,20},{20,16},{24,28},{28,24},{1,5},{5... | collective-permute-start | bytes 196616 | tf_op jit(solution)/shard_map/ppermute | solution.py:24
  54.9 6.7 %collective-permute-start.27 = (bf16[16,2048]{1,0:T(8,128)(2,1)S(1)}, bf16[16,2048]{1,0:T(8,128)(2,1)S(1)}, u32[]{:S(2)}, u32[]{:S(2)}) collective-permute-start(bf16[16,2048]{1,0:T(8,128)(2,1)S(1)} %get-tuple-element.66), channel_id=1, source_target_pairs={{0,8},{4,12},{8,0},{12,4},{16,24},{20,28},{24,16},{28,20},{1,9},{5... | collective-permute-start | bytes 196616 | tf_op jit(solution)/shard_map/ppermute | solution.py:24
  55.4 6.2 %collective-permute-start.28 = (bf16[16,2048]{1,0:T(8,128)(2,1)S(1)}, bf16[16,2048]{1,0:T(8,128)(2,1)S(1)}, u32[]{:S(2)}, u32[]{:S(2)}) collective-permute-start(bf16[16,2048]{1,0:T(8,128)(2,1)S(1)} %get-tuple-element.67), channel_id=1, source_target_pairs={{0,12},{4,8},{8,4},{12,0},{16,28},{20,24},{24,20},{28,16},{1,13},{... | collective-permute-start | bytes 196616 | tf_op jit(solution)/shard_map/ppermute | solution.py:24
  57.8 6.3 %collective-permute-start.25 = (bf16[16,2048]{1,0:T(8,128)(2,1)S(1)}, bf16[16,2048]{1,0:T(8,128)(2,1)S(1)}, u32[]{:S(2)}, u32[]{:S(2)}) collective-permute-start(bf16[16,2048]{1,0:T(8,128)(2,1)S(1)} %shard_map.163), channel_id=1, source_target_pairs={{0,24},{4,28},{8,16},{12,20},{16,8},{20,12},{24,0},{28,4},{1,25},{... | collective-permute-start | bytes 196616 | tf_op jit(solution)/shard_map/ppermute | solution.py:24
  60.7 18.6 %slice-start = ((s8[7340032]{0:T(1024)(128)(4,1)}), s8[4194304]{0:T(1024)(128)(4,1)S(1)}, s32[]{:S(2)}) async-start(s8[7340032]{0:T(1024)(128)(4,1)} %bitcast.12), calls=%async_computation | async-start | bytes 8388608
  60.8 5.3 %collective-permute-start.23 = (bf16[16,2048]{1,0:T(8,128)(2,1)S(1)}, bf16[16,2048]{1,0:T(8,128)(2,1)S(1)}, u32[]{:S(2)}, u32[]{:S(2)}) collective-permute-start(bf16[16,2048]{1,0:T(8,128)(2,1)S(1)} %get-tuple-element.63), channel_id=1, source_target_pairs={{0,16},{4,20},{8,24},{12,28},{16,0},{20,4},{24,8},{28,12},{1,17},{... | collective-permute-start | bytes 196616 | tf_op jit(solution)/shard_map/ppermute | solution.py:24
  60.8 18.5 %slice-start.1 = ((s8[7340032]{0:T(1024)(128)(4,1)}), s8[3145728]{0:T(1024)(128)(4,1)S(1)}, s32[]{:S(2)}) async-start(s8[7340032]{0:T(1024)(128)(4,1)} %bitcast.12), calls=%async_computation.1 | async-start | bytes 6291456
  60.9 5.2 %collective-permute-start.26 = (bf16[16,2048]{1,0:T(8,128)(2,1)S(1)}, bf16[16,2048]{1,0:T(8,128)(2,1)S(1)}, u32[]{:S(2)}, u32[]{:S(2)}) collective-permute-start(bf16[16,2048]{1,0:T(8,128)(2,1)S(1)} %get-tuple-element.65), channel_id=1, source_target_pairs={{0,4},{4,0},{8,12},{12,8},{16,20},{20,16},{24,28},{28,24},{1,5},{5... | collective-permute-start | bytes 196616 | tf_op jit(solution)/shard_map/ppermute | solution.py:24
  66.0 13.4 %copy-start.8 = (f32[2048]{0:T(1024)S(1)}, f32[2048]{0:T(1024)}, u32[]{:S(2)}) copy-start(f32[2048]{0:T(1024)} %param.20) | copy-start | bytes 24580
  66.0 15.3 %slice-start.2 = ((s8[7340032]{0:T(1024)(128)(4,1)}), s8[4194304]{0:T(1024)(128)(4,1)S(1)}, s32[]{:S(2)}) async-start(s8[7340032]{0:T(1024)(128)(4,1)} %bitcast.14), calls=%async_computation.2 | async-start | bytes 8388608
  66.7 6.8 %collective-permute-start.32 = (bf16[16,2048]{1,0:T(8,128)(2,1)S(1)}, bf16[16,2048]{1,0:T(8,128)(2,1)S(1)}, u32[]{:S(2)}, u32[]{:S(2)}) collective-permute-start(bf16[16,2048]{1,0:T(8,128)(2,1)S(1)} %get-tuple-element.69.refs_0_), channel_id=1, source_target_pairs={{0,16},{4,20},{8,24},{12,28},{16,0},{20,4},{24,8},{28,12},{1,17},{... | collective-permute-start | bytes 196616 | tf_op jit(solution)/shard_map/ppermute | solution.py:24
  68.7 6.4 %collective-permute-start.34 = (bf16[16,2048]{1,0:T(8,128)(2,1)S(1)}, bf16[16,2048]{1,0:T(8,128)(2,1)S(1)}, u32[]{:S(2)}, u32[]{:S(2)}) collective-permute-start(bf16[16,2048]{1,0:T(8,128)(2,1)S(1)} %get-tuple-element.69.refs_0_), channel_id=1, source_target_pairs={{0,24},{4,28},{8,16},{12,20},{16,8},{20,12},{24,0},{28,4},{1,25},{... | collective-permute-start | bytes 196616 | tf_op jit(solution)/shard_map/ppermute | solution.py:24
  70.0 6.0 %collective-permute-start.29 = (bf16[16,2048]{1,0:T(8,128)(2,1)S(1)}, bf16[16,2048]{1,0:T(8,128)(2,1)S(1)}, u32[]{:S(2)}, u32[]{:S(2)}) collective-permute-start(bf16[16,2048]{1,0:T(8,128)(2,1)S(1)} %get-tuple-element.69.refs_0_), channel_id=1, source_target_pairs={{0,4},{4,0},{8,12},{12,8},{16,20},{20,16},{24,28},{28,24},{1,5},{5... | collective-permute-start | bytes 196616 | tf_op jit(solution)/shard_map/ppermute | solution.py:24
  70.8 5.2 %collective-permute-start.30 = (bf16[16,2048]{1,0:T(8,128)(2,1)S(1)}, bf16[16,2048]{1,0:T(8,128)(2,1)S(1)}, u32[]{:S(2)}, u32[]{:S(2)}) collective-permute-start(bf16[16,2048]{1,0:T(8,128)(2,1)S(1)} %get-tuple-element.69.refs_0_), channel_id=1, source_target_pairs={{0,8},{4,12},{8,0},{12,4},{16,24},{20,28},{24,16},{28,20},{1,9},{5... | collective-permute-start | bytes 196616 | tf_op jit(solution)/shard_map/ppermute | solution.py:24
  71.0 5.7 %collective-permute-start.31 = (bf16[16,2048]{1,0:T(8,128)(2,1)S(1)}, bf16[16,2048]{1,0:T(8,128)(2,1)S(1)}, u32[]{:S(2)}, u32[]{:S(2)}) collective-permute-start(bf16[16,2048]{1,0:T(8,128)(2,1)S(1)} %get-tuple-element.69.refs_0_), channel_id=1, source_target_pairs={{0,12},{4,8},{8,4},{12,0},{16,28},{20,24},{24,20},{28,16},{1,13},{... | collective-permute-start | bytes 196616 | tf_op jit(solution)/shard_map/ppermute | solution.py:24
  73.5 4.6 %collective-permute-start.33 = (bf16[16,2048]{1,0:T(8,128)(2,1)S(1)}, bf16[16,2048]{1,0:T(8,128)(2,1)S(1)}, u32[]{:S(2)}, u32[]{:S(2)}) collective-permute-start(bf16[16,2048]{1,0:T(8,128)(2,1)S(1)} %collective-permute-done.32.refs_4_), channel_id=1, source_target_pairs={{0,4},{4,0},{8,12},{12,8},{16,20},{20,16},{24,28},{28,24},{1,5},{5... | collective-permute-start | bytes 196616 | tf_op jit(solution)/shard_map/ppermute | solution.py:24
  75.1 4.3 %collective-permute-start.35 = (bf16[16,2048]{1,0:T(8,128)(2,1)S(1)}, bf16[16,2048]{1,0:T(8,128)(2,1)S(1)}, u32[]{:S(2)}, u32[]{:S(2)}) collective-permute-start(bf16[16,2048]{1,0:T(8,128)(2,1)S(1)} %collective-permute-done.34.refs_6_), channel_id=1, source_target_pairs={{0,4},{4,0},{8,12},{12,8},{16,20},{20,16},{24,28},{28,24},{1,5},{5... | collective-permute-start | bytes 196616 | tf_op jit(solution)/shard_map/ppermute | solution.py:24
  79.4 17.8 %slice-start.4 = ((s8[7340032]{0:T(1024)(128)(4,1)}), s8[4194304]{0:T(1024)(128)(4,1)S(1)}, s32[]{:S(2)}) async-start(s8[7340032]{0:T(1024)(128)(4,1)} %bitcast.16), calls=%async_computation.4 | async-start | bytes 8388608
  81.2 1.8 %collective-permute-start.36 = (bf16[64,1920]{1,0:T(8,128)(2,1)S(1)}, bf16[64,1920]{1,0:T(8,128)(2,1)S(1)}, u32[]{:S(2)}, u32[]{:S(2)}) collective-permute-start(bf16[64,1920]{1,0:T(8,128)(2,1)S(1)} %get-tuple-element.71), channel_id=1, source_target_pairs={{0,1},{1,0},{2,3},{3,2},{4,5},{5,4},{6,7},{7,6},{8,9},{9,8},{10,11... | collective-permute-start | bytes 737288 | tf_op jit(solution)/shard_map/ppermute | solution.py:24
  81.3 15.9 %slice-start.5 = ((s8[7340032]{0:T(1024)(128)(4,1)}), s8[3145728]{0:T(1024)(128)(4,1)S(1)}, s32[]{:S(2)}) async-start(s8[7340032]{0:T(1024)(128)(4,1)} %bitcast.16), calls=%async_computation.5 | async-start | bytes 6291456
  82.5 1.8 %collective-permute-start.38 = (bf16[64,1792]{1,0:T(8,128)(2,1)S(1)}, bf16[64,1792]{1,0:T(8,128)(2,1)S(1)}, u32[]{:S(2)}, u32[]{:S(2)}) collective-permute-start(bf16[64,1792]{1,0:T(8,128)(2,1)S(1)} %get-tuple-element.74), channel_id=1, source_target_pairs={{0,1},{1,0},{2,3},{3,2},{4,5},{5,4},{6,7},{7,6},{8,9},{9,8},{10,11... | collective-permute-start | bytes 688136 | tf_op jit(solution)/shard_map/ppermute | solution.py:24
  83.1 6.2 %collective-permute-start.37 = (bf16[32,1920]{1,0:T(8,128)(2,1)S(1)}, bf16[32,1920]{1,0:T(8,128)(2,1)S(1)}, u32[]{:S(2)}, u32[]{:S(2)}) collective-permute-start(bf16[32,1920]{1,0:T(8,128)(2,1)S(1)} %slice.64), channel_id=1, source_target_pairs={{0,2},{1,3},{2,0},{3,1},{4,6},{5,7},{6,4},{7,5},{8,10},{9,11},{10,... | collective-permute-start | bytes 368648 | tf_op jit(solution)/shard_map/ppermute | solution.py:24
  84.4 6.6 %collective-permute-start.39 = (bf16[32,1792]{1,0:T(8,128)(2,1)S(1)}, bf16[32,1792]{1,0:T(8,128)(2,1)S(1)}, u32[]{:S(2)}, u32[]{:S(2)}) collective-permute-start(bf16[32,1792]{1,0:T(8,128)(2,1)S(1)} %slice.65), channel_id=1, source_target_pairs={{0,2},{1,3},{2,0},{3,1},{4,6},{5,7},{6,4},{7,5},{8,10},{9,11},{10,... | collective-permute-start | bytes 344072 | tf_op jit(solution)/shard_map/ppermute | solution.py:24
  91.1 4.9 %collective-permute-start.41 = (bf16[32,1792]{1,0:T(8,128)(2,1)S(1)}, bf16[32,1792]{1,0:T(8,128)(2,1)S(1)}, u32[]{:S(2)}, u32[]{:S(2)}) collective-permute-start(bf16[32,1792]{1,0:T(8,128)(2,1)S(1)} %fusion.2.refs_0_), channel_id=1, source_target_pairs={{0,2},{1,3},{2,0},{3,1},{4,6},{5,7},{6,4},{7,5},{8,10},{9,11},{10,... | collective-permute-start | bytes 344072 | tf_op jit(solution)/shard_map/ppermute | solution.py:24
  92.2 3.7 %collective-permute-start.40 = (bf16[32,1792]{1,0:T(8,128)(2,1)S(1)}, bf16[32,1792]{1,0:T(8,128)(2,1)S(1)}, u32[]{:S(2)}, u32[]{:S(2)}) collective-permute-start(bf16[32,1792]{1,0:T(8,128)(2,1)S(1)} %fusion.2.refs_0_), channel_id=1, source_target_pairs={{0,1},{1,0},{2,3},{3,2},{4,5},{5,4},{6,7},{7,6},{8,9},{9,8},{10,11... | collective-permute-start | bytes 344072 | tf_op jit(solution)/shard_map/ppermute | solution.py:24
  95.9 1.3 %collective-permute-start.42 = (bf16[32,1792]{1,0:T(8,128)(2,1)S(1)}, bf16[32,1792]{1,0:T(8,128)(2,1)S(1)}, u32[]{:S(2)}, u32[]{:S(2)}) collective-permute-start(bf16[32,1792]{1,0:T(8,128)(2,1)S(1)} %collective-permute-done.41.refs_2_), channel_id=1, source_target_pairs={{0,1},{1,0},{2,3},{3,2},{4,5},{5,4},{6,7},{7,6},{8,9},{9,8},{10,11... | collective-permute-start | bytes 344072 | tf_op jit(solution)/shard_map/ppermute | solution.py:24
  99.0 4.9 %collective-permute-start.45 = (bf16[16,2048]{1,0:T(8,128)(2,1)S(1)}, bf16[16,2048]{1,0:T(8,128)(2,1)S(1)}, u32[]{:S(2)}, u32[]{:S(2)}) collective-permute-start(bf16[16,2048]{1,0:T(8,128)(2,1)S(1)} %get-tuple-element.80), channel_id=1, source_target_pairs={{0,4},{4,0},{8,12},{12,8},{16,20},{20,16},{24,28},{28,24},{1,5},{5... | collective-permute-start | bytes 196616 | tf_op jit(solution)/shard_map/ppermute | solution.py:24
  100.0 6.3 %collective-permute-start.43 = (bf16[16,2048]{1,0:T(8,128)(2,1)S(1)}, bf16[16,2048]{1,0:T(8,128)(2,1)S(1)}, u32[]{:S(2)}, u32[]{:S(2)}) collective-permute-start(bf16[16,2048]{1,0:T(8,128)(2,1)S(1)} %get-tuple-element.77), channel_id=1, source_target_pairs={{0,4},{4,0},{8,12},{12,8},{16,20},{20,16},{24,28},{28,24},{1,5},{5... | collective-permute-start | bytes 196616 | tf_op jit(solution)/shard_map/ppermute | solution.py:24
  101.0 6.4 %collective-permute-start.48 = (bf16[16,2048]{1,0:T(8,128)(2,1)S(1)}, bf16[16,2048]{1,0:T(8,128)(2,1)S(1)}, u32[]{:S(2)}, u32[]{:S(2)}) collective-permute-start(bf16[16,2048]{1,0:T(8,128)(2,1)S(1)} %get-tuple-element.82), channel_id=1, source_target_pairs={{0,8},{4,12},{8,0},{12,4},{16,24},{20,28},{24,16},{28,20},{1,9},{5... | collective-permute-start | bytes 196616 | tf_op jit(solution)/shard_map/ppermute | solution.py:24
  101.8 5.7 %collective-permute-start.49 = (bf16[16,2048]{1,0:T(8,128)(2,1)S(1)}, bf16[16,2048]{1,0:T(8,128)(2,1)S(1)}, u32[]{:S(2)}, u32[]{:S(2)}) collective-permute-start(bf16[16,2048]{1,0:T(8,128)(2,1)S(1)} %get-tuple-element.83), channel_id=1, source_target_pairs={{0,12},{4,8},{8,4},{12,0},{16,28},{20,24},{24,20},{28,16},{1,13},{... | collective-permute-start | bytes 196616 | tf_op jit(solution)/shard_map/ppermute | solution.py:24
  103.9 6.1 %collective-permute-start.46 = (bf16[16,2048]{1,0:T(8,128)(2,1)S(1)}, bf16[16,2048]{1,0:T(8,128)(2,1)S(1)}, u32[]{:S(2)}, u32[]{:S(2)}) collective-permute-start(bf16[16,2048]{1,0:T(8,128)(2,1)S(1)} %shard_map.169), channel_id=1, source_target_pairs={{0,24},{4,28},{8,16},{12,20},{16,8},{20,12},{24,0},{28,4},{1,25},{... | collective-permute-start | bytes 196616 | tf_op jit(solution)/shard_map/ppermute | solution.py:24
  106.3 5.8 %collective-permute-start.44 = (bf16[16,2048]{1,0:T(8,128)(2,1)S(1)}, bf16[16,2048]{1,0:T(8,128)(2,1)S(1)}, u32[]{:S(2)}, u32[]{:S(2)}) collective-permute-start(bf16[16,2048]{1,0:T(8,128)(2,1)S(1)} %get-tuple-element.79), channel_id=1, source_target_pairs={{0,16},{4,20},{8,24},{12,28},{16,0},{20,4},{24,8},{28,12},{1,17},{... | collective-permute-start | bytes 196616 | tf_op jit(solution)/shard_map/ppermute | solution.py:24
  106.4 5.7 %collective-permute-start.47 = (bf16[16,2048]{1,0:T(8,128)(2,1)S(1)}, bf16[16,2048]{1,0:T(8,128)(2,1)S(1)}, u32[]{:S(2)}, u32[]{:S(2)}) collective-permute-start(bf16[16,2048]{1,0:T(8,128)(2,1)S(1)} %get-tuple-element.81), channel_id=1, source_target_pairs={{0,4},{4,0},{8,12},{12,8},{16,20},{20,16},{24,28},{28,24},{1,5},{5... | collective-permute-start | bytes 196616 | tf_op jit(solution)/shard_map/ppermute | solution.py:24
  (3 other events, 3.5 us)

commit v16 on v13

--- a/solution.py
+++ b/solution.py
@@ -481,8 +481,8 @@
 def sum_rows(parts, pair):
     own, *near, keep, one, two = parts
     count = one.shape[0] // pair
-    sums = add_pairs(keep, swap(one, "dp", 1), 0, pair, near[:2])
-    sums, near = list(sums[:count]), [*sums[count:], *near[2:]]
+    sums = add_pairs(keep, swap(one, "dp", 1), 0, pair, near[:1])
+    sums, near = list(sums[:count]), [*sums[count:], *near[1:]]
     sums += add_pairs(keep, swap(two, "dp", 1), one.shape[0], pair)
     arrived = [swap(piece, "dp", len(near) + 1 + 2 * i) for i, piece in enumerate(sums)]
     arrived += [swap(piece, "dp", k + 1) for k, piece in enumerate(near)]

time: 112 us -> 111 us (level)
  starting transfers between devices: 65.3 us -> 60.8 us
  waiting for transfers between devices: 28.7 us -> 32.2 us
    ppermute x47, starting transfers between devices: 60 us -> 55.5 us  [swap(): return lax.ppermute(x, axis, [(i, i ^ bits) for i in range(size)])]
    ppermute x47, waiting for transfers between devices: 28.7 us -> 32.2 us  [swap(): return lax.ppermute(x, axis, [(i, i ^ bits) for i in range(size)])]
where the time goes in v16:
time: 111 us
  starting transfers between devices  60.8 us (55%)
  waiting for transfers between devices  32.2 us (29%)
  Pallas kernels  14.5 us (13%)
  local copies, waits for them, and re-layouts  1.97 us (2%)
    ppermute x47, starting transfers between devices, swap(): return lax.ppermute(x, axis, [(i, i ^ bits) for i in range(size)])  55.5 us
    ppermute x47, waiting for transfers between devices, swap(): return lax.ppermute(x, axis, [(i, i ^ bits) for i in range(size)])  32.2 us
    pallas_call x23, Pallas kernels, call(): pl.pallas_call(body, out_shape=outs, in_specs=specs, out_specs=jax.tree.m...  14.5 us
    ppermute x4, starting transfers between devices, send_keyvals(): moved.append(lax.ppermute(piece, ('dp', 'tensor'), pairs))  5.32 us
  transfers between devices with their start and end apart: 51, of which 21 were waited for; matrix products, arithmetic and copies ran while one was open for 1% of the time, Pallas kernels for 6%

profile of v16, /device:TPU:0, one launch (start us, length us, event | category | flops | bytes accessed | tf_op | source)
XLA Modules:
  0.0 111.2 jit_solution(17684892812855362105)
XLA Ops:
  0.7 0.8 copy-done.5
  1.5 0.8 copy-done.6
  2.2 4.0 %collective-permute-start.3 = (bf16[16,2048]{1,0:T(8,128)(2,1)S(1)}, bf16[16,2048]{1,0:T(8,128)(2,1)S(1)}, u32[]{:S(2)}, u32[]{:S(2)}) collective-permute-start(bf16[16,2048]{1,0:T(8,128)(2,1)S(1)} %shard_map.149.x_ref.refs_0_.refs_10_.after_ref.refs_5_), channel_id=1, source_target_pairs={{0,16},{4,20},{8,24},{12,28},{16,0},{20,4},{24,8},{28,12},{1,17},{... | collective-permute-start | bytes 196616 | tf_op jit(solution)/shard_map/ppermute | solution.py:24
  6.3 1.3 %collective-permute-start.5 = (bf16[16,2048]{1,0:T(8,128)(2,1)S(1)}, bf16[16,2048]{1,0:T(8,128)(2,1)S(1)}, u32[]{:S(2)}, u32[]{:S(2)}) collective-permute-start(bf16[16,2048]{1,0:T(8,128)(2,1)S(1)} %shard_map.149.x_ref.refs_0_.refs_10_.after_ref.refs_5_), channel_id=1, source_target_pairs={{0,24},{4,28},{8,16},{12,20},{16,8},{20,12},{24,0},{28,4},{1,25},{... | collective-permute-start | bytes 196616 | tf_op jit(solution)/shard_map/ppermute | solution.py:24
  7.7 0.6 shard_map.150
  8.3 1.6 %collective-permute-start = (bf16[24,2048]{1,0:T(8,128)(2,1)S(1)}, bf16[24,2048]{1,0:T(8,128)(2,1)S(1)}, u32[]{:S(2)}, u32[]{:S(2)}) collective-permute-start(bf16[24,2048]{1,0:T(8,128)(2,1)S(1)} %get-tuple-element.43), channel_id=1, source_target_pairs={{0,4},{4,0},{8,12},{12,8},{16,20},{20,16},{24,28},{28,24},{1,5},{5... | collective-permute-start | bytes 294920 | tf_op jit(solution)/shard_map/ppermute | solution.py:24
  10.1 1.8 %collective-permute-start.2 = (bf16[24,2048]{1,0:T(8,128)(2,1)S(1)}, bf16[24,2048]{1,0:T(8,128)(2,1)S(1)}, u32[]{:S(2)}, u32[]{:S(2)}) collective-permute-start(bf16[24,2048]{1,0:T(8,128)(2,1)S(1)} %get-tuple-element.45), channel_id=1, source_target_pairs={{0,12},{4,8},{8,4},{12,0},{16,28},{20,24},{24,20},{28,16},{1,13},{... | collective-permute-start | bytes 294920 | tf_op jit(solution)/shard_map/ppermute | solution.py:24
  13.1 2.8 %collective-permute-start.15 = (bf16[2,8,2048]{2,1,0:T(8,128)(2,1)S(1)}, bf16[2,8,2048]{2,1,0:T(8,128)(2,1)S(1)}, u32[]{:S(2)}, u32[]{:S(2)}) collective-permute-start(bf16[2,8,2048]{2,1,0:T(8,128)(2,1)S(1)} %get-tuple-element.53), channel_id=1, source_target_pairs={{0,16},{4,20},{8,24},{12,28},{16,0},{20,4},{24,8},{28,12},{1,17},{... | collective-permute-start | bytes 196616 | tf_op jit(solution)/shard_map/ppermute | solution.py:24
  16.3 1.6 %collective-permute-start.4 = (bf16[16,2048]{1,0:T(8,128)(2,1)S(1)}, bf16[16,2048]{1,0:T(8,128)(2,1)S(1)}, u32[]{:S(2)}, u32[]{:S(2)}) collective-permute-start(bf16[16,2048]{1,0:T(8,128)(2,1)S(1)} %collective-permute-done.3.refs_4_.refs_0_), channel_id=1, source_target_pairs={{0,4},{4,0},{8,12},{12,8},{16,20},{20,16},{24,28},{28,24},{1,5},{5... | collective-permute-start | bytes 196616 | tf_op jit(solution)/shard_map/ppermute | solution.py:24
  18.4 1.8 %collective-permute-start.13 = (bf16[4,8,2048]{2,1,0:T(8,128)(2,1)S(1)}, bf16[4,8,2048]{2,1,0:T(8,128)(2,1)S(1)}, u32[]{:S(2)}, u32[]{:S(2)}) collective-permute-start(bf16[4,8,2048]{2,1,0:T(8,128)(2,1)S(1)} %shard_map.154.refs_0_.refs_2_), channel_id=1, source_target_pairs={{0,2},{1,3},{2,0},{3,1},{4,6},{5,7},{6,4},{7,5},{8,10},{9,11},{10,... | collective-permute-start | bytes 393224 | tf_op jit(solution)/shard_map/ppermute | solution.py:24
  20.2 1.8 %collective-permute-done.16.refs_1_ = bf16[2,8,2048]{2,1,0:T(8,128)(2,1)S(1)} collective-permute-done((bf16[2,8,2048]{2,1,0:T(8,128)(2,1)S(1)}, bf16[2,8,2048]{2,1,0:T(8,128)(2,1)S(1)}, u32[]{:S(2)}, u32[]{:S(2)}) %collective-permute-start.16) | collective-permute-done | bytes 65568 | tf_op jit(solution)/shard_map/ppermute | solution.py:24
  22.0 1.5 %collective-permute-start.17 = (bf16[2,8,2048]{2,1,0:T(8,128)(2,1)S(1)}, bf16[2,8,2048]{2,1,0:T(8,128)(2,1)S(1)}, u32[]{:S(2)}, u32[]{:S(2)}) collective-permute-start(bf16[2,8,2048]{2,1,0:T(8,128)(2,1)S(1)} %shard_map.157), channel_id=1, source_target_pairs={{0,4},{4,0},{8,12},{12,8},{16,20},{20,16},{24,28},{28,24},{1,5},{5... | collective-permute-start | bytes 196616 | tf_op jit(solution)/shard_map/ppermute | solution.py:24
  23.6 1.5 %shard_map.151 = (bf16[128,896]{1,0:T(8,128)(2,1)S(1)}, f32[64,1024]{1,0:T(8,128)S(1)}) custom-call(s32[2]{0:T(128)S(1)} %pad_add_fusion.3.where_ref, f32[1,2048]{1,0:T(1,128)S(1)} %bitcast.18, bf16[16,2048]{1,0:T(8,128)(2,1)S(1)} %shard_map.149.x_ref.refs_0_.refs_10_.after_ref.refs_5_, bf16[24,2048]{1,0:T(8,128)(2,1)S(1)} %collective-permute-done.refs_1_.refs_0_, ...), custom_call_target="tpu_custom_call" | custom-call | flops 6039797760 | bytes 6291456 | tf_op jit(solution)/shard_map/pallas_call | solution.py:45
  25.2 1.1 collective-permute-done.17.refs_2_
  26.3 1.6 %collective-permute-start.18 = (bf16[4,8,2048]{2,1,0:T(8,128)(2,1)S(1)}, bf16[4,8,2048]{2,1,0:T(8,128)(2,1)S(1)}, u32[]{:S(2)}, u32[]{:S(2)}) collective-permute-start(bf16[4,8,2048]{2,1,0:T(8,128)(2,1)S(1)} %shard_map.158.refs_0_.refs_5_), channel_id=1, source_target_pairs={{0,2},{1,3},{2,0},{3,1},{4,6},{5,7},{6,4},{7,5},{8,10},{9,11},{10,... | collective-permute-start | bytes 393224 | tf_op jit(solution)/shard_map/ppermute | solution.py:24
  27.9 0.7 shard_map.152
  29.3 1.6 %collective-permute-start.11 = (bf16[128,128]{1,0:T(8,128)(2,1)S(1)}, bf16[128,128]{1,0:T(8,128)(2,1)S(1)}, u32[]{:S(2)}, u32[]{:S(2)}) collective-permute-start(bf16[128,128]{1,0:T(8,128)(2,1)S(1)} %get-tuple-element.50), channel_id=1, source_target_pairs={{0,4},{1,5},{2,6},{3,7},{4,12},{5,13},{6,14},{7,15},{8,20},{9,21},... | collective-permute-start | bytes 98312 | tf_op jit(solution)/shard_map/ppermute | solution.py:653
  30.9 1.5 %collective-permute-start.12 = (bf16[128,128]{1,0:T(8,128)(2,1)S(1)}, bf16[128,128]{1,0:T(8,128)(2,1)S(1)}, u32[]{:S(2)}, u32[]{:S(2)}) collective-permute-start(bf16[128,128]{1,0:T(8,128)(2,1)S(1)} %get-tuple-element.50), channel_id=1, source_target_pairs={{0,6},{1,7},{2,4},{3,5},{4,14},{5,15},{6,12},{7,13},{8,22},{9,23},... | collective-permute-start | bytes 98312 | tf_op jit(solution)/shard_map/ppermute | solution.py:653
  32.5 1.5 %collective-permute-start.10 = (bf16[128,128]{1,0:T(8,128)(2,1)S(1)}, bf16[128,128]{1,0:T(8,128)(2,1)S(1)}, u32[]{:S(2)}, u32[]{:S(2)}) collective-permute-start(bf16[128,128]{1,0:T(8,128)(2,1)S(1)} %get-tuple-element.49), channel_id=1, source_target_pairs={{0,2},{1,3},{2,0},{3,1},{4,10},{5,11},{6,8},{7,9},{8,18},{9,19},{1... | collective-permute-start | bytes 98312 | tf_op jit(solution)/shard_map/ppermute | solution.py:653
  35.0 0.8 collective-permute-done.19.refs_7_
  35.8 0.7 collective-permute-start.9
  36.5 2.4 %shard_map.160 = (bf16[256,128]{1,0:T(8,128)(2,1)S(1)}, f32[256,128]{1,0:T(8,128)S(1)}, f32[256,128]{1,0:T(8,128)S(1)}, f32[256,128]{1,0:T(8,128)S(1)}) custom-call(s32[2]{0:T(128)S(1)} %pad_add_fusion.3.where_ref, s32[16]{0:T(128)S(1)} %get-tuple-element.85.anc_ref, f32[4,128]{1,0:T(4,128)S(1)} %copy-done.9, f32[128,128]{1,0:T(8,128)S(1)} %shard_map.153.scale_ref, ...), custom_call_target="tpu_custom_call" | custom-call | flops 5368709120 | bytes 4194304 | tf_op jit(solution)/shard_map/pallas_call | solution.py:45
  38.9 1.1 %shard_map.161.refs_0_ = bf16[32,1024]{1,0:T(8,128)(2,1)S(1)} custom-call(s32[2]{0:T(128)S(1)} %pad_add_fusion.3.where_ref, f32[4,128]{1,0:T(4,128)S(1)} %copy-done.9, s32[256,2]{1,0:T(8,128)S(1)} %copy.20.target_ref, f32[128,128]{1,0:T(8,128)S(1)} %shard_map.153.scale_ref, bf16[128,128]{1,0:T(8,128)(2,1)S(1)} %collective-permute-done.9.refs_0_, ...), custom_call_target="tpu_custom_call" | custom-call | flops 5368709120 | bytes 1048576 | tf_op jit(solution)/shard_map/pallas_call | solution.py:45
  40.0 1.6 %collective-permute-start.21 = (bf16[32,1024]{1,0:T(8,128)(2,1)S(1)}, bf16[32,1024]{1,0:T(8,128)(2,1)S(1)}, u32[]{:S(2)}, u32[]{:S(2)}) collective-permute-start(bf16[32,1024]{1,0:T(8,128)(2,1)S(1)} %shard_map.161.refs_0_), channel_id=1, source_target_pairs={{0,2},{1,3},{2,0},{3,1},{4,6},{5,7},{6,4},{7,5},{8,10},{9,11},{10,... | collective-permute-start | bytes 196616 | tf_op jit(solution)/shard_map/ppermute | solution.py:24
  41.6 2.7 %collective-permute-done.21.refs_2_ = bf16[32,1024]{1,0:T(8,128)(2,1)S(1)} collective-permute-done((bf16[32,1024]{1,0:T(8,128)(2,1)S(1)}, bf16[32,1024]{1,0:T(8,128)(2,1)S(1)}, u32[]{:S(2)}, u32[]{:S(2)}) %collective-permute-start.21) | collective-permute-done | bytes 65568 | tf_op jit(solution)/shard_map/ppermute | solution.py:24
  44.4 1.2 %collective-permute-done.22.refs_3_ = bf16[32,1024]{1,0:T(8,128)(2,1)S(1)} collective-permute-done((bf16[32,1024]{1,0:T(8,128)(2,1)S(1)}, bf16[32,1024]{1,0:T(8,128)(2,1)S(1)}, u32[]{:S(2)}, u32[]{:S(2)}) %collective-permute-start.22) | collective-permute-done | bytes 65568 | tf_op jit(solution)/shard_map/ppermute | solution.py:24
  45.6 1.3 %shard_map.162 = (f32[16,2048]{1,0:T(8,128)S(1)}, bf16[16,2048]{1,0:T(8,128)(2,1)S(1)}, bf16[16,2048]{1,0:T(8,128)(2,1)S(1)}, bf16[16,2048]{1,0:T(8,128)(2,1)S(1...) custom-call(s32[2]{0:T(128)S(1)} %pad_add_fusion.3.where_ref, ...), custom_call_target="tpu_custom_call" | custom-call | flops 5905580032 | bytes 4194304 | tf_op jit(solution)/shard_map/pallas_call | solution.py:45
  46.9 5.8 %collective-permute-start.25 = (bf16[16,2048]{1,0:T(8,128)(2,1)S(1)}, bf16[16,2048]{1,0:T(8,128)(2,1)S(1)}, u32[]{:S(2)}, u32[]{:S(2)}) collective-permute-start(bf16[16,2048]{1,0:T(8,128)(2,1)S(1)} %get-tuple-element.64), channel_id=1, source_target_pairs={{0,4},{4,0},{8,12},{12,8},{16,20},{20,16},{24,28},{28,24},{1,5},{5... | collective-permute-start | bytes 196616 | tf_op jit(solution)/shard_map/ppermute | solution.py:24
  52.8 1.0 collective-permute-start.28
  53.8 2.4 %collective-permute-start.29 = (bf16[16,2048]{1,0:T(8,128)(2,1)S(1)}, bf16[16,2048]{1,0:T(8,128)(2,1)S(1)}, u32[]{:S(2)}, u32[]{:S(2)}) collective-permute-start(bf16[16,2048]{1,0:T(8,128)(2,1)S(1)} %get-tuple-element.67), channel_id=1, source_target_pairs={{0,12},{4,8},{8,4},{12,0},{16,28},{20,24},{24,20},{28,16},{1,13},{... | collective-permute-start | bytes 196616 | tf_op jit(solution)/shard_map/ppermute | solution.py:24
  56.2 3.0 %collective-permute-start.26 = (bf16[16,2048]{1,0:T(8,128)(2,1)S(1)}, bf16[16,2048]{1,0:T(8,128)(2,1)S(1)}, u32[]{:S(2)}, u32[]{:S(2)}) collective-permute-start(bf16[16,2048]{1,0:T(8,128)(2,1)S(1)} %shard_map.164), channel_id=1, source_target_pairs={{0,24},{4,28},{8,16},{12,20},{16,8},{20,12},{24,0},{28,4},{1,25},{... | collective-permute-start | bytes 196616 | tf_op jit(solution)/shard_map/ppermute | solution.py:24
  59.3 0.7 collective-permute-start.27
  60.0 2.3 %collective-permute-done.26.refs_1_ = bf16[16,2048]{1,0:T(8,128)(2,1)S(1)} collective-permute-done((bf16[16,2048]{1,0:T(8,128)(2,1)S(1)}, bf16[16,2048]{1,0:T(8,128)(2,1)S(1)}, u32[]{:S(2)}, u32[]{:S(2)}) %collective-permute-start.26) | collective-permute-done | bytes 65568 | tf_op jit(solution)/shard_map/ppermute | solution.py:24
  62.4 2.2 %collective-permute-done.24.refs_0_ = bf16[16,2048]{1,0:T(8,128)(2,1)S(1)} collective-permute-done((bf16[16,2048]{1,0:T(8,128)(2,1)S(1)}, bf16[16,2048]{1,0:T(8,128)(2,1)S(1)}, u32[]{:S(2)}, u32[]{:S(2)}) %collective-permute-start.24) | collective-permute-done | bytes 65568 | tf_op jit(solution)/shard_map/ppermute | solution.py:24
  64.5 0.7 shard_map.165
  65.2 1.9 %collective-permute-start.33 = (bf16[16,2048]{1,0:T(8,128)(2,1)S(1)}, bf16[16,2048]{1,0:T(8,128)(2,1)S(1)}, u32[]{:S(2)}, u32[]{:S(2)}) collective-permute-start(bf16[16,2048]{1,0:T(8,128)(2,1)S(1)} %get-tuple-element.69.refs_0_), channel_id=1, source_target_pairs={{0,16},{4,20},{8,24},{12,28},{16,0},{20,4},{24,8},{28,12},{1,17},{... | collective-permute-start | bytes 196616 | tf_op jit(solution)/shard_map/ppermute | solution.py:24
  67.2 1.0 collective-permute-start.35
  68.2 1.2 %collective-permute-start.30 = (bf16[16,2048]{1,0:T(8,128)(2,1)S(1)}, bf16[16,2048]{1,0:T(8,128)(2,1)S(1)}, u32[]{:S(2)}, u32[]{:S(2)}) collective-permute-start(bf16[16,2048]{1,0:T(8,128)(2,1)S(1)} %get-tuple-element.69.refs_0_), channel_id=1, source_target_pairs={{0,4},{4,0},{8,12},{12,8},{16,20},{20,16},{24,28},{28,24},{1,5},{5... | collective-permute-start | bytes 196616 | tf_op jit(solution)/shard_map/ppermute | solution.py:24
  69.6 2.1 %collective-permute-start.32 = (bf16[16,2048]{1,0:T(8,128)(2,1)S(1)}, bf16[16,2048]{1,0:T(8,128)(2,1)S(1)}, u32[]{:S(2)}, u32[]{:S(2)}) collective-permute-start(bf16[16,2048]{1,0:T(8,128)(2,1)S(1)} %get-tuple-element.69.refs_0_), channel_id=1, source_target_pairs={{0,12},{4,8},{8,4},{12,0},{16,28},{20,24},{24,20},{28,16},{1,13},{... | collective-permute-start | bytes 196616 | tf_op jit(solution)/shard_map/ppermute | solution.py:24
  71.8 1.2 %collective-permute-start.34 = (bf16[16,2048]{1,0:T(8,128)(2,1)S(1)}, bf16[16,2048]{1,0:T(8,128)(2,1)S(1)}, u32[]{:S(2)}, u32[]{:S(2)}) collective-permute-start(bf16[16,2048]{1,0:T(8,128)(2,1)S(1)} %collective-permute-done.33.refs_4_), channel_id=1, source_target_pairs={{0,4},{4,0},{8,12},{12,8},{16,20},{20,16},{24,28},{28,24},{1,5},{5... | collective-permute-start | bytes 196616 | tf_op jit(solution)/shard_map/ppermute | solution.py:24
  72.9 0.7 collective-permute-done.35.refs_6_
  73.6 0.8 collective-permute-start.36
  74.4 0.6 collective-permute-done.32.refs_3_
  75.1 1.4 %collective-permute-done.34.refs_5_ = bf16[16,2048]{1,0:T(8,128)(2,1)S(1)} collective-permute-done((bf16[16,2048]{1,0:T(8,128)(2,1)S(1)}, bf16[16,2048]{1,0:T(8,128)(2,1)S(1)}, u32[]{:S(2)}, u32[]{:S(2)}) %collective-permute-start.34) | collective-permute-done | bytes 65568 | tf_op jit(solution)/shard_map/ppermute | solution.py:24
  76.4 1.5 %collective-permute-done.36.refs_7_ = bf16[16,2048]{1,0:T(8,128)(2,1)S(1)} collective-permute-done((bf16[16,2048]{1,0:T(8,128)(2,1)S(1)}, bf16[16,2048]{1,0:T(8,128)(2,1)S(1)}, u32[]{:S(2)}, u32[]{:S(2)}) %collective-permute-start.36) | collective-permute-done | bytes 65568 | tf_op jit(solution)/shard_map/ppermute | solution.py:24
  78.0 1.8 %shard_map.166 = (bf16[128,2048]{1,0:T(8,128)(2,1)S(1)}, f32[64,1920]{1,0:T(8,128)S(1)}, bf16[64,1920]{1,0:T(8,128)(2,1)S(1)}) custom-call(s32[2]{0:T(128)S(1)} %pad_add_fusion.3.where_ref, f32[1,2048]{1,0:T(1,128)S(1)} %bitcast.19, bf16[16,2048]{1,0:T(8,128)(2,1)S(1)} %get-tuple-element.69.refs_0_, bf16[16,2048]{1,0:T(8,128)(2,1)S(1)} %collective-permute-done.30.refs_1_, ...), custom_call_target="tpu_custom_call" | custom-call | flops 6308233216 | bytes 8388608 | tf_op jit(solution)/shard_map/pallas_call | solution.py:45
  79.9 1.1 %shard_map.167 = (f32[64,1792]{1,0:T(8,128)S(1)}, bf16[64,1792]{1,0:T(8,128)(2,1)S(1)}) custom-call(bf16[128,2048]{1,0:T(8,128)(2,1)S(1)} %get-tuple-element.72.h_ref, bf16[2048,1792]{1,0:T(8,128)(2,1)S(1)} %bitcast.15), custom_call_target="tpu_custom_call" | custom-call | flops 6308233216 | bytes 7340032 | tf_op jit(solution)/shard_map/pallas_call | solution.py:45
  81.7 1.4 %collective-permute-start.38 = (bf16[32,1920]{1,0:T(8,128)(2,1)S(1)}, bf16[32,1920]{1,0:T(8,128)(2,1)S(1)}, u32[]{:S(2)}, u32[]{:S(2)}) collective-permute-start(bf16[32,1920]{1,0:T(8,128)(2,1)S(1)} %slice.64), channel_id=1, source_target_pairs={{0,2},{1,3},{2,0},{3,1},{4,6},{5,7},{6,4},{7,5},{8,10},{9,11},{10,... | collective-permute-start | bytes 368648 | tf_op jit(solution)/shard_map/ppermute | solution.py:24
  83.1 1.0 collective-permute-start.40
  84.2 3.7 %collective-permute-done.38 = bf16[32,1920]{1,0:T(8,128)(2,1)S(1)} collective-permute-done((bf16[32,1920]{1,0:T(8,128)(2,1)S(1)}, bf16[32,1920]{1,0:T(8,128)(2,1)S(1)}, u32[]{:S(2)}, u32[]{:S(2)}) %collective-permute-start.38) | collective-permute-done | bytes 122912 | tf_op jit(solution)/shard_map/ppermute | solution.py:24
  88.1 1.3 %collective-permute-done.40 = bf16[32,1792]{1,0:T(8,128)(2,1)S(1)} collective-permute-done((bf16[32,1792]{1,0:T(8,128)(2,1)S(1)}, bf16[32,1792]{1,0:T(8,128)(2,1)S(1)}, u32[]{:S(2)}, u32[]{:S(2)}) %collective-permute-start.40) | collective-permute-done | bytes 114720 | tf_op jit(solution)/shard_map/ppermute | solution.py:24
  89.6 1.4 %collective-permute-start.42 = (bf16[32,1792]{1,0:T(8,128)(2,1)S(1)}, bf16[32,1792]{1,0:T(8,128)(2,1)S(1)}, u32[]{:S(2)}, u32[]{:S(2)}) collective-permute-start(bf16[32,1792]{1,0:T(8,128)(2,1)S(1)} %fusion.2.refs_0_), channel_id=1, source_target_pairs={{0,2},{1,3},{2,0},{3,1},{4,6},{5,7},{6,4},{7,5},{8,10},{9,11},{10,... | collective-permute-start | bytes 344072 | tf_op jit(solution)/shard_map/ppermute | solution.py:24
  91.0 3.5 %collective-permute-done.42.refs_2_ = bf16[32,1792]{1,0:T(8,128)(2,1)S(1)} collective-permute-done((bf16[32,1792]{1,0:T(8,128)(2,1)S(1)}, bf16[32,1792]{1,0:T(8,128)(2,1)S(1)}, u32[]{:S(2)}, u32[]{:S(2)}) %collective-permute-start.42) | collective-permute-done | bytes 114720 | tf_op jit(solution)/shard_map/ppermute | solution.py:24
  94.5 1.3 %collective-permute-done.43.refs_3_ = bf16[32,1792]{1,0:T(8,128)(2,1)S(1)} collective-permute-done((bf16[32,1792]{1,0:T(8,128)(2,1)S(1)}, bf16[32,1792]{1,0:T(8,128)(2,1)S(1)}, u32[]{:S(2)}, u32[]{:S(2)}) %collective-permute-start.43) | collective-permute-done | bytes 114720 | tf_op jit(solution)/shard_map/ppermute | solution.py:24
  95.8 1.7 %shard_map.168 = (f32[16,2048]{1,0:T(8,128)S(1)}, bf16[16,2048]{1,0:T(8,128)(2,1)S(1)}, bf16[16,2048]{1,0:T(8,128)(2,1)S(1)}, bf16[16,2048]{1,0:T(8,128)(2,1)S(1...) custom-call(s32[2]{0:T(128)S(1)} %pad_add_fusion.3.where_ref, ...), custom_call_target="tpu_custom_call" | custom-call | flops 6308233216 | bytes 7340032 | tf_op jit(solution)/shard_map/pallas_call | solution.py:45
  97.5 0.9 collective-permute-start.46
  98.3 1.2 %collective-permute-start.44 = (bf16[16,2048]{1,0:T(8,128)(2,1)S(1)}, bf16[16,2048]{1,0:T(8,128)(2,1)S(1)}, u32[]{:S(2)}, u32[]{:S(2)}) collective-permute-start(bf16[16,2048]{1,0:T(8,128)(2,1)S(1)} %get-tuple-element.77), channel_id=1, source_target_pairs={{0,4},{4,0},{8,12},{12,8},{16,20},{20,16},{24,28},{28,24},{1,5},{5... | collective-permute-start | bytes 196616 | tf_op jit(solution)/shard_map/ppermute | solution.py:24
  99.6 0.7 collective-permute-start.49
  100.3 1.6 %collective-permute-start.50 = (bf16[16,2048]{1,0:T(8,128)(2,1)S(1)}, bf16[16,2048]{1,0:T(8,128)(2,1)S(1)}, u32[]{:S(2)}, u32[]{:S(2)}) collective-permute-start(bf16[16,2048]{1,0:T(8,128)(2,1)S(1)} %get-tuple-element.83), channel_id=1, source_target_pairs={{0,12},{4,8},{8,4},{12,0},{16,28},{20,24},{24,20},{28,16},{1,13},{... | collective-permute-start | bytes 196616 | tf_op jit(solution)/shard_map/ppermute | solution.py:24
  102.4 2.4 %collective-permute-start.47 = (bf16[16,2048]{1,0:T(8,128)(2,1)S(1)}, bf16[16,2048]{1,0:T(8,128)(2,1)S(1)}, u32[]{:S(2)}, u32[]{:S(2)}) collective-permute-start(bf16[16,2048]{1,0:T(8,128)(2,1)S(1)} %shard_map.170), channel_id=1, source_target_pairs={{0,24},{4,28},{8,16},{12,20},{16,8},{20,12},{24,0},{28,4},{1,25},{... | collective-permute-start | bytes 196616 | tf_op jit(solution)/shard_map/ppermute | solution.py:24
  104.9 0.9 collective-permute-start.48
  105.8 2.8 %collective-permute-done.47.refs_1_ = bf16[16,2048]{1,0:T(8,128)(2,1)S(1)} collective-permute-done((bf16[16,2048]{1,0:T(8,128)(2,1)S(1)}, bf16[16,2048]{1,0:T(8,128)(2,1)S(1)}, u32[]{:S(2)}, u32[]{:S(2)}) %collective-permute-start.47) | collective-permute-done | bytes 65568 | tf_op jit(solution)/shard_map/ppermute | solution.py:24
  108.6 2.0 %collective-permute-done.45.refs_0_ = bf16[16,2048]{1,0:T(8,128)(2,1)S(1)} collective-permute-done((bf16[16,2048]{1,0:T(8,128)(2,1)S(1)}, bf16[16,2048]{1,0:T(8,128)(2,1)S(1)}, u32[]{:S(2)}, u32[]{:S(2)}) %collective-permute-start.45) | collective-permute-done | bytes 65568 | tf_op jit(solution)/shard_map/ppermute | solution.py:24
  110.6 0.7 shard_map.171
  (116 shorter events, 6.5 us)
Async XLA Ops:
  0.6 7.0 %copy-start.3 = (bf16[8,8,1024]{2,1,0:T(8,128)(2,1)S(1)}, bf16[8,8,1024]{2,1,0:T(8,128)(2,1)}, u32[]{:S(2)}) copy-start(bf16[8,8,1024]{2,1,0:T(8,128)(2,1)} %keys_ref.3) | copy-start | bytes 393220
  0.6 7.0 %copy-start.4 = (bf16[8,8,1024]{2,1,0:T(8,128)(2,1)S(1)}, bf16[8,8,1024]{2,1,0:T(8,128)(2,1)}, u32[]{:S(2)}) copy-start(bf16[8,8,1024]{2,1,0:T(8,128)(2,1)} %values_ref.3) | copy-start | bytes 393220
  2.2 9.9 %collective-permute-start.3 = (bf16[16,2048]{1,0:T(8,128)(2,1)S(1)}, bf16[16,2048]{1,0:T(8,128)(2,1)S(1)}, u32[]{:S(2)}, u32[]{:S(2)}) collective-permute-start(bf16[16,2048]{1,0:T(8,128)(2,1)S(1)} %shard_map.149.x_ref.refs_0_.refs_10_.after_ref.refs_5_), channel_id=1, source_target_pairs={{0,16},{4,20},{8,24},{12,28},{16,0},{20,4},{24,8},{28,12},{1,17},{... | collective-permute-start | bytes 196616 | tf_op jit(solution)/shard_map/ppermute | solution.py:24
  6.3 6.2 %collective-permute-start.5 = (bf16[16,2048]{1,0:T(8,128)(2,1)S(1)}, bf16[16,2048]{1,0:T(8,128)(2,1)S(1)}, u32[]{:S(2)}, u32[]{:S(2)}) collective-permute-start(bf16[16,2048]{1,0:T(8,128)(2,1)S(1)} %shard_map.149.x_ref.refs_0_.refs_10_.after_ref.refs_5_), channel_id=1, source_target_pairs={{0,24},{4,28},{8,16},{12,20},{16,8},{20,12},{24,0},{28,4},{1,25},{... | collective-permute-start | bytes 196616 | tf_op jit(solution)/shard_map/ppermute | solution.py:24
  7.7 4.2 %copy-start.10 = (s32[64]{0:T(128)S(1)}, s32[64]{0:T(128)}, u32[]{:S(2)}) copy-start(s32[64]{0:T(128)} %param.18) | copy-start | bytes 772
  8.3 8.0 %collective-permute-start = (bf16[24,2048]{1,0:T(8,128)(2,1)S(1)}, bf16[24,2048]{1,0:T(8,128)(2,1)S(1)}, u32[]{:S(2)}, u32[]{:S(2)}) collective-permute-start(bf16[24,2048]{1,0:T(8,128)(2,1)S(1)} %get-tuple-element.43), channel_id=1, source_target_pairs={{0,4},{4,0},{8,12},{12,8},{16,20},{20,16},{24,28},{28,24},{1,5},{5... | collective-permute-start | bytes 294920 | tf_op jit(solution)/shard_map/ppermute | solution.py:24
  9.8 8.1 %collective-permute-start.1 = (bf16[24,2048]{1,0:T(8,128)(2,1)S(1)}, bf16[24,2048]{1,0:T(8,128)(2,1)S(1)}, u32[]{:S(2)}, u32[]{:S(2)}) collective-permute-start(bf16[24,2048]{1,0:T(8,128)(2,1)S(1)} %get-tuple-element.44), channel_id=1, source_target_pairs={{0,8},{4,12},{8,0},{12,4},{16,24},{20,28},{24,16},{28,20},{1,9},{5... | collective-permute-start | bytes 294920 | tf_op jit(solution)/shard_map/ppermute | solution.py:24
  10.1 8.3 %collective-permute-start.2 = (bf16[24,2048]{1,0:T(8,128)(2,1)S(1)}, bf16[24,2048]{1,0:T(8,128)(2,1)S(1)}, u32[]{:S(2)}, u32[]{:S(2)}) collective-permute-start(bf16[24,2048]{1,0:T(8,128)(2,1)S(1)} %get-tuple-element.45), channel_id=1, source_target_pairs={{0,12},{4,8},{8,4},{12,0},{16,28},{20,24},{24,20},{28,16},{1,13},{... | collective-permute-start | bytes 294920 | tf_op jit(solution)/shard_map/ppermute | solution.py:24
  13.1 7.1 %collective-permute-start.15 = (bf16[2,8,2048]{2,1,0:T(8,128)(2,1)S(1)}, bf16[2,8,2048]{2,1,0:T(8,128)(2,1)S(1)}, u32[]{:S(2)}, u32[]{:S(2)}) collective-permute-start(bf16[2,8,2048]{2,1,0:T(8,128)(2,1)S(1)} %get-tuple-element.53), channel_id=1, source_target_pairs={{0,16},{4,20},{8,24},{12,28},{16,0},{20,4},{24,8},{28,12},{1,17},{... | collective-permute-start | bytes 196616 | tf_op jit(solution)/shard_map/ppermute | solution.py:24
  15.9 6.2 %collective-permute-start.16 = (bf16[2,8,2048]{2,1,0:T(8,128)(2,1)S(1)}, bf16[2,8,2048]{2,1,0:T(8,128)(2,1)S(1)}, u32[]{:S(2)}, u32[]{:S(2)}) collective-permute-start(bf16[2,8,2048]{2,1,0:T(8,128)(2,1)S(1)} %get-tuple-element.54), channel_id=1, source_target_pairs={{0,24},{4,28},{8,16},{12,20},{16,8},{20,12},{24,0},{28,4},{1,25},{... | collective-permute-start | bytes 196616 | tf_op jit(solution)/shard_map/ppermute | solution.py:24
  16.3 7.3 %collective-permute-start.4 = (bf16[16,2048]{1,0:T(8,128)(2,1)S(1)}, bf16[16,2048]{1,0:T(8,128)(2,1)S(1)}, u32[]{:S(2)}, u32[]{:S(2)}) collective-permute-start(bf16[16,2048]{1,0:T(8,128)(2,1)S(1)} %collective-permute-done.3.refs_4_.refs_0_), channel_id=1, source_target_pairs={{0,4},{4,0},{8,12},{12,8},{16,20},{20,16},{24,28},{28,24},{1,5},{5... | collective-permute-start | bytes 196616 | tf_op jit(solution)/shard_map/ppermute | solution.py:24
  17.9 5.7 %collective-permute-start.6 = (bf16[16,2048]{1,0:T(8,128)(2,1)S(1)}, bf16[16,2048]{1,0:T(8,128)(2,1)S(1)}, u32[]{:S(2)}, u32[]{:S(2)}) collective-permute-start(bf16[16,2048]{1,0:T(8,128)(2,1)S(1)} %collective-permute-done.5.refs_6_.refs_1_), channel_id=1, source_target_pairs={{0,4},{4,0},{8,12},{12,8},{16,20},{20,16},{24,28},{28,24},{1,5},{5... | collective-permute-start | bytes 196616 | tf_op jit(solution)/shard_map/ppermute | solution.py:24
  18.3 5.2 %copy-start = (bf16[2048,1024]{1,0:T(8,128)(2,1)S(1)}, bf16[2048,1024]{1,0:T(8,128)(2,1)}, u32[]{:S(2)}) copy-start(bf16[2048,1024]{1,0:T(8,128)(2,1)} %refs_9_.1) | copy-start | bytes 12582916
  18.4 5.2 %copy-start.2 = (bf16[2048,256]{1,0:T(8,128)(2,1)S(1)}, bf16[2048,256]{1,0:T(8,128)(2,1)}, u32[]{:S(2)}) copy-start(bf16[2048,256]{1,0:T(8,128)(2,1)} %refs_8_.2) | copy-start | bytes 3145732
  18.4 5.2 %copy-start.7 = (f32[2048]{0:T(1024)S(1)}, f32[2048]{0:T(1024)}, u32[]{:S(2)}) copy-start(f32[2048]{0:T(1024)} %param.19) | copy-start | bytes 24580
  18.4 15.9 %collective-permute-start.13 = (bf16[4,8,2048]{2,1,0:T(8,128)(2,1)S(1)}, bf16[4,8,2048]{2,1,0:T(8,128)(2,1)S(1)}, u32[]{:S(2)}, u32[]{:S(2)}) collective-permute-start(bf16[4,8,2048]{2,1,0:T(8,128)(2,1)S(1)} %shard_map.154.refs_0_.refs_2_), channel_id=1, source_target_pairs={{0,2},{1,3},{2,0},{3,1},{4,6},{5,7},{6,4},{7,5},{8,10},{9,11},{10,... | collective-permute-start | bytes 393224 | tf_op jit(solution)/shard_map/ppermute | solution.py:24
  22.0 4.3 %collective-permute-start.17 = (bf16[2,8,2048]{2,1,0:T(8,128)(2,1)S(1)}, bf16[2,8,2048]{2,1,0:T(8,128)(2,1)S(1)}, u32[]{:S(2)}, u32[]{:S(2)}) collective-permute-start(bf16[2,8,2048]{2,1,0:T(8,128)(2,1)S(1)} %shard_map.157), channel_id=1, source_target_pairs={{0,4},{4,0},{8,12},{12,8},{16,20},{20,16},{24,28},{28,24},{1,5},{5... | collective-permute-start | bytes 196616 | tf_op jit(solution)/shard_map/ppermute | solution.py:24
  25.1 2.8 %collective-permute-start.7 = (bf16[128,896]{1,0:T(8,128)(2,1)S(1)}, bf16[128,896]{1,0:T(8,128)(2,1)S(1)}, u32[]{:S(2)}, u32[]{:S(2)}) collective-permute-start(bf16[128,896]{1,0:T(8,128)(2,1)S(1)} %get-tuple-element.46.own_ref), channel_id=1, source_target_pairs={{0,1},{1,0},{2,3},{3,2},{4,5},{5,4},{6,7},{7,6},{8,9},{9,8},{10,11... | collective-permute-start | bytes 688136 | tf_op jit(solution)/shard_map/ppermute | solution.py:24
  26.3 6.1 %collective-permute-start.18 = (bf16[4,8,2048]{2,1,0:T(8,128)(2,1)S(1)}, bf16[4,8,2048]{2,1,0:T(8,128)(2,1)S(1)}, u32[]{:S(2)}, u32[]{:S(2)}) collective-permute-start(bf16[4,8,2048]{2,1,0:T(8,128)(2,1)S(1)} %shard_map.158.refs_0_.refs_5_), channel_id=1, source_target_pairs={{0,2},{1,3},{2,0},{3,1},{4,6},{5,7},{6,4},{7,5},{8,10},{9,11},{10,... | collective-permute-start | bytes 393224 | tf_op jit(solution)/shard_map/ppermute | solution.py:24
  28.6 5.5 %collective-permute-start.8 = (bf16[128,384]{1,0:T(8,128)(2,1)S(1)}, bf16[128,384]{1,0:T(8,128)(2,1)S(1)}, u32[]{:S(2)}, u32[]{:S(2)}) collective-permute-start(bf16[128,384]{1,0:T(8,128)(2,1)S(1)} %get-tuple-element.48.own_ref), channel_id=1, source_target_pairs={{0,2},{1,3},{2,0},{3,1},{4,6},{5,7},{6,4},{7,5},{8,10},{9,11},{10,... | collective-permute-start | bytes 294920 | tf_op jit(solution)/shard_map/ppermute | solution.py:24
  29.3 9.5 %collective-permute-start.11 = (bf16[128,128]{1,0:T(8,128)(2,1)S(1)}, bf16[128,128]{1,0:T(8,128)(2,1)S(1)}, u32[]{:S(2)}, u32[]{:S(2)}) collective-permute-start(bf16[128,128]{1,0:T(8,128)(2,1)S(1)} %get-tuple-element.50), channel_id=1, source_target_pairs={{0,4},{1,5},{2,6},{3,7},{4,12},{5,13},{6,14},{7,15},{8,20},{9,21},... | collective-permute-start | bytes 98312 | tf_op jit(solution)/shard_map/ppermute | solution.py:653
  30.9 7.9 %collective-permute-start.12 = (bf16[128,128]{1,0:T(8,128)(2,1)S(1)}, bf16[128,128]{1,0:T(8,128)(2,1)S(1)}, u32[]{:S(2)}, u32[]{:S(2)}) collective-permute-start(bf16[128,128]{1,0:T(8,128)(2,1)S(1)} %get-tuple-element.50), channel_id=1, source_target_pairs={{0,6},{1,7},{2,4},{3,5},{4,14},{5,15},{6,12},{7,13},{8,22},{9,23},... | collective-permute-start | bytes 98312 | tf_op jit(solution)/shard_map/ppermute | solution.py:653
  32.5 6.4 %collective-permute-start.10 = (bf16[128,128]{1,0:T(8,128)(2,1)S(1)}, bf16[128,128]{1,0:T(8,128)(2,1)S(1)}, u32[]{:S(2)}, u32[]{:S(2)}) collective-permute-start(bf16[128,128]{1,0:T(8,128)(2,1)S(1)} %get-tuple-element.49), channel_id=1, source_target_pairs={{0,2},{1,3},{2,0},{3,1},{4,10},{5,11},{6,8},{7,9},{8,18},{9,19},{1... | collective-permute-start | bytes 98312 | tf_op jit(solution)/shard_map/ppermute | solution.py:653
  34.2 1.6 %collective-permute-start.19 = (bf16[2,4,8,2048]{3,2,1,0:T(8,128)(2,1)S(1)}, bf16[2,4,8,2048]{3,2,1,0:T(8,128)(2,1)S(1)}, u32[]{:S(2)}, u32[]{:S(2)}) collective-permute-start(bf16[2,4,8,2048]{3,2,1,0:T(8,128)(2,1)S(1)} %shard_map.159), channel_id=1, source_target_pairs={{0,1},{1,0},{2,3},{3,2},{4,5},{5,4},{6,7},{7,6},{8,9},{9,8},{10,11... | collective-permute-start | bytes 786440 | tf_op jit(solution)/shard_map/ppermute | solution.py:24
  34.3 2.1 %collective-permute-start.14 = (bf16[2,4,8,2048]{3,2,1,0:T(8,128)(2,1)S(1)}, bf16[2,4,8,2048]{3,2,1,0:T(8,128)(2,1)S(1)}, u32[]{:S(2)}, u32[]{:S(2)}) collective-permute-start(bf16[2,4,8,2048]{3,2,1,0:T(8,128)(2,1)S(1)} %shard_map.155), channel_id=1, source_target_pairs={{0,1},{1,0},{2,3},{3,2},{4,5},{5,4},{6,7},{7,6},{8,9},{9,8},{10,11... | collective-permute-start | bytes 786440 | tf_op jit(solution)/shard_map/ppermute | solution.py:24
  35.8 3.1 %collective-permute-start.9 = (bf16[128,128]{1,0:T(8,128)(2,1)S(1)}, bf16[128,128]{1,0:T(8,128)(2,1)S(1)}, u32[]{:S(2)}, u32[]{:S(2)}) collective-permute-start(bf16[128,128]{1,0:T(8,128)(2,1)S(1)} %get-tuple-element.49), channel_id=1, source_target_pairs={{0,0},{1,1},{2,2},{3,3},{4,8},{5,9},{6,10},{7,11},{8,16},{9,17},{1... | collective-permute-start | bytes 98312 | tf_op jit(solution)/shard_map/ppermute | solution.py:653
  38.9 6.7 %copy-start.1 = (bf16[1024,2048]{1,0:T(8,128)(2,1)S(1)}, bf16[1024,2048]{1,0:T(8,128)(2,1)}, u32[]{:S(2)}) copy-start(bf16[1024,2048]{1,0:T(8,128)(2,1)} %refs_4_.2) | copy-start | bytes 12582916
  40.0 4.3 %collective-permute-start.21 = (bf16[32,1024]{1,0:T(8,128)(2,1)S(1)}, bf16[32,1024]{1,0:T(8,128)(2,1)S(1)}, u32[]{:S(2)}, u32[]{:S(2)}) collective-permute-start(bf16[32,1024]{1,0:T(8,128)(2,1)S(1)} %shard_map.161.refs_0_), channel_id=1, source_target_pairs={{0,2},{1,3},{2,0},{3,1},{4,6},{5,7},{6,4},{7,5},{8,10},{9,11},{10,... | collective-permute-start | bytes 196616 | tf_op jit(solution)/shard_map/ppermute | solution.py:24
  41.6 2.7 %collective-permute-start.20 = (bf16[32,1024]{1,0:T(8,128)(2,1)S(1)}, bf16[32,1024]{1,0:T(8,128)(2,1)S(1)}, u32[]{:S(2)}, u32[]{:S(2)}) collective-permute-start(bf16[32,1024]{1,0:T(8,128)(2,1)S(1)} %shard_map.161.refs_0_), channel_id=1, source_target_pairs={{0,1},{1,0},{2,3},{3,2},{4,5},{5,4},{6,7},{7,6},{8,9},{9,8},{10,11... | collective-permute-start | bytes 196616 | tf_op jit(solution)/shard_map/ppermute | solution.py:24
  44.4 1.3 %collective-permute-start.22 = (bf16[32,1024]{1,0:T(8,128)(2,1)S(1)}, bf16[32,1024]{1,0:T(8,128)(2,1)S(1)}, u32[]{:S(2)}, u32[]{:S(2)}) collective-permute-start(bf16[32,1024]{1,0:T(8,128)(2,1)S(1)} %collective-permute-done.21.refs_2_), channel_id=1, source_target_pairs={{0,1},{1,0},{2,3},{3,2},{4,5},{5,4},{6,7},{7,6},{8,9},{9,8},{10,11... | collective-permute-start | bytes 196616 | tf_op jit(solution)/shard_map/ppermute | solution.py:24
  46.9 9.3 %collective-permute-start.25 = (bf16[16,2048]{1,0:T(8,128)(2,1)S(1)}, bf16[16,2048]{1,0:T(8,128)(2,1)S(1)}, u32[]{:S(2)}, u32[]{:S(2)}) collective-permute-start(bf16[16,2048]{1,0:T(8,128)(2,1)S(1)} %get-tuple-element.64), channel_id=1, source_target_pairs={{0,4},{4,0},{8,12},{12,8},{16,20},{20,16},{24,28},{28,24},{1,5},{5... | collective-permute-start | bytes 196616 | tf_op jit(solution)/shard_map/ppermute | solution.py:24
  52.7 6.5 %collective-permute-start.23 = (bf16[16,2048]{1,0:T(8,128)(2,1)S(1)}, bf16[16,2048]{1,0:T(8,128)(2,1)S(1)}, u32[]{:S(2)}, u32[]{:S(2)}) collective-permute-start(bf16[16,2048]{1,0:T(8,128)(2,1)S(1)} %get-tuple-element.61), channel_id=1, source_target_pairs={{0,4},{4,0},{8,12},{12,8},{16,20},{20,16},{24,28},{28,24},{1,5},{5... | collective-permute-start | bytes 196616 | tf_op jit(solution)/shard_map/ppermute | solution.py:24
  52.8 7.2 %collective-permute-start.28 = (bf16[16,2048]{1,0:T(8,128)(2,1)S(1)}, bf16[16,2048]{1,0:T(8,128)(2,1)S(1)}, u32[]{:S(2)}, u32[]{:S(2)}) collective-permute-start(bf16[16,2048]{1,0:T(8,128)(2,1)S(1)} %get-tuple-element.66), channel_id=1, source_target_pairs={{0,8},{4,12},{8,0},{12,4},{16,24},{20,28},{24,16},{28,20},{1,9},{5... | collective-permute-start | bytes 196616 | tf_op jit(solution)/shard_map/ppermute | solution.py:24
  53.8 6.3 %collective-permute-start.29 = (bf16[16,2048]{1,0:T(8,128)(2,1)S(1)}, bf16[16,2048]{1,0:T(8,128)(2,1)S(1)}, u32[]{:S(2)}, u32[]{:S(2)}) collective-permute-start(bf16[16,2048]{1,0:T(8,128)(2,1)S(1)} %get-tuple-element.67), channel_id=1, source_target_pairs={{0,12},{4,8},{8,4},{12,0},{16,28},{20,24},{24,20},{28,16},{1,13},{... | collective-permute-start | bytes 196616 | tf_op jit(solution)/shard_map/ppermute | solution.py:24
  56.2 6.1 %collective-permute-start.26 = (bf16[16,2048]{1,0:T(8,128)(2,1)S(1)}, bf16[16,2048]{1,0:T(8,128)(2,1)S(1)}, u32[]{:S(2)}, u32[]{:S(2)}) collective-permute-start(bf16[16,2048]{1,0:T(8,128)(2,1)S(1)} %shard_map.164), channel_id=1, source_target_pairs={{0,24},{4,28},{8,16},{12,20},{16,8},{20,12},{24,0},{28,4},{1,25},{... | collective-permute-start | bytes 196616 | tf_op jit(solution)/shard_map/ppermute | solution.py:24
  59.2 18.7 %slice-start = ((s8[7340032]{0:T(1024)(128)(4,1)}), s8[4194304]{0:T(1024)(128)(4,1)S(1)}, s32[]{:S(2)}) async-start(s8[7340032]{0:T(1024)(128)(4,1)} %bitcast.12), calls=%async_computation | async-start | bytes 8388608
  59.2 5.3 %collective-permute-start.24 = (bf16[16,2048]{1,0:T(8,128)(2,1)S(1)}, bf16[16,2048]{1,0:T(8,128)(2,1)S(1)}, u32[]{:S(2)}, u32[]{:S(2)}) collective-permute-start(bf16[16,2048]{1,0:T(8,128)(2,1)S(1)} %get-tuple-element.63), channel_id=1, source_target_pairs={{0,16},{4,20},{8,24},{12,28},{16,0},{20,4},{24,8},{28,12},{1,17},{... | collective-permute-start | bytes 196616 | tf_op jit(solution)/shard_map/ppermute | solution.py:24
  59.3 18.6 %slice-start.1 = ((s8[7340032]{0:T(1024)(128)(4,1)}), s8[3145728]{0:T(1024)(128)(4,1)S(1)}, s32[]{:S(2)}) async-start(s8[7340032]{0:T(1024)(128)(4,1)} %bitcast.12), calls=%async_computation.1 | async-start | bytes 6291456
  59.3 5.2 %collective-permute-start.27 = (bf16[16,2048]{1,0:T(8,128)(2,1)S(1)}, bf16[16,2048]{1,0:T(8,128)(2,1)S(1)}, u32[]{:S(2)}, u32[]{:S(2)}) collective-permute-start(bf16[16,2048]{1,0:T(8,128)(2,1)S(1)} %get-tuple-element.65), channel_id=1, source_target_pairs={{0,4},{4,0},{8,12},{12,8},{16,20},{20,16},{24,28},{28,24},{1,5},{5... | collective-permute-start | bytes 196616 | tf_op jit(solution)/shard_map/ppermute | solution.py:24
  64.5 13.4 %copy-start.8 = (f32[2048]{0:T(1024)S(1)}, f32[2048]{0:T(1024)}, u32[]{:S(2)}) copy-start(f32[2048]{0:T(1024)} %param.20) | copy-start | bytes 24580
  64.5 15.3 %slice-start.2 = ((s8[7340032]{0:T(1024)(128)(4,1)}), s8[4194304]{0:T(1024)(128)(4,1)S(1)}, s32[]{:S(2)}) async-start(s8[7340032]{0:T(1024)(128)(4,1)} %bitcast.14), calls=%async_computation.2 | async-start | bytes 8388608
  65.2 6.5 %collective-permute-start.33 = (bf16[16,2048]{1,0:T(8,128)(2,1)S(1)}, bf16[16,2048]{1,0:T(8,128)(2,1)S(1)}, u32[]{:S(2)}, u32[]{:S(2)}) collective-permute-start(bf16[16,2048]{1,0:T(8,128)(2,1)S(1)} %get-tuple-element.69.refs_0_), channel_id=1, source_target_pairs={{0,16},{4,20},{8,24},{12,28},{16,0},{20,4},{24,8},{28,12},{1,17},{... | collective-permute-start | bytes 196616 | tf_op jit(solution)/shard_map/ppermute | solution.py:24
  67.2 6.5 %collective-permute-start.35 = (bf16[16,2048]{1,0:T(8,128)(2,1)S(1)}, bf16[16,2048]{1,0:T(8,128)(2,1)S(1)}, u32[]{:S(2)}, u32[]{:S(2)}) collective-permute-start(bf16[16,2048]{1,0:T(8,128)(2,1)S(1)} %get-tuple-element.69.refs_0_), channel_id=1, source_target_pairs={{0,24},{4,28},{8,16},{12,20},{16,8},{20,12},{24,0},{28,4},{1,25},{... | collective-permute-start | bytes 196616 | tf_op jit(solution)/shard_map/ppermute | solution.py:24
  68.2 6.2 %collective-permute-start.30 = (bf16[16,2048]{1,0:T(8,128)(2,1)S(1)}, bf16[16,2048]{1,0:T(8,128)(2,1)S(1)}, u32[]{:S(2)}, u32[]{:S(2)}) collective-permute-start(bf16[16,2048]{1,0:T(8,128)(2,1)S(1)} %get-tuple-element.69.refs_0_), channel_id=1, source_target_pairs={{0,4},{4,0},{8,12},{12,8},{16,20},{20,16},{24,28},{28,24},{1,5},{5... | collective-permute-start | bytes 196616 | tf_op jit(solution)/shard_map/ppermute | solution.py:24
  69.5 5.0 %collective-permute-start.31 = (bf16[16,2048]{1,0:T(8,128)(2,1)S(1)}, bf16[16,2048]{1,0:T(8,128)(2,1)S(1)}, u32[]{:S(2)}, u32[]{:S(2)}) collective-permute-start(bf16[16,2048]{1,0:T(8,128)(2,1)S(1)} %get-tuple-element.69.refs_0_), channel_id=1, source_target_pairs={{0,8},{4,12},{8,0},{12,4},{16,24},{20,28},{24,16},{28,20},{1,9},{5... | collective-permute-start | bytes 196616 | tf_op jit(solution)/shard_map/ppermute | solution.py:24
  69.6 5.5 %collective-permute-start.32 = (bf16[16,2048]{1,0:T(8,128)(2,1)S(1)}, bf16[16,2048]{1,0:T(8,128)(2,1)S(1)}, u32[]{:S(2)}, u32[]{:S(2)}) collective-permute-start(bf16[16,2048]{1,0:T(8,128)(2,1)S(1)} %get-tuple-element.69.refs_0_), channel_id=1, source_target_pairs={{0,12},{4,8},{8,4},{12,0},{16,28},{20,24},{24,20},{28,16},{1,13},{... | collective-permute-start | bytes 196616 | tf_op jit(solution)/shard_map/ppermute | solution.py:24
  71.8 4.7 %collective-permute-start.34 = (bf16[16,2048]{1,0:T(8,128)(2,1)S(1)}, bf16[16,2048]{1,0:T(8,128)(2,1)S(1)}, u32[]{:S(2)}, u32[]{:S(2)}) collective-permute-start(bf16[16,2048]{1,0:T(8,128)(2,1)S(1)} %collective-permute-done.33.refs_4_), channel_id=1, source_target_pairs={{0,4},{4,0},{8,12},{12,8},{16,20},{20,16},{24,28},{28,24},{1,5},{5... | collective-permute-start | bytes 196616 | tf_op jit(solution)/shard_map/ppermute | solution.py:24
  73.6 4.3 %collective-permute-start.36 = (bf16[16,2048]{1,0:T(8,128)(2,1)S(1)}, bf16[16,2048]{1,0:T(8,128)(2,1)S(1)}, u32[]{:S(2)}, u32[]{:S(2)}) collective-permute-start(bf16[16,2048]{1,0:T(8,128)(2,1)S(1)} %collective-permute-done.35.refs_6_), channel_id=1, source_target_pairs={{0,4},{4,0},{8,12},{12,8},{16,20},{20,16},{24,28},{28,24},{1,5},{5... | collective-permute-start | bytes 196616 | tf_op jit(solution)/shard_map/ppermute | solution.py:24
  77.9 17.8 %slice-start.4 = ((s8[7340032]{0:T(1024)(128)(4,1)}), s8[4194304]{0:T(1024)(128)(4,1)S(1)}, s32[]{:S(2)}) async-start(s8[7340032]{0:T(1024)(128)(4,1)} %bitcast.16), calls=%async_computation.4 | async-start | bytes 8388608
  79.8 1.8 %collective-permute-start.37 = (bf16[64,1920]{1,0:T(8,128)(2,1)S(1)}, bf16[64,1920]{1,0:T(8,128)(2,1)S(1)}, u32[]{:S(2)}, u32[]{:S(2)}) collective-permute-start(bf16[64,1920]{1,0:T(8,128)(2,1)S(1)} %get-tuple-element.71), channel_id=1, source_target_pairs={{0,1},{1,0},{2,3},{3,2},{4,5},{5,4},{6,7},{7,6},{8,9},{9,8},{10,11... | collective-permute-start | bytes 737288 | tf_op jit(solution)/shard_map/ppermute | solution.py:24
  79.9 15.9 %slice-start.5 = ((s8[7340032]{0:T(1024)(128)(4,1)}), s8[3145728]{0:T(1024)(128)(4,1)S(1)}, s32[]{:S(2)}) async-start(s8[7340032]{0:T(1024)(128)(4,1)} %bitcast.16), calls=%async_computation.5 | async-start | bytes 6291456
  81.0 2.0 %collective-permute-start.39 = (bf16[64,1792]{1,0:T(8,128)(2,1)S(1)}, bf16[64,1792]{1,0:T(8,128)(2,1)S(1)}, u32[]{:S(2)}, u32[]{:S(2)}) collective-permute-start(bf16[64,1792]{1,0:T(8,128)(2,1)S(1)} %get-tuple-element.74), channel_id=1, source_target_pairs={{0,1},{1,0},{2,3},{3,2},{4,5},{5,4},{6,7},{7,6},{8,9},{9,8},{10,11... | collective-permute-start | bytes 688136 | tf_op jit(solution)/shard_map/ppermute | solution.py:24
  81.7 6.2 %collective-permute-start.38 = (bf16[32,1920]{1,0:T(8,128)(2,1)S(1)}, bf16[32,1920]{1,0:T(8,128)(2,1)S(1)}, u32[]{:S(2)}, u32[]{:S(2)}) collective-permute-start(bf16[32,1920]{1,0:T(8,128)(2,1)S(1)} %slice.64), channel_id=1, source_target_pairs={{0,2},{1,3},{2,0},{3,1},{4,6},{5,7},{6,4},{7,5},{8,10},{9,11},{10,... | collective-permute-start | bytes 368648 | tf_op jit(solution)/shard_map/ppermute | solution.py:24
  83.1 6.3 %collective-permute-start.40 = (bf16[32,1792]{1,0:T(8,128)(2,1)S(1)}, bf16[32,1792]{1,0:T(8,128)(2,1)S(1)}, u32[]{:S(2)}, u32[]{:S(2)}) collective-permute-start(bf16[32,1792]{1,0:T(8,128)(2,1)S(1)} %slice.65), channel_id=1, source_target_pairs={{0,2},{1,3},{2,0},{3,1},{4,6},{5,7},{6,4},{7,5},{8,10},{9,11},{10,... | collective-permute-start | bytes 344072 | tf_op jit(solution)/shard_map/ppermute | solution.py:24
  89.6 4.9 %collective-permute-start.42 = (bf16[32,1792]{1,0:T(8,128)(2,1)S(1)}, bf16[32,1792]{1,0:T(8,128)(2,1)S(1)}, u32[]{:S(2)}, u32[]{:S(2)}) collective-permute-start(bf16[32,1792]{1,0:T(8,128)(2,1)S(1)} %fusion.2.refs_0_), channel_id=1, source_target_pairs={{0,2},{1,3},{2,0},{3,1},{4,6},{5,7},{6,4},{7,5},{8,10},{9,11},{10,... | collective-permute-start | bytes 344072 | tf_op jit(solution)/shard_map/ppermute | solution.py:24
  91.0 3.5 %collective-permute-start.41 = (bf16[32,1792]{1,0:T(8,128)(2,1)S(1)}, bf16[32,1792]{1,0:T(8,128)(2,1)S(1)}, u32[]{:S(2)}, u32[]{:S(2)}) collective-permute-start(bf16[32,1792]{1,0:T(8,128)(2,1)S(1)} %fusion.2.refs_0_), channel_id=1, source_target_pairs={{0,1},{1,0},{2,3},{3,2},{4,5},{5,4},{6,7},{7,6},{8,9},{9,8},{10,11... | collective-permute-start | bytes 344072 | tf_op jit(solution)/shard_map/ppermute | solution.py:24
  94.5 1.3 %collective-permute-start.43 = (bf16[32,1792]{1,0:T(8,128)(2,1)S(1)}, bf16[32,1792]{1,0:T(8,128)(2,1)S(1)}, u32[]{:S(2)}, u32[]{:S(2)}) collective-permute-start(bf16[32,1792]{1,0:T(8,128)(2,1)S(1)} %collective-permute-done.42.refs_2_), channel_id=1, source_target_pairs={{0,1},{1,0},{2,3},{3,2},{4,5},{5,4},{6,7},{7,6},{8,9},{9,8},{10,11... | collective-permute-start | bytes 344072 | tf_op jit(solution)/shard_map/ppermute | solution.py:24
  97.5 4.9 %collective-permute-start.46 = (bf16[16,2048]{1,0:T(8,128)(2,1)S(1)}, bf16[16,2048]{1,0:T(8,128)(2,1)S(1)}, u32[]{:S(2)}, u32[]{:S(2)}) collective-permute-start(bf16[16,2048]{1,0:T(8,128)(2,1)S(1)} %get-tuple-element.80), channel_id=1, source_target_pairs={{0,4},{4,0},{8,12},{12,8},{16,20},{20,16},{24,28},{28,24},{1,5},{5... | collective-permute-start | bytes 196616 | tf_op jit(solution)/shard_map/ppermute | solution.py:24
  98.3 6.4 %collective-permute-start.44 = (bf16[16,2048]{1,0:T(8,128)(2,1)S(1)}, bf16[16,2048]{1,0:T(8,128)(2,1)S(1)}, u32[]{:S(2)}, u32[]{:S(2)}) collective-permute-start(bf16[16,2048]{1,0:T(8,128)(2,1)S(1)} %get-tuple-element.77), channel_id=1, source_target_pairs={{0,4},{4,0},{8,12},{12,8},{16,20},{20,16},{24,28},{28,24},{1,5},{5... | collective-permute-start | bytes 196616 | tf_op jit(solution)/shard_map/ppermute | solution.py:24
  99.6 6.2 %collective-permute-start.49 = (bf16[16,2048]{1,0:T(8,128)(2,1)S(1)}, bf16[16,2048]{1,0:T(8,128)(2,1)S(1)}, u32[]{:S(2)}, u32[]{:S(2)}) collective-permute-start(bf16[16,2048]{1,0:T(8,128)(2,1)S(1)} %get-tuple-element.82), channel_id=1, source_target_pairs={{0,8},{4,12},{8,0},{12,4},{16,24},{20,28},{24,16},{28,20},{1,9},{5... | collective-permute-start | bytes 196616 | tf_op jit(solution)/shard_map/ppermute | solution.py:24
  100.3 5.5 %collective-permute-start.50 = (bf16[16,2048]{1,0:T(8,128)(2,1)S(1)}, bf16[16,2048]{1,0:T(8,128)(2,1)S(1)}, u32[]{:S(2)}, u32[]{:S(2)}) collective-permute-start(bf16[16,2048]{1,0:T(8,128)(2,1)S(1)} %get-tuple-element.83), channel_id=1, source_target_pairs={{0,12},{4,8},{8,4},{12,0},{16,28},{20,24},{24,20},{28,16},{1,13},{... | collective-permute-start | bytes 196616 | tf_op jit(solution)/shard_map/ppermute | solution.py:24
  102.4 6.1 %collective-permute-start.47 = (bf16[16,2048]{1,0:T(8,128)(2,1)S(1)}, bf16[16,2048]{1,0:T(8,128)(2,1)S(1)}, u32[]{:S(2)}, u32[]{:S(2)}) collective-permute-start(bf16[16,2048]{1,0:T(8,128)(2,1)S(1)} %shard_map.170), channel_id=1, source_target_pairs={{0,24},{4,28},{8,16},{12,20},{16,8},{20,12},{24,0},{28,4},{1,25},{... | collective-permute-start | bytes 196616 | tf_op jit(solution)/shard_map/ppermute | solution.py:24
  104.8 5.7 %collective-permute-start.45 = (bf16[16,2048]{1,0:T(8,128)(2,1)S(1)}, bf16[16,2048]{1,0:T(8,128)(2,1)S(1)}, u32[]{:S(2)}, u32[]{:S(2)}) collective-permute-start(bf16[16,2048]{1,0:T(8,128)(2,1)S(1)} %get-tuple-element.79), channel_id=1, source_target_pairs={{0,16},{4,20},{8,24},{12,28},{16,0},{20,4},{24,8},{28,12},{1,17},{... | collective-permute-start | bytes 196616 | tf_op jit(solution)/shard_map/ppermute | solution.py:24
  104.9 5.7 %collective-permute-start.48 = (bf16[16,2048]{1,0:T(8,128)(2,1)S(1)}, bf16[16,2048]{1,0:T(8,128)(2,1)S(1)}, u32[]{:S(2)}, u32[]{:S(2)}) collective-permute-start(bf16[16,2048]{1,0:T(8,128)(2,1)S(1)} %get-tuple-element.81), channel_id=1, source_target_pairs={{0,4},{4,0},{8,12},{12,8},{16,20},{20,16},{24,28},{28,24},{1,5},{5... | collective-permute-start | bytes 196616 | tf_op jit(solution)/shard_map/ppermute | solution.py:24
  (4 other events, 5.6 us)

commit v17 on v16

--- a/solution.py
+++ b/solution.py
@@ -609,7 +609,7 @@
         if len(pieces) == 2:
             one, two = [ref[...].astype(F32) for ref in piece_refs]
         else:
-            one, two = [piece_refs[i][...].astype(F32) + piece_refs[i + 1][...].astype(F32) for i in (0, 2)]
+            two, one = [piece_refs[i][...].astype(F32) + piece_refs[i + 1][...].astype(F32) for i in (0, 2)]
             one, two = [(x * scale_ref[...]).astype(BF16).astype(F32) for x in (one, two)]
         plain = jnp.where(even, one, two)
         values = jnp.where(even, two, one).astype(BF16)
@@ -651,7 +651,7 @@
         for k in (0, 2):
             pairs = [(i * tensor + t, to[i] * tensor + (t ^ k)) for i in range(groups) for t in range(tensor)]
             moved.append(lax.ppermute(piece, ("dp", "tensor"), pairs))
-    return moved
+    return moved[2:] + moved[:2]
 
 
 def move_keyvals(pieces):

time: 111 us -> 111 us (level)
  waiting for transfers between devices: 32.2 us -> 30.9 us
    ppermute x4, starting transfers between devices: 5.32 us -> 7.83 us  [send_keyvals(): moved.append(lax.ppermute(piece, ('dp', 'tensor'), pairs))]
    ppermute x47, starting transfers between devices: 55.5 us -> 53.5 us  [swap(): return lax.ppermute(x, axis, [(i, i ^ bits) for i in range(size)])]
    ppermute x47, waiting for transfers between devices: 32.2 us -> 30.9 us  [swap(): return lax.ppermute(x, axis, [(i, i ^ bits) for i in range(size)])]
  transfers between devices with their start and end apart: 51 -> 51, of which waited for: 21 -> 19; matrix products, arithmetic and copies ran while one was open for 1% -> 1% of each run, Pallas kernels for 6% -> 7%
where the time goes in v17:
time: 111 us; the launch traced here: 110 us
  starting transfers between devices  61.3 us (55%)
  waiting for transfers between devices  30.9 us (28%)
  Pallas kernels  14.5 us (13%)
  local copies, waits for them, and re-layouts  1.97 us (2%)
    ppermute x47, starting transfers between devices, swap(): return lax.ppermute(x, axis, [(i, i ^ bits) for i in range(size)])  53.5 us
    ppermute x47, waiting for transfers between devices, swap(): return lax.ppermute(x, axis, [(i, i ^ bits) for i in range(size)])  30.9 us
    pallas_call x23, Pallas kernels, call(): pl.pallas_call(body, out_shape=outs, in_specs=specs, out_specs=jax.tree.m...  14.5 us
    ppermute x4, starting transfers between devices, send_keyvals(): moved.append(lax.ppermute(piece, ('dp', 'tensor'), pairs))  7.83 us
  transfers between devices with their start and end apart: 51, of which 19 were waited for; matrix products, arithmetic and copies ran while one was open for 1% of the time, Pallas kernels for 7%

profile of v17, /device:TPU:0, one launch (start us, length us, event | category | flops | bytes accessed | tf_op | source)
XLA Modules:
  0.0 110.4 jit_solution(15433515680049155983)
XLA Ops:
  0.7 0.8 copy-done.5
  1.5 0.8 copy-done.6
  2.2 4.0 %collective-permute-start.3 = (bf16[16,2048]{1,0:T(8,128)(2,1)S(1)}, bf16[16,2048]{1,0:T(8,128)(2,1)S(1)}, u32[]{:S(2)}, u32[]{:S(2)}) collective-permute-start(bf16[16,2048]{1,0:T(8,128)(2,1)S(1)} %shard_map.149.x_ref.refs_0_.refs_10_.after_ref.refs_5_), channel_id=1, source_target_pairs={{0,16},{4,20},{8,24},{12,28},{16,0},{20,4},{24,8},{28,12},{1,17},{... | collective-permute-start | bytes 196616 | tf_op jit(solution)/shard_map/ppermute | solution.py:24
  6.3 1.3 %collective-permute-start.5 = (bf16[16,2048]{1,0:T(8,128)(2,1)S(1)}, bf16[16,2048]{1,0:T(8,128)(2,1)S(1)}, u32[]{:S(2)}, u32[]{:S(2)}) collective-permute-start(bf16[16,2048]{1,0:T(8,128)(2,1)S(1)} %shard_map.149.x_ref.refs_0_.refs_10_.after_ref.refs_5_), channel_id=1, source_target_pairs={{0,24},{4,28},{8,16},{12,20},{16,8},{20,12},{24,0},{28,4},{1,25},{... | collective-permute-start | bytes 196616 | tf_op jit(solution)/shard_map/ppermute | solution.py:24
  8.3 1.6 %collective-permute-start = (bf16[24,2048]{1,0:T(8,128)(2,1)S(1)}, bf16[24,2048]{1,0:T(8,128)(2,1)S(1)}, u32[]{:S(2)}, u32[]{:S(2)}) collective-permute-start(bf16[24,2048]{1,0:T(8,128)(2,1)S(1)} %get-tuple-element.43), channel_id=1, source_target_pairs={{0,4},{4,0},{8,12},{12,8},{16,20},{20,16},{24,28},{28,24},{1,5},{5... | collective-permute-start | bytes 294920 | tf_op jit(solution)/shard_map/ppermute | solution.py:24
  10.1 1.8 %collective-permute-start.2 = (bf16[24,2048]{1,0:T(8,128)(2,1)S(1)}, bf16[24,2048]{1,0:T(8,128)(2,1)S(1)}, u32[]{:S(2)}, u32[]{:S(2)}) collective-permute-start(bf16[24,2048]{1,0:T(8,128)(2,1)S(1)} %get-tuple-element.45), channel_id=1, source_target_pairs={{0,12},{4,8},{8,4},{12,0},{16,28},{20,24},{24,20},{28,16},{1,13},{... | collective-permute-start | bytes 294920 | tf_op jit(solution)/shard_map/ppermute | solution.py:24
  12.5 0.6 shard_map.156
  13.1 2.8 %collective-permute-start.15 = (bf16[2,8,2048]{2,1,0:T(8,128)(2,1)S(1)}, bf16[2,8,2048]{2,1,0:T(8,128)(2,1)S(1)}, u32[]{:S(2)}, u32[]{:S(2)}) collective-permute-start(bf16[2,8,2048]{2,1,0:T(8,128)(2,1)S(1)} %get-tuple-element.53), channel_id=1, source_target_pairs={{0,16},{4,20},{8,24},{12,28},{16,0},{20,4},{24,8},{28,12},{1,17},{... | collective-permute-start | bytes 196616 | tf_op jit(solution)/shard_map/ppermute | solution.py:24
  16.3 1.6 %collective-permute-start.4 = (bf16[16,2048]{1,0:T(8,128)(2,1)S(1)}, bf16[16,2048]{1,0:T(8,128)(2,1)S(1)}, u32[]{:S(2)}, u32[]{:S(2)}) collective-permute-start(bf16[16,2048]{1,0:T(8,128)(2,1)S(1)} %collective-permute-done.3.refs_4_.refs_0_), channel_id=1, source_target_pairs={{0,4},{4,0},{8,12},{12,8},{16,20},{20,16},{24,28},{28,24},{1,5},{5... | collective-permute-start | bytes 196616 | tf_op jit(solution)/shard_map/ppermute | solution.py:24
  18.4 1.8 %collective-permute-start.13 = (bf16[4,8,2048]{2,1,0:T(8,128)(2,1)S(1)}, bf16[4,8,2048]{2,1,0:T(8,128)(2,1)S(1)}, u32[]{:S(2)}, u32[]{:S(2)}) collective-permute-start(bf16[4,8,2048]{2,1,0:T(8,128)(2,1)S(1)} %shard_map.154.refs_0_.refs_2_), channel_id=1, source_target_pairs={{0,2},{1,3},{2,0},{3,1},{4,6},{5,7},{6,4},{7,5},{8,10},{9,11},{10,... | collective-permute-start | bytes 393224 | tf_op jit(solution)/shard_map/ppermute | solution.py:24
  20.2 1.8 %collective-permute-done.16.refs_1_ = bf16[2,8,2048]{2,1,0:T(8,128)(2,1)S(1)} collective-permute-done((bf16[2,8,2048]{2,1,0:T(8,128)(2,1)S(1)}, bf16[2,8,2048]{2,1,0:T(8,128)(2,1)S(1)}, u32[]{:S(2)}, u32[]{:S(2)}) %collective-permute-start.16) | collective-permute-done | bytes 65568 | tf_op jit(solution)/shard_map/ppermute | solution.py:24
  22.0 1.5 %collective-permute-start.17 = (bf16[2,8,2048]{2,1,0:T(8,128)(2,1)S(1)}, bf16[2,8,2048]{2,1,0:T(8,128)(2,1)S(1)}, u32[]{:S(2)}, u32[]{:S(2)}) collective-permute-start(bf16[2,8,2048]{2,1,0:T(8,128)(2,1)S(1)} %shard_map.157), channel_id=1, source_target_pairs={{0,4},{4,0},{8,12},{12,8},{16,20},{20,16},{24,28},{28,24},{1,5},{5... | collective-permute-start | bytes 196616 | tf_op jit(solution)/shard_map/ppermute | solution.py:24
  23.6 1.5 %shard_map.151 = (bf16[128,896]{1,0:T(8,128)(2,1)S(1)}, f32[64,1024]{1,0:T(8,128)S(1)}) custom-call(s32[2]{0:T(128)S(1)} %pad_add_fusion.3.where_ref, f32[1,2048]{1,0:T(1,128)S(1)} %bitcast.18, bf16[16,2048]{1,0:T(8,128)(2,1)S(1)} %shard_map.149.x_ref.refs_0_.refs_10_.after_ref.refs_5_, bf16[24,2048]{1,0:T(8,128)(2,1)S(1)} %collective-permute-done.refs_1_.refs_0_, ...), custom_call_target="tpu_custom_call" | custom-call | flops 6039797760 | bytes 6291456 | tf_op jit(solution)/shard_map/pallas_call | solution.py:45
  25.2 1.1 collective-permute-done.17.refs_2_
  26.3 1.6 %collective-permute-start.18 = (bf16[4,8,2048]{2,1,0:T(8,128)(2,1)S(1)}, bf16[4,8,2048]{2,1,0:T(8,128)(2,1)S(1)}, u32[]{:S(2)}, u32[]{:S(2)}) collective-permute-start(bf16[4,8,2048]{2,1,0:T(8,128)(2,1)S(1)} %shard_map.158.refs_0_.refs_5_), channel_id=1, source_target_pairs={{0,2},{1,3},{2,0},{3,1},{4,6},{5,7},{6,4},{7,5},{8,10},{9,11},{10,... | collective-permute-start | bytes 393224 | tf_op jit(solution)/shard_map/ppermute | solution.py:24
  27.9 0.7 shard_map.152
  29.3 0.7 collective-permute-start.11
  30.0 1.6 %collective-permute-start.12 = (bf16[128,128]{1,0:T(8,128)(2,1)S(1)}, bf16[128,128]{1,0:T(8,128)(2,1)S(1)}, u32[]{:S(2)}, u32[]{:S(2)}) collective-permute-start(bf16[128,128]{1,0:T(8,128)(2,1)S(1)} %get-tuple-element.50), channel_id=1, source_target_pairs={{0,2},{1,3},{2,0},{3,1},{4,10},{5,11},{6,8},{7,9},{8,18},{9,19},{1... | collective-permute-start | bytes 98312 | tf_op jit(solution)/shard_map/ppermute | solution.py:653
  31.6 0.8 collective-permute-done.18.refs_1_.refs_6_
  32.4 3.1 %collective-permute-start.10 = (bf16[128,128]{1,0:T(8,128)(2,1)S(1)}, bf16[128,128]{1,0:T(8,128)(2,1)S(1)}, u32[]{:S(2)}, u32[]{:S(2)}) collective-permute-start(bf16[128,128]{1,0:T(8,128)(2,1)S(1)} %get-tuple-element.49), channel_id=1, source_target_pairs={{0,6},{1,7},{2,4},{3,5},{4,14},{5,15},{6,12},{7,13},{8,22},{9,23},... | collective-permute-start | bytes 98312 | tf_op jit(solution)/shard_map/ppermute | solution.py:653
  36.4 0.8 collective-permute-done.19.refs_7_
  37.1 2.5 %collective-permute-start.9 = (bf16[128,128]{1,0:T(8,128)(2,1)S(1)}, bf16[128,128]{1,0:T(8,128)(2,1)S(1)}, u32[]{:S(2)}, u32[]{:S(2)}) collective-permute-start(bf16[128,128]{1,0:T(8,128)(2,1)S(1)} %get-tuple-element.49), channel_id=1, source_target_pairs={{0,4},{1,5},{2,6},{3,7},{4,12},{5,13},{6,14},{7,15},{8,20},{9,21},... | collective-permute-start | bytes 98312 | tf_op jit(solution)/shard_map/ppermute | solution.py:653
  39.6 2.4 %shard_map.160 = (bf16[256,128]{1,0:T(8,128)(2,1)S(1)}, f32[256,128]{1,0:T(8,128)S(1)}, f32[256,128]{1,0:T(8,128)S(1)}, f32[256,128]{1,0:T(8,128)S(1)}) custom-call(s32[2]{0:T(128)S(1)} %pad_add_fusion.3.where_ref, s32[16]{0:T(128)S(1)} %get-tuple-element.85.anc_ref, f32[4,128]{1,0:T(4,128)S(1)} %copy-done.9, f32[128,128]{1,0:T(8,128)S(1)} %shard_map.153.scale_ref, ...), custom_call_target="tpu_custom_call" | custom-call | flops 5368709120 | bytes 4194304 | tf_op jit(solution)/shard_map/pallas_call | solution.py:45
  42.0 1.1 %shard_map.161.refs_0_ = bf16[32,1024]{1,0:T(8,128)(2,1)S(1)} custom-call(s32[2]{0:T(128)S(1)} %pad_add_fusion.3.where_ref, f32[4,128]{1,0:T(4,128)S(1)} %copy-done.9, s32[256,2]{1,0:T(8,128)S(1)} %copy.20.target_ref, f32[128,128]{1,0:T(8,128)S(1)} %shard_map.153.scale_ref, bf16[128,128]{1,0:T(8,128)(2,1)S(1)} %collective-permute-done.9.refs_0_, ...), custom_call_target="tpu_custom_call" | custom-call | flops 5368709120 | bytes 1048576 | tf_op jit(solution)/shard_map/pallas_call | solution.py:45
  43.2 1.6 %collective-permute-start.21 = (bf16[32,1024]{1,0:T(8,128)(2,1)S(1)}, bf16[32,1024]{1,0:T(8,128)(2,1)S(1)}, u32[]{:S(2)}, u32[]{:S(2)}) collective-permute-start(bf16[32,1024]{1,0:T(8,128)(2,1)S(1)} %shard_map.161.refs_0_), channel_id=1, source_target_pairs={{0,2},{1,3},{2,0},{3,1},{4,6},{5,7},{6,4},{7,5},{8,10},{9,11},{10,... | collective-permute-start | bytes 196616 | tf_op jit(solution)/shard_map/ppermute | solution.py:24
  44.7 2.8 %collective-permute-done.21.refs_2_ = bf16[32,1024]{1,0:T(8,128)(2,1)S(1)} collective-permute-done((bf16[32,1024]{1,0:T(8,128)(2,1)S(1)}, bf16[32,1024]{1,0:T(8,128)(2,1)S(1)}, u32[]{:S(2)}, u32[]{:S(2)}) %collective-permute-start.21) | collective-permute-done | bytes 65568 | tf_op jit(solution)/shard_map/ppermute | solution.py:24
  47.5 1.2 %collective-permute-done.22.refs_3_ = bf16[32,1024]{1,0:T(8,128)(2,1)S(1)} collective-permute-done((bf16[32,1024]{1,0:T(8,128)(2,1)S(1)}, bf16[32,1024]{1,0:T(8,128)(2,1)S(1)}, u32[]{:S(2)}, u32[]{:S(2)}) %collective-permute-start.22) | collective-permute-done | bytes 65568 | tf_op jit(solution)/shard_map/ppermute | solution.py:24
  48.7 1.3 %shard_map.162 = (f32[16,2048]{1,0:T(8,128)S(1)}, bf16[16,2048]{1,0:T(8,128)(2,1)S(1)}, bf16[16,2048]{1,0:T(8,128)(2,1)S(1)}, bf16[16,2048]{1,0:T(8,128)(2,1)S(1...) custom-call(s32[2]{0:T(128)S(1)} %pad_add_fusion.3.where_ref, ...), custom_call_target="tpu_custom_call" | custom-call | flops 5905580032 | bytes 4194304 | tf_op jit(solution)/shard_map/pallas_call | solution.py:45
  50.0 1.5 %collective-permute-start.25 = (bf16[16,2048]{1,0:T(8,128)(2,1)S(1)}, bf16[16,2048]{1,0:T(8,128)(2,1)S(1)}, u32[]{:S(2)}, u32[]{:S(2)}) collective-permute-start(bf16[16,2048]{1,0:T(8,128)(2,1)S(1)} %get-tuple-element.64), channel_id=1, source_target_pairs={{0,4},{4,0},{8,12},{12,8},{16,20},{20,16},{24,28},{28,24},{1,5},{5... | collective-permute-start | bytes 196616 | tf_op jit(solution)/shard_map/ppermute | solution.py:24
  52.1 1.8 %collective-permute-start.28 = (bf16[16,2048]{1,0:T(8,128)(2,1)S(1)}, bf16[16,2048]{1,0:T(8,128)(2,1)S(1)}, u32[]{:S(2)}, u32[]{:S(2)}) collective-permute-start(bf16[16,2048]{1,0:T(8,128)(2,1)S(1)} %get-tuple-element.66), channel_id=1, source_target_pairs={{0,8},{4,12},{8,0},{12,4},{16,24},{20,28},{24,16},{28,20},{1,9},{5... | collective-permute-start | bytes 196616 | tf_op jit(solution)/shard_map/ppermute | solution.py:24
  54.0 1.1 collective-permute-start.29
  55.1 2.1 %collective-permute-start.26 = (bf16[16,2048]{1,0:T(8,128)(2,1)S(1)}, bf16[16,2048]{1,0:T(8,128)(2,1)S(1)}, u32[]{:S(2)}, u32[]{:S(2)}) collective-permute-start(bf16[16,2048]{1,0:T(8,128)(2,1)S(1)} %shard_map.164), channel_id=1, source_target_pairs={{0,24},{4,28},{8,16},{12,20},{16,8},{20,12},{24,0},{28,4},{1,25},{... | collective-permute-start | bytes 196616 | tf_op jit(solution)/shard_map/ppermute | solution.py:24
  57.2 1.3 %collective-permute-start.24 = (bf16[16,2048]{1,0:T(8,128)(2,1)S(1)}, bf16[16,2048]{1,0:T(8,128)(2,1)S(1)}, u32[]{:S(2)}, u32[]{:S(2)}) collective-permute-start(bf16[16,2048]{1,0:T(8,128)(2,1)S(1)} %get-tuple-element.63), channel_id=1, source_target_pairs={{0,16},{4,20},{8,24},{12,28},{16,0},{20,4},{24,8},{28,12},{1,17},{... | collective-permute-start | bytes 196616 | tf_op jit(solution)/shard_map/ppermute | solution.py:24
  58.5 1.7 %collective-permute-start.27 = (bf16[16,2048]{1,0:T(8,128)(2,1)S(1)}, bf16[16,2048]{1,0:T(8,128)(2,1)S(1)}, u32[]{:S(2)}, u32[]{:S(2)}) collective-permute-start(bf16[16,2048]{1,0:T(8,128)(2,1)S(1)} %get-tuple-element.65), channel_id=1, source_target_pairs={{0,4},{4,0},{8,12},{12,8},{16,20},{20,16},{24,28},{28,24},{1,5},{5... | collective-permute-start | bytes 196616 | tf_op jit(solution)/shard_map/ppermute | solution.py:24
  60.2 1.3 %collective-permute-done.26.refs_1_ = bf16[16,2048]{1,0:T(8,128)(2,1)S(1)} collective-permute-done((bf16[16,2048]{1,0:T(8,128)(2,1)S(1)}, bf16[16,2048]{1,0:T(8,128)(2,1)S(1)}, u32[]{:S(2)}, u32[]{:S(2)}) %collective-permute-start.26) | collective-permute-done | bytes 65568 | tf_op jit(solution)/shard_map/ppermute | solution.py:24
  61.5 2.6 %collective-permute-done.24.refs_0_ = bf16[16,2048]{1,0:T(8,128)(2,1)S(1)} collective-permute-done((bf16[16,2048]{1,0:T(8,128)(2,1)S(1)}, bf16[16,2048]{1,0:T(8,128)(2,1)S(1)}, u32[]{:S(2)}, u32[]{:S(2)}) %collective-permute-start.24) | collective-permute-done | bytes 65568 | tf_op jit(solution)/shard_map/ppermute | solution.py:24
  64.1 0.7 shard_map.165
  65.1 1.9 %collective-permute-start.35 = (bf16[16,2048]{1,0:T(8,128)(2,1)S(1)}, bf16[16,2048]{1,0:T(8,128)(2,1)S(1)}, u32[]{:S(2)}, u32[]{:S(2)}) collective-permute-start(bf16[16,2048]{1,0:T(8,128)(2,1)S(1)} %get-tuple-element.69.refs_0_), channel_id=1, source_target_pairs={{0,24},{4,28},{8,16},{12,20},{16,8},{20,12},{24,0},{28,4},{1,25},{... | collective-permute-start | bytes 196616 | tf_op jit(solution)/shard_map/ppermute | solution.py:24
  67.1 1.3 %collective-permute-start.30 = (bf16[16,2048]{1,0:T(8,128)(2,1)S(1)}, bf16[16,2048]{1,0:T(8,128)(2,1)S(1)}, u32[]{:S(2)}, u32[]{:S(2)}) collective-permute-start(bf16[16,2048]{1,0:T(8,128)(2,1)S(1)} %get-tuple-element.69.refs_0_), channel_id=1, source_target_pairs={{0,4},{4,0},{8,12},{12,8},{16,20},{20,16},{24,28},{28,24},{1,5},{5... | collective-permute-start | bytes 196616 | tf_op jit(solution)/shard_map/ppermute | solution.py:24
  68.3 0.6 collective-permute-start.31
  68.9 1.6 %collective-permute-start.32 = (bf16[16,2048]{1,0:T(8,128)(2,1)S(1)}, bf16[16,2048]{1,0:T(8,128)(2,1)S(1)}, u32[]{:S(2)}, u32[]{:S(2)}) collective-permute-start(bf16[16,2048]{1,0:T(8,128)(2,1)S(1)} %get-tuple-element.69.refs_0_), channel_id=1, source_target_pairs={{0,12},{4,8},{8,4},{12,0},{16,28},{20,24},{24,20},{28,16},{1,13},{... | collective-permute-start | bytes 196616 | tf_op jit(solution)/shard_map/ppermute | solution.py:24
  70.6 1.0 collective-permute-done.33.refs_4_
  71.8 1.8 %collective-permute-start.36 = (bf16[16,2048]{1,0:T(8,128)(2,1)S(1)}, bf16[16,2048]{1,0:T(8,128)(2,1)S(1)}, u32[]{:S(2)}, u32[]{:S(2)}) collective-permute-start(bf16[16,2048]{1,0:T(8,128)(2,1)S(1)} %collective-permute-done.35.refs_6_), channel_id=1, source_target_pairs={{0,4},{4,0},{8,12},{12,8},{16,20},{20,16},{24,28},{28,24},{1,5},{5... | collective-permute-start | bytes 196616 | tf_op jit(solution)/shard_map/ppermute | solution.py:24
  74.1 1.8 %collective-permute-done.34.refs_5_ = bf16[16,2048]{1,0:T(8,128)(2,1)S(1)} collective-permute-done((bf16[16,2048]{1,0:T(8,128)(2,1)S(1)}, bf16[16,2048]{1,0:T(8,128)(2,1)S(1)}, u32[]{:S(2)}, u32[]{:S(2)}) %collective-permute-start.34) | collective-permute-done | bytes 65568 | tf_op jit(solution)/shard_map/ppermute | solution.py:24
  75.9 0.7 collective-permute-done.36.refs_7_
  76.6 1.8 %shard_map.166 = (bf16[128,2048]{1,0:T(8,128)(2,1)S(1)}, f32[64,1920]{1,0:T(8,128)S(1)}, bf16[64,1920]{1,0:T(8,128)(2,1)S(1)}) custom-call(s32[2]{0:T(128)S(1)} %pad_add_fusion.3.where_ref, f32[1,2048]{1,0:T(1,128)S(1)} %bitcast.19, bf16[16,2048]{1,0:T(8,128)(2,1)S(1)} %get-tuple-element.69.refs_0_, bf16[16,2048]{1,0:T(8,128)(2,1)S(1)} %collective-permute-done.30.refs_1_, ...), custom_call_target="tpu_custom_call" | custom-call | flops 6308233216 | bytes 8388608 | tf_op jit(solution)/shard_map/pallas_call | solution.py:45
  78.6 1.1 %shard_map.167 = (f32[64,1792]{1,0:T(8,128)S(1)}, bf16[64,1792]{1,0:T(8,128)(2,1)S(1)}) custom-call(bf16[128,2048]{1,0:T(8,128)(2,1)S(1)} %get-tuple-element.72.h_ref, bf16[2048,1792]{1,0:T(8,128)(2,1)S(1)} %bitcast.15), custom_call_target="tpu_custom_call" | custom-call | flops 6308233216 | bytes 7340032 | tf_op jit(solution)/shard_map/pallas_call | solution.py:45
  80.3 1.9 %collective-permute-start.38 = (bf16[32,1920]{1,0:T(8,128)(2,1)S(1)}, bf16[32,1920]{1,0:T(8,128)(2,1)S(1)}, u32[]{:S(2)}, u32[]{:S(2)}) collective-permute-start(bf16[32,1920]{1,0:T(8,128)(2,1)S(1)} %slice.64), channel_id=1, source_target_pairs={{0,2},{1,3},{2,0},{3,1},{4,6},{5,7},{6,4},{7,5},{8,10},{9,11},{10,... | collective-permute-start | bytes 368648 | tf_op jit(solution)/shard_map/ppermute | solution.py:24
  82.3 1.0 collective-permute-start.40
  83.3 3.2 %collective-permute-done.38 = bf16[32,1920]{1,0:T(8,128)(2,1)S(1)} collective-permute-done((bf16[32,1920]{1,0:T(8,128)(2,1)S(1)}, bf16[32,1920]{1,0:T(8,128)(2,1)S(1)}, u32[]{:S(2)}, u32[]{:S(2)}) %collective-permute-start.38) | collective-permute-done | bytes 122912 | tf_op jit(solution)/shard_map/ppermute | solution.py:24
  86.8 1.4 %collective-permute-done.40 = bf16[32,1792]{1,0:T(8,128)(2,1)S(1)} collective-permute-done((bf16[32,1792]{1,0:T(8,128)(2,1)S(1)}, bf16[32,1792]{1,0:T(8,128)(2,1)S(1)}, u32[]{:S(2)}, u32[]{:S(2)}) %collective-permute-start.40) | collective-permute-done | bytes 114720 | tf_op jit(solution)/shard_map/ppermute | solution.py:24
  88.3 1.8 %collective-permute-start.42 = (bf16[32,1792]{1,0:T(8,128)(2,1)S(1)}, bf16[32,1792]{1,0:T(8,128)(2,1)S(1)}, u32[]{:S(2)}, u32[]{:S(2)}) collective-permute-start(bf16[32,1792]{1,0:T(8,128)(2,1)S(1)} %fusion.2.refs_0_), channel_id=1, source_target_pairs={{0,2},{1,3},{2,0},{3,1},{4,6},{5,7},{6,4},{7,5},{8,10},{9,11},{10,... | collective-permute-start | bytes 344072 | tf_op jit(solution)/shard_map/ppermute | solution.py:24
  90.2 3.0 %collective-permute-done.42.refs_2_ = bf16[32,1792]{1,0:T(8,128)(2,1)S(1)} collective-permute-done((bf16[32,1792]{1,0:T(8,128)(2,1)S(1)}, bf16[32,1792]{1,0:T(8,128)(2,1)S(1)}, u32[]{:S(2)}, u32[]{:S(2)}) %collective-permute-start.42) | collective-permute-done | bytes 114720 | tf_op jit(solution)/shard_map/ppermute | solution.py:24
  93.2 1.3 %collective-permute-done.43.refs_3_ = bf16[32,1792]{1,0:T(8,128)(2,1)S(1)} collective-permute-done((bf16[32,1792]{1,0:T(8,128)(2,1)S(1)}, bf16[32,1792]{1,0:T(8,128)(2,1)S(1)}, u32[]{:S(2)}, u32[]{:S(2)}) %collective-permute-start.43) | collective-permute-done | bytes 114720 | tf_op jit(solution)/shard_map/ppermute | solution.py:24
  94.5 1.7 %shard_map.168 = (f32[16,2048]{1,0:T(8,128)S(1)}, bf16[16,2048]{1,0:T(8,128)(2,1)S(1)}, bf16[16,2048]{1,0:T(8,128)(2,1)S(1)}, bf16[16,2048]{1,0:T(8,128)(2,1)S(1...) custom-call(s32[2]{0:T(128)S(1)} %pad_add_fusion.3.where_ref, ...), custom_call_target="tpu_custom_call" | custom-call | flops 6308233216 | bytes 7340032 | tf_op jit(solution)/shard_map/pallas_call | solution.py:45
  96.2 1.4 %collective-permute-start.46 = (bf16[16,2048]{1,0:T(8,128)(2,1)S(1)}, bf16[16,2048]{1,0:T(8,128)(2,1)S(1)}, u32[]{:S(2)}, u32[]{:S(2)}) collective-permute-start(bf16[16,2048]{1,0:T(8,128)(2,1)S(1)} %get-tuple-element.80), channel_id=1, source_target_pairs={{0,4},{4,0},{8,12},{12,8},{16,20},{20,16},{24,28},{28,24},{1,5},{5... | collective-permute-start | bytes 196616 | tf_op jit(solution)/shard_map/ppermute | solution.py:24
  97.6 0.7 collective-permute-start.44
  98.3 0.7 collective-permute-start.49
  99.1 2.1 %collective-permute-start.50 = (bf16[16,2048]{1,0:T(8,128)(2,1)S(1)}, bf16[16,2048]{1,0:T(8,128)(2,1)S(1)}, u32[]{:S(2)}, u32[]{:S(2)}) collective-permute-start(bf16[16,2048]{1,0:T(8,128)(2,1)S(1)} %get-tuple-element.83), channel_id=1, source_target_pairs={{0,12},{4,8},{8,4},{12,0},{16,28},{20,24},{24,20},{28,16},{1,13},{... | collective-permute-start | bytes 196616 | tf_op jit(solution)/shard_map/ppermute | solution.py:24
  101.1 1.9 %collective-permute-start.47 = (bf16[16,2048]{1,0:T(8,128)(2,1)S(1)}, bf16[16,2048]{1,0:T(8,128)(2,1)S(1)}, u32[]{:S(2)}, u32[]{:S(2)}) collective-permute-start(bf16[16,2048]{1,0:T(8,128)(2,1)S(1)} %shard_map.170), channel_id=1, source_target_pairs={{0,24},{4,28},{8,16},{12,20},{16,8},{20,12},{24,0},{28,4},{1,25},{... | collective-permute-start | bytes 196616 | tf_op jit(solution)/shard_map/ppermute | solution.py:24
  103.5 1.1 %collective-permute-start.48 = (bf16[16,2048]{1,0:T(8,128)(2,1)S(1)}, bf16[16,2048]{1,0:T(8,128)(2,1)S(1)}, u32[]{:S(2)}, u32[]{:S(2)}) collective-permute-start(bf16[16,2048]{1,0:T(8,128)(2,1)S(1)} %get-tuple-element.81), channel_id=1, source_target_pairs={{0,4},{4,0},{8,12},{12,8},{16,20},{20,16},{24,28},{28,24},{1,5},{5... | collective-permute-start | bytes 196616 | tf_op jit(solution)/shard_map/ppermute | solution.py:24
  104.6 2.8 %collective-permute-done.47.refs_1_ = bf16[16,2048]{1,0:T(8,128)(2,1)S(1)} collective-permute-done((bf16[16,2048]{1,0:T(8,128)(2,1)S(1)}, bf16[16,2048]{1,0:T(8,128)(2,1)S(1)}, u32[]{:S(2)}, u32[]{:S(2)}) %collective-permute-start.47) | collective-permute-done | bytes 65568 | tf_op jit(solution)/shard_map/ppermute | solution.py:24
  107.4 2.3 %collective-permute-done.45.refs_0_ = bf16[16,2048]{1,0:T(8,128)(2,1)S(1)} collective-permute-done((bf16[16,2048]{1,0:T(8,128)(2,1)S(1)}, bf16[16,2048]{1,0:T(8,128)(2,1)S(1)}, u32[]{:S(2)}, u32[]{:S(2)}) %collective-permute-start.45) | collective-permute-done | bytes 65568 | tf_op jit(solution)/shard_map/ppermute | solution.py:24
  109.7 0.7 shard_map.171
  (116 shorter events, 7.3 us)
Async XLA Ops:
  0.6 7.0 %copy-start.3 = (bf16[8,8,1024]{2,1,0:T(8,128)(2,1)S(1)}, bf16[8,8,1024]{2,1,0:T(8,128)(2,1)}, u32[]{:S(2)}) copy-start(bf16[8,8,1024]{2,1,0:T(8,128)(2,1)} %keys_ref.3) | copy-start | bytes 393220
  0.6 7.0 %copy-start.4 = (bf16[8,8,1024]{2,1,0:T(8,128)(2,1)S(1)}, bf16[8,8,1024]{2,1,0:T(8,128)(2,1)}, u32[]{:S(2)}) copy-start(bf16[8,8,1024]{2,1,0:T(8,128)(2,1)} %values_ref.3) | copy-start | bytes 393220
  2.2 9.9 %collective-permute-start.3 = (bf16[16,2048]{1,0:T(8,128)(2,1)S(1)}, bf16[16,2048]{1,0:T(8,128)(2,1)S(1)}, u32[]{:S(2)}, u32[]{:S(2)}) collective-permute-start(bf16[16,2048]{1,0:T(8,128)(2,1)S(1)} %shard_map.149.x_ref.refs_0_.refs_10_.after_ref.refs_5_), channel_id=1, source_target_pairs={{0,16},{4,20},{8,24},{12,28},{16,0},{20,4},{24,8},{28,12},{1,17},{... | collective-permute-start | bytes 196616 | tf_op jit(solution)/shard_map/ppermute | solution.py:24
  6.3 6.2 %collective-permute-start.5 = (bf16[16,2048]{1,0:T(8,128)(2,1)S(1)}, bf16[16,2048]{1,0:T(8,128)(2,1)S(1)}, u32[]{:S(2)}, u32[]{:S(2)}) collective-permute-start(bf16[16,2048]{1,0:T(8,128)(2,1)S(1)} %shard_map.149.x_ref.refs_0_.refs_10_.after_ref.refs_5_), channel_id=1, source_target_pairs={{0,24},{4,28},{8,16},{12,20},{16,8},{20,12},{24,0},{28,4},{1,25},{... | collective-permute-start | bytes 196616 | tf_op jit(solution)/shard_map/ppermute | solution.py:24
  7.7 4.2 %copy-start.10 = (s32[64]{0:T(128)S(1)}, s32[64]{0:T(128)}, u32[]{:S(2)}) copy-start(s32[64]{0:T(128)} %param.18) | copy-start | bytes 772
  8.3 8.0 %collective-permute-start = (bf16[24,2048]{1,0:T(8,128)(2,1)S(1)}, bf16[24,2048]{1,0:T(8,128)(2,1)S(1)}, u32[]{:S(2)}, u32[]{:S(2)}) collective-permute-start(bf16[24,2048]{1,0:T(8,128)(2,1)S(1)} %get-tuple-element.43), channel_id=1, source_target_pairs={{0,4},{4,0},{8,12},{12,8},{16,20},{20,16},{24,28},{28,24},{1,5},{5... | collective-permute-start | bytes 294920 | tf_op jit(solution)/shard_map/ppermute | solution.py:24
  9.8 8.1 %collective-permute-start.1 = (bf16[24,2048]{1,0:T(8,128)(2,1)S(1)}, bf16[24,2048]{1,0:T(8,128)(2,1)S(1)}, u32[]{:S(2)}, u32[]{:S(2)}) collective-permute-start(bf16[24,2048]{1,0:T(8,128)(2,1)S(1)} %get-tuple-element.44), channel_id=1, source_target_pairs={{0,8},{4,12},{8,0},{12,4},{16,24},{20,28},{24,16},{28,20},{1,9},{5... | collective-permute-start | bytes 294920 | tf_op jit(solution)/shard_map/ppermute | solution.py:24
  10.1 8.3 %collective-permute-start.2 = (bf16[24,2048]{1,0:T(8,128)(2,1)S(1)}, bf16[24,2048]{1,0:T(8,128)(2,1)S(1)}, u32[]{:S(2)}, u32[]{:S(2)}) collective-permute-start(bf16[24,2048]{1,0:T(8,128)(2,1)S(1)} %get-tuple-element.45), channel_id=1, source_target_pairs={{0,12},{4,8},{8,4},{12,0},{16,28},{20,24},{24,20},{28,16},{1,13},{... | collective-permute-start | bytes 294920 | tf_op jit(solution)/shard_map/ppermute | solution.py:24
  13.1 7.1 %collective-permute-start.15 = (bf16[2,8,2048]{2,1,0:T(8,128)(2,1)S(1)}, bf16[2,8,2048]{2,1,0:T(8,128)(2,1)S(1)}, u32[]{:S(2)}, u32[]{:S(2)}) collective-permute-start(bf16[2,8,2048]{2,1,0:T(8,128)(2,1)S(1)} %get-tuple-element.53), channel_id=1, source_target_pairs={{0,16},{4,20},{8,24},{12,28},{16,0},{20,4},{24,8},{28,12},{1,17},{... | collective-permute-start | bytes 196616 | tf_op jit(solution)/shard_map/ppermute | solution.py:24
  15.9 6.2 %collective-permute-start.16 = (bf16[2,8,2048]{2,1,0:T(8,128)(2,1)S(1)}, bf16[2,8,2048]{2,1,0:T(8,128)(2,1)S(1)}, u32[]{:S(2)}, u32[]{:S(2)}) collective-permute-start(bf16[2,8,2048]{2,1,0:T(8,128)(2,1)S(1)} %get-tuple-element.54), channel_id=1, source_target_pairs={{0,24},{4,28},{8,16},{12,20},{16,8},{20,12},{24,0},{28,4},{1,25},{... | collective-permute-start | bytes 196616 | tf_op jit(solution)/shard_map/ppermute | solution.py:24
  16.3 7.3 %collective-permute-start.4 = (bf16[16,2048]{1,0:T(8,128)(2,1)S(1)}, bf16[16,2048]{1,0:T(8,128)(2,1)S(1)}, u32[]{:S(2)}, u32[]{:S(2)}) collective-permute-start(bf16[16,2048]{1,0:T(8,128)(2,1)S(1)} %collective-permute-done.3.refs_4_.refs_0_), channel_id=1, source_target_pairs={{0,4},{4,0},{8,12},{12,8},{16,20},{20,16},{24,28},{28,24},{1,5},{5... | collective-permute-start | bytes 196616 | tf_op jit(solution)/shard_map/ppermute | solution.py:24
  17.9 5.7 %collective-permute-start.6 = (bf16[16,2048]{1,0:T(8,128)(2,1)S(1)}, bf16[16,2048]{1,0:T(8,128)(2,1)S(1)}, u32[]{:S(2)}, u32[]{:S(2)}) collective-permute-start(bf16[16,2048]{1,0:T(8,128)(2,1)S(1)} %collective-permute-done.5.refs_6_.refs_1_), channel_id=1, source_target_pairs={{0,4},{4,0},{8,12},{12,8},{16,20},{20,16},{24,28},{28,24},{1,5},{5... | collective-permute-start | bytes 196616 | tf_op jit(solution)/shard_map/ppermute | solution.py:24
  18.3 5.2 %copy-start = (bf16[2048,1024]{1,0:T(8,128)(2,1)S(1)}, bf16[2048,1024]{1,0:T(8,128)(2,1)}, u32[]{:S(2)}) copy-start(bf16[2048,1024]{1,0:T(8,128)(2,1)} %refs_9_.1) | copy-start | bytes 12582916
  18.4 5.2 %copy-start.2 = (bf16[2048,256]{1,0:T(8,128)(2,1)S(1)}, bf16[2048,256]{1,0:T(8,128)(2,1)}, u32[]{:S(2)}) copy-start(bf16[2048,256]{1,0:T(8,128)(2,1)} %refs_8_.2) | copy-start | bytes 3145732
  18.4 5.2 %copy-start.7 = (f32[2048]{0:T(1024)S(1)}, f32[2048]{0:T(1024)}, u32[]{:S(2)}) copy-start(f32[2048]{0:T(1024)} %param.19) | copy-start | bytes 24580
  18.4 17.2 %collective-permute-start.13 = (bf16[4,8,2048]{2,1,0:T(8,128)(2,1)S(1)}, bf16[4,8,2048]{2,1,0:T(8,128)(2,1)S(1)}, u32[]{:S(2)}, u32[]{:S(2)}) collective-permute-start(bf16[4,8,2048]{2,1,0:T(8,128)(2,1)S(1)} %shard_map.154.refs_0_.refs_2_), channel_id=1, source_target_pairs={{0,2},{1,3},{2,0},{3,1},{4,6},{5,7},{6,4},{7,5},{8,10},{9,11},{10,... | collective-permute-start | bytes 393224 | tf_op jit(solution)/shard_map/ppermute | solution.py:24
  22.0 4.3 %collective-permute-start.17 = (bf16[2,8,2048]{2,1,0:T(8,128)(2,1)S(1)}, bf16[2,8,2048]{2,1,0:T(8,128)(2,1)S(1)}, u32[]{:S(2)}, u32[]{:S(2)}) collective-permute-start(bf16[2,8,2048]{2,1,0:T(8,128)(2,1)S(1)} %shard_map.157), channel_id=1, source_target_pairs={{0,4},{4,0},{8,12},{12,8},{16,20},{20,16},{24,28},{28,24},{1,5},{5... | collective-permute-start | bytes 196616 | tf_op jit(solution)/shard_map/ppermute | solution.py:24
  25.1 2.8 %collective-permute-start.7 = (bf16[128,896]{1,0:T(8,128)(2,1)S(1)}, bf16[128,896]{1,0:T(8,128)(2,1)S(1)}, u32[]{:S(2)}, u32[]{:S(2)}) collective-permute-start(bf16[128,896]{1,0:T(8,128)(2,1)S(1)} %get-tuple-element.46.own_ref), channel_id=1, source_target_pairs={{0,1},{1,0},{2,3},{3,2},{4,5},{5,4},{6,7},{7,6},{8,9},{9,8},{10,11... | collective-permute-start | bytes 688136 | tf_op jit(solution)/shard_map/ppermute | solution.py:24
  26.3 6.0 %collective-permute-start.18 = (bf16[4,8,2048]{2,1,0:T(8,128)(2,1)S(1)}, bf16[4,8,2048]{2,1,0:T(8,128)(2,1)S(1)}, u32[]{:S(2)}, u32[]{:S(2)}) collective-permute-start(bf16[4,8,2048]{2,1,0:T(8,128)(2,1)S(1)} %shard_map.158.refs_0_.refs_5_), channel_id=1, source_target_pairs={{0,2},{1,3},{2,0},{3,1},{4,6},{5,7},{6,4},{7,5},{8,10},{9,11},{10,... | collective-permute-start | bytes 393224 | tf_op jit(solution)/shard_map/ppermute | solution.py:24
  28.6 6.9 %collective-permute-start.8 = (bf16[128,384]{1,0:T(8,128)(2,1)S(1)}, bf16[128,384]{1,0:T(8,128)(2,1)S(1)}, u32[]{:S(2)}, u32[]{:S(2)}) collective-permute-start(bf16[128,384]{1,0:T(8,128)(2,1)S(1)} %get-tuple-element.48.own_ref), channel_id=1, source_target_pairs={{0,2},{1,3},{2,0},{3,1},{4,6},{5,7},{6,4},{7,5},{8,10},{9,11},{10,... | collective-permute-start | bytes 294920 | tf_op jit(solution)/shard_map/ppermute | solution.py:24
  29.3 12.6 %collective-permute-start.11 = (bf16[128,128]{1,0:T(8,128)(2,1)S(1)}, bf16[128,128]{1,0:T(8,128)(2,1)S(1)}, u32[]{:S(2)}, u32[]{:S(2)}) collective-permute-start(bf16[128,128]{1,0:T(8,128)(2,1)S(1)} %get-tuple-element.50), channel_id=1, source_target_pairs={{0,0},{1,1},{2,2},{3,3},{4,8},{5,9},{6,10},{7,11},{8,16},{9,17},{1... | collective-permute-start | bytes 98312 | tf_op jit(solution)/shard_map/ppermute | solution.py:653
  30.0 12.0 %collective-permute-start.12 = (bf16[128,128]{1,0:T(8,128)(2,1)S(1)}, bf16[128,128]{1,0:T(8,128)(2,1)S(1)}, u32[]{:S(2)}, u32[]{:S(2)}) collective-permute-start(bf16[128,128]{1,0:T(8,128)(2,1)S(1)} %get-tuple-element.50), channel_id=1, source_target_pairs={{0,2},{1,3},{2,0},{3,1},{4,10},{5,11},{6,8},{7,9},{8,18},{9,19},{1... | collective-permute-start | bytes 98312 | tf_op jit(solution)/shard_map/ppermute | solution.py:653
  32.4 9.6 %collective-permute-start.10 = (bf16[128,128]{1,0:T(8,128)(2,1)S(1)}, bf16[128,128]{1,0:T(8,128)(2,1)S(1)}, u32[]{:S(2)}, u32[]{:S(2)}) collective-permute-start(bf16[128,128]{1,0:T(8,128)(2,1)S(1)} %get-tuple-element.49), channel_id=1, source_target_pairs={{0,6},{1,7},{2,4},{3,5},{4,14},{5,15},{6,12},{7,13},{8,22},{9,23},... | collective-permute-start | bytes 98312 | tf_op jit(solution)/shard_map/ppermute | solution.py:653
  35.5 1.6 %collective-permute-start.19 = (bf16[2,4,8,2048]{3,2,1,0:T(8,128)(2,1)S(1)}, bf16[2,4,8,2048]{3,2,1,0:T(8,128)(2,1)S(1)}, u32[]{:S(2)}, u32[]{:S(2)}) collective-permute-start(bf16[2,4,8,2048]{3,2,1,0:T(8,128)(2,1)S(1)} %shard_map.159), channel_id=1, source_target_pairs={{0,1},{1,0},{2,3},{3,2},{4,5},{5,4},{6,7},{7,6},{8,9},{9,8},{10,11... | collective-permute-start | bytes 786440 | tf_op jit(solution)/shard_map/ppermute | solution.py:24
  35.6 3.9 %collective-permute-start.14 = (bf16[2,4,8,2048]{3,2,1,0:T(8,128)(2,1)S(1)}, bf16[2,4,8,2048]{3,2,1,0:T(8,128)(2,1)S(1)}, u32[]{:S(2)}, u32[]{:S(2)}) collective-permute-start(bf16[2,4,8,2048]{3,2,1,0:T(8,128)(2,1)S(1)} %shard_map.155), channel_id=1, source_target_pairs={{0,1},{1,0},{2,3},{3,2},{4,5},{5,4},{6,7},{7,6},{8,9},{9,8},{10,11... | collective-permute-start | bytes 786440 | tf_op jit(solution)/shard_map/ppermute | solution.py:24
  37.1 4.9 %collective-permute-start.9 = (bf16[128,128]{1,0:T(8,128)(2,1)S(1)}, bf16[128,128]{1,0:T(8,128)(2,1)S(1)}, u32[]{:S(2)}, u32[]{:S(2)}) collective-permute-start(bf16[128,128]{1,0:T(8,128)(2,1)S(1)} %get-tuple-element.49), channel_id=1, source_target_pairs={{0,4},{1,5},{2,6},{3,7},{4,12},{5,13},{6,14},{7,15},{8,20},{9,21},... | collective-permute-start | bytes 98312 | tf_op jit(solution)/shard_map/ppermute | solution.py:653
  42.0 6.7 %copy-start.1 = (bf16[1024,2048]{1,0:T(8,128)(2,1)S(1)}, bf16[1024,2048]{1,0:T(8,128)(2,1)}, u32[]{:S(2)}) copy-start(bf16[1024,2048]{1,0:T(8,128)(2,1)} %refs_4_.2) | copy-start | bytes 12582916
  43.2 4.3 %collective-permute-start.21 = (bf16[32,1024]{1,0:T(8,128)(2,1)S(1)}, bf16[32,1024]{1,0:T(8,128)(2,1)S(1)}, u32[]{:S(2)}, u32[]{:S(2)}) collective-permute-start(bf16[32,1024]{1,0:T(8,128)(2,1)S(1)} %shard_map.161.refs_0_), channel_id=1, source_target_pairs={{0,2},{1,3},{2,0},{3,1},{4,6},{5,7},{6,4},{7,5},{8,10},{9,11},{10,... | collective-permute-start | bytes 196616 | tf_op jit(solution)/shard_map/ppermute | solution.py:24
  44.7 2.8 %collective-permute-start.20 = (bf16[32,1024]{1,0:T(8,128)(2,1)S(1)}, bf16[32,1024]{1,0:T(8,128)(2,1)S(1)}, u32[]{:S(2)}, u32[]{:S(2)}) collective-permute-start(bf16[32,1024]{1,0:T(8,128)(2,1)S(1)} %shard_map.161.refs_0_), channel_id=1, source_target_pairs={{0,1},{1,0},{2,3},{3,2},{4,5},{5,4},{6,7},{7,6},{8,9},{9,8},{10,11... | collective-permute-start | bytes 196616 | tf_op jit(solution)/shard_map/ppermute | solution.py:24
  47.5 1.3 %collective-permute-start.22 = (bf16[32,1024]{1,0:T(8,128)(2,1)S(1)}, bf16[32,1024]{1,0:T(8,128)(2,1)S(1)}, u32[]{:S(2)}, u32[]{:S(2)}) collective-permute-start(bf16[32,1024]{1,0:T(8,128)(2,1)S(1)} %collective-permute-done.21.refs_2_), channel_id=1, source_target_pairs={{0,1},{1,0},{2,3},{3,2},{4,5},{5,4},{6,7},{7,6},{8,9},{9,8},{10,11... | collective-permute-start | bytes 196616 | tf_op jit(solution)/shard_map/ppermute | solution.py:24
  50.0 5.0 %collective-permute-start.25 = (bf16[16,2048]{1,0:T(8,128)(2,1)S(1)}, bf16[16,2048]{1,0:T(8,128)(2,1)S(1)}, u32[]{:S(2)}, u32[]{:S(2)}) collective-permute-start(bf16[16,2048]{1,0:T(8,128)(2,1)S(1)} %get-tuple-element.64), channel_id=1, source_target_pairs={{0,4},{4,0},{8,12},{12,8},{16,20},{20,16},{24,28},{28,24},{1,5},{5... | collective-permute-start | bytes 196616 | tf_op jit(solution)/shard_map/ppermute | solution.py:24
  51.6 5.6 %collective-permute-start.23 = (bf16[16,2048]{1,0:T(8,128)(2,1)S(1)}, bf16[16,2048]{1,0:T(8,128)(2,1)S(1)}, u32[]{:S(2)}, u32[]{:S(2)}) collective-permute-start(bf16[16,2048]{1,0:T(8,128)(2,1)S(1)} %get-tuple-element.61), channel_id=1, source_target_pairs={{0,4},{4,0},{8,12},{12,8},{16,20},{20,16},{24,28},{28,24},{1,5},{5... | collective-permute-start | bytes 196616 | tf_op jit(solution)/shard_map/ppermute | solution.py:24
  52.1 8.1 %collective-permute-start.28 = (bf16[16,2048]{1,0:T(8,128)(2,1)S(1)}, bf16[16,2048]{1,0:T(8,128)(2,1)S(1)}, u32[]{:S(2)}, u32[]{:S(2)}) collective-permute-start(bf16[16,2048]{1,0:T(8,128)(2,1)S(1)} %get-tuple-element.66), channel_id=1, source_target_pairs={{0,8},{4,12},{8,0},{12,4},{16,24},{20,28},{24,16},{28,20},{1,9},{5... | collective-permute-start | bytes 196616 | tf_op jit(solution)/shard_map/ppermute | solution.py:24
  54.0 6.3 %collective-permute-start.29 = (bf16[16,2048]{1,0:T(8,128)(2,1)S(1)}, bf16[16,2048]{1,0:T(8,128)(2,1)S(1)}, u32[]{:S(2)}, u32[]{:S(2)}) collective-permute-start(bf16[16,2048]{1,0:T(8,128)(2,1)S(1)} %get-tuple-element.67), channel_id=1, source_target_pairs={{0,12},{4,8},{8,4},{12,0},{16,28},{20,24},{24,20},{28,16},{1,13},{... | collective-permute-start | bytes 196616 | tf_op jit(solution)/shard_map/ppermute | solution.py:24
  55.1 6.4 %collective-permute-start.26 = (bf16[16,2048]{1,0:T(8,128)(2,1)S(1)}, bf16[16,2048]{1,0:T(8,128)(2,1)S(1)}, u32[]{:S(2)}, u32[]{:S(2)}) collective-permute-start(bf16[16,2048]{1,0:T(8,128)(2,1)S(1)} %shard_map.164), channel_id=1, source_target_pairs={{0,24},{4,28},{8,16},{12,20},{16,8},{20,12},{24,0},{28,4},{1,25},{... | collective-permute-start | bytes 196616 | tf_op jit(solution)/shard_map/ppermute | solution.py:24
  57.2 19.4 %slice-start = ((s8[7340032]{0:T(1024)(128)(4,1)}), s8[4194304]{0:T(1024)(128)(4,1)S(1)}, s32[]{:S(2)}) async-start(s8[7340032]{0:T(1024)(128)(4,1)} %bitcast.12), calls=%async_computation | async-start | bytes 8388608
  57.2 6.9 %collective-permute-start.24 = (bf16[16,2048]{1,0:T(8,128)(2,1)S(1)}, bf16[16,2048]{1,0:T(8,128)(2,1)S(1)}, u32[]{:S(2)}, u32[]{:S(2)}) collective-permute-start(bf16[16,2048]{1,0:T(8,128)(2,1)S(1)} %get-tuple-element.63), channel_id=1, source_target_pairs={{0,16},{4,20},{8,24},{12,28},{16,0},{20,4},{24,8},{28,12},{1,17},{... | collective-permute-start | bytes 196616 | tf_op jit(solution)/shard_map/ppermute | solution.py:24
  58.5 18.1 %slice-start.1 = ((s8[7340032]{0:T(1024)(128)(4,1)}), s8[3145728]{0:T(1024)(128)(4,1)S(1)}, s32[]{:S(2)}) async-start(s8[7340032]{0:T(1024)(128)(4,1)} %bitcast.12), calls=%async_computation.1 | async-start | bytes 6291456
  58.5 5.6 %collective-permute-start.27 = (bf16[16,2048]{1,0:T(8,128)(2,1)S(1)}, bf16[16,2048]{1,0:T(8,128)(2,1)S(1)}, u32[]{:S(2)}, u32[]{:S(2)}) collective-permute-start(bf16[16,2048]{1,0:T(8,128)(2,1)S(1)} %get-tuple-element.65), channel_id=1, source_target_pairs={{0,4},{4,0},{8,12},{12,8},{16,20},{20,16},{24,28},{28,24},{1,5},{5... | collective-permute-start | bytes 196616 | tf_op jit(solution)/shard_map/ppermute | solution.py:24
  64.1 12.4 %copy-start.8 = (f32[2048]{0:T(1024)S(1)}, f32[2048]{0:T(1024)}, u32[]{:S(2)}) copy-start(f32[2048]{0:T(1024)} %param.20) | copy-start | bytes 24580
  64.1 14.4 %slice-start.2 = ((s8[7340032]{0:T(1024)(128)(4,1)}), s8[4194304]{0:T(1024)(128)(4,1)S(1)}, s32[]{:S(2)}) async-start(s8[7340032]{0:T(1024)(128)(4,1)} %bitcast.14), calls=%async_computation.2 | async-start | bytes 8388608
  64.8 6.8 %collective-permute-start.33 = (bf16[16,2048]{1,0:T(8,128)(2,1)S(1)}, bf16[16,2048]{1,0:T(8,128)(2,1)S(1)}, u32[]{:S(2)}, u32[]{:S(2)}) collective-permute-start(bf16[16,2048]{1,0:T(8,128)(2,1)S(1)} %get-tuple-element.69.refs_0_), channel_id=1, source_target_pairs={{0,16},{4,20},{8,24},{12,28},{16,0},{20,4},{24,8},{28,12},{1,17},{... | collective-permute-start | bytes 196616 | tf_op jit(solution)/shard_map/ppermute | solution.py:24
  65.1 6.7 %collective-permute-start.35 = (bf16[16,2048]{1,0:T(8,128)(2,1)S(1)}, bf16[16,2048]{1,0:T(8,128)(2,1)S(1)}, u32[]{:S(2)}, u32[]{:S(2)}) collective-permute-start(bf16[16,2048]{1,0:T(8,128)(2,1)S(1)} %get-tuple-element.69.refs_0_), channel_id=1, source_target_pairs={{0,24},{4,28},{8,16},{12,20},{16,8},{20,12},{24,0},{28,4},{1,25},{... | collective-permute-start | bytes 196616 | tf_op jit(solution)/shard_map/ppermute | solution.py:24
  67.1 6.6 %collective-permute-start.30 = (bf16[16,2048]{1,0:T(8,128)(2,1)S(1)}, bf16[16,2048]{1,0:T(8,128)(2,1)S(1)}, u32[]{:S(2)}, u32[]{:S(2)}) collective-permute-start(bf16[16,2048]{1,0:T(8,128)(2,1)S(1)} %get-tuple-element.69.refs_0_), channel_id=1, source_target_pairs={{0,4},{4,0},{8,12},{12,8},{16,20},{20,16},{24,28},{28,24},{1,5},{5... | collective-permute-start | bytes 196616 | tf_op jit(solution)/shard_map/ppermute | solution.py:24
  68.3 5.3 %collective-permute-start.31 = (bf16[16,2048]{1,0:T(8,128)(2,1)S(1)}, bf16[16,2048]{1,0:T(8,128)(2,1)S(1)}, u32[]{:S(2)}, u32[]{:S(2)}) collective-permute-start(bf16[16,2048]{1,0:T(8,128)(2,1)S(1)} %get-tuple-element.69.refs_0_), channel_id=1, source_target_pairs={{0,8},{4,12},{8,0},{12,4},{16,24},{20,28},{24,16},{28,20},{1,9},{5... | collective-permute-start | bytes 196616 | tf_op jit(solution)/shard_map/ppermute | solution.py:24
  68.9 5.2 %collective-permute-start.32 = (bf16[16,2048]{1,0:T(8,128)(2,1)S(1)}, bf16[16,2048]{1,0:T(8,128)(2,1)S(1)}, u32[]{:S(2)}, u32[]{:S(2)}) collective-permute-start(bf16[16,2048]{1,0:T(8,128)(2,1)S(1)} %get-tuple-element.69.refs_0_), channel_id=1, source_target_pairs={{0,12},{4,8},{8,4},{12,0},{16,28},{20,24},{24,20},{28,16},{1,13},{... | collective-permute-start | bytes 196616 | tf_op jit(solution)/shard_map/ppermute | solution.py:24
  71.6 4.3 %collective-permute-start.34 = (bf16[16,2048]{1,0:T(8,128)(2,1)S(1)}, bf16[16,2048]{1,0:T(8,128)(2,1)S(1)}, u32[]{:S(2)}, u32[]{:S(2)}) collective-permute-start(bf16[16,2048]{1,0:T(8,128)(2,1)S(1)} %collective-permute-done.33.refs_4_), channel_id=1, source_target_pairs={{0,4},{4,0},{8,12},{12,8},{16,20},{20,16},{24,28},{28,24},{1,5},{5... | collective-permute-start | bytes 196616 | tf_op jit(solution)/shard_map/ppermute | solution.py:24
  71.8 4.8 %collective-permute-start.36 = (bf16[16,2048]{1,0:T(8,128)(2,1)S(1)}, bf16[16,2048]{1,0:T(8,128)(2,1)S(1)}, u32[]{:S(2)}, u32[]{:S(2)}) collective-permute-start(bf16[16,2048]{1,0:T(8,128)(2,1)S(1)} %collective-permute-done.35.refs_6_), channel_id=1, source_target_pairs={{0,4},{4,0},{8,12},{12,8},{16,20},{20,16},{24,28},{28,24},{1,5},{5... | collective-permute-start | bytes 196616 | tf_op jit(solution)/shard_map/ppermute | solution.py:24
  76.6 17.9 %slice-start.4 = ((s8[7340032]{0:T(1024)(128)(4,1)}), s8[4194304]{0:T(1024)(128)(4,1)S(1)}, s32[]{:S(2)}) async-start(s8[7340032]{0:T(1024)(128)(4,1)} %bitcast.16), calls=%async_computation.4 | async-start | bytes 8388608
  78.4 1.8 %collective-permute-start.37 = (bf16[64,1920]{1,0:T(8,128)(2,1)S(1)}, bf16[64,1920]{1,0:T(8,128)(2,1)S(1)}, u32[]{:S(2)}, u32[]{:S(2)}) collective-permute-start(bf16[64,1920]{1,0:T(8,128)(2,1)S(1)} %get-tuple-element.71), channel_id=1, source_target_pairs={{0,1},{1,0},{2,3},{3,2},{4,5},{5,4},{6,7},{7,6},{8,9},{9,8},{10,11... | collective-permute-start | bytes 737288 | tf_op jit(solution)/shard_map/ppermute | solution.py:24
  78.5 16.0 %slice-start.5 = ((s8[7340032]{0:T(1024)(128)(4,1)}), s8[3145728]{0:T(1024)(128)(4,1)S(1)}, s32[]{:S(2)}) async-start(s8[7340032]{0:T(1024)(128)(4,1)} %bitcast.16), calls=%async_computation.5 | async-start | bytes 6291456
  79.7 2.5 %collective-permute-start.39 = (bf16[64,1792]{1,0:T(8,128)(2,1)S(1)}, bf16[64,1792]{1,0:T(8,128)(2,1)S(1)}, u32[]{:S(2)}, u32[]{:S(2)}) collective-permute-start(bf16[64,1792]{1,0:T(8,128)(2,1)S(1)} %get-tuple-element.74), channel_id=1, source_target_pairs={{0,1},{1,0},{2,3},{3,2},{4,5},{5,4},{6,7},{7,6},{8,9},{9,8},{10,11... | collective-permute-start | bytes 688136 | tf_op jit(solution)/shard_map/ppermute | solution.py:24
  80.3 6.2 %collective-permute-start.38 = (bf16[32,1920]{1,0:T(8,128)(2,1)S(1)}, bf16[32,1920]{1,0:T(8,128)(2,1)S(1)}, u32[]{:S(2)}, u32[]{:S(2)}) collective-permute-start(bf16[32,1920]{1,0:T(8,128)(2,1)S(1)} %slice.64), channel_id=1, source_target_pairs={{0,2},{1,3},{2,0},{3,1},{4,6},{5,7},{6,4},{7,5},{8,10},{9,11},{10,... | collective-permute-start | bytes 368648 | tf_op jit(solution)/shard_map/ppermute | solution.py:24
  82.3 5.9 %collective-permute-start.40 = (bf16[32,1792]{1,0:T(8,128)(2,1)S(1)}, bf16[32,1792]{1,0:T(8,128)(2,1)S(1)}, u32[]{:S(2)}, u32[]{:S(2)}) collective-permute-start(bf16[32,1792]{1,0:T(8,128)(2,1)S(1)} %slice.65), channel_id=1, source_target_pairs={{0,2},{1,3},{2,0},{3,1},{4,6},{5,7},{6,4},{7,5},{8,10},{9,11},{10,... | collective-permute-start | bytes 344072 | tf_op jit(solution)/shard_map/ppermute | solution.py:24
  88.3 4.9 %collective-permute-start.42 = (bf16[32,1792]{1,0:T(8,128)(2,1)S(1)}, bf16[32,1792]{1,0:T(8,128)(2,1)S(1)}, u32[]{:S(2)}, u32[]{:S(2)}) collective-permute-start(bf16[32,1792]{1,0:T(8,128)(2,1)S(1)} %fusion.2.refs_0_), channel_id=1, source_target_pairs={{0,2},{1,3},{2,0},{3,1},{4,6},{5,7},{6,4},{7,5},{8,10},{9,11},{10,... | collective-permute-start | bytes 344072 | tf_op jit(solution)/shard_map/ppermute | solution.py:24
  90.2 3.1 %collective-permute-start.41 = (bf16[32,1792]{1,0:T(8,128)(2,1)S(1)}, bf16[32,1792]{1,0:T(8,128)(2,1)S(1)}, u32[]{:S(2)}, u32[]{:S(2)}) collective-permute-start(bf16[32,1792]{1,0:T(8,128)(2,1)S(1)} %fusion.2.refs_0_), channel_id=1, source_target_pairs={{0,1},{1,0},{2,3},{3,2},{4,5},{5,4},{6,7},{7,6},{8,9},{9,8},{10,11... | collective-permute-start | bytes 344072 | tf_op jit(solution)/shard_map/ppermute | solution.py:24
  93.2 1.3 %collective-permute-start.43 = (bf16[32,1792]{1,0:T(8,128)(2,1)S(1)}, bf16[32,1792]{1,0:T(8,128)(2,1)S(1)}, u32[]{:S(2)}, u32[]{:S(2)}) collective-permute-start(bf16[32,1792]{1,0:T(8,128)(2,1)S(1)} %collective-permute-done.42.refs_2_), channel_id=1, source_target_pairs={{0,1},{1,0},{2,3},{3,2},{4,5},{5,4},{6,7},{7,6},{8,9},{9,8},{10,11... | collective-permute-start | bytes 344072 | tf_op jit(solution)/shard_map/ppermute | solution.py:24
  96.2 4.9 %collective-permute-start.46 = (bf16[16,2048]{1,0:T(8,128)(2,1)S(1)}, bf16[16,2048]{1,0:T(8,128)(2,1)S(1)}, u32[]{:S(2)}, u32[]{:S(2)}) collective-permute-start(bf16[16,2048]{1,0:T(8,128)(2,1)S(1)} %get-tuple-element.80), channel_id=1, source_target_pairs={{0,4},{4,0},{8,12},{12,8},{16,20},{20,16},{24,28},{28,24},{1,5},{5... | collective-permute-start | bytes 196616 | tf_op jit(solution)/shard_map/ppermute | solution.py:24
  97.6 5.5 %collective-permute-start.44 = (bf16[16,2048]{1,0:T(8,128)(2,1)S(1)}, bf16[16,2048]{1,0:T(8,128)(2,1)S(1)}, u32[]{:S(2)}, u32[]{:S(2)}) collective-permute-start(bf16[16,2048]{1,0:T(8,128)(2,1)S(1)} %get-tuple-element.77), channel_id=1, source_target_pairs={{0,4},{4,0},{8,12},{12,8},{16,20},{20,16},{24,28},{28,24},{1,5},{5... | collective-permute-start | bytes 196616 | tf_op jit(solution)/shard_map/ppermute | solution.py:24
  98.3 6.3 %collective-permute-start.49 = (bf16[16,2048]{1,0:T(8,128)(2,1)S(1)}, bf16[16,2048]{1,0:T(8,128)(2,1)S(1)}, u32[]{:S(2)}, u32[]{:S(2)}) collective-permute-start(bf16[16,2048]{1,0:T(8,128)(2,1)S(1)} %get-tuple-element.82), channel_id=1, source_target_pairs={{0,8},{4,12},{8,0},{12,4},{16,24},{20,28},{24,16},{28,20},{1,9},{5... | collective-permute-start | bytes 196616 | tf_op jit(solution)/shard_map/ppermute | solution.py:24
  99.1 5.6 %collective-permute-start.50 = (bf16[16,2048]{1,0:T(8,128)(2,1)S(1)}, bf16[16,2048]{1,0:T(8,128)(2,1)S(1)}, u32[]{:S(2)}, u32[]{:S(2)}) collective-permute-start(bf16[16,2048]{1,0:T(8,128)(2,1)S(1)} %get-tuple-element.83), channel_id=1, source_target_pairs={{0,12},{4,8},{8,4},{12,0},{16,28},{20,24},{24,20},{28,16},{1,13},{... | collective-permute-start | bytes 196616 | tf_op jit(solution)/shard_map/ppermute | solution.py:24
  101.1 6.3 %collective-permute-start.47 = (bf16[16,2048]{1,0:T(8,128)(2,1)S(1)}, bf16[16,2048]{1,0:T(8,128)(2,1)S(1)}, u32[]{:S(2)}, u32[]{:S(2)}) collective-permute-start(bf16[16,2048]{1,0:T(8,128)(2,1)S(1)} %shard_map.170), channel_id=1, source_target_pairs={{0,24},{4,28},{8,16},{12,20},{16,8},{20,12},{24,0},{28,4},{1,25},{... | collective-permute-start | bytes 196616 | tf_op jit(solution)/shard_map/ppermute | solution.py:24
  103.1 6.6 %collective-permute-start.45 = (bf16[16,2048]{1,0:T(8,128)(2,1)S(1)}, bf16[16,2048]{1,0:T(8,128)(2,1)S(1)}, u32[]{:S(2)}, u32[]{:S(2)}) collective-permute-start(bf16[16,2048]{1,0:T(8,128)(2,1)S(1)} %get-tuple-element.79), channel_id=1, source_target_pairs={{0,16},{4,20},{8,24},{12,28},{16,0},{20,4},{24,8},{28,12},{1,17},{... | collective-permute-start | bytes 196616 | tf_op jit(solution)/shard_map/ppermute | solution.py:24
  103.5 6.2 %collective-permute-start.48 = (bf16[16,2048]{1,0:T(8,128)(2,1)S(1)}, bf16[16,2048]{1,0:T(8,128)(2,1)S(1)}, u32[]{:S(2)}, u32[]{:S(2)}) collective-permute-start(bf16[16,2048]{1,0:T(8,128)(2,1)S(1)} %get-tuple-element.81), channel_id=1, source_target_pairs={{0,4},{4,0},{8,12},{12,8},{16,20},{20,16},{24,28},{28,24},{1,5},{5... | collective-permute-start | bytes 196616 | tf_op jit(solution)/shard_map/ppermute | solution.py:24
  (4 other events, 7.4 us)
